TPU v7x, 32 devices: a whole 2x2x4 slice. The times are simulated.
32 devices in a mesh: slab: 8 (over z, y), led: 4 (over x, core).
Axes of the slice: x: 2, y: 2, z: 4, core: 2. Of those that a mesh axis runs over, the one named last changes fastest.
Arguments:
- spectrum: float32 [2, 2048, 2048], P(None, 'slab'), may hold values from -6 to 6
- led_rows: int32 [8], P('led'), may hold values from 256 to 768
- led_cols: int32 [8], P('led'), may hold values from 0 to 1024
- images: float32 [8, 1024, 1024], P('led', 'slab'), may hold values from 0.05 to 4
Outputs:
- updated: float32 [2, 2048, 2048], P(None, 'slab', 'led')
All inputs are finite; a program needn't handle non-finite values.
Results may differ from a plain program's by a relative error of at most 0.0065.
Values may be sent and summed in bfloat16 or wider, within the bound.
No kernel may reach another device: no remote copies, remote signals or barrier semaphores. Data moves between devices by JAX's collectives and lax.ppermute only.
A program may use at most 64 MiB of HBM per device.

v0:
```python
import functools

import jax
import jax.numpy as jnp
import numpy as np
from jax import lax
from jax.experimental import pallas as pl
from jax.experimental.pallas import tpu as pltpu
from jax.sharding import PartitionSpec as P

LANES = 128


def as_sent(value):
    return jax.tree.map(lambda a: a.astype(jnp.bfloat16) if a.dtype == jnp.float32 else a, value)


def host_tables(width):
    index = np.arange(width, dtype=np.int64)
    angle_index = (index[:, None] * index[None, :] % width).astype(np.float32)
    angle = angle_index * np.float32(2.0 * 3.141592653589793 / width)
    scale = np.float32(1.0) / np.sqrt(np.float32(width))
    return (
        (np.cos(angle) * scale).astype(jnp.bfloat16),
        (np.sin(angle) * scale).astype(jnp.bfloat16),
    )


def make_pupil(row_index, col_index, width):
    row_term = (2 * row_index + 1 - width) * (2 * row_index + 1 - width)
    col_term = (2 * col_index + 1 - width) * (2 * col_index + 1 - width)
    return (row_term[:, None] + col_term[None, :] < width * width).astype(jnp.float32)


def contract(form, left, right):
    return jnp.einsum(form, left, right, preferred_element_type=jnp.float32)


def take_rows(strip, start, width):
    return lax.dynamic_slice_in_dim(strip, start, width, 1)


def place_rows(block, start, total, axis_dim):
    shape = list(block.shape)
    shape[axis_dim] = total
    holder = jnp.zeros(tuple(shape), block.dtype)
    return lax.dynamic_update_slice_in_dim(holder, block, start, axis_dim)


def modulus_step(field_in_re, field_in_im, image, cos_table, sin_table):
    field_re = contract("lka,am->lkm", field_in_re, cos_table) + contract(
        "lka,am->lkm", field_in_im, sin_table
    )
    field_im = contract("lka,am->lkm", field_in_im, cos_table) - contract(
        "lka,am->lkm", field_in_re, sin_table
    )
    factor = jnp.sqrt(image) / jnp.sqrt(field_re * field_re + field_im * field_im + 0.25) - 1.0
    diff_re = (field_re * factor).astype(jnp.bfloat16)
    diff_im = (field_im * factor).astype(jnp.bfloat16)
    back_re = (
        contract("lkm,ma->lka", diff_re, cos_table) - contract("lkm,ma->lka", diff_im, sin_table)
    ).astype(jnp.bfloat16)
    back_im = (
        contract("lkm,ma->lka", diff_im, cos_table) + contract("lkm,ma->lka", diff_re, sin_table)
    ).astype(jnp.bfloat16)
    return (back_re, back_im)


def body_any(spectrum, led_rows, led_cols, images):
    width = images.shape[2]
    slab_rows = spectrum.shape[1]
    columns = spectrum.shape[2]
    slabs = lax.axis_size("slab")
    total_rows = slab_rows * slabs
    position = lax.axis_index("slab")
    cos_table, sin_table = (jnp.asarray(t) for t in host_tables(width))
    own_rows = position * slab_rows + jnp.arange(slab_rows, dtype=jnp.int32)
    col_index = jnp.arange(width, dtype=jnp.int32)

    def take_cols(start):
        return lax.dynamic_slice_in_dim(spectrum, start, width, 2)

    def owner_mask(start):
        return make_pupil(own_rows - start, col_index, width)

    windows = jax.vmap(take_cols)(led_cols)
    masks = jax.vmap(owner_mask)(led_rows)
    win_re = (windows[:, 0] * masks).astype(jnp.bfloat16)
    win_im = (windows[:, 1] * masks).astype(jnp.bfloat16)

    def slice_strip(block, start):
        return take_rows(block, start, width)

    row_re = (
        contract("lgb,bk->lkg", win_re, cos_table) + contract("lgb,bk->lkg", win_im, sin_table)
    ).astype(jnp.bfloat16)
    row_im = (
        contract("lgb,bk->lkg", win_im, cos_table) - contract("lgb,bk->lkg", win_re, sin_table)
    ).astype(jnp.bfloat16)
    col_re, col_im = (
        lax.all_to_all(row_re, "slab", split_axis=1, concat_axis=2, tiled=True),
        lax.all_to_all(row_im, "slab", split_axis=1, concat_axis=2, tiled=True),
    )
    field_in_re = jax.vmap(slice_strip)(col_re, led_rows)
    field_in_im = jax.vmap(slice_strip)(col_im, led_rows)
    back_re, back_im = modulus_step(field_in_re, field_in_im, images, cos_table, sin_table)

    def place_strip(block, start):
        return place_rows(block, start, total_rows, 1)

    full_re = jax.vmap(place_strip)(back_re, led_rows)
    full_im = jax.vmap(place_strip)(back_im, led_rows)
    home_re, home_im = (
        lax.all_to_all(as_sent(full_re), "slab", split_axis=2, concat_axis=1, tiled=True).astype(
            full_re.dtype
        ),
        lax.all_to_all(as_sent(full_im), "slab", split_axis=2, concat_axis=1, tiled=True).astype(
            full_im.dtype
        ),
    )
    upd_re = contract("lkg,kb->lgb", home_re, cos_table) - contract(
        "lkg,kb->lgb", home_im, sin_table
    )
    upd_im = contract("lkg,kb->lgb", home_im, cos_table) + contract(
        "lkg,kb->lgb", home_re, sin_table
    )
    upd_re = upd_re * masks
    upd_im = upd_im * masks

    def add_window(number, gradient):
        start = led_cols[number]
        piece = jnp.stack([upd_re[number], upd_im[number]])
        current = lax.dynamic_slice_in_dim(gradient, start, width, 2)
        return lax.dynamic_update_slice_in_dim(gradient, current + piece, start, 2)

    gradient = lax.fori_loop(
        0, led_rows.shape[0], add_window, jnp.zeros((2, slab_rows, columns), jnp.float32)
    )
    summed = lax.psum_scatter(gradient, "led", scatter_dimension=2, tiled=True)
    share = summed.shape[2]
    own_part = lax.dynamic_slice_in_dim(spectrum, lax.axis_index("led") * share, share, 2)
    return own_part + summed


SLABS = 8
PERIOD = 4
FIRST, LAST = 0, 7
EARLY = (5, 7)
LATE = (0, 1, 2, 3, 4, 6)
PASSED = {4: 0, 6: 1}
PASSED_FROM = {FIRST: 1, LAST: 6}


def dot(left, right):
    return jnp.dot(left, right, preferred_element_type=jnp.float32)


def window_mask(first_row, row_start, col_start, rows, first_col, cols, width):
    shape = (rows, cols)
    at_row = lax.broadcasted_iota(jnp.int32, shape, 0) + (first_row - row_start)
    at_col = lax.broadcasted_iota(jnp.int32, shape, 1) + (first_col - col_start)
    wraps = at_col < 0
    at_col = jnp.where(wraps, at_col + width, at_col)
    row_term = 2 * at_row + 1 - width
    col_term = 2 * at_col + 1 - width
    return row_term * row_term + col_term * col_term < width * width, wraps


def row_block(window, table):
    both = dot(window, table)
    half = both.shape[0] // 2
    row_re = both[:half, :LANES] + both[half:, LANES:]
    row_im = both[half:, :LANES] - both[:half, LANES:]
    return row_re.astype(jnp.bfloat16), row_im.astype(jnp.bfloat16)


def store_parts(out, values):
    per = out.shape[0] // 2
    rows = out.shape[1]
    for plane, value in enumerate(values):
        for led in range(per):
            out[plane * per + led] = value[led * rows : (led + 1) * rows]


def first_kernel(led_rows, led_cols, spectrum_any, table_any, window, *rest):
    outs = rest[: len(EARLY)]
    early, spectrum, table, sems = rest[len(EARLY) :]
    position = lax.axis_index("slab")
    leds = led_rows.shape[0]
    rows = spectrum.shape[1]
    width = window.shape[1]
    chunks = 4
    step = rows // chunks
    fetches = [
        pltpu.make_async_copy(
            spectrum_any.at[:, pl.ds(i * step, step)],
            spectrum.at[:, pl.ds(i * step, step)],
            sems.at[i],
        )
        for i in range(chunks)
    ]
    tables = [
        pltpu.make_async_copy(
            table_any.at[jnp.bitwise_xor(position, d)], table.at[i], sems.at[chunks + i]
        )
        for i, d in enumerate(EARLY)
    ]
    for copy in fetches + tables:
        copy.start()
    for i in range(chunks):
        fetches[i].wait()
        here = slice(i * step, (i + 1) * step)
        for led in range(leds):
            inside, wraps = window_mask(
                position * rows + i * step, led_rows[led], led_cols[led], step, 0, width, width
            )
            for plane in range(2):
                value = jnp.where(
                    wraps, spectrum[plane, here, width:], spectrum[plane, here, :width]
                )
                at = (plane * leds + led) * rows + i * step
                window[at : at + step, :] = jnp.where(inside, value, 0.0).astype(jnp.bfloat16)
    for i in range(len(EARLY)):
        tables[i].wait()
        values = row_block(window[...], table[i])
        store_parts(outs[i], values)
        store_parts(early.at[i], values)


def second_kernel(window, table, *outs):
    position = lax.axis_index("slab")
    for d, out in zip(LATE, outs):
        store_parts(out, row_block(window[...], table[jnp.bitwise_xor(position, d)]))


def field_kernel(amplitude, table, *rest):
    blocks = rest[:SLABS]
    outs = rest[SLABS : SLABS + PERIOD]
    field_in, diff = rest[SLABS + PERIOD :]
    position = lax.axis_index("slab")
    parts, rows, _ = blocks[0].shape
    half = parts // 2 * LANES
    width = field_in.shape[0]
    steps = width // LANES
    group = 4
    for d in range(SLABS):
        source = jnp.bitwise_xor(position, d)
        if d in PASSED:
            for by, origin in PASSED_FROM.items():
                source = jnp.where(source == by, origin, source)
        at = pl.multiple_of(jnp.bitwise_and(source, PERIOD - 1) * rows, rows)
        for part in range(parts):
            where = (pl.ds(at, rows), slice(part * LANES, (part + 1) * LANES))
            if d < PERIOD:
                field_in[where] = blocks[d][part]
            else:
                field_in[where] += blocks[d][part]
    for first in range(0, steps, group):
        product = dot(
            table[first : first + group].reshape(group * 2 * LANES, width), field_in[...]
        )
        for j in range(first, first + group):
            both = product[(j - first) * 2 * LANES : (j - first + 1) * 2 * LANES]
            field_re = both[:LANES, :half] + both[LANES:, half:]
            field_im = both[:LANES, half:] - both[LANES:, :half]
            here = pl.ds(j * LANES, LANES)
            factor = (
                amplitude[here, :] * lax.rsqrt(field_re * field_re + field_im * field_im + 0.25)
                - 1.0
            )
            diff[here, :half] = (field_re * factor).astype(jnp.bfloat16)
            diff[here, half:] = (field_im * factor).astype(jnp.bfloat16)
    pieces = rows // LANES
    for i in range(PERIOD):
        first = jnp.bitwise_and(jnp.bitwise_xor(position, i), PERIOD - 1) * pieces
        product = dot(table[pl.ds(first, pieces)].reshape(pieces * 2 * LANES, width), diff[...])
        for h in range(pieces):
            both = product[h * 2 * LANES : (h + 1) * 2 * LANES]
            here = pl.ds(h * LANES, LANES)
            back_re = (both[:LANES, :half] - both[LANES:, half:]).astype(jnp.bfloat16)
            back_im = (both[:LANES, half:] + both[LANES:, :half]).astype(jnp.bfloat16)
            for part in range(parts // 2):
                cols = slice(part * LANES, (part + 1) * LANES)
                outs[i][part, here, :] = back_re[:, cols]
                outs[i][parts // 2 + part, here, :] = back_im[:, cols]


def update_columns(first_step, last_step, led_rows, led_cols, table, back, out):
    position = lax.axis_index("slab")
    led_at = lax.axis_index("led")
    core = jnp.bitwise_and(led_at, 1)
    plane_x = jnp.right_shift(led_at, 1)
    leds = led_rows.shape[0]
    rows = back.shape[0] // (2 * leds)
    width = back.shape[1]
    group = width // LANES // 2
    for n in range(first_step, last_step):
        owner = 1 - core if n < group else core
        block = owner * group + n % group
        both = dot(back[...], table[block])
        half = leds * rows
        update = (
            both[:half, :LANES] - both[half:, LANES:],
            both[half:, :LANES] + both[:half, LANES:],
        )
        low = [0.0, 0.0]
        high = [0.0, 0.0]
        for led in range(leds):
            inside, wraps = window_mask(
                position * rows, led_rows[led], led_cols[led], rows, block * LANES, LANES, width
            )
            for plane in range(2):
                piece = jnp.where(inside, update[plane][led * rows : (led + 1) * rows], 0.0)
                low[plane] += jnp.where(wraps, 0.0, piece)
                high[plane] += jnp.where(wraps, piece, 0.0)
        cols = slice((n - first_step) * LANES, (n - first_step + 1) * LANES)
        for plane in range(2):
            out[1 - plane_x, plane, :, cols] = low[plane].astype(out.dtype)
            out[plane_x, plane, :, cols] = high[plane].astype(out.dtype)


def sent_kernel(led_rows, led_cols, table, *rest):
    blocks = rest[:SLABS]
    out, back = rest[SLABS:]
    position = lax.axis_index("slab")
    parts, rows, _ = blocks[0].shape
    for d in range(SLABS):
        at = pl.multiple_of(jnp.bitwise_xor(position, d) * LANES, LANES)
        for part in range(parts):
            back[part * rows : (part + 1) * rows, pl.ds(at, LANES)] = blocks[d][part]
    half = back.shape[1] // LANES // 2
    update_columns(0, half, led_rows, led_cols, table, back, out)


def kept_kernel(led_rows, led_cols, table, back, out):
    half = back.shape[1] // LANES // 2
    update_columns(half, 2 * half, led_rows, led_cols, table, back, out)


def local_call(kernel, out_shape, spaces, scratch, flops, moved, name):
    return pl.pallas_call(
        kernel,
        out_shape=out_shape,
        in_specs=[pl.BlockSpec(memory_space=space) for space in spaces],
        out_specs=jax.tree.map(lambda _: pl.BlockSpec(memory_space=pltpu.VMEM), out_shape),
        scratch_shapes=scratch,
        compiler_params=pltpu.CompilerParams(vmem_limit_bytes=32 * 2**20),
        cost_estimate=pl.CostEstimate(flops=flops, bytes_accessed=moved, transcendentals=0),
        name=name,
    )


def body_slabs(spectrum, led_rows, led_cols, images):
    leds, block, width = images.shape
    rows = spectrum.shape[1]
    led_at = lax.axis_index("led")
    bf16 = jnp.bfloat16
    vmem, smem, hbm = pltpu.VMEM, pltpu.SMEM, pltpu.HBM
    cos_table, sin_table = host_tables(width)
    steps = width // LANES
    by_col = np.stack(
        [
            np.concatenate([t[:, j * LANES : (j + 1) * LANES] for t in (cos_table, sin_table)], 1)
            for j in range(steps)
        ]
    )
    by_row = jnp.asarray(np.ascontiguousarray(by_col.transpose(0, 2, 1)))
    by_col = jnp.asarray(by_col)
    parts = 2 * leds
    sent_block = jax.ShapeDtypeStruct((parts, rows, LANES), bf16)
    flops = 8 * leds * rows * width * width

    window, *outs, early = local_call(
        first_kernel,
        [
            jax.ShapeDtypeStruct((parts * rows, width), bf16),
            *[sent_block] * len(EARLY),
            jax.ShapeDtypeStruct((len(EARLY),) + sent_block.shape, bf16),
        ],
        [smem, smem, hbm, hbm],
        [
            pltpu.VMEM(spectrum.shape, jnp.float32),
            pltpu.VMEM((len(EARLY),) + by_col.shape[1:], bf16),
            pltpu.SemaphoreType.DMA((4 + len(EARLY),)),
        ],
        flops // 4,
        8 * 2**20,
        "windows_and_early_rows",
    )(led_rows, led_cols, spectrum, by_col)
    passed = lax.ppermute(early, "slab", [(s, by) for by, s in PASSED_FROM.items()])
    windowed = range(FIRST + 1, LAST)
    col_blocks = {}
    for d, sent in zip(EARLY, outs):
        pairs = [(s, s ^ d) for s in windowed if s not in PASSED_FROM.values()]
        col_blocks[d] = lax.ppermute(sent, "slab", pairs)
    row_blocks = local_call(
        second_kernel,
        [sent_block] * len(LATE),
        [vmem, vmem],
        [],
        3 * flops // 4,
        8 * 2**20,
        "late_rows",
    )(window, by_col)
    for d, sent in zip(LATE, row_blocks):
        if d == 0:
            col_blocks[d] = sent
        elif d in PASSED:
            pairs = [(s, s ^ d) for s in range(SLABS)]
            col_blocks[d] = lax.ppermute(sent + passed[PASSED[d]], "slab", pairs)
        else:
            col_blocks[d] = lax.ppermute(sent, "slab", [(s, s ^ d) for s in windowed])

    amplitude = jnp.sqrt(images).transpose(2, 0, 1).reshape(width, leds * block)
    back_blocks = local_call(
        field_kernel,
        [sent_block] * PERIOD,
        [vmem] * (2 + SLABS),
        [pltpu.VMEM((width, parts * block), bf16)] * 2,
        16 * leds * block * width * width,
        12 * 2**20,
        "modulus_step",
    )(amplitude, by_row, *[col_blocks[d] for d in range(SLABS)])

    def to_rows(d):
        sent = back_blocks[d % PERIOD]
        if d == 0:
            return sent
        return lax.ppermute(sent, "slab", [(s, s ^ d) for s in range(SLABS) if s ^ d in windowed])

    home = [to_rows(d) for d in range(SLABS)]
    share = width // 2
    sent, back = local_call(
        sent_kernel,
        [
            jax.ShapeDtypeStruct((2, 2, rows, share), bf16),
            jax.ShapeDtypeStruct((parts * rows, width), bf16),
        ],
        [smem, smem] + [vmem] * (1 + SLABS),
        [],
        flops // 2,
        8 * 2**20,
        "update_sent",
    )(led_rows, led_cols, by_col, *home)
    got = lax.ppermute(sent, "led", [(0, 1), (1, 0), (2, 3), (3, 2)])
    kept = local_call(
        kept_kernel,
        jax.ShapeDtypeStruct((2, 2, rows, share), jnp.float32),
        [smem, smem, vmem, vmem],
        [],
        flops // 2,
        8 * 2**20,
        "update_kept",
    )(led_rows, led_cols, by_col, back)
    over = (kept[0] + got[0].astype(jnp.float32)).astype(bf16)
    got_x = lax.ppermute(over, "led", [(0, 2), (2, 0), (1, 3), (3, 1)])
    own_part = lax.dynamic_slice_in_dim(spectrum, led_at * share, share, 2)
    base = own_part + (kept[1] + got[1].astype(jnp.float32))
    base, got_x = lax.optimization_barrier((base, got_x))
    return base + got_x.astype(jnp.float32)


def solution(mesh):
    placed = (P(None, "slab", None), P("led"), P("led"), P("led", "slab", None))
    fits = mesh.shape["slab"] == 8 and mesh.shape["led"] == 4

    def body(spectrum, led_rows, led_cols, images):
        shapes = (spectrum.shape, images.shape)
        if fits and shapes == ((2, 256, 2048), (2, 128, 1024)):
            return body_slabs(spectrum, led_rows, led_cols, images)
        return body_any(spectrum, led_rows, led_cols, images)

    return jax.shard_map(
        body, mesh=mesh, in_specs=placed, out_specs=P(None, "slab", "led"), check_vma=False
    )
```

profile of v0, /device:TPU:4, one launch (start us, length us, event | category | flops | bytes accessed | tf_op | source)
XLA Modules:
  0.0 141.0 jit_solution(3843165806216558926)
XLA Ops:
  0.0 2.2 %copy-done = bf16[8,1024,256]{2,1,0:T(8,128)(2,1)S(1)} copy-done((bf16[8,1024,256]{2,1,0:T(8,128)(2,1)S(1)}, bf16[8,1024,256]{2,1,0:T(8,128)(2,1)}, u32[]{:S(2)}) %copy-start) | copy-done | bytes 4194328
  2.2 2.2 %copy-done.3 = f32[2,256,2048]{2,1,0:T(8,128)S(1)} copy-done((f32[2,256,2048]{2,1,0:T(8,128)S(1)}, f32[2,256,2048]{2,1,0:T(8,128)}, u32[]{:S(2)}) %copy-start.3) | copy-done | bytes 4194328
  4.4 0.7 copy-done.4
  5.0 0.7 copy-done.6
  5.7 4.1 %windows_and_early_rows.1 = (bf16[1024,1024]{1,0:T(8,128)(2,1)S(1)}, bf16[4,256,128]{2,1,0:T(8,128)(2,1)S(1)}, bf16[4,256,128]{2,1,0:T(8,128)(2,1)S(1)}, bf16[2,4,256,128]{3,2,1,0:T(8,128)(2,1)S(1)}) custom-call(s32[2]{0:T(128)S(1)} %copy-done.4, s32[2]{0:T(128)S(1)} %copy-done.6, f32[2,256,2048]{2,1,0:T(8,128)S(1)} %copy-done.3, ...), custom_call_target="tpu_custom_call" | custom-call | flops 1073741824 | bytes 8388608 | tf_op jit(solution)/shard_map/windows_and_early_rows/pallas_call | solution.py:373
  9.8 1.3 collective-permute-start.3
  11.2 3.4 %late_rows.1 = (bf16[4,256,128]{2,1,0:T(8,128)(2,1)S(1)}, bf16[4,256,128]{2,1,0:T(8,128)(2,1)S(1)}, bf16[4,256,128]{2,1,0:T(8,128)(2,1)S(1)}, bf16[4,256,128]{2,...) custom-call(bf16[1024,1024]{1,0:T(8,128)(2,1)S(1)} %get-tuple-element.23.window, ...), custom_call_target="tpu_custom_call" | custom-call | flops 3221225472 | bytes 8388608 | tf_op jit(solution)/shard_map/late_rows/pallas_call | solution.py:396
  14.6 0.0 copy-start.11
  14.6 1.4 %collective-permute-start = (bf16[4,256,128]{2,1,0:T(8,128)(2,1)S(1)}, bf16[4,256,128]{2,1,0:T(8,128)(2,1)S(1)}, u32[]{:S(2)}, u32[]{:S(2)}) collective-permute-start(bf16[4,256,128]{2,1,0:T(8,128)(2,1)S(1)} %get-tuple-element.25), channel_id=1, source_target_pairs={{4,0},{8,12},{12,8},{16,20},{20,16},{24,28},{5,1},{9,13},{13,9},{1... | collective-permute-start | bytes 786440 | tf_op jit(solution)/shard_map/ppermute | solution.py:412
  16.1 4.0 %collective-permute-start.1 = (bf16[4,256,128]{2,1,0:T(8,128)(2,1)S(1)}, bf16[4,256,128]{2,1,0:T(8,128)(2,1)S(1)}, u32[]{:S(2)}, u32[]{:S(2)}) collective-permute-start(bf16[4,256,128]{2,1,0:T(8,128)(2,1)S(1)} %get-tuple-element.26), channel_id=1, source_target_pairs={{4,12},{8,0},{12,4},{16,24},{20,28},{24,16},{5,13},{9,1},{13,5},{1... | collective-permute-start | bytes 786440 | tf_op jit(solution)/shard_map/ppermute | solution.py:412
  20.0 2.3 %collective-permute-start.2 = (bf16[4,256,128]{2,1,0:T(8,128)(2,1)S(1)}, bf16[4,256,128]{2,1,0:T(8,128)(2,1)S(1)}, u32[]{:S(2)}, u32[]{:S(2)}) collective-permute-start(bf16[4,256,128]{2,1,0:T(8,128)(2,1)S(1)} %get-tuple-element.27), channel_id=1, source_target_pairs={{4,8},{8,4},{12,0},{16,28},{20,24},{24,20},{5,9},{9,5},{13,1},{17,... | collective-permute-start | bytes 786440 | tf_op jit(solution)/shard_map/ppermute | solution.py:412
  22.3 1.3 collective-permute-start.5
  23.6 0.0 collective-permute-done.3
  23.6 0.7 collective-permute-start.7
  24.3 0.9 fusion.4
  25.2 14.3 %collective-permute-done.rest_1_ = bf16[4,256,128]{2,1,0:T(8,128)(2,1)S(1)} collective-permute-done((bf16[4,256,128]{2,1,0:T(8,128)(2,1)S(1)}, bf16[4,256,128]{2,1,0:T(8,128)(2,1)S(1)}, u32[]{:S(2)}, u32[]{:S(2)}) %collective-permute-start) | collective-permute-done | bytes 262176 | tf_op jit(solution)/shard_map/ppermute | solution.py:412
  39.4 0.0 collective-permute-start.4
  39.4 0.0 collective-permute-done.1.rest_2_
  39.4 6.4 %collective-permute-start.6 = (bf16[4,256,128]{2,1,0:T(8,128)(2,1)}, bf16[4,256,128]{2,1,0:T(8,128)(2,1)}, u32[]{:S(2)}, u32[]{:S(2)}) collective-permute-start(bf16[4,256,128]{2,1,0:T(8,128)(2,1)} %get-tuple-element.41), channel_id=1, source_target_pairs={{0,24},{4,28},{8,16},{12,20},{16,8},{20,12},{24,0},{28,4},{1,25},{... | collective-permute-start | bytes 786440 | tf_op jit(solution)/shard_map/ppermute | solution.py:410
  45.9 1.2 sqrt.3
  47.1 1.6 %copy.8.amplitude = f32[1024,256]{1,0:T(8,128)S(1)} copy(f32[1024,256]{0,1:T(8,128)} %bitcast.17) | data formatting | bytes 2097152 | tf_op jit(solution)/shard_map/reshape | solution.py:414
  48.6 0.0 collective-permute-done.2.rest_3_
  48.7 0.0 collective-permute-done.7.rest_7_
  48.7 12.4 %collective-permute-done.4.rest_4_ = bf16[4,256,128]{2,1,0:T(8,128)(2,1)S(1)} collective-permute-done((bf16[4,256,128]{2,1,0:T(8,128)(2,1)}, bf16[4,256,128]{2,1,0:T(8,128)(2,1)S(1)}, u32[]{:S(2)}, u32[]{:S(2)}) %collective-permute-start.4) | collective-permute-done | bytes 262176 | tf_op jit(solution)/shard_map/ppermute | solution.py:410
  61.0 2.2 %copy-done.8 = bf16[8,256,1024]{2,1,0:T(8,128)(2,1)S(1)} copy-done((bf16[8,256,1024]{2,1,0:T(8,128)(2,1)S(1)}, bf16[8,256,1024]{2,1,0:T(8,128)(2,1)}, u32[]{:S(2)}) %copy-start.8) | copy-done | bytes 4194328
  63.2 0.9 copy-done.10
  64.2 6.2 %modulus_step.1 = (bf16[4,256,128]{2,1,0:T(8,128)(2,1)S(1)}, bf16[4,256,128]{2,1,0:T(8,128)(2,1)S(1)}, bf16[4,256,128]{2,1,0:T(8,128)(2,1)S(1)}, bf16[4,256,128]{2,1,0:T(8,128)(2,1)S(1)}) custom-call(f32[1024,256]{1,0:T(8,128)S(1)} %copy.8.amplitude, bf16[8,256,1024]{2,1,0:T(8,128)(2,1)S(1)} %copy-done.8, bf16[4,256,128]{2,1,0:T(8,128)(2,1)S(1)} %copy-done.10, ...), custom_call_target="tpu_custom_call" | custom-call | flops 4294967296 | bytes 12582912 | tf_op jit(solution)/shard_map/modulus_step/pallas_call | solution.py:415
  70.4 8.4 %collective-permute-start.10 = (bf16[4,256,128]{2,1,0:T(8,128)(2,1)S(1)}, bf16[4,256,128]{2,1,0:T(8,128)(2,1)S(1)}, u32[]{:S(2)}, u32[]{:S(2)}) collective-permute-start(bf16[4,256,128]{2,1,0:T(8,128)(2,1)S(1)} %get-tuple-element.36), channel_id=1, source_target_pairs={{0,12},{4,8},{8,4},{20,24},{24,20},{28,16},{1,13},{5,9},{9,5},{21,... | collective-permute-start | bytes 786440 | tf_op jit(solution)/shard_map/ppermute | solution.py:429
  78.8 1.9 %collective-permute-start.11 = (bf16[4,256,128]{2,1,0:T(8,128)(2,1)S(1)}, bf16[4,256,128]{2,1,0:T(8,128)(2,1)S(1)}, u32[]{:S(2)}, u32[]{:S(2)}) collective-permute-start(bf16[4,256,128]{2,1,0:T(8,128)(2,1)S(1)} %get-tuple-element.33.rest_0_), channel_id=1, source_target_pairs={{0,16},{4,20},{8,24},{20,4},{24,8},{28,12},{1,17},{5,21},{9,25},{2... | collective-permute-start | bytes 786440 | tf_op jit(solution)/shard_map/ppermute | solution.py:429
  80.7 4.3 %collective-permute-start.14 = (bf16[4,256,128]{2,1,0:T(8,128)(2,1)S(1)}, bf16[4,256,128]{2,1,0:T(8,128)(2,1)S(1)}, u32[]{:S(2)}, u32[]{:S(2)}) collective-permute-start(bf16[4,256,128]{2,1,0:T(8,128)(2,1)S(1)} %get-tuple-element.36), channel_id=1, source_target_pairs={{4,24},{8,20},{12,16},{16,12},{20,8},{24,4},{5,25},{9,21},{13,17},... | collective-permute-start | bytes 786440 | tf_op jit(solution)/shard_map/ppermute | solution.py:429
  85.0 1.9 %collective-permute-start.12 = (bf16[4,256,128]{2,1,0:T(8,128)(2,1)S(1)}, bf16[4,256,128]{2,1,0:T(8,128)(2,1)S(1)}, u32[]{:S(2)}, u32[]{:S(2)}) collective-permute-start(bf16[4,256,128]{2,1,0:T(8,128)(2,1)S(1)} %get-tuple-element.34), channel_id=1, source_target_pairs={{0,20},{4,16},{12,24},{16,4},{24,12},{28,8},{1,21},{5,17},{13,25},... | collective-permute-start | bytes 786440 | tf_op jit(solution)/shard_map/ppermute | solution.py:429
  86.9 1.3 collective-permute-start.13
  88.2 0.0 collective-permute-done.10.rest_3_
  88.2 1.3 collective-permute-start.8
  89.5 18.2 %collective-permute-done.11.rest_4_ = bf16[4,256,128]{2,1,0:T(8,128)(2,1)S(1)} collective-permute-done((bf16[4,256,128]{2,1,0:T(8,128)(2,1)S(1)}, bf16[4,256,128]{2,1,0:T(8,128)(2,1)S(1)}, u32[]{:S(2)}, u32[]{:S(2)}) %collective-permute-start.11) | collective-permute-done | bytes 262176 | tf_op jit(solution)/shard_map/ppermute | solution.py:429
  107.7 2.1 %collective-permute-start.9 = (bf16[4,256,128]{2,1,0:T(8,128)(2,1)S(1)}, bf16[4,256,128]{2,1,0:T(8,128)(2,1)S(1)}, u32[]{:S(2)}, u32[]{:S(2)}) collective-permute-start(bf16[4,256,128]{2,1,0:T(8,128)(2,1)S(1)} %get-tuple-element.35), channel_id=1, source_target_pairs={{0,8},{4,12},{12,4},{16,24},{24,16},{28,20},{1,9},{5,13},{13,5},{1... | collective-permute-start | bytes 786440 | tf_op jit(solution)/shard_map/ppermute | solution.py:429
  109.8 1.9 %collective-permute-done.12.rest_5_ = bf16[4,256,128]{2,1,0:T(8,128)(2,1)S(1)} collective-permute-done((bf16[4,256,128]{2,1,0:T(8,128)(2,1)S(1)}, bf16[4,256,128]{2,1,0:T(8,128)(2,1)S(1)}, u32[]{:S(2)}, u32[]{:S(2)}) %collective-permute-start.12) | collective-permute-done | bytes 262176 | tf_op jit(solution)/shard_map/ppermute | solution.py:429
  111.7 0.0 collective-permute-done.13.rest_6_
  111.7 0.0 collective-permute-done.14.rest_7_
  111.7 4.3 %collective-permute-done.9.rest_2_ = bf16[4,256,128]{2,1,0:T(8,128)(2,1)S(1)} collective-permute-done((bf16[4,256,128]{2,1,0:T(8,128)(2,1)S(1)}, bf16[4,256,128]{2,1,0:T(8,128)(2,1)S(1)}, u32[]{:S(2)}, u32[]{:S(2)}) %collective-permute-start.9) | collective-permute-done | bytes 262176 | tf_op jit(solution)/shard_map/ppermute | solution.py:429
  116.0 3.8 %update_sent.1 = (bf16[2,2,256,512]{3,2,1,0:T(8,128)(2,1)S(1)}, bf16[1024,1024]{1,0:T(8,128)(2,1)S(1)}) custom-call(s32[2]{0:T(128)S(1)} %copy-done.5, s32[2]{0:T(128)S(1)} %copy-done.7, bf16[8,1024,256]{2,1,0:T(8,128)(2,1)S(1)} %copy-done.2, bf16[4,256,128]{2,1,0:T(8,128)(2,1)S(1)} %get-tuple-element.33.rest_0_, ...), custom_call_target="tpu_custom_call" | custom-call | flops 2147483648 | bytes 8388608 | tf_op jit(solution)/shard_map/update_sent/pallas_call | solution.py:433
  119.9 0.1 collective-permute-start.15
  119.9 3.1 %update_kept.1 = f32[2,2,256,512]{3,2,1,0:T(8,128)S(1)} custom-call(s32[2]{0:T(128)S(1)} %copy-done.5, s32[2]{0:T(128)S(1)} %copy-done.7, bf16[8,1024,256]{2,1,0:T(8,128)(2,1)S(1)} %copy-done.2, bf16[1024,1024]{1,0:T(8,128)(2,1)S(1)} %get-tuple-element.37.back), custom_call_target="tpu_custom_call" | custom-call | flops 2147483648 | bytes 8388608 | tf_op jit(solution)/shard_map/update_kept/pallas_call | solution.py:446
  123.1 1.0 fusion.3
  124.1 1.9 %collective-permute-start.16 = (bf16[2,256,512]{2,1,0:T(8,128)(2,1)}, bf16[2,256,512]{2,1,0:T(8,128)(2,1)}, u32[]{:S(2)}, u32[]{:S(2)}) collective-permute-start(bf16[2,256,512]{2,1,0:T(8,128)(2,1)} %fusion.3), channel_id=1, source_target_pairs={{0,2},{2,0},{1,3},{3,1},{4,6},{6,4},{5,7},{7,5},{8,10},{10,8},{9,1... | collective-permute-start | bytes 1572872 | tf_op jit(solution)/shard_map/ppermute | solution.py:456
  125.9 1.5 %fusion.2 = f32[2,256,512]{2,1,0:T(8,128)S(1)} fusion(f32[2,2,256,512]{3,2,1,0:T(8,128)S(1)} %update_kept.1, f32[2,256,2048]{2,1,0:T(8,128)} %spectrum_any.1, s32[]{:T(128)S(6)} %select_n.3, bf16[2,2,256,512]{3,2,1,0:T(8,128)(2,1)S(1)} %collective-permute-done.15), kind=kLoop, calls=%fused_computation.4 | loop fusion | flops 786432 | bytes 3670020 | tf_op jit(solution)/shard_map/add | solution.py:458
  127.4 11.4 %collective-permute-done.16 = bf16[2,256,512]{2,1,0:T(8,128)(2,1)} collective-permute-done((bf16[2,256,512]{2,1,0:T(8,128)(2,1)}, bf16[2,256,512]{2,1,0:T(8,128)(2,1)}, u32[]{:S(2)}, u32[]{:S(2)}) %collective-permute-start.16) | collective-permute-done | bytes 524320 | tf_op jit(solution)/shard_map/ppermute | solution.py:456
  138.8 2.2 %convert_add_fusion = f32[2,256,512]{2,1,0:T(8,128)} fusion(f32[2,256,512]{2,1,0:T(8,128)S(1)} %fusion.2, bf16[2,256,512]{2,1,0:T(8,128)(2,1)} %collective-permute-done.16), kind=kLoop, calls=%fused_computation.5 | loop fusion | flops 524288 | bytes 2621440 | tf_op jit(solution)/shard_map/add | solution.py:460
  (21 shorter events, 0.0 us)
Async XLA Ops:
  0.0 2.2 %copy-start = (bf16[8,1024,256]{2,1,0:T(8,128)(2,1)S(1)}, bf16[8,1024,256]{2,1,0:T(8,128)(2,1)}, u32[]{:S(2)}) copy-start(bf16[8,1024,256]{2,1,0:T(8,128)(2,1)} %constant.15.clone.table_any.table) | copy-start | bytes 12582916
  2.2 2.2 %copy-start.3 = (f32[2,256,2048]{2,1,0:T(8,128)S(1)}, f32[2,256,2048]{2,1,0:T(8,128)}, u32[]{:S(2)}) copy-start(f32[2,256,2048]{2,1,0:T(8,128)} %spectrum_any.1) | copy-start | bytes 12582916
  4.4 0.7 copy-start.4
  5.0 0.7 copy-start.6
  5.7 5.5 %copy-start.1 = (bf16[8,1024,256]{2,1,0:T(8,128)(2,1)S(1)}, bf16[8,1024,256]{2,1,0:T(8,128)(2,1)}, u32[]{:S(2)}) copy-start(bf16[8,1024,256]{2,1,0:T(8,128)(2,1)} %constant.15.clone.table_any.table) | copy-start | bytes 12582916
  9.8 13.8 %collective-permute-start.3 = (bf16[2,4,256,128]{3,2,1,0:T(8,128)(2,1)S(1)}, bf16[2,4,256,128]{3,2,1,0:T(8,128)(2,1)S(1)}, u32[]{:S(2)}, u32[]{:S(2)}) collective-permute-start(bf16[2,4,256,128]{3,2,1,0:T(8,128)(2,1)S(1)} %get-tuple-element.29), channel_id=1, source_target_pairs={{4,0},{24,28},{5,1},{25,29},{6,2},{26,30},{7,3},{27,31}} | collective-permute-start | bytes 1572872 | tf_op jit(solution)/shard_map/ppermute | solution.py:390
  14.6 32.5 %copy-start.9 = (bf16[4,256,128]{2,1,0:T(8,128)(2,1)}, bf16[4,256,128]{2,1,0:T(8,128)(2,1)S(1)}, u32[]{:S(2)}) copy-start(bf16[4,256,128]{2,1,0:T(8,128)(2,1)S(1)} %get-tuple-element.24.rest_0_) | copy-start | bytes 786436
  14.6 31.2 %copy-start.11 = (f32[2,128,1024]{2,1,0:T(8,128)S(1)}, f32[2,128,1024]{2,1,0:T(8,128)}, u32[]{:S(2)}) copy-start(f32[2,128,1024]{2,1,0:T(8,128)} %param.9) | copy-start | bytes 3145732
  14.6 24.8 %collective-permute-start = (bf16[4,256,128]{2,1,0:T(8,128)(2,1)S(1)}, bf16[4,256,128]{2,1,0:T(8,128)(2,1)S(1)}, u32[]{:S(2)}, u32[]{:S(2)}) collective-permute-start(bf16[4,256,128]{2,1,0:T(8,128)(2,1)S(1)} %get-tuple-element.25), channel_id=1, source_target_pairs={{4,0},{8,12},{12,8},{16,20},{20,16},{24,28},{5,1},{9,13},{13,9},{1... | collective-permute-start | bytes 786440 | tf_op jit(solution)/shard_map/ppermute | solution.py:412
  16.1 23.4 %collective-permute-start.1 = (bf16[4,256,128]{2,1,0:T(8,128)(2,1)S(1)}, bf16[4,256,128]{2,1,0:T(8,128)(2,1)S(1)}, u32[]{:S(2)}, u32[]{:S(2)}) collective-permute-start(bf16[4,256,128]{2,1,0:T(8,128)(2,1)S(1)} %get-tuple-element.26), channel_id=1, source_target_pairs={{4,12},{8,0},{12,4},{16,24},{20,28},{24,16},{5,13},{9,1},{13,5},{1... | collective-permute-start | bytes 786440 | tf_op jit(solution)/shard_map/ppermute | solution.py:412
  20.0 28.6 %collective-permute-start.2 = (bf16[4,256,128]{2,1,0:T(8,128)(2,1)S(1)}, bf16[4,256,128]{2,1,0:T(8,128)(2,1)S(1)}, u32[]{:S(2)}, u32[]{:S(2)}) collective-permute-start(bf16[4,256,128]{2,1,0:T(8,128)(2,1)S(1)} %get-tuple-element.27), channel_id=1, source_target_pairs={{4,8},{8,4},{12,0},{16,28},{20,24},{24,20},{5,9},{9,5},{13,1},{17,... | collective-permute-start | bytes 786440 | tf_op jit(solution)/shard_map/ppermute | solution.py:412
  22.3 26.3 %collective-permute-start.5 = (bf16[4,256,128]{2,1,0:T(8,128)(2,1)S(1)}, bf16[4,256,128]{2,1,0:T(8,128)(2,1)S(1)}, u32[]{:S(2)}, u32[]{:S(2)}) collective-permute-start(bf16[4,256,128]{2,1,0:T(8,128)(2,1)S(1)} %get-tuple-element.30), channel_id=1, source_target_pairs={{8,28},{12,24},{16,4},{20,0},{9,29},{13,25},{17,5},{21,1},{10,30},... | collective-permute-start | bytes 786440 | tf_op jit(solution)/shard_map/ppermute | solution.py:395
  23.6 25.0 %collective-permute-start.7 = (bf16[4,256,128]{2,1,0:T(8,128)(2,1)S(1)}, bf16[4,256,128]{2,1,0:T(8,128)(2,1)S(1)}, u32[]{:S(2)}, u32[]{:S(2)}) collective-permute-start(bf16[4,256,128]{2,1,0:T(8,128)(2,1)S(1)} %get-tuple-element.32), channel_id=1, source_target_pairs={{8,20},{12,16},{16,12},{20,8},{9,21},{13,17},{17,13},{21,9},{10,22... | collective-permute-start | bytes 786440 | tf_op jit(solution)/shard_map/ppermute | solution.py:395
  39.4 21.6 %collective-permute-start.4 = (bf16[4,256,128]{2,1,0:T(8,128)(2,1)}, bf16[4,256,128]{2,1,0:T(8,128)(2,1)S(1)}, u32[]{:S(2)}, u32[]{:S(2)}) collective-permute-start(bf16[4,256,128]{2,1,0:T(8,128)(2,1)} %get-tuple-element.42), channel_id=1, source_target_pairs={{0,16},{4,20},{8,24},{12,28},{16,0},{20,4},{24,8},{28,12},{1,17},{... | collective-permute-start | bytes 786440 | tf_op jit(solution)/shard_map/ppermute | solution.py:410
  39.4 21.6 %collective-permute-start.6 = (bf16[4,256,128]{2,1,0:T(8,128)(2,1)}, bf16[4,256,128]{2,1,0:T(8,128)(2,1)}, u32[]{:S(2)}, u32[]{:S(2)}) collective-permute-start(bf16[4,256,128]{2,1,0:T(8,128)(2,1)} %get-tuple-element.41), channel_id=1, source_target_pairs={{0,24},{4,28},{8,16},{12,20},{16,8},{20,12},{24,0},{28,4},{1,25},{... | collective-permute-start | bytes 786440 | tf_op jit(solution)/shard_map/ppermute | solution.py:410
  61.0 2.2 %copy-start.8 = (bf16[8,256,1024]{2,1,0:T(8,128)(2,1)S(1)}, bf16[8,256,1024]{2,1,0:T(8,128)(2,1)}, u32[]{:S(2)}) copy-start(bf16[8,256,1024]{2,1,0:T(8,128)(2,1)} %constant.14.clone.table) | copy-start | bytes 12582916
  63.2 0.9 copy-start.10
  64.2 51.8 %copy-start.2 = (bf16[8,1024,256]{2,1,0:T(8,128)(2,1)S(1)}, bf16[8,1024,256]{2,1,0:T(8,128)(2,1)}, u32[]{:S(2)}) copy-start(bf16[8,1024,256]{2,1,0:T(8,128)(2,1)} %constant.15.clone.table_any.table) | copy-start | bytes 12582916
  64.2 51.8 %copy-start.5 = (s32[2]{0:T(128)S(1)}, s32[2]{0:T(128)}, u32[]{:S(2)}) copy-start(s32[2]{0:T(128)} %led_rows.5) | copy-start | bytes 28
  64.2 51.8 %copy-start.7 = (s32[2]{0:T(128)S(1)}, s32[2]{0:T(128)}, u32[]{:S(2)}) copy-start(s32[2]{0:T(128)} %led_cols.5) | copy-start | bytes 28
  70.4 17.8 %collective-permute-start.10 = (bf16[4,256,128]{2,1,0:T(8,128)(2,1)S(1)}, bf16[4,256,128]{2,1,0:T(8,128)(2,1)S(1)}, u32[]{:S(2)}, u32[]{:S(2)}) collective-permute-start(bf16[4,256,128]{2,1,0:T(8,128)(2,1)S(1)} %get-tuple-element.36), channel_id=1, source_target_pairs={{0,12},{4,8},{8,4},{20,24},{24,20},{28,16},{1,13},{5,9},{9,5},{21,... | collective-permute-start | bytes 786440 | tf_op jit(solution)/shard_map/ppermute | solution.py:429
  78.8 29.0 %collective-permute-start.11 = (bf16[4,256,128]{2,1,0:T(8,128)(2,1)S(1)}, bf16[4,256,128]{2,1,0:T(8,128)(2,1)S(1)}, u32[]{:S(2)}, u32[]{:S(2)}) collective-permute-start(bf16[4,256,128]{2,1,0:T(8,128)(2,1)S(1)} %get-tuple-element.33.rest_0_), channel_id=1, source_target_pairs={{0,16},{4,20},{8,24},{20,4},{24,8},{28,12},{1,17},{5,21},{9,25},{2... | collective-permute-start | bytes 786440 | tf_op jit(solution)/shard_map/ppermute | solution.py:429
  80.7 31.0 %collective-permute-start.14 = (bf16[4,256,128]{2,1,0:T(8,128)(2,1)S(1)}, bf16[4,256,128]{2,1,0:T(8,128)(2,1)S(1)}, u32[]{:S(2)}, u32[]{:S(2)}) collective-permute-start(bf16[4,256,128]{2,1,0:T(8,128)(2,1)S(1)} %get-tuple-element.36), channel_id=1, source_target_pairs={{4,24},{8,20},{12,16},{16,12},{20,8},{24,4},{5,25},{9,21},{13,17},... | collective-permute-start | bytes 786440 | tf_op jit(solution)/shard_map/ppermute | solution.py:429
  85.0 26.8 %collective-permute-start.12 = (bf16[4,256,128]{2,1,0:T(8,128)(2,1)S(1)}, bf16[4,256,128]{2,1,0:T(8,128)(2,1)S(1)}, u32[]{:S(2)}, u32[]{:S(2)}) collective-permute-start(bf16[4,256,128]{2,1,0:T(8,128)(2,1)S(1)} %get-tuple-element.34), channel_id=1, source_target_pairs={{0,20},{4,16},{12,24},{16,4},{24,12},{28,8},{1,21},{5,17},{13,25},... | collective-permute-start | bytes 786440 | tf_op jit(solution)/shard_map/ppermute | solution.py:429
  86.9 24.8 %collective-permute-start.13 = (bf16[4,256,128]{2,1,0:T(8,128)(2,1)S(1)}, bf16[4,256,128]{2,1,0:T(8,128)(2,1)S(1)}, u32[]{:S(2)}, u32[]{:S(2)}) collective-permute-start(bf16[4,256,128]{2,1,0:T(8,128)(2,1)S(1)} %get-tuple-element.35), channel_id=1, source_target_pairs={{0,24},{8,16},{12,20},{16,8},{20,12},{28,4},{1,25},{9,17},{13,21},... | collective-permute-start | bytes 786440 | tf_op jit(solution)/shard_map/ppermute | solution.py:429
  88.2 23.5 %collective-permute-start.8 = (bf16[4,256,128]{2,1,0:T(8,128)(2,1)S(1)}, bf16[4,256,128]{2,1,0:T(8,128)(2,1)S(1)}, u32[]{:S(2)}, u32[]{:S(2)}) collective-permute-start(bf16[4,256,128]{2,1,0:T(8,128)(2,1)S(1)} %get-tuple-element.34), channel_id=1, source_target_pairs={{0,4},{8,12},{12,8},{16,20},{20,16},{28,24},{1,5},{9,13},{13,9},{1... | collective-permute-start | bytes 786440 | tf_op jit(solution)/shard_map/ppermute | solution.py:429
  107.7 8.3 %collective-permute-start.9 = (bf16[4,256,128]{2,1,0:T(8,128)(2,1)S(1)}, bf16[4,256,128]{2,1,0:T(8,128)(2,1)S(1)}, u32[]{:S(2)}, u32[]{:S(2)}) collective-permute-start(bf16[4,256,128]{2,1,0:T(8,128)(2,1)S(1)} %get-tuple-element.35), channel_id=1, source_target_pairs={{0,8},{4,12},{12,4},{16,24},{24,16},{28,20},{1,9},{5,13},{13,5},{1... | collective-permute-start | bytes 786440 | tf_op jit(solution)/shard_map/ppermute | solution.py:429
  119.9 3.2 %collective-permute-start.15 = (bf16[2,2,256,512]{3,2,1,0:T(8,128)(2,1)S(1)}, bf16[2,2,256,512]{3,2,1,0:T(8,128)(2,1)S(1)}, u32[]{:S(2)}, u32[]{:S(2)}) collective-permute-start(bf16[2,2,256,512]{3,2,1,0:T(8,128)(2,1)S(1)} %get-tuple-element.38), channel_id=1, source_target_pairs={{0,1},{1,0},{2,3},{3,2},{4,5},{5,4},{6,7},{7,6},{8,9},{9,8},{10,11... | collective-permute-start | bytes 3145736 | tf_op jit(solution)/shard_map/ppermute | solution.py:445
  124.1 14.8 %collective-permute-start.16 = (bf16[2,256,512]{2,1,0:T(8,128)(2,1)}, bf16[2,256,512]{2,1,0:T(8,128)(2,1)}, u32[]{:S(2)}, u32[]{:S(2)}) collective-permute-start(bf16[2,256,512]{2,1,0:T(8,128)(2,1)} %fusion.3), channel_id=1, source_target_pairs={{0,2},{2,0},{1,3},{3,1},{4,6},{6,4},{5,7},{7,5},{8,10},{10,8},{9,1... | collective-permute-start | bytes 1572872 | tf_op jit(solution)/shard_map/ppermute | solution.py:456
where the time goes:
time: 143 us; the launch traced here: 141 us
  waiting for transfers between devices  62.4 us (44%)
  starting transfers between devices  40.4 us (28%)
  Pallas kernels  20.8 us (15%)
  local copies, waits for them, and re-layouts  11.6 us (8%)
  other arithmetic  5.49 us (4%)
    ppermute x7, waiting for transfers between devices, to_rows(): lax.ppermute(sent, 'slab', [(s, s ^ d) for s in range(SLABS) if s ^ d in...  24.4 us
    ppermute x7, starting transfers between devices, to_rows(): lax.ppermute(sent, 'slab', [(s, s ^ d) for s in range(SLABS) if s ^ d in...  21.1 us
    ppermute x3, waiting for transfers between devices, body_slabs(): col_blocks[d] = lax.ppermute(sent, 'slab', [(s, s ^ d) for s in windowed])  14.3 us
    ppermute x2, waiting for transfers between devices, body_slabs(): col_blocks[d] = lax.ppermute(sent + passed[PASSED[d]], 'slab', pairs)  12.4 us
    ppermute x1, waiting for transfers between devices, body_slabs(): got_x = lax.ppermute(over, 'led', [(0, 2), (2, 0), (1, 3), (3, 1)])  11.4 us
    unnamed x24, local copies, waits for them, and re-layouts  8.85 us
    ppermute x3, starting transfers between devices, body_slabs(): col_blocks[d] = lax.ppermute(sent, 'slab', [(s, s ^ d) for s in windowed])  7.66 us
    ppermute x2, starting transfers between devices, body_slabs(): col_blocks[d] = lax.ppermute(sent + passed[PASSED[d]], 'slab', pairs)  6.41 us
  transfers between devices with their start and end apart: 17, of which 6 were waited for; matrix products, arithmetic and copies ran while one was open for 4% of the time, Pallas kernels for 5%

commit v1 on v0

--- a/solution.py
+++ b/solution.py
@@ -151,6 +151,30 @@
 PASSED_FROM = {FIRST: 1, LAST: 6}
 
 
+class Stream:
+    def __init__(self, source, target, sems, blocks):
+        self.target = target
+        self.copies = [
+            pltpu.make_async_copy(source.at[block], target.at[i], sems.at[i])
+            for i, block in enumerate(blocks)
+        ]
+        self.started = 0
+        self.taken = 0
+        self.start()
+        self.start()
+
+    def start(self):
+        if self.started < len(self.copies):
+            self.copies[self.started].start()
+            self.started += 1
+
+    def take(self):
+        self.copies[self.taken].wait()
+        self.start()
+        self.taken += 1
+        return self.target[self.taken - 1]
+
+
 def dot(left, right):
     return jnp.dot(left, right, preferred_element_type=jnp.float32)
 
@@ -182,11 +206,11 @@
             out[plane * per + led] = value[led * rows : (led + 1) * rows]
 
 
-def first_kernel(led_rows, led_cols, spectrum_any, table_any, window, *rest):
+def first_kernel(starts, spectrum_any, table_any, window, *rest):
     outs = rest[: len(EARLY)]
-    early, spectrum, table, sems = rest[len(EARLY) :]
+    early, table, spectrum, sems, table_sems = rest[len(EARLY) :]
     position = lax.axis_index("slab")
-    leds = led_rows.shape[0]
+    leds = starts.shape[0] // 2
     rows = spectrum.shape[1]
     width = window.shape[1]
     chunks = 4
@@ -199,20 +223,17 @@
         )
         for i in range(chunks)
     ]
-    tables = [
-        pltpu.make_async_copy(
-            table_any.at[jnp.bitwise_xor(position, d)], table.at[i], sems.at[chunks + i]
-        )
-        for i, d in enumerate(EARLY)
-    ]
-    for copy in fetches + tables:
+    for copy in fetches:
         copy.start()
     for i in range(chunks):
         fetches[i].wait()
+        if i == chunks - 1:
+            blocks = [jnp.bitwise_xor(position, d) for d in EARLY]
+            tables = Stream(table_any, table, table_sems, blocks)
         here = slice(i * step, (i + 1) * step)
         for led in range(leds):
             inside, wraps = window_mask(
-                position * rows + i * step, led_rows[led], led_cols[led], step, 0, width, width
+                position * rows + i * step, starts[led], starts[leds + led], step, 0, width, width
             )
             for plane in range(2):
                 value = jnp.where(
@@ -221,28 +242,30 @@
                 at = (plane * leds + led) * rows + i * step
                 window[at : at + step, :] = jnp.where(inside, value, 0.0).astype(jnp.bfloat16)
     for i in range(len(EARLY)):
-        tables[i].wait()
-        values = row_block(window[...], table[i])
+        values = row_block(window[...], tables.take())
         store_parts(outs[i], values)
         store_parts(early.at[i], values)
 
 
-def second_kernel(window, table, *outs):
+def second_kernel(window, table_any, *rest):
+    outs = rest[: len(LATE)]
     position = lax.axis_index("slab")
-    for d, out in zip(LATE, outs):
-        store_parts(out, row_block(window[...], table[jnp.bitwise_xor(position, d)]))
-
-
-def field_kernel(amplitude, table, *rest):
+    tables = Stream(table_any, *rest[len(LATE) :], [jnp.bitwise_xor(position, d) for d in LATE])
+    for out in outs:
+        store_parts(out, row_block(window[...], tables.take()))
+
+
+def field_kernel(amplitude, table_any, *rest):
     blocks = rest[:SLABS]
     outs = rest[SLABS : SLABS + PERIOD]
-    field_in, diff = rest[SLABS + PERIOD :]
+    field_in, diff, table, sems = rest[SLABS + PERIOD :]
     position = lax.axis_index("slab")
     parts, rows, _ = blocks[0].shape
     half = parts // 2 * LANES
     width = field_in.shape[0]
     steps = width // LANES
     group = 4
+    tables = Stream(table_any, table, sems, range(steps))
     for d in range(SLABS):
         source = jnp.bitwise_xor(position, d)
         if d in PASSED:
@@ -256,6 +279,8 @@
             else:
                 field_in[where] += blocks[d][part]
     for first in range(0, steps, group):
+        for _ in range(group):
+            tables.take()
         product = dot(
             table[first : first + group].reshape(group * 2 * LANES, width), field_in[...]
         )
@@ -272,7 +297,7 @@
             diff[here, half:] = (field_im * factor).astype(jnp.bfloat16)
     pieces = rows // LANES
     for i in range(PERIOD):
-        first = jnp.bitwise_and(jnp.bitwise_xor(position, i), PERIOD - 1) * pieces
+        first = lax.rem(position + i, PERIOD) * pieces
         product = dot(table[pl.ds(first, pieces)].reshape(pieces * 2 * LANES, width), diff[...])
         for h in range(pieces):
             both = product[h * 2 * LANES : (h + 1) * 2 * LANES]
@@ -285,19 +310,24 @@
                 outs[i][parts // 2 + part, here, :] = back_im[:, cols]
 
 
-def update_columns(first_step, last_step, led_rows, led_cols, table, back, out):
+def update_columns(first_step, last_step, starts, table_any, back, out, table, sems, fill=None):
     position = lax.axis_index("slab")
     led_at = lax.axis_index("led")
     core = jnp.bitwise_and(led_at, 1)
     plane_x = jnp.right_shift(led_at, 1)
-    leds = led_rows.shape[0]
+    leds = starts.shape[0] // 2
     rows = back.shape[0] // (2 * leds)
     width = back.shape[1]
     group = width // LANES // 2
+    blocks = [
+        (1 - core if n < group else core) * group + n % group for n in range(first_step, last_step)
+    ]
+    tables = Stream(table_any, table, sems, blocks)
+    if fill is not None:
+        fill()
     for n in range(first_step, last_step):
-        owner = 1 - core if n < group else core
-        block = owner * group + n % group
-        both = dot(back[...], table[block])
+        block = blocks[n - first_step]
+        both = dot(back[...], tables.take())
         half = leds * rows
         update = (
             both[:half, :LANES] - both[half:, LANES:],
@@ -307,7 +337,7 @@
         high = [0.0, 0.0]
         for led in range(leds):
             inside, wraps = window_mask(
-                position * rows, led_rows[led], led_cols[led], rows, block * LANES, LANES, width
+                position * rows, starts[led], starts[leds + led], rows, block * LANES, LANES, width
             )
             for plane in range(2):
                 piece = jnp.where(inside, update[plane][led * rows : (led + 1) * rows], 0.0)
@@ -319,22 +349,25 @@
             out[plane_x, plane, :, cols] = high[plane].astype(out.dtype)
 
 
-def sent_kernel(led_rows, led_cols, table, *rest):
+def sent_kernel(starts, table_any, *rest):
     blocks = rest[:SLABS]
-    out, back = rest[SLABS:]
+    out, back, table, sems = rest[SLABS:]
     position = lax.axis_index("slab")
     parts, rows, _ = blocks[0].shape
-    for d in range(SLABS):
-        at = pl.multiple_of(jnp.bitwise_xor(position, d) * LANES, LANES)
-        for part in range(parts):
-            back[part * rows : (part + 1) * rows, pl.ds(at, LANES)] = blocks[d][part]
     half = back.shape[1] // LANES // 2
-    update_columns(0, half, led_rows, led_cols, table, back, out)
-
-
-def kept_kernel(led_rows, led_cols, table, back, out):
+
+    def fill():
+        for d in range(SLABS):
+            at = pl.multiple_of(lax.rem(position + SLABS - d, SLABS) * LANES, LANES)
+            for part in range(parts):
+                back[part * rows : (part + 1) * rows, pl.ds(at, LANES)] = blocks[d][part]
+
+    update_columns(0, half, starts, table_any, back, out, table, sems, fill)
+
+
+def kept_kernel(starts, table_any, back, out, table, sems):
     half = back.shape[1] // LANES // 2
-    update_columns(half, 2 * half, led_rows, led_cols, table, back, out)
+    update_columns(half, 2 * half, starts, table_any, back, out, table, sems)
 
 
 def local_call(kernel, out_shape, spaces, scratch, flops, moved, name):
@@ -344,10 +377,17 @@
         in_specs=[pl.BlockSpec(memory_space=space) for space in spaces],
         out_specs=jax.tree.map(lambda _: pl.BlockSpec(memory_space=pltpu.VMEM), out_shape),
         scratch_shapes=scratch,
-        compiler_params=pltpu.CompilerParams(vmem_limit_bytes=32 * 2**20),
+        compiler_params=pltpu.CompilerParams(vmem_limit_bytes=48 * 2**20),
         cost_estimate=pl.CostEstimate(flops=flops, bytes_accessed=moved, transcendentals=0),
         name=name,
     )
+
+
+def table_scratch(table, count):
+    return [
+        pltpu.VMEM((count,) + table.shape[1:], table.dtype),
+        pltpu.SemaphoreType.DMA((count,)),
+    ]
 
 
 def body_slabs(spectrum, led_rows, led_cols, images):
@@ -355,7 +395,7 @@
     rows = spectrum.shape[1]
     led_at = lax.axis_index("led")
     bf16 = jnp.bfloat16
-    vmem, smem, hbm = pltpu.VMEM, pltpu.SMEM, pltpu.HBM
+    vmem, smem = pltpu.VMEM, pltpu.SMEM
     cos_table, sin_table = host_tables(width)
     steps = width // LANES
     by_col = np.stack(
@@ -370,6 +410,7 @@
     sent_block = jax.ShapeDtypeStruct((parts, rows, LANES), bf16)
     flops = 8 * leds * rows * width * width
 
+    starts = jnp.concatenate([led_rows, led_cols]).astype(jnp.int32)
     window, *outs, early = local_call(
         first_kernel,
         [
@@ -377,16 +418,17 @@
             *[sent_block] * len(EARLY),
             jax.ShapeDtypeStruct((len(EARLY),) + sent_block.shape, bf16),
         ],
-        [smem, smem, hbm, hbm],
+        [smem, pl.ANY, pl.ANY],
         [
+            pltpu.VMEM((len(EARLY),) + by_col.shape[1:], bf16),
             pltpu.VMEM(spectrum.shape, jnp.float32),
-            pltpu.VMEM((len(EARLY),) + by_col.shape[1:], bf16),
-            pltpu.SemaphoreType.DMA((4 + len(EARLY),)),
+            pltpu.SemaphoreType.DMA((4,)),
+            pltpu.SemaphoreType.DMA((len(EARLY),)),
         ],
         flops // 4,
         8 * 2**20,
         "windows_and_early_rows",
-    )(led_rows, led_cols, spectrum, by_col)
+    )(starts, spectrum, by_col)
     passed = lax.ppermute(early, "slab", [(s, by) for by, s in PASSED_FROM.items()])
     windowed = range(FIRST + 1, LAST)
     col_blocks = {}
@@ -396,27 +438,31 @@
     row_blocks = local_call(
         second_kernel,
         [sent_block] * len(LATE),
-        [vmem, vmem],
-        [],
+        [vmem, pl.ANY],
+        table_scratch(by_col, len(LATE)),
         3 * flops // 4,
         8 * 2**20,
         "late_rows",
     )(window, by_col)
-    for d, sent in zip(LATE, row_blocks):
-        if d == 0:
-            col_blocks[d] = sent
-        elif d in PASSED:
-            pairs = [(s, s ^ d) for s in range(SLABS)]
-            col_blocks[d] = lax.ppermute(sent + passed[PASSED[d]], "slab", pairs)
-        else:
-            col_blocks[d] = lax.ppermute(sent, "slab", [(s, s ^ d) for s in windowed])
+    passed, col_blocks, *row_blocks = lax.optimization_barrier((passed, col_blocks, *row_blocks))
+    row_blocks = dict(zip(LATE, row_blocks))
+    col_blocks[0] = row_blocks[0]
+    for d in PASSED:
+        pairs = [(s, s ^ d) for s in range(SLABS)]
+        col_blocks[d] = lax.ppermute(row_blocks[d] + passed[PASSED[d]], "slab", pairs)
+    col_blocks[2] = lax.ppermute(row_blocks[2], "slab", [(s, s ^ 2) for s in windowed])
+    col_blocks[2], row_blocks[1], row_blocks[3] = lax.optimization_barrier(
+        (col_blocks[2], row_blocks[1], row_blocks[3])
+    )
+    for d in (1, 3):
+        col_blocks[d] = lax.ppermute(row_blocks[d], "slab", [(s, s ^ d) for s in windowed])
 
     amplitude = jnp.sqrt(images).transpose(2, 0, 1).reshape(width, leds * block)
     back_blocks = local_call(
         field_kernel,
         [sent_block] * PERIOD,
-        [vmem] * (2 + SLABS),
-        [pltpu.VMEM((width, parts * block), bf16)] * 2,
+        [vmem, pl.ANY] + [vmem] * SLABS,
+        [pltpu.VMEM((width, parts * block), bf16)] * 2 + table_scratch(by_row, steps),
         16 * leds * block * width * width,
         12 * 2**20,
         "modulus_step",
@@ -426,7 +472,8 @@
         sent = back_blocks[d % PERIOD]
         if d == 0:
             return sent
-        return lax.ppermute(sent, "slab", [(s, s ^ d) for s in range(SLABS) if s ^ d in windowed])
+        pairs = [(s, (s + d) % SLABS) for s in range(SLABS) if (s + d) % SLABS in windowed]
+        return lax.ppermute(sent, "slab", pairs)
 
     home = [to_rows(d) for d in range(SLABS)]
     share = width // 2
@@ -436,22 +483,22 @@
             jax.ShapeDtypeStruct((2, 2, rows, share), bf16),
             jax.ShapeDtypeStruct((parts * rows, width), bf16),
         ],
-        [smem, smem] + [vmem] * (1 + SLABS),
-        [],
+        [smem, pl.ANY] + [vmem] * SLABS,
+        table_scratch(by_col, steps // 2),
         flops // 2,
         8 * 2**20,
         "update_sent",
-    )(led_rows, led_cols, by_col, *home)
+    )(starts, by_col, *home)
     got = lax.ppermute(sent, "led", [(0, 1), (1, 0), (2, 3), (3, 2)])
     kept = local_call(
         kept_kernel,
         jax.ShapeDtypeStruct((2, 2, rows, share), jnp.float32),
-        [smem, smem, vmem, vmem],
-        [],
+        [smem, pl.ANY, vmem],
+        table_scratch(by_col, steps // 2),
         flops // 2,
         8 * 2**20,
         "update_kept",
-    )(led_rows, led_cols, by_col, back)
+    )(starts, by_col, back)
     over = (kept[0] + got[0].astype(jnp.float32)).astype(bf16)
     got_x = lax.ppermute(over, "led", [(0, 2), (2, 0), (1, 3), (3, 1)])
     own_part = lax.dynamic_slice_in_dim(spectrum, led_at * share, share, 2)

time: 143 us -> 143 us (level)
  the two profiles are of different devices: /device:TPU:4 before, /device:TPU:22 now
where the time goes in v1:
time: 143 us; the launch traced here: 142 us
  starting transfers between devices  58.3 us (41%)
  Pallas kernels  41 us (29%)
  waiting for transfers between devices  32.3 us (23%)
  other arithmetic  6.25 us (4%)
  local copies, waits for them, and re-layouts  3.73 us (3%)
    ppermute x7, starting transfers between devices, to_rows(): return lax.ppermute(sent, 'slab', pairs)  34 us
    ppermute x1, waiting for transfers between devices, body_slabs(): got_x = lax.ppermute(over, 'led', [(0, 2), (2, 0), (1, 3), (3, 1)])  12.6 us
    pallas_call x1, Pallas kernels, body_slabs(): local_call(field_kernel, [sent_block] * PERIOD, [vmem, pl.ANY] + [vmem] *...  10.4 us
    pallas_call x1, Pallas kernels, body_slabs(): local_call(second_kernel, [sent_block] * len(LATE), [vmem, pl.ANY], table...  9.63 us
    ppermute x2, starting transfers between devices, body_slabs(): col_blocks[d] = lax.ppermute(sent, 'slab', pairs)  8.36 us
    ppermute x7, waiting for transfers between devices, to_rows(): return lax.ppermute(sent, 'slab', pairs)  8.17 us
    ppermute x2, starting transfers between devices, body_slabs(): lax.ppermute(row_blocks[d], 'slab', [(s, s ^ d) for s in windowed])  7.94 us
    pallas_call x1, Pallas kernels, body_slabs(): local_call(kept_kernel, jax.ShapeDtypeStruct((2, 2, rows, share), jnp.flo...  7.29 us
  transfers between devices with their start and end apart: 17, of which 5 were waited for; matrix products, arithmetic and copies ran while one was open for 4% of the time, Pallas kernels for 12%

profile of v1, /device:TPU:22, one launch (start us, length us, event | category | flops | bytes accessed | tf_op | source)
XLA Modules:
  0.0 141.8 jit_solution(17630065937946159549)
XLA Ops:
  0.0 0.7 pad_add_fusion.starts
  0.7 6.4 %windows_and_early_rows.1 = (bf16[1024,1024]{1,0:T(8,128)(2,1)S(1)}, bf16[4,256,128]{2,1,0:T(8,128)(2,1)S(1)}, bf16[4,256,128]{2,1,0:T(8,128)(2,1)S(1)}, bf16[2,4,256,128]{3,2,1,0:T(8,128)(2,1)S(1)}) custom-call(s32[4]{0:T(128)S(1)} %pad_add_fusion.starts, f32[2,256,2048]{2,1,0:T(8,128)} %spectrum_any.1, bf16[8,1024,256]{2,1,0:T(8,128)(2,1)} %constant.15.clone.table_any), custom_call_target="tpu_custom_call" | custom-call | flops 1073741824 | bytes 8388608 | tf_op jit(solution)/shard_map/windows_and_early_rows/pallas_call | solution.py:414
  7.2 0.7 collective-permute-start
  7.9 2.8 %collective-permute-start.1 = (bf16[4,256,128]{2,1,0:T(8,128)(2,1)S(1)}, bf16[4,256,128]{2,1,0:T(8,128)(2,1)S(1)}, u32[]{:S(2)}, u32[]{:S(2)}) collective-permute-start(bf16[4,256,128]{2,1,0:T(8,128)(2,1)S(1)} %get-tuple-element.36), channel_id=1, source_target_pairs={{8,28},{12,24},{16,4},{20,0},{9,29},{13,25},{17,5},{21,1},{10,30},... | collective-permute-start | bytes 786440 | tf_op jit(solution)/shard_map/ppermute | solution.py:437
  10.7 5.6 %collective-permute-start.2 = (bf16[4,256,128]{2,1,0:T(8,128)(2,1)S(1)}, bf16[4,256,128]{2,1,0:T(8,128)(2,1)S(1)}, u32[]{:S(2)}, u32[]{:S(2)}) collective-permute-start(bf16[4,256,128]{2,1,0:T(8,128)(2,1)S(1)} %get-tuple-element.37), channel_id=1, source_target_pairs={{8,20},{12,16},{16,12},{20,8},{9,21},{13,17},{17,13},{21,9},{10,22... | collective-permute-start | bytes 786440 | tf_op jit(solution)/shard_map/ppermute | solution.py:437
  16.2 9.6 %late_rows.1 = (bf16[4,256,128]{2,1,0:T(8,128)(2,1)S(1)}, bf16[4,256,128]{2,1,0:T(8,128)(2,1)S(1)}, bf16[4,256,128]{2,1,0:T(8,128)(2,1)S(1)}, bf16[4,256,128]{2,...) custom-call(bf16[1024,1024]{1,0:T(8,128)(2,1)S(1)} %get-tuple-element.38.window, ...), custom_call_target="tpu_custom_call" | custom-call | flops 3221225472 | bytes 8388608 | tf_op jit(solution)/shard_map/late_rows/pallas_call | solution.py:438
  25.9 0.0 copy-start.2
  25.9 0.0 collective-permute-done.1.rest_5_
  25.9 0.0 collective-permute-done.2.rest_7_
  25.9 0.0 collective-permute-done
  25.9 5.9 %collective-permute-start.3 = (bf16[4,256,128]{2,1,0:T(8,128)(2,1)S(1)}, bf16[4,256,128]{2,1,0:T(8,128)(2,1)S(1)}, u32[]{:S(2)}, u32[]{:S(2)}) collective-permute-start(bf16[4,256,128]{2,1,0:T(8,128)(2,1)S(1)} %get-tuple-element.46), channel_id=1, source_target_pairs={{4,12},{8,0},{12,4},{16,24},{20,28},{24,16},{5,13},{9,1},{13,5},{1... | collective-permute-start | bytes 786440 | tf_op jit(solution)/shard_map/ppermute | solution.py:453
  31.8 0.9 bitcast_add_fusion
  32.7 0.0 collective-permute-start.6
  32.7 0.8 collective-permute-start.7
  33.5 5.9 %collective-permute-done.3.rest_2_ = bf16[4,256,128]{2,1,0:T(8,128)(2,1)S(1)} collective-permute-done((bf16[4,256,128]{2,1,0:T(8,128)(2,1)S(1)}, bf16[4,256,128]{2,1,0:T(8,128)(2,1)S(1)}, u32[]{:S(2)}, u32[]{:S(2)}) %collective-permute-start.3) | collective-permute-done | bytes 262176 | tf_op jit(solution)/shard_map/ppermute | solution.py:453
  39.4 2.4 %collective-permute-start.4 = (bf16[4,256,128]{2,1,0:T(8,128)(2,1)S(1)}, bf16[4,256,128]{2,1,0:T(8,128)(2,1)S(1)}, u32[]{:S(2)}, u32[]{:S(2)}) collective-permute-start(bf16[4,256,128]{2,1,0:T(8,128)(2,1)S(1)} %get-tuple-element.49), channel_id=1, source_target_pairs={{4,0},{8,12},{12,8},{16,20},{20,16},{24,28},{5,1},{9,13},{13,9},{1... | collective-permute-start | bytes 786440 | tf_op jit(solution)/shard_map/ppermute | solution.py:458
  41.8 5.6 %collective-permute-start.5 = (bf16[4,256,128]{2,1,0:T(8,128)(2,1)S(1)}, bf16[4,256,128]{2,1,0:T(8,128)(2,1)S(1)}, u32[]{:S(2)}, u32[]{:S(2)}) collective-permute-start(bf16[4,256,128]{2,1,0:T(8,128)(2,1)S(1)} %get-tuple-element.51), channel_id=1, source_target_pairs={{4,8},{8,4},{12,0},{16,28},{20,24},{24,20},{5,9},{9,5},{13,1},{17,... | collective-permute-start | bytes 786440 | tf_op jit(solution)/shard_map/ppermute | solution.py:458
  47.4 1.2 sqrt.3
  48.6 1.6 %copy.8.amplitude = f32[1024,256]{1,0:T(8,128)S(1)} copy(f32[1024,256]{0,1:T(8,128)} %bitcast.13) | data formatting | bytes 2097152 | tf_op jit(solution)/shard_map/reshape | solution.py:460
  50.1 0.0 collective-permute-done.6.rest_4_
  50.1 5.6 %collective-permute-done.7.rest_6_ = bf16[4,256,128]{2,1,0:T(8,128)(2,1)S(1)} collective-permute-done((bf16[4,256,128]{2,1,0:T(8,128)(2,1)}, bf16[4,256,128]{2,1,0:T(8,128)(2,1)S(1)}, u32[]{:S(2)}, u32[]{:S(2)}) %collective-permute-start.7) | collective-permute-done | bytes 262176 | tf_op jit(solution)/shard_map/ppermute | solution.py:452
  55.8 0.0 collective-permute-done.4.rest_1_
  55.8 0.0 collective-permute-done.5.rest_3_
  55.8 0.9 copy-done.1
  56.7 10.4 %modulus_step.1 = (bf16[4,256,128]{2,1,0:T(8,128)(2,1)S(1)}, bf16[4,256,128]{2,1,0:T(8,128)(2,1)S(1)}, bf16[4,256,128]{2,1,0:T(8,128)(2,1)S(1)}, bf16[4,256,128]{2,1,0:T(8,128)(2,1)S(1)}) custom-call(f32[1024,256]{1,0:T(8,128)S(1)} %copy.8.amplitude, bf16[8,256,1024]{2,1,0:T(8,128)(2,1)} %constant.14.clone.table_any, bf16[4,256,128]{2,1,0:T(8,128)(2,1)S(1)} %copy-done.1, ...), custom_call_target="tpu_custom_call" | custom-call | flops 4294967296 | bytes 12582912 | tf_op jit(solution)/shard_map/modulus_step/pallas_call | solution.py:461
  67.1 1.3 collective-permute-start.10
  68.4 6.1 %collective-permute-start.11 = (bf16[4,256,128]{2,1,0:T(8,128)(2,1)S(1)}, bf16[4,256,128]{2,1,0:T(8,128)(2,1)S(1)}, u32[]{:S(2)}, u32[]{:S(2)}) collective-permute-start(bf16[4,256,128]{2,1,0:T(8,128)(2,1)S(1)} %get-tuple-element.57.rest_0_), channel_id=1, source_target_pairs={{0,16},{4,20},{8,24},{20,4},{24,8},{28,12},{1,17},{5,21},{9,25},{2... | collective-permute-start | bytes 786440 | tf_op jit(solution)/shard_map/ppermute | solution.py:476
  74.6 1.9 %collective-permute-start.14 = (bf16[4,256,128]{2,1,0:T(8,128)(2,1)S(1)}, bf16[4,256,128]{2,1,0:T(8,128)(2,1)S(1)}, u32[]{:S(2)}, u32[]{:S(2)}) collective-permute-start(bf16[4,256,128]{2,1,0:T(8,128)(2,1)S(1)} %get-tuple-element.60), channel_id=1, source_target_pairs={{8,4},{12,8},{16,12},{20,16},{24,20},{28,24},{9,5},{13,9},{17,13},... | collective-permute-start | bytes 786440 | tf_op jit(solution)/shard_map/ppermute | solution.py:476
  76.5 4.0 %collective-permute-start.12 = (bf16[4,256,128]{2,1,0:T(8,128)(2,1)S(1)}, bf16[4,256,128]{2,1,0:T(8,128)(2,1)S(1)}, u32[]{:S(2)}, u32[]{:S(2)}) collective-permute-start(bf16[4,256,128]{2,1,0:T(8,128)(2,1)S(1)} %get-tuple-element.58), channel_id=1, source_target_pairs={{0,20},{4,24},{16,4},{20,8},{24,12},{28,16},{1,21},{5,25},{17,5},{... | collective-permute-start | bytes 786440 | tf_op jit(solution)/shard_map/ppermute | solution.py:476
  80.5 1.9 %collective-permute-start.13 = (bf16[4,256,128]{2,1,0:T(8,128)(2,1)S(1)}, bf16[4,256,128]{2,1,0:T(8,128)(2,1)S(1)}, u32[]{:S(2)}, u32[]{:S(2)}) collective-permute-start(bf16[4,256,128]{2,1,0:T(8,128)(2,1)S(1)} %get-tuple-element.59), channel_id=1, source_target_pairs={{0,24},{12,4},{16,8},{20,12},{24,16},{28,20},{1,25},{13,5},{17,9},... | collective-permute-start | bytes 786440 | tf_op jit(solution)/shard_map/ppermute | solution.py:476
  82.4 0.0 collective-permute-done.10.rest_3_
  82.4 17.3 %collective-permute-start.8 = (bf16[4,256,128]{2,1,0:T(8,128)(2,1)S(1)}, bf16[4,256,128]{2,1,0:T(8,128)(2,1)S(1)}, u32[]{:S(2)}, u32[]{:S(2)}) collective-permute-start(bf16[4,256,128]{2,1,0:T(8,128)(2,1)S(1)} %get-tuple-element.58), channel_id=1, source_target_pairs={{0,4},{4,8},{8,12},{12,16},{16,20},{20,24},{1,5},{5,9},{9,13},{13,... | collective-permute-start | bytes 786440 | tf_op jit(solution)/shard_map/ppermute | solution.py:476
  99.7 0.0 collective-permute-done.11.rest_4_
  99.7 1.5 %collective-permute-start.9 = (bf16[4,256,128]{2,1,0:T(8,128)(2,1)S(1)}, bf16[4,256,128]{2,1,0:T(8,128)(2,1)S(1)}, u32[]{:S(2)}, u32[]{:S(2)}) collective-permute-start(bf16[4,256,128]{2,1,0:T(8,128)(2,1)S(1)} %get-tuple-element.59), channel_id=1, source_target_pairs={{0,8},{4,12},{8,16},{12,20},{16,24},{28,4},{1,9},{5,13},{9,17},{13... | collective-permute-start | bytes 786440 | tf_op jit(solution)/shard_map/ppermute | solution.py:476
  101.2 0.0 collective-permute-done.12.rest_5_
  101.2 5.2 %collective-permute-done.13.rest_6_ = bf16[4,256,128]{2,1,0:T(8,128)(2,1)S(1)} collective-permute-done((bf16[4,256,128]{2,1,0:T(8,128)(2,1)S(1)}, bf16[4,256,128]{2,1,0:T(8,128)(2,1)S(1)}, u32[]{:S(2)}, u32[]{:S(2)}) %collective-permute-start.13) | collective-permute-done | bytes 262176 | tf_op jit(solution)/shard_map/ppermute | solution.py:476
  106.4 0.0 collective-permute-done.14.rest_7_
  106.4 0.0 collective-permute-done.8.rest_1_
  106.5 2.9 %collective-permute-done.9.rest_2_ = bf16[4,256,128]{2,1,0:T(8,128)(2,1)S(1)} collective-permute-done((bf16[4,256,128]{2,1,0:T(8,128)(2,1)S(1)}, bf16[4,256,128]{2,1,0:T(8,128)(2,1)S(1)}, u32[]{:S(2)}, u32[]{:S(2)}) %collective-permute-start.9) | collective-permute-done | bytes 262176 | tf_op jit(solution)/shard_map/ppermute | solution.py:476
  109.4 7.3 %update_sent.1 = (bf16[2,2,256,512]{3,2,1,0:T(8,128)(2,1)S(1)}, bf16[1024,1024]{1,0:T(8,128)(2,1)S(1)}) custom-call(s32[4]{0:T(128)S(1)} %pad_add_fusion.starts, bf16[8,1024,256]{2,1,0:T(8,128)(2,1)} %constant.15.clone.table_any, bf16[4,256,128]{2,1,0:T(8,128)(2,1)S(1)} %get-tuple-element.57.rest_0_, ...), custom_call_target="tpu_custom_call" | custom-call | flops 2147483648 | bytes 8388608 | tf_op jit(solution)/shard_map/update_sent/pallas_call | solution.py:480
  116.7 0.1 collective-permute-start.15
  116.8 7.3 %update_kept.1 = f32[2,2,256,512]{3,2,1,0:T(8,128)S(1)} custom-call(s32[4]{0:T(128)S(1)} %pad_add_fusion.starts, bf16[8,1024,256]{2,1,0:T(8,128)(2,1)} %constant.15.clone.table_any, bf16[1024,1024]{1,0:T(8,128)(2,1)S(1)} %get-tuple-element.61.back), custom_call_target="tpu_custom_call" | custom-call | flops 2147483648 | bytes 8388608 | tf_op jit(solution)/shard_map/update_kept/pallas_call | solution.py:493
  124.1 0.0 collective-permute-done.15
  124.1 1.0 fusion.3
  125.0 0.5 collective-permute-start.16
  125.5 1.5 %fusion.2 = f32[2,256,512]{2,1,0:T(8,128)S(1)} fusion(f32[2,2,256,512]{3,2,1,0:T(8,128)S(1)} %update_kept.1, f32[2,256,2048]{2,1,0:T(8,128)} %spectrum_any.1, s32[]{:T(128)S(6)} %select_n.3, bf16[2,2,256,512]{3,2,1,0:T(8,128)(2,1)S(1)} %collective-permute-done.15), kind=kLoop, calls=%fused_computation.4 | loop fusion | flops 786432 | bytes 3670020 | tf_op jit(solution)/shard_map/add | solution.py:505
  127.1 12.6 %collective-permute-done.16 = bf16[2,256,512]{2,1,0:T(8,128)(2,1)} collective-permute-done((bf16[2,256,512]{2,1,0:T(8,128)(2,1)}, bf16[2,256,512]{2,1,0:T(8,128)(2,1)}, u32[]{:S(2)}, u32[]{:S(2)}) %collective-permute-start.16) | collective-permute-done | bytes 524320 | tf_op jit(solution)/shard_map/ppermute | solution.py:503
  139.7 2.2 %convert_add_fusion = f32[2,256,512]{2,1,0:T(8,128)} fusion(f32[2,256,512]{2,1,0:T(8,128)S(1)} %fusion.2, bf16[2,256,512]{2,1,0:T(8,128)(2,1)} %collective-permute-done.16), kind=kLoop, calls=%fused_computation.5 | loop fusion | flops 524288 | bytes 2621440 | tf_op jit(solution)/shard_map/add | solution.py:507
  (4 shorter events, 0.0 us)
Async XLA Ops:
  7.2 18.8 %collective-permute-start = (bf16[2,4,256,128]{3,2,1,0:T(8,128)(2,1)S(1)}, bf16[2,4,256,128]{3,2,1,0:T(8,128)(2,1)S(1)}, u32[]{:S(2)}, u32[]{:S(2)}) collective-permute-start(bf16[2,4,256,128]{3,2,1,0:T(8,128)(2,1)S(1)} %get-tuple-element.35), channel_id=1, source_target_pairs={{4,0},{24,28},{5,1},{25,29},{6,2},{26,30},{7,3},{27,31}} | collective-permute-start | bytes 1572872 | tf_op jit(solution)/shard_map/ppermute | solution.py:432
  7.9 18.0 %collective-permute-start.1 = (bf16[4,256,128]{2,1,0:T(8,128)(2,1)S(1)}, bf16[4,256,128]{2,1,0:T(8,128)(2,1)S(1)}, u32[]{:S(2)}, u32[]{:S(2)}) collective-permute-start(bf16[4,256,128]{2,1,0:T(8,128)(2,1)S(1)} %get-tuple-element.36), channel_id=1, source_target_pairs={{8,28},{12,24},{16,4},{20,0},{9,29},{13,25},{17,5},{21,1},{10,30},... | collective-permute-start | bytes 786440 | tf_op jit(solution)/shard_map/ppermute | solution.py:437
  10.7 15.3 %collective-permute-start.2 = (bf16[4,256,128]{2,1,0:T(8,128)(2,1)S(1)}, bf16[4,256,128]{2,1,0:T(8,128)(2,1)S(1)}, u32[]{:S(2)}, u32[]{:S(2)}) collective-permute-start(bf16[4,256,128]{2,1,0:T(8,128)(2,1)S(1)} %get-tuple-element.37), channel_id=1, source_target_pairs={{8,20},{12,16},{16,12},{20,8},{9,21},{13,17},{17,13},{21,9},{10,22... | collective-permute-start | bytes 786440 | tf_op jit(solution)/shard_map/ppermute | solution.py:437
  25.9 22.7 %copy-start = (bf16[4,256,128]{2,1,0:T(8,128)(2,1)}, bf16[4,256,128]{2,1,0:T(8,128)(2,1)S(1)}, u32[]{:S(2)}) copy-start(bf16[4,256,128]{2,1,0:T(8,128)(2,1)S(1)} %get-tuple-element.45.rest_0_) | copy-start | bytes 786436
  25.9 21.5 %copy-start.2 = (f32[2,128,1024]{2,1,0:T(8,128)S(1)}, f32[2,128,1024]{2,1,0:T(8,128)}, u32[]{:S(2)}) copy-start(f32[2,128,1024]{2,1,0:T(8,128)} %param.9) | copy-start | bytes 3145732
  25.9 13.5 %collective-permute-start.3 = (bf16[4,256,128]{2,1,0:T(8,128)(2,1)S(1)}, bf16[4,256,128]{2,1,0:T(8,128)(2,1)S(1)}, u32[]{:S(2)}, u32[]{:S(2)}) collective-permute-start(bf16[4,256,128]{2,1,0:T(8,128)(2,1)S(1)} %get-tuple-element.46), channel_id=1, source_target_pairs={{4,12},{8,0},{12,4},{16,24},{20,28},{24,16},{5,13},{9,1},{13,5},{1... | collective-permute-start | bytes 786440 | tf_op jit(solution)/shard_map/ppermute | solution.py:453
  32.7 17.4 %collective-permute-start.6 = (bf16[4,256,128]{2,1,0:T(8,128)(2,1)}, bf16[4,256,128]{2,1,0:T(8,128)(2,1)S(1)}, u32[]{:S(2)}, u32[]{:S(2)}) collective-permute-start(bf16[4,256,128]{2,1,0:T(8,128)(2,1)} %get-tuple-element.66), channel_id=1, source_target_pairs={{0,16},{4,20},{8,24},{12,28},{16,0},{20,4},{24,8},{28,12},{1,17},{... | collective-permute-start | bytes 786440 | tf_op jit(solution)/shard_map/ppermute | solution.py:452
  32.7 23.1 %collective-permute-start.7 = (bf16[4,256,128]{2,1,0:T(8,128)(2,1)}, bf16[4,256,128]{2,1,0:T(8,128)(2,1)S(1)}, u32[]{:S(2)}, u32[]{:S(2)}) collective-permute-start(bf16[4,256,128]{2,1,0:T(8,128)(2,1)} %get-tuple-element.65), channel_id=1, source_target_pairs={{0,24},{4,28},{8,16},{12,20},{16,8},{20,12},{24,0},{28,4},{1,25},{... | collective-permute-start | bytes 786440 | tf_op jit(solution)/shard_map/ppermute | solution.py:452
  39.4 16.4 %collective-permute-start.4 = (bf16[4,256,128]{2,1,0:T(8,128)(2,1)S(1)}, bf16[4,256,128]{2,1,0:T(8,128)(2,1)S(1)}, u32[]{:S(2)}, u32[]{:S(2)}) collective-permute-start(bf16[4,256,128]{2,1,0:T(8,128)(2,1)S(1)} %get-tuple-element.49), channel_id=1, source_target_pairs={{4,0},{8,12},{12,8},{16,20},{20,16},{24,28},{5,1},{9,13},{13,9},{1... | collective-permute-start | bytes 786440 | tf_op jit(solution)/shard_map/ppermute | solution.py:458
  41.8 14.0 %collective-permute-start.5 = (bf16[4,256,128]{2,1,0:T(8,128)(2,1)S(1)}, bf16[4,256,128]{2,1,0:T(8,128)(2,1)S(1)}, u32[]{:S(2)}, u32[]{:S(2)}) collective-permute-start(bf16[4,256,128]{2,1,0:T(8,128)(2,1)S(1)} %get-tuple-element.51), channel_id=1, source_target_pairs={{4,8},{8,4},{12,0},{16,28},{20,24},{24,20},{5,9},{9,5},{13,1},{17,... | collective-permute-start | bytes 786440 | tf_op jit(solution)/shard_map/ppermute | solution.py:458
  55.8 1.0 copy-start.1
  67.1 15.3 %collective-permute-start.10 = (bf16[4,256,128]{2,1,0:T(8,128)(2,1)S(1)}, bf16[4,256,128]{2,1,0:T(8,128)(2,1)S(1)}, u32[]{:S(2)}, u32[]{:S(2)}) collective-permute-start(bf16[4,256,128]{2,1,0:T(8,128)(2,1)S(1)} %get-tuple-element.60), channel_id=1, source_target_pairs={{0,12},{4,16},{8,20},{12,24},{24,4},{28,8},{1,13},{5,17},{9,21},{1... | collective-permute-start | bytes 786440 | tf_op jit(solution)/shard_map/ppermute | solution.py:476
  68.4 31.2 %collective-permute-start.11 = (bf16[4,256,128]{2,1,0:T(8,128)(2,1)S(1)}, bf16[4,256,128]{2,1,0:T(8,128)(2,1)S(1)}, u32[]{:S(2)}, u32[]{:S(2)}) collective-permute-start(bf16[4,256,128]{2,1,0:T(8,128)(2,1)S(1)} %get-tuple-element.57.rest_0_), channel_id=1, source_target_pairs={{0,16},{4,20},{8,24},{20,4},{24,8},{28,12},{1,17},{5,21},{9,25},{2... | collective-permute-start | bytes 786440 | tf_op jit(solution)/shard_map/ppermute | solution.py:476
  74.6 31.9 %collective-permute-start.14 = (bf16[4,256,128]{2,1,0:T(8,128)(2,1)S(1)}, bf16[4,256,128]{2,1,0:T(8,128)(2,1)S(1)}, u32[]{:S(2)}, u32[]{:S(2)}) collective-permute-start(bf16[4,256,128]{2,1,0:T(8,128)(2,1)S(1)} %get-tuple-element.60), channel_id=1, source_target_pairs={{8,4},{12,8},{16,12},{20,16},{24,20},{28,24},{9,5},{13,9},{17,13},... | collective-permute-start | bytes 786440 | tf_op jit(solution)/shard_map/ppermute | solution.py:476
  76.5 24.7 %collective-permute-start.12 = (bf16[4,256,128]{2,1,0:T(8,128)(2,1)S(1)}, bf16[4,256,128]{2,1,0:T(8,128)(2,1)S(1)}, u32[]{:S(2)}, u32[]{:S(2)}) collective-permute-start(bf16[4,256,128]{2,1,0:T(8,128)(2,1)S(1)} %get-tuple-element.58), channel_id=1, source_target_pairs={{0,20},{4,24},{16,4},{20,8},{24,12},{28,16},{1,21},{5,25},{17,5},{... | collective-permute-start | bytes 786440 | tf_op jit(solution)/shard_map/ppermute | solution.py:476
  80.5 26.0 %collective-permute-start.13 = (bf16[4,256,128]{2,1,0:T(8,128)(2,1)S(1)}, bf16[4,256,128]{2,1,0:T(8,128)(2,1)S(1)}, u32[]{:S(2)}, u32[]{:S(2)}) collective-permute-start(bf16[4,256,128]{2,1,0:T(8,128)(2,1)S(1)} %get-tuple-element.59), channel_id=1, source_target_pairs={{0,24},{12,4},{16,8},{20,12},{24,16},{28,20},{1,25},{13,5},{17,9},... | collective-permute-start | bytes 786440 | tf_op jit(solution)/shard_map/ppermute | solution.py:476
  82.4 24.0 %collective-permute-start.8 = (bf16[4,256,128]{2,1,0:T(8,128)(2,1)S(1)}, bf16[4,256,128]{2,1,0:T(8,128)(2,1)S(1)}, u32[]{:S(2)}, u32[]{:S(2)}) collective-permute-start(bf16[4,256,128]{2,1,0:T(8,128)(2,1)S(1)} %get-tuple-element.58), channel_id=1, source_target_pairs={{0,4},{4,8},{8,12},{12,16},{16,20},{20,24},{1,5},{5,9},{9,13},{13,... | collective-permute-start | bytes 786440 | tf_op jit(solution)/shard_map/ppermute | solution.py:476
  99.7 9.7 %collective-permute-start.9 = (bf16[4,256,128]{2,1,0:T(8,128)(2,1)S(1)}, bf16[4,256,128]{2,1,0:T(8,128)(2,1)S(1)}, u32[]{:S(2)}, u32[]{:S(2)}) collective-permute-start(bf16[4,256,128]{2,1,0:T(8,128)(2,1)S(1)} %get-tuple-element.59), channel_id=1, source_target_pairs={{0,8},{4,12},{8,16},{12,20},{16,24},{28,4},{1,9},{5,13},{9,17},{13... | collective-permute-start | bytes 786440 | tf_op jit(solution)/shard_map/ppermute | solution.py:476
  116.7 7.4 %collective-permute-start.15 = (bf16[2,2,256,512]{3,2,1,0:T(8,128)(2,1)S(1)}, bf16[2,2,256,512]{3,2,1,0:T(8,128)(2,1)S(1)}, u32[]{:S(2)}, u32[]{:S(2)}) collective-permute-start(bf16[2,2,256,512]{3,2,1,0:T(8,128)(2,1)S(1)} %get-tuple-element.62), channel_id=1, source_target_pairs={{0,1},{1,0},{2,3},{3,2},{4,5},{5,4},{6,7},{7,6},{8,9},{9,8},{10,11... | collective-permute-start | bytes 3145736 | tf_op jit(solution)/shard_map/ppermute | solution.py:492
  125.0 14.6 %collective-permute-start.16 = (bf16[2,256,512]{2,1,0:T(8,128)(2,1)}, bf16[2,256,512]{2,1,0:T(8,128)(2,1)}, u32[]{:S(2)}, u32[]{:S(2)}) collective-permute-start(bf16[2,256,512]{2,1,0:T(8,128)(2,1)} %fusion.3), channel_id=1, source_target_pairs={{0,2},{2,0},{1,3},{3,1},{4,6},{6,4},{5,7},{7,5},{8,10},{10,8},{9,1... | collective-permute-start | bytes 1572872 | tf_op jit(solution)/shard_map/ppermute | solution.py:503

commit v2 on v1

--- a/solution.py
+++ b/solution.py
@@ -143,36 +143,37 @@
 
 
 SLABS = 8
-PERIOD = 4
+HALF = 4
 FIRST, LAST = 0, 7
-EARLY = (5, 7)
-LATE = (0, 1, 2, 3, 4, 6)
-PASSED = {4: 0, 6: 1}
-PASSED_FROM = {FIRST: 1, LAST: 6}
+CROSS = (4, 5, 6, 7)
+LATE = (5, 7)
+PASSED = {1: 0, 6: 7}
+PIECES = 4
 
 
 class Stream:
     def __init__(self, source, target, sems, blocks):
         self.target = target
+        step = source.shape[1] // PIECES
         self.copies = [
-            pltpu.make_async_copy(source.at[block], target.at[i], sems.at[i])
+            [
+                pltpu.make_async_copy(
+                    source.at[block, pl.ds(piece * step, step)],
+                    target.at[i, pl.ds(piece * step, step)],
+                    sems.at[i, piece],
+                )
+                for piece in range(PIECES)
+            ]
             for i, block in enumerate(blocks)
         ]
-        self.started = 0
-        self.taken = 0
-        self.start()
-        self.start()
-
-    def start(self):
-        if self.started < len(self.copies):
-            self.copies[self.started].start()
-            self.started += 1
-
-    def take(self):
-        self.copies[self.taken].wait()
-        self.start()
-        self.taken += 1
-        return self.target[self.taken - 1]
+        for copies in self.copies:
+            for copy in copies:
+                copy.start()
+
+    def take(self, i):
+        for copy in self.copies[i]:
+            copy.wait()
+        return self.target[i]
 
 
 def dot(left, right):
@@ -207,29 +208,34 @@
 
 
 def first_kernel(starts, spectrum_any, table_any, window, *rest):
-    outs = rest[: len(EARLY)]
-    early, table, spectrum, sems, table_sems = rest[len(EARLY) :]
+    outs = rest[: len(CROSS)]
+    late, spectrum, sems, table, table_sems = rest[len(CROSS) :]
     position = lax.axis_index("slab")
     leds = starts.shape[0] // 2
     rows = spectrum.shape[1]
     width = window.shape[1]
-    chunks = 4
+    chunks = sems.shape[0]
     step = rows // chunks
     fetches = [
-        pltpu.make_async_copy(
-            spectrum_any.at[:, pl.ds(i * step, step)],
-            spectrum.at[:, pl.ds(i * step, step)],
-            sems.at[i],
-        )
+        [
+            pltpu.make_async_copy(
+                spectrum_any.at[plane, pl.ds(i * step, step)],
+                spectrum.at[plane, pl.ds(i * step, step)],
+                sems.at[i, plane],
+            )
+            for plane in range(2)
+        ]
         for i in range(chunks)
     ]
-    for copy in fetches:
-        copy.start()
+    for pair in fetches:
+        for copy in pair:
+            copy.start()
+    tables = Stream(
+        table_any, table, table_sems, [jnp.bitwise_xor(position, d) for d in CROSS]
+    )
     for i in range(chunks):
-        fetches[i].wait()
-        if i == chunks - 1:
-            blocks = [jnp.bitwise_xor(position, d) for d in EARLY]
-            tables = Stream(table_any, table, table_sems, blocks)
+        for copy in fetches[i]:
+            copy.wait()
         here = slice(i * step, (i + 1) * step)
         for led in range(leds):
             inside, wraps = window_mask(
@@ -241,46 +247,46 @@
                 )
                 at = (plane * leds + led) * rows + i * step
                 window[at : at + step, :] = jnp.where(inside, value, 0.0).astype(jnp.bfloat16)
-    for i in range(len(EARLY)):
-        values = row_block(window[...], tables.take())
+    for i, d in enumerate(CROSS):
+        values = row_block(window[...], tables.take(i))
         store_parts(outs[i], values)
-        store_parts(early.at[i], values)
-
-
-def second_kernel(window, table_any, *rest):
-    outs = rest[: len(LATE)]
+        if d in LATE:
+            store_parts(late.at[LATE.index(d)], values)
+
+
+def second_kernel(window, table_any, out, table, sems):
     position = lax.axis_index("slab")
-    tables = Stream(table_any, *rest[len(LATE) :], [jnp.bitwise_xor(position, d) for d in LATE])
-    for out in outs:
-        store_parts(out, row_block(window[...], tables.take()))
-
-
-def field_kernel(amplitude, table_any, *rest):
-    blocks = rest[:SLABS]
-    outs = rest[SLABS : SLABS + PERIOD]
-    field_in, diff, table, sems = rest[SLABS + PERIOD :]
+    base = position - jnp.bitwise_and(position, HALF - 1)
+    tables = Stream(table_any, table, sems, [base + i for i in range(HALF)])
+    for i in range(HALF):
+        store_parts(out.at[i], row_block(window[...], tables.take(i)))
+
+
+def field_kernel(amplitude, table_any, near, *rest):
+    far = rest[: len(CROSS)]
+    near_out = rest[len(CROSS)]
+    far_out = rest[len(CROSS) + 1 : 2 * len(CROSS) + 1]
+    field_in, diff, table, sems = rest[2 * len(CROSS) + 1 :]
     position = lax.axis_index("slab")
-    parts, rows, _ = blocks[0].shape
+    _, parts, rows, _ = near.shape
     half = parts // 2 * LANES
     width = field_in.shape[0]
     steps = width // LANES
     group = 4
     tables = Stream(table_any, table, sems, range(steps))
-    for d in range(SLABS):
-        source = jnp.bitwise_xor(position, d)
-        if d in PASSED:
-            for by, origin in PASSED_FROM.items():
-                source = jnp.where(source == by, origin, source)
-        at = pl.multiple_of(jnp.bitwise_and(source, PERIOD - 1) * rows, rows)
+    for i in range(HALF):
         for part in range(parts):
-            where = (pl.ds(at, rows), slice(part * LANES, (part + 1) * LANES))
-            if d < PERIOD:
-                field_in[where] = blocks[d][part]
-            else:
-                field_in[where] += blocks[d][part]
+            cols = slice(part * LANES, (part + 1) * LANES)
+            field_in[i * rows : (i + 1) * rows, cols] = near[i, part]
+    for d, block in zip(CROSS, far):
+        source = jnp.bitwise_and(jnp.bitwise_xor(position, d), HALF - 1)
+        at = pl.multiple_of(source * rows, rows)
+        for part in range(parts):
+            cols = slice(part * LANES, (part + 1) * LANES)
+            field_in[pl.ds(at, rows), cols] += block[part]
     for first in range(0, steps, group):
-        for _ in range(group):
-            tables.take()
+        for j in range(first, first + group):
+            tables.take(j)
         product = dot(
             table[first : first + group].reshape(group * 2 * LANES, width), field_in[...]
         )
@@ -296,9 +302,10 @@
             diff[here, :half] = (field_re * factor).astype(jnp.bfloat16)
             diff[here, half:] = (field_im * factor).astype(jnp.bfloat16)
     pieces = rows // LANES
-    for i in range(PERIOD):
-        first = lax.rem(position + i, PERIOD) * pieces
-        product = dot(table[pl.ds(first, pieces)].reshape(pieces * 2 * LANES, width), diff[...])
+    for i in range(HALF):
+        product = dot(
+            table[i * pieces : (i + 1) * pieces].reshape(pieces * 2 * LANES, width), diff[...]
+        )
         for h in range(pieces):
             both = product[h * 2 * LANES : (h + 1) * 2 * LANES]
             here = pl.ds(h * LANES, LANES)
@@ -306,8 +313,10 @@
             back_im = (both[:LANES, half:] + both[LANES:, :half]).astype(jnp.bfloat16)
             for part in range(parts // 2):
                 cols = slice(part * LANES, (part + 1) * LANES)
-                outs[i][part, here, :] = back_re[:, cols]
-                outs[i][parts // 2 + part, here, :] = back_im[:, cols]
+                near_out[i, part, here, :] = back_re[:, cols]
+                near_out[i, parts // 2 + part, here, :] = back_im[:, cols]
+    for d, out in zip(CROSS, far_out):
+        out[...] = near_out[jnp.bitwise_and(jnp.bitwise_xor(position, d), HALF - 1)]
 
 
 def update_columns(first_step, last_step, starts, table_any, back, out, table, sems, fill=None):
@@ -327,7 +336,7 @@
         fill()
     for n in range(first_step, last_step):
         block = blocks[n - first_step]
-        both = dot(back[...], tables.take())
+        both = dot(back[...], tables.take(n - first_step))
         half = leds * rows
         update = (
             both[:half, :LANES] - both[half:, LANES:],
@@ -349,18 +358,23 @@
             out[plane_x, plane, :, cols] = high[plane].astype(out.dtype)
 
 
-def sent_kernel(starts, table_any, *rest):
-    blocks = rest[:SLABS]
-    out, back, table, sems = rest[SLABS:]
+def sent_kernel(starts, table_any, near, *rest):
+    far = rest[: len(CROSS)]
+    out, back, table, sems = rest[len(CROSS) :]
     position = lax.axis_index("slab")
-    parts, rows, _ = blocks[0].shape
+    base = position - jnp.bitwise_and(position, HALF - 1)
+    _, parts, rows, _ = near.shape
     half = back.shape[1] // LANES // 2
 
     def fill():
-        for d in range(SLABS):
-            at = pl.multiple_of(lax.rem(position + SLABS - d, SLABS) * LANES, LANES)
+        for i in range(HALF):
+            at = pl.multiple_of((base + i) * LANES, LANES)
             for part in range(parts):
-                back[part * rows : (part + 1) * rows, pl.ds(at, LANES)] = blocks[d][part]
+                back[part * rows : (part + 1) * rows, pl.ds(at, LANES)] = near[i, part]
+        for d, block in zip(CROSS, far):
+            at = pl.multiple_of(jnp.bitwise_xor(position, d) * LANES, LANES)
+            for part in range(parts):
+                back[part * rows : (part + 1) * rows, pl.ds(at, LANES)] = block[part]
 
     update_columns(0, half, starts, table_any, back, out, table, sems, fill)
 
@@ -386,7 +400,7 @@
 def table_scratch(table, count):
     return [
         pltpu.VMEM((count,) + table.shape[1:], table.dtype),
-        pltpu.SemaphoreType.DMA((count,)),
+        pltpu.SemaphoreType.DMA((count, PIECES)),
     ]
 
 
@@ -408,74 +422,67 @@
     by_col = jnp.asarray(by_col)
     parts = 2 * leds
     sent_block = jax.ShapeDtypeStruct((parts, rows, LANES), bf16)
+    near_block = jax.ShapeDtypeStruct((HALF,) + sent_block.shape, bf16)
     flops = 8 * leds * rows * width * width
 
     starts = jnp.concatenate([led_rows, led_cols]).astype(jnp.int32)
-    window, *outs, early = local_call(
+    window, *outs, late = local_call(
         first_kernel,
         [
             jax.ShapeDtypeStruct((parts * rows, width), bf16),
-            *[sent_block] * len(EARLY),
-            jax.ShapeDtypeStruct((len(EARLY),) + sent_block.shape, bf16),
+            *[sent_block] * len(CROSS),
+            jax.ShapeDtypeStruct((len(LATE),) + sent_block.shape, bf16),
         ],
         [smem, pl.ANY, pl.ANY],
-        [
-            pltpu.VMEM((len(EARLY),) + by_col.shape[1:], bf16),
-            pltpu.VMEM(spectrum.shape, jnp.float32),
-            pltpu.SemaphoreType.DMA((4,)),
-            pltpu.SemaphoreType.DMA((len(EARLY),)),
-        ],
-        flops // 4,
+        [pltpu.VMEM(spectrum.shape, jnp.float32), pltpu.SemaphoreType.DMA((8, 2))]
+        + table_scratch(by_col, len(CROSS)),
+        flops // 2,
         8 * 2**20,
-        "windows_and_early_rows",
+        "windows_and_far_rows",
     )(starts, spectrum, by_col)
-    passed = lax.ppermute(early, "slab", [(s, by) for by, s in PASSED_FROM.items()])
+    outs = dict(zip(CROSS, outs))
+    passed = lax.ppermute(late, "slab", list(PASSED.items()))
     windowed = range(FIRST + 1, LAST)
-    col_blocks = {}
-    for d, sent in zip(EARLY, outs):
-        pairs = [(s, s ^ d) for s in windowed if s not in PASSED_FROM.values()]
-        col_blocks[d] = lax.ppermute(sent, "slab", pairs)
-    row_blocks = local_call(
+    columns = {}
+    for d in CROSS:
+        if d not in LATE:
+            columns[d] = lax.ppermute(outs[d], "slab", [(s, s ^ d) for s in windowed])
+    near_rows = local_call(
         second_kernel,
-        [sent_block] * len(LATE),
+        near_block,
         [vmem, pl.ANY],
-        table_scratch(by_col, len(LATE)),
-        3 * flops // 4,
-        8 * 2**20,
-        "late_rows",
+        table_scratch(by_col, HALF),
+        flops // 2,
+        5 * 2**20,
+        "near_rows",
     )(window, by_col)
-    passed, col_blocks, *row_blocks = lax.optimization_barrier((passed, col_blocks, *row_blocks))
-    row_blocks = dict(zip(LATE, row_blocks))
-    col_blocks[0] = row_blocks[0]
-    for d in PASSED:
-        pairs = [(s, s ^ d) for s in range(SLABS)]
-        col_blocks[d] = lax.ppermute(row_blocks[d] + passed[PASSED[d]], "slab", pairs)
-    col_blocks[2] = lax.ppermute(row_blocks[2], "slab", [(s, s ^ 2) for s in windowed])
-    col_blocks[2], row_blocks[1], row_blocks[3] = lax.optimization_barrier(
-        (col_blocks[2], row_blocks[1], row_blocks[3])
-    )
-    for d in (1, 3):
-        col_blocks[d] = lax.ppermute(row_blocks[d], "slab", [(s, s ^ d) for s in windowed])
-
+    passed, near_rows = lax.optimization_barrier((passed, near_rows))
+    for i, d in enumerate(LATE):
+        pairs = [(PASSED.get(s, s), s ^ d) for s in windowed]
+        columns[d] = lax.ppermute(outs[d] + passed[i], "slab", pairs)
+    halves = [list(range(HALF)), list(range(HALF, SLABS))]
+
+    def within_half(blocks):
+        return lax.all_to_all(
+            blocks, "slab", split_axis=0, concat_axis=0, axis_index_groups=halves, tiled=True
+        )
+
+    near_columns = within_half(near_rows)
     amplitude = jnp.sqrt(images).transpose(2, 0, 1).reshape(width, leds * block)
-    back_blocks = local_call(
+    near_strips, *far_strips = local_call(
         field_kernel,
-        [sent_block] * PERIOD,
-        [vmem, pl.ANY] + [vmem] * SLABS,
+        [near_block] + [sent_block] * len(CROSS),
+        [vmem, pl.ANY, vmem] + [vmem] * len(CROSS),
         [pltpu.VMEM((width, parts * block), bf16)] * 2 + table_scratch(by_row, steps),
         16 * leds * block * width * width,
         12 * 2**20,
         "modulus_step",
-    )(amplitude, by_row, *[col_blocks[d] for d in range(SLABS)])
-
-    def to_rows(d):
-        sent = back_blocks[d % PERIOD]
-        if d == 0:
-            return sent
-        pairs = [(s, (s + d) % SLABS) for s in range(SLABS) if (s + d) % SLABS in windowed]
-        return lax.ppermute(sent, "slab", pairs)
-
-    home = [to_rows(d) for d in range(SLABS)]
+    )(amplitude, by_row, near_columns, *[columns[d] for d in CROSS])
+    far_home = [
+        lax.ppermute(sent, "slab", [(s, s ^ d) for s in range(SLABS) if s ^ d in windowed])
+        for d, sent in zip(CROSS, far_strips)
+    ]
+    near_home = within_half(near_strips)
     share = width // 2
     sent, back = local_call(
         sent_kernel,
@@ -483,12 +490,12 @@
             jax.ShapeDtypeStruct((2, 2, rows, share), bf16),
             jax.ShapeDtypeStruct((parts * rows, width), bf16),
         ],
-        [smem, pl.ANY] + [vmem] * SLABS,
+        [smem, pl.ANY, vmem] + [vmem] * len(CROSS),
         table_scratch(by_col, steps // 2),
         flops // 2,
         8 * 2**20,
         "update_sent",
-    )(starts, by_col, *home)
+    )(starts, by_col, near_home, *far_home)
     got = lax.ppermute(sent, "led", [(0, 1), (1, 0), (2, 3), (3, 2)])
     kept = local_call(
         kept_kernel,

time: 143 us -> 159 us (1.11)
  the two profiles are of different devices: /device:TPU:22 before, /device:TPU:12 now
where the time goes in v2:
time: 159 us; the launch traced here: 158 us
  waiting for transfers between devices  57.2 us (36%)
  starting transfers between devices  46.2 us (29%)
  Pallas kernels  42.9 us (27%)
  other arithmetic  6.25 us (4%)
  local copies, waits for them, and re-layouts  5.39 us (3%)
    ppermute x4, waiting for transfers between devices, body_slabs(): lax.ppermute(sent, 'slab', [(s, s ^ d) for s in range(SLABS) if s ^ d in...  27.2 us
    ppermute x4, starting transfers between devices, body_slabs(): lax.ppermute(sent, 'slab', [(s, s ^ d) for s in range(SLABS) if s ^ d in...  14.9 us
    all_to_all x2, starting transfers between devices, within_half(): lax.all_to_all(blocks, 'slab', split_axis=0, concat_axis=0, axis_index_gr...  14.4 us
    ppermute x1, waiting for transfers between devices, body_slabs(): got_x = lax.ppermute(over, 'led', [(0, 2), (2, 0), (1, 3), (3, 1)])  11.6 us
    pallas_call x1, Pallas kernels, body_slabs(): local_call(field_kernel, [near_block] + [sent_block] * len(CROSS), [vmem,...  10.8 us
    ppermute x2, waiting for transfers between devices, body_slabs(): columns[d] = lax.ppermute(outs[d], 'slab', [(s, s ^ d) for s in windowed])  9.6 us
    pallas_call x1, Pallas kernels, body_slabs(): local_call(first_kernel, [jax.ShapeDtypeStruct((parts * rows, width), bf1...  9.29 us
    ppermute x2, waiting for transfers between devices, body_slabs(): columns[d] = lax.ppermute(outs[d] + passed[i], 'slab', pairs)  8.76 us
  transfers between devices with their start and end apart: 13, of which 9 were waited for; matrix products, arithmetic and copies ran while one was open for 4% of the time, Pallas kernels for 10%

profile of v2, /device:TPU:12, one launch (start us, length us, event | category | flops | bytes accessed | tf_op | source)
XLA Modules:
  0.0 158.1 jit_solution(3560932675793941856)
XLA Ops:
  0.0 0.7 pad_add_fusion.starts
  0.7 9.3 %windows_and_far_rows.1 = (bf16[1024,1024]{1,0:T(8,128)(2,1)S(1)}, bf16[4,256,128]{2,1,0:T(8,128)(2,1)S(1)}, bf16[4,256,128]{2,1,0:T(8,128)(2,1)S(1)}, bf16[4,25...) custom-call(s32[4]{0:T(128)S(1)} %pad_add_fusion.starts, ...), custom_call_target="tpu_custom_call" | custom-call | flops 2147483648 | bytes 8388608 | tf_op jit(solution)/shard_map/windows_and_far_rows/pallas_call | solution.py:429
  10.0 0.7 collective-permute-start
  10.8 7.8 %near_rows.1 = bf16[4,4,256,128]{3,2,1,0:T(8,128)(2,1)} custom-call(bf16[1024,1024]{1,0:T(8,128)(2,1)S(1)} %get-tuple-element.23.window, bf16[8,1024,256]{2,1,0:T(8,128)(2,1)} %constant.15.clone.table_any), custom_call_target="tpu_custom_call" | custom-call | flops 2147483648 | bytes 5242880 | tf_op jit(solution)/shard_map/near_rows/pallas_call | solution.py:450
  18.6 0.0 collective-permute-done
  18.6 10.0 %all-to-all-start = ((bf16[4,4,256,128]{3,2,1,0:T(8,128)(2,1)}), bf16[4,4,256,128]{3,2,1,0:T(8,128)(2,1)S(1)}, u32[]{:S(2)}, u32[]{:S(2)}) async-start(bf16[4,4,256,128]{3,2,1,0:T(8,128)(2,1)} %near_rows.1), calls=%async_computation | async-start | bytes 2097152 | tf_op jit(solution)/shard_map/all_to_all | solution.py:466
  28.7 5.6 %collective-permute-start.1 = (bf16[4,256,128]{2,1,0:T(8,128)(2,1)S(1)}, bf16[4,256,128]{2,1,0:T(8,128)(2,1)S(1)}, u32[]{:S(2)}, u32[]{:S(2)}) collective-permute-start(bf16[4,256,128]{2,1,0:T(8,128)(2,1)S(1)} %get-tuple-element.25), channel_id=1, source_target_pairs={{4,20},{8,24},{12,28},{16,0},{20,4},{24,8},{5,21},{9,25},{13,29},{... | collective-permute-start | bytes 786440 | tf_op jit(solution)/shard_map/ppermute | solution.py:449
  34.3 1.9 %collective-permute-start.3 = (bf16[4,256,128]{2,1,0:T(8,128)(2,1)S(1)}, bf16[4,256,128]{2,1,0:T(8,128)(2,1)S(1)}, u32[]{:S(2)}, u32[]{:S(2)}) collective-permute-start(bf16[4,256,128]{2,1,0:T(8,128)(2,1)S(1)} %get-tuple-element.28), channel_id=1, source_target_pairs={{4,28},{8,16},{12,20},{16,8},{20,12},{24,0},{5,29},{9,17},{13,21},... | collective-permute-start | bytes 786440 | tf_op jit(solution)/shard_map/ppermute | solution.py:449
  36.2 0.9 bitcast_add_fusion
  37.1 1.9 %collective-permute-start.2 = (bf16[4,256,128]{2,1,0:T(8,128)(2,1)}, bf16[4,256,128]{2,1,0:T(8,128)(2,1)S(1)}, u32[]{:S(2)}, u32[]{:S(2)}) collective-permute-start(bf16[4,256,128]{2,1,0:T(8,128)(2,1)} %get-tuple-element.40), channel_id=1, source_target_pairs={{0,16},{8,28},{12,24},{16,4},{20,0},{28,12},{1,17},{9,29},{13,25},... | collective-permute-start | bytes 786440 | tf_op jit(solution)/shard_map/ppermute | solution.py:462
  39.0 5.3 %collective-permute-start.4 = (bf16[4,256,128]{2,1,0:T(8,128)(2,1)}, bf16[4,256,128]{2,1,0:T(8,128)(2,1)}, u32[]{:S(2)}, u32[]{:S(2)}) collective-permute-start(bf16[4,256,128]{2,1,0:T(8,128)(2,1)} %get-tuple-element.39), channel_id=1, source_target_pairs={{0,24},{8,20},{12,16},{16,12},{20,8},{28,4},{1,25},{9,21},{13,17},... | collective-permute-start | bytes 786440 | tf_op jit(solution)/shard_map/ppermute | solution.py:462
  44.3 2.4 %sqrt.3 = f32[2,128,1024]{2,1,0:T(8,128)} sqrt(f32[2,128,1024]{2,1,0:T(8,128)} %param.9) | non-fusion elementwise | bytes 2097152 | tf_op jit(solution)/shard_map/sqrt | solution.py:471
  46.7 1.6 copy.8.amplitude
  48.3 4.0 %collective-permute-done.1.rest_0_ = bf16[4,256,128]{2,1,0:T(8,128)(2,1)S(1)} collective-permute-done((bf16[4,256,128]{2,1,0:T(8,128)(2,1)S(1)}, bf16[4,256,128]{2,1,0:T(8,128)(2,1)S(1)}, u32[]{:S(2)}, u32[]{:S(2)}) %collective-permute-start.1) | collective-permute-done | bytes 262176 | tf_op jit(solution)/shard_map/ppermute | solution.py:449
  52.3 5.6 %collective-permute-done.3.rest_2_ = bf16[4,256,128]{2,1,0:T(8,128)(2,1)S(1)} collective-permute-done((bf16[4,256,128]{2,1,0:T(8,128)(2,1)S(1)}, bf16[4,256,128]{2,1,0:T(8,128)(2,1)S(1)}, u32[]{:S(2)}, u32[]{:S(2)}) %collective-permute-start.3) | collective-permute-done | bytes 262176 | tf_op jit(solution)/shard_map/ppermute | solution.py:449
  57.9 5.7 %collective-permute-done.2.rest_1_ = bf16[4,256,128]{2,1,0:T(8,128)(2,1)S(1)} collective-permute-done((bf16[4,256,128]{2,1,0:T(8,128)(2,1)}, bf16[4,256,128]{2,1,0:T(8,128)(2,1)S(1)}, u32[]{:S(2)}, u32[]{:S(2)}) %collective-permute-start.2) | collective-permute-done | bytes 262176 | tf_op jit(solution)/shard_map/ppermute | solution.py:462
  63.6 3.0 %collective-permute-done.4.rest_3_ = bf16[4,256,128]{2,1,0:T(8,128)(2,1)} collective-permute-done((bf16[4,256,128]{2,1,0:T(8,128)(2,1)}, bf16[4,256,128]{2,1,0:T(8,128)(2,1)}, u32[]{:S(2)}, u32[]{:S(2)}) %collective-permute-start.4) | collective-permute-done | bytes 262176 | tf_op jit(solution)/shard_map/ppermute | solution.py:462
  66.6 0.0 all-to-all-done.near
  66.6 10.8 %modulus_step.1 = (bf16[4,4,256,128]{3,2,1,0:T(8,128)(2,1)}, bf16[4,256,128]{2,1,0:T(8,128)(2,1)S(1)}, bf16[4,256,128]{2,1,0:T(8,128)(2,1)S(1)}, bf16[4,256,128]...) custom-call(f32[1024,256]{1,0:T(8,128)S(1)} %copy.8.amplitude, bf16[8,256,1024]{2,1,0:T(8,128)(2,1)} %constant.14.clone.table_any, ...), custom_call_target="tpu_custom_call" | custom-call | flops 4294967296 | bytes 12582912 | tf_op jit(solution)/shard_map/modulus_step/pallas_call | solution.py:472
  77.5 0.0 copy-start
  77.5 0.7 copy-done
  78.2 0.0 copy-start.2
  78.2 0.7 copy-done.2
  78.9 0.0 copy-start.3
  78.9 0.0 copy-start.1
  78.9 4.3 %all-to-all-start.1 = ((bf16[4,4,256,128]{3,2,1,0:T(8,128)(2,1)}), bf16[4,4,256,128]{3,2,1,0:T(8,128)(2,1)S(1)}, u32[]{:S(2)}, u32[]{:S(2)}) async-start(bf16[4,4,256,128]{3,2,1,0:T(8,128)(2,1)} %get-tuple-element.30), calls=%async_computation.1 | async-start | bytes 2097152 | tf_op jit(solution)/shard_map/all_to_all | solution.py:466
  83.2 0.0 copy-done.3
  83.2 1.3 collective-permute-start.5
  84.5 0.0 copy-done.1
  84.5 6.6 %collective-permute-start.6 = (bf16[4,256,128]{2,1,0:T(8,128)(2,1)S(1)}, bf16[4,256,128]{2,1,0:T(8,128)(2,1)S(1)}, u32[]{:S(2)}, u32[]{:S(2)}) collective-permute-start(bf16[4,256,128]{2,1,0:T(8,128)(2,1)S(1)} %copy-done.1), channel_id=1, source_target_pairs={{0,20},{4,16},{12,24},{16,4},{24,12},{28,8},{1,21},{5,17},{13,25},... | collective-permute-start | bytes 786440 | tf_op jit(solution)/shard_map/ppermute | solution.py:482
  91.2 1.9 %collective-permute-start.7 = (bf16[4,256,128]{2,1,0:T(8,128)(2,1)S(1)}, bf16[4,256,128]{2,1,0:T(8,128)(2,1)S(1)}, u32[]{:S(2)}, u32[]{:S(2)}) collective-permute-start(bf16[4,256,128]{2,1,0:T(8,128)(2,1)S(1)} %get-tuple-element.33), channel_id=1, source_target_pairs={{0,24},{8,16},{12,20},{16,8},{20,12},{28,4},{1,25},{9,17},{13,21},... | collective-permute-start | bytes 786440 | tf_op jit(solution)/shard_map/ppermute | solution.py:482
  93.1 5.0 %collective-permute-start.8 = (bf16[4,256,128]{2,1,0:T(8,128)(2,1)S(1)}, bf16[4,256,128]{2,1,0:T(8,128)(2,1)S(1)}, u32[]{:S(2)}, u32[]{:S(2)}) collective-permute-start(bf16[4,256,128]{2,1,0:T(8,128)(2,1)S(1)} %get-tuple-element.34), channel_id=1, source_target_pairs={{4,24},{8,20},{12,16},{16,12},{20,8},{24,4},{5,25},{9,21},{13,17},... | collective-permute-start | bytes 786440 | tf_op jit(solution)/shard_map/ppermute | solution.py:482
  98.1 7.9 %collective-permute-done.5.rest_0_ = bf16[4,256,128]{2,1,0:T(8,128)(2,1)S(1)} collective-permute-done((bf16[4,256,128]{2,1,0:T(8,128)(2,1)S(1)}, bf16[4,256,128]{2,1,0:T(8,128)(2,1)S(1)}, u32[]{:S(2)}, u32[]{:S(2)}) %collective-permute-start.5) | collective-permute-done | bytes 262176 | tf_op jit(solution)/shard_map/ppermute | solution.py:482
  106.1 7.6 %collective-permute-done.6.rest_1_ = bf16[4,256,128]{2,1,0:T(8,128)(2,1)S(1)} collective-permute-done((bf16[4,256,128]{2,1,0:T(8,128)(2,1)S(1)}, bf16[4,256,128]{2,1,0:T(8,128)(2,1)S(1)}, u32[]{:S(2)}, u32[]{:S(2)}) %collective-permute-start.6) | collective-permute-done | bytes 262176 | tf_op jit(solution)/shard_map/ppermute | solution.py:482
  113.7 5.6 %collective-permute-done.7.rest_2_ = bf16[4,256,128]{2,1,0:T(8,128)(2,1)S(1)} collective-permute-done((bf16[4,256,128]{2,1,0:T(8,128)(2,1)S(1)}, bf16[4,256,128]{2,1,0:T(8,128)(2,1)S(1)}, u32[]{:S(2)}, u32[]{:S(2)}) %collective-permute-start.7) | collective-permute-done | bytes 262176 | tf_op jit(solution)/shard_map/ppermute | solution.py:482
  119.3 6.0 %collective-permute-done.8.rest_3_ = bf16[4,256,128]{2,1,0:T(8,128)(2,1)S(1)} collective-permute-done((bf16[4,256,128]{2,1,0:T(8,128)(2,1)S(1)}, bf16[4,256,128]{2,1,0:T(8,128)(2,1)S(1)}, u32[]{:S(2)}, u32[]{:S(2)}) %collective-permute-start.8) | collective-permute-done | bytes 262176 | tf_op jit(solution)/shard_map/ppermute | solution.py:482
  125.3 0.0 all-to-all-done.1.near
  125.3 7.4 %update_sent.1 = (bf16[2,2,256,512]{3,2,1,0:T(8,128)(2,1)S(1)}, bf16[1024,1024]{1,0:T(8,128)(2,1)S(1)}) custom-call(s32[4]{0:T(128)S(1)} %pad_add_fusion.starts, bf16[8,1024,256]{2,1,0:T(8,128)(2,1)} %constant.15.clone.table_any, bf16[4,4,256,128]{3,2,1,0:T(8,128)(2,1)S(1)} %all-to-all-done.1.near, bf16[4,256,128]{2,1,0:T(8,128)(2,1)S(1)} %collective-permute-done.5.rest_0_, ...), custom_call_target="tpu_custom_call" | custom-call | flops 2147483648 | bytes 8388608 | tf_op jit(solution)/shard_map/update_sent/pallas_call | solution.py:487
  132.8 0.1 collective-permute-start.9
  132.9 7.5 %update_kept.1 = f32[2,2,256,512]{3,2,1,0:T(8,128)S(1)} custom-call(s32[4]{0:T(128)S(1)} %pad_add_fusion.starts, bf16[8,1024,256]{2,1,0:T(8,128)(2,1)} %constant.15.clone.table_any, bf16[1024,1024]{1,0:T(8,128)(2,1)S(1)} %get-tuple-element.35.back), custom_call_target="tpu_custom_call" | custom-call | flops 2147483648 | bytes 8388608 | tf_op jit(solution)/shard_map/update_kept/pallas_call | solution.py:500
  140.3 0.0 collective-permute-done.9
  140.3 1.0 fusion.3
  141.3 1.5 collective-permute-start.10
  142.8 1.5 fusion.2
  144.3 11.6 %collective-permute-done.10 = bf16[2,256,512]{2,1,0:T(8,128)(2,1)} collective-permute-done((bf16[2,256,512]{2,1,0:T(8,128)(2,1)}, bf16[2,256,512]{2,1,0:T(8,128)(2,1)}, u32[]{:S(2)}, u32[]{:S(2)}) %collective-permute-start.10) | collective-permute-done | bytes 524320 | tf_op jit(solution)/shard_map/ppermute | solution.py:510
  155.9 2.2 %convert_add_fusion = f32[2,256,512]{2,1,0:T(8,128)} fusion(f32[2,256,512]{2,1,0:T(8,128)S(1)} %fusion.2, bf16[2,256,512]{2,1,0:T(8,128)(2,1)} %collective-permute-done.10), kind=kLoop, calls=%fused_computation.5 | loop fusion | flops 524288 | bytes 2621440 | tf_op jit(solution)/shard_map/add | solution.py:514
Async XLA Ops:
  10.0 8.6 %collective-permute-start = (bf16[2,4,256,128]{3,2,1,0:T(8,128)(2,1)S(1)}, bf16[2,4,256,128]{3,2,1,0:T(8,128)(2,1)S(1)}, u32[]{:S(2)}, u32[]{:S(2)}) collective-permute-start(bf16[2,4,256,128]{3,2,1,0:T(8,128)(2,1)S(1)} %get-tuple-element.22), channel_id=1, source_target_pairs={{4,0},{24,28},{5,1},{25,29},{6,2},{26,30},{7,3},{27,31}} | collective-permute-start | bytes 1572872 | tf_op jit(solution)/shard_map/ppermute | solution.py:444
  18.6 48.0 %all-to-all-start = ((bf16[4,4,256,128]{3,2,1,0:T(8,128)(2,1)}), bf16[4,4,256,128]{3,2,1,0:T(8,128)(2,1)S(1)}, u32[]{:S(2)}, u32[]{:S(2)}) async-start(bf16[4,4,256,128]{3,2,1,0:T(8,128)(2,1)} %near_rows.1), calls=%async_computation | async-start | bytes 2097152 | tf_op jit(solution)/shard_map/all_to_all | solution.py:466
  28.7 23.6 %collective-permute-start.1 = (bf16[4,256,128]{2,1,0:T(8,128)(2,1)S(1)}, bf16[4,256,128]{2,1,0:T(8,128)(2,1)S(1)}, u32[]{:S(2)}, u32[]{:S(2)}) collective-permute-start(bf16[4,256,128]{2,1,0:T(8,128)(2,1)S(1)} %get-tuple-element.25), channel_id=1, source_target_pairs={{4,20},{8,24},{12,28},{16,0},{20,4},{24,8},{5,21},{9,25},{13,29},{... | collective-permute-start | bytes 786440 | tf_op jit(solution)/shard_map/ppermute | solution.py:449
  34.3 23.6 %collective-permute-start.3 = (bf16[4,256,128]{2,1,0:T(8,128)(2,1)S(1)}, bf16[4,256,128]{2,1,0:T(8,128)(2,1)S(1)}, u32[]{:S(2)}, u32[]{:S(2)}) collective-permute-start(bf16[4,256,128]{2,1,0:T(8,128)(2,1)S(1)} %get-tuple-element.28), channel_id=1, source_target_pairs={{4,28},{8,16},{12,20},{16,8},{20,12},{24,0},{5,29},{9,17},{13,21},... | collective-permute-start | bytes 786440 | tf_op jit(solution)/shard_map/ppermute | solution.py:449
  37.1 26.5 %collective-permute-start.2 = (bf16[4,256,128]{2,1,0:T(8,128)(2,1)}, bf16[4,256,128]{2,1,0:T(8,128)(2,1)S(1)}, u32[]{:S(2)}, u32[]{:S(2)}) collective-permute-start(bf16[4,256,128]{2,1,0:T(8,128)(2,1)} %get-tuple-element.40), channel_id=1, source_target_pairs={{0,16},{8,28},{12,24},{16,4},{20,0},{28,12},{1,17},{9,29},{13,25},... | collective-permute-start | bytes 786440 | tf_op jit(solution)/shard_map/ppermute | solution.py:462
  39.0 27.6 %collective-permute-start.4 = (bf16[4,256,128]{2,1,0:T(8,128)(2,1)}, bf16[4,256,128]{2,1,0:T(8,128)(2,1)}, u32[]{:S(2)}, u32[]{:S(2)}) collective-permute-start(bf16[4,256,128]{2,1,0:T(8,128)(2,1)} %get-tuple-element.39), channel_id=1, source_target_pairs={{0,24},{8,20},{12,16},{16,12},{20,8},{28,4},{1,25},{9,21},{13,17},... | collective-permute-start | bytes 786440 | tf_op jit(solution)/shard_map/ppermute | solution.py:462
  77.5 0.7 copy-start
  78.2 0.7 copy-start.2
  78.9 4.3 %copy-start.3 = (bf16[4,256,128]{2,1,0:T(8,128)(2,1)S(1)}, bf16[4,256,128]{2,1,0:T(8,128)(2,1)}, u32[]{:S(2)}) copy-start(bf16[4,256,128]{2,1,0:T(8,128)(2,1)} %copy-done.2) | copy-start | bytes 786436
  78.9 5.6 %copy-start.1 = (bf16[4,256,128]{2,1,0:T(8,128)(2,1)S(1)}, bf16[4,256,128]{2,1,0:T(8,128)(2,1)}, u32[]{:S(2)}) copy-start(bf16[4,256,128]{2,1,0:T(8,128)(2,1)} %copy-done) | copy-start | bytes 786436
  78.9 46.4 %all-to-all-start.1 = ((bf16[4,4,256,128]{3,2,1,0:T(8,128)(2,1)}), bf16[4,4,256,128]{3,2,1,0:T(8,128)(2,1)S(1)}, u32[]{:S(2)}, u32[]{:S(2)}) async-start(bf16[4,4,256,128]{3,2,1,0:T(8,128)(2,1)} %get-tuple-element.30), calls=%async_computation.1 | async-start | bytes 2097152 | tf_op jit(solution)/shard_map/all_to_all | solution.py:466
  83.2 22.8 %collective-permute-start.5 = (bf16[4,256,128]{2,1,0:T(8,128)(2,1)S(1)}, bf16[4,256,128]{2,1,0:T(8,128)(2,1)S(1)}, u32[]{:S(2)}, u32[]{:S(2)}) collective-permute-start(bf16[4,256,128]{2,1,0:T(8,128)(2,1)S(1)} %copy-done.3), channel_id=1, source_target_pairs={{0,16},{4,20},{8,24},{20,4},{24,8},{28,12},{1,17},{5,21},{9,25},{2... | collective-permute-start | bytes 786440 | tf_op jit(solution)/shard_map/ppermute | solution.py:482
  84.5 29.2 %collective-permute-start.6 = (bf16[4,256,128]{2,1,0:T(8,128)(2,1)S(1)}, bf16[4,256,128]{2,1,0:T(8,128)(2,1)S(1)}, u32[]{:S(2)}, u32[]{:S(2)}) collective-permute-start(bf16[4,256,128]{2,1,0:T(8,128)(2,1)S(1)} %copy-done.1), channel_id=1, source_target_pairs={{0,20},{4,16},{12,24},{16,4},{24,12},{28,8},{1,21},{5,17},{13,25},... | collective-permute-start | bytes 786440 | tf_op jit(solution)/shard_map/ppermute | solution.py:482
  91.2 28.2 %collective-permute-start.7 = (bf16[4,256,128]{2,1,0:T(8,128)(2,1)S(1)}, bf16[4,256,128]{2,1,0:T(8,128)(2,1)S(1)}, u32[]{:S(2)}, u32[]{:S(2)}) collective-permute-start(bf16[4,256,128]{2,1,0:T(8,128)(2,1)S(1)} %get-tuple-element.33), channel_id=1, source_target_pairs={{0,24},{8,16},{12,20},{16,8},{20,12},{28,4},{1,25},{9,17},{13,21},... | collective-permute-start | bytes 786440 | tf_op jit(solution)/shard_map/ppermute | solution.py:482
  93.1 32.2 %collective-permute-start.8 = (bf16[4,256,128]{2,1,0:T(8,128)(2,1)S(1)}, bf16[4,256,128]{2,1,0:T(8,128)(2,1)S(1)}, u32[]{:S(2)}, u32[]{:S(2)}) collective-permute-start(bf16[4,256,128]{2,1,0:T(8,128)(2,1)S(1)} %get-tuple-element.34), channel_id=1, source_target_pairs={{4,24},{8,20},{12,16},{16,12},{20,8},{24,4},{5,25},{9,21},{13,17},... | collective-permute-start | bytes 786440 | tf_op jit(solution)/shard_map/ppermute | solution.py:482
  132.8 7.6 %collective-permute-start.9 = (bf16[2,2,256,512]{3,2,1,0:T(8,128)(2,1)S(1)}, bf16[2,2,256,512]{3,2,1,0:T(8,128)(2,1)S(1)}, u32[]{:S(2)}, u32[]{:S(2)}) collective-permute-start(bf16[2,2,256,512]{3,2,1,0:T(8,128)(2,1)S(1)} %get-tuple-element.36), channel_id=1, source_target_pairs={{0,1},{1,0},{2,3},{3,2},{4,5},{5,4},{6,7},{7,6},{8,9},{9,8},{10,11... | collective-permute-start | bytes 3145736 | tf_op jit(solution)/shard_map/ppermute | solution.py:499
  141.3 14.6 %collective-permute-start.10 = (bf16[2,256,512]{2,1,0:T(8,128)(2,1)}, bf16[2,256,512]{2,1,0:T(8,128)(2,1)}, u32[]{:S(2)}, u32[]{:S(2)}) collective-permute-start(bf16[2,256,512]{2,1,0:T(8,128)(2,1)} %fusion.3), channel_id=1, source_target_pairs={{0,2},{2,0},{1,3},{3,1},{4,6},{6,4},{5,7},{7,5},{8,10},{10,8},{9,1... | collective-permute-start | bytes 1572872 | tf_op jit(solution)/shard_map/ppermute | solution.py:510

commit v3 on v0

--- a/solution.py
+++ b/solution.py
@@ -143,12 +143,11 @@
 
 
 SLABS = 8
-PERIOD = 4
+HALF = 4
 FIRST, LAST = 0, 7
-EARLY = (5, 7)
-LATE = (0, 1, 2, 3, 4, 6)
-PASSED = {4: 0, 6: 1}
-PASSED_FROM = {FIRST: 1, LAST: 6}
+CROSS = (4, 5, 6, 7)
+PASSED = {1: 0, 6: 7}
+INNER = (2, 3, 4, 5)
 
 
 def dot(left, right):
@@ -182,79 +181,77 @@
             out[plane * per + led] = value[led * rows : (led + 1) * rows]
 
 
-def first_kernel(led_rows, led_cols, spectrum_any, table_any, window, *rest):
-    outs = rest[: len(EARLY)]
-    early, spectrum, table, sems = rest[len(EARLY) :]
-    position = lax.axis_index("slab")
-    leds = led_rows.shape[0]
+def is_one_of(position, slabs):
+    return functools.reduce(jnp.logical_or, [position == slab for slab in slabs])
+
+
+def window_kernel(starts, spectrum, window):
+    position = lax.axis_index("slab")
+    leds = starts.shape[0] // 2
     rows = spectrum.shape[1]
     width = window.shape[1]
-    chunks = 4
-    step = rows // chunks
-    fetches = [
-        pltpu.make_async_copy(
-            spectrum_any.at[:, pl.ds(i * step, step)],
-            spectrum.at[:, pl.ds(i * step, step)],
-            sems.at[i],
+    for led in range(leds):
+        inside, wraps = window_mask(
+            position * rows, starts[led], starts[leds + led], rows, 0, width, width
         )
-        for i in range(chunks)
-    ]
-    tables = [
-        pltpu.make_async_copy(
-            table_any.at[jnp.bitwise_xor(position, d)], table.at[i], sems.at[chunks + i]
-        )
-        for i, d in enumerate(EARLY)
-    ]
-    for copy in fetches + tables:
-        copy.start()
-    for i in range(chunks):
-        fetches[i].wait()
-        here = slice(i * step, (i + 1) * step)
-        for led in range(leds):
-            inside, wraps = window_mask(
-                position * rows + i * step, led_rows[led], led_cols[led], step, 0, width, width
-            )
-            for plane in range(2):
-                value = jnp.where(
-                    wraps, spectrum[plane, here, width:], spectrum[plane, here, :width]
-                )
-                at = (plane * leds + led) * rows + i * step
-                window[at : at + step, :] = jnp.where(inside, value, 0.0).astype(jnp.bfloat16)
-    for i in range(len(EARLY)):
-        tables[i].wait()
-        values = row_block(window[...], table[i])
-        store_parts(outs[i], values)
-        store_parts(early.at[i], values)
-
-
-def second_kernel(window, table, *outs):
-    position = lax.axis_index("slab")
-    for d, out in zip(LATE, outs):
+        for plane in range(2):
+            value = jnp.where(wraps, spectrum[plane, :, width:], spectrum[plane, :, :width])
+            at = (plane * leds + led) * rows
+            window[at : at + rows, :] = jnp.where(inside, value, 0.0).astype(jnp.bfloat16)
+
+
+def far_kernel(window, table, *outs):
+    position = lax.axis_index("slab")
+    hands_over = is_one_of(position, PASSED)
+    classes = (jnp.where(hands_over, 5, 6), 7, 2, 4, jnp.where(hands_over, 6, 5))
+    for out, d in zip(outs, classes):
         store_parts(out, row_block(window[...], table[jnp.bitwise_xor(position, d)]))
 
 
+def near_kernel(window, table, *outs):
+    position = lax.axis_index("slab")
+    for out, d in zip(outs, (0, 1, 3)):
+        store_parts(out, row_block(window[...], table[jnp.bitwise_xor(position, d)]))
+
+
 def field_kernel(amplitude, table, *rest):
-    blocks = rest[:SLABS]
-    outs = rest[SLABS : SLABS + PERIOD]
-    field_in, diff = rest[SLABS + PERIOD :]
-    position = lax.axis_index("slab")
-    parts, rows, _ = blocks[0].shape
+    near, far = rest[:HALF], rest[HALF : HALF + 5]
+    outs = rest[HALF + 5 : 2 * HALF + 5]
+    field_in, diff, strips = rest[2 * HALF + 5 :]
+    position = lax.axis_index("slab")
+    parts, rows, _ = near[0].shape
     half = parts // 2 * LANES
     width = field_in.shape[0]
     steps = width // LANES
     group = 4
-    for d in range(SLABS):
-        source = jnp.bitwise_xor(position, d)
-        if d in PASSED:
-            for by, origin in PASSED_FROM.items():
-                source = jnp.where(source == by, origin, source)
-        at = pl.multiple_of(jnp.bitwise_and(source, PERIOD - 1) * rows, rows)
+    for d, block in enumerate(near):
+        at = pl.multiple_of(jnp.bitwise_and(jnp.bitwise_xor(position, d), HALF - 1) * rows, rows)
         for part in range(parts):
-            where = (pl.ds(at, rows), slice(part * LANES, (part + 1) * LANES))
-            if d < PERIOD:
-                field_in[where] = blocks[d][part]
-            else:
-                field_in[where] += blocks[d][part]
+            cols = slice(part * LANES, (part + 1) * LANES)
+            field_in[pl.ds(at, rows), cols] = block[part]
+
+    def add(block, origin):
+        at = pl.multiple_of(jnp.bitwise_and(origin, HALF - 1) * rows, rows)
+        for part in range(parts):
+            cols = slice(part * LANES, (part + 1) * LANES)
+            field_in[pl.ds(at, rows), cols] += block[part]
+
+    passes = is_one_of(position, PASSED.values())
+    hands_over = is_one_of(position, PASSED)
+    ends = is_one_of(position, [to ^ 4 for to in PASSED.values()])
+
+    @pl.when(is_one_of(position, INNER))
+    def _():
+        add(far[0], jnp.bitwise_xor(position, 6))
+        add(far[1], jnp.bitwise_xor(position, 7))
+        add(far[2], jnp.bitwise_xor(position, jnp.where(ends, 5, 4)))
+
+    @pl.when(jnp.logical_or(passes, hands_over))
+    def _():
+        add(far[2], jnp.bitwise_xor(position, 4))
+        add(far[3], jnp.bitwise_xor(position, jnp.where(hands_over, 7, 6)))
+        add(far[4], jnp.bitwise_xor(position, 5))
+
     for first in range(0, steps, group):
         product = dot(
             table[first : first + group].reshape(group * 2 * LANES, width), field_in[...]
@@ -271,9 +268,10 @@
             diff[here, :half] = (field_re * factor).astype(jnp.bfloat16)
             diff[here, half:] = (field_im * factor).astype(jnp.bfloat16)
     pieces = rows // LANES
-    for i in range(PERIOD):
-        first = jnp.bitwise_and(jnp.bitwise_xor(position, i), PERIOD - 1) * pieces
-        product = dot(table[pl.ds(first, pieces)].reshape(pieces * 2 * LANES, width), diff[...])
+    for i in range(HALF):
+        product = dot(
+            table[i * pieces : (i + 1) * pieces].reshape(pieces * 2 * LANES, width), diff[...]
+        )
         for h in range(pieces):
             both = product[h * 2 * LANES : (h + 1) * 2 * LANES]
             here = pl.ds(h * LANES, LANES)
@@ -281,22 +279,26 @@
             back_im = (both[:LANES, half:] + both[LANES:, :half]).astype(jnp.bfloat16)
             for part in range(parts // 2):
                 cols = slice(part * LANES, (part + 1) * LANES)
-                outs[i][part, here, :] = back_re[:, cols]
-                outs[i][parts // 2 + part, here, :] = back_im[:, cols]
-
-
-def update_columns(first_step, last_step, led_rows, led_cols, table, back, out):
+                strips[i, part, here, :] = back_re[:, cols]
+                strips[i, parts // 2 + part, here, :] = back_im[:, cols]
+    for d, out in enumerate(outs):
+        out[...] = strips[jnp.bitwise_and(jnp.bitwise_xor(position, d), HALF - 1)]
+
+
+def update_columns(first_step, last_step, starts, table, back, out):
     position = lax.axis_index("slab")
     led_at = lax.axis_index("led")
     core = jnp.bitwise_and(led_at, 1)
     plane_x = jnp.right_shift(led_at, 1)
-    leds = led_rows.shape[0]
+    leds = starts.shape[0] // 2
     rows = back.shape[0] // (2 * leds)
     width = back.shape[1]
     group = width // LANES // 2
+    blocks = [
+        (1 - core if n < group else core) * group + n % group for n in range(first_step, last_step)
+    ]
     for n in range(first_step, last_step):
-        owner = 1 - core if n < group else core
-        block = owner * group + n % group
+        block = blocks[n - first_step]
         both = dot(back[...], table[block])
         half = leds * rows
         update = (
@@ -307,7 +309,7 @@
         high = [0.0, 0.0]
         for led in range(leds):
             inside, wraps = window_mask(
-                position * rows, led_rows[led], led_cols[led], rows, block * LANES, LANES, width
+                position * rows, starts[led], starts[leds + led], rows, block * LANES, LANES, width
             )
             for plane in range(2):
                 piece = jnp.where(inside, update[plane][led * rows : (led + 1) * rows], 0.0)
@@ -319,22 +321,22 @@
             out[plane_x, plane, :, cols] = high[plane].astype(out.dtype)
 
 
-def sent_kernel(led_rows, led_cols, table, *rest):
+def sent_kernel(starts, table, *rest):
     blocks = rest[:SLABS]
     out, back = rest[SLABS:]
     position = lax.axis_index("slab")
     parts, rows, _ = blocks[0].shape
-    for d in range(SLABS):
+    half = back.shape[1] // LANES // 2
+    for d, block in enumerate(blocks):
         at = pl.multiple_of(jnp.bitwise_xor(position, d) * LANES, LANES)
         for part in range(parts):
-            back[part * rows : (part + 1) * rows, pl.ds(at, LANES)] = blocks[d][part]
+            back[part * rows : (part + 1) * rows, pl.ds(at, LANES)] = block[part]
+    update_columns(0, half, starts, table, back, out)
+
+
+def kept_kernel(starts, table, back, out):
     half = back.shape[1] // LANES // 2
-    update_columns(0, half, led_rows, led_cols, table, back, out)
-
-
-def kept_kernel(led_rows, led_cols, table, back, out):
-    half = back.shape[1] // LANES // 2
-    update_columns(half, 2 * half, led_rows, led_cols, table, back, out)
+    update_columns(half, 2 * half, starts, table, back, out)
 
 
 def local_call(kernel, out_shape, spaces, scratch, flops, moved, name):
@@ -355,7 +357,7 @@
     rows = spectrum.shape[1]
     led_at = lax.axis_index("led")
     bf16 = jnp.bfloat16
-    vmem, smem, hbm = pltpu.VMEM, pltpu.SMEM, pltpu.HBM
+    vmem, smem = pltpu.VMEM, pltpu.SMEM
     cos_table, sin_table = host_tables(width)
     steps = width // LANES
     by_col = np.stack(
@@ -370,65 +372,77 @@
     sent_block = jax.ShapeDtypeStruct((parts, rows, LANES), bf16)
     flops = 8 * leds * rows * width * width
 
-    window, *outs, early = local_call(
-        first_kernel,
-        [
-            jax.ShapeDtypeStruct((parts * rows, width), bf16),
-            *[sent_block] * len(EARLY),
-            jax.ShapeDtypeStruct((len(EARLY),) + sent_block.shape, bf16),
-        ],
-        [smem, smem, hbm, hbm],
-        [
-            pltpu.VMEM(spectrum.shape, jnp.float32),
-            pltpu.VMEM((len(EARLY),) + by_col.shape[1:], bf16),
-            pltpu.SemaphoreType.DMA((4 + len(EARLY),)),
-        ],
-        flops // 4,
-        8 * 2**20,
-        "windows_and_early_rows",
-    )(led_rows, led_cols, spectrum, by_col)
-    passed = lax.ppermute(early, "slab", [(s, by) for by, s in PASSED_FROM.items()])
-    windowed = range(FIRST + 1, LAST)
-    col_blocks = {}
-    for d, sent in zip(EARLY, outs):
-        pairs = [(s, s ^ d) for s in windowed if s not in PASSED_FROM.values()]
-        col_blocks[d] = lax.ppermute(sent, "slab", pairs)
-    row_blocks = local_call(
-        second_kernel,
-        [sent_block] * len(LATE),
+    starts = jnp.concatenate([led_rows, led_cols]).astype(jnp.int32)
+    window = local_call(
+        window_kernel,
+        jax.ShapeDtypeStruct((parts * rows, width), bf16),
+        [smem, vmem],
+        [],
+        0,
+        6 * 2**20,
+        "windows",
+    )(starts, spectrum)
+    first_a, first_b, near_2, second_a, second_b = local_call(
+        far_kernel,
+        [sent_block] * 5,
         [vmem, vmem],
         [],
-        3 * flops // 4,
-        8 * 2**20,
-        "late_rows",
+        flops * 5 // 8,
+        5 * 2**20,
+        "far_rows",
     )(window, by_col)
-    for d, sent in zip(LATE, row_blocks):
-        if d == 0:
-            col_blocks[d] = sent
-        elif d in PASSED:
-            pairs = [(s, s ^ d) for s in range(SLABS)]
-            col_blocks[d] = lax.ppermute(sent + passed[PASSED[d]], "slab", pairs)
-        else:
-            col_blocks[d] = lax.ppermute(sent, "slab", [(s, s ^ d) for s in windowed])
-
+
+    def permute(sent, pairs):
+        return lax.ppermute(sent, "slab", pairs)
+
+    handed = list(PASSED.items())
+    windowed = range(FIRST + 1, LAST)
+    got_a = permute(first_a, [(s, s ^ 6) for s in INNER] + handed)
+    got_b = permute(first_b, [(s, s ^ 7) for s in INNER] + handed)
+    near_2 = permute(near_2, [(s, s ^ 2) for s in windowed])
+    near_0, near_1, near_3 = local_call(
+        near_kernel,
+        [sent_block] * 3,
+        [vmem, vmem],
+        [],
+        flops * 3 // 8,
+        5 * 2**20,
+        "near_rows",
+    )(window, by_col)
+    got_a, got_b, second_a, second_b, near_1, near_2, near_3 = lax.optimization_barrier(
+        (got_a, got_b, second_a, second_b, near_1, near_2, near_3)
+    )
+    passes = is_one_of(lax.axis_index("slab"), PASSED.values())
+    outer_pairs = [(s, s ^ 6) for s in range(SLABS) if s not in INNER]
+    far_columns = [
+        got_a,
+        got_b,
+        permute(jnp.where(passes, got_a, second_a), [(s, s ^ 4) for s in range(SLABS)]),
+        permute(jnp.where(passes, got_b, second_b), outer_pairs),
+        permute(second_b, [(s, s ^ 5) for s in INNER]),
+    ]
+    near_1 = permute(near_1, [(s, s ^ 1) for s in windowed])
+    near_3 = permute(near_3, [(s, s ^ 3) for s in windowed])
+    near_columns = [near_0, near_1, near_2, near_3]
     amplitude = jnp.sqrt(images).transpose(2, 0, 1).reshape(width, leds * block)
-    back_blocks = local_call(
+    strips = local_call(
         field_kernel,
-        [sent_block] * PERIOD,
-        [vmem] * (2 + SLABS),
-        [pltpu.VMEM((width, parts * block), bf16)] * 2,
+        [sent_block] * HALF,
+        [vmem] * 11,
+        [pltpu.VMEM((width, parts * block), bf16)] * 2
+        + [pltpu.VMEM((HALF,) + sent_block.shape, bf16)],
         16 * leds * block * width * width,
         12 * 2**20,
         "modulus_step",
-    )(amplitude, by_row, *[col_blocks[d] for d in range(SLABS)])
-
-    def to_rows(d):
-        sent = back_blocks[d % PERIOD]
-        if d == 0:
-            return sent
-        return lax.ppermute(sent, "slab", [(s, s ^ d) for s in range(SLABS) if s ^ d in windowed])
-
-    home = [to_rows(d) for d in range(SLABS)]
+    )(amplitude, by_row, *near_columns, *far_columns)
+
+    def send_home(sent, d):
+        return permute(sent, [(s, s ^ d) for s in range(SLABS) if FIRST < s ^ d < LAST])
+
+    far_home = [send_home(strips[d % HALF], d) for d in CROSS]
+    far_home[0], *late_strips = lax.optimization_barrier((far_home[0], *strips[1:]))
+    near_home = [send_home(sent, d) for d, sent in enumerate(late_strips, 1)]
+    home = [strips[0], *near_home, *far_home]
     share = width // 2
     sent, back = local_call(
         sent_kernel,
@@ -436,22 +450,22 @@
             jax.ShapeDtypeStruct((2, 2, rows, share), bf16),
             jax.ShapeDtypeStruct((parts * rows, width), bf16),
         ],
-        [smem, smem] + [vmem] * (1 + SLABS),
+        [smem] + [vmem] * (1 + SLABS),
         [],
         flops // 2,
         8 * 2**20,
         "update_sent",
-    )(led_rows, led_cols, by_col, *home)
+    )(starts, by_col, *home)
     got = lax.ppermute(sent, "led", [(0, 1), (1, 0), (2, 3), (3, 2)])
     kept = local_call(
         kept_kernel,
         jax.ShapeDtypeStruct((2, 2, rows, share), jnp.float32),
-        [smem, smem, vmem, vmem],
+        [smem, vmem, vmem],
         [],
         flops // 2,
         8 * 2**20,
         "update_kept",
-    )(led_rows, led_cols, by_col, back)
+    )(starts, by_col, back)
     over = (kept[0] + got[0].astype(jnp.float32)).astype(bf16)
     got_x = lax.ppermute(over, "led", [(0, 2), (2, 0), (1, 3), (3, 1)])
     own_part = lax.dynamic_slice_in_dim(spectrum, led_at * share, share, 2)

time: 143 us -> 134 us (0.937)
  the two profiles are of different devices: /device:TPU:4 before, /device:TPU:14 now
where the time goes in v3:
time: 134 us; the launch traced here: 133 us
  starting transfers between devices  55.7 us (42%)
  waiting for transfers between devices  39.7 us (30%)
  Pallas kernels  20.4 us (15%)
  local copies, waits for them, and re-layouts  10.2 us (8%)
  other arithmetic  6.88 us (5%)
    ppermute x15, starting transfers between devices, permute(): return lax.ppermute(sent, 'slab', pairs)  55.3 us
    ppermute x15, waiting for transfers between devices, permute(): return lax.ppermute(sent, 'slab', pairs)  26.9 us
    ppermute x1, waiting for transfers between devices, body_slabs(): got_x = lax.ppermute(over, 'led', [(0, 2), (2, 0), (1, 3), (3, 1)])  12.8 us
    unnamed x16, local copies, waits for them, and re-layouts  7.41 us
    pallas_call x1, Pallas kernels, body_slabs(): local_call(field_kernel, [sent_block] * HALF, [vmem] * 11, [pltpu.VMEM((w...  6.28 us
    pallas_call x1, Pallas kernels, body_slabs(): local_call(sent_kernel, [jax.ShapeDtypeStruct((2, 2, rows, share), bf16),...  3.83 us
    pallas_call x1, Pallas kernels, body_slabs(): local_call(far_kernel, [sent_block] * 5, [vmem, vmem], [], flops * 5 // 8...  3.24 us
    pallas_call x1, Pallas kernels, body_slabs(): local_call(kept_kernel, jax.ShapeDtypeStruct((2, 2, rows, share), jnp.flo...  3.13 us
  transfers between devices with their start and end apart: 17, of which 6 were waited for; matrix products, arithmetic and copies ran while one was open for 4% of the time, Pallas kernels for 4%

profile of v3, /device:TPU:14, one launch (start us, length us, event | category | flops | bytes accessed | tf_op | source)
XLA Modules:
  0.0 133.2 jit_solution(3198580409406735140)
XLA Ops:
  0.0 0.7 pad_add_fusion.starts
  0.7 2.2 %copy-done.3 = f32[2,256,2048]{2,1,0:T(8,128)S(1)} copy-done((f32[2,256,2048]{2,1,0:T(8,128)S(1)}, f32[2,256,2048]{2,1,0:T(8,128)}, u32[]{:S(2)}) %copy-start.3) | copy-done | bytes 4194328
  2.9 1.4 %windows.1.window = bf16[1024,1024]{1,0:T(8,128)(2,1)S(1)} custom-call(s32[4]{0:T(128)S(1)} %pad_add_fusion.starts, f32[2,256,2048]{2,1,0:T(8,128)S(1)} %copy-done.3), custom_call_target="tpu_custom_call" | custom-call | bytes 6291456 | tf_op jit(solution)/shard_map/windows/pallas_call | solution.py:376
  4.3 0.8 copy-done
  5.1 3.2 %far_rows.1 = (bf16[4,256,128]{2,1,0:T(8,128)(2,1)}, bf16[4,256,128]{2,1,0:T(8,128)(2,1)}, bf16[4,256,128]{2,1,0:T(8,128)(2,1)}, bf16[4,256,128]{2,1,0:T(8,128)(2,1)S(1)}, bf16[4,256,128]{2,1,0:T(8,128)(2,1)S(1)}) custom-call(bf16[1024,1024]{1,0:T(8,128)(2,1)S(1)} %windows.1.window, bf16[8,1024,256]{2,1,0:T(8,128)(2,1)S(1)} %copy-done), custom_call_target="tpu_custom_call" | custom-call | flops 2684354560 | bytes 5242880 | tf_op jit(solution)/shard_map/far_rows/pallas_call | solution.py:385
  8.4 3.5 %collective-permute-start = (bf16[4,256,128]{2,1,0:T(8,128)(2,1)}, bf16[4,256,128]{2,1,0:T(8,128)(2,1)S(1)}, u32[]{:S(2)}, u32[]{:S(2)}) collective-permute-start(bf16[4,256,128]{2,1,0:T(8,128)(2,1)} %get-tuple-element.33), channel_id=1, source_target_pairs={{8,16},{12,20},{16,8},{20,12},{4,0},{24,28},{9,17},{13,21},{17,9},... | collective-permute-start | bytes 786440 | tf_op jit(solution)/shard_map/ppermute | solution.py:396
  11.8 2.3 %collective-permute-start.1 = (bf16[4,256,128]{2,1,0:T(8,128)(2,1)}, bf16[4,256,128]{2,1,0:T(8,128)(2,1)S(1)}, u32[]{:S(2)}, u32[]{:S(2)}) collective-permute-start(bf16[4,256,128]{2,1,0:T(8,128)(2,1)} %get-tuple-element.34), channel_id=1, source_target_pairs={{8,20},{12,16},{16,12},{20,8},{4,0},{24,28},{9,21},{13,17},{17,13}... | collective-permute-start | bytes 786440 | tf_op jit(solution)/shard_map/ppermute | solution.py:396
  14.2 1.9 %collective-permute-start.2 = (bf16[4,256,128]{2,1,0:T(8,128)(2,1)}, bf16[4,256,128]{2,1,0:T(8,128)(2,1)S(1)}, u32[]{:S(2)}, u32[]{:S(2)}) collective-permute-start(bf16[4,256,128]{2,1,0:T(8,128)(2,1)} %get-tuple-element.38), channel_id=1, source_target_pairs={{4,12},{8,0},{12,4},{16,24},{20,28},{24,16},{5,13},{9,1},{13,5},{1... | collective-permute-start | bytes 786440 | tf_op jit(solution)/shard_map/ppermute | solution.py:396
  16.1 0.0 copy-start.1
  16.1 2.2 %copy-done.1 = bf16[8,1024,256]{2,1,0:T(8,128)(2,1)S(1)} copy-done((bf16[8,1024,256]{2,1,0:T(8,128)(2,1)S(1)}, bf16[8,1024,256]{2,1,0:T(8,128)(2,1)}, u32[]{:S(2)}) %copy-start.1) | copy-done | bytes 4194328
  18.3 2.6 %near_rows.1 = (bf16[4,256,128]{2,1,0:T(8,128)(2,1)S(1)}, bf16[4,256,128]{2,1,0:T(8,128)(2,1)}, bf16[4,256,128]{2,1,0:T(8,128)(2,1)}) custom-call(bf16[1024,1024]{1,0:T(8,128)(2,1)S(1)} %windows.1.window, bf16[8,1024,256]{2,1,0:T(8,128)(2,1)S(1)} %copy-done.1), custom_call_target="tpu_custom_call" | custom-call | flops 1610612736 | bytes 5242880 | tf_op jit(solution)/shard_map/near_rows/pallas_call | solution.py:403
  20.9 3.2 %collective-permute-done.1.rest_5_ = bf16[4,256,128]{2,1,0:T(8,128)(2,1)S(1)} collective-permute-done((bf16[4,256,128]{2,1,0:T(8,128)(2,1)}, bf16[4,256,128]{2,1,0:T(8,128)(2,1)S(1)}, u32[]{:S(2)}, u32[]{:S(2)}) %collective-permute-start.1) | collective-permute-done | bytes 262176 | tf_op jit(solution)/shard_map/ppermute | solution.py:396
  24.1 0.0 collective-permute-done.2.rest_2_
  24.1 3.8 %collective-permute-start.7 = (bf16[4,256,128]{2,1,0:T(8,128)(2,1)S(1)}, bf16[4,256,128]{2,1,0:T(8,128)(2,1)S(1)}, u32[]{:S(2)}, u32[]{:S(2)}) collective-permute-start(bf16[4,256,128]{2,1,0:T(8,128)(2,1)S(1)} %get-tuple-element.46), channel_id=1, source_target_pairs={{8,28},{12,24},{16,4},{20,0},{9,29},{13,25},{17,5},{21,1},{10,30},... | collective-permute-start | bytes 786440 | tf_op jit(solution)/shard_map/ppermute | solution.py:396
  27.9 0.7 broadcast_select_fusion
  28.7 0.7 collective-permute-start.6
  29.3 0.7 broadcast_select_fusion.1
  30.1 1.3 collective-permute-start.5
  31.4 2.7 %collective-permute-start.3 = (bf16[4,256,128]{2,1,0:T(8,128)(2,1)}, bf16[4,256,128]{2,1,0:T(8,128)(2,1)S(1)}, u32[]{:S(2)}, u32[]{:S(2)}) collective-permute-start(bf16[4,256,128]{2,1,0:T(8,128)(2,1)} %get-tuple-element.40), channel_id=1, source_target_pairs={{4,0},{8,12},{12,8},{16,20},{20,16},{24,28},{5,1},{9,13},{13,9},{1... | collective-permute-start | bytes 786440 | tf_op jit(solution)/shard_map/ppermute | solution.py:396
  34.2 2.0 %collective-permute-start.4 = (bf16[4,256,128]{2,1,0:T(8,128)(2,1)}, bf16[4,256,128]{2,1,0:T(8,128)(2,1)}, u32[]{:S(2)}, u32[]{:S(2)}) collective-permute-start(bf16[4,256,128]{2,1,0:T(8,128)(2,1)} %get-tuple-element.42), channel_id=1, source_target_pairs={{4,8},{8,4},{12,0},{16,28},{20,24},{24,20},{5,9},{9,5},{13,1},{17,... | collective-permute-start | bytes 786440 | tf_op jit(solution)/shard_map/ppermute | solution.py:396
  36.2 1.2 sqrt.3
  37.4 1.6 %copy.8.amplitude = f32[1024,256]{1,0:T(8,128)S(1)} copy(f32[1024,256]{0,1:T(8,128)} %bitcast.9) | data formatting | bytes 2097152 | tf_op jit(solution)/shard_map/reshape | solution.py:427
  39.0 0.0 collective-permute-done.6.rest_7_
  39.0 10.4 %collective-permute-done.5.rest_6_ = bf16[4,256,128]{2,1,0:T(8,128)(2,1)S(1)} collective-permute-done((bf16[4,256,128]{2,1,0:T(8,128)(2,1)}, bf16[4,256,128]{2,1,0:T(8,128)(2,1)S(1)}, u32[]{:S(2)}, u32[]{:S(2)}) %collective-permute-start.5) | collective-permute-done | bytes 262176 | tf_op jit(solution)/shard_map/ppermute | solution.py:396
  49.4 0.0 collective-permute-done.3.rest_1_
  49.4 0.1 collective-permute-done.4.rest_3_
  49.4 2.2 %copy-done.6 = bf16[8,256,1024]{2,1,0:T(8,128)(2,1)S(1)} copy-done((bf16[8,256,1024]{2,1,0:T(8,128)(2,1)S(1)}, bf16[8,256,1024]{2,1,0:T(8,128)(2,1)}, u32[]{:S(2)}) %copy-start.6) | copy-done | bytes 4194328
  51.6 6.3 %modulus_step.1 = (bf16[4,256,128]{2,1,0:T(8,128)(2,1)S(1)}, bf16[4,256,128]{2,1,0:T(8,128)(2,1)S(1)}, bf16[4,256,128]{2,1,0:T(8,128)(2,1)S(1)}, bf16[4,256,128]{2,1,0:T(8,128)(2,1)S(1)}) custom-call(f32[1024,256]{1,0:T(8,128)S(1)} %copy.8.amplitude, bf16[8,256,1024]{2,1,0:T(8,128)(2,1)S(1)} %copy-done.6, bf16[4,256,128]{2,1,0:T(8,128)(2,1)S(1)} %copy-done.5, ...), custom_call_target="tpu_custom_call" | custom-call | flops 4294967296 | bytes 12582912 | tf_op jit(solution)/shard_map/modulus_step/pallas_call | solution.py:428
  57.9 1.3 collective-permute-start.8
  59.2 7.6 %collective-permute-start.12 = (bf16[4,256,128]{2,1,0:T(8,128)(2,1)S(1)}, bf16[4,256,128]{2,1,0:T(8,128)(2,1)S(1)}, u32[]{:S(2)}, u32[]{:S(2)}) collective-permute-start(bf16[4,256,128]{2,1,0:T(8,128)(2,1)S(1)} %get-tuple-element.51), channel_id=1, source_target_pairs={{0,20},{4,16},{12,24},{16,4},{24,12},{28,8},{1,21},{5,17},{13,25},... | collective-permute-start | bytes 786440 | tf_op jit(solution)/shard_map/ppermute | solution.py:396
  66.9 1.9 %collective-permute-start.13 = (bf16[4,256,128]{2,1,0:T(8,128)(2,1)S(1)}, bf16[4,256,128]{2,1,0:T(8,128)(2,1)S(1)}, u32[]{:S(2)}, u32[]{:S(2)}) collective-permute-start(bf16[4,256,128]{2,1,0:T(8,128)(2,1)S(1)} %get-tuple-element.52), channel_id=1, source_target_pairs={{0,24},{8,16},{12,20},{16,8},{20,12},{28,4},{1,25},{9,17},{13,21},... | collective-permute-start | bytes 786440 | tf_op jit(solution)/shard_map/ppermute | solution.py:396
  68.8 3.3 %collective-permute-start.14 = (bf16[4,256,128]{2,1,0:T(8,128)(2,1)S(1)}, bf16[4,256,128]{2,1,0:T(8,128)(2,1)S(1)}, u32[]{:S(2)}, u32[]{:S(2)}) collective-permute-start(bf16[4,256,128]{2,1,0:T(8,128)(2,1)S(1)} %get-tuple-element.53), channel_id=1, source_target_pairs={{4,24},{8,20},{12,16},{16,12},{20,8},{24,4},{5,25},{9,21},{13,17},... | collective-permute-start | bytes 786440 | tf_op jit(solution)/shard_map/ppermute | solution.py:396
  72.1 0.0 collective-permute-done.8.rest_4_
  72.1 17.4 %collective-permute-start.10 = (bf16[4,256,128]{2,1,0:T(8,128)(2,1)S(1)}, bf16[4,256,128]{2,1,0:T(8,128)(2,1)S(1)}, u32[]{:S(2)}, u32[]{:S(2)}) collective-permute-start(bf16[4,256,128]{2,1,0:T(8,128)(2,1)S(1)} %get-tuple-element.52), channel_id=1, source_target_pairs={{0,8},{4,12},{12,4},{16,24},{24,16},{28,20},{1,9},{5,13},{13,5},{1... | collective-permute-start | bytes 786440 | tf_op jit(solution)/shard_map/ppermute | solution.py:396
  89.5 1.3 collective-permute-start.11
  90.8 0.0 collective-permute-done.12.rest_5_
  90.8 4.2 %collective-permute-start.9 = (bf16[4,256,128]{2,1,0:T(8,128)(2,1)S(1)}, bf16[4,256,128]{2,1,0:T(8,128)(2,1)S(1)}, u32[]{:S(2)}, u32[]{:S(2)}) collective-permute-start(bf16[4,256,128]{2,1,0:T(8,128)(2,1)S(1)} %get-tuple-element.51), channel_id=1, source_target_pairs={{0,4},{8,12},{12,8},{16,20},{20,16},{28,24},{1,5},{9,13},{13,9},{1... | collective-permute-start | bytes 786440 | tf_op jit(solution)/shard_map/ppermute | solution.py:396
  95.0 0.0 collective-permute-done.13.rest_6_
  95.0 8.1 %collective-permute-done.14.rest_7_ = bf16[4,256,128]{2,1,0:T(8,128)(2,1)S(1)} collective-permute-done((bf16[4,256,128]{2,1,0:T(8,128)(2,1)S(1)}, bf16[4,256,128]{2,1,0:T(8,128)(2,1)S(1)}, u32[]{:S(2)}, u32[]{:S(2)}) %collective-permute-start.14) | collective-permute-done | bytes 262176 | tf_op jit(solution)/shard_map/ppermute | solution.py:396
  103.1 5.2 %collective-permute-done.9.rest_1_ = bf16[4,256,128]{2,1,0:T(8,128)(2,1)S(1)} collective-permute-done((bf16[4,256,128]{2,1,0:T(8,128)(2,1)S(1)}, bf16[4,256,128]{2,1,0:T(8,128)(2,1)S(1)}, u32[]{:S(2)}, u32[]{:S(2)}) %collective-permute-start.9) | collective-permute-done | bytes 262176 | tf_op jit(solution)/shard_map/ppermute | solution.py:396
  108.4 3.8 %update_sent.1 = (bf16[2,2,256,512]{3,2,1,0:T(8,128)(2,1)S(1)}, bf16[1024,1024]{1,0:T(8,128)(2,1)S(1)}) custom-call(s32[4]{0:T(128)S(1)} %pad_add_fusion.starts, bf16[8,1024,256]{2,1,0:T(8,128)(2,1)S(1)} %copy-done.2, bf16[4,256,128]{2,1,0:T(8,128)(2,1)S(1)} %get-tuple-element.47.rest_0_, bf16[4,256,128]{2,1,0:T(8,128)(2,1)S(1)} %collective-permute-done.9.rest_1_, ...), custom_call_target="tpu_custom_call" | custom-call | flops 2147483648 | bytes 8388608 | tf_op jit(solution)/shard_map/update_sent/pallas_call | solution.py:447
  112.2 0.1 collective-permute-start.15
  112.3 3.1 %update_kept.1 = f32[2,2,256,512]{3,2,1,0:T(8,128)S(1)} custom-call(s32[4]{0:T(128)S(1)} %pad_add_fusion.starts, bf16[8,1024,256]{2,1,0:T(8,128)(2,1)S(1)} %copy-done.2, bf16[1024,1024]{1,0:T(8,128)(2,1)S(1)} %get-tuple-element.55.back), custom_call_target="tpu_custom_call" | custom-call | flops 2147483648 | bytes 8388608 | tf_op jit(solution)/shard_map/update_kept/pallas_call | solution.py:460
  115.4 1.0 fusion.3
  116.4 0.4 collective-permute-start.16
  116.8 1.5 %fusion.2 = f32[2,256,512]{2,1,0:T(8,128)S(1)} fusion(f32[2,2,256,512]{3,2,1,0:T(8,128)S(1)} %update_kept.1, f32[2,256,2048]{2,1,0:T(8,128)} %spectrum.1, s32[]{:T(128)S(6)} %select_n.15, bf16[2,2,256,512]{3,2,1,0:T(8,128)(2,1)S(1)} %collective-permute-done.15), kind=kLoop, calls=%fused_computation.4 | loop fusion | flops 786432 | bytes 3670020 | tf_op jit(solution)/shard_map/add | solution.py:472
  118.3 12.8 %collective-permute-done.16 = bf16[2,256,512]{2,1,0:T(8,128)(2,1)} collective-permute-done((bf16[2,256,512]{2,1,0:T(8,128)(2,1)}, bf16[2,256,512]{2,1,0:T(8,128)(2,1)}, u32[]{:S(2)}, u32[]{:S(2)}) %collective-permute-start.16) | collective-permute-done | bytes 524320 | tf_op jit(solution)/shard_map/ppermute | solution.py:470
  131.0 2.2 %convert_add_fusion = f32[2,256,512]{2,1,0:T(8,128)} fusion(f32[2,256,512]{2,1,0:T(8,128)S(1)} %fusion.2, bf16[2,256,512]{2,1,0:T(8,128)(2,1)} %collective-permute-done.16), kind=kLoop, calls=%fused_computation.5 | loop fusion | flops 524288 | bytes 2621440 | tf_op jit(solution)/shard_map/add | solution.py:474
  (16 shorter events, 0.0 us)
Async XLA Ops:
  0.7 2.2 %copy-start.3 = (f32[2,256,2048]{2,1,0:T(8,128)S(1)}, f32[2,256,2048]{2,1,0:T(8,128)}, u32[]{:S(2)}) copy-start(f32[2,256,2048]{2,1,0:T(8,128)} %spectrum.1) | copy-start | bytes 12582916
  2.9 2.2 %copy-start = (bf16[8,1024,256]{2,1,0:T(8,128)(2,1)S(1)}, bf16[8,1024,256]{2,1,0:T(8,128)(2,1)}, u32[]{:S(2)}) copy-start(bf16[8,1024,256]{2,1,0:T(8,128)(2,1)} %constant.22.clone.table) | copy-start | bytes 12582916
  8.4 12.5 %collective-permute-start = (bf16[4,256,128]{2,1,0:T(8,128)(2,1)}, bf16[4,256,128]{2,1,0:T(8,128)(2,1)S(1)}, u32[]{:S(2)}, u32[]{:S(2)}) collective-permute-start(bf16[4,256,128]{2,1,0:T(8,128)(2,1)} %get-tuple-element.33), channel_id=1, source_target_pairs={{8,16},{12,20},{16,8},{20,12},{4,0},{24,28},{9,17},{13,21},{17,9},... | collective-permute-start | bytes 786440 | tf_op jit(solution)/shard_map/ppermute | solution.py:396
  11.8 12.2 %collective-permute-start.1 = (bf16[4,256,128]{2,1,0:T(8,128)(2,1)}, bf16[4,256,128]{2,1,0:T(8,128)(2,1)S(1)}, u32[]{:S(2)}, u32[]{:S(2)}) collective-permute-start(bf16[4,256,128]{2,1,0:T(8,128)(2,1)} %get-tuple-element.34), channel_id=1, source_target_pairs={{8,20},{12,16},{16,12},{20,8},{4,0},{24,28},{9,21},{13,17},{17,13}... | collective-permute-start | bytes 786440 | tf_op jit(solution)/shard_map/ppermute | solution.py:396
  14.2 9.9 %collective-permute-start.2 = (bf16[4,256,128]{2,1,0:T(8,128)(2,1)}, bf16[4,256,128]{2,1,0:T(8,128)(2,1)S(1)}, u32[]{:S(2)}, u32[]{:S(2)}) collective-permute-start(bf16[4,256,128]{2,1,0:T(8,128)(2,1)} %get-tuple-element.38), channel_id=1, source_target_pairs={{4,12},{8,0},{12,4},{16,24},{20,28},{24,16},{5,13},{9,1},{13,5},{1... | collective-permute-start | bytes 786440 | tf_op jit(solution)/shard_map/ppermute | solution.py:396
  16.1 2.2 %copy-start.1 = (bf16[8,1024,256]{2,1,0:T(8,128)(2,1)S(1)}, bf16[8,1024,256]{2,1,0:T(8,128)(2,1)}, u32[]{:S(2)}) copy-start(bf16[8,1024,256]{2,1,0:T(8,128)(2,1)} %constant.22.clone.table) | copy-start | bytes 12582916
  20.9 16.5 %copy-start.4 = (bf16[4,256,128]{2,1,0:T(8,128)(2,1)}, bf16[4,256,128]{2,1,0:T(8,128)(2,1)S(1)}, u32[]{:S(2)}) copy-start(bf16[4,256,128]{2,1,0:T(8,128)(2,1)S(1)} %get-tuple-element.32.rest_0_) | copy-start | bytes 786436
  20.9 15.3 %copy-start.7 = (f32[2,128,1024]{2,1,0:T(8,128)S(1)}, f32[2,128,1024]{2,1,0:T(8,128)}, u32[]{:S(2)}) copy-start(f32[2,128,1024]{2,1,0:T(8,128)} %param.9) | copy-start | bytes 3145732
  24.1 25.3 %collective-permute-start.7 = (bf16[4,256,128]{2,1,0:T(8,128)(2,1)S(1)}, bf16[4,256,128]{2,1,0:T(8,128)(2,1)S(1)}, u32[]{:S(2)}, u32[]{:S(2)}) collective-permute-start(bf16[4,256,128]{2,1,0:T(8,128)(2,1)S(1)} %get-tuple-element.46), channel_id=1, source_target_pairs={{8,28},{12,24},{16,4},{20,0},{9,29},{13,25},{17,5},{21,1},{10,30},... | collective-permute-start | bytes 786440 | tf_op jit(solution)/shard_map/ppermute | solution.py:396
  28.7 10.3 %collective-permute-start.6 = (bf16[4,256,128]{2,1,0:T(8,128)(2,1)}, bf16[4,256,128]{2,1,0:T(8,128)(2,1)S(1)}, u32[]{:S(2)}, u32[]{:S(2)}) collective-permute-start(bf16[4,256,128]{2,1,0:T(8,128)(2,1)} %broadcast_select_fusion), channel_id=1, source_target_pairs={{0,24},{4,28},{24,0},{28,4},{1,25},{5,29},{25,1},{29,5},{2,26},{6,... | collective-permute-start | bytes 786440 | tf_op jit(solution)/shard_map/ppermute | solution.py:396
  30.1 19.3 %collective-permute-start.5 = (bf16[4,256,128]{2,1,0:T(8,128)(2,1)}, bf16[4,256,128]{2,1,0:T(8,128)(2,1)S(1)}, u32[]{:S(2)}, u32[]{:S(2)}) collective-permute-start(bf16[4,256,128]{2,1,0:T(8,128)(2,1)} %broadcast_select_fusion.1), channel_id=1, source_target_pairs={{0,16},{4,20},{8,24},{12,28},{16,0},{20,4},{24,8},{28,12},{1,17},{... | collective-permute-start | bytes 786440 | tf_op jit(solution)/shard_map/ppermute | solution.py:396
  31.4 18.0 %collective-permute-start.3 = (bf16[4,256,128]{2,1,0:T(8,128)(2,1)}, bf16[4,256,128]{2,1,0:T(8,128)(2,1)S(1)}, u32[]{:S(2)}, u32[]{:S(2)}) collective-permute-start(bf16[4,256,128]{2,1,0:T(8,128)(2,1)} %get-tuple-element.40), channel_id=1, source_target_pairs={{4,0},{8,12},{12,8},{16,20},{20,16},{24,28},{5,1},{9,13},{13,9},{1... | collective-permute-start | bytes 786440 | tf_op jit(solution)/shard_map/ppermute | solution.py:396
  34.2 15.3 %collective-permute-start.4 = (bf16[4,256,128]{2,1,0:T(8,128)(2,1)}, bf16[4,256,128]{2,1,0:T(8,128)(2,1)}, u32[]{:S(2)}, u32[]{:S(2)}) collective-permute-start(bf16[4,256,128]{2,1,0:T(8,128)(2,1)} %get-tuple-element.42), channel_id=1, source_target_pairs={{4,8},{8,4},{12,0},{16,28},{20,24},{24,20},{5,9},{9,5},{13,1},{17,... | collective-permute-start | bytes 786440 | tf_op jit(solution)/shard_map/ppermute | solution.py:396
  37.4 12.1 %copy-start.5 = (bf16[4,256,128]{2,1,0:T(8,128)(2,1)S(1)}, bf16[4,256,128]{2,1,0:T(8,128)(2,1)}, u32[]{:S(2)}) copy-start(bf16[4,256,128]{2,1,0:T(8,128)(2,1)} %copy-done.4) | copy-start | bytes 786436
  49.4 2.2 %copy-start.6 = (bf16[8,256,1024]{2,1,0:T(8,128)(2,1)S(1)}, bf16[8,256,1024]{2,1,0:T(8,128)(2,1)}, u32[]{:S(2)}) copy-start(bf16[8,256,1024]{2,1,0:T(8,128)(2,1)} %constant.21.clone.table) | copy-start | bytes 12582916
  51.6 56.7 %copy-start.2 = (bf16[8,1024,256]{2,1,0:T(8,128)(2,1)S(1)}, bf16[8,1024,256]{2,1,0:T(8,128)(2,1)}, u32[]{:S(2)}) copy-start(bf16[8,1024,256]{2,1,0:T(8,128)(2,1)} %constant.22.clone.table) | copy-start | bytes 12582916
  57.9 14.2 %collective-permute-start.8 = (bf16[4,256,128]{2,1,0:T(8,128)(2,1)S(1)}, bf16[4,256,128]{2,1,0:T(8,128)(2,1)S(1)}, u32[]{:S(2)}, u32[]{:S(2)}) collective-permute-start(bf16[4,256,128]{2,1,0:T(8,128)(2,1)S(1)} %get-tuple-element.47.rest_0_), channel_id=1, source_target_pairs={{0,16},{4,20},{8,24},{20,4},{24,8},{28,12},{1,17},{5,21},{9,25},{2... | collective-permute-start | bytes 786440 | tf_op jit(solution)/shard_map/ppermute | solution.py:396
  59.2 31.6 %collective-permute-start.12 = (bf16[4,256,128]{2,1,0:T(8,128)(2,1)S(1)}, bf16[4,256,128]{2,1,0:T(8,128)(2,1)S(1)}, u32[]{:S(2)}, u32[]{:S(2)}) collective-permute-start(bf16[4,256,128]{2,1,0:T(8,128)(2,1)S(1)} %get-tuple-element.51), channel_id=1, source_target_pairs={{0,20},{4,16},{12,24},{16,4},{24,12},{28,8},{1,21},{5,17},{13,25},... | collective-permute-start | bytes 786440 | tf_op jit(solution)/shard_map/ppermute | solution.py:396
  66.9 28.2 %collective-permute-start.13 = (bf16[4,256,128]{2,1,0:T(8,128)(2,1)S(1)}, bf16[4,256,128]{2,1,0:T(8,128)(2,1)S(1)}, u32[]{:S(2)}, u32[]{:S(2)}) collective-permute-start(bf16[4,256,128]{2,1,0:T(8,128)(2,1)S(1)} %get-tuple-element.52), channel_id=1, source_target_pairs={{0,24},{8,16},{12,20},{16,8},{20,12},{28,4},{1,25},{9,17},{13,21},... | collective-permute-start | bytes 786440 | tf_op jit(solution)/shard_map/ppermute | solution.py:396
  68.8 34.3 %collective-permute-start.14 = (bf16[4,256,128]{2,1,0:T(8,128)(2,1)S(1)}, bf16[4,256,128]{2,1,0:T(8,128)(2,1)S(1)}, u32[]{:S(2)}, u32[]{:S(2)}) collective-permute-start(bf16[4,256,128]{2,1,0:T(8,128)(2,1)S(1)} %get-tuple-element.53), channel_id=1, source_target_pairs={{4,24},{8,20},{12,16},{16,12},{20,8},{24,4},{5,25},{9,21},{13,17},... | collective-permute-start | bytes 786440 | tf_op jit(solution)/shard_map/ppermute | solution.py:396
  72.1 31.0 %collective-permute-start.10 = (bf16[4,256,128]{2,1,0:T(8,128)(2,1)S(1)}, bf16[4,256,128]{2,1,0:T(8,128)(2,1)S(1)}, u32[]{:S(2)}, u32[]{:S(2)}) collective-permute-start(bf16[4,256,128]{2,1,0:T(8,128)(2,1)S(1)} %get-tuple-element.52), channel_id=1, source_target_pairs={{0,8},{4,12},{12,4},{16,24},{24,16},{28,20},{1,9},{5,13},{13,5},{1... | collective-permute-start | bytes 786440 | tf_op jit(solution)/shard_map/ppermute | solution.py:396
  89.5 13.6 %collective-permute-start.11 = (bf16[4,256,128]{2,1,0:T(8,128)(2,1)S(1)}, bf16[4,256,128]{2,1,0:T(8,128)(2,1)S(1)}, u32[]{:S(2)}, u32[]{:S(2)}) collective-permute-start(bf16[4,256,128]{2,1,0:T(8,128)(2,1)S(1)} %get-tuple-element.53), channel_id=1, source_target_pairs={{0,12},{4,8},{8,4},{20,24},{24,20},{28,16},{1,13},{5,9},{9,5},{21,... | collective-permute-start | bytes 786440 | tf_op jit(solution)/shard_map/ppermute | solution.py:396
  90.8 17.5 %collective-permute-start.9 = (bf16[4,256,128]{2,1,0:T(8,128)(2,1)S(1)}, bf16[4,256,128]{2,1,0:T(8,128)(2,1)S(1)}, u32[]{:S(2)}, u32[]{:S(2)}) collective-permute-start(bf16[4,256,128]{2,1,0:T(8,128)(2,1)S(1)} %get-tuple-element.51), channel_id=1, source_target_pairs={{0,4},{8,12},{12,8},{16,20},{20,16},{28,24},{1,5},{9,13},{13,9},{1... | collective-permute-start | bytes 786440 | tf_op jit(solution)/shard_map/ppermute | solution.py:396
  112.2 3.2 %collective-permute-start.15 = (bf16[2,2,256,512]{3,2,1,0:T(8,128)(2,1)S(1)}, bf16[2,2,256,512]{3,2,1,0:T(8,128)(2,1)S(1)}, u32[]{:S(2)}, u32[]{:S(2)}) collective-permute-start(bf16[2,2,256,512]{3,2,1,0:T(8,128)(2,1)S(1)} %get-tuple-element.56), channel_id=1, source_target_pairs={{0,1},{1,0},{2,3},{3,2},{4,5},{5,4},{6,7},{7,6},{8,9},{9,8},{10,11... | collective-permute-start | bytes 3145736 | tf_op jit(solution)/shard_map/ppermute | solution.py:459
  116.4 14.6 %collective-permute-start.16 = (bf16[2,256,512]{2,1,0:T(8,128)(2,1)}, bf16[2,256,512]{2,1,0:T(8,128)(2,1)}, u32[]{:S(2)}, u32[]{:S(2)}) collective-permute-start(bf16[2,256,512]{2,1,0:T(8,128)(2,1)} %fusion.3), channel_id=1, source_target_pairs={{0,2},{2,0},{1,3},{3,1},{4,6},{6,4},{5,7},{7,5},{8,10},{10,8},{9,1... | collective-permute-start | bytes 1572872 | tf_op jit(solution)/shard_map/ppermute | solution.py:470

commit v4 on v3

--- a/solution.py
+++ b/solution.py
@@ -165,8 +165,14 @@
     return row_term * row_term + col_term * col_term < width * width, wraps
 
 
+def dot_t(left, right):
+    return lax.dot_general(
+        left, right, (((1,), (1,)), ((), ())), preferred_element_type=jnp.float32
+    )
+
+
 def row_block(window, table):
-    both = dot(window, table)
+    both = dot_t(window, table)
     half = both.shape[0] // 2
     row_re = both[:half, :LANES] + both[half:, LANES:]
     row_im = both[half:, :LANES] - both[:half, LANES:]
@@ -200,17 +206,14 @@
             window[at : at + rows, :] = jnp.where(inside, value, 0.0).astype(jnp.bfloat16)
 
 
-def far_kernel(window, table, *outs):
-    position = lax.axis_index("slab")
+def classes_of(position):
     hands_over = is_one_of(position, PASSED)
-    classes = (jnp.where(hands_over, 5, 6), 7, 2, 4, jnp.where(hands_over, 6, 5))
-    for out, d in zip(outs, classes):
-        store_parts(out, row_block(window[...], table[jnp.bitwise_xor(position, d)]))
-
-
-def near_kernel(window, table, *outs):
-    position = lax.axis_index("slab")
-    for out, d in zip(outs, (0, 1, 3)):
+    return (jnp.where(hands_over, 5, 6), 7, 2, 4, jnp.where(hands_over, 6, 5), 0, 1, 3)
+
+
+def rows_kernel(which, window, table, *outs):
+    position = lax.axis_index("slab")
+    for out, d in zip(outs, classes_of(position)[which]):
         store_parts(out, row_block(window[...], table[jnp.bitwise_xor(position, d)]))
 
 
@@ -285,6 +288,12 @@
         out[...] = strips[jnp.bitwise_and(jnp.bitwise_xor(position, d), HALF - 1)]
 
 
+def layout_kernel(*refs):
+    position = lax.axis_index("slab")
+    for d, strip in enumerate(refs[:-1]):
+        refs[-1][jnp.bitwise_and(jnp.bitwise_xor(position, d), HALF - 1)] = strip[...]
+
+
 def update_columns(first_step, last_step, starts, table, back, out):
     position = lax.axis_index("slab")
     led_at = lax.axis_index("led")
@@ -299,7 +308,7 @@
     ]
     for n in range(first_step, last_step):
         block = blocks[n - first_step]
-        both = dot(back[...], table[block])
+        both = dot_t(back[...], table[block])
         half = leds * rows
         update = (
             both[:half, :LANES] - both[half:, LANES:],
@@ -321,14 +330,17 @@
             out[plane_x, plane, :, cols] = high[plane].astype(out.dtype)
 
 
-def sent_kernel(starts, table, *rest):
-    blocks = rest[:SLABS]
-    out, back = rest[SLABS:]
-    position = lax.axis_index("slab")
-    parts, rows, _ = blocks[0].shape
+def sent_kernel(starts, table, near, *rest):
+    far = rest[: len(CROSS)]
+    out, back = rest[len(CROSS) :]
+    position = lax.axis_index("slab")
+    base = position - jnp.bitwise_and(position, HALF - 1)
+    _, parts, rows, _ = near.shape
     half = back.shape[1] // LANES // 2
-    for d, block in enumerate(blocks):
-        at = pl.multiple_of(jnp.bitwise_xor(position, d) * LANES, LANES)
+    blocks = [(base + i, near.at[i]) for i in range(HALF)]
+    blocks += [(jnp.bitwise_xor(position, d), block) for d, block in zip(CROSS, far)]
+    for source, block in blocks:
+        at = pl.multiple_of(source * LANES, LANES)
         for part in range(parts):
             back[part * rows : (part + 1) * rows, pl.ds(at, LANES)] = block[part]
     update_columns(0, half, starts, table, back, out)
@@ -339,14 +351,14 @@
     update_columns(half, 2 * half, starts, table, back, out)
 
 
-def local_call(kernel, out_shape, spaces, scratch, flops, moved, name):
+def local_call(kernel, out_shape, spaces, scratch, flops, moved, limit, name):
     return pl.pallas_call(
         kernel,
         out_shape=out_shape,
         in_specs=[pl.BlockSpec(memory_space=space) for space in spaces],
         out_specs=jax.tree.map(lambda _: pl.BlockSpec(memory_space=pltpu.VMEM), out_shape),
         scratch_shapes=scratch,
-        compiler_params=pltpu.CompilerParams(vmem_limit_bytes=32 * 2**20),
+        compiler_params=pltpu.CompilerParams(vmem_limit_bytes=limit * 2**20),
         cost_estimate=pl.CostEstimate(flops=flops, bytes_accessed=moved, transcendentals=0),
         name=name,
     )
@@ -360,14 +372,14 @@
     vmem, smem = pltpu.VMEM, pltpu.SMEM
     cos_table, sin_table = host_tables(width)
     steps = width // LANES
-    by_col = np.stack(
-        [
-            np.concatenate([t[:, j * LANES : (j + 1) * LANES] for t in (cos_table, sin_table)], 1)
-            for j in range(steps)
-        ]
-    )
-    by_row = jnp.asarray(np.ascontiguousarray(by_col.transpose(0, 2, 1)))
-    by_col = jnp.asarray(by_col)
+    table = jnp.asarray(
+        np.stack(
+            [
+                np.concatenate([t[j * LANES : (j + 1) * LANES] for t in (cos_table, sin_table)])
+                for j in range(steps)
+            ]
+        )
+    )
     parts = 2 * leds
     sent_block = jax.ShapeDtypeStruct((parts, rows, LANES), bf16)
     flops = 8 * leds * rows * width * width
@@ -380,18 +392,24 @@
         [],
         0,
         6 * 2**20,
+        12,
         "windows",
     )(starts, spectrum)
-    first_a, first_b, near_2, second_a, second_b = local_call(
-        far_kernel,
-        [sent_block] * 5,
-        [vmem, vmem],
-        [],
-        flops * 5 // 8,
-        5 * 2**20,
-        "far_rows",
-    )(window, by_col)
-
+
+    def rows_call(which, name):
+        count = which.stop - which.start
+        return local_call(
+            functools.partial(rows_kernel, which),
+            [sent_block] * count,
+            [vmem, vmem],
+            [],
+            flops * count // SLABS,
+            5 * 2**20,
+            16,
+            name,
+        )(window, table)
+
+    first_a, first_b, near_2 = rows_call(slice(0, 3), "rows_round_1")
     def permute(sent, pairs):
         return lax.ppermute(sent, "slab", pairs)
 
@@ -400,15 +418,7 @@
     got_a = permute(first_a, [(s, s ^ 6) for s in INNER] + handed)
     got_b = permute(first_b, [(s, s ^ 7) for s in INNER] + handed)
     near_2 = permute(near_2, [(s, s ^ 2) for s in windowed])
-    near_0, near_1, near_3 = local_call(
-        near_kernel,
-        [sent_block] * 3,
-        [vmem, vmem],
-        [],
-        flops * 3 // 8,
-        5 * 2**20,
-        "near_rows",
-    )(window, by_col)
+    second_a, second_b, near_0, near_1, near_3 = rows_call(slice(3, SLABS), "rows_round_2")
     got_a, got_b, second_a, second_b, near_1, near_2, near_3 = lax.optimization_barrier(
         (got_a, got_b, second_a, second_b, near_1, near_2, near_3)
     )
@@ -433,16 +443,32 @@
         + [pltpu.VMEM((HALF,) + sent_block.shape, bf16)],
         16 * leds * block * width * width,
         12 * 2**20,
+        20,
         "modulus_step",
-    )(amplitude, by_row, *near_columns, *far_columns)
+    )(amplitude, table, *near_columns, *far_columns)
 
     def send_home(sent, d):
         return permute(sent, [(s, s ^ d) for s in range(SLABS) if FIRST < s ^ d < LAST])
 
     far_home = [send_home(strips[d % HALF], d) for d in CROSS]
-    far_home[0], *late_strips = lax.optimization_barrier((far_home[0], *strips[1:]))
-    near_home = [send_home(sent, d) for d, sent in enumerate(late_strips, 1)]
-    home = [strips[0], *near_home, *far_home]
+    near_strips = local_call(
+        layout_kernel,
+        jax.ShapeDtypeStruct((HALF,) + sent_block.shape, bf16),
+        [vmem] * HALF,
+        [],
+        0,
+        12 * 2**20,
+        8,
+        "near_strips",
+    )(*strips)
+    near_home = lax.all_to_all(
+        near_strips,
+        "slab",
+        split_axis=0,
+        concat_axis=0,
+        axis_index_groups=[list(range(HALF)), list(range(HALF, SLABS))],
+        tiled=True,
+    )
     share = width // 2
     sent, back = local_call(
         sent_kernel,
@@ -450,12 +476,13 @@
             jax.ShapeDtypeStruct((2, 2, rows, share), bf16),
             jax.ShapeDtypeStruct((parts * rows, width), bf16),
         ],
-        [smem] + [vmem] * (1 + SLABS),
+        [smem] + [vmem] * (2 + len(CROSS)),
         [],
         flops // 2,
         8 * 2**20,
+        20,
         "update_sent",
-    )(starts, by_col, *home)
+    )(starts, table, near_home, *far_home)
     got = lax.ppermute(sent, "led", [(0, 1), (1, 0), (2, 3), (3, 2)])
     kept = local_call(
         kept_kernel,
@@ -464,8 +491,9 @@
         [],
         flops // 2,
         8 * 2**20,
+        20,
         "update_kept",
-    )(starts, by_col, back)
+    )(starts, table, back)
     over = (kept[0] + got[0].astype(jnp.float32)).astype(bf16)
     got_x = lax.ppermute(over, "led", [(0, 2), (2, 0), (1, 3), (3, 1)])
     own_part = lax.dynamic_slice_in_dim(spectrum, led_at * share, share, 2)

time: 134 us -> 136 us (1.015)
  the two profiles are of different devices: /device:TPU:14 before, /device:TPU:4 now
where the time goes in v4:
time: 136 us; the launch traced here: 135 us
  waiting for transfers between devices  45.4 us (33%)
  starting transfers between devices  41.3 us (30%)
  Pallas kernels  21.7 us (16%)
  local copies, waits for them, and re-layouts  19.9 us (15%)
  other arithmetic  6.89 us (5%)
    ppermute x12, starting transfers between devices, permute(): return lax.ppermute(sent, 'slab', pairs)  35 us
    ppermute x12, waiting for transfers between devices, permute(): return lax.ppermute(sent, 'slab', pairs)  33.8 us
    unnamed x32, local copies, waits for them, and re-layouts  17.2 us
    ppermute x1, waiting for transfers between devices, body_slabs(): got_x = lax.ppermute(over, 'led', [(0, 2), (2, 0), (1, 3), (3, 1)])  11.6 us
    pallas_call x2, Pallas kernels, rows_call(): local_call(functools.partial(rows_kernel, which), [sent_block] * count, [...  6.25 us
    pallas_call x1, Pallas kernels, body_slabs(): local_call(field_kernel, [sent_block] * HALF, [vmem] * 11, [pltpu.VMEM((w...  6.1 us
    all_to_all x1, starting transfers between devices, body_slabs(): lax.all_to_all(near_strips, 'slab', split_axis=0, concat_axis=0, axis_ind...  4.74 us
    pallas_call x1, Pallas kernels, body_slabs(): local_call(sent_kernel, [jax.ShapeDtypeStruct((2, 2, rows, share), bf16),...  3.78 us
  transfers between devices with their start and end apart: 15, of which 8 were waited for; matrix products, arithmetic and copies ran while one was open for 4% of the time, Pallas kernels for 5%

profile of v4, /device:TPU:4, one launch (start us, length us, event | category | flops | bytes accessed | tf_op | source)
XLA Modules:
  0.0 135.4 jit_solution(201618354977245049)
XLA Ops:
  0.0 0.7 pad_add_fusion.starts
  0.7 2.2 %copy-done.4 = f32[2,256,2048]{2,1,0:T(8,128)S(1)} copy-done((f32[2,256,2048]{2,1,0:T(8,128)S(1)}, f32[2,256,2048]{2,1,0:T(8,128)}, u32[]{:S(2)}) %copy-start.4) | copy-done | bytes 4194328
  2.9 1.4 windows.1.window
  4.3 0.8 copy-done
  5.1 2.6 %rows_round_1.1 = (bf16[4,256,128]{2,1,0:T(8,128)(2,1)}, bf16[4,256,128]{2,1,0:T(8,128)(2,1)}, bf16[4,256,128]{2,1,0:T(8,128)(2,1)}) custom-call(bf16[1024,1024]{1,0:T(8,128)(2,1)S(1)} %windows.1.window, bf16[8,256,1024]{2,1,0:T(8,128)(2,1)S(1)} %copy-done), custom_call_target="tpu_custom_call" | custom-call | flops 1610612736 | bytes 5242880 | tf_op jit(solution)/shard_map/rows_round_1/pallas_call | solution.py:401
  7.8 1.3 collective-permute-start
  9.1 1.3 collective-permute-start.1
  10.4 6.7 %collective-permute-start.2 = (bf16[4,256,128]{2,1,0:T(8,128)(2,1)}, bf16[4,256,128]{2,1,0:T(8,128)(2,1)S(1)}, u32[]{:S(2)}, u32[]{:S(2)}) collective-permute-start(bf16[4,256,128]{2,1,0:T(8,128)(2,1)} %get-tuple-element.34), channel_id=1, source_target_pairs={{4,12},{8,0},{12,4},{16,24},{20,28},{24,16},{5,13},{9,1},{13,5},{1... | collective-permute-start | bytes 786440 | tf_op jit(solution)/shard_map/ppermute | solution.py:414
  17.1 2.2 %copy-done.1 = bf16[8,256,1024]{2,1,0:T(8,128)(2,1)S(1)} copy-done((bf16[8,256,1024]{2,1,0:T(8,128)(2,1)S(1)}, bf16[8,256,1024]{2,1,0:T(8,128)(2,1)}, u32[]{:S(2)}) %copy-start.1) | copy-done | bytes 4194328
  19.2 3.6 %rows_round_2.1 = (bf16[4,256,128]{2,1,0:T(8,128)(2,1)S(1)}, bf16[4,256,128]{2,1,0:T(8,128)(2,1)S(1)}, bf16[4,256,128]{2,1,0:T(8,128)(2,1)S(1)}, bf16[4,256,128]{2,1,0:T(8,128)(2,1)}, bf16[4,256,128]{2,1,0:T(8,128)(2,1)S(1)}) custom-call(bf16[1024,1024]{1,0:T(8,128)(2,1)S(1)} %windows.1.window, bf16[8,256,1024]{2,1,0:T(8,128)(2,1)S(1)} %copy-done.1), custom_call_target="tpu_custom_call" | custom-call | flops 2684354560 | bytes 5242880 | tf_op jit(solution)/shard_map/rows_round_2/pallas_call | solution.py:401
  23.0 1.4 %collective-permute-start.7 = (bf16[4,256,128]{2,1,0:T(8,128)(2,1)S(1)}, bf16[4,256,128]{2,1,0:T(8,128)(2,1)S(1)}, u32[]{:S(2)}, u32[]{:S(2)}) collective-permute-start(bf16[4,256,128]{2,1,0:T(8,128)(2,1)S(1)} %get-tuple-element.42), channel_id=1, source_target_pairs={{8,28},{12,24},{16,4},{20,0},{9,29},{13,25},{17,5},{21,1},{10,30},... | collective-permute-start | bytes 786440 | tf_op jit(solution)/shard_map/ppermute | solution.py:414
  24.4 0.8 broadcast_select_fusion
  25.2 5.9 %collective-permute-start.6 = (bf16[4,256,128]{2,1,0:T(8,128)(2,1)}, bf16[4,256,128]{2,1,0:T(8,128)(2,1)S(1)}, u32[]{:S(2)}, u32[]{:S(2)}) collective-permute-start(bf16[4,256,128]{2,1,0:T(8,128)(2,1)} %broadcast_select_fusion), channel_id=1, source_target_pairs={{0,24},{4,28},{24,0},{28,4},{1,25},{5,29},{25,1},{29,5},{2,26},{6,... | collective-permute-start | bytes 786440 | tf_op jit(solution)/shard_map/ppermute | solution.py:414
  31.1 0.7 broadcast_select_fusion.1
  31.8 1.9 %collective-permute-start.3 = (bf16[4,256,128]{2,1,0:T(8,128)(2,1)}, bf16[4,256,128]{2,1,0:T(8,128)(2,1)S(1)}, u32[]{:S(2)}, u32[]{:S(2)}) collective-permute-start(bf16[4,256,128]{2,1,0:T(8,128)(2,1)} %get-tuple-element.36), channel_id=1, source_target_pairs={{4,0},{8,12},{12,8},{16,20},{20,16},{24,28},{5,1},{9,13},{13,9},{1... | collective-permute-start | bytes 786440 | tf_op jit(solution)/shard_map/ppermute | solution.py:414
  33.7 3.9 %collective-permute-start.4 = (bf16[4,256,128]{2,1,0:T(8,128)(2,1)S(1)}, bf16[4,256,128]{2,1,0:T(8,128)(2,1)}, u32[]{:S(2)}, u32[]{:S(2)}) collective-permute-start(bf16[4,256,128]{2,1,0:T(8,128)(2,1)S(1)} %get-tuple-element.38), channel_id=1, source_target_pairs={{4,8},{8,4},{12,0},{16,28},{20,24},{24,20},{5,9},{9,5},{13,1},{17,... | collective-permute-start | bytes 786440 | tf_op jit(solution)/shard_map/ppermute | solution.py:414
  37.7 1.2 sqrt.3
  38.9 1.6 %copy.7.amplitude = f32[1024,256]{1,0:T(8,128)S(1)} copy(f32[1024,256]{0,1:T(8,128)} %bitcast.9) | data formatting | bytes 2097152 | tf_op jit(solution)/shard_map/reshape | solution.py:437
  40.5 0.7 copy-done.7
  41.2 8.7 %collective-permute-done.5.rest_6_ = bf16[4,256,128]{2,1,0:T(8,128)(2,1)S(1)} collective-permute-done((bf16[4,256,128]{2,1,0:T(8,128)(2,1)}, bf16[4,256,128]{2,1,0:T(8,128)(2,1)S(1)}, u32[]{:S(2)}, u32[]{:S(2)}) %collective-permute-start.5) | collective-permute-done | bytes 262176 | tf_op jit(solution)/shard_map/ppermute | solution.py:414
  49.9 0.7 copy-done.9
  50.6 0.7 copy-done.5
  51.3 0.7 copy-done.11
  52.0 0.3 collective-permute-done.4.rest_3_
  52.3 2.2 %copy-done.2 = bf16[8,256,1024]{2,1,0:T(8,128)(2,1)S(1)} copy-done((bf16[8,256,1024]{2,1,0:T(8,128)(2,1)S(1)}, bf16[8,256,1024]{2,1,0:T(8,128)(2,1)}, u32[]{:S(2)}) %copy-start.2) | copy-done | bytes 4194328
  54.5 0.9 copy-done.6
  55.4 0.9 copy-done.8
  56.4 0.9 copy-done.10
  57.3 0.9 copy-done.12
  58.3 0.9 copy-done.14
  59.2 6.1 %modulus_step.1 = (bf16[4,256,128]{2,1,0:T(8,128)(2,1)S(1)}, bf16[4,256,128]{2,1,0:T(8,128)(2,1)S(1)}, bf16[4,256,128]{2,1,0:T(8,128)(2,1)S(1)}, bf16[4,256,128]{2,1,0:T(8,128)(2,1)S(1)}) custom-call(f32[1024,256]{1,0:T(8,128)S(1)} %copy.7.amplitude, bf16[8,256,1024]{2,1,0:T(8,128)(2,1)S(1)} %copy-done.2, bf16[4,256,128]{2,1,0:T(8,128)(2,1)S(1)} %copy-done.14, ...), custom_call_target="tpu_custom_call" | custom-call | flops 4294967296 | bytes 12582912 | tf_op jit(solution)/shard_map/modulus_step/pallas_call | solution.py:438
  65.3 1.1 near_strips.1
  66.4 4.7 %all-to-all-start = ((bf16[4,4,256,128]{3,2,1,0:T(8,128)(2,1)}), bf16[4,4,256,128]{3,2,1,0:T(8,128)(2,1)S(1)}, u32[]{:S(2)}, u32[]{:S(2)}) async-start(bf16[4,4,256,128]{3,2,1,0:T(8,128)(2,1)} %near_strips.1), calls=%async_computation | async-start | bytes 2097152 | tf_op jit(solution)/shard_map/all_to_all | solution.py:464
  71.1 1.3 collective-permute-start.10
  72.4 5.5 %collective-permute-start.11 = (bf16[4,256,128]{2,1,0:T(8,128)(2,1)S(1)}, bf16[4,256,128]{2,1,0:T(8,128)(2,1)S(1)}, u32[]{:S(2)}, u32[]{:S(2)}) collective-permute-start(bf16[4,256,128]{2,1,0:T(8,128)(2,1)S(1)} %get-tuple-element.46.refs_3_), channel_id=1, source_target_pairs={{4,24},{8,20},{12,16},{16,12},{20,8},{24,4},{5,25},{9,21},{13,17},... | collective-permute-start | bytes 786440 | tf_op jit(solution)/shard_map/ppermute | solution.py:414
  77.9 2.9 %collective-permute-start.8 = (bf16[4,256,128]{2,1,0:T(8,128)(2,1)S(1)}, bf16[4,256,128]{2,1,0:T(8,128)(2,1)S(1)}, u32[]{:S(2)}, u32[]{:S(2)}) collective-permute-start(bf16[4,256,128]{2,1,0:T(8,128)(2,1)S(1)} %get-tuple-element.43.refs_0_), channel_id=1, source_target_pairs={{0,16},{4,20},{8,24},{20,4},{24,8},{28,12},{1,17},{5,21},{9,25},{2... | collective-permute-start | bytes 786440 | tf_op jit(solution)/shard_map/ppermute | solution.py:414
  80.8 2.9 %collective-permute-start.9 = (bf16[4,256,128]{2,1,0:T(8,128)(2,1)S(1)}, bf16[4,256,128]{2,1,0:T(8,128)(2,1)S(1)}, u32[]{:S(2)}, u32[]{:S(2)}) collective-permute-start(bf16[4,256,128]{2,1,0:T(8,128)(2,1)S(1)} %get-tuple-element.44.refs_1_), channel_id=1, source_target_pairs={{0,20},{4,16},{12,24},{16,4},{24,12},{28,8},{1,21},{5,17},{13,25},... | collective-permute-start | bytes 786440 | tf_op jit(solution)/shard_map/ppermute | solution.py:414
  83.7 9.5 %collective-permute-done.10.rest_2_ = bf16[4,256,128]{2,1,0:T(8,128)(2,1)S(1)} collective-permute-done((bf16[4,256,128]{2,1,0:T(8,128)(2,1)S(1)}, bf16[4,256,128]{2,1,0:T(8,128)(2,1)S(1)}, u32[]{:S(2)}, u32[]{:S(2)}) %collective-permute-start.10) | collective-permute-done | bytes 262176 | tf_op jit(solution)/shard_map/ppermute | solution.py:414
  93.4 14.7 %collective-permute-done.8.rest_0_ = bf16[4,256,128]{2,1,0:T(8,128)(2,1)S(1)} collective-permute-done((bf16[4,256,128]{2,1,0:T(8,128)(2,1)S(1)}, bf16[4,256,128]{2,1,0:T(8,128)(2,1)S(1)}, u32[]{:S(2)}, u32[]{:S(2)}) %collective-permute-start.8) | collective-permute-done | bytes 262176 | tf_op jit(solution)/shard_map/ppermute | solution.py:414
  108.1 0.3 collective-permute-done.9.rest_1_
  108.4 2.2 %copy-done.3 = bf16[8,256,1024]{2,1,0:T(8,128)(2,1)S(1)} copy-done((bf16[8,256,1024]{2,1,0:T(8,128)(2,1)S(1)}, bf16[8,256,1024]{2,1,0:T(8,128)(2,1)}, u32[]{:S(2)}) %copy-start.3) | copy-done | bytes 4194328
  110.6 3.8 %update_sent.1 = (bf16[2,2,256,512]{3,2,1,0:T(8,128)(2,1)S(1)}, bf16[1024,1024]{1,0:T(8,128)(2,1)S(1)}) custom-call(s32[4]{0:T(128)S(1)} %pad_add_fusion.starts, bf16[8,256,1024]{2,1,0:T(8,128)(2,1)S(1)} %copy-done.3, bf16[4,4,256,128]{3,2,1,0:T(8,128)(2,1)S(1)} %all-to-all-done.near, bf16[4,256,128]{2,1,0:T(8,128)(2,1)S(1)} %collective-permute-done.8.rest_0_, ...), custom_call_target="tpu_custom_call" | custom-call | flops 2147483648 | bytes 8388608 | tf_op jit(solution)/shard_map/update_sent/pallas_call | solution.py:473
  114.4 3.2 %update_kept.1 = f32[2,2,256,512]{3,2,1,0:T(8,128)S(1)} custom-call(s32[4]{0:T(128)S(1)} %pad_add_fusion.starts, bf16[8,256,1024]{2,1,0:T(8,128)(2,1)S(1)} %copy-done.3, bf16[1024,1024]{1,0:T(8,128)(2,1)S(1)} %get-tuple-element.47.back), custom_call_target="tpu_custom_call" | custom-call | flops 2147483648 | bytes 8388608 | tf_op jit(solution)/shard_map/update_kept/pallas_call | solution.py:487
  117.6 1.0 fusion.3
  118.6 1.5 %collective-permute-start.13 = (bf16[2,256,512]{2,1,0:T(8,128)(2,1)}, bf16[2,256,512]{2,1,0:T(8,128)(2,1)}, u32[]{:S(2)}, u32[]{:S(2)}) collective-permute-start(bf16[2,256,512]{2,1,0:T(8,128)(2,1)} %fusion.3), channel_id=1, source_target_pairs={{0,2},{2,0},{1,3},{3,1},{4,6},{6,4},{5,7},{7,5},{8,10},{10,8},{9,1... | collective-permute-start | bytes 1572872 | tf_op jit(solution)/shard_map/ppermute | solution.py:498
  120.1 1.5 %fusion.2 = f32[2,256,512]{2,1,0:T(8,128)S(1)} fusion(f32[2,2,256,512]{3,2,1,0:T(8,128)S(1)} %update_kept.1, f32[2,256,2048]{2,1,0:T(8,128)} %spectrum.1, s32[]{:T(128)S(6)} %select_n.15, bf16[2,2,256,512]{3,2,1,0:T(8,128)(2,1)S(1)} %collective-permute-done.12), kind=kLoop, calls=%fused_computation.4 | loop fusion | flops 786432 | bytes 3670020 | tf_op jit(solution)/shard_map/add | solution.py:500
  121.6 11.6 %collective-permute-done.13 = bf16[2,256,512]{2,1,0:T(8,128)(2,1)} collective-permute-done((bf16[2,256,512]{2,1,0:T(8,128)(2,1)}, bf16[2,256,512]{2,1,0:T(8,128)(2,1)}, u32[]{:S(2)}, u32[]{:S(2)}) %collective-permute-start.13) | collective-permute-done | bytes 524320 | tf_op jit(solution)/shard_map/ppermute | solution.py:498
  133.2 2.2 %convert_add_fusion = f32[2,256,512]{2,1,0:T(8,128)} fusion(f32[2,256,512]{2,1,0:T(8,128)S(1)} %fusion.2, bf16[2,256,512]{2,1,0:T(8,128)(2,1)} %collective-permute-done.13), kind=kLoop, calls=%fused_computation.5 | loop fusion | flops 524288 | bytes 2621440 | tf_op jit(solution)/shard_map/add | solution.py:502
  (29 shorter events, 0.4 us)
Async XLA Ops:
  0.7 2.2 %copy-start.4 = (f32[2,256,2048]{2,1,0:T(8,128)S(1)}, f32[2,256,2048]{2,1,0:T(8,128)}, u32[]{:S(2)}) copy-start(f32[2,256,2048]{2,1,0:T(8,128)} %spectrum.1) | copy-start | bytes 12582916
  2.9 2.2 %copy-start = (bf16[8,256,1024]{2,1,0:T(8,128)(2,1)S(1)}, bf16[8,256,1024]{2,1,0:T(8,128)(2,1)}, u32[]{:S(2)}) copy-start(bf16[8,256,1024]{2,1,0:T(8,128)(2,1)} %constant.19.clone.table) | copy-start | bytes 12582916
  7.8 15.1 %collective-permute-start = (bf16[4,256,128]{2,1,0:T(8,128)(2,1)}, bf16[4,256,128]{2,1,0:T(8,128)(2,1)S(1)}, u32[]{:S(2)}, u32[]{:S(2)}) collective-permute-start(bf16[4,256,128]{2,1,0:T(8,128)(2,1)} %get-tuple-element.29), channel_id=1, source_target_pairs={{8,16},{12,20},{16,8},{20,12},{4,0},{24,28},{9,17},{13,21},{17,9},... | collective-permute-start | bytes 786440 | tf_op jit(solution)/shard_map/ppermute | solution.py:414
  9.1 13.8 %collective-permute-start.1 = (bf16[4,256,128]{2,1,0:T(8,128)(2,1)}, bf16[4,256,128]{2,1,0:T(8,128)(2,1)S(1)}, u32[]{:S(2)}, u32[]{:S(2)}) collective-permute-start(bf16[4,256,128]{2,1,0:T(8,128)(2,1)} %get-tuple-element.30), channel_id=1, source_target_pairs={{8,20},{12,16},{16,12},{20,8},{4,0},{24,28},{9,21},{13,17},{17,13}... | collective-permute-start | bytes 786440 | tf_op jit(solution)/shard_map/ppermute | solution.py:414
  10.4 12.6 %collective-permute-start.2 = (bf16[4,256,128]{2,1,0:T(8,128)(2,1)}, bf16[4,256,128]{2,1,0:T(8,128)(2,1)S(1)}, u32[]{:S(2)}, u32[]{:S(2)}) collective-permute-start(bf16[4,256,128]{2,1,0:T(8,128)(2,1)} %get-tuple-element.34), channel_id=1, source_target_pairs={{4,12},{8,0},{12,4},{16,24},{20,28},{24,16},{5,13},{9,1},{13,5},{1... | collective-permute-start | bytes 786440 | tf_op jit(solution)/shard_map/ppermute | solution.py:414
  17.1 2.2 %copy-start.1 = (bf16[8,256,1024]{2,1,0:T(8,128)(2,1)S(1)}, bf16[8,256,1024]{2,1,0:T(8,128)(2,1)}, u32[]{:S(2)}) copy-start(bf16[8,256,1024]{2,1,0:T(8,128)(2,1)} %constant.19.clone.table) | copy-start | bytes 12582916
  22.9 16.0 %copy-start.13 = (bf16[4,256,128]{2,1,0:T(8,128)(2,1)}, bf16[4,256,128]{2,1,0:T(8,128)(2,1)S(1)}, u32[]{:S(2)}) copy-start(bf16[4,256,128]{2,1,0:T(8,128)(2,1)S(1)} %get-tuple-element.28.rest_0_) | copy-start | bytes 786436
  22.9 14.8 %copy-start.15 = (f32[2,128,1024]{2,1,0:T(8,128)S(1)}, f32[2,128,1024]{2,1,0:T(8,128)}, u32[]{:S(2)}) copy-start(f32[2,128,1024]{2,1,0:T(8,128)} %param.8) | copy-start | bytes 3145732
  23.0 27.6 %collective-permute-start.7 = (bf16[4,256,128]{2,1,0:T(8,128)(2,1)S(1)}, bf16[4,256,128]{2,1,0:T(8,128)(2,1)S(1)}, u32[]{:S(2)}, u32[]{:S(2)}) collective-permute-start(bf16[4,256,128]{2,1,0:T(8,128)(2,1)S(1)} %get-tuple-element.42), channel_id=1, source_target_pairs={{8,28},{12,24},{16,4},{20,0},{9,29},{13,25},{17,5},{21,1},{10,30},... | collective-permute-start | bytes 786440 | tf_op jit(solution)/shard_map/ppermute | solution.py:414
  25.2 15.3 %collective-permute-start.6 = (bf16[4,256,128]{2,1,0:T(8,128)(2,1)}, bf16[4,256,128]{2,1,0:T(8,128)(2,1)S(1)}, u32[]{:S(2)}, u32[]{:S(2)}) collective-permute-start(bf16[4,256,128]{2,1,0:T(8,128)(2,1)} %broadcast_select_fusion), channel_id=1, source_target_pairs={{0,24},{4,28},{24,0},{28,4},{1,25},{5,29},{25,1},{29,5},{2,26},{6,... | collective-permute-start | bytes 786440 | tf_op jit(solution)/shard_map/ppermute | solution.py:414
  31.8 18.1 %collective-permute-start.5 = (bf16[4,256,128]{2,1,0:T(8,128)(2,1)}, bf16[4,256,128]{2,1,0:T(8,128)(2,1)S(1)}, u32[]{:S(2)}, u32[]{:S(2)}) collective-permute-start(bf16[4,256,128]{2,1,0:T(8,128)(2,1)} %broadcast_select_fusion.1), channel_id=1, source_target_pairs={{0,16},{4,20},{8,24},{12,28},{16,0},{20,4},{24,8},{28,12},{1,17},{... | collective-permute-start | bytes 786440 | tf_op jit(solution)/shard_map/ppermute | solution.py:414
  31.8 19.5 %collective-permute-start.3 = (bf16[4,256,128]{2,1,0:T(8,128)(2,1)}, bf16[4,256,128]{2,1,0:T(8,128)(2,1)S(1)}, u32[]{:S(2)}, u32[]{:S(2)}) collective-permute-start(bf16[4,256,128]{2,1,0:T(8,128)(2,1)} %get-tuple-element.36), channel_id=1, source_target_pairs={{4,0},{8,12},{12,8},{16,20},{20,16},{24,28},{5,1},{9,13},{13,9},{1... | collective-permute-start | bytes 786440 | tf_op jit(solution)/shard_map/ppermute | solution.py:414
  33.7 18.6 %collective-permute-start.4 = (bf16[4,256,128]{2,1,0:T(8,128)(2,1)S(1)}, bf16[4,256,128]{2,1,0:T(8,128)(2,1)}, u32[]{:S(2)}, u32[]{:S(2)}) collective-permute-start(bf16[4,256,128]{2,1,0:T(8,128)(2,1)S(1)} %get-tuple-element.38), channel_id=1, source_target_pairs={{4,8},{8,4},{12,0},{16,28},{20,24},{24,20},{5,9},{9,5},{13,1},{17,... | collective-permute-start | bytes 786440 | tf_op jit(solution)/shard_map/ppermute | solution.py:414
  40.5 0.7 copy-start.7
  49.9 0.7 copy-start.9
  50.6 0.7 copy-start.5
  51.3 0.7 copy-start.11
  52.3 2.2 %copy-start.2 = (bf16[8,256,1024]{2,1,0:T(8,128)(2,1)S(1)}, bf16[8,256,1024]{2,1,0:T(8,128)(2,1)}, u32[]{:S(2)}) copy-start(bf16[8,256,1024]{2,1,0:T(8,128)(2,1)} %constant.19.clone.table) | copy-start | bytes 12582916
  54.5 0.9 copy-start.6
  55.4 0.9 copy-start.8
  56.4 0.9 copy-start.10
  57.3 0.9 copy-start.12
  58.3 0.9 copy-start.14
  66.4 42.0 %all-to-all-start = ((bf16[4,4,256,128]{3,2,1,0:T(8,128)(2,1)}), bf16[4,4,256,128]{3,2,1,0:T(8,128)(2,1)S(1)}, u32[]{:S(2)}, u32[]{:S(2)}) async-start(bf16[4,4,256,128]{3,2,1,0:T(8,128)(2,1)} %near_strips.1), calls=%async_computation | async-start | bytes 2097152 | tf_op jit(solution)/shard_map/all_to_all | solution.py:464
  71.1 22.1 %collective-permute-start.10 = (bf16[4,256,128]{2,1,0:T(8,128)(2,1)S(1)}, bf16[4,256,128]{2,1,0:T(8,128)(2,1)S(1)}, u32[]{:S(2)}, u32[]{:S(2)}) collective-permute-start(bf16[4,256,128]{2,1,0:T(8,128)(2,1)S(1)} %get-tuple-element.45.refs_2_), channel_id=1, source_target_pairs={{0,24},{8,16},{12,20},{16,8},{20,12},{28,4},{1,25},{9,17},{13,21},... | collective-permute-start | bytes 786440 | tf_op jit(solution)/shard_map/ppermute | solution.py:414
  72.4 21.0 %collective-permute-start.11 = (bf16[4,256,128]{2,1,0:T(8,128)(2,1)S(1)}, bf16[4,256,128]{2,1,0:T(8,128)(2,1)S(1)}, u32[]{:S(2)}, u32[]{:S(2)}) collective-permute-start(bf16[4,256,128]{2,1,0:T(8,128)(2,1)S(1)} %get-tuple-element.46.refs_3_), channel_id=1, source_target_pairs={{4,24},{8,20},{12,16},{16,12},{20,8},{24,4},{5,25},{9,21},{13,17},... | collective-permute-start | bytes 786440 | tf_op jit(solution)/shard_map/ppermute | solution.py:414
  77.9 30.2 %collective-permute-start.8 = (bf16[4,256,128]{2,1,0:T(8,128)(2,1)S(1)}, bf16[4,256,128]{2,1,0:T(8,128)(2,1)S(1)}, u32[]{:S(2)}, u32[]{:S(2)}) collective-permute-start(bf16[4,256,128]{2,1,0:T(8,128)(2,1)S(1)} %get-tuple-element.43.refs_0_), channel_id=1, source_target_pairs={{0,16},{4,20},{8,24},{20,4},{24,8},{28,12},{1,17},{5,21},{9,25},{2... | collective-permute-start | bytes 786440 | tf_op jit(solution)/shard_map/ppermute | solution.py:414
  80.8 27.6 %collective-permute-start.9 = (bf16[4,256,128]{2,1,0:T(8,128)(2,1)S(1)}, bf16[4,256,128]{2,1,0:T(8,128)(2,1)S(1)}, u32[]{:S(2)}, u32[]{:S(2)}) collective-permute-start(bf16[4,256,128]{2,1,0:T(8,128)(2,1)S(1)} %get-tuple-element.44.refs_1_), channel_id=1, source_target_pairs={{0,20},{4,16},{12,24},{16,4},{24,12},{28,8},{1,21},{5,17},{13,25},... | collective-permute-start | bytes 786440 | tf_op jit(solution)/shard_map/ppermute | solution.py:414
  108.4 2.2 %copy-start.3 = (bf16[8,256,1024]{2,1,0:T(8,128)(2,1)S(1)}, bf16[8,256,1024]{2,1,0:T(8,128)(2,1)}, u32[]{:S(2)}) copy-start(bf16[8,256,1024]{2,1,0:T(8,128)(2,1)} %constant.19.clone.table) | copy-start | bytes 12582916
  114.4 3.3 %collective-permute-start.12 = (bf16[2,2,256,512]{3,2,1,0:T(8,128)(2,1)S(1)}, bf16[2,2,256,512]{3,2,1,0:T(8,128)(2,1)S(1)}, u32[]{:S(2)}, u32[]{:S(2)}) collective-permute-start(bf16[2,2,256,512]{3,2,1,0:T(8,128)(2,1)S(1)} %get-tuple-element.48), channel_id=1, source_target_pairs={{0,1},{1,0},{2,3},{3,2},{4,5},{5,4},{6,7},{7,6},{8,9},{9,8},{10,11... | collective-permute-start | bytes 3145736 | tf_op jit(solution)/shard_map/ppermute | solution.py:486
  118.6 14.6 %collective-permute-start.13 = (bf16[2,256,512]{2,1,0:T(8,128)(2,1)}, bf16[2,256,512]{2,1,0:T(8,128)(2,1)}, u32[]{:S(2)}, u32[]{:S(2)}) collective-permute-start(bf16[2,256,512]{2,1,0:T(8,128)(2,1)} %fusion.3), channel_id=1, source_target_pairs={{0,2},{2,0},{1,3},{3,1},{4,6},{6,4},{5,7},{7,5},{8,10},{10,8},{9,1... | collective-permute-start | bytes 1572872 | tf_op jit(solution)/shard_map/ppermute | solution.py:498

commit v5 on v3

--- a/solution.py
+++ b/solution.py
@@ -200,22 +200,42 @@
             window[at : at + rows, :] = jnp.where(inside, value, 0.0).astype(jnp.bfloat16)
 
 
-def far_kernel(window, table, *outs):
+def classes_of(position):
+    hands_over = is_one_of(position, PASSED)
+    return (jnp.where(hands_over, 5, 6), 7, 2, 4, jnp.where(hands_over, 6, 5), 0, 1, 3)
+
+
+def rows_kernel(which, window, table, *outs):
     position = lax.axis_index("slab")
-    hands_over = is_one_of(position, PASSED)
-    classes = (jnp.where(hands_over, 5, 6), 7, 2, 4, jnp.where(hands_over, 6, 5))
-    for out, d in zip(outs, classes):
+    for out, d in zip(outs, classes_of(position)[which]):
         store_parts(out, row_block(window[...], table[jnp.bitwise_xor(position, d)]))
 
 
-def near_kernel(window, table, *outs):
-    position = lax.axis_index("slab")
-    for out, d in zip(outs, (0, 1, 3)):
-        store_parts(out, row_block(window[...], table[jnp.bitwise_xor(position, d)]))
+def choose_kernel(got_a, got_b, own_a, own_b, out_a, out_b):
+    passes = is_one_of(lax.axis_index("slab"), PASSED.values())
+
+    @pl.when(passes)
+    def _():
+        out_a[...] = got_a[...]
+        out_b[...] = got_b[...]
+
+    @pl.when(jnp.logical_not(passes))
+    def _():
+        out_a[...] = own_a[...]
+        out_b[...] = own_b[...]
+
+
+def amplitude_kernel(images, table, out, table_out):
+    leds, block, width = images.shape
+    for led in range(leds):
+        for j in range(width // LANES):
+            piece = jnp.sqrt(images[led, :, j * LANES : (j + 1) * LANES])
+            out[j * LANES : (j + 1) * LANES, led * block : (led + 1) * block] = piece.T
+    table_out[...] = table[...]
 
 
 def field_kernel(amplitude, table, *rest):
-    near, far = rest[:HALF], rest[HALF : HALF + 5]
+    far, near = rest[:5], rest[5 : HALF + 5]
     outs = rest[HALF + 5 : 2 * HALF + 5]
     field_in, diff, strips = rest[2 * HALF + 5 :]
     position = lax.axis_index("slab")
@@ -282,7 +302,7 @@
                 strips[i, part, here, :] = back_re[:, cols]
                 strips[i, parts // 2 + part, here, :] = back_im[:, cols]
     for d, out in enumerate(outs):
-        out[...] = strips[jnp.bitwise_and(jnp.bitwise_xor(position, d), HALF - 1)]
+        out[...] = strips[jnp.bitwise_and(position + d, HALF - 1)]
 
 
 def update_columns(first_step, last_step, starts, table, back, out):
@@ -328,7 +348,7 @@
     parts, rows, _ = blocks[0].shape
     half = back.shape[1] // LANES // 2
     for d, block in enumerate(blocks):
-        at = pl.multiple_of(jnp.bitwise_xor(position, d) * LANES, LANES)
+        at = pl.multiple_of(lax.rem(position + SLABS - d, SLABS) * LANES, LANES)
         for part in range(parts):
             back[part * rows : (part + 1) * rows, pl.ds(at, LANES)] = block[part]
     update_columns(0, half, starts, table, back, out)
@@ -382,15 +402,20 @@
         6 * 2**20,
         "windows",
     )(starts, spectrum)
-    first_a, first_b, near_2, second_a, second_b = local_call(
-        far_kernel,
-        [sent_block] * 5,
-        [vmem, vmem],
-        [],
-        flops * 5 // 8,
-        5 * 2**20,
-        "far_rows",
-    )(window, by_col)
+
+    def rows_call(which, name):
+        count = which.stop - which.start
+        return local_call(
+            functools.partial(rows_kernel, which),
+            [sent_block] * count,
+            [vmem, vmem],
+            [],
+            flops * count // SLABS,
+            5 * 2**20,
+            name,
+        )(window, by_col)
+
+    first_a, first_b, near_2 = rows_call(slice(0, 3), "rows_round_1")
 
     def permute(sent, pairs):
         return lax.ppermute(sent, "slab", pairs)
@@ -400,31 +425,43 @@
     got_a = permute(first_a, [(s, s ^ 6) for s in INNER] + handed)
     got_b = permute(first_b, [(s, s ^ 7) for s in INNER] + handed)
     near_2 = permute(near_2, [(s, s ^ 2) for s in windowed])
-    near_0, near_1, near_3 = local_call(
-        near_kernel,
-        [sent_block] * 3,
-        [vmem, vmem],
+    second_a, second_b, near_0, near_1, near_3 = rows_call(slice(3, SLABS), "rows_round_2")
+    inner_b = second_b
+    second_a, second_b = local_call(
+        choose_kernel,
+        [sent_block] * 2,
+        [vmem] * 4,
         [],
-        flops * 3 // 8,
-        5 * 2**20,
-        "near_rows",
-    )(window, by_col)
-    got_a, got_b, second_a, second_b, near_1, near_2, near_3 = lax.optimization_barrier(
-        (got_a, got_b, second_a, second_b, near_1, near_2, near_3)
-    )
-    passes = is_one_of(lax.axis_index("slab"), PASSED.values())
+        0,
+        2**20,
+        "round_2_blocks",
+    )(got_a, got_b, second_a, second_b)
+    second_a, second_b, inner_b, near_1, near_2, near_3, images = lax.optimization_barrier(
+        (second_a, second_b, inner_b, near_1, near_2, near_3, images)
+    )
     outer_pairs = [(s, s ^ 6) for s in range(SLABS) if s not in INNER]
     far_columns = [
         got_a,
         got_b,
-        permute(jnp.where(passes, got_a, second_a), [(s, s ^ 4) for s in range(SLABS)]),
-        permute(jnp.where(passes, got_b, second_b), outer_pairs),
-        permute(second_b, [(s, s ^ 5) for s in INNER]),
+        permute(second_a, [(s, s ^ 4) for s in range(SLABS)]),
+        permute(second_b, outer_pairs),
+        permute(inner_b, [(s, s ^ 5) for s in INNER]),
     ]
     near_1 = permute(near_1, [(s, s ^ 1) for s in windowed])
     near_3 = permute(near_3, [(s, s ^ 3) for s in windowed])
     near_columns = [near_0, near_1, near_2, near_3]
-    amplitude = jnp.sqrt(images).transpose(2, 0, 1).reshape(width, leds * block)
+    amplitude, by_row = local_call(
+        amplitude_kernel,
+        [
+            jax.ShapeDtypeStruct((width, leds * block), jnp.float32),
+            jax.ShapeDtypeStruct(by_row.shape, bf16),
+        ],
+        [vmem] * 2,
+        [],
+        0,
+        10 * 2**20,
+        "amplitude",
+    )(images, by_row)
     strips = local_call(
         field_kernel,
         [sent_block] * HALF,
@@ -434,15 +471,20 @@
         16 * leds * block * width * width,
         12 * 2**20,
         "modulus_step",
-    )(amplitude, by_row, *near_columns, *far_columns)
-
-    def send_home(sent, d):
-        return permute(sent, [(s, s ^ d) for s in range(SLABS) if FIRST < s ^ d < LAST])
-
-    far_home = [send_home(strips[d % HALF], d) for d in CROSS]
-    far_home[0], *late_strips = lax.optimization_barrier((far_home[0], *strips[1:]))
-    near_home = [send_home(sent, d) for d, sent in enumerate(late_strips, 1)]
-    home = [strips[0], *near_home, *far_home]
+    )(amplitude, by_row, *far_columns, *near_columns)
+
+    def send_home(d):
+        pairs = [(s, (s + d) % SLABS) for s in range(SLABS) if FIRST < (s + d) % SLABS < LAST]
+        return permute(strips[d % HALF], pairs)
+
+    strips = list(strips)
+    home = {0: strips[0]}
+    for d in (4, 5, 1, 6, 2):
+        home[d] = send_home(d)
+    for d, before in ((7, 4), (3, 5)):
+        home[before], strips[3] = lax.optimization_barrier((home[before], strips[3]))
+        home[d] = send_home(d)
+    home = [home[d] for d in range(SLABS)]
     share = width // 2
     sent, back = local_call(
         sent_kernel,

time: 134 us -> 130 us (0.970)
  the two profiles are of different devices: /device:TPU:14 before, /device:TPU:8 now
where the time goes in v5:
time: 130 us; the launch traced here: 129 us
  waiting for transfers between devices  56.5 us (43%)
  starting transfers between devices  46 us (35%)
  Pallas kernels  18.7 us (14%)
  other arithmetic  5.53 us (4%)
  local copies, waits for them, and re-layouts  2.4 us (2%)
    ppermute x15, waiting for transfers between devices, permute(): return lax.ppermute(sent, 'slab', pairs)  44.8 us
    ppermute x15, starting transfers between devices, permute(): return lax.ppermute(sent, 'slab', pairs)  44.5 us
    ppermute x1, waiting for transfers between devices, body_slabs(): got_x = lax.ppermute(over, 'led', [(0, 2), (2, 0), (1, 3), (3, 1)])  11.7 us
    pallas_call x1, Pallas kernels, body_slabs(): local_call(field_kernel, [sent_block] * HALF, [vmem] * 11, [pltpu.VMEM((w...  5.15 us
    pallas_call x2, Pallas kernels, rows_call(): local_call(functools.partial(rows_kernel, which), [sent_block] * count, [...  4.69 us
    pallas_call x1, Pallas kernels, body_slabs(): local_call(sent_kernel, [jax.ShapeDtypeStruct((2, 2, rows, share), bf16),...  3.83 us
    pallas_call x1, Pallas kernels, body_slabs(): local_call(kept_kernel, jax.ShapeDtypeStruct((2, 2, rows, share), jnp.flo...  3.12 us
  transfers between devices with their start and end apart: 17, of which 10 were waited for; matrix products, arithmetic and copies ran while one was open for 1% of the time, Pallas kernels for 5%

profile of v5, /device:TPU:8, one launch (start us, length us, event | category | flops | bytes accessed | tf_op | source)
XLA Modules:
  0.0 129.5 jit_solution(16233147832092598685)
XLA Ops:
  0.0 0.9 pad_add_fusion.starts
  0.9 2.4 %copy-done.1 = f32[2,256,2048]{2,1,0:T(8,128)S(1)} copy-done((f32[2,256,2048]{2,1,0:T(8,128)S(1)}, f32[2,256,2048]{2,1,0:T(8,128)}, u32[]{:S(2)}) %copy-start.1) | copy-done | bytes 4194328
  3.3 1.4 %windows.1.window = bf16[1024,1024]{1,0:T(8,128)(2,1)S(1)} custom-call(s32[4]{0:T(128)S(1)} %pad_add_fusion.starts, f32[2,256,2048]{2,1,0:T(8,128)S(1)} %copy-done.1), custom_call_target="tpu_custom_call" | custom-call | bytes 6291456 | tf_op jit(solution)/shard_map/windows/pallas_call | solution.py:396
  4.7 1.8 %rows_round_1.1 = (bf16[4,256,128]{2,1,0:T(8,128)(2,1)S(1)}, bf16[4,256,128]{2,1,0:T(8,128)(2,1)S(1)}, bf16[4,256,128]{2,1,0:T(8,128)(2,1)S(1)}) custom-call(bf16[1024,1024]{1,0:T(8,128)(2,1)S(1)} %windows.1.window, bf16[8,1024,256]{2,1,0:T(8,128)(2,1)S(1)} %copy-done), custom_call_target="tpu_custom_call" | custom-call | flops 1610612736 | bytes 5242880 | tf_op jit(solution)/shard_map/rows_round_1/pallas_call | solution.py:408
  6.5 3.5 %collective-permute-start = (bf16[4,256,128]{2,1,0:T(8,128)(2,1)S(1)}, bf16[4,256,128]{2,1,0:T(8,128)(2,1)S(1)}, u32[]{:S(2)}, u32[]{:S(2)}) collective-permute-start(bf16[4,256,128]{2,1,0:T(8,128)(2,1)S(1)} %get-tuple-element.36), channel_id=1, source_target_pairs={{8,16},{12,20},{16,8},{20,12},{4,0},{24,28},{9,17},{13,21},{17,9},... | collective-permute-start | bytes 786440 | tf_op jit(solution)/shard_map/ppermute | solution.py:421
  10.0 3.3 %collective-permute-start.1 = (bf16[4,256,128]{2,1,0:T(8,128)(2,1)S(1)}, bf16[4,256,128]{2,1,0:T(8,128)(2,1)S(1)}, u32[]{:S(2)}, u32[]{:S(2)}) collective-permute-start(bf16[4,256,128]{2,1,0:T(8,128)(2,1)S(1)} %get-tuple-element.37), channel_id=1, source_target_pairs={{8,20},{12,16},{16,12},{20,8},{4,0},{24,28},{9,21},{13,17},{17,13}... | collective-permute-start | bytes 786440 | tf_op jit(solution)/shard_map/ppermute | solution.py:421
  13.3 0.0 copy-start.2
  13.3 0.0 copy-start.3
  13.3 1.6 %collective-permute-start.2 = (bf16[4,256,128]{2,1,0:T(8,128)(2,1)S(1)}, bf16[4,256,128]{2,1,0:T(8,128)(2,1)S(1)}, u32[]{:S(2)}, u32[]{:S(2)}) collective-permute-start(bf16[4,256,128]{2,1,0:T(8,128)(2,1)S(1)} %get-tuple-element.43), channel_id=1, source_target_pairs={{4,12},{8,0},{12,4},{16,24},{20,28},{24,16},{5,13},{9,1},{13,5},{1... | collective-permute-start | bytes 786440 | tf_op jit(solution)/shard_map/ppermute | solution.py:421
  14.9 2.9 %rows_round_2.1 = (bf16[4,256,128]{2,1,0:T(8,128)(2,1)S(1)}, bf16[4,256,128]{2,1,0:T(8,128)(2,1)S(1)}, bf16[4,256,128]{2,1,0:T(8,128)(2,1)S(1)}, bf16[4,256,128]...) custom-call(bf16[1024,1024]{1,0:T(8,128)(2,1)S(1)} %windows.1.window, bf16[8,1024,256]{2,1,0:T(8,128)(2,1)S(1)} %copy-done), custom_call_target="tpu_custom_call" | custom-call | flops 2684354560 | bytes 5242880 | tf_op jit(solution)/shard_map/rows_round_2/pallas_call | solution.py:408
  17.8 0.0 collective-permute-done.got_a.rest_0_
  17.8 5.2 %collective-permute-done.1.got_b.rest_1_ = bf16[4,256,128]{2,1,0:T(8,128)(2,1)S(1)} collective-permute-done((bf16[4,256,128]{2,1,0:T(8,128)(2,1)S(1)}, bf16[4,256,128]{2,1,0:T(8,128)(2,1)S(1)}, u32[]{:S(2)}, u32[]{:S(2)}) %collective-permute-start.1) | collective-permute-done | bytes 262176 | tf_op jit(solution)/shard_map/ppermute | solution.py:421
  23.0 0.0 collective-permute-done.2.rest_7_
  23.0 1.4 %collective-permute-start.3 = (bf16[4,256,128]{2,1,0:T(8,128)(2,1)S(1)}, bf16[4,256,128]{2,1,0:T(8,128)(2,1)S(1)}, u32[]{:S(2)}, u32[]{:S(2)}) collective-permute-start(bf16[4,256,128]{2,1,0:T(8,128)(2,1)S(1)} %get-tuple-element.48), channel_id=1, source_target_pairs={{0,16},{4,20},{8,24},{12,28},{16,0},{20,4},{24,8},{28,12},{1,17},{... | collective-permute-start | bytes 786440 | tf_op jit(solution)/shard_map/ppermute | solution.py:421
  24.4 0.7 collective-permute-start.4
  25.1 7.2 %collective-permute-start.5 = (bf16[4,256,128]{2,1,0:T(8,128)(2,1)S(1)}, bf16[4,256,128]{2,1,0:T(8,128)(2,1)S(1)}, u32[]{:S(2)}, u32[]{:S(2)}) collective-permute-start(bf16[4,256,128]{2,1,0:T(8,128)(2,1)S(1)} %get-tuple-element.50.own_b), channel_id=1, source_target_pairs={{8,28},{12,24},{16,4},{20,0},{9,29},{13,25},{17,5},{21,1},{10,30},... | collective-permute-start | bytes 786440 | tf_op jit(solution)/shard_map/ppermute | solution.py:421
  32.3 3.4 %collective-permute-start.6 = (bf16[4,256,128]{2,1,0:T(8,128)(2,1)S(1)}, bf16[4,256,128]{2,1,0:T(8,128)(2,1)S(1)}, u32[]{:S(2)}, u32[]{:S(2)}) collective-permute-start(bf16[4,256,128]{2,1,0:T(8,128)(2,1)S(1)} %get-tuple-element.52), channel_id=1, source_target_pairs={{4,0},{8,12},{12,8},{16,20},{20,16},{24,28},{5,1},{9,13},{13,9},{1... | collective-permute-start | bytes 786440 | tf_op jit(solution)/shard_map/ppermute | solution.py:421
  35.7 1.9 %collective-permute-start.7 = (bf16[4,256,128]{2,1,0:T(8,128)(2,1)S(1)}, bf16[4,256,128]{2,1,0:T(8,128)(2,1)S(1)}, u32[]{:S(2)}, u32[]{:S(2)}) collective-permute-start(bf16[4,256,128]{2,1,0:T(8,128)(2,1)S(1)} %get-tuple-element.54), channel_id=1, source_target_pairs={{4,8},{8,4},{12,0},{16,28},{20,24},{24,20},{5,9},{9,5},{13,1},{17,... | collective-permute-start | bytes 786440 | tf_op jit(solution)/shard_map/ppermute | solution.py:421
  37.7 0.6 amplitude.1
  38.2 3.5 %collective-permute-done.3.rest_2_ = bf16[4,256,128]{2,1,0:T(8,128)(2,1)S(1)} collective-permute-done((bf16[4,256,128]{2,1,0:T(8,128)(2,1)S(1)}, bf16[4,256,128]{2,1,0:T(8,128)(2,1)S(1)}, u32[]{:S(2)}, u32[]{:S(2)}) %collective-permute-start.3) | collective-permute-done | bytes 262176 | tf_op jit(solution)/shard_map/ppermute | solution.py:421
  41.7 0.0 collective-permute-done.4.rest_3_
  41.7 4.0 %collective-permute-done.5.rest_4_ = bf16[4,256,128]{2,1,0:T(8,128)(2,1)S(1)} collective-permute-done((bf16[4,256,128]{2,1,0:T(8,128)(2,1)S(1)}, bf16[4,256,128]{2,1,0:T(8,128)(2,1)S(1)}, u32[]{:S(2)}, u32[]{:S(2)}) %collective-permute-start.5) | collective-permute-done | bytes 262176 | tf_op jit(solution)/shard_map/ppermute | solution.py:421
  45.7 0.5 collective-permute-done.6.rest_6_
  46.2 5.4 %collective-permute-done.7.rest_8_ = bf16[4,256,128]{2,1,0:T(8,128)(2,1)S(1)} collective-permute-done((bf16[4,256,128]{2,1,0:T(8,128)(2,1)S(1)}, bf16[4,256,128]{2,1,0:T(8,128)(2,1)S(1)}, u32[]{:S(2)}, u32[]{:S(2)}) %collective-permute-start.7) | collective-permute-done | bytes 262176 | tf_op jit(solution)/shard_map/ppermute | solution.py:421
  51.6 5.2 %modulus_step.1 = (bf16[4,256,128]{2,1,0:T(8,128)(2,1)S(1)}, bf16[4,256,128]{2,1,0:T(8,128)(2,1)S(1)}, bf16[4,256,128]{2,1,0:T(8,128)(2,1)S(1)}, bf16[4,256,128]{2,1,0:T(8,128)(2,1)S(1)}) custom-call(f32[1024,256]{1,0:T(8,128)S(1)} %get-tuple-element.46.amplitude, bf16[8,256,1024]{2,1,0:T(8,128)(2,1)S(1)} %get-tuple-element.47.table, ...), custom_call_target="tpu_custom_call" | custom-call | flops 4294967296 | bytes 12582912 | tf_op jit(solution)/shard_map/modulus_step/pallas_call | solution.py:465
  56.7 6.4 %collective-permute-start.11 = (bf16[4,256,128]{2,1,0:T(8,128)(2,1)S(1)}, bf16[4,256,128]{2,1,0:T(8,128)(2,1)S(1)}, u32[]{:S(2)}, u32[]{:S(2)}) collective-permute-start(bf16[4,256,128]{2,1,0:T(8,128)(2,1)S(1)} %get-tuple-element.55.rest_0_), channel_id=1, source_target_pairs={{0,16},{4,20},{8,24},{20,4},{24,8},{28,12},{1,17},{5,21},{9,25},{2... | collective-permute-start | bytes 786440 | tf_op jit(solution)/shard_map/ppermute | solution.py:421
  63.1 1.3 collective-permute-start.10
  64.4 1.9 %collective-permute-start.8 = (bf16[4,256,128]{2,1,0:T(8,128)(2,1)S(1)}, bf16[4,256,128]{2,1,0:T(8,128)(2,1)S(1)}, u32[]{:S(2)}, u32[]{:S(2)}) collective-permute-start(bf16[4,256,128]{2,1,0:T(8,128)(2,1)S(1)} %get-tuple-element.56), channel_id=1, source_target_pairs={{0,4},{4,8},{8,12},{12,16},{16,20},{20,24},{1,5},{5,9},{9,13},{13,... | collective-permute-start | bytes 786440 | tf_op jit(solution)/shard_map/ppermute | solution.py:421
  66.4 1.3 collective-permute-start.13
  67.7 6.6 %collective-permute-start.9 = (bf16[4,256,128]{2,1,0:T(8,128)(2,1)S(1)}, bf16[4,256,128]{2,1,0:T(8,128)(2,1)S(1)}, u32[]{:S(2)}, u32[]{:S(2)}) collective-permute-start(bf16[4,256,128]{2,1,0:T(8,128)(2,1)S(1)} %get-tuple-element.57), channel_id=1, source_target_pairs={{0,8},{4,12},{8,16},{12,20},{16,24},{28,4},{1,9},{5,13},{9,17},{13... | collective-permute-start | bytes 786440 | tf_op jit(solution)/shard_map/ppermute | solution.py:421
  74.3 9.1 %collective-permute-done.11.rest_4_ = bf16[4,256,128]{2,1,0:T(8,128)(2,1)S(1)} collective-permute-done((bf16[4,256,128]{2,1,0:T(8,128)(2,1)S(1)}, bf16[4,256,128]{2,1,0:T(8,128)(2,1)S(1)}, u32[]{:S(2)}, u32[]{:S(2)}) %collective-permute-start.11) | collective-permute-done | bytes 262176 | tf_op jit(solution)/shard_map/ppermute | solution.py:421
  83.4 3.8 %collective-permute-done.10.rest_5_ = bf16[4,256,128]{2,1,0:T(8,128)(2,1)S(1)} collective-permute-done((bf16[4,256,128]{2,1,0:T(8,128)(2,1)S(1)}, bf16[4,256,128]{2,1,0:T(8,128)(2,1)S(1)}, u32[]{:S(2)}, u32[]{:S(2)}) %collective-permute-start.10) | collective-permute-done | bytes 262176 | tf_op jit(solution)/shard_map/ppermute | solution.py:421
  87.2 1.9 %collective-permute-start.12 = (bf16[4,256,128]{2,1,0:T(8,128)(2,1)S(1)}, bf16[4,256,128]{2,1,0:T(8,128)(2,1)S(1)}, u32[]{:S(2)}, u32[]{:S(2)}) collective-permute-start(bf16[4,256,128]{2,1,0:T(8,128)(2,1)S(1)} %get-tuple-element.60), channel_id=1, source_target_pairs={{0,12},{4,16},{8,20},{12,24},{24,4},{28,8},{1,13},{5,17},{9,21},{1... | collective-permute-start | bytes 786440 | tf_op jit(solution)/shard_map/ppermute | solution.py:421
  89.1 2.1 %collective-permute-start.14 = (bf16[4,256,128]{2,1,0:T(8,128)(2,1)S(1)}, bf16[4,256,128]{2,1,0:T(8,128)(2,1)S(1)}, u32[]{:S(2)}, u32[]{:S(2)}) collective-permute-start(bf16[4,256,128]{2,1,0:T(8,128)(2,1)S(1)} %get-tuple-element.60), channel_id=1, source_target_pairs={{8,4},{12,8},{16,12},{20,16},{24,20},{28,24},{9,5},{13,9},{17,13},... | collective-permute-start | bytes 786440 | tf_op jit(solution)/shard_map/ppermute | solution.py:421
  91.2 0.0 collective-permute-done.13.rest_6_
  91.2 0.0 collective-permute-done.8.rest_1_
  91.3 0.0 collective-permute-done.9.rest_2_
  91.3 7.9 %collective-permute-done.12.rest_3_ = bf16[4,256,128]{2,1,0:T(8,128)(2,1)S(1)} collective-permute-done((bf16[4,256,128]{2,1,0:T(8,128)(2,1)S(1)}, bf16[4,256,128]{2,1,0:T(8,128)(2,1)S(1)}, u32[]{:S(2)}, u32[]{:S(2)}) %collective-permute-start.12) | collective-permute-done | bytes 262176 | tf_op jit(solution)/shard_map/ppermute | solution.py:421
  99.1 5.5 %collective-permute-done.14.rest_7_ = bf16[4,256,128]{2,1,0:T(8,128)(2,1)S(1)} collective-permute-done((bf16[4,256,128]{2,1,0:T(8,128)(2,1)S(1)}, bf16[4,256,128]{2,1,0:T(8,128)(2,1)S(1)}, u32[]{:S(2)}, u32[]{:S(2)}) %collective-permute-start.14) | collective-permute-done | bytes 262176 | tf_op jit(solution)/shard_map/ppermute | solution.py:421
  104.6 3.8 %update_sent.1 = (bf16[2,2,256,512]{3,2,1,0:T(8,128)(2,1)S(1)}, bf16[1024,1024]{1,0:T(8,128)(2,1)S(1)}) custom-call(s32[4]{0:T(128)S(1)} %pad_add_fusion.starts, bf16[8,1024,256]{2,1,0:T(8,128)(2,1)S(1)} %copy-done, bf16[4,256,128]{2,1,0:T(8,128)(2,1)S(1)} %get-tuple-element.55.rest_0_, bf16[4,256,128]{2,1,0:T(8,128)(2,1)S(1)} %collective-permute-done.8.rest_1_, ...), custom_call_target="tpu_custom_call" | custom-call | flops 2147483648 | bytes 8388608 | tf_op jit(solution)/shard_map/update_sent/pallas_call | solution.py:489
  108.5 0.1 collective-permute-start.15
  108.6 3.1 %update_kept.1 = f32[2,2,256,512]{3,2,1,0:T(8,128)S(1)} custom-call(s32[4]{0:T(128)S(1)} %pad_add_fusion.starts, bf16[8,1024,256]{2,1,0:T(8,128)(2,1)S(1)} %copy-done, bf16[1024,1024]{1,0:T(8,128)(2,1)S(1)} %get-tuple-element.63.back), custom_call_target="tpu_custom_call" | custom-call | flops 2147483648 | bytes 8388608 | tf_op jit(solution)/shard_map/update_kept/pallas_call | solution.py:502
  111.7 0.0 collective-permute-done.15
  111.7 1.0 fusion.3
  112.7 1.5 %collective-permute-start.16 = (bf16[2,256,512]{2,1,0:T(8,128)(2,1)}, bf16[2,256,512]{2,1,0:T(8,128)(2,1)}, u32[]{:S(2)}, u32[]{:S(2)}) collective-permute-start(bf16[2,256,512]{2,1,0:T(8,128)(2,1)} %fusion.3), channel_id=1, source_target_pairs={{0,2},{2,0},{1,3},{3,1},{4,6},{6,4},{5,7},{7,5},{8,10},{10,8},{9,1... | collective-permute-start | bytes 1572872 | tf_op jit(solution)/shard_map/ppermute | solution.py:512
  114.1 1.5 %fusion.2 = f32[2,256,512]{2,1,0:T(8,128)S(1)} fusion(f32[2,2,256,512]{3,2,1,0:T(8,128)S(1)} %update_kept.1, f32[2,256,2048]{2,1,0:T(8,128)} %spectrum.1, s32[]{:T(128)S(6)} %select_n.3, bf16[2,2,256,512]{3,2,1,0:T(8,128)(2,1)S(1)} %collective-permute-done.15), kind=kLoop, calls=%fused_computation.4 | loop fusion | flops 786432 | bytes 3670020 | tf_op jit(solution)/shard_map/add | solution.py:514
  115.6 11.7 %collective-permute-done.16 = bf16[2,256,512]{2,1,0:T(8,128)(2,1)} collective-permute-done((bf16[2,256,512]{2,1,0:T(8,128)(2,1)}, bf16[2,256,512]{2,1,0:T(8,128)(2,1)}, u32[]{:S(2)}, u32[]{:S(2)}) %collective-permute-start.16) | collective-permute-done | bytes 524320 | tf_op jit(solution)/shard_map/ppermute | solution.py:512
  127.3 2.2 %convert_add_fusion = f32[2,256,512]{2,1,0:T(8,128)} fusion(f32[2,256,512]{2,1,0:T(8,128)S(1)} %fusion.2, bf16[2,256,512]{2,1,0:T(8,128)(2,1)} %collective-permute-done.16), kind=kLoop, calls=%fused_computation.5 | loop fusion | flops 524288 | bytes 2621440 | tf_op jit(solution)/shard_map/add | solution.py:516
  (6 shorter events, 0.0 us)
Async XLA Ops:
  0.0 4.6 %copy-start = (bf16[8,1024,256]{2,1,0:T(8,128)(2,1)S(1)}, bf16[8,1024,256]{2,1,0:T(8,128)(2,1)}, u32[]{:S(2)}) copy-start(bf16[8,1024,256]{2,1,0:T(8,128)(2,1)} %constant.15.clone.table) | copy-start | bytes 12582916
  0.9 2.4 %copy-start.1 = (f32[2,256,2048]{2,1,0:T(8,128)S(1)}, f32[2,256,2048]{2,1,0:T(8,128)}, u32[]{:S(2)}) copy-start(f32[2,256,2048]{2,1,0:T(8,128)} %spectrum.1) | copy-start | bytes 12582916
  6.5 11.3 %collective-permute-start = (bf16[4,256,128]{2,1,0:T(8,128)(2,1)S(1)}, bf16[4,256,128]{2,1,0:T(8,128)(2,1)S(1)}, u32[]{:S(2)}, u32[]{:S(2)}) collective-permute-start(bf16[4,256,128]{2,1,0:T(8,128)(2,1)S(1)} %get-tuple-element.36), channel_id=1, source_target_pairs={{8,16},{12,20},{16,8},{20,12},{4,0},{24,28},{9,17},{13,21},{17,9},... | collective-permute-start | bytes 786440 | tf_op jit(solution)/shard_map/ppermute | solution.py:421
  10.0 13.0 %collective-permute-start.1 = (bf16[4,256,128]{2,1,0:T(8,128)(2,1)S(1)}, bf16[4,256,128]{2,1,0:T(8,128)(2,1)S(1)}, u32[]{:S(2)}, u32[]{:S(2)}) collective-permute-start(bf16[4,256,128]{2,1,0:T(8,128)(2,1)S(1)} %get-tuple-element.37), channel_id=1, source_target_pairs={{8,20},{12,16},{16,12},{20,8},{4,0},{24,28},{9,21},{13,17},{17,13}... | collective-permute-start | bytes 786440 | tf_op jit(solution)/shard_map/ppermute | solution.py:421
  13.3 24.4 %copy-start.2 = (bf16[8,256,1024]{2,1,0:T(8,128)(2,1)S(1)}, bf16[8,256,1024]{2,1,0:T(8,128)(2,1)}, u32[]{:S(2)}) copy-start(bf16[8,256,1024]{2,1,0:T(8,128)(2,1)} %constant.14.clone.table) | copy-start | bytes 12582916
  13.3 24.4 %copy-start.3 = (f32[2,128,1024]{2,1,0:T(8,128)S(1)}, f32[2,128,1024]{2,1,0:T(8,128)}, u32[]{:S(2)}) copy-start(f32[2,128,1024]{2,1,0:T(8,128)} %images) | copy-start | bytes 3145732
  13.3 9.7 %collective-permute-start.2 = (bf16[4,256,128]{2,1,0:T(8,128)(2,1)S(1)}, bf16[4,256,128]{2,1,0:T(8,128)(2,1)S(1)}, u32[]{:S(2)}, u32[]{:S(2)}) collective-permute-start(bf16[4,256,128]{2,1,0:T(8,128)(2,1)S(1)} %get-tuple-element.43), channel_id=1, source_target_pairs={{4,12},{8,0},{12,4},{16,24},{20,28},{24,16},{5,13},{9,1},{13,5},{1... | collective-permute-start | bytes 786440 | tf_op jit(solution)/shard_map/ppermute | solution.py:421
  23.0 18.7 %collective-permute-start.3 = (bf16[4,256,128]{2,1,0:T(8,128)(2,1)S(1)}, bf16[4,256,128]{2,1,0:T(8,128)(2,1)S(1)}, u32[]{:S(2)}, u32[]{:S(2)}) collective-permute-start(bf16[4,256,128]{2,1,0:T(8,128)(2,1)S(1)} %get-tuple-element.48), channel_id=1, source_target_pairs={{0,16},{4,20},{8,24},{12,28},{16,0},{20,4},{24,8},{28,12},{1,17},{... | collective-permute-start | bytes 786440 | tf_op jit(solution)/shard_map/ppermute | solution.py:421
  24.4 17.3 %collective-permute-start.4 = (bf16[4,256,128]{2,1,0:T(8,128)(2,1)S(1)}, bf16[4,256,128]{2,1,0:T(8,128)(2,1)S(1)}, u32[]{:S(2)}, u32[]{:S(2)}) collective-permute-start(bf16[4,256,128]{2,1,0:T(8,128)(2,1)S(1)} %get-tuple-element.49), channel_id=1, source_target_pairs={{0,24},{4,28},{24,0},{28,4},{1,25},{5,29},{25,1},{29,5},{2,26},{6,... | collective-permute-start | bytes 786440 | tf_op jit(solution)/shard_map/ppermute | solution.py:421
  25.1 20.6 %collective-permute-start.5 = (bf16[4,256,128]{2,1,0:T(8,128)(2,1)S(1)}, bf16[4,256,128]{2,1,0:T(8,128)(2,1)S(1)}, u32[]{:S(2)}, u32[]{:S(2)}) collective-permute-start(bf16[4,256,128]{2,1,0:T(8,128)(2,1)S(1)} %get-tuple-element.50.own_b), channel_id=1, source_target_pairs={{8,28},{12,24},{16,4},{20,0},{9,29},{13,25},{17,5},{21,1},{10,30},... | collective-permute-start | bytes 786440 | tf_op jit(solution)/shard_map/ppermute | solution.py:421
  32.3 13.9 %collective-permute-start.6 = (bf16[4,256,128]{2,1,0:T(8,128)(2,1)S(1)}, bf16[4,256,128]{2,1,0:T(8,128)(2,1)S(1)}, u32[]{:S(2)}, u32[]{:S(2)}) collective-permute-start(bf16[4,256,128]{2,1,0:T(8,128)(2,1)S(1)} %get-tuple-element.52), channel_id=1, source_target_pairs={{4,0},{8,12},{12,8},{16,20},{20,16},{24,28},{5,1},{9,13},{13,9},{1... | collective-permute-start | bytes 786440 | tf_op jit(solution)/shard_map/ppermute | solution.py:421
  35.7 15.9 %collective-permute-start.7 = (bf16[4,256,128]{2,1,0:T(8,128)(2,1)S(1)}, bf16[4,256,128]{2,1,0:T(8,128)(2,1)S(1)}, u32[]{:S(2)}, u32[]{:S(2)}) collective-permute-start(bf16[4,256,128]{2,1,0:T(8,128)(2,1)S(1)} %get-tuple-element.54), channel_id=1, source_target_pairs={{4,8},{8,4},{12,0},{16,28},{20,24},{24,20},{5,9},{9,5},{13,1},{17,... | collective-permute-start | bytes 786440 | tf_op jit(solution)/shard_map/ppermute | solution.py:421
  56.7 26.6 %collective-permute-start.11 = (bf16[4,256,128]{2,1,0:T(8,128)(2,1)S(1)}, bf16[4,256,128]{2,1,0:T(8,128)(2,1)S(1)}, u32[]{:S(2)}, u32[]{:S(2)}) collective-permute-start(bf16[4,256,128]{2,1,0:T(8,128)(2,1)S(1)} %get-tuple-element.55.rest_0_), channel_id=1, source_target_pairs={{0,16},{4,20},{8,24},{20,4},{24,8},{28,12},{1,17},{5,21},{9,25},{2... | collective-permute-start | bytes 786440 | tf_op jit(solution)/shard_map/ppermute | solution.py:421
  63.1 24.1 %collective-permute-start.10 = (bf16[4,256,128]{2,1,0:T(8,128)(2,1)S(1)}, bf16[4,256,128]{2,1,0:T(8,128)(2,1)S(1)}, u32[]{:S(2)}, u32[]{:S(2)}) collective-permute-start(bf16[4,256,128]{2,1,0:T(8,128)(2,1)S(1)} %get-tuple-element.56), channel_id=1, source_target_pairs={{0,20},{4,24},{16,4},{20,8},{24,12},{28,16},{1,21},{5,25},{17,5},{... | collective-permute-start | bytes 786440 | tf_op jit(solution)/shard_map/ppermute | solution.py:421
  64.4 26.8 %collective-permute-start.8 = (bf16[4,256,128]{2,1,0:T(8,128)(2,1)S(1)}, bf16[4,256,128]{2,1,0:T(8,128)(2,1)S(1)}, u32[]{:S(2)}, u32[]{:S(2)}) collective-permute-start(bf16[4,256,128]{2,1,0:T(8,128)(2,1)S(1)} %get-tuple-element.56), channel_id=1, source_target_pairs={{0,4},{4,8},{8,12},{12,16},{16,20},{20,24},{1,5},{5,9},{9,13},{13,... | collective-permute-start | bytes 786440 | tf_op jit(solution)/shard_map/ppermute | solution.py:421
  66.4 24.9 %collective-permute-start.13 = (bf16[4,256,128]{2,1,0:T(8,128)(2,1)S(1)}, bf16[4,256,128]{2,1,0:T(8,128)(2,1)S(1)}, u32[]{:S(2)}, u32[]{:S(2)}) collective-permute-start(bf16[4,256,128]{2,1,0:T(8,128)(2,1)S(1)} %get-tuple-element.57), channel_id=1, source_target_pairs={{0,24},{12,4},{16,8},{20,12},{24,16},{28,20},{1,25},{13,5},{17,9},... | collective-permute-start | bytes 786440 | tf_op jit(solution)/shard_map/ppermute | solution.py:421
  67.7 23.6 %collective-permute-start.9 = (bf16[4,256,128]{2,1,0:T(8,128)(2,1)S(1)}, bf16[4,256,128]{2,1,0:T(8,128)(2,1)S(1)}, u32[]{:S(2)}, u32[]{:S(2)}) collective-permute-start(bf16[4,256,128]{2,1,0:T(8,128)(2,1)S(1)} %get-tuple-element.57), channel_id=1, source_target_pairs={{0,8},{4,12},{8,16},{12,20},{16,24},{28,4},{1,9},{5,13},{9,17},{13... | collective-permute-start | bytes 786440 | tf_op jit(solution)/shard_map/ppermute | solution.py:421
  87.2 11.9 %collective-permute-start.12 = (bf16[4,256,128]{2,1,0:T(8,128)(2,1)S(1)}, bf16[4,256,128]{2,1,0:T(8,128)(2,1)S(1)}, u32[]{:S(2)}, u32[]{:S(2)}) collective-permute-start(bf16[4,256,128]{2,1,0:T(8,128)(2,1)S(1)} %get-tuple-element.60), channel_id=1, source_target_pairs={{0,12},{4,16},{8,20},{12,24},{24,4},{28,8},{1,13},{5,17},{9,21},{1... | collective-permute-start | bytes 786440 | tf_op jit(solution)/shard_map/ppermute | solution.py:421
  89.1 15.5 %collective-permute-start.14 = (bf16[4,256,128]{2,1,0:T(8,128)(2,1)S(1)}, bf16[4,256,128]{2,1,0:T(8,128)(2,1)S(1)}, u32[]{:S(2)}, u32[]{:S(2)}) collective-permute-start(bf16[4,256,128]{2,1,0:T(8,128)(2,1)S(1)} %get-tuple-element.60), channel_id=1, source_target_pairs={{8,4},{12,8},{16,12},{20,16},{24,20},{28,24},{9,5},{13,9},{17,13},... | collective-permute-start | bytes 786440 | tf_op jit(solution)/shard_map/ppermute | solution.py:421
  108.5 3.2 %collective-permute-start.15 = (bf16[2,2,256,512]{3,2,1,0:T(8,128)(2,1)S(1)}, bf16[2,2,256,512]{3,2,1,0:T(8,128)(2,1)S(1)}, u32[]{:S(2)}, u32[]{:S(2)}) collective-permute-start(bf16[2,2,256,512]{3,2,1,0:T(8,128)(2,1)S(1)} %get-tuple-element.64), channel_id=1, source_target_pairs={{0,1},{1,0},{2,3},{3,2},{4,5},{5,4},{6,7},{7,6},{8,9},{9,8},{10,11... | collective-permute-start | bytes 3145736 | tf_op jit(solution)/shard_map/ppermute | solution.py:501
  112.7 14.6 %collective-permute-start.16 = (bf16[2,256,512]{2,1,0:T(8,128)(2,1)}, bf16[2,256,512]{2,1,0:T(8,128)(2,1)}, u32[]{:S(2)}, u32[]{:S(2)}) collective-permute-start(bf16[2,256,512]{2,1,0:T(8,128)(2,1)} %fusion.3), channel_id=1, source_target_pairs={{0,2},{2,0},{1,3},{3,1},{4,6},{6,4},{5,7},{7,5},{8,10},{10,8},{9,1... | collective-permute-start | bytes 1572872 | tf_op jit(solution)/shard_map/ppermute | solution.py:512

commit v6 on v5

--- a/solution.py
+++ b/solution.py
@@ -211,18 +211,20 @@
         store_parts(out, row_block(window[...], table[jnp.bitwise_xor(position, d)]))
 
 
-def choose_kernel(got_a, got_b, own_a, own_b, out_a, out_b):
+def choose_kernel(got, own, out):
     passes = is_one_of(lax.axis_index("slab"), PASSED.values())
 
     @pl.when(passes)
     def _():
-        out_a[...] = got_a[...]
-        out_b[...] = got_b[...]
+        out[...] = got[...]
 
     @pl.when(jnp.logical_not(passes))
     def _():
-        out_a[...] = own_a[...]
-        out_b[...] = own_b[...]
+        out[...] = own[...]
+
+
+def partner_at(position, d):
+    return 1 - jnp.bitwise_and(position if d == 1 else jnp.right_shift(position, 1), 1)
 
 
 def amplitude_kernel(images, table, out, table_out):
@@ -245,6 +247,7 @@
     steps = width // LANES
     group = 4
     for d, block in enumerate(near):
+        block = block.at[partner_at(position, d)] if d else block
         at = pl.multiple_of(jnp.bitwise_and(jnp.bitwise_xor(position, d), HALF - 1) * rows, rows)
         for part in range(parts):
             cols = slice(part * LANES, (part + 1) * LANES)
@@ -302,7 +305,7 @@
                 strips[i, part, here, :] = back_re[:, cols]
                 strips[i, parts // 2 + part, here, :] = back_im[:, cols]
     for d, out in enumerate(outs):
-        out[...] = strips[jnp.bitwise_and(position + d, HALF - 1)]
+        out[...] = strips[jnp.bitwise_and(jnp.bitwise_xor(position, d), HALF - 1)]
 
 
 def update_columns(first_step, last_step, starts, table, back, out):
@@ -348,7 +351,8 @@
     parts, rows, _ = blocks[0].shape
     half = back.shape[1] // LANES // 2
     for d, block in enumerate(blocks):
-        at = pl.multiple_of(lax.rem(position + SLABS - d, SLABS) * LANES, LANES)
+        block = block.at[partner_at(position, d)] if 0 < d < HALF else block
+        at = pl.multiple_of(jnp.bitwise_xor(position, d) * LANES, LANES)
         for part in range(parts):
             back[part * rows : (part + 1) * rows, pl.ds(at, LANES)] = block[part]
     update_columns(0, half, starts, table, back, out)
@@ -420,36 +424,32 @@
     def permute(sent, pairs):
         return lax.ppermute(sent, "slab", pairs)
 
+    def swap_near(sent, d):
+        pairs = [[s, s ^ d] for s in range(SLABS) if s < s ^ d]
+        return lax.all_gather(sent, "slab", axis_index_groups=pairs)
+
+    def choose(got, own, name):
+        return local_call(
+            choose_kernel, sent_block, [vmem] * 2, [], 0, 2**19, name
+        )(got, own)
+
     handed = list(PASSED.items())
-    windowed = range(FIRST + 1, LAST)
     got_a = permute(first_a, [(s, s ^ 6) for s in INNER] + handed)
     got_b = permute(first_b, [(s, s ^ 7) for s in INNER] + handed)
-    near_2 = permute(near_2, [(s, s ^ 2) for s in windowed])
+    near_2 = swap_near(near_2, 2)
     second_a, second_b, near_0, near_1, near_3 = rows_call(slice(3, SLABS), "rows_round_2")
-    inner_b = second_b
-    second_a, second_b = local_call(
-        choose_kernel,
-        [sent_block] * 2,
-        [vmem] * 4,
-        [],
-        0,
-        2**20,
-        "round_2_blocks",
-    )(got_a, got_b, second_a, second_b)
-    second_a, second_b, inner_b, near_1, near_2, near_3, images = lax.optimization_barrier(
-        (second_a, second_b, inner_b, near_1, near_2, near_3, images)
+    got_a, second_a, second_b, near_1, near_3, images = lax.optimization_barrier(
+        (got_a, second_a, second_b, near_1, near_3, images)
     )
     outer_pairs = [(s, s ^ 6) for s in range(SLABS) if s not in INNER]
     far_columns = [
         got_a,
         got_b,
-        permute(second_a, [(s, s ^ 4) for s in range(SLABS)]),
-        permute(second_b, outer_pairs),
-        permute(inner_b, [(s, s ^ 5) for s in INNER]),
+        permute(choose(got_a, second_a, "class_4_blocks"), [(s, s ^ 4) for s in range(SLABS)]),
+        permute(choose(got_b, second_b, "class_6_blocks"), outer_pairs),
+        permute(second_b, [(s, s ^ 5) for s in INNER]),
     ]
-    near_1 = permute(near_1, [(s, s ^ 1) for s in windowed])
-    near_3 = permute(near_3, [(s, s ^ 3) for s in windowed])
-    near_columns = [near_0, near_1, near_2, near_3]
+    near_columns = [near_0, swap_near(near_1, 1), near_2, swap_near(near_3, 3)]
     amplitude, by_row = local_call(
         amplitude_kernel,
         [
@@ -473,18 +473,12 @@
         "modulus_step",
     )(amplitude, by_row, *far_columns, *near_columns)
 
-    def send_home(d):
-        pairs = [(s, (s + d) % SLABS) for s in range(SLABS) if FIRST < (s + d) % SLABS < LAST]
-        return permute(strips[d % HALF], pairs)
-
-    strips = list(strips)
-    home = {0: strips[0]}
-    for d in (4, 5, 1, 6, 2):
-        home[d] = send_home(d)
-    for d, before in ((7, 4), (3, 5)):
-        home[before], strips[3] = lax.optimization_barrier((home[before], strips[3]))
-        home[d] = send_home(d)
-    home = [home[d] for d in range(SLABS)]
+    home = [strips[0]]
+    home += [swap_near(strips[d], d) for d in range(1, HALF)]
+    home += [
+        permute(strips[d % HALF], [(s, s ^ d) for s in range(SLABS) if FIRST < s ^ d < LAST])
+        for d in CROSS
+    ]
     share = width // 2
     sent, back = local_call(
         sent_kernel,

time: 130 us -> 136 us (1.046)
  the two profiles are of different devices: /device:TPU:8 before, /device:TPU:10 now
where the time goes in v6:
time: 136 us; the launch traced here: 135 us
  blocking collectives  68.2 us (50%)
  starting transfers between devices  26.3 us (19%)
  Pallas kernels  18.8 us (14%)
  waiting for transfers between devices  13.9 us (10%)
  other arithmetic  5.53 us (4%)
  local copies, waits for them, and re-layouts  2.4 us (2%)
    all_gather x6, blocking collectives, swap_near(): return lax.all_gather(sent, 'slab', axis_index_groups=pairs)  68.2 us
    ppermute x9, starting transfers between devices, permute(): return lax.ppermute(sent, 'slab', pairs)  25.7 us
    ppermute x1, waiting for transfers between devices, body_slabs(): got_x = lax.ppermute(over, 'led', [(0, 2), (2, 0), (1, 3), (3, 1)])  12.6 us
    pallas_call x1, Pallas kernels, body_slabs(): local_call(field_kernel, [sent_block] * HALF, [vmem] * 11, [pltpu.VMEM((w...  5.17 us
    pallas_call x2, Pallas kernels, rows_call(): local_call(functools.partial(rows_kernel, which), [sent_block] * count, [...  4.68 us
    pallas_call x1, Pallas kernels, body_slabs(): local_call(sent_kernel, [jax.ShapeDtypeStruct((2, 2, rows, share), bf16),...  3.82 us
    pallas_call x1, Pallas kernels, body_slabs(): local_call(kept_kernel, jax.ShapeDtypeStruct((2, 2, rows, share), jnp.flo...  3.12 us
  transfers between devices with their start and end apart: 11, of which 2 were waited for; matrix products, arithmetic and copies ran while one was open for 1% of the time, Pallas kernels for 5%

profile of v6, /device:TPU:10, one launch (start us, length us, event | category | flops | bytes accessed | tf_op | source)
XLA Modules:
  0.0 135.2 jit_solution(8855571822674178680)
XLA Ops:
  0.0 0.0 copy-start
  0.0 0.9 pad_add_fusion.starts
  0.9 0.0 copy-start.1
  0.9 2.4 %copy-done.1 = f32[2,256,2048]{2,1,0:T(8,128)S(1)} copy-done((f32[2,256,2048]{2,1,0:T(8,128)S(1)}, f32[2,256,2048]{2,1,0:T(8,128)}, u32[]{:S(2)}) %copy-start.1) | copy-done | bytes 4194328
  3.3 1.4 %windows.1.window = bf16[1024,1024]{1,0:T(8,128)(2,1)S(1)} custom-call(s32[4]{0:T(128)S(1)} %pad_add_fusion.starts, f32[2,256,2048]{2,1,0:T(8,128)S(1)} %copy-done.1), custom_call_target="tpu_custom_call" | custom-call | bytes 6291456 | tf_op jit(solution)/shard_map/windows/pallas_call | solution.py:400
  4.6 0.0 copy-done
  4.7 1.8 %rows_round_1.1 = (bf16[4,256,128]{2,1,0:T(8,128)(2,1)S(1)}, bf16[4,256,128]{2,1,0:T(8,128)(2,1)S(1)}, bf16[4,256,128]{2,1,0:T(8,128)(2,1)S(1)}) custom-call(bf16[1024,1024]{1,0:T(8,128)(2,1)S(1)} %windows.1.window, bf16[8,1024,256]{2,1,0:T(8,128)(2,1)S(1)} %copy-done), custom_call_target="tpu_custom_call" | custom-call | flops 1610612736 | bytes 5242880 | tf_op jit(solution)/shard_map/rows_round_1/pallas_call | solution.py:412
  6.5 3.5 %collective-permute-start = (bf16[4,256,128]{2,1,0:T(8,128)(2,1)S(1)}, bf16[4,256,128]{2,1,0:T(8,128)(2,1)S(1)}, u32[]{:S(2)}, u32[]{:S(2)}) collective-permute-start(bf16[4,256,128]{2,1,0:T(8,128)(2,1)S(1)} %get-tuple-element.29), channel_id=1, source_target_pairs={{8,16},{12,20},{16,8},{20,12},{4,0},{24,28},{9,17},{13,21},{17,9},... | collective-permute-start | bytes 786440 | tf_op jit(solution)/shard_map/ppermute | solution.py:425
  10.0 3.3 %collective-permute-start.1 = (bf16[4,256,128]{2,1,0:T(8,128)(2,1)S(1)}, bf16[4,256,128]{2,1,0:T(8,128)(2,1)S(1)}, u32[]{:S(2)}, u32[]{:S(2)}) collective-permute-start(bf16[4,256,128]{2,1,0:T(8,128)(2,1)S(1)} %get-tuple-element.38), channel_id=1, source_target_pairs={{8,20},{12,16},{16,12},{20,8},{4,0},{24,28},{9,21},{13,17},{17,13}... | collective-permute-start | bytes 786440 | tf_op jit(solution)/shard_map/ppermute | solution.py:425
  13.3 8.2 %all-gather.1 = bf16[8,256,128]{2,1,0:T(8,128)(2,1)S(1)} all-gather(bf16[4,256,128]{2,1,0:T(8,128)(2,1)S(1)} %get-tuple-element.43), channel_id=3, replica_groups={{0,8},{4,12},{16,24},{20,28},{1,9},{5,13},{17,25},{21,29},{2,10},{6,14}..., dimensions={0}, use_global_device_ids=true | all-gather | bytes 786432 | tf_op jit(solution)/shard_map/all_gather | solution.py:429
  21.4 0.0 copy-start.2
  21.4 0.0 copy-start.3
  21.5 2.9 %rows_round_2.1 = (bf16[4,256,128]{2,1,0:T(8,128)(2,1)S(1)}, bf16[4,256,128]{2,1,0:T(8,128)(2,1)S(1)}, bf16[4,256,128]{2,1,0:T(8,128)(2,1)S(1)}, bf16[4,256,128]...) custom-call(bf16[1024,1024]{1,0:T(8,128)(2,1)S(1)} %windows.1.window, bf16[8,1024,256]{2,1,0:T(8,128)(2,1)S(1)} %copy-done), custom_call_target="tpu_custom_call" | custom-call | flops 2684354560 | bytes 5242880 | tf_op jit(solution)/shard_map/rows_round_2/pallas_call | solution.py:412
  24.3 0.0 collective-permute-done.got.rest_0_
  24.4 1.4 collective-permute-start.2
  25.7 3.5 %collective-permute-start.4 = (bf16[4,256,128]{2,1,0:T(8,128)(2,1)S(1)}, bf16[4,256,128]{2,1,0:T(8,128)(2,1)S(1)}, u32[]{:S(2)}, u32[]{:S(2)}) collective-permute-start(bf16[4,256,128]{2,1,0:T(8,128)(2,1)S(1)} %get-tuple-element.40.own), channel_id=1, source_target_pairs={{8,28},{12,24},{16,4},{20,0},{9,29},{13,25},{17,5},{21,1},{10,30},... | collective-permute-start | bytes 786440 | tf_op jit(solution)/shard_map/ppermute | solution.py:425
  29.2 0.0 collective-permute-done.1.got.rest_1_
  29.3 0.7 collective-permute-start.3
  30.0 0.0 copy-done.2
  30.0 0.0 copy-done.3
  30.0 0.6 amplitude.1
  30.6 7.0 %all-gather = bf16[8,256,128]{2,1,0:T(8,128)(2,1)S(1)} all-gather(bf16[4,256,128]{2,1,0:T(8,128)(2,1)S(1)} %get-tuple-element.42), channel_id=2, replica_groups={{0,4},{8,12},{16,20},{24,28},{1,5},{9,13},{17,21},{25,29},{2,6},{10,14}..., dimensions={0}, use_global_device_ids=true | all-gather | bytes 786432 | tf_op jit(solution)/shard_map/all_gather | solution.py:429
  37.6 14.9 %all-gather.2 = bf16[8,256,128]{2,1,0:T(8,128)(2,1)S(1)} all-gather(bf16[4,256,128]{2,1,0:T(8,128)(2,1)S(1)} %get-tuple-element.44), channel_id=4, replica_groups={{0,12},{4,8},{16,28},{20,24},{1,13},{5,9},{17,29},{21,25},{2,14},{6,10}..., dimensions={0}, use_global_device_ids=true | all-gather | bytes 786432 | tf_op jit(solution)/shard_map/all_gather | solution.py:429
  52.5 0.0 collective-permute-done.2.rest_2_
  52.5 0.0 collective-permute-done.3.rest_3_
  52.5 0.0 collective-permute-done.4.rest_4_
  52.5 5.2 %modulus_step.1 = (bf16[4,256,128]{2,1,0:T(8,128)(2,1)S(1)}, bf16[4,256,128]{2,1,0:T(8,128)(2,1)S(1)}, bf16[4,256,128]{2,1,0:T(8,128)(2,1)S(1)}, bf16[4,256,128]{2,1,0:T(8,128)(2,1)S(1)}) custom-call(f32[1024,256]{1,0:T(8,128)S(1)} %get-tuple-element.35.amplitude, bf16[8,256,1024]{2,1,0:T(8,128)(2,1)S(1)} %get-tuple-element.36.table, ...), custom_call_target="tpu_custom_call" | custom-call | flops 4294967296 | bytes 12582912 | tf_op jit(solution)/shard_map/modulus_step/pallas_call | solution.py:465
  57.7 8.9 %all-gather.3 = bf16[8,256,128]{2,1,0:T(8,128)(2,1)S(1)} all-gather(bf16[4,256,128]{2,1,0:T(8,128)(2,1)S(1)} %get-tuple-element.46), channel_id=5, replica_groups={{0,4},{8,12},{16,20},{24,28},{1,5},{9,13},{17,21},{25,29},{2,6},{10,14}..., dimensions={0}, use_global_device_ids=true | all-gather | bytes 786432 | tf_op jit(solution)/shard_map/all_gather | solution.py:429
  66.6 1.3 collective-permute-start.6
  67.8 6.0 %collective-permute-start.5 = (bf16[4,256,128]{2,1,0:T(8,128)(2,1)S(1)}, bf16[4,256,128]{2,1,0:T(8,128)(2,1)S(1)}, u32[]{:S(2)}, u32[]{:S(2)}) collective-permute-start(bf16[4,256,128]{2,1,0:T(8,128)(2,1)S(1)} %get-tuple-element.45.rest_0_), channel_id=1, source_target_pairs={{0,16},{4,20},{8,24},{20,4},{24,8},{28,12},{1,17},{5,21},{9,25},{2... | collective-permute-start | bytes 786440 | tf_op jit(solution)/shard_map/ppermute | solution.py:425
  73.8 2.7 %collective-permute-start.7 = (bf16[4,256,128]{2,1,0:T(8,128)(2,1)S(1)}, bf16[4,256,128]{2,1,0:T(8,128)(2,1)S(1)}, u32[]{:S(2)}, u32[]{:S(2)}) collective-permute-start(bf16[4,256,128]{2,1,0:T(8,128)(2,1)S(1)} %get-tuple-element.47), channel_id=1, source_target_pairs={{0,24},{8,16},{12,20},{16,8},{20,12},{28,4},{1,25},{9,17},{13,21},... | collective-permute-start | bytes 786440 | tf_op jit(solution)/shard_map/ppermute | solution.py:425
  76.5 3.5 %collective-permute-start.8 = (bf16[4,256,128]{2,1,0:T(8,128)(2,1)S(1)}, bf16[4,256,128]{2,1,0:T(8,128)(2,1)S(1)}, u32[]{:S(2)}, u32[]{:S(2)}) collective-permute-start(bf16[4,256,128]{2,1,0:T(8,128)(2,1)S(1)} %get-tuple-element.48), channel_id=1, source_target_pairs={{4,24},{8,20},{12,16},{16,12},{20,8},{24,4},{5,25},{9,21},{13,17},... | collective-permute-start | bytes 786440 | tf_op jit(solution)/shard_map/ppermute | solution.py:425
  80.0 16.2 %all-gather.4 = bf16[8,256,128]{2,1,0:T(8,128)(2,1)S(1)} all-gather(bf16[4,256,128]{2,1,0:T(8,128)(2,1)S(1)} %get-tuple-element.47), channel_id=6, replica_groups={{0,8},{4,12},{16,24},{20,28},{1,9},{5,13},{17,25},{21,29},{2,10},{6,14}..., dimensions={0}, use_global_device_ids=true | all-gather | bytes 786432 | tf_op jit(solution)/shard_map/all_gather | solution.py:429
  96.1 13.0 %all-gather.5 = bf16[8,256,128]{2,1,0:T(8,128)(2,1)S(1)} all-gather(bf16[4,256,128]{2,1,0:T(8,128)(2,1)S(1)} %get-tuple-element.48), channel_id=7, replica_groups={{0,12},{4,8},{16,28},{20,24},{1,13},{5,9},{17,29},{21,25},{2,14},{6,10}..., dimensions={0}, use_global_device_ids=true | all-gather | bytes 786432 | tf_op jit(solution)/shard_map/all_gather | solution.py:429
  109.2 0.0 collective-permute-done.5.rest_4_
  109.2 0.0 collective-permute-done.6.rest_5_
  109.2 0.0 collective-permute-done.7.rest_6_
  109.2 1.2 collective-permute-done.8.rest_7_
  110.4 3.8 %update_sent.1 = (bf16[2,2,256,512]{3,2,1,0:T(8,128)(2,1)S(1)}, bf16[1024,1024]{1,0:T(8,128)(2,1)S(1)}) custom-call(s32[4]{0:T(128)S(1)} %pad_add_fusion.starts, bf16[8,1024,256]{2,1,0:T(8,128)(2,1)S(1)} %copy-done, bf16[4,256,128]{2,1,0:T(8,128)(2,1)S(1)} %get-tuple-element.45.rest_0_, bf16[2,4,256,128]{3,2,1,0:T(8,128)(2,1)S(1)} %bitcast.13, ...), custom_call_target="tpu_custom_call" | custom-call | flops 2147483648 | bytes 8388608 | tf_op jit(solution)/shard_map/update_sent/pallas_call | solution.py:483
  114.2 0.1 collective-permute-start.9
  114.3 3.1 %update_kept.1 = f32[2,2,256,512]{3,2,1,0:T(8,128)S(1)} custom-call(s32[4]{0:T(128)S(1)} %pad_add_fusion.starts, bf16[8,1024,256]{2,1,0:T(8,128)(2,1)S(1)} %copy-done, bf16[1024,1024]{1,0:T(8,128)(2,1)S(1)} %get-tuple-element.49.back), custom_call_target="tpu_custom_call" | custom-call | flops 2147483648 | bytes 8388608 | tf_op jit(solution)/shard_map/update_kept/pallas_call | solution.py:496
  117.4 0.0 collective-permute-done.9
  117.4 1.0 fusion.3
  118.4 0.5 collective-permute-start.10
  118.9 1.5 %fusion.2 = f32[2,256,512]{2,1,0:T(8,128)S(1)} fusion(f32[2,2,256,512]{3,2,1,0:T(8,128)S(1)} %update_kept.1, f32[2,256,2048]{2,1,0:T(8,128)} %spectrum.1, s32[]{:T(128)S(6)} %select_n.3, bf16[2,2,256,512]{3,2,1,0:T(8,128)(2,1)S(1)} %collective-permute-done.9), kind=kLoop, calls=%fused_computation.4 | loop fusion | flops 786432 | bytes 3670020 | tf_op jit(solution)/shard_map/add | solution.py:508
  120.4 12.6 %collective-permute-done.10 = bf16[2,256,512]{2,1,0:T(8,128)(2,1)} collective-permute-done((bf16[2,256,512]{2,1,0:T(8,128)(2,1)}, bf16[2,256,512]{2,1,0:T(8,128)(2,1)}, u32[]{:S(2)}, u32[]{:S(2)}) %collective-permute-start.10) | collective-permute-done | bytes 524320 | tf_op jit(solution)/shard_map/ppermute | solution.py:506
  133.0 2.2 %convert_add_fusion = f32[2,256,512]{2,1,0:T(8,128)} fusion(f32[2,256,512]{2,1,0:T(8,128)S(1)} %fusion.2, bf16[2,256,512]{2,1,0:T(8,128)(2,1)} %collective-permute-done.10), kind=kLoop, calls=%fused_computation.5 | loop fusion | flops 524288 | bytes 2621440 | tf_op jit(solution)/shard_map/add | solution.py:510
  (2 shorter events, 0.1 us)
Async XLA Ops:
  0.0 4.6 %copy-start = (bf16[8,1024,256]{2,1,0:T(8,128)(2,1)S(1)}, bf16[8,1024,256]{2,1,0:T(8,128)(2,1)}, u32[]{:S(2)}) copy-start(bf16[8,1024,256]{2,1,0:T(8,128)(2,1)} %constant.15.clone.table) | copy-start | bytes 12582916
  0.9 2.4 %copy-start.1 = (f32[2,256,2048]{2,1,0:T(8,128)S(1)}, f32[2,256,2048]{2,1,0:T(8,128)}, u32[]{:S(2)}) copy-start(f32[2,256,2048]{2,1,0:T(8,128)} %spectrum.1) | copy-start | bytes 12582916
  6.5 17.9 %collective-permute-start = (bf16[4,256,128]{2,1,0:T(8,128)(2,1)S(1)}, bf16[4,256,128]{2,1,0:T(8,128)(2,1)S(1)}, u32[]{:S(2)}, u32[]{:S(2)}) collective-permute-start(bf16[4,256,128]{2,1,0:T(8,128)(2,1)S(1)} %get-tuple-element.29), channel_id=1, source_target_pairs={{8,16},{12,20},{16,8},{20,12},{4,0},{24,28},{9,17},{13,21},{17,9},... | collective-permute-start | bytes 786440 | tf_op jit(solution)/shard_map/ppermute | solution.py:425
  10.0 19.3 %collective-permute-start.1 = (bf16[4,256,128]{2,1,0:T(8,128)(2,1)S(1)}, bf16[4,256,128]{2,1,0:T(8,128)(2,1)S(1)}, u32[]{:S(2)}, u32[]{:S(2)}) collective-permute-start(bf16[4,256,128]{2,1,0:T(8,128)(2,1)S(1)} %get-tuple-element.38), channel_id=1, source_target_pairs={{8,20},{12,16},{16,12},{20,8},{4,0},{24,28},{9,21},{13,17},{17,13}... | collective-permute-start | bytes 786440 | tf_op jit(solution)/shard_map/ppermute | solution.py:425
  21.4 8.5 %copy-start.2 = (bf16[8,256,1024]{2,1,0:T(8,128)(2,1)S(1)}, bf16[8,256,1024]{2,1,0:T(8,128)(2,1)}, u32[]{:S(2)}) copy-start(bf16[8,256,1024]{2,1,0:T(8,128)(2,1)} %constant.14.clone.table) | copy-start | bytes 12582916
  21.4 8.5 %copy-start.3 = (f32[2,128,1024]{2,1,0:T(8,128)S(1)}, f32[2,128,1024]{2,1,0:T(8,128)}, u32[]{:S(2)}) copy-start(f32[2,128,1024]{2,1,0:T(8,128)} %images) | copy-start | bytes 3145732
  24.4 28.1 %collective-permute-start.2 = (bf16[4,256,128]{2,1,0:T(8,128)(2,1)S(1)}, bf16[4,256,128]{2,1,0:T(8,128)(2,1)S(1)}, u32[]{:S(2)}, u32[]{:S(2)}) collective-permute-start(bf16[4,256,128]{2,1,0:T(8,128)(2,1)S(1)} %class_4_blocks.1), channel_id=1, source_target_pairs={{0,16},{4,20},{8,24},{12,28},{16,0},{20,4},{24,8},{28,12},{1,17},{... | collective-permute-start | bytes 786440 | tf_op jit(solution)/shard_map/ppermute | solution.py:425
  25.7 26.7 %collective-permute-start.4 = (bf16[4,256,128]{2,1,0:T(8,128)(2,1)S(1)}, bf16[4,256,128]{2,1,0:T(8,128)(2,1)S(1)}, u32[]{:S(2)}, u32[]{:S(2)}) collective-permute-start(bf16[4,256,128]{2,1,0:T(8,128)(2,1)S(1)} %get-tuple-element.40.own), channel_id=1, source_target_pairs={{8,28},{12,24},{16,4},{20,0},{9,29},{13,25},{17,5},{21,1},{10,30},... | collective-permute-start | bytes 786440 | tf_op jit(solution)/shard_map/ppermute | solution.py:425
  29.3 23.2 %collective-permute-start.3 = (bf16[4,256,128]{2,1,0:T(8,128)(2,1)S(1)}, bf16[4,256,128]{2,1,0:T(8,128)(2,1)S(1)}, u32[]{:S(2)}, u32[]{:S(2)}) collective-permute-start(bf16[4,256,128]{2,1,0:T(8,128)(2,1)S(1)} %class_6_blocks.1), channel_id=1, source_target_pairs={{0,24},{4,28},{24,0},{28,4},{1,25},{5,29},{25,1},{29,5},{2,26},{6,... | collective-permute-start | bytes 786440 | tf_op jit(solution)/shard_map/ppermute | solution.py:425
  66.6 42.6 %collective-permute-start.6 = (bf16[4,256,128]{2,1,0:T(8,128)(2,1)S(1)}, bf16[4,256,128]{2,1,0:T(8,128)(2,1)S(1)}, u32[]{:S(2)}, u32[]{:S(2)}) collective-permute-start(bf16[4,256,128]{2,1,0:T(8,128)(2,1)S(1)} %get-tuple-element.46), channel_id=1, source_target_pairs={{0,20},{4,16},{12,24},{16,4},{24,12},{28,8},{1,21},{5,17},{13,25},... | collective-permute-start | bytes 786440 | tf_op jit(solution)/shard_map/ppermute | solution.py:425
  67.8 41.3 %collective-permute-start.5 = (bf16[4,256,128]{2,1,0:T(8,128)(2,1)S(1)}, bf16[4,256,128]{2,1,0:T(8,128)(2,1)S(1)}, u32[]{:S(2)}, u32[]{:S(2)}) collective-permute-start(bf16[4,256,128]{2,1,0:T(8,128)(2,1)S(1)} %get-tuple-element.45.rest_0_), channel_id=1, source_target_pairs={{0,16},{4,20},{8,24},{20,4},{24,8},{28,12},{1,17},{5,21},{9,25},{2... | collective-permute-start | bytes 786440 | tf_op jit(solution)/shard_map/ppermute | solution.py:425
  73.8 35.3 %collective-permute-start.7 = (bf16[4,256,128]{2,1,0:T(8,128)(2,1)S(1)}, bf16[4,256,128]{2,1,0:T(8,128)(2,1)S(1)}, u32[]{:S(2)}, u32[]{:S(2)}) collective-permute-start(bf16[4,256,128]{2,1,0:T(8,128)(2,1)S(1)} %get-tuple-element.47), channel_id=1, source_target_pairs={{0,24},{8,16},{12,20},{16,8},{20,12},{28,4},{1,25},{9,17},{13,21},... | collective-permute-start | bytes 786440 | tf_op jit(solution)/shard_map/ppermute | solution.py:425
  76.5 33.9 %collective-permute-start.8 = (bf16[4,256,128]{2,1,0:T(8,128)(2,1)S(1)}, bf16[4,256,128]{2,1,0:T(8,128)(2,1)S(1)}, u32[]{:S(2)}, u32[]{:S(2)}) collective-permute-start(bf16[4,256,128]{2,1,0:T(8,128)(2,1)S(1)} %get-tuple-element.48), channel_id=1, source_target_pairs={{4,24},{8,20},{12,16},{16,12},{20,8},{24,4},{5,25},{9,21},{13,17},... | collective-permute-start | bytes 786440 | tf_op jit(solution)/shard_map/ppermute | solution.py:425
  114.2 3.2 %collective-permute-start.9 = (bf16[2,2,256,512]{3,2,1,0:T(8,128)(2,1)S(1)}, bf16[2,2,256,512]{3,2,1,0:T(8,128)(2,1)S(1)}, u32[]{:S(2)}, u32[]{:S(2)}) collective-permute-start(bf16[2,2,256,512]{3,2,1,0:T(8,128)(2,1)S(1)} %get-tuple-element.50), channel_id=1, source_target_pairs={{0,1},{1,0},{2,3},{3,2},{4,5},{5,4},{6,7},{7,6},{8,9},{9,8},{10,11... | collective-permute-start | bytes 3145736 | tf_op jit(solution)/shard_map/ppermute | solution.py:495
  118.4 14.6 %collective-permute-start.10 = (bf16[2,256,512]{2,1,0:T(8,128)(2,1)}, bf16[2,256,512]{2,1,0:T(8,128)(2,1)}, u32[]{:S(2)}, u32[]{:S(2)}) collective-permute-start(bf16[2,256,512]{2,1,0:T(8,128)(2,1)} %fusion.3), channel_id=1, source_target_pairs={{0,2},{2,0},{1,3},{3,1},{4,6},{6,4},{5,7},{7,5},{8,10},{10,8},{9,1... | collective-permute-start | bytes 1572872 | tf_op jit(solution)/shard_map/ppermute | solution.py:506

commit v7 on v6

--- a/solution.py
+++ b/solution.py
@@ -145,7 +145,6 @@
 SLABS = 8
 HALF = 4
 FIRST, LAST = 0, 7
-CROSS = (4, 5, 6, 7)
 PASSED = {1: 0, 6: 7}
 INNER = (2, 3, 4, 5)
 
@@ -223,10 +222,6 @@
         out[...] = own[...]
 
 
-def partner_at(position, d):
-    return 1 - jnp.bitwise_and(position if d == 1 else jnp.right_shift(position, 1), 1)
-
-
 def amplitude_kernel(images, table, out, table_out):
     leds, block, width = images.shape
     for led in range(leds):
@@ -247,7 +242,6 @@
     steps = width // LANES
     group = 4
     for d, block in enumerate(near):
-        block = block.at[partner_at(position, d)] if d else block
         at = pl.multiple_of(jnp.bitwise_and(jnp.bitwise_xor(position, d), HALF - 1) * rows, rows)
         for part in range(parts):
             cols = slice(part * LANES, (part + 1) * LANES)
@@ -308,59 +302,72 @@
         out[...] = strips[jnp.bitwise_and(jnp.bitwise_xor(position, d), HALF - 1)]
 
 
-def update_columns(first_step, last_step, starts, table, back, out):
+def update_columns(own_core, starts, table, back, outs):
     position = lax.axis_index("slab")
     led_at = lax.axis_index("led")
     core = jnp.bitwise_and(led_at, 1)
     plane_x = jnp.right_shift(led_at, 1)
+    which_half = jnp.right_shift(position, 2)
+    first_row = jnp.bitwise_and(position, HALF - 1)
     leds = starts.shape[0] // 2
     rows = back.shape[0] // (2 * leds)
-    width = back.shape[1]
+    depth = back.shape[1]
+    width = table.shape[1]
     group = width // LANES // 2
-    blocks = [
-        (1 - core if n < group else core) * group + n % group for n in range(first_step, last_step)
-    ]
-    for n in range(first_step, last_step):
-        block = blocks[n - first_step]
-        both = dot(back[...], table[block])
+    owner = core if own_core else 1 - core
+    shape = (rows, LANES)
+    for n in range(group):
+        block = owner * group + n
+        both = dot(
+            back[...], table[block, pl.ds(pl.multiple_of(which_half * depth, depth), depth)]
+        )
         half = leds * rows
         update = (
             both[:half, :LANES] - both[half:, LANES:],
             both[half:, :LANES] + both[:half, LANES:],
         )
-        low = [0.0, 0.0]
-        high = [0.0, 0.0]
+        sums = [[0.0, 0.0] for _ in outs]
         for led in range(leds):
-            inside, wraps = window_mask(
-                position * rows, starts[led], starts[leds + led], rows, block * LANES, LANES, width
+            at_row = lax.broadcasted_iota(jnp.int32, shape, 0) + (
+                first_row * rows - starts[led]
             )
+            at_col = lax.broadcasted_iota(jnp.int32, shape, 1) + (
+                block * LANES - starts[leds + led]
+            )
+            row_term = 2 * jnp.where(at_row < 0, at_row + width, at_row) + 1 - width
+            col_term = 2 * jnp.where(at_col < 0, at_col + width, at_col) + 1 - width
+            inside = row_term * row_term + col_term * col_term < width * width
+            this_slab = jnp.where(at_row < 0, 1, 0) == which_half
+            this_x = jnp.where(at_col < 0, 1, 0) == plane_x
             for plane in range(2):
                 piece = jnp.where(inside, update[plane][led * rows : (led + 1) * rows], 0.0)
-                low[plane] += jnp.where(wraps, 0.0, piece)
-                high[plane] += jnp.where(wraps, piece, 0.0)
-        cols = slice((n - first_step) * LANES, (n - first_step + 1) * LANES)
-        for plane in range(2):
-            out[1 - plane_x, plane, :, cols] = low[plane].astype(out.dtype)
-            out[plane_x, plane, :, cols] = high[plane].astype(out.dtype)
+                for i, at_slab in enumerate(
+                    (jnp.where(this_slab, piece, 0.0), jnp.where(this_slab, 0.0, piece))
+                ):
+                    sums[2 * i][plane] += jnp.where(this_x, at_slab, 0.0)
+                    sums[2 * i + 1][plane] += jnp.where(this_x, 0.0, at_slab)
+        cols = slice(n * LANES, (n + 1) * LANES)
+        for out, both_planes in zip(outs, sums):
+            for plane in range(2):
+                out[plane, :, cols] = both_planes[plane].astype(out.dtype)
 
 
 def sent_kernel(starts, table, *rest):
-    blocks = rest[:SLABS]
-    out, back = rest[SLABS:]
+    blocks = rest[:HALF]
+    this_slab, that_slab, back = rest[HALF:]
     position = lax.axis_index("slab")
     parts, rows, _ = blocks[0].shape
-    half = back.shape[1] // LANES // 2
     for d, block in enumerate(blocks):
-        block = block.at[partner_at(position, d)] if 0 < d < HALF else block
-        at = pl.multiple_of(jnp.bitwise_xor(position, d) * LANES, LANES)
+        source = jnp.bitwise_and(jnp.bitwise_xor(position, d), HALF - 1)
+        at = pl.multiple_of(source * LANES, LANES)
         for part in range(parts):
             back[part * rows : (part + 1) * rows, pl.ds(at, LANES)] = block[part]
-    update_columns(0, half, starts, table, back, out)
-
-
-def kept_kernel(starts, table, back, out):
-    half = back.shape[1] // LANES // 2
-    update_columns(half, 2 * half, starts, table, back, out)
+    outs = [out.at[i] for out in (this_slab, that_slab) for i in range(2)]
+    update_columns(False, starts, table, back, outs)
+
+
+def kept_kernel(starts, table, back, *outs):
+    update_columns(True, starts, table, back, outs)
 
 
 def local_call(kernel, out_shape, spaces, scratch, flops, moved, name):
@@ -424,19 +431,16 @@
     def permute(sent, pairs):
         return lax.ppermute(sent, "slab", pairs)
 
-    def swap_near(sent, d):
-        pairs = [[s, s ^ d] for s in range(SLABS) if s < s ^ d]
-        return lax.all_gather(sent, "slab", axis_index_groups=pairs)
-
     def choose(got, own, name):
         return local_call(
             choose_kernel, sent_block, [vmem] * 2, [], 0, 2**19, name
         )(got, own)
 
     handed = list(PASSED.items())
+    windowed = range(FIRST + 1, LAST)
     got_a = permute(first_a, [(s, s ^ 6) for s in INNER] + handed)
     got_b = permute(first_b, [(s, s ^ 7) for s in INNER] + handed)
-    near_2 = swap_near(near_2, 2)
+    near_2 = permute(near_2, [(s, s ^ 2) for s in windowed])
     second_a, second_b, near_0, near_1, near_3 = rows_call(slice(3, SLABS), "rows_round_2")
     got_a, second_a, second_b, near_1, near_3, images = lax.optimization_barrier(
         (got_a, second_a, second_b, near_1, near_3, images)
@@ -449,7 +453,9 @@
         permute(choose(got_b, second_b, "class_6_blocks"), outer_pairs),
         permute(second_b, [(s, s ^ 5) for s in INNER]),
     ]
-    near_columns = [near_0, swap_near(near_1, 1), near_2, swap_near(near_3, 3)]
+    near_1 = permute(near_1, [(s, s ^ 1) for s in windowed])
+    near_3 = permute(near_3, [(s, s ^ 3) for s in windowed])
+    near_columns = [near_0, near_1, near_2, near_3]
     amplitude, by_row = local_call(
         amplitude_kernel,
         [
@@ -473,41 +479,67 @@
         "modulus_step",
     )(amplitude, by_row, *far_columns, *near_columns)
 
+    def send_home(d):
+        pairs = [(s, (s + d) % SLABS) for s in range(SLABS) if FIRST < (s + d) % SLABS < LAST]
+        return permute(strips[d % HALF], pairs)
+
     home = [strips[0]]
-    home += [swap_near(strips[d], d) for d in range(1, HALF)]
     home += [
-        permute(strips[d % HALF], [(s, s ^ d) for s in range(SLABS) if FIRST < s ^ d < LAST])
-        for d in CROSS
+        permute(strips[d], [(s, s ^ d) for s in range(SLABS)]) for d in range(1, HALF)
     ]
     share = width // 2
-    sent, back = local_call(
+    piece = (2, rows, share)
+    sent_this, sent_that, back = local_call(
         sent_kernel,
         [
-            jax.ShapeDtypeStruct((2, 2, rows, share), bf16),
-            jax.ShapeDtypeStruct((parts * rows, width), bf16),
+            jax.ShapeDtypeStruct((2,) + piece, bf16),
+            jax.ShapeDtypeStruct((2,) + piece, bf16),
+            jax.ShapeDtypeStruct((parts * rows, HALF * LANES), bf16),
         ],
-        [smem] + [vmem] * (1 + SLABS),
+        [smem] + [vmem] * (1 + HALF),
         [],
-        flops // 2,
+        flops // 4,
         8 * 2**20,
         "update_sent",
     )(starts, by_col, *home)
-    got = lax.ppermute(sent, "led", [(0, 1), (1, 0), (2, 3), (3, 2)])
-    kept = local_call(
+    cores = [(0, 1), (1, 0), (2, 3), (3, 2)]
+    planes = [(0, 2), (2, 0), (1, 3), (3, 1)]
+    got_that = lax.ppermute(sent_that, "led", cores)
+    got_this = lax.ppermute(sent_this, "led", cores)
+    this_near, this_far, that_near, that_far = local_call(
         kept_kernel,
-        jax.ShapeDtypeStruct((2, 2, rows, share), jnp.float32),
+        [jax.ShapeDtypeStruct(piece, jnp.float32)] * 4,
         [smem, vmem, vmem],
         [],
-        flops // 2,
-        8 * 2**20,
+        flops // 4,
+        10 * 2**20,
         "update_kept",
     )(starts, by_col, back)
-    over = (kept[0] + got[0].astype(jnp.float32)).astype(bf16)
-    got_x = lax.ppermute(over, "led", [(0, 2), (2, 0), (1, 3), (3, 1)])
+
+    def summed(*values):
+        return sum(value.astype(jnp.float32) for value in values)
+
+    across = [(s, s ^ 4) for s in range(SLABS) if FIRST < s ^ 4 < LAST]
+    from_x = []
+    for i in range(2):
+        here = slice(i * rows // 2, (i + 1) * rows // 2)
+        over = summed(that_far[:, here], got_that[1, :, here]).astype(bf16)
+        from_x.append((here, lax.ppermute(over, "led", planes)))
+    from_z = []
+    over = None
+    over_this = summed(this_far, got_this[1]).astype(bf16)
+    for here, got in from_x:
+        if over is None:
+            got, over_this = lax.optimization_barrier((got, over_this))
+        else:
+            over, got = lax.optimization_barrier((over, got))
+        over = summed(that_near[:, here], got_that[0, :, here], got).astype(bf16)
+        from_z.append(permute(over, across))
+    over_this = lax.ppermute(over_this, "led", planes)
     own_part = lax.dynamic_slice_in_dim(spectrum, led_at * share, share, 2)
-    base = own_part + (kept[1] + got[1].astype(jnp.float32))
-    base, got_x = lax.optimization_barrier((base, got_x))
-    return base + got_x.astype(jnp.float32)
+    base = own_part + summed(this_near, got_this[0], over_this)
+    base, *from_z = lax.optimization_barrier((base, *from_z))
+    return base + summed(jnp.concatenate(from_z, 1))
 
 
 def solution(mesh):

time: 136 us -> 123 us (0.904)
  the two profiles are of different devices: /device:TPU:10 before, /device:TPU:4 now
where the time goes in v7:
time: 123 us; the launch traced here: 122 us
  waiting for transfers between devices  51.1 us (42%)
  starting transfers between devices  43.4 us (35%)
  Pallas kernels  17.1 us (14%)
  other arithmetic  7.97 us (6%)
  local copies, waits for them, and re-layouts  2.41 us (2%)
    ppermute x13, starting transfers between devices, permute(): return lax.ppermute(sent, 'slab', pairs)  39.3 us
    ppermute x13, waiting for transfers between devices, permute(): return lax.ppermute(sent, 'slab', pairs)  31.3 us
    ppermute x2, waiting for transfers between devices, body_slabs(): from_x.append((here, lax.ppermute(over, 'led', planes)))  19.8 us
    pallas_call x1, Pallas kernels, body_slabs(): local_call(field_kernel, [sent_block] * HALF, [vmem] * 11, [pltpu.VMEM((w...  5.3 us
    pallas_call x2, Pallas kernels, rows_call(): local_call(functools.partial(rows_kernel, which), [sent_block] * count, [...  4.69 us
    pallas_call x1, Pallas kernels, body_slabs(): local_call(sent_kernel, [jax.ShapeDtypeStruct((2,) + piece, bf16), jax.Sh...  2.66 us
  transfers between devices with their start and end apart: 18, of which 8 were waited for; matrix products, arithmetic and copies ran while one was open for 5% of the time, Pallas kernels for 5%

profile of v7, /device:TPU:4, one launch (start us, length us, event | category | flops | bytes accessed | tf_op | source)
XLA Modules:
  0.0 122.2 jit_solution(6471763231393326637)
XLA Ops:
  0.0 0.9 pad_add_fusion.starts
  0.9 2.4 %copy-done.1 = f32[2,256,2048]{2,1,0:T(8,128)S(1)} copy-done((f32[2,256,2048]{2,1,0:T(8,128)S(1)}, f32[2,256,2048]{2,1,0:T(8,128)}, u32[]{:S(2)}) %copy-start.1) | copy-done | bytes 4194328
  3.3 1.4 %windows.1.window = bf16[1024,1024]{1,0:T(8,128)(2,1)S(1)} custom-call(s32[4]{0:T(128)S(1)} %pad_add_fusion.starts, f32[2,256,2048]{2,1,0:T(8,128)S(1)} %copy-done.1), custom_call_target="tpu_custom_call" | custom-call | bytes 6291456 | tf_op jit(solution)/shard_map/windows/pallas_call | solution.py:407
  4.7 1.8 %rows_round_1.1 = (bf16[4,256,128]{2,1,0:T(8,128)(2,1)S(1)}, bf16[4,256,128]{2,1,0:T(8,128)(2,1)S(1)}, bf16[4,256,128]{2,1,0:T(8,128)(2,1)S(1)}) custom-call(bf16[1024,1024]{1,0:T(8,128)(2,1)S(1)} %windows.1.window, bf16[8,1024,256]{2,1,0:T(8,128)(2,1)S(1)} %copy-done), custom_call_target="tpu_custom_call" | custom-call | flops 1610612736 | bytes 5242880 | tf_op jit(solution)/shard_map/rows_round_1/pallas_call | solution.py:419
  6.5 1.3 %collective-permute-start = (bf16[4,256,128]{2,1,0:T(8,128)(2,1)S(1)}, bf16[4,256,128]{2,1,0:T(8,128)(2,1)S(1)}, u32[]{:S(2)}, u32[]{:S(2)}) collective-permute-start(bf16[4,256,128]{2,1,0:T(8,128)(2,1)S(1)} %get-tuple-element.38), channel_id=1, source_target_pairs={{8,16},{12,20},{16,8},{20,12},{4,0},{24,28},{9,17},{13,21},{17,9},... | collective-permute-start | bytes 786440 | tf_op jit(solution)/shard_map/ppermute | solution.py:432
  7.8 1.3 %collective-permute-start.1 = (bf16[4,256,128]{2,1,0:T(8,128)(2,1)S(1)}, bf16[4,256,128]{2,1,0:T(8,128)(2,1)S(1)}, u32[]{:S(2)}, u32[]{:S(2)}) collective-permute-start(bf16[4,256,128]{2,1,0:T(8,128)(2,1)S(1)} %get-tuple-element.47), channel_id=1, source_target_pairs={{8,20},{12,16},{16,12},{20,8},{4,0},{24,28},{9,21},{13,17},{17,13}... | collective-permute-start | bytes 786440 | tf_op jit(solution)/shard_map/ppermute | solution.py:432
  9.1 0.0 copy-start.2
  9.1 0.0 copy-start.3
  9.1 6.9 %collective-permute-start.6 = (bf16[4,256,128]{2,1,0:T(8,128)(2,1)S(1)}, bf16[4,256,128]{2,1,0:T(8,128)(2,1)S(1)}, u32[]{:S(2)}, u32[]{:S(2)}) collective-permute-start(bf16[4,256,128]{2,1,0:T(8,128)(2,1)S(1)} %get-tuple-element.52), channel_id=1, source_target_pairs={{4,12},{8,0},{12,4},{16,24},{20,28},{24,16},{5,13},{9,1},{13,5},{1... | collective-permute-start | bytes 786440 | tf_op jit(solution)/shard_map/ppermute | solution.py:432
  16.1 2.9 %rows_round_2.1 = (bf16[4,256,128]{2,1,0:T(8,128)(2,1)S(1)}, bf16[4,256,128]{2,1,0:T(8,128)(2,1)S(1)}, bf16[4,256,128]{2,1,0:T(8,128)(2,1)S(1)}, bf16[4,256,128]...) custom-call(bf16[1024,1024]{1,0:T(8,128)(2,1)S(1)} %windows.1.window, bf16[8,1024,256]{2,1,0:T(8,128)(2,1)S(1)} %copy-done), custom_call_target="tpu_custom_call" | custom-call | flops 2684354560 | bytes 5242880 | tf_op jit(solution)/shard_map/rows_round_2/pallas_call | solution.py:419
  18.9 0.0 collective-permute-done.got.rest_0_
  19.0 1.2 %collective-permute-start.2 = (bf16[4,256,128]{2,1,0:T(8,128)(2,1)S(1)}, bf16[4,256,128]{2,1,0:T(8,128)(2,1)S(1)}, u32[]{:S(2)}, u32[]{:S(2)}) collective-permute-start(bf16[4,256,128]{2,1,0:T(8,128)(2,1)S(1)} %class_4_blocks.1), channel_id=1, source_target_pairs={{0,16},{4,20},{8,24},{12,28},{16,0},{20,4},{24,8},{28,12},{1,17},{... | collective-permute-start | bytes 786440 | tf_op jit(solution)/shard_map/ppermute | solution.py:432
  20.2 1.3 %collective-permute-start.4 = (bf16[4,256,128]{2,1,0:T(8,128)(2,1)S(1)}, bf16[4,256,128]{2,1,0:T(8,128)(2,1)S(1)}, u32[]{:S(2)}, u32[]{:S(2)}) collective-permute-start(bf16[4,256,128]{2,1,0:T(8,128)(2,1)S(1)} %get-tuple-element.49.own), channel_id=1, source_target_pairs={{8,28},{12,24},{16,4},{20,0},{9,29},{13,25},{17,5},{21,1},{10,30},... | collective-permute-start | bytes 786440 | tf_op jit(solution)/shard_map/ppermute | solution.py:432
  21.5 0.0 collective-permute-done.1.got.rest_1_
  21.6 6.0 %collective-permute-start.3 = (bf16[4,256,128]{2,1,0:T(8,128)(2,1)S(1)}, bf16[4,256,128]{2,1,0:T(8,128)(2,1)S(1)}, u32[]{:S(2)}, u32[]{:S(2)}) collective-permute-start(bf16[4,256,128]{2,1,0:T(8,128)(2,1)S(1)} %class_6_blocks.1), channel_id=1, source_target_pairs={{0,24},{4,28},{24,0},{28,4},{1,25},{5,29},{25,1},{29,5},{2,26},{6,... | collective-permute-start | bytes 786440 | tf_op jit(solution)/shard_map/ppermute | solution.py:432
  27.6 1.5 %collective-permute-start.5 = (bf16[4,256,128]{2,1,0:T(8,128)(2,1)S(1)}, bf16[4,256,128]{2,1,0:T(8,128)(2,1)S(1)}, u32[]{:S(2)}, u32[]{:S(2)}) collective-permute-start(bf16[4,256,128]{2,1,0:T(8,128)(2,1)S(1)} %get-tuple-element.51), channel_id=1, source_target_pairs={{4,0},{8,12},{12,8},{16,20},{20,16},{24,28},{5,1},{9,13},{13,9},{1... | collective-permute-start | bytes 786440 | tf_op jit(solution)/shard_map/ppermute | solution.py:432
  29.0 0.0 collective-permute-done.6.rest_7_
  29.0 12.4 %collective-permute-start.7 = (bf16[4,256,128]{2,1,0:T(8,128)(2,1)S(1)}, bf16[4,256,128]{2,1,0:T(8,128)(2,1)S(1)}, u32[]{:S(2)}, u32[]{:S(2)}) collective-permute-start(bf16[4,256,128]{2,1,0:T(8,128)(2,1)S(1)} %get-tuple-element.53), channel_id=1, source_target_pairs={{4,8},{8,4},{12,0},{16,28},{20,24},{24,20},{5,9},{9,5},{13,1},{17,... | collective-permute-start | bytes 786440 | tf_op jit(solution)/shard_map/ppermute | solution.py:432
  41.5 0.6 amplitude.1
  42.0 3.5 %collective-permute-done.4.rest_4_ = bf16[4,256,128]{2,1,0:T(8,128)(2,1)S(1)} collective-permute-done((bf16[4,256,128]{2,1,0:T(8,128)(2,1)S(1)}, bf16[4,256,128]{2,1,0:T(8,128)(2,1)S(1)}, u32[]{:S(2)}, u32[]{:S(2)}) %collective-permute-start.4) | collective-permute-done | bytes 262176 | tf_op jit(solution)/shard_map/ppermute | solution.py:432
  45.6 0.0 collective-permute-done.5.rest_6_
  45.6 5.5 %collective-permute-done.7.rest_8_ = bf16[4,256,128]{2,1,0:T(8,128)(2,1)S(1)} collective-permute-done((bf16[4,256,128]{2,1,0:T(8,128)(2,1)S(1)}, bf16[4,256,128]{2,1,0:T(8,128)(2,1)S(1)}, u32[]{:S(2)}, u32[]{:S(2)}) %collective-permute-start.7) | collective-permute-done | bytes 262176 | tf_op jit(solution)/shard_map/ppermute | solution.py:432
  51.1 5.3 %modulus_step.1 = (bf16[4,256,128]{2,1,0:T(8,128)(2,1)S(1)}, bf16[4,256,128]{2,1,0:T(8,128)(2,1)S(1)}, bf16[4,256,128]{2,1,0:T(8,128)(2,1)S(1)}, bf16[4,256,128]{2,1,0:T(8,128)(2,1)S(1)}) custom-call(f32[1024,256]{1,0:T(8,128)S(1)} %get-tuple-element.44.amplitude, bf16[8,256,1024]{2,1,0:T(8,128)(2,1)S(1)} %get-tuple-element.45.table, ...), custom_call_target="tpu_custom_call" | custom-call | flops 4294967296 | bytes 12582912 | tf_op jit(solution)/shard_map/modulus_step/pallas_call | solution.py:471
  56.4 0.2 collective-permute-start.10
  56.6 1.5 %collective-permute-start.8 = (bf16[4,256,128]{2,1,0:T(8,128)(2,1)S(1)}, bf16[4,256,128]{2,1,0:T(8,128)(2,1)S(1)}, u32[]{:S(2)}, u32[]{:S(2)}) collective-permute-start(bf16[4,256,128]{2,1,0:T(8,128)(2,1)S(1)} %get-tuple-element.55), channel_id=1, source_target_pairs={{0,4},{4,0},{8,12},{12,8},{16,20},{20,16},{24,28},{28,24},{1,5},{5... | collective-permute-start | bytes 786440 | tf_op jit(solution)/shard_map/ppermute | solution.py:432
  58.1 1.9 %collective-permute-start.9 = (bf16[4,256,128]{2,1,0:T(8,128)(2,1)S(1)}, bf16[4,256,128]{2,1,0:T(8,128)(2,1)S(1)}, u32[]{:S(2)}, u32[]{:S(2)}) collective-permute-start(bf16[4,256,128]{2,1,0:T(8,128)(2,1)S(1)} %get-tuple-element.56), channel_id=1, source_target_pairs={{0,8},{4,12},{8,0},{12,4},{16,24},{20,28},{24,16},{28,20},{1,9},{5... | collective-permute-start | bytes 786440 | tf_op jit(solution)/shard_map/ppermute | solution.py:432
  59.9 6.6 %collective-permute-done.10.rest_3_ = bf16[4,256,128]{2,1,0:T(8,128)(2,1)S(1)} collective-permute-done((bf16[4,256,128]{2,1,0:T(8,128)(2,1)S(1)}, bf16[4,256,128]{2,1,0:T(8,128)(2,1)S(1)}, u32[]{:S(2)}, u32[]{:S(2)}) %collective-permute-start.10) | collective-permute-done | bytes 262176 | tf_op jit(solution)/shard_map/ppermute | solution.py:432
  66.6 3.8 %collective-permute-done.8.rest_1_ = bf16[4,256,128]{2,1,0:T(8,128)(2,1)S(1)} collective-permute-done((bf16[4,256,128]{2,1,0:T(8,128)(2,1)S(1)}, bf16[4,256,128]{2,1,0:T(8,128)(2,1)S(1)}, u32[]{:S(2)}, u32[]{:S(2)}) %collective-permute-start.8) | collective-permute-done | bytes 262176 | tf_op jit(solution)/shard_map/ppermute | solution.py:432
  70.4 0.9 collective-permute-done.9.rest_2_
  71.3 2.7 %update_sent.1 = (bf16[2,2,256,512]{3,2,1,0:T(8,128)(2,1)S(1)}, bf16[2,2,256,512]{3,2,1,0:T(8,128)(2,1)S(1)}, bf16[1024,512]{1,0:T(8,128)(2,1)S(1)}) custom-call(s32[4]{0:T(128)S(1)} %pad_add_fusion.starts, bf16[8,1024,256]{2,1,0:T(8,128)(2,1)S(1)} %copy-done, bf16[4,256,128]{2,1,0:T(8,128)(2,1)S(1)} %get-tuple-element.54.rest_0_, ...), custom_call_target="tpu_custom_call" | custom-call | flops 1073741824 | bytes 8388608 | tf_op jit(solution)/shard_map/update_sent/pallas_call | solution.py:492
  74.0 0.1 collective-permute-start.12
  74.0 0.5 collective-permute-start.11
  74.5 2.4 %update_kept.1 = (f32[2,256,512]{2,1,0:T(8,128)S(1)}, f32[2,256,512]{2,1,0:T(8,128)S(1)}, f32[2,256,512]{2,1,0:T(8,128)S(1)}, f32[2,256,512]{2,1,0:T(8,128)S(1)}) custom-call(s32[4]{0:T(128)S(1)} %pad_add_fusion.starts, bf16[8,1024,256]{2,1,0:T(8,128)(2,1)S(1)} %copy-done, bf16[1024,512]{1,0:T(8,128)(2,1)S(1)} %get-tuple-element.58.back), custom_call_target="tpu_custom_call" | custom-call | flops 1073741824 | bytes 10485760 | tf_op jit(solution)/shard_map/update_kept/pallas_call | solution.py:509
  77.0 0.0 copy-start.4
  77.0 1.0 fusion.3
  78.0 1.5 %collective-permute-start.13 = (bf16[2,128,512]{2,1,0:T(8,128)(2,1)S(1)}, bf16[2,128,512]{2,1,0:T(8,128)(2,1)S(1)}, u32[]{:S(2)}, u32[]{:S(2)}) collective-permute-start(bf16[2,128,512]{2,1,0:T(8,128)(2,1)S(1)} %get-tuple-element.72), channel_id=1, source_target_pairs={{0,2},{2,0},{1,3},{3,1},{4,6},{6,4},{5,7},{7,5},{8,10},{10,8},{9,1... | collective-permute-start | bytes 786440 | tf_op jit(solution)/shard_map/ppermute | solution.py:527
  79.5 1.0 fusion
  80.5 5.8 %collective-permute-done.13 = bf16[2,128,512]{2,1,0:T(8,128)(2,1)S(1)} collective-permute-done((bf16[2,128,512]{2,1,0:T(8,128)(2,1)S(1)}, bf16[2,128,512]{2,1,0:T(8,128)(2,1)S(1)}, u32[]{:S(2)}, u32[]{:S(2)}) %collective-permute-start.13) | collective-permute-done | bytes 262176 | tf_op jit(solution)/shard_map/ppermute | solution.py:527
  86.3 1.5 %collective-permute-start.14 = (bf16[2,256,512]{2,1,0:T(8,128)(2,1)}, bf16[2,256,512]{2,1,0:T(8,128)(2,1)}, u32[]{:S(2)}, u32[]{:S(2)}) collective-permute-start(bf16[2,256,512]{2,1,0:T(8,128)(2,1)} %fusion), channel_id=1, source_target_pairs={{0,2},{2,0},{1,3},{3,1},{4,6},{6,4},{5,7},{7,5},{8,10},{10,8},{9,1... | collective-permute-start | bytes 1572872 | tf_op jit(solution)/shard_map/ppermute | solution.py:538
  87.8 0.5 collective-permute-start.16
  88.3 1.1 fusion.7
  89.4 1.9 %collective-permute-start.15 = (bf16[2,128,512]{2,1,0:T(8,128)(2,1)S(1)}, bf16[2,128,512]{2,1,0:T(8,128)(2,1)S(1)}, u32[]{:S(2)}, u32[]{:S(2)}) collective-permute-start(bf16[2,128,512]{2,1,0:T(8,128)(2,1)S(1)} %fusion.7), channel_id=1, source_target_pairs={{0,16},{4,20},{8,24},{20,4},{24,8},{28,12},{1,17},{5,21},{9,25},{2... | collective-permute-start | bytes 786440 | tf_op jit(solution)/shard_map/ppermute | solution.py:432
  91.4 14.0 %collective-permute-done.16 = bf16[2,128,512]{2,1,0:T(8,128)(2,1)} collective-permute-done((bf16[2,128,512]{2,1,0:T(8,128)(2,1)}, bf16[2,128,512]{2,1,0:T(8,128)(2,1)}, u32[]{:S(2)}, u32[]{:S(2)}) %collective-permute-start.16) | collective-permute-done | bytes 262176 | tf_op jit(solution)/shard_map/ppermute | solution.py:527
  105.3 1.1 fusion.5
  106.5 1.9 %collective-permute-start.17 = (bf16[2,128,512]{2,1,0:T(8,128)(2,1)S(1)}, bf16[2,128,512]{2,1,0:T(8,128)(2,1)S(1)}, u32[]{:S(2)}, u32[]{:S(2)}) collective-permute-start(bf16[2,128,512]{2,1,0:T(8,128)(2,1)S(1)} %fusion.5), channel_id=1, source_target_pairs={{0,16},{4,20},{8,24},{20,4},{24,8},{28,12},{1,17},{5,21},{9,25},{2... | collective-permute-start | bytes 786440 | tf_op jit(solution)/shard_map/ppermute | solution.py:432
  108.4 1.7 %fusion.2 = f32[2,256,512]{2,1,0:T(8,128)S(1)} fusion(f32[2,256,512]{2,1,0:T(8,128)S(1)} %get-tuple-element.59, bf16[2,256,512]{2,1,0:T(8,128)(2,1)} %collective-permute-done.14, f32[2,256,2048]{2,1,0:T(8,128)} %spectrum.1, s32[]{:T(128)S(6)} %select_n.3, bf16[2,2,256,512]{3,2,1,0:T(8,128)(2,1)S(1)} %collective-permute-done.11), kind=kLoop, calls=%fused_computation.4 | loop fusion | flops 1310720 | bytes 4194308 | tf_op jit(solution)/shard_map/add | solution.py:540
  110.1 10.9 %collective-permute-done.17 = bf16[2,128,512]{2,1,0:T(8,128)(2,1)S(1)} collective-permute-done((bf16[2,128,512]{2,1,0:T(8,128)(2,1)S(1)}, bf16[2,128,512]{2,1,0:T(8,128)(2,1)S(1)}, u32[]{:S(2)}, u32[]{:S(2)}) %collective-permute-start.17) | collective-permute-done | bytes 262176 | tf_op jit(solution)/shard_map/ppermute | solution.py:432
  121.1 1.1 convert_add_fusion.2
  (14 shorter events, 0.1 us)
Async XLA Ops:
  0.0 4.6 %copy-start = (bf16[8,1024,256]{2,1,0:T(8,128)(2,1)S(1)}, bf16[8,1024,256]{2,1,0:T(8,128)(2,1)}, u32[]{:S(2)}) copy-start(bf16[8,1024,256]{2,1,0:T(8,128)(2,1)} %constant.15.clone.table) | copy-start | bytes 12582916
  0.9 2.4 %copy-start.1 = (f32[2,256,2048]{2,1,0:T(8,128)S(1)}, f32[2,256,2048]{2,1,0:T(8,128)}, u32[]{:S(2)}) copy-start(f32[2,256,2048]{2,1,0:T(8,128)} %spectrum.1) | copy-start | bytes 12582916
  6.5 12.5 %collective-permute-start = (bf16[4,256,128]{2,1,0:T(8,128)(2,1)S(1)}, bf16[4,256,128]{2,1,0:T(8,128)(2,1)S(1)}, u32[]{:S(2)}, u32[]{:S(2)}) collective-permute-start(bf16[4,256,128]{2,1,0:T(8,128)(2,1)S(1)} %get-tuple-element.38), channel_id=1, source_target_pairs={{8,16},{12,20},{16,8},{20,12},{4,0},{24,28},{9,17},{13,21},{17,9},... | collective-permute-start | bytes 786440 | tf_op jit(solution)/shard_map/ppermute | solution.py:432
  7.8 13.7 %collective-permute-start.1 = (bf16[4,256,128]{2,1,0:T(8,128)(2,1)S(1)}, bf16[4,256,128]{2,1,0:T(8,128)(2,1)S(1)}, u32[]{:S(2)}, u32[]{:S(2)}) collective-permute-start(bf16[4,256,128]{2,1,0:T(8,128)(2,1)S(1)} %get-tuple-element.47), channel_id=1, source_target_pairs={{8,20},{12,16},{16,12},{20,8},{4,0},{24,28},{9,21},{13,17},{17,13}... | collective-permute-start | bytes 786440 | tf_op jit(solution)/shard_map/ppermute | solution.py:432
  9.1 32.4 %copy-start.2 = (bf16[8,256,1024]{2,1,0:T(8,128)(2,1)S(1)}, bf16[8,256,1024]{2,1,0:T(8,128)(2,1)}, u32[]{:S(2)}) copy-start(bf16[8,256,1024]{2,1,0:T(8,128)(2,1)} %constant.14.clone.table) | copy-start | bytes 12582916
  9.1 32.4 %copy-start.3 = (f32[2,128,1024]{2,1,0:T(8,128)S(1)}, f32[2,128,1024]{2,1,0:T(8,128)}, u32[]{:S(2)}) copy-start(f32[2,128,1024]{2,1,0:T(8,128)} %images) | copy-start | bytes 3145732
  9.1 19.9 %collective-permute-start.6 = (bf16[4,256,128]{2,1,0:T(8,128)(2,1)S(1)}, bf16[4,256,128]{2,1,0:T(8,128)(2,1)S(1)}, u32[]{:S(2)}, u32[]{:S(2)}) collective-permute-start(bf16[4,256,128]{2,1,0:T(8,128)(2,1)S(1)} %get-tuple-element.52), channel_id=1, source_target_pairs={{4,12},{8,0},{12,4},{16,24},{20,28},{24,16},{5,13},{9,1},{13,5},{1... | collective-permute-start | bytes 786440 | tf_op jit(solution)/shard_map/ppermute | solution.py:432
  19.0 23.0 %collective-permute-start.2 = (bf16[4,256,128]{2,1,0:T(8,128)(2,1)S(1)}, bf16[4,256,128]{2,1,0:T(8,128)(2,1)S(1)}, u32[]{:S(2)}, u32[]{:S(2)}) collective-permute-start(bf16[4,256,128]{2,1,0:T(8,128)(2,1)S(1)} %class_4_blocks.1), channel_id=1, source_target_pairs={{0,16},{4,20},{8,24},{12,28},{16,0},{20,4},{24,8},{28,12},{1,17},{... | collective-permute-start | bytes 786440 | tf_op jit(solution)/shard_map/ppermute | solution.py:432
  20.2 25.3 %collective-permute-start.4 = (bf16[4,256,128]{2,1,0:T(8,128)(2,1)S(1)}, bf16[4,256,128]{2,1,0:T(8,128)(2,1)S(1)}, u32[]{:S(2)}, u32[]{:S(2)}) collective-permute-start(bf16[4,256,128]{2,1,0:T(8,128)(2,1)S(1)} %get-tuple-element.49.own), channel_id=1, source_target_pairs={{8,28},{12,24},{16,4},{20,0},{9,29},{13,25},{17,5},{21,1},{10,30},... | collective-permute-start | bytes 786440 | tf_op jit(solution)/shard_map/ppermute | solution.py:432
  21.6 20.5 %collective-permute-start.3 = (bf16[4,256,128]{2,1,0:T(8,128)(2,1)S(1)}, bf16[4,256,128]{2,1,0:T(8,128)(2,1)S(1)}, u32[]{:S(2)}, u32[]{:S(2)}) collective-permute-start(bf16[4,256,128]{2,1,0:T(8,128)(2,1)S(1)} %class_6_blocks.1), channel_id=1, source_target_pairs={{0,24},{4,28},{24,0},{28,4},{1,25},{5,29},{25,1},{29,5},{2,26},{6,... | collective-permute-start | bytes 786440 | tf_op jit(solution)/shard_map/ppermute | solution.py:432
  27.6 18.0 %collective-permute-start.5 = (bf16[4,256,128]{2,1,0:T(8,128)(2,1)S(1)}, bf16[4,256,128]{2,1,0:T(8,128)(2,1)S(1)}, u32[]{:S(2)}, u32[]{:S(2)}) collective-permute-start(bf16[4,256,128]{2,1,0:T(8,128)(2,1)S(1)} %get-tuple-element.51), channel_id=1, source_target_pairs={{4,0},{8,12},{12,8},{16,20},{20,16},{24,28},{5,1},{9,13},{13,9},{1... | collective-permute-start | bytes 786440 | tf_op jit(solution)/shard_map/ppermute | solution.py:432
  29.0 22.0 %collective-permute-start.7 = (bf16[4,256,128]{2,1,0:T(8,128)(2,1)S(1)}, bf16[4,256,128]{2,1,0:T(8,128)(2,1)S(1)}, u32[]{:S(2)}, u32[]{:S(2)}) collective-permute-start(bf16[4,256,128]{2,1,0:T(8,128)(2,1)S(1)} %get-tuple-element.53), channel_id=1, source_target_pairs={{4,8},{8,4},{12,0},{16,28},{20,24},{24,20},{5,9},{9,5},{13,1},{17,... | collective-permute-start | bytes 786440 | tf_op jit(solution)/shard_map/ppermute | solution.py:432
  56.4 10.2 %collective-permute-start.10 = (bf16[4,256,128]{2,1,0:T(8,128)(2,1)S(1)}, bf16[4,256,128]{2,1,0:T(8,128)(2,1)S(1)}, u32[]{:S(2)}, u32[]{:S(2)}) collective-permute-start(bf16[4,256,128]{2,1,0:T(8,128)(2,1)S(1)} %get-tuple-element.57), channel_id=1, source_target_pairs={{0,12},{4,8},{8,4},{12,0},{16,28},{20,24},{24,20},{28,16},{1,13},{... | collective-permute-start | bytes 786440 | tf_op jit(solution)/shard_map/ppermute | solution.py:432
  56.6 13.8 %collective-permute-start.8 = (bf16[4,256,128]{2,1,0:T(8,128)(2,1)S(1)}, bf16[4,256,128]{2,1,0:T(8,128)(2,1)S(1)}, u32[]{:S(2)}, u32[]{:S(2)}) collective-permute-start(bf16[4,256,128]{2,1,0:T(8,128)(2,1)S(1)} %get-tuple-element.55), channel_id=1, source_target_pairs={{0,4},{4,0},{8,12},{12,8},{16,20},{20,16},{24,28},{28,24},{1,5},{5... | collective-permute-start | bytes 786440 | tf_op jit(solution)/shard_map/ppermute | solution.py:432
  58.1 13.2 %collective-permute-start.9 = (bf16[4,256,128]{2,1,0:T(8,128)(2,1)S(1)}, bf16[4,256,128]{2,1,0:T(8,128)(2,1)S(1)}, u32[]{:S(2)}, u32[]{:S(2)}) collective-permute-start(bf16[4,256,128]{2,1,0:T(8,128)(2,1)S(1)} %get-tuple-element.56), channel_id=1, source_target_pairs={{0,8},{4,12},{8,0},{12,4},{16,24},{20,28},{24,16},{28,20},{1,9},{5... | collective-permute-start | bytes 786440 | tf_op jit(solution)/shard_map/ppermute | solution.py:432
  74.0 3.0 %collective-permute-start.12 = (bf16[2,2,256,512]{3,2,1,0:T(8,128)(2,1)S(1)}, bf16[2,2,256,512]{3,2,1,0:T(8,128)(2,1)S(1)}, u32[]{:S(2)}, u32[]{:S(2)}) collective-permute-start(bf16[2,2,256,512]{3,2,1,0:T(8,128)(2,1)S(1)} %get-tuple-element.62), channel_id=1, source_target_pairs={{0,1},{1,0},{2,3},{3,2},{4,5},{5,4},{6,7},{7,6},{8,9},{9,8},{10,11... | collective-permute-start | bytes 3145736 | tf_op jit(solution)/shard_map/ppermute | solution.py:507
  74.0 5.5 %collective-permute-start.11 = (bf16[2,2,256,512]{3,2,1,0:T(8,128)(2,1)S(1)}, bf16[2,2,256,512]{3,2,1,0:T(8,128)(2,1)S(1)}, u32[]{:S(2)}, u32[]{:S(2)}) collective-permute-start(bf16[2,2,256,512]{3,2,1,0:T(8,128)(2,1)S(1)} %get-tuple-element.60), channel_id=1, source_target_pairs={{0,1},{1,0},{2,3},{3,2},{4,5},{5,4},{6,7},{7,6},{8,9},{9,8},{10,11... | collective-permute-start | bytes 3145736 | tf_op jit(solution)/shard_map/ppermute | solution.py:508
  77.0 3.5 %copy-start.4 = (bf16[2,2,256,512]{3,2,1,0:T(8,128)(2,1)}, bf16[2,2,256,512]{3,2,1,0:T(8,128)(2,1)S(1)}, u32[]{:S(2)}) copy-start(bf16[2,2,256,512]{3,2,1,0:T(8,128)(2,1)S(1)} %collective-permute-done.12) | copy-start | bytes 3145732
  78.0 8.3 %collective-permute-start.13 = (bf16[2,128,512]{2,1,0:T(8,128)(2,1)S(1)}, bf16[2,128,512]{2,1,0:T(8,128)(2,1)S(1)}, u32[]{:S(2)}, u32[]{:S(2)}) collective-permute-start(bf16[2,128,512]{2,1,0:T(8,128)(2,1)S(1)} %get-tuple-element.72), channel_id=1, source_target_pairs={{0,2},{2,0},{1,3},{3,1},{4,6},{6,4},{5,7},{7,5},{8,10},{10,8},{9,1... | collective-permute-start | bytes 786440 | tf_op jit(solution)/shard_map/ppermute | solution.py:527
  86.3 22.1 %collective-permute-start.14 = (bf16[2,256,512]{2,1,0:T(8,128)(2,1)}, bf16[2,256,512]{2,1,0:T(8,128)(2,1)}, u32[]{:S(2)}, u32[]{:S(2)}) collective-permute-start(bf16[2,256,512]{2,1,0:T(8,128)(2,1)} %fusion), channel_id=1, source_target_pairs={{0,2},{2,0},{1,3},{3,1},{4,6},{6,4},{5,7},{7,5},{8,10},{10,8},{9,1... | collective-permute-start | bytes 1572872 | tf_op jit(solution)/shard_map/ppermute | solution.py:538
  87.8 17.5 %collective-permute-start.16 = (bf16[2,128,512]{2,1,0:T(8,128)(2,1)}, bf16[2,128,512]{2,1,0:T(8,128)(2,1)}, u32[]{:S(2)}, u32[]{:S(2)}) collective-permute-start(bf16[2,128,512]{2,1,0:T(8,128)(2,1)} %get-tuple-element.71), channel_id=1, source_target_pairs={{0,2},{2,0},{1,3},{3,1},{4,6},{6,4},{5,7},{7,5},{8,10},{10,8},{9,1... | collective-permute-start | bytes 786440 | tf_op jit(solution)/shard_map/ppermute | solution.py:527
  89.4 31.7 %collective-permute-start.15 = (bf16[2,128,512]{2,1,0:T(8,128)(2,1)S(1)}, bf16[2,128,512]{2,1,0:T(8,128)(2,1)S(1)}, u32[]{:S(2)}, u32[]{:S(2)}) collective-permute-start(bf16[2,128,512]{2,1,0:T(8,128)(2,1)S(1)} %fusion.7), channel_id=1, source_target_pairs={{0,16},{4,20},{8,24},{20,4},{24,8},{28,12},{1,17},{5,21},{9,25},{2... | collective-permute-start | bytes 786440 | tf_op jit(solution)/shard_map/ppermute | solution.py:432
  106.5 14.6 %collective-permute-start.17 = (bf16[2,128,512]{2,1,0:T(8,128)(2,1)S(1)}, bf16[2,128,512]{2,1,0:T(8,128)(2,1)S(1)}, u32[]{:S(2)}, u32[]{:S(2)}) collective-permute-start(bf16[2,128,512]{2,1,0:T(8,128)(2,1)S(1)} %fusion.5), channel_id=1, source_target_pairs={{0,16},{4,20},{8,24},{20,4},{24,8},{28,12},{1,17},{5,21},{9,25},{2... | collective-permute-start | bytes 786440 | tf_op jit(solution)/shard_map/ppermute | solution.py:432

commit v8 on v7

--- a/solution.py
+++ b/solution.py
@@ -145,8 +145,26 @@
 SLABS = 8
 HALF = 4
 FIRST, LAST = 0, 7
-PASSED = {1: 0, 6: 7}
-INNER = (2, 3, 4, 5)
+HANDED = {1: (0, 4), 6: (7, 3)}
+FAR = (
+    {1: 4, 2: 4, 3: 5, 4: 2, 5: 3, 6: 3},
+    {1: 6, 2: 7, 3: 4, 4: 3, 5: 0, 6: 1},
+    {1: 7, 2: 5, 3: 6, 4: 1, 5: 2, 6: 0},
+    {1: 5, 2: 6, 3: 7, 4: 0, 5: 1, 6: 2},
+)
+
+
+def look_up(position, table):
+    return sum(jnp.where(position == slab, value, 0) for slab, value in table.items())
+
+
+def origins(far):
+    table = {to: slab for slab, to in far.items()}
+    if far is FAR[0]:
+        table = {to: slab for slab, to in far.items() if slab not in HANDED}
+    if far is FAR[-1]:
+        table.update({to: slab for slab, (_, to) in HANDED.items()})
+    return table
 
 
 def dot(left, right):
@@ -199,19 +217,16 @@
             window[at : at + rows, :] = jnp.where(inside, value, 0.0).astype(jnp.bfloat16)
 
 
-def classes_of(position):
-    hands_over = is_one_of(position, PASSED)
-    return (jnp.where(hands_over, 5, 6), 7, 2, 4, jnp.where(hands_over, 6, 5), 0, 1, 3)
-
-
 def rows_kernel(which, window, table, *outs):
     position = lax.axis_index("slab")
-    for out, d in zip(outs, classes_of(position)[which]):
-        store_parts(out, row_block(window[...], table[jnp.bitwise_xor(position, d)]))
+    blocks = [look_up(position, far) for far in FAR]
+    blocks += [jnp.bitwise_xor(position, d) for d in (0, 2, 1, 3)]
+    for out, block in zip(outs, blocks[which]):
+        store_parts(out, row_block(window[...], table[block]))
 
 
 def choose_kernel(got, own, out):
-    passes = is_one_of(lax.axis_index("slab"), PASSED.values())
+    passes = is_one_of(lax.axis_index("slab"), [by for by, _ in HANDED.values()])
 
     @pl.when(passes)
     def _():
@@ -232,9 +247,9 @@
 
 
 def field_kernel(amplitude, table, *rest):
-    far, near = rest[:5], rest[5 : HALF + 5]
-    outs = rest[HALF + 5 : 2 * HALF + 5]
-    field_in, diff, strips = rest[2 * HALF + 5 :]
+    far, near = rest[: len(FAR)], rest[len(FAR) : len(FAR) + HALF]
+    outs = rest[len(FAR) + HALF : len(FAR) + 2 * HALF]
+    field_in, diff, strips = rest[len(FAR) + 2 * HALF :]
     position = lax.axis_index("slab")
     parts, rows, _ = near[0].shape
     half = parts // 2 * LANES
@@ -253,21 +268,12 @@
             cols = slice(part * LANES, (part + 1) * LANES)
             field_in[pl.ds(at, rows), cols] += block[part]
 
-    passes = is_one_of(position, PASSED.values())
-    hands_over = is_one_of(position, PASSED)
-    ends = is_one_of(position, [to ^ 4 for to in PASSED.values()])
-
-    @pl.when(is_one_of(position, INNER))
-    def _():
-        add(far[0], jnp.bitwise_xor(position, 6))
-        add(far[1], jnp.bitwise_xor(position, 7))
-        add(far[2], jnp.bitwise_xor(position, jnp.where(ends, 5, 4)))
-
-    @pl.when(jnp.logical_or(passes, hands_over))
-    def _():
-        add(far[2], jnp.bitwise_xor(position, 4))
-        add(far[3], jnp.bitwise_xor(position, jnp.where(hands_over, 7, 6)))
-        add(far[4], jnp.bitwise_xor(position, 5))
+    for block, permute in zip(far, FAR):
+        table_of = origins(permute)
+
+        @pl.when(is_one_of(position, table_of))
+        def _():
+            add(block, look_up(position, table_of))
 
     for first in range(0, steps, group):
         product = dot(
@@ -302,15 +308,15 @@
         out[...] = strips[jnp.bitwise_and(jnp.bitwise_xor(position, d), HALF - 1)]
 
 
-def update_columns(own_core, starts, table, back, outs):
+def update_columns(own_core, row_half, starts, table, back, outs):
     position = lax.axis_index("slab")
     led_at = lax.axis_index("led")
     core = jnp.bitwise_and(led_at, 1)
     plane_x = jnp.right_shift(led_at, 1)
     which_half = jnp.right_shift(position, 2)
-    first_row = jnp.bitwise_and(position, HALF - 1)
     leds = starts.shape[0] // 2
     rows = back.shape[0] // (2 * leds)
+    first_row = (jnp.bitwise_and(position, HALF - 1) * 2 + row_half) * rows
     depth = back.shape[1]
     width = table.shape[1]
     group = width // LANES // 2
@@ -328,9 +334,7 @@
         )
         sums = [[0.0, 0.0] for _ in outs]
         for led in range(leds):
-            at_row = lax.broadcasted_iota(jnp.int32, shape, 0) + (
-                first_row * rows - starts[led]
-            )
+            at_row = lax.broadcasted_iota(jnp.int32, shape, 0) + (first_row - starts[led])
             at_col = lax.broadcasted_iota(jnp.int32, shape, 1) + (
                 block * LANES - starts[leds + led]
             )
@@ -352,22 +356,54 @@
                 out[plane, :, cols] = both_planes[plane].astype(out.dtype)
 
 
-def sent_kernel(starts, table, *rest):
+def sent_kernel(row_half, starts, table, *rest):
     blocks = rest[:HALF]
     this_slab, that_slab, back = rest[HALF:]
     position = lax.axis_index("slab")
     parts, rows, _ = blocks[0].shape
+    rows = rows // 2
     for d, block in enumerate(blocks):
         source = jnp.bitwise_and(jnp.bitwise_xor(position, d), HALF - 1)
         at = pl.multiple_of(source * LANES, LANES)
         for part in range(parts):
-            back[part * rows : (part + 1) * rows, pl.ds(at, LANES)] = block[part]
+            back[part * rows : (part + 1) * rows, pl.ds(at, LANES)] = block[
+                part, row_half * rows : (row_half + 1) * rows
+            ]
     outs = [out.at[i] for out in (this_slab, that_slab) for i in range(2)]
-    update_columns(False, starts, table, back, outs)
-
-
-def kept_kernel(starts, table, back, *outs):
-    update_columns(True, starts, table, back, outs)
+    update_columns(False, row_half, starts, table, back, outs)
+
+
+def kept_kernel(row_half, starts, table, back, *outs):
+    update_columns(True, row_half, starts, table, back, outs)
+
+
+def sum_kernel(picks, *refs):
+    total = 0.0
+    for ref, pick in zip(refs, picks):
+        value = ref[...] if pick is None else ref[pick]
+        total = total + value.astype(jnp.float32)
+    refs[-1][...] = total.astype(refs[-1].dtype)
+
+
+def final_kernel(*refs):
+    base, got, out = refs[-3:]
+    out[...] = base[...] + got[...].astype(jnp.float32)
+
+
+def final_call(row_half, before, base, got):
+    planes, rows, share = base.shape
+    vmem = pl.BlockSpec(memory_space=pltpu.VMEM)
+    first = before is None
+    return pl.pallas_call(
+        final_kernel,
+        out_shape=jax.ShapeDtypeStruct((planes, 2 * rows, share), base.dtype),
+        grid=(1,),
+        in_specs=([] if first else [pl.BlockSpec(memory_space=pl.ANY)]) + [vmem] * 2,
+        out_specs=pl.BlockSpec((planes, rows, share), lambda _: (0, row_half, 0)),
+        input_output_aliases={} if first else {0: 0},
+        cost_estimate=pl.CostEstimate(flops=0, bytes_accessed=2**20, transcendentals=0),
+        name=f"updated_{row_half}",
+    )(*([] if first else [before]), base, got)
 
 
 def local_call(kernel, out_shape, spaces, scratch, flops, moved, name):
@@ -426,7 +462,7 @@
             name,
         )(window, by_col)
 
-    first_a, first_b, near_2 = rows_call(slice(0, 3), "rows_round_1")
+    far_sent = list(rows_call(slice(0, 3), "rows_far"))
 
     def permute(sent, pairs):
         return lax.ppermute(sent, "slab", pairs)
@@ -436,23 +472,23 @@
             choose_kernel, sent_block, [vmem] * 2, [], 0, 2**19, name
         )(got, own)
 
-    handed = list(PASSED.items())
     windowed = range(FIRST + 1, LAST)
-    got_a = permute(first_a, [(s, s ^ 6) for s in INNER] + handed)
-    got_b = permute(first_b, [(s, s ^ 7) for s in INNER] + handed)
+    far_columns = []
+    for far, sent in zip(FAR, far_sent):
+        pairs = dict(far)
+        if far is FAR[0]:
+            pairs.update({slab: by for slab, (by, _) in HANDED.items()})
+        far_columns.append(permute(sent, list(pairs.items())))
+    last, near_0, near_2, near_1, near_3 = rows_call(slice(3, SLABS), "rows_near")
     near_2 = permute(near_2, [(s, s ^ 2) for s in windowed])
-    second_a, second_b, near_0, near_1, near_3 = rows_call(slice(3, SLABS), "rows_round_2")
-    got_a, second_a, second_b, near_1, near_3, images = lax.optimization_barrier(
-        (got_a, second_a, second_b, near_1, near_3, images)
-    )
-    outer_pairs = [(s, s ^ 6) for s in range(SLABS) if s not in INNER]
-    far_columns = [
-        got_a,
-        got_b,
-        permute(choose(got_a, second_a, "class_4_blocks"), [(s, s ^ 4) for s in range(SLABS)]),
-        permute(choose(got_b, second_b, "class_6_blocks"), outer_pairs),
-        permute(second_b, [(s, s ^ 5) for s in INNER]),
-    ]
+    far_columns[0], last, near_1, near_3, images = lax.optimization_barrier(
+        (far_columns[0], last, near_1, near_3, images)
+    )
+    last = local_call(
+        choose_kernel, sent_block, [vmem] * 2, [], 0, 2**19, "last_far_blocks"
+    )(far_columns[0], last)
+    pairs = list(FAR[-1].items()) + list(HANDED.values())
+    far_columns.append(permute(last, pairs))
     near_1 = permute(near_1, [(s, s ^ 1) for s in windowed])
     near_3 = permute(near_3, [(s, s ^ 3) for s in windowed])
     near_columns = [near_0, near_1, near_2, near_3]
@@ -471,7 +507,7 @@
     strips = local_call(
         field_kernel,
         [sent_block] * HALF,
-        [vmem] * 11,
+        [vmem] * (2 + len(FAR) + HALF),
         [pltpu.VMEM((width, parts * block), bf16)] * 2
         + [pltpu.VMEM((HALF,) + sent_block.shape, bf16)],
         16 * leds * block * width * width,
@@ -488,58 +524,74 @@
         permute(strips[d], [(s, s ^ d) for s in range(SLABS)]) for d in range(1, HALF)
     ]
     share = width // 2
-    piece = (2, rows, share)
-    sent_this, sent_that, back = local_call(
-        sent_kernel,
-        [
-            jax.ShapeDtypeStruct((2,) + piece, bf16),
-            jax.ShapeDtypeStruct((2,) + piece, bf16),
-            jax.ShapeDtypeStruct((parts * rows, HALF * LANES), bf16),
-        ],
-        [smem] + [vmem] * (1 + HALF),
-        [],
-        flops // 4,
-        8 * 2**20,
-        "update_sent",
-    )(starts, by_col, *home)
+    piece = (2, rows // 2, share)
     cores = [(0, 1), (1, 0), (2, 3), (3, 2)]
     planes = [(0, 2), (2, 0), (1, 3), (3, 1)]
-    got_that = lax.ppermute(sent_that, "led", cores)
-    got_this = lax.ppermute(sent_this, "led", cores)
-    this_near, this_far, that_near, that_far = local_call(
-        kept_kernel,
-        [jax.ShapeDtypeStruct(piece, jnp.float32)] * 4,
-        [smem, vmem, vmem],
-        [],
-        flops // 4,
-        10 * 2**20,
-        "update_kept",
-    )(starts, by_col, back)
 
     def summed(*values):
         return sum(value.astype(jnp.float32) for value in values)
 
+    def sum_call(values, picks, name):
+        return local_call(
+            functools.partial(sum_kernel, picks),
+            jax.ShapeDtypeStruct(piece, bf16),
+            [vmem] * len(values),
+            [],
+            0,
+            2**20,
+            name,
+        )(*values)
+
+    halves = []
+    for i in range(2):
+        sent_this, sent_that, back = local_call(
+            functools.partial(sent_kernel, i),
+            [
+                jax.ShapeDtypeStruct((2,) + piece, bf16),
+                jax.ShapeDtypeStruct((2,) + piece, bf16),
+                jax.ShapeDtypeStruct((parts * rows // 2, HALF * LANES), bf16),
+            ],
+            [smem] + [vmem] * (1 + HALF),
+            [],
+            flops // 8,
+            6 * 2**20,
+            f"update_sent_{i}",
+        )(starts, by_col, *home)
+        got_that = lax.ppermute(sent_that, "led", cores)
+        halves.append((back, sent_this, got_that))
     across = [(s, s ^ 4) for s in range(SLABS) if FIRST < s ^ 4 < LAST]
-    from_x = []
+    own_part = lax.dynamic_slice_in_dim(spectrum, led_at * share, share, 2)
+    from_z = []
+    base = []
+    over_x = None
+    for i, (back, sent_this, got_that) in enumerate(halves):
+        if i:
+            over_x, back = lax.optimization_barrier((over_x, back))
+        this_near, this_far, that_near, that_far = local_call(
+            functools.partial(kept_kernel, i),
+            [jax.ShapeDtypeStruct(piece, jnp.float32)] * 4,
+            [smem, vmem, vmem],
+            [],
+            flops // 8,
+            8 * 2**20,
+            f"update_kept_{i}",
+        )(starts, by_col, back)
+        over_x = sum_call((that_far, got_that), (None, 1), f"over_x_{i}")
+        got_x = lax.ppermute(over_x, "led", planes)
+        if i:
+            from_z[0], got_x = lax.optimization_barrier((from_z[0], got_x))
+        over_z = sum_call((that_near, got_that, got_x), (None, 0, None), f"over_z_{i}")
+        from_z.append(permute(over_z, across))
+        got_this = lax.ppermute(sent_this, "led", cores)
+        over_this = sum_call((this_far, got_this), (None, 1), f"over_this_{i}")
+        over_this, _ = lax.optimization_barrier((over_this, over_z))
+        got_x = lax.ppermute(over_this, "led", planes)
+        here = slice(i * rows // 2, (i + 1) * rows // 2)
+        base.append(own_part[:, here] + summed(this_near, got_this[0], got_x))
+    updated = None
     for i in range(2):
-        here = slice(i * rows // 2, (i + 1) * rows // 2)
-        over = summed(that_far[:, here], got_that[1, :, here]).astype(bf16)
-        from_x.append((here, lax.ppermute(over, "led", planes)))
-    from_z = []
-    over = None
-    over_this = summed(this_far, got_this[1]).astype(bf16)
-    for here, got in from_x:
-        if over is None:
-            got, over_this = lax.optimization_barrier((got, over_this))
-        else:
-            over, got = lax.optimization_barrier((over, got))
-        over = summed(that_near[:, here], got_that[0, :, here], got).astype(bf16)
-        from_z.append(permute(over, across))
-    over_this = lax.ppermute(over_this, "led", planes)
-    own_part = lax.dynamic_slice_in_dim(spectrum, led_at * share, share, 2)
-    base = own_part + summed(this_near, got_this[0], over_this)
-    base, *from_z = lax.optimization_barrier((base, *from_z))
-    return base + summed(jnp.concatenate(from_z, 1))
+        updated = final_call(i, updated, base[i], from_z[i])
+    return updated
 
 
 def solution(mesh):

time: 123 us -> 124 us (level); the launches traced: 122 us -> 122 us
  Pallas kernels: 17.1 us -> 22.7 us
  other arithmetic: 7.97 us -> 3.47 us
  waiting for transfers between devices: 51.1 us -> 49.2 us
    ppermute x3 -> x4, waiting for transfers between devices: 19.8 us -> 8 us  [the longest x2 5.46 us: body_slabs(): got_x = lax.ppermute(over_x, 'led', planes)]
    ppermute x13 -> x12, waiting for transfers between devices: 31.3 us -> 41.2 us  [permute(): return lax.ppermute(sent, 'slab', pairs)]
    pallas_call x5 -> x14, Pallas kernels: 10.5 us -> 16.1 us  [the longest x1 5.35 us: body_slabs(): local_call(field_kernel, [sent_block] * HALF, [vmem] * (2 + len(FAR) + HA...]
    ppermute x13 -> x12, starting transfers between devices: 39.3 us -> 34.5 us  [permute(): return lax.ppermute(sent, 'slab', pairs)]
    ppermute x3 -> x4, starting transfers between devices: 3.51 us -> 8.05 us  [the longest x2 5.89 us: body_slabs(): got_x = lax.ppermute(over_this, 'led', planes)]
    convert_element_type x4 -> x0, other arithmetic: 4.23 us -> none  [the longest x2 2.19 us: body_slabs(): over = summed(that_near[:, here], got_that[0, :, here], got).astype(bf16)]
    add x2 -> x1, other arithmetic: 2.85 us -> 2.57 us  [body_slabs(): base.append(own_part[:, here] + summed(this_near, got_this[0], got_x))]
  transfers between devices with their start and end apart: 18 -> 20, of which waited for: 8 -> 8; matrix products, arithmetic and copies ran while one was open for 5% -> 2% of each run, Pallas kernels for 5% -> 9%
where the time goes in v8:
time: 124 us; the launch traced here: 122 us
  waiting for transfers between devices  49.2 us (40%)
  starting transfers between devices  43.7 us (35%)
  Pallas kernels  22.7 us (18%)
  other arithmetic  3.47 us (3%)
  local copies, waits for them, and re-layouts  2.41 us (2%)
    ppermute x12, waiting for transfers between devices, permute(): return lax.ppermute(sent, 'slab', pairs)  41.2 us
    ppermute x12, starting transfers between devices, permute(): return lax.ppermute(sent, 'slab', pairs)  34.5 us
    ppermute x2, starting transfers between devices, body_slabs(): got_x = lax.ppermute(over_this, 'led', planes)  5.89 us
    ppermute x2, waiting for transfers between devices, body_slabs(): got_x = lax.ppermute(over_x, 'led', planes)  5.46 us
    pallas_call x1, Pallas kernels, body_slabs(): local_call(field_kernel, [sent_block] * HALF, [vmem] * (2 + len(FAR) + HA...  5.35 us
    pallas_call x2, Pallas kernels, rows_call(): local_call(functools.partial(rows_kernel, which), [sent_block] * count, [...  4.7 us
    pallas_call x2, Pallas kernels, final_call(): pl.pallas_call(final_kernel, out_shape=jax.ShapeDtypeStruct((planes, 2 *...  3.89 us
    pallas_call x2, Pallas kernels, body_slabs(): local_call(functools.partial(sent_kernel, i), [jax.ShapeDtypeStruct((2,)...  3.34 us
  transfers between devices with their start and end apart: 20, of which 8 were waited for; matrix products, arithmetic and copies ran while one was open for 2% of the time, Pallas kernels for 9%

profile of v8, /device:TPU:4, one launch (start us, length us, event | category | flops | bytes accessed | tf_op | source)
XLA Modules:
  0.0 121.8 jit_solution(14386309196992118486)
XLA Ops:
  0.0 0.9 pad_add_fusion.starts
  0.9 2.4 %copy-done.1 = f32[2,256,2048]{2,1,0:T(8,128)S(1)} copy-done((f32[2,256,2048]{2,1,0:T(8,128)S(1)}, f32[2,256,2048]{2,1,0:T(8,128)}, u32[]{:S(2)}) %copy-start.1) | copy-done | bytes 4194328
  3.3 1.4 %windows.1.window = bf16[1024,1024]{1,0:T(8,128)(2,1)S(1)} custom-call(s32[4]{0:T(128)S(1)} %pad_add_fusion.starts, f32[2,256,2048]{2,1,0:T(8,128)S(1)} %copy-done.1), custom_call_target="tpu_custom_call" | custom-call | bytes 6291456 | tf_op jit(solution)/shard_map/windows/pallas_call | solution.py:443
  4.7 1.8 %rows_far.1 = (bf16[4,256,128]{2,1,0:T(8,128)(2,1)S(1)}, bf16[4,256,128]{2,1,0:T(8,128)(2,1)S(1)}, bf16[4,256,128]{2,1,0:T(8,128)(2,1)S(1)}) custom-call(bf16[1024,1024]{1,0:T(8,128)(2,1)S(1)} %windows.1.window, bf16[8,1024,256]{2,1,0:T(8,128)(2,1)S(1)} %copy-done), custom_call_target="tpu_custom_call" | custom-call | flops 1610612736 | bytes 5242880 | tf_op jit(solution)/shard_map/rows_far/pallas_call | solution.py:455
  6.5 0.0 copy-start.2
  6.5 0.0 copy-start.3
  6.5 1.6 %collective-permute-start = (bf16[4,256,128]{2,1,0:T(8,128)(2,1)S(1)}, bf16[4,256,128]{2,1,0:T(8,128)(2,1)S(1)}, u32[]{:S(2)}, u32[]{:S(2)}) collective-permute-start(bf16[4,256,128]{2,1,0:T(8,128)(2,1)S(1)} %get-tuple-element.43), channel_id=1, source_target_pairs={{4,0},{8,16},{12,20},{16,8},{20,12},{24,28},{5,1},{9,17},{13,21},{... | collective-permute-start | bytes 786440 | tf_op jit(solution)/shard_map/ppermute | solution.py:468
  8.1 2.9 %rows_near.1 = (bf16[4,256,128]{2,1,0:T(8,128)(2,1)S(1)}, bf16[4,256,128]{2,1,0:T(8,128)(2,1)S(1)}, bf16[4,256,128]{2,1,0:T(8,128)(2,1)S(1)}, bf16[4,256,128]{2,1,0:T(8,128)(2,1)S(1)}, bf16[4,256,128]{2,1,0:T(8,128)(2,1)S(1)}) custom-call(bf16[1024,1024]{1,0:T(8,128)(2,1)S(1)} %windows.1.window, bf16[8,1024,256]{2,1,0:T(8,128)(2,1)S(1)} %copy-done), custom_call_target="tpu_custom_call" | custom-call | flops 2684354560 | bytes 5242880 | tf_op jit(solution)/shard_map/rows_near/pallas_call | solution.py:455
  11.0 5.7 %collective-permute-start.5 = (bf16[4,256,128]{2,1,0:T(8,128)(2,1)S(1)}, bf16[4,256,128]{2,1,0:T(8,128)(2,1)S(1)}, u32[]{:S(2)}, u32[]{:S(2)}) collective-permute-start(bf16[4,256,128]{2,1,0:T(8,128)(2,1)S(1)} %get-tuple-element.56), channel_id=1, source_target_pairs={{4,12},{8,0},{12,4},{16,24},{20,28},{24,16},{5,13},{9,1},{13,5},{1... | collective-permute-start | bytes 786440 | tf_op jit(solution)/shard_map/ppermute | solution.py:468
  16.6 3.8 %collective-permute-start.1 = (bf16[4,256,128]{2,1,0:T(8,128)(2,1)S(1)}, bf16[4,256,128]{2,1,0:T(8,128)(2,1)S(1)}, u32[]{:S(2)}, u32[]{:S(2)}) collective-permute-start(bf16[4,256,128]{2,1,0:T(8,128)(2,1)S(1)} %get-tuple-element.51), channel_id=1, source_target_pairs={{4,24},{8,28},{12,16},{16,12},{20,0},{24,4},{5,25},{9,29},{13,17},... | collective-permute-start | bytes 786440 | tf_op jit(solution)/shard_map/ppermute | solution.py:468
  20.5 1.9 %collective-permute-start.2 = (bf16[4,256,128]{2,1,0:T(8,128)(2,1)S(1)}, bf16[4,256,128]{2,1,0:T(8,128)(2,1)S(1)}, u32[]{:S(2)}, u32[]{:S(2)}) collective-permute-start(bf16[4,256,128]{2,1,0:T(8,128)(2,1)S(1)} %get-tuple-element.52), channel_id=1, source_target_pairs={{4,28},{8,20},{12,24},{16,4},{20,8},{24,0},{5,29},{9,21},{13,25},{... | collective-permute-start | bytes 786440 | tf_op jit(solution)/shard_map/ppermute | solution.py:468
  22.4 0.0 collective-permute-done.got.rest_0_
  22.5 0.3 collective-permute-start.3
  22.7 6.1 %collective-permute-start.4 = (bf16[4,256,128]{2,1,0:T(8,128)(2,1)S(1)}, bf16[4,256,128]{2,1,0:T(8,128)(2,1)S(1)}, u32[]{:S(2)}, u32[]{:S(2)}) collective-permute-start(bf16[4,256,128]{2,1,0:T(8,128)(2,1)S(1)} %get-tuple-element.55), channel_id=1, source_target_pairs={{4,0},{8,12},{12,8},{16,20},{20,16},{24,28},{5,1},{9,13},{13,9},{1... | collective-permute-start | bytes 786440 | tf_op jit(solution)/shard_map/ppermute | solution.py:468
  28.9 2.3 %collective-permute-start.6 = (bf16[4,256,128]{2,1,0:T(8,128)(2,1)S(1)}, bf16[4,256,128]{2,1,0:T(8,128)(2,1)S(1)}, u32[]{:S(2)}, u32[]{:S(2)}) collective-permute-start(bf16[4,256,128]{2,1,0:T(8,128)(2,1)S(1)} %get-tuple-element.57), channel_id=1, source_target_pairs={{4,8},{8,4},{12,0},{16,28},{20,24},{24,20},{5,9},{9,5},{13,1},{17,... | collective-permute-start | bytes 786440 | tf_op jit(solution)/shard_map/ppermute | solution.py:468
  31.2 0.6 amplitude.1
  31.8 18.9 %collective-permute-done.2.rest_2_ = bf16[4,256,128]{2,1,0:T(8,128)(2,1)S(1)} collective-permute-done((bf16[4,256,128]{2,1,0:T(8,128)(2,1)S(1)}, bf16[4,256,128]{2,1,0:T(8,128)(2,1)S(1)}, u32[]{:S(2)}, u32[]{:S(2)}) %collective-permute-start.2) | collective-permute-done | bytes 262176 | tf_op jit(solution)/shard_map/ppermute | solution.py:468
  50.7 5.4 %modulus_step.1 = (bf16[4,256,128]{2,1,0:T(8,128)(2,1)S(1)}, bf16[4,256,128]{2,1,0:T(8,128)(2,1)S(1)}, bf16[4,256,128]{2,1,0:T(8,128)(2,1)S(1)}, bf16[4,256,128]{2,1,0:T(8,128)(2,1)S(1)}) custom-call(f32[1024,256]{1,0:T(8,128)S(1)} %get-tuple-element.48.amplitude, bf16[8,256,1024]{2,1,0:T(8,128)(2,1)S(1)} %get-tuple-element.49.table, ...), custom_call_target="tpu_custom_call" | custom-call | flops 4294967296 | bytes 12582912 | tf_op jit(solution)/shard_map/modulus_step/pallas_call | solution.py:507
  56.1 4.8 %collective-permute-start.7 = (bf16[4,256,128]{2,1,0:T(8,128)(2,1)S(1)}, bf16[4,256,128]{2,1,0:T(8,128)(2,1)S(1)}, u32[]{:S(2)}, u32[]{:S(2)}) collective-permute-start(bf16[4,256,128]{2,1,0:T(8,128)(2,1)S(1)} %get-tuple-element.59), channel_id=1, source_target_pairs={{0,4},{4,0},{8,12},{12,8},{16,20},{20,16},{24,28},{28,24},{1,5},{5... | collective-permute-start | bytes 786440 | tf_op jit(solution)/shard_map/ppermute | solution.py:468
  60.9 1.5 %collective-permute-start.9 = (bf16[4,256,128]{2,1,0:T(8,128)(2,1)S(1)}, bf16[4,256,128]{2,1,0:T(8,128)(2,1)S(1)}, u32[]{:S(2)}, u32[]{:S(2)}) collective-permute-start(bf16[4,256,128]{2,1,0:T(8,128)(2,1)S(1)} %get-tuple-element.61), channel_id=1, source_target_pairs={{0,12},{4,8},{8,4},{12,0},{16,28},{20,24},{24,20},{28,16},{1,13},{... | collective-permute-start | bytes 786440 | tf_op jit(solution)/shard_map/ppermute | solution.py:468
  62.4 4.7 %collective-permute-done.7.rest_1_ = bf16[4,256,128]{2,1,0:T(8,128)(2,1)S(1)} collective-permute-done((bf16[4,256,128]{2,1,0:T(8,128)(2,1)S(1)}, bf16[4,256,128]{2,1,0:T(8,128)(2,1)S(1)}, u32[]{:S(2)}, u32[]{:S(2)}) %collective-permute-start.7) | collective-permute-done | bytes 262176 | tf_op jit(solution)/shard_map/ppermute | solution.py:468
  67.1 3.0 %collective-permute-done.8.rest_2_ = bf16[4,256,128]{2,1,0:T(8,128)(2,1)S(1)} collective-permute-done((bf16[4,256,128]{2,1,0:T(8,128)(2,1)S(1)}, bf16[4,256,128]{2,1,0:T(8,128)(2,1)S(1)}, u32[]{:S(2)}, u32[]{:S(2)}) %collective-permute-start.8) | collective-permute-done | bytes 262176 | tf_op jit(solution)/shard_map/ppermute | solution.py:468
  70.1 2.7 %collective-permute-done.9.rest_3_ = bf16[4,256,128]{2,1,0:T(8,128)(2,1)S(1)} collective-permute-done((bf16[4,256,128]{2,1,0:T(8,128)(2,1)S(1)}, bf16[4,256,128]{2,1,0:T(8,128)(2,1)S(1)}, u32[]{:S(2)}, u32[]{:S(2)}) %collective-permute-start.9) | collective-permute-done | bytes 262176 | tf_op jit(solution)/shard_map/ppermute | solution.py:468
  72.8 1.7 %update_sent_0.1 = (bf16[2,2,128,512]{3,2,1,0:T(8,128)(2,1)S(1)}, bf16[2,2,128,512]{3,2,1,0:T(8,128)(2,1)S(1)}, bf16[512,512]{1,0:T(8,128)(2,1)S(1)}) custom-call(s32[4]{0:T(128)S(1)} %pad_add_fusion.starts, bf16[8,1024,256]{2,1,0:T(8,128)(2,1)S(1)} %copy-done, bf16[4,256,128]{2,1,0:T(8,128)(2,1)S(1)} %get-tuple-element.58.rest_0_, ...), custom_call_target="tpu_custom_call" | custom-call | flops 536870912 | bytes 6291456 | tf_op jit(solution)/shard_map/update_sent_0/pallas_call | solution.py:547
  74.5 0.1 collective-permute-start.11
  74.6 1.7 %update_sent_1.1 = (bf16[2,2,128,512]{3,2,1,0:T(8,128)(2,1)S(1)}, bf16[2,2,128,512]{3,2,1,0:T(8,128)(2,1)S(1)}, bf16[512,512]{1,0:T(8,128)(2,1)S(1)}) custom-call(s32[4]{0:T(128)S(1)} %pad_add_fusion.starts, bf16[8,1024,256]{2,1,0:T(8,128)(2,1)S(1)} %copy-done, bf16[4,256,128]{2,1,0:T(8,128)(2,1)S(1)} %get-tuple-element.58.rest_0_, ...), custom_call_target="tpu_custom_call" | custom-call | flops 536870912 | bytes 6291456 | tf_op jit(solution)/shard_map/update_sent_1/pallas_call | solution.py:547
  76.3 0.6 collective-permute-start.15
  76.8 0.1 collective-permute-start.10
  76.9 0.4 collective-permute-start.17
  77.3 1.5 %update_kept_0.1 = (f32[2,128,512]{2,1,0:T(8,128)S(1)}, f32[2,128,512]{2,1,0:T(8,128)S(1)}, f32[2,128,512]{2,1,0:T(8,128)S(1)}, f32[2,128,512]{2,1,0:T(8,128)S(1)}) custom-call(s32[4]{0:T(128)S(1)} %pad_add_fusion.starts, bf16[8,1024,256]{2,1,0:T(8,128)(2,1)S(1)} %copy-done, bf16[512,512]{1,0:T(8,128)(2,1)S(1)} %get-tuple-element.62.back), custom_call_target="tpu_custom_call" | custom-call | flops 536870912 | bytes 8388608 | tf_op jit(solution)/shard_map/update_kept_0/pallas_call | solution.py:570
  78.9 0.1 over_x_0.1
  79.0 1.6 %collective-permute-start.12 = (bf16[2,128,512]{2,1,0:T(8,128)(2,1)S(1)}, bf16[2,128,512]{2,1,0:T(8,128)(2,1)S(1)}, u32[]{:S(2)}, u32[]{:S(2)}) collective-permute-start(bf16[2,128,512]{2,1,0:T(8,128)(2,1)S(1)} %over_x_0.1), channel_id=1, source_target_pairs={{0,2},{2,0},{1,3},{3,1},{4,6},{6,4},{5,7},{7,5},{8,10},{10,8},{9,1... | collective-permute-start | bytes 786440 | tf_op jit(solution)/shard_map/ppermute | solution.py:580
  80.5 1.5 %update_kept_1.1 = (f32[2,128,512]{2,1,0:T(8,128)S(1)}, f32[2,128,512]{2,1,0:T(8,128)S(1)}, f32[2,128,512]{2,1,0:T(8,128)S(1)}, f32[2,128,512]{2,1,0:T(8,128)S(1)}) custom-call(s32[4]{0:T(128)S(1)} %pad_add_fusion.starts, bf16[8,1024,256]{2,1,0:T(8,128)(2,1)S(1)} %copy-done, bf16[512,512]{1,0:T(8,128)(2,1)S(1)} %get-tuple-element.71.back), custom_call_target="tpu_custom_call" | custom-call | flops 536870912 | bytes 8388608 | tf_op jit(solution)/shard_map/update_kept_1/pallas_call | solution.py:570
  82.1 0.6 collective-permute-start.16
  82.7 5.5 %collective-permute-done.12.refs_2_ = bf16[2,128,512]{2,1,0:T(8,128)(2,1)S(1)} collective-permute-done((bf16[2,128,512]{2,1,0:T(8,128)(2,1)S(1)}, bf16[2,128,512]{2,1,0:T(8,128)(2,1)S(1)}, u32[]{:S(2)}, u32[]{:S(2)}) %collective-permute-start.12) | collective-permute-done | bytes 262176 | tf_op jit(solution)/shard_map/ppermute | solution.py:580
  88.2 0.1 over_z_0.1
  88.3 4.6 %collective-permute-start.14 = (bf16[2,128,512]{2,1,0:T(8,128)(2,1)S(1)}, bf16[2,128,512]{2,1,0:T(8,128)(2,1)S(1)}, u32[]{:S(2)}, u32[]{:S(2)}) collective-permute-start(bf16[2,128,512]{2,1,0:T(8,128)(2,1)S(1)} %over_z_0.1), channel_id=1, source_target_pairs={{0,16},{4,20},{8,24},{20,4},{24,8},{28,12},{1,17},{5,21},{9,25},{2... | collective-permute-start | bytes 786440 | tf_op jit(solution)/shard_map/ppermute | solution.py:468
  93.0 0.1 over_this_1.1
  93.0 1.5 %collective-permute-start.13 = (bf16[2,128,512]{2,1,0:T(8,128)(2,1)S(1)}, bf16[2,128,512]{2,1,0:T(8,128)(2,1)S(1)}, u32[]{:S(2)}, u32[]{:S(2)}) collective-permute-start(bf16[2,128,512]{2,1,0:T(8,128)(2,1)S(1)} %over_this_0.1), channel_id=1, source_target_pairs={{0,2},{2,0},{1,3},{3,1},{4,6},{6,4},{5,7},{7,5},{8,10},{10,8},{9,1... | collective-permute-start | bytes 786440 | tf_op jit(solution)/shard_map/ppermute | solution.py:588
  94.6 11.6 %collective-permute-done.14.refs_1_ = bf16[2,128,512]{2,1,0:T(8,128)(2,1)S(1)} collective-permute-done((bf16[2,128,512]{2,1,0:T(8,128)(2,1)S(1)}, bf16[2,128,512]{2,1,0:T(8,128)(2,1)S(1)}, u32[]{:S(2)}, u32[]{:S(2)}) %collective-permute-start.14) | collective-permute-done | bytes 262176 | tf_op jit(solution)/shard_map/ppermute | solution.py:468
  106.1 0.1 over_z_1.1
  106.2 4.3 %collective-permute-start.18 = (bf16[2,128,512]{2,1,0:T(8,128)(2,1)S(1)}, bf16[2,128,512]{2,1,0:T(8,128)(2,1)}, u32[]{:S(2)}, u32[]{:S(2)}) collective-permute-start(bf16[2,128,512]{2,1,0:T(8,128)(2,1)S(1)} %over_this_1.1), channel_id=1, source_target_pairs={{0,2},{2,0},{1,3},{3,1},{4,6},{6,4},{5,7},{7,5},{8,10},{10,8},{9,1... | collective-permute-start | bytes 786440 | tf_op jit(solution)/shard_map/ppermute | solution.py:588
  110.6 1.9 %collective-permute-start.19 = (bf16[2,128,512]{2,1,0:T(8,128)(2,1)S(1)}, bf16[2,128,512]{2,1,0:T(8,128)(2,1)}, u32[]{:S(2)}, u32[]{:S(2)}) collective-permute-start(bf16[2,128,512]{2,1,0:T(8,128)(2,1)S(1)} %over_z_1.1), channel_id=1, source_target_pairs={{0,16},{4,20},{8,24},{20,4},{24,8},{28,12},{1,17},{5,21},{9,25},{2... | collective-permute-start | bytes 786440 | tf_op jit(solution)/shard_map/ppermute | solution.py:468
  112.5 2.5 %collective-permute-done.18 = bf16[2,128,512]{2,1,0:T(8,128)(2,1)} collective-permute-done((bf16[2,128,512]{2,1,0:T(8,128)(2,1)S(1)}, bf16[2,128,512]{2,1,0:T(8,128)(2,1)}, u32[]{:S(2)}, u32[]{:S(2)}) %collective-permute-start.18) | collective-permute-done | bytes 262176 | tf_op jit(solution)/shard_map/ppermute | solution.py:588
  115.0 2.6 %dynamic-slice_add_fusion = (f32[2,128,512]{2,1,0:T(8,128)}, f32[2,128,512]{2,1,0:T(8,128)}) fusion(f32[2,256,2048]{2,1,0:T(8,128)} %spectrum.1, s32[]{:T(128)S(6)} %add.29, s32[]{:T(128)S(6)} %select_n.3, f32[2,128,512]{2,1,0:T(8,128)S(1)} %get-tuple-element.75, bf16[2,128,512]{2,1,0:T(8,128)(2,1)} %collective-permute-done.18, ...), kind=kLoop, calls=%fused_computation | loop fusion | flops 1310720 | bytes 4194312 | tf_op jit(solution)/shard_map/add | solution.py:590
  117.6 1.9 %updated_0.1.refs_0_ = f32[2,256,512]{2,1,0:T(8,128)} custom-call(f32[2,128,512]{2,1,0:T(8,128)} %get-tuple-element.82.refs_0_, bf16[2,128,512]{2,1,0:T(8,128)(2,1)} %copy-done.4), custom_call_target="tpu_custom_call" | custom-call | bytes 1048576 | tf_op jit(solution)/shard_map/updated_0/pallas_call | solution.py:397
  119.6 0.3 collective-permute-done.19.refs_2_
  119.8 1.9 %updated_1.1 = f32[2,256,512]{2,1,0:T(8,128)} custom-call(f32[2,256,512]{2,1,0:T(8,128)} %updated_0.1.refs_0_, f32[2,128,512]{2,1,0:T(8,128)} %get-tuple-element.81.refs_1_, bf16[2,128,512]{2,1,0:T(8,128)(2,1)} %collective-permute-done.19.refs_2_), custom_call_target="tpu_custom_call", output_to_operand_aliasing={{}: (0, {})} | custom-call | bytes 1048576 | tf_op jit(solution)/shard_map/updated_1/pallas_call | solution.py:397
  (22 shorter events, 0.2 us)
Async XLA Ops:
  0.0 4.6 %copy-start = (bf16[8,1024,256]{2,1,0:T(8,128)(2,1)S(1)}, bf16[8,1024,256]{2,1,0:T(8,128)(2,1)}, u32[]{:S(2)}) copy-start(bf16[8,1024,256]{2,1,0:T(8,128)(2,1)} %constant.15.clone.table) | copy-start | bytes 12582916
  0.9 2.4 %copy-start.1 = (f32[2,256,2048]{2,1,0:T(8,128)S(1)}, f32[2,256,2048]{2,1,0:T(8,128)}, u32[]{:S(2)}) copy-start(f32[2,256,2048]{2,1,0:T(8,128)} %spectrum.1) | copy-start | bytes 12582916
  6.5 24.7 %copy-start.2 = (bf16[8,256,1024]{2,1,0:T(8,128)(2,1)S(1)}, bf16[8,256,1024]{2,1,0:T(8,128)(2,1)}, u32[]{:S(2)}) copy-start(bf16[8,256,1024]{2,1,0:T(8,128)(2,1)} %constant.14.clone.table) | copy-start | bytes 12582916
  6.5 24.7 %copy-start.3 = (f32[2,128,1024]{2,1,0:T(8,128)S(1)}, f32[2,128,1024]{2,1,0:T(8,128)}, u32[]{:S(2)}) copy-start(f32[2,128,1024]{2,1,0:T(8,128)} %images) | copy-start | bytes 3145732
  6.5 15.9 %collective-permute-start = (bf16[4,256,128]{2,1,0:T(8,128)(2,1)S(1)}, bf16[4,256,128]{2,1,0:T(8,128)(2,1)S(1)}, u32[]{:S(2)}, u32[]{:S(2)}) collective-permute-start(bf16[4,256,128]{2,1,0:T(8,128)(2,1)S(1)} %get-tuple-element.43), channel_id=1, source_target_pairs={{4,0},{8,16},{12,20},{16,8},{20,12},{24,28},{5,1},{9,17},{13,21},{... | collective-permute-start | bytes 786440 | tf_op jit(solution)/shard_map/ppermute | solution.py:468
  11.0 17.9 %collective-permute-start.5 = (bf16[4,256,128]{2,1,0:T(8,128)(2,1)S(1)}, bf16[4,256,128]{2,1,0:T(8,128)(2,1)S(1)}, u32[]{:S(2)}, u32[]{:S(2)}) collective-permute-start(bf16[4,256,128]{2,1,0:T(8,128)(2,1)S(1)} %get-tuple-element.56), channel_id=1, source_target_pairs={{4,12},{8,0},{12,4},{16,24},{20,28},{24,16},{5,13},{9,1},{13,5},{1... | collective-permute-start | bytes 786440 | tf_op jit(solution)/shard_map/ppermute | solution.py:468
  16.6 15.1 %collective-permute-start.1 = (bf16[4,256,128]{2,1,0:T(8,128)(2,1)S(1)}, bf16[4,256,128]{2,1,0:T(8,128)(2,1)S(1)}, u32[]{:S(2)}, u32[]{:S(2)}) collective-permute-start(bf16[4,256,128]{2,1,0:T(8,128)(2,1)S(1)} %get-tuple-element.51), channel_id=1, source_target_pairs={{4,24},{8,28},{12,16},{16,12},{20,0},{24,4},{5,25},{9,29},{13,17},... | collective-permute-start | bytes 786440 | tf_op jit(solution)/shard_map/ppermute | solution.py:468
  20.5 30.2 %collective-permute-start.2 = (bf16[4,256,128]{2,1,0:T(8,128)(2,1)S(1)}, bf16[4,256,128]{2,1,0:T(8,128)(2,1)S(1)}, u32[]{:S(2)}, u32[]{:S(2)}) collective-permute-start(bf16[4,256,128]{2,1,0:T(8,128)(2,1)S(1)} %get-tuple-element.52), channel_id=1, source_target_pairs={{4,28},{8,20},{12,24},{16,4},{20,8},{24,0},{5,29},{9,21},{13,25},{... | collective-permute-start | bytes 786440 | tf_op jit(solution)/shard_map/ppermute | solution.py:468
  22.5 28.2 %collective-permute-start.3 = (bf16[4,256,128]{2,1,0:T(8,128)(2,1)S(1)}, bf16[4,256,128]{2,1,0:T(8,128)(2,1)S(1)}, u32[]{:S(2)}, u32[]{:S(2)}) collective-permute-start(bf16[4,256,128]{2,1,0:T(8,128)(2,1)S(1)} %last_far_blocks.1), channel_id=1, source_target_pairs={{4,20},{8,24},{12,28},{16,0},{20,4},{24,8},{0,16},{28,12},{5,21},{... | collective-permute-start | bytes 786440 | tf_op jit(solution)/shard_map/ppermute | solution.py:468
  22.7 28.0 %collective-permute-start.4 = (bf16[4,256,128]{2,1,0:T(8,128)(2,1)S(1)}, bf16[4,256,128]{2,1,0:T(8,128)(2,1)S(1)}, u32[]{:S(2)}, u32[]{:S(2)}) collective-permute-start(bf16[4,256,128]{2,1,0:T(8,128)(2,1)S(1)} %get-tuple-element.55), channel_id=1, source_target_pairs={{4,0},{8,12},{12,8},{16,20},{20,16},{24,28},{5,1},{9,13},{13,9},{1... | collective-permute-start | bytes 786440 | tf_op jit(solution)/shard_map/ppermute | solution.py:468
  28.9 21.9 %collective-permute-start.6 = (bf16[4,256,128]{2,1,0:T(8,128)(2,1)S(1)}, bf16[4,256,128]{2,1,0:T(8,128)(2,1)S(1)}, u32[]{:S(2)}, u32[]{:S(2)}) collective-permute-start(bf16[4,256,128]{2,1,0:T(8,128)(2,1)S(1)} %get-tuple-element.57), channel_id=1, source_target_pairs={{4,8},{8,4},{12,0},{16,28},{20,24},{24,20},{5,9},{9,5},{13,1},{17,... | collective-permute-start | bytes 786440 | tf_op jit(solution)/shard_map/ppermute | solution.py:468
  56.1 11.0 %collective-permute-start.7 = (bf16[4,256,128]{2,1,0:T(8,128)(2,1)S(1)}, bf16[4,256,128]{2,1,0:T(8,128)(2,1)S(1)}, u32[]{:S(2)}, u32[]{:S(2)}) collective-permute-start(bf16[4,256,128]{2,1,0:T(8,128)(2,1)S(1)} %get-tuple-element.59), channel_id=1, source_target_pairs={{0,4},{4,0},{8,12},{12,8},{16,20},{20,16},{24,28},{28,24},{1,5},{5... | collective-permute-start | bytes 786440 | tf_op jit(solution)/shard_map/ppermute | solution.py:468
  60.8 9.2 %collective-permute-start.8 = (bf16[4,256,128]{2,1,0:T(8,128)(2,1)S(1)}, bf16[4,256,128]{2,1,0:T(8,128)(2,1)S(1)}, u32[]{:S(2)}, u32[]{:S(2)}) collective-permute-start(bf16[4,256,128]{2,1,0:T(8,128)(2,1)S(1)} %get-tuple-element.60), channel_id=1, source_target_pairs={{0,8},{4,12},{8,0},{12,4},{16,24},{20,28},{24,16},{28,20},{1,9},{5... | collective-permute-start | bytes 786440 | tf_op jit(solution)/shard_map/ppermute | solution.py:468
  60.9 12.0 %collective-permute-start.9 = (bf16[4,256,128]{2,1,0:T(8,128)(2,1)S(1)}, bf16[4,256,128]{2,1,0:T(8,128)(2,1)S(1)}, u32[]{:S(2)}, u32[]{:S(2)}) collective-permute-start(bf16[4,256,128]{2,1,0:T(8,128)(2,1)S(1)} %get-tuple-element.61), channel_id=1, source_target_pairs={{0,12},{4,8},{8,4},{12,0},{16,28},{20,24},{24,20},{28,16},{1,13},{... | collective-permute-start | bytes 786440 | tf_op jit(solution)/shard_map/ppermute | solution.py:468
  74.5 4.4 %collective-permute-start.11 = (bf16[2,2,128,512]{3,2,1,0:T(8,128)(2,1)S(1)}, bf16[2,2,128,512]{3,2,1,0:T(8,128)(2,1)S(1)}, u32[]{:S(2)}, u32[]{:S(2)}) collective-permute-start(bf16[2,2,128,512]{3,2,1,0:T(8,128)(2,1)S(1)} %get-tuple-element.67), channel_id=1, source_target_pairs={{0,1},{1,0},{2,3},{3,2},{4,5},{5,4},{6,7},{7,6},{8,9},{9,8},{10,11... | collective-permute-start | bytes 1572872 | tf_op jit(solution)/shard_map/ppermute | solution.py:560
  76.3 5.8 %collective-permute-start.15 = (bf16[2,2,128,512]{3,2,1,0:T(8,128)(2,1)S(1)}, bf16[2,2,128,512]{3,2,1,0:T(8,128)(2,1)S(1)}, u32[]{:S(2)}, u32[]{:S(2)}) collective-permute-start(bf16[2,2,128,512]{3,2,1,0:T(8,128)(2,1)S(1)} %get-tuple-element.73), channel_id=1, source_target_pairs={{0,1},{1,0},{2,3},{3,2},{4,5},{5,4},{6,7},{7,6},{8,9},{9,8},{10,11... | collective-permute-start | bytes 1572872 | tf_op jit(solution)/shard_map/ppermute | solution.py:560
  76.8 16.1 %collective-permute-start.10 = (bf16[2,2,128,512]{3,2,1,0:T(8,128)(2,1)S(1)}, bf16[2,2,128,512]{3,2,1,0:T(8,128)(2,1)S(1)}, u32[]{:S(2)}, u32[]{:S(2)}) collective-permute-start(bf16[2,2,128,512]{3,2,1,0:T(8,128)(2,1)S(1)} %get-tuple-element.64), channel_id=1, source_target_pairs={{0,1},{1,0},{2,3},{3,2},{4,5},{5,4},{6,7},{7,6},{8,9},{9,8},{10,11... | collective-permute-start | bytes 1572872 | tf_op jit(solution)/shard_map/ppermute | solution.py:585
  76.9 16.0 %collective-permute-start.17 = (bf16[2,2,128,512]{3,2,1,0:T(8,128)(2,1)S(1)}, bf16[2,2,128,512]{3,2,1,0:T(8,128)(2,1)S(1)}, u32[]{:S(2)}, u32[]{:S(2)}) collective-permute-start(bf16[2,2,128,512]{3,2,1,0:T(8,128)(2,1)S(1)} %get-tuple-element.76), channel_id=1, source_target_pairs={{0,1},{1,0},{2,3},{3,2},{4,5},{5,4},{6,7},{7,6},{8,9},{9,8},{10,11... | collective-permute-start | bytes 1572872 | tf_op jit(solution)/shard_map/ppermute | solution.py:585
  79.0 9.2 %collective-permute-start.12 = (bf16[2,128,512]{2,1,0:T(8,128)(2,1)S(1)}, bf16[2,128,512]{2,1,0:T(8,128)(2,1)S(1)}, u32[]{:S(2)}, u32[]{:S(2)}) collective-permute-start(bf16[2,128,512]{2,1,0:T(8,128)(2,1)S(1)} %over_x_0.1), channel_id=1, source_target_pairs={{0,2},{2,0},{1,3},{3,1},{4,6},{6,4},{5,7},{7,5},{8,10},{10,8},{9,1... | collective-permute-start | bytes 786440 | tf_op jit(solution)/shard_map/ppermute | solution.py:580
  82.1 12.4 %collective-permute-start.16 = (bf16[2,128,512]{2,1,0:T(8,128)(2,1)S(1)}, bf16[2,128,512]{2,1,0:T(8,128)(2,1)S(1)}, u32[]{:S(2)}, u32[]{:S(2)}) collective-permute-start(bf16[2,128,512]{2,1,0:T(8,128)(2,1)S(1)} %over_x_1.1), channel_id=1, source_target_pairs={{0,2},{2,0},{1,3},{3,1},{4,6},{6,4},{5,7},{7,5},{8,10},{10,8},{9,1... | collective-permute-start | bytes 786440 | tf_op jit(solution)/shard_map/ppermute | solution.py:580
  88.3 17.9 %collective-permute-start.14 = (bf16[2,128,512]{2,1,0:T(8,128)(2,1)S(1)}, bf16[2,128,512]{2,1,0:T(8,128)(2,1)S(1)}, u32[]{:S(2)}, u32[]{:S(2)}) collective-permute-start(bf16[2,128,512]{2,1,0:T(8,128)(2,1)S(1)} %over_z_0.1), channel_id=1, source_target_pairs={{0,16},{4,20},{8,24},{20,4},{24,8},{28,12},{1,17},{5,21},{9,25},{2... | collective-permute-start | bytes 786440 | tf_op jit(solution)/shard_map/ppermute | solution.py:468
  93.0 19.5 %collective-permute-start.13 = (bf16[2,128,512]{2,1,0:T(8,128)(2,1)S(1)}, bf16[2,128,512]{2,1,0:T(8,128)(2,1)S(1)}, u32[]{:S(2)}, u32[]{:S(2)}) collective-permute-start(bf16[2,128,512]{2,1,0:T(8,128)(2,1)S(1)} %over_this_0.1), channel_id=1, source_target_pairs={{0,2},{2,0},{1,3},{3,1},{4,6},{6,4},{5,7},{7,5},{8,10},{10,8},{9,1... | collective-permute-start | bytes 786440 | tf_op jit(solution)/shard_map/ppermute | solution.py:588
  106.1 11.5 %copy-start.4 = (bf16[2,128,512]{2,1,0:T(8,128)(2,1)}, bf16[2,128,512]{2,1,0:T(8,128)(2,1)S(1)}, u32[]{:S(2)}) copy-start(bf16[2,128,512]{2,1,0:T(8,128)(2,1)S(1)} %collective-permute-done.14.refs_1_) | copy-start | bytes 786436
  106.2 8.8 %collective-permute-start.18 = (bf16[2,128,512]{2,1,0:T(8,128)(2,1)S(1)}, bf16[2,128,512]{2,1,0:T(8,128)(2,1)}, u32[]{:S(2)}, u32[]{:S(2)}) collective-permute-start(bf16[2,128,512]{2,1,0:T(8,128)(2,1)S(1)} %over_this_1.1), channel_id=1, source_target_pairs={{0,2},{2,0},{1,3},{3,1},{4,6},{6,4},{5,7},{7,5},{8,10},{10,8},{9,1... | collective-permute-start | bytes 786440 | tf_op jit(solution)/shard_map/ppermute | solution.py:588
  110.6 9.3 %collective-permute-start.19 = (bf16[2,128,512]{2,1,0:T(8,128)(2,1)S(1)}, bf16[2,128,512]{2,1,0:T(8,128)(2,1)}, u32[]{:S(2)}, u32[]{:S(2)}) collective-permute-start(bf16[2,128,512]{2,1,0:T(8,128)(2,1)S(1)} %over_z_1.1), channel_id=1, source_target_pairs={{0,16},{4,20},{8,24},{20,4},{24,8},{28,12},{1,17},{5,21},{9,25},{2... | collective-permute-start | bytes 786440 | tf_op jit(solution)/shard_map/ppermute | solution.py:468

commit v9 on v7

--- a/solution.py
+++ b/solution.py
@@ -145,8 +145,26 @@
 SLABS = 8
 HALF = 4
 FIRST, LAST = 0, 7
-PASSED = {1: 0, 6: 7}
-INNER = (2, 3, 4, 5)
+HANDED = {1: (0, 4), 6: (7, 3)}
+FAR = (
+    {1: 4, 2: 4, 3: 5, 4: 2, 5: 3, 6: 3},
+    {1: 6, 2: 7, 3: 4, 4: 3, 5: 0, 6: 1},
+    {1: 7, 2: 5, 3: 6, 4: 1, 5: 2, 6: 0},
+    {1: 5, 2: 6, 3: 7, 4: 0, 5: 1, 6: 2},
+)
+
+
+def look_up(position, table):
+    return sum(jnp.where(position == slab, value, 0) for slab, value in table.items())
+
+
+def origins(far):
+    table = {to: slab for slab, to in far.items()}
+    if far is FAR[0]:
+        table = {to: slab for slab, to in far.items() if slab not in HANDED}
+    if far is FAR[-1]:
+        table.update({to: slab for slab, (_, to) in HANDED.items()})
+    return table
 
 
 def dot(left, right):
@@ -199,19 +217,16 @@
             window[at : at + rows, :] = jnp.where(inside, value, 0.0).astype(jnp.bfloat16)
 
 
-def classes_of(position):
-    hands_over = is_one_of(position, PASSED)
-    return (jnp.where(hands_over, 5, 6), 7, 2, 4, jnp.where(hands_over, 6, 5), 0, 1, 3)
-
-
 def rows_kernel(which, window, table, *outs):
     position = lax.axis_index("slab")
-    for out, d in zip(outs, classes_of(position)[which]):
-        store_parts(out, row_block(window[...], table[jnp.bitwise_xor(position, d)]))
+    blocks = [look_up(position, far) for far in FAR]
+    blocks += [jnp.bitwise_xor(position, d) for d in (0, 2, 1, 3)]
+    for out, block in zip(outs, blocks[which]):
+        store_parts(out, row_block(window[...], table[block]))
 
 
 def choose_kernel(got, own, out):
-    passes = is_one_of(lax.axis_index("slab"), PASSED.values())
+    passes = is_one_of(lax.axis_index("slab"), [by for by, _ in HANDED.values()])
 
     @pl.when(passes)
     def _():
@@ -232,9 +247,9 @@
 
 
 def field_kernel(amplitude, table, *rest):
-    far, near = rest[:5], rest[5 : HALF + 5]
-    outs = rest[HALF + 5 : 2 * HALF + 5]
-    field_in, diff, strips = rest[2 * HALF + 5 :]
+    far, near = rest[: len(FAR)], rest[len(FAR) : len(FAR) + HALF]
+    outs = rest[len(FAR) + HALF : len(FAR) + 2 * HALF]
+    field_in, diff, strips = rest[len(FAR) + 2 * HALF :]
     position = lax.axis_index("slab")
     parts, rows, _ = near[0].shape
     half = parts // 2 * LANES
@@ -253,21 +268,12 @@
             cols = slice(part * LANES, (part + 1) * LANES)
             field_in[pl.ds(at, rows), cols] += block[part]
 
-    passes = is_one_of(position, PASSED.values())
-    hands_over = is_one_of(position, PASSED)
-    ends = is_one_of(position, [to ^ 4 for to in PASSED.values()])
-
-    @pl.when(is_one_of(position, INNER))
-    def _():
-        add(far[0], jnp.bitwise_xor(position, 6))
-        add(far[1], jnp.bitwise_xor(position, 7))
-        add(far[2], jnp.bitwise_xor(position, jnp.where(ends, 5, 4)))
-
-    @pl.when(jnp.logical_or(passes, hands_over))
-    def _():
-        add(far[2], jnp.bitwise_xor(position, 4))
-        add(far[3], jnp.bitwise_xor(position, jnp.where(hands_over, 7, 6)))
-        add(far[4], jnp.bitwise_xor(position, 5))
+    for block, permute in zip(far, FAR):
+        table_of = origins(permute)
+
+        @pl.when(is_one_of(position, table_of))
+        def _():
+            add(block, look_up(position, table_of))
 
     for first in range(0, steps, group):
         product = dot(
@@ -370,6 +376,32 @@
     update_columns(True, starts, table, back, outs)
 
 
+def z_first_kernel(that_near, that_far, got_that, out):
+    cols = out.shape[3]
+    for i, kept in enumerate((that_near, that_far)):
+        total = kept[:, :, :cols] + got_that[i, :, :, :cols].astype(jnp.float32)
+        out[i] = total.astype(out.dtype)
+
+
+def x_first_kernel(that_far, got_that, out):
+    cols = that_far.shape[2] - out.shape[2]
+    total = that_far[:, :, cols:] + got_that[1, :, :, cols:].astype(jnp.float32)
+    out[...] = total.astype(out.dtype)
+
+
+def z_second_kernel(that_near, got_that, got_x, out):
+    cols = that_near.shape[2] - out.shape[2]
+    total = that_near[:, :, cols:] + got_that[0, :, :, cols:].astype(jnp.float32)
+    out[...] = (total + got_x[...].astype(jnp.float32)).astype(out.dtype)
+
+
+def x_second_kernel(this_far, got_this, got_z, out):
+    cols = got_z.shape[3]
+    total = this_far[...] + got_this[1].astype(jnp.float32)
+    out[:, :, cols:] = total[:, :, cols:].astype(out.dtype)
+    out[:, :, :cols] = (total[:, :, :cols] + got_z[1].astype(jnp.float32)).astype(out.dtype)
+
+
 def local_call(kernel, out_shape, spaces, scratch, flops, moved, name):
     return pl.pallas_call(
         kernel,
@@ -414,7 +446,7 @@
         "windows",
     )(starts, spectrum)
 
-    def rows_call(which, name):
+    def rows_call(which, name, window):
         count = which.stop - which.start
         return local_call(
             functools.partial(rows_kernel, which),
@@ -426,7 +458,7 @@
             name,
         )(window, by_col)
 
-    first_a, first_b, near_2 = rows_call(slice(0, 3), "rows_round_1")
+    *far_sent, last = rows_call(slice(0, 4), "rows_far", window)
 
     def permute(sent, pairs):
         return lax.ppermute(sent, "slab", pairs)
@@ -436,23 +468,21 @@
             choose_kernel, sent_block, [vmem] * 2, [], 0, 2**19, name
         )(got, own)
 
-    handed = list(PASSED.items())
     windowed = range(FIRST + 1, LAST)
-    got_a = permute(first_a, [(s, s ^ 6) for s in INNER] + handed)
-    got_b = permute(first_b, [(s, s ^ 7) for s in INNER] + handed)
+    far_columns = []
+    for far, sent in zip(FAR, far_sent):
+        pairs = dict(far)
+        if far is FAR[0]:
+            pairs.update({slab: by for slab, (by, _) in HANDED.items()})
+        far_columns.append(permute(sent, list(pairs.items())))
+    far_columns[0], window, images = lax.optimization_barrier((far_columns[0], window, images))
+    last = local_call(
+        choose_kernel, sent_block, [vmem] * 2, [], 0, 2**19, "last_far_blocks"
+    )(far_columns[0], last)
+    near_0, near_2, near_1, near_3 = rows_call(slice(4, SLABS), "rows_near", window)
+    pairs = list(FAR[-1].items()) + list(HANDED.values())
+    far_columns.append(permute(last, pairs))
     near_2 = permute(near_2, [(s, s ^ 2) for s in windowed])
-    second_a, second_b, near_0, near_1, near_3 = rows_call(slice(3, SLABS), "rows_round_2")
-    got_a, second_a, second_b, near_1, near_3, images = lax.optimization_barrier(
-        (got_a, second_a, second_b, near_1, near_3, images)
-    )
-    outer_pairs = [(s, s ^ 6) for s in range(SLABS) if s not in INNER]
-    far_columns = [
-        got_a,
-        got_b,
-        permute(choose(got_a, second_a, "class_4_blocks"), [(s, s ^ 4) for s in range(SLABS)]),
-        permute(choose(got_b, second_b, "class_6_blocks"), outer_pairs),
-        permute(second_b, [(s, s ^ 5) for s in INNER]),
-    ]
     near_1 = permute(near_1, [(s, s ^ 1) for s in windowed])
     near_3 = permute(near_3, [(s, s ^ 3) for s in windowed])
     near_columns = [near_0, near_1, near_2, near_3]
@@ -471,7 +501,7 @@
     strips = local_call(
         field_kernel,
         [sent_block] * HALF,
-        [vmem] * 11,
+        [vmem] * (2 + len(FAR) + HALF),
         [pltpu.VMEM((width, parts * block), bf16)] * 2
         + [pltpu.VMEM((HALF,) + sent_block.shape, bf16)],
         16 * leds * block * width * width,
@@ -488,7 +518,11 @@
         permute(strips[d], [(s, s ^ d) for s in range(SLABS)]) for d in range(1, HALF)
     ]
     share = width // 2
+    first = share // 4
     piece = (2, rows, share)
+    cores = [(0, 1), (1, 0), (2, 3), (3, 2)]
+    planes = [(0, 2), (2, 0), (1, 3), (3, 1)]
+    across = [(s, s ^ 4) for s in range(SLABS) if FIRST < s ^ 4 < LAST]
     sent_this, sent_that, back = local_call(
         sent_kernel,
         [
@@ -502,8 +536,6 @@
         8 * 2**20,
         "update_sent",
     )(starts, by_col, *home)
-    cores = [(0, 1), (1, 0), (2, 3), (3, 2)]
-    planes = [(0, 2), (2, 0), (1, 3), (3, 1)]
     got_that = lax.ppermute(sent_that, "led", cores)
     got_this = lax.ppermute(sent_this, "led", cores)
     this_near, this_far, that_near, that_far = local_call(
@@ -516,30 +548,29 @@
         "update_kept",
     )(starts, by_col, back)
 
-    def summed(*values):
-        return sum(value.astype(jnp.float32) for value in values)
-
-    across = [(s, s ^ 4) for s in range(SLABS) if FIRST < s ^ 4 < LAST]
-    from_x = []
-    for i in range(2):
-        here = slice(i * rows // 2, (i + 1) * rows // 2)
-        over = summed(that_far[:, here], got_that[1, :, here]).astype(bf16)
-        from_x.append((here, lax.ppermute(over, "led", planes)))
-    from_z = []
-    over = None
-    over_this = summed(this_far, got_this[1]).astype(bf16)
-    for here, got in from_x:
-        if over is None:
-            got, over_this = lax.optimization_barrier((got, over_this))
-        else:
-            over, got = lax.optimization_barrier((over, got))
-        over = summed(that_near[:, here], got_that[0, :, here], got).astype(bf16)
-        from_z.append(permute(over, across))
-    over_this = lax.ppermute(over_this, "led", planes)
-    own_part = lax.dynamic_slice_in_dim(spectrum, led_at * share, share, 2)
-    base = own_part + summed(this_near, got_this[0], over_this)
-    base, *from_z = lax.optimization_barrier((base, *from_z))
-    return base + summed(jnp.concatenate(from_z, 1))
+    def sum_call(kernel, shape, *values):
+        out_shape = jax.ShapeDtypeStruct(shape, bf16)
+        specs = [vmem] * len(values)
+        return local_call(kernel, out_shape, specs, [], 0, 2**20, kernel.__name__)(*values)
+
+    over = sum_call(z_first_kernel, (2, 2, rows, first), that_near, that_far, got_that)
+    got_z_first = permute(over, across)
+    over = sum_call(x_first_kernel, (2, rows, share - first), that_far, got_that)
+    got_x = lax.ppermute(over, "led", planes)
+    over = sum_call(z_second_kernel, (2, rows, share - first), that_near, got_that, got_x)
+    got_z_second = permute(over, across)
+    over = sum_call(x_second_kernel, piece, this_far, got_this, got_z_first)
+    got_x = lax.ppermute(over, "led", planes)
+
+    def widen(value, before):
+        after = share - before - value.shape[2]
+        return jnp.pad(value.astype(jnp.float32), ((0, 0), (0, 0), (before, after)))
+
+    base = lax.dynamic_slice_in_dim(spectrum, led_at * share, share, 2)
+    base += this_near + got_this[0].astype(jnp.float32) + got_x.astype(jnp.float32)
+    base += widen(got_z_first[0], 0)
+    base, got_z_second = lax.optimization_barrier((base, got_z_second))
+    return base + widen(got_z_second, first)
 
 
 def solution(mesh):

time: 123 us -> 120 us (0.976)
  other arithmetic: 7.97 us -> 4.04 us
  Pallas kernels: 17.1 us -> 19.9 us
  waiting for transfers between devices: 51.1 us -> 48.7 us
    ppermute x3 -> x2, waiting for transfers between devices: 19.8 us -> 9.63 us  [body_slabs(): got_x = lax.ppermute(over, 'led', planes)]
    ppermute x13 -> x12, waiting for transfers between devices: 31.3 us -> 39.1 us  [permute(): return lax.ppermute(sent, 'slab', pairs)]
    convert_element_type x4 -> x0, other arithmetic: 4.23 us -> none  [the longest x2 2.19 us: body_slabs(): over = summed(that_near[:, here], got_that[0, :, here], got).astype(bf16)]
    pallas_call x3 -> x6, Pallas kernels: 5.37 us -> 8.33 us  [the longest x1 5.33 us: body_slabs(): local_call(field_kernel, [sent_block] * HALF, [vmem] * (2 + len(FAR) + HA...]
    ppermute x13 -> x12, starting transfers between devices: 39.3 us -> 40.2 us  [permute(): return lax.ppermute(sent, 'slab', pairs)]
    ppermute x3 -> x2, starting transfers between devices: 3.51 us -> 2.94 us  [body_slabs(): got_x = lax.ppermute(over, 'led', planes)]
  transfers between devices with their start and end apart: 18 -> 16, of which waited for: 8 -> 8; matrix products, arithmetic and copies ran while one was open for 5% -> 2% of each run, Pallas kernels for 5% -> 7%
where the time goes in v9:
time: 120 us; the launch traced here: 119 us
  waiting for transfers between devices  48.7 us (41%)
  starting transfers between devices  43.7 us (36%)
  Pallas kernels  19.9 us (17%)
  other arithmetic  4.04 us (3%)
  local copies, waits for them, and re-layouts  2.42 us (2%)
    ppermute x12, starting transfers between devices, permute(): return lax.ppermute(sent, 'slab', pairs)  40.2 us
    ppermute x12, waiting for transfers between devices, permute(): return lax.ppermute(sent, 'slab', pairs)  39.1 us
    ppermute x2, waiting for transfers between devices, body_slabs(): got_x = lax.ppermute(over, 'led', planes)  9.63 us
    pallas_call x1, Pallas kernels, body_slabs(): local_call(field_kernel, [sent_block] * HALF, [vmem] * (2 + len(FAR) + HA...  5.33 us
    pallas_call x2, Pallas kernels, rows_call(): local_call(functools.partial(rows_kernel, which), [sent_block] * count, [...  4.69 us
    pallas_call x4, Pallas kernels, sum_call(): local_call(kernel, out_shape, specs, [], 0, 2 ** 20, kernel.__name__)  2.96 us
    ppermute x2, starting transfers between devices, body_slabs(): got_x = lax.ppermute(over, 'led', planes)  2.94 us
    pallas_call x1, Pallas kernels, body_slabs(): local_call(sent_kernel, [jax.ShapeDtypeStruct((2,) + piece, bf16), jax.Sh...  2.66 us
  transfers between devices with their start and end apart: 16, of which 8 were waited for; matrix products, arithmetic and copies ran while one was open for 2% of the time, Pallas kernels for 7%

profile of v9, /device:TPU:4, one launch (start us, length us, event | category | flops | bytes accessed | tf_op | source)
XLA Modules:
  0.0 119.0 jit_solution(9968276199492706167)
XLA Ops:
  0.0 0.9 pad_add_fusion.starts
  0.9 2.4 %copy-done.1 = f32[2,256,2048]{2,1,0:T(8,128)S(1)} copy-done((f32[2,256,2048]{2,1,0:T(8,128)S(1)}, f32[2,256,2048]{2,1,0:T(8,128)}, u32[]{:S(2)}) %copy-start.1) | copy-done | bytes 4194328
  3.3 1.2 %windows.1.window = bf16[1024,1024]{1,0:T(8,128)(2,1)S(1)} custom-call(s32[4]{0:T(128)S(1)} %pad_add_fusion.starts, f32[2,256,2048]{2,1,0:T(8,128)S(1)} %copy-done.1), custom_call_target="tpu_custom_call" | custom-call | bytes 6291456 | tf_op jit(solution)/shard_map/windows/pallas_call | solution.py:439
  4.5 2.4 %rows_far.1 = (bf16[4,256,128]{2,1,0:T(8,128)(2,1)S(1)}, bf16[4,256,128]{2,1,0:T(8,128)(2,1)S(1)}, bf16[4,256,128]{2,1,0:T(8,128)(2,1)S(1)}, bf16[4,256,128]{2,1,0:T(8,128)(2,1)S(1)}) custom-call(bf16[1024,1024]{1,0:T(8,128)(2,1)S(1)} %windows.1.window, bf16[8,1024,256]{2,1,0:T(8,128)(2,1)S(1)} %copy-done), custom_call_target="tpu_custom_call" | custom-call | flops 2147483648 | bytes 5242880 | tf_op jit(solution)/shard_map/rows_far/pallas_call | solution.py:451
  6.9 1.3 %collective-permute-start = (bf16[4,256,128]{2,1,0:T(8,128)(2,1)S(1)}, bf16[4,256,128]{2,1,0:T(8,128)(2,1)S(1)}, u32[]{:S(2)}, u32[]{:S(2)}) collective-permute-start(bf16[4,256,128]{2,1,0:T(8,128)(2,1)S(1)} %get-tuple-element.31), channel_id=1, source_target_pairs={{4,0},{8,16},{12,20},{16,8},{20,12},{24,28},{5,1},{9,17},{13,21},{... | collective-permute-start | bytes 786440 | tf_op jit(solution)/shard_map/ppermute | solution.py:464
  8.2 7.6 %collective-permute-start.1 = (bf16[4,256,128]{2,1,0:T(8,128)(2,1)S(1)}, bf16[4,256,128]{2,1,0:T(8,128)(2,1)S(1)}, u32[]{:S(2)}, u32[]{:S(2)}) collective-permute-start(bf16[4,256,128]{2,1,0:T(8,128)(2,1)S(1)} %get-tuple-element.36), channel_id=1, source_target_pairs={{4,24},{8,28},{12,16},{16,12},{20,0},{24,4},{5,25},{9,29},{13,17},... | collective-permute-start | bytes 786440 | tf_op jit(solution)/shard_map/ppermute | solution.py:464
  15.8 1.9 %collective-permute-start.2 = (bf16[4,256,128]{2,1,0:T(8,128)(2,1)S(1)}, bf16[4,256,128]{2,1,0:T(8,128)(2,1)S(1)}, u32[]{:S(2)}, u32[]{:S(2)}) collective-permute-start(bf16[4,256,128]{2,1,0:T(8,128)(2,1)S(1)} %get-tuple-element.37), channel_id=1, source_target_pairs={{4,28},{8,20},{12,24},{16,4},{20,8},{24,0},{5,29},{9,21},{13,25},{... | collective-permute-start | bytes 786440 | tf_op jit(solution)/shard_map/ppermute | solution.py:464
  17.7 0.0 copy-start.2
  17.7 0.0 copy-start.3
  17.8 16.9 %collective-permute-start.3 = (bf16[4,256,128]{2,1,0:T(8,128)(2,1)S(1)}, bf16[4,256,128]{2,1,0:T(8,128)(2,1)S(1)}, u32[]{:S(2)}, u32[]{:S(2)}) collective-permute-start(bf16[4,256,128]{2,1,0:T(8,128)(2,1)S(1)} %last_far_blocks.1), channel_id=1, source_target_pairs={{4,20},{8,24},{12,28},{16,0},{20,4},{24,8},{0,16},{28,12},{5,21},{... | collective-permute-start | bytes 786440 | tf_op jit(solution)/shard_map/ppermute | solution.py:464
  34.7 2.3 %rows_near.1 = (bf16[4,256,128]{2,1,0:T(8,128)(2,1)S(1)}, bf16[4,256,128]{2,1,0:T(8,128)(2,1)S(1)}, bf16[4,256,128]{2,1,0:T(8,128)(2,1)S(1)}, bf16[4,256,128]{2,1,0:T(8,128)(2,1)S(1)}) custom-call(bf16[1024,1024]{1,0:T(8,128)(2,1)S(1)} %windows.1.window, bf16[8,1024,256]{2,1,0:T(8,128)(2,1)S(1)} %copy-done), custom_call_target="tpu_custom_call" | custom-call | flops 2147483648 | bytes 5242880 | tf_op jit(solution)/shard_map/rows_near/pallas_call | solution.py:451
  37.0 1.3 %collective-permute-start.4 = (bf16[4,256,128]{2,1,0:T(8,128)(2,1)S(1)}, bf16[4,256,128]{2,1,0:T(8,128)(2,1)S(1)}, u32[]{:S(2)}, u32[]{:S(2)}) collective-permute-start(bf16[4,256,128]{2,1,0:T(8,128)(2,1)S(1)} %get-tuple-element.41), channel_id=1, source_target_pairs={{4,0},{8,12},{12,8},{16,20},{20,16},{24,28},{5,1},{9,13},{13,9},{1... | collective-permute-start | bytes 786440 | tf_op jit(solution)/shard_map/ppermute | solution.py:464
  38.3 1.9 %collective-permute-start.5 = (bf16[4,256,128]{2,1,0:T(8,128)(2,1)S(1)}, bf16[4,256,128]{2,1,0:T(8,128)(2,1)S(1)}, u32[]{:S(2)}, u32[]{:S(2)}) collective-permute-start(bf16[4,256,128]{2,1,0:T(8,128)(2,1)S(1)} %get-tuple-element.42), channel_id=1, source_target_pairs={{4,12},{8,0},{12,4},{16,24},{20,28},{24,16},{5,13},{9,1},{13,5},{1... | collective-permute-start | bytes 786440 | tf_op jit(solution)/shard_map/ppermute | solution.py:464
  40.3 0.0 collective-permute-done.1.rest_1_
  40.3 1.9 %collective-permute-start.6 = (bf16[4,256,128]{2,1,0:T(8,128)(2,1)S(1)}, bf16[4,256,128]{2,1,0:T(8,128)(2,1)S(1)}, u32[]{:S(2)}, u32[]{:S(2)}) collective-permute-start(bf16[4,256,128]{2,1,0:T(8,128)(2,1)S(1)} %get-tuple-element.43), channel_id=1, source_target_pairs={{4,8},{8,4},{12,0},{16,28},{20,24},{24,20},{5,9},{9,5},{13,1},{17,... | collective-permute-start | bytes 786440 | tf_op jit(solution)/shard_map/ppermute | solution.py:464
  42.2 0.6 amplitude.1
  42.8 4.3 %collective-permute-done.2.rest_2_ = bf16[4,256,128]{2,1,0:T(8,128)(2,1)S(1)} collective-permute-done((bf16[4,256,128]{2,1,0:T(8,128)(2,1)S(1)}, bf16[4,256,128]{2,1,0:T(8,128)(2,1)S(1)}, u32[]{:S(2)}, u32[]{:S(2)}) %collective-permute-start.2) | collective-permute-done | bytes 262176 | tf_op jit(solution)/shard_map/ppermute | solution.py:464
  47.1 0.0 collective-permute-done.3.rest_3_
  47.1 0.0 collective-permute-done.4.rest_5_
  47.1 0.4 collective-permute-done.5.rest_6_
  47.5 11.8 %collective-permute-done.6.rest_7_ = bf16[4,256,128]{2,1,0:T(8,128)(2,1)S(1)} collective-permute-done((bf16[4,256,128]{2,1,0:T(8,128)(2,1)S(1)}, bf16[4,256,128]{2,1,0:T(8,128)(2,1)S(1)}, u32[]{:S(2)}, u32[]{:S(2)}) %collective-permute-start.6) | collective-permute-done | bytes 262176 | tf_op jit(solution)/shard_map/ppermute | solution.py:464
  59.3 5.3 %modulus_step.1 = (bf16[4,256,128]{2,1,0:T(8,128)(2,1)S(1)}, bf16[4,256,128]{2,1,0:T(8,128)(2,1)S(1)}, bf16[4,256,128]{2,1,0:T(8,128)(2,1)S(1)}, bf16[4,256,128]{2,1,0:T(8,128)(2,1)S(1)}) custom-call(f32[1024,256]{1,0:T(8,128)S(1)} %get-tuple-element.33.amplitude, bf16[8,256,1024]{2,1,0:T(8,128)(2,1)S(1)} %get-tuple-element.34.table, ...), custom_call_target="tpu_custom_call" | custom-call | flops 4294967296 | bytes 12582912 | tf_op jit(solution)/shard_map/modulus_step/pallas_call | solution.py:501
  64.7 0.1 collective-permute-start.7
  64.7 0.1 collective-permute-start.8
  64.9 3.3 %collective-permute-start.9 = (bf16[4,256,128]{2,1,0:T(8,128)(2,1)S(1)}, bf16[4,256,128]{2,1,0:T(8,128)(2,1)S(1)}, u32[]{:S(2)}, u32[]{:S(2)}) collective-permute-start(bf16[4,256,128]{2,1,0:T(8,128)(2,1)S(1)} %get-tuple-element.47), channel_id=1, source_target_pairs={{0,12},{4,8},{8,4},{12,0},{16,28},{20,24},{24,20},{28,16},{1,13},{... | collective-permute-start | bytes 786440 | tf_op jit(solution)/shard_map/ppermute | solution.py:464
  68.2 5.2 %collective-permute-done.7.rest_1_ = bf16[4,256,128]{2,1,0:T(8,128)(2,1)S(1)} collective-permute-done((bf16[4,256,128]{2,1,0:T(8,128)(2,1)S(1)}, bf16[4,256,128]{2,1,0:T(8,128)(2,1)S(1)}, u32[]{:S(2)}, u32[]{:S(2)}) %collective-permute-start.7) | collective-permute-done | bytes 262176 | tf_op jit(solution)/shard_map/ppermute | solution.py:464
  73.4 0.0 collective-permute-done.8.rest_2_
  73.4 2.8 %collective-permute-done.9.rest_3_ = bf16[4,256,128]{2,1,0:T(8,128)(2,1)S(1)} collective-permute-done((bf16[4,256,128]{2,1,0:T(8,128)(2,1)S(1)}, bf16[4,256,128]{2,1,0:T(8,128)(2,1)S(1)}, u32[]{:S(2)}, u32[]{:S(2)}) %collective-permute-start.9) | collective-permute-done | bytes 262176 | tf_op jit(solution)/shard_map/ppermute | solution.py:464
  76.2 2.7 %update_sent.1 = (bf16[2,2,256,512]{3,2,1,0:T(8,128)(2,1)S(1)}, bf16[2,2,256,512]{3,2,1,0:T(8,128)(2,1)S(1)}, bf16[1024,512]{1,0:T(8,128)(2,1)S(1)}) custom-call(s32[4]{0:T(128)S(1)} %pad_add_fusion.starts, bf16[8,1024,256]{2,1,0:T(8,128)(2,1)S(1)} %copy-done, bf16[4,256,128]{2,1,0:T(8,128)(2,1)S(1)} %get-tuple-element.44.rest_0_, ...), custom_call_target="tpu_custom_call" | custom-call | flops 1073741824 | bytes 8388608 | tf_op jit(solution)/shard_map/update_sent/pallas_call | solution.py:526
  78.9 0.1 collective-permute-start.11
  78.9 0.5 collective-permute-start.10
  79.4 2.4 %update_kept.1 = (f32[2,256,512]{2,1,0:T(8,128)S(1)}, f32[2,256,512]{2,1,0:T(8,128)S(1)}, f32[2,256,512]{2,1,0:T(8,128)S(1)}, f32[2,256,512]{2,1,0:T(8,128)S(1)}) custom-call(s32[4]{0:T(128)S(1)} %pad_add_fusion.starts, bf16[8,1024,256]{2,1,0:T(8,128)(2,1)S(1)} %copy-done, bf16[1024,512]{1,0:T(8,128)(2,1)S(1)} %get-tuple-element.48.back), custom_call_target="tpu_custom_call" | custom-call | flops 1073741824 | bytes 10485760 | tf_op jit(solution)/shard_map/update_kept/pallas_call | solution.py:541
  81.9 0.0 copy-start.4
  81.9 0.0 collective-permute-done.11.got_that
  81.9 0.1 z_first_kernel.1
  82.0 1.9 %collective-permute-start.12 = (bf16[2,2,256,128]{3,2,1,0:T(8,128)(2,1)S(1)}, bf16[2,2,256,128]{3,2,1,0:T(8,128)(2,1)S(1)}, u32[]{:S(2)}, u32[]{:S(2)}) collective-permute-start(bf16[2,2,256,128]{3,2,1,0:T(8,128)(2,1)S(1)} %z_first_kernel.1), channel_id=1, source_target_pairs={{0,16},{4,20},{8,24},{20,4},{24,8},{28,12},{1,17},{5,21},{9,25},{2... | collective-permute-start | bytes 786440 | tf_op jit(solution)/shard_map/ppermute | solution.py:464
  83.9 0.8 x_first_kernel.1
  84.8 1.5 %collective-permute-start.14 = (bf16[2,256,384]{2,1,0:T(8,128)(2,1)}, bf16[2,256,384]{2,1,0:T(8,128)(2,1)}, u32[]{:S(2)}, u32[]{:S(2)}) collective-permute-start(bf16[2,256,384]{2,1,0:T(8,128)(2,1)} %x_first_kernel.1), channel_id=1, source_target_pairs={{0,2},{2,0},{1,3},{3,1},{4,6},{6,4},{5,7},{7,5},{8,10},{10,8},{9,1... | collective-permute-start | bytes 1179656 | tf_op jit(solution)/shard_map/ppermute | solution.py:559
  86.2 0.0 collective-permute-done.10.got_this
  86.2 12.2 %collective-permute-done.12.got_z = bf16[2,2,256,128]{3,2,1,0:T(8,128)(2,1)S(1)} collective-permute-done((bf16[2,2,256,128]{3,2,1,0:T(8,128)(2,1)S(1)}, bf16[2,2,256,128]{3,2,1,0:T(8,128)(2,1)S(1)}, u32[]{:S(2)}, u32[]{:S(2)}) %collective-permute-start.12) | collective-permute-done | bytes 262176 | tf_op jit(solution)/shard_map/ppermute | solution.py:464
  98.5 0.9 x_second_kernel.1
  99.4 1.5 %collective-permute-start.13 = (bf16[2,256,512]{2,1,0:T(8,128)(2,1)}, bf16[2,256,512]{2,1,0:T(8,128)(2,1)}, u32[]{:S(2)}, u32[]{:S(2)}) collective-permute-start(bf16[2,256,512]{2,1,0:T(8,128)(2,1)} %x_second_kernel.1), channel_id=1, source_target_pairs={{0,2},{2,0},{1,3},{3,1},{4,6},{6,4},{5,7},{7,5},{8,10},{10,8},{9,1... | collective-permute-start | bytes 1572872 | tf_op jit(solution)/shard_map/ppermute | solution.py:563
  100.9 1.1 z_second_kernel.1
  102.0 1.9 %collective-permute-start.15 = (bf16[2,256,384]{2,1,0:T(8,128)(2,1)S(1)}, bf16[2,256,384]{2,1,0:T(8,128)(2,1)S(1)}, u32[]{:S(2)}, u32[]{:S(2)}) collective-permute-start(bf16[2,256,384]{2,1,0:T(8,128)(2,1)S(1)} %z_second_kernel.1), channel_id=1, source_target_pairs={{0,16},{4,20},{8,24},{20,4},{24,8},{28,12},{1,17},{5,21},{9,25},{2... | collective-permute-start | bytes 1179656 | tf_op jit(solution)/shard_map/ppermute | solution.py:464
  103.9 9.6 %collective-permute-done.13 = bf16[2,256,512]{2,1,0:T(8,128)(2,1)} collective-permute-done((bf16[2,256,512]{2,1,0:T(8,128)(2,1)}, bf16[2,256,512]{2,1,0:T(8,128)(2,1)}, u32[]{:S(2)}, u32[]{:S(2)}) %collective-permute-start.13) | collective-permute-done | bytes 524320 | tf_op jit(solution)/shard_map/ppermute | solution.py:563
  113.6 2.0 %fusion.2 = f32[2,256,512]{2,1,0:T(8,128)S(1)} fusion(f32[2,256,512]{2,1,0:T(8,128)} %copy-done.4, bf16[2,256,512]{2,1,0:T(8,128)(2,1)} %collective-permute-done.13, f32[2,256,2048]{2,1,0:T(8,128)} %spectrum.1, s32[]{:T(128)S(6)} %select_n.3, bf16[2,2,256,512]{3,2,1,0:T(8,128)(2,1)S(1)} %collective-permute-done.10.got_this, ...), kind=kLoop, calls=%fused_computation.3 | loop fusion | flops 1835008 | bytes 4325380 | tf_op jit(solution)/shard_map/add | solution.py:571
  115.6 2.3 %collective-permute-done.15 = bf16[2,256,384]{2,1,0:T(8,128)(2,1)S(1)} collective-permute-done((bf16[2,256,384]{2,1,0:T(8,128)(2,1)S(1)}, bf16[2,256,384]{2,1,0:T(8,128)(2,1)S(1)}, u32[]{:S(2)}, u32[]{:S(2)}) %collective-permute-start.15) | collective-permute-done | bytes 393248 | tf_op jit(solution)/shard_map/ppermute | solution.py:464
  117.9 1.1 convert_add_fusion.1
  (10 shorter events, 0.1 us)
Async XLA Ops:
  0.0 4.5 %copy-start = (bf16[8,1024,256]{2,1,0:T(8,128)(2,1)S(1)}, bf16[8,1024,256]{2,1,0:T(8,128)(2,1)}, u32[]{:S(2)}) copy-start(bf16[8,1024,256]{2,1,0:T(8,128)(2,1)} %constant.18.clone.table) | copy-start | bytes 12582916
  0.9 2.4 %copy-start.1 = (f32[2,256,2048]{2,1,0:T(8,128)S(1)}, f32[2,256,2048]{2,1,0:T(8,128)}, u32[]{:S(2)}) copy-start(f32[2,256,2048]{2,1,0:T(8,128)} %spectrum.1) | copy-start | bytes 12582916
  6.9 10.8 %collective-permute-start = (bf16[4,256,128]{2,1,0:T(8,128)(2,1)S(1)}, bf16[4,256,128]{2,1,0:T(8,128)(2,1)S(1)}, u32[]{:S(2)}, u32[]{:S(2)}) collective-permute-start(bf16[4,256,128]{2,1,0:T(8,128)(2,1)S(1)} %get-tuple-element.31), channel_id=1, source_target_pairs={{4,0},{8,16},{12,20},{16,8},{20,12},{24,28},{5,1},{9,17},{13,21},{... | collective-permute-start | bytes 786440 | tf_op jit(solution)/shard_map/ppermute | solution.py:464
  8.2 32.1 %collective-permute-start.1 = (bf16[4,256,128]{2,1,0:T(8,128)(2,1)S(1)}, bf16[4,256,128]{2,1,0:T(8,128)(2,1)S(1)}, u32[]{:S(2)}, u32[]{:S(2)}) collective-permute-start(bf16[4,256,128]{2,1,0:T(8,128)(2,1)S(1)} %get-tuple-element.36), channel_id=1, source_target_pairs={{4,24},{8,28},{12,16},{16,12},{20,0},{24,4},{5,25},{9,29},{13,17},... | collective-permute-start | bytes 786440 | tf_op jit(solution)/shard_map/ppermute | solution.py:464
  15.8 31.3 %collective-permute-start.2 = (bf16[4,256,128]{2,1,0:T(8,128)(2,1)S(1)}, bf16[4,256,128]{2,1,0:T(8,128)(2,1)S(1)}, u32[]{:S(2)}, u32[]{:S(2)}) collective-permute-start(bf16[4,256,128]{2,1,0:T(8,128)(2,1)S(1)} %get-tuple-element.37), channel_id=1, source_target_pairs={{4,28},{8,20},{12,24},{16,4},{20,8},{24,0},{5,29},{9,21},{13,25},{... | collective-permute-start | bytes 786440 | tf_op jit(solution)/shard_map/ppermute | solution.py:464
  17.7 24.5 %copy-start.2 = (bf16[8,256,1024]{2,1,0:T(8,128)(2,1)S(1)}, bf16[8,256,1024]{2,1,0:T(8,128)(2,1)}, u32[]{:S(2)}) copy-start(bf16[8,256,1024]{2,1,0:T(8,128)(2,1)} %constant.17.clone.table) | copy-start | bytes 12582916
  17.7 24.5 %copy-start.3 = (f32[2,128,1024]{2,1,0:T(8,128)S(1)}, f32[2,128,1024]{2,1,0:T(8,128)}, u32[]{:S(2)}) copy-start(f32[2,128,1024]{2,1,0:T(8,128)} %images) | copy-start | bytes 3145732
  17.8 29.3 %collective-permute-start.3 = (bf16[4,256,128]{2,1,0:T(8,128)(2,1)S(1)}, bf16[4,256,128]{2,1,0:T(8,128)(2,1)S(1)}, u32[]{:S(2)}, u32[]{:S(2)}) collective-permute-start(bf16[4,256,128]{2,1,0:T(8,128)(2,1)S(1)} %last_far_blocks.1), channel_id=1, source_target_pairs={{4,20},{8,24},{12,28},{16,0},{20,4},{24,8},{0,16},{28,12},{5,21},{... | collective-permute-start | bytes 786440 | tf_op jit(solution)/shard_map/ppermute | solution.py:464
  37.0 10.1 %collective-permute-start.4 = (bf16[4,256,128]{2,1,0:T(8,128)(2,1)S(1)}, bf16[4,256,128]{2,1,0:T(8,128)(2,1)S(1)}, u32[]{:S(2)}, u32[]{:S(2)}) collective-permute-start(bf16[4,256,128]{2,1,0:T(8,128)(2,1)S(1)} %get-tuple-element.41), channel_id=1, source_target_pairs={{4,0},{8,12},{12,8},{16,20},{20,16},{24,28},{5,1},{9,13},{13,9},{1... | collective-permute-start | bytes 786440 | tf_op jit(solution)/shard_map/ppermute | solution.py:464
  38.3 9.2 %collective-permute-start.5 = (bf16[4,256,128]{2,1,0:T(8,128)(2,1)S(1)}, bf16[4,256,128]{2,1,0:T(8,128)(2,1)S(1)}, u32[]{:S(2)}, u32[]{:S(2)}) collective-permute-start(bf16[4,256,128]{2,1,0:T(8,128)(2,1)S(1)} %get-tuple-element.42), channel_id=1, source_target_pairs={{4,12},{8,0},{12,4},{16,24},{20,28},{24,16},{5,13},{9,1},{13,5},{1... | collective-permute-start | bytes 786440 | tf_op jit(solution)/shard_map/ppermute | solution.py:464
  40.3 19.0 %collective-permute-start.6 = (bf16[4,256,128]{2,1,0:T(8,128)(2,1)S(1)}, bf16[4,256,128]{2,1,0:T(8,128)(2,1)S(1)}, u32[]{:S(2)}, u32[]{:S(2)}) collective-permute-start(bf16[4,256,128]{2,1,0:T(8,128)(2,1)S(1)} %get-tuple-element.43), channel_id=1, source_target_pairs={{4,8},{8,4},{12,0},{16,28},{20,24},{24,20},{5,9},{9,5},{13,1},{17,... | collective-permute-start | bytes 786440 | tf_op jit(solution)/shard_map/ppermute | solution.py:464
  64.7 8.7 %collective-permute-start.7 = (bf16[4,256,128]{2,1,0:T(8,128)(2,1)S(1)}, bf16[4,256,128]{2,1,0:T(8,128)(2,1)S(1)}, u32[]{:S(2)}, u32[]{:S(2)}) collective-permute-start(bf16[4,256,128]{2,1,0:T(8,128)(2,1)S(1)} %get-tuple-element.45), channel_id=1, source_target_pairs={{0,4},{4,0},{8,12},{12,8},{16,20},{20,16},{24,28},{28,24},{1,5},{5... | collective-permute-start | bytes 786440 | tf_op jit(solution)/shard_map/ppermute | solution.py:464
  64.7 8.6 %collective-permute-start.8 = (bf16[4,256,128]{2,1,0:T(8,128)(2,1)S(1)}, bf16[4,256,128]{2,1,0:T(8,128)(2,1)S(1)}, u32[]{:S(2)}, u32[]{:S(2)}) collective-permute-start(bf16[4,256,128]{2,1,0:T(8,128)(2,1)S(1)} %get-tuple-element.46), channel_id=1, source_target_pairs={{0,8},{4,12},{8,0},{12,4},{16,24},{20,28},{24,16},{28,20},{1,9},{5... | collective-permute-start | bytes 786440 | tf_op jit(solution)/shard_map/ppermute | solution.py:464
  64.9 11.3 %collective-permute-start.9 = (bf16[4,256,128]{2,1,0:T(8,128)(2,1)S(1)}, bf16[4,256,128]{2,1,0:T(8,128)(2,1)S(1)}, u32[]{:S(2)}, u32[]{:S(2)}) collective-permute-start(bf16[4,256,128]{2,1,0:T(8,128)(2,1)S(1)} %get-tuple-element.47), channel_id=1, source_target_pairs={{0,12},{4,8},{8,4},{12,0},{16,28},{20,24},{24,20},{28,16},{1,13},{... | collective-permute-start | bytes 786440 | tf_op jit(solution)/shard_map/ppermute | solution.py:464
  78.9 3.0 %collective-permute-start.11 = (bf16[2,2,256,512]{3,2,1,0:T(8,128)(2,1)S(1)}, bf16[2,2,256,512]{3,2,1,0:T(8,128)(2,1)S(1)}, u32[]{:S(2)}, u32[]{:S(2)}) collective-permute-start(bf16[2,2,256,512]{3,2,1,0:T(8,128)(2,1)S(1)} %get-tuple-element.54), channel_id=1, source_target_pairs={{0,1},{1,0},{2,3},{3,2},{4,5},{5,4},{6,7},{7,6},{8,9},{9,8},{10,11... | collective-permute-start | bytes 3145736 | tf_op jit(solution)/shard_map/ppermute | solution.py:539
  78.9 7.3 %collective-permute-start.10 = (bf16[2,2,256,512]{3,2,1,0:T(8,128)(2,1)S(1)}, bf16[2,2,256,512]{3,2,1,0:T(8,128)(2,1)S(1)}, u32[]{:S(2)}, u32[]{:S(2)}) collective-permute-start(bf16[2,2,256,512]{3,2,1,0:T(8,128)(2,1)S(1)} %get-tuple-element.50), channel_id=1, source_target_pairs={{0,1},{1,0},{2,3},{3,2},{4,5},{5,4},{6,7},{7,6},{8,9},{9,8},{10,11... | collective-permute-start | bytes 3145736 | tf_op jit(solution)/shard_map/ppermute | solution.py:540
  81.9 17.5 %copy-start.4 = (f32[2,256,512]{2,1,0:T(8,128)}, f32[2,256,512]{2,1,0:T(8,128)S(1)}, u32[]{:S(2)}) copy-start(f32[2,256,512]{2,1,0:T(8,128)S(1)} %get-tuple-element.49) | copy-start | bytes 3145732
  82.0 16.5 %collective-permute-start.12 = (bf16[2,2,256,128]{3,2,1,0:T(8,128)(2,1)S(1)}, bf16[2,2,256,128]{3,2,1,0:T(8,128)(2,1)S(1)}, u32[]{:S(2)}, u32[]{:S(2)}) collective-permute-start(bf16[2,2,256,128]{3,2,1,0:T(8,128)(2,1)S(1)} %z_first_kernel.1), channel_id=1, source_target_pairs={{0,16},{4,20},{8,24},{20,4},{24,8},{28,12},{1,17},{5,21},{9,25},{2... | collective-permute-start | bytes 786440 | tf_op jit(solution)/shard_map/ppermute | solution.py:464
  84.8 16.1 %collective-permute-start.14 = (bf16[2,256,384]{2,1,0:T(8,128)(2,1)}, bf16[2,256,384]{2,1,0:T(8,128)(2,1)}, u32[]{:S(2)}, u32[]{:S(2)}) collective-permute-start(bf16[2,256,384]{2,1,0:T(8,128)(2,1)} %x_first_kernel.1), channel_id=1, source_target_pairs={{0,2},{2,0},{1,3},{3,1},{4,6},{6,4},{5,7},{7,5},{8,10},{10,8},{9,1... | collective-permute-start | bytes 1179656 | tf_op jit(solution)/shard_map/ppermute | solution.py:559
  99.4 14.2 %collective-permute-start.13 = (bf16[2,256,512]{2,1,0:T(8,128)(2,1)}, bf16[2,256,512]{2,1,0:T(8,128)(2,1)}, u32[]{:S(2)}, u32[]{:S(2)}) collective-permute-start(bf16[2,256,512]{2,1,0:T(8,128)(2,1)} %x_second_kernel.1), channel_id=1, source_target_pairs={{0,2},{2,0},{1,3},{3,1},{4,6},{6,4},{5,7},{7,5},{8,10},{10,8},{9,1... | collective-permute-start | bytes 1572872 | tf_op jit(solution)/shard_map/ppermute | solution.py:563
  102.0 15.9 %collective-permute-start.15 = (bf16[2,256,384]{2,1,0:T(8,128)(2,1)S(1)}, bf16[2,256,384]{2,1,0:T(8,128)(2,1)S(1)}, u32[]{:S(2)}, u32[]{:S(2)}) collective-permute-start(bf16[2,256,384]{2,1,0:T(8,128)(2,1)S(1)} %z_second_kernel.1), channel_id=1, source_target_pairs={{0,16},{4,20},{8,24},{20,4},{24,8},{28,12},{1,17},{5,21},{9,25},{2... | collective-permute-start | bytes 1179656 | tf_op jit(solution)/shard_map/ppermute | solution.py:464

commit v10 on v9

--- a/solution.py
+++ b/solution.py
@@ -219,8 +219,9 @@
 
 def rows_kernel(which, window, table, *outs):
     position = lax.axis_index("slab")
-    blocks = [look_up(position, far) for far in FAR]
-    blocks += [jnp.bitwise_xor(position, d) for d in (0, 2, 1, 3)]
+    blocks = [jnp.bitwise_xor(position, 2)]
+    blocks += [look_up(position, far) for far in FAR]
+    blocks += [jnp.bitwise_xor(position, d) for d in (0, 1, 3)]
     for out, block in zip(outs, blocks[which]):
         store_parts(out, row_block(window[...], table[block]))
 
@@ -458,7 +459,7 @@
             name,
         )(window, by_col)
 
-    *far_sent, last = rows_call(slice(0, 4), "rows_far", window)
+    near_2, *far_sent = rows_call(slice(0, 5), "rows_far", window)
 
     def permute(sent, pairs):
         return lax.ppermute(sent, "slab", pairs)
@@ -470,19 +471,22 @@
 
     windowed = range(FIRST + 1, LAST)
     far_columns = []
-    for far, sent in zip(FAR, far_sent):
+    for far, sent in zip(FAR[:2], far_sent):
         pairs = dict(far)
         if far is FAR[0]:
             pairs.update({slab: by for slab, (by, _) in HANDED.items()})
         far_columns.append(permute(sent, list(pairs.items())))
-    far_columns[0], window, images = lax.optimization_barrier((far_columns[0], window, images))
+    near_2 = permute(near_2, [(s, s ^ 2) for s in windowed])
+    third, last = far_sent[2:]
+    far_columns[0], third, window, images = lax.optimization_barrier(
+        (far_columns[0], third, window, images)
+    )
     last = local_call(
         choose_kernel, sent_block, [vmem] * 2, [], 0, 2**19, "last_far_blocks"
     )(far_columns[0], last)
-    near_0, near_2, near_1, near_3 = rows_call(slice(4, SLABS), "rows_near", window)
-    pairs = list(FAR[-1].items()) + list(HANDED.values())
-    far_columns.append(permute(last, pairs))
-    near_2 = permute(near_2, [(s, s ^ 2) for s in windowed])
+    near_0, near_1, near_3 = rows_call(slice(5, SLABS), "rows_near", window)
+    far_columns.append(permute(third, list(FAR[2].items())))
+    far_columns.append(permute(last, list(FAR[3].items()) + list(HANDED.values())))
     near_1 = permute(near_1, [(s, s ^ 1) for s in windowed])
     near_3 = permute(near_3, [(s, s ^ 3) for s in windowed])
     near_columns = [near_0, near_1, near_2, near_3]
@@ -559,6 +563,7 @@
     got_x = lax.ppermute(over, "led", planes)
     over = sum_call(z_second_kernel, (2, rows, share - first), that_near, got_that, got_x)
     got_z_second = permute(over, across)
+    got_z_first, _ = lax.optimization_barrier((got_z_first, over))
     over = sum_call(x_second_kernel, piece, this_far, got_this, got_z_first)
     got_x = lax.ppermute(over, "led", planes)
 

time: 120 us -> 121 us (level)
  waiting for transfers between devices: 48.7 us -> 60 us
  starting transfers between devices: 43.7 us -> 37 us
  Pallas kernels: 19.9 us -> 17.5 us
    ppermute x2, waiting for transfers between devices: 9.63 us -> 18.3 us  [body_slabs(): got_x = lax.ppermute(over, 'led', planes)]
    ppermute x12, starting transfers between devices: 40.2 us -> 34.8 us  [permute(): return lax.ppermute(sent, 'slab', pairs)]
    ppermute x12, waiting for transfers between devices: 39.1 us -> 41.7 us  [permute(): return lax.ppermute(sent, 'slab', pairs)]
    pallas_call x4, Pallas kernels: 2.96 us -> 0.46 us  [sum_call(): local_call(kernel, out_shape, specs, [], 0, 2 ** 20, kernel.__name__)]
    ppermute x2, starting transfers between devices: 2.94 us -> 1.63 us  [body_slabs(): got_x = lax.ppermute(over, 'led', planes)]
  transfers between devices with their start and end apart: 16 -> 16, of which waited for: 8 -> 7; matrix products, arithmetic and copies ran while one was open for 2% -> 1% of each run, Pallas kernels for 7% -> 4%
where the time goes in v10:
time: 121 us
  waiting for transfers between devices  60 us (50%)
  starting transfers between devices  37 us (31%)
  Pallas kernels  17.5 us (14%)
  other arithmetic  3.72 us (3%)
  local copies, waits for them, and re-layouts  2.42 us (2%)
    ppermute x12, waiting for transfers between devices, permute(): return lax.ppermute(sent, 'slab', pairs)  41.7 us
    ppermute x12, starting transfers between devices, permute(): return lax.ppermute(sent, 'slab', pairs)  34.8 us
    ppermute x2, waiting for transfers between devices, body_slabs(): got_x = lax.ppermute(over, 'led', planes)  18.3 us
    pallas_call x1, Pallas kernels, body_slabs(): local_call(field_kernel, [sent_block] * HALF, [vmem] * (2 + len(FAR) + HA...  5.33 us
    pallas_call x2, Pallas kernels, rows_call(): local_call(functools.partial(rows_kernel, which), [sent_block] * count, [...  4.67 us
    pallas_call x1, Pallas kernels, body_slabs(): local_call(sent_kernel, [jax.ShapeDtypeStruct((2,) + piece, bf16), jax.Sh...  2.66 us
    pallas_call x1, Pallas kernels, body_slabs(): local_call(kept_kernel, [jax.ShapeDtypeStruct(piece, jnp.float32)] * 4, [...  2.43 us
  transfers between devices with their start and end apart: 16, of which 7 were waited for; matrix products, arithmetic and copies ran while one was open for 1% of the time, Pallas kernels for 4%

profile of v10, /device:TPU:4, one launch (start us, length us, event | category | flops | bytes accessed | tf_op | source)
XLA Modules:
  0.0 120.9 jit_solution(4319717781173338297)
XLA Ops:
  0.0 0.9 pad_add_fusion.starts
  0.9 2.4 %copy-done.1 = f32[2,256,2048]{2,1,0:T(8,128)S(1)} copy-done((f32[2,256,2048]{2,1,0:T(8,128)S(1)}, f32[2,256,2048]{2,1,0:T(8,128)}, u32[]{:S(2)}) %copy-start.1) | copy-done | bytes 4194328
  3.3 1.4 %windows.1.window = bf16[1024,1024]{1,0:T(8,128)(2,1)S(1)} custom-call(s32[4]{0:T(128)S(1)} %pad_add_fusion.starts, f32[2,256,2048]{2,1,0:T(8,128)S(1)} %copy-done.1), custom_call_target="tpu_custom_call" | custom-call | bytes 6291456 | tf_op jit(solution)/shard_map/windows/pallas_call | solution.py:440
  4.7 2.9 %rows_far.1 = (bf16[4,256,128]{2,1,0:T(8,128)(2,1)S(1)}, bf16[4,256,128]{2,1,0:T(8,128)(2,1)S(1)}, bf16[4,256,128]{2,1,0:T(8,128)(2,1)S(1)}, bf16[4,256,128]{2,1,0:T(8,128)(2,1)S(1)}, bf16[4,256,128]{2,1,0:T(8,128)(2,1)S(1)}) custom-call(bf16[1024,1024]{1,0:T(8,128)(2,1)S(1)} %windows.1.window, bf16[8,1024,256]{2,1,0:T(8,128)(2,1)S(1)} %copy-done), custom_call_target="tpu_custom_call" | custom-call | flops 2684354560 | bytes 5242880 | tf_op jit(solution)/shard_map/rows_far/pallas_call | solution.py:452
  7.6 0.0 copy-start.2
  7.6 0.0 copy-start.3
  7.6 1.6 %collective-permute-start = (bf16[4,256,128]{2,1,0:T(8,128)(2,1)S(1)}, bf16[4,256,128]{2,1,0:T(8,128)(2,1)S(1)}, u32[]{:S(2)}, u32[]{:S(2)}) collective-permute-start(bf16[4,256,128]{2,1,0:T(8,128)(2,1)S(1)} %get-tuple-element.33), channel_id=1, source_target_pairs={{4,0},{8,16},{12,20},{16,8},{20,12},{24,28},{5,1},{9,17},{13,21},{... | collective-permute-start | bytes 786440 | tf_op jit(solution)/shard_map/ppermute | solution.py:465
  9.2 7.6 %collective-permute-start.1 = (bf16[4,256,128]{2,1,0:T(8,128)(2,1)S(1)}, bf16[4,256,128]{2,1,0:T(8,128)(2,1)S(1)}, u32[]{:S(2)}, u32[]{:S(2)}) collective-permute-start(bf16[4,256,128]{2,1,0:T(8,128)(2,1)S(1)} %get-tuple-element.39), channel_id=1, source_target_pairs={{4,24},{8,28},{12,16},{16,12},{20,0},{24,4},{5,25},{9,29},{13,17},... | collective-permute-start | bytes 786440 | tf_op jit(solution)/shard_map/ppermute | solution.py:465
  16.7 1.9 %collective-permute-start.5 = (bf16[4,256,128]{2,1,0:T(8,128)(2,1)S(1)}, bf16[4,256,128]{2,1,0:T(8,128)(2,1)S(1)}, u32[]{:S(2)}, u32[]{:S(2)}) collective-permute-start(bf16[4,256,128]{2,1,0:T(8,128)(2,1)S(1)} %get-tuple-element.45), channel_id=1, source_target_pairs={{4,12},{8,0},{12,4},{16,24},{20,28},{24,16},{5,13},{9,1},{13,5},{1... | collective-permute-start | bytes 786440 | tf_op jit(solution)/shard_map/ppermute | solution.py:465
  18.7 0.0 collective-permute-done.got.rest_0_
  18.7 8.5 %collective-permute-start.3 = (bf16[4,256,128]{2,1,0:T(8,128)(2,1)S(1)}, bf16[4,256,128]{2,1,0:T(8,128)(2,1)S(1)}, u32[]{:S(2)}, u32[]{:S(2)}) collective-permute-start(bf16[4,256,128]{2,1,0:T(8,128)(2,1)S(1)} %last_far_blocks.1), channel_id=1, source_target_pairs={{4,20},{8,24},{12,28},{16,0},{20,4},{24,8},{0,16},{28,12},{5,21},{... | collective-permute-start | bytes 786440 | tf_op jit(solution)/shard_map/ppermute | solution.py:465
  27.2 1.8 %rows_near.1 = (bf16[4,256,128]{2,1,0:T(8,128)(2,1)S(1)}, bf16[4,256,128]{2,1,0:T(8,128)(2,1)S(1)}, bf16[4,256,128]{2,1,0:T(8,128)(2,1)S(1)}) custom-call(bf16[1024,1024]{1,0:T(8,128)(2,1)S(1)} %windows.1.window, bf16[8,1024,256]{2,1,0:T(8,128)(2,1)S(1)} %copy-done), custom_call_target="tpu_custom_call" | custom-call | flops 1610612736 | bytes 5242880 | tf_op jit(solution)/shard_map/rows_near/pallas_call | solution.py:452
  29.0 1.3 %collective-permute-start.4 = (bf16[4,256,128]{2,1,0:T(8,128)(2,1)S(1)}, bf16[4,256,128]{2,1,0:T(8,128)(2,1)S(1)}, u32[]{:S(2)}, u32[]{:S(2)}) collective-permute-start(bf16[4,256,128]{2,1,0:T(8,128)(2,1)S(1)} %get-tuple-element.44), channel_id=1, source_target_pairs={{4,0},{8,12},{12,8},{16,20},{20,16},{24,28},{5,1},{9,13},{13,9},{1... | collective-permute-start | bytes 786440 | tf_op jit(solution)/shard_map/ppermute | solution.py:465
  30.3 1.9 %collective-permute-start.6 = (bf16[4,256,128]{2,1,0:T(8,128)(2,1)S(1)}, bf16[4,256,128]{2,1,0:T(8,128)(2,1)S(1)}, u32[]{:S(2)}, u32[]{:S(2)}) collective-permute-start(bf16[4,256,128]{2,1,0:T(8,128)(2,1)S(1)} %get-tuple-element.46), channel_id=1, source_target_pairs={{4,8},{8,4},{12,0},{16,28},{20,24},{24,20},{5,9},{9,5},{13,1},{17,... | collective-permute-start | bytes 786440 | tf_op jit(solution)/shard_map/ppermute | solution.py:465
  32.3 0.0 collective-permute-done.1.rest_1_
  32.3 3.4 %collective-permute-start.2 = (bf16[4,256,128]{2,1,0:T(8,128)(2,1)S(1)}, bf16[4,256,128]{2,1,0:T(8,128)(2,1)S(1)}, u32[]{:S(2)}, u32[]{:S(2)}) collective-permute-start(bf16[4,256,128]{2,1,0:T(8,128)(2,1)S(1)} %get-tuple-element.40), channel_id=1, source_target_pairs={{4,28},{8,20},{12,24},{16,4},{20,8},{24,0},{5,29},{9,21},{13,25},{... | collective-permute-start | bytes 786440 | tf_op jit(solution)/shard_map/ppermute | solution.py:465
  35.7 0.6 amplitude.1
  36.3 0.0 collective-permute-done.5.rest_6_
  36.3 1.0 collective-permute-done.3.rest_3_
  37.3 0.0 collective-permute-done.4.rest_5_
  37.3 17.9 %collective-permute-done.6.rest_7_ = bf16[4,256,128]{2,1,0:T(8,128)(2,1)S(1)} collective-permute-done((bf16[4,256,128]{2,1,0:T(8,128)(2,1)S(1)}, bf16[4,256,128]{2,1,0:T(8,128)(2,1)S(1)}, u32[]{:S(2)}, u32[]{:S(2)}) %collective-permute-start.6) | collective-permute-done | bytes 262176 | tf_op jit(solution)/shard_map/ppermute | solution.py:465
  55.2 0.0 collective-permute-done.2.rest_2_
  55.2 5.3 %modulus_step.1 = (bf16[4,256,128]{2,1,0:T(8,128)(2,1)S(1)}, bf16[4,256,128]{2,1,0:T(8,128)(2,1)S(1)}, bf16[4,256,128]{2,1,0:T(8,128)(2,1)S(1)}, bf16[4,256,128]{2,1,0:T(8,128)(2,1)S(1)}) custom-call(f32[1024,256]{1,0:T(8,128)S(1)} %get-tuple-element.36.amplitude, bf16[8,256,1024]{2,1,0:T(8,128)(2,1)S(1)} %get-tuple-element.37.table, ...), custom_call_target="tpu_custom_call" | custom-call | flops 4294967296 | bytes 12582912 | tf_op jit(solution)/shard_map/modulus_step/pallas_call | solution.py:505
  60.6 0.1 collective-permute-start.7
  60.6 0.1 collective-permute-start.8
  60.8 3.4 %collective-permute-start.9 = (bf16[4,256,128]{2,1,0:T(8,128)(2,1)S(1)}, bf16[4,256,128]{2,1,0:T(8,128)(2,1)S(1)}, u32[]{:S(2)}, u32[]{:S(2)}) collective-permute-start(bf16[4,256,128]{2,1,0:T(8,128)(2,1)S(1)} %get-tuple-element.50), channel_id=1, source_target_pairs={{0,12},{4,8},{8,4},{12,0},{16,28},{20,24},{24,20},{28,16},{1,13},{... | collective-permute-start | bytes 786440 | tf_op jit(solution)/shard_map/ppermute | solution.py:465
  64.1 4.9 %collective-permute-done.7.rest_1_ = bf16[4,256,128]{2,1,0:T(8,128)(2,1)S(1)} collective-permute-done((bf16[4,256,128]{2,1,0:T(8,128)(2,1)S(1)}, bf16[4,256,128]{2,1,0:T(8,128)(2,1)S(1)}, u32[]{:S(2)}, u32[]{:S(2)}) %collective-permute-start.7) | collective-permute-done | bytes 262176 | tf_op jit(solution)/shard_map/ppermute | solution.py:465
  69.1 0.0 collective-permute-done.8.rest_2_
  69.1 2.8 %collective-permute-done.9.rest_3_ = bf16[4,256,128]{2,1,0:T(8,128)(2,1)S(1)} collective-permute-done((bf16[4,256,128]{2,1,0:T(8,128)(2,1)S(1)}, bf16[4,256,128]{2,1,0:T(8,128)(2,1)S(1)}, u32[]{:S(2)}, u32[]{:S(2)}) %collective-permute-start.9) | collective-permute-done | bytes 262176 | tf_op jit(solution)/shard_map/ppermute | solution.py:465
  71.9 2.7 %update_sent.1 = (bf16[2,2,256,512]{3,2,1,0:T(8,128)(2,1)S(1)}, bf16[2,2,256,512]{3,2,1,0:T(8,128)(2,1)S(1)}, bf16[1024,512]{1,0:T(8,128)(2,1)S(1)}) custom-call(s32[4]{0:T(128)S(1)} %pad_add_fusion.starts, bf16[8,1024,256]{2,1,0:T(8,128)(2,1)S(1)} %copy-done, bf16[4,256,128]{2,1,0:T(8,128)(2,1)S(1)} %get-tuple-element.47.rest_0_, ...), custom_call_target="tpu_custom_call" | custom-call | flops 1073741824 | bytes 8388608 | tf_op jit(solution)/shard_map/update_sent/pallas_call | solution.py:530
  74.6 0.1 collective-permute-start.11
  74.6 0.5 collective-permute-start.10
  75.1 2.4 %update_kept.1 = (f32[2,256,512]{2,1,0:T(8,128)S(1)}, f32[2,256,512]{2,1,0:T(8,128)S(1)}, f32[2,256,512]{2,1,0:T(8,128)S(1)}, f32[2,256,512]{2,1,0:T(8,128)S(1)}) custom-call(s32[4]{0:T(128)S(1)} %pad_add_fusion.starts, bf16[8,1024,256]{2,1,0:T(8,128)(2,1)S(1)} %copy-done, bf16[1024,512]{1,0:T(8,128)(2,1)S(1)} %get-tuple-element.51.back), custom_call_target="tpu_custom_call" | custom-call | flops 1073741824 | bytes 10485760 | tf_op jit(solution)/shard_map/update_kept/pallas_call | solution.py:545
  77.6 0.0 collective-permute-done.11.got_that
  77.6 0.1 x_first_kernel.1
  77.7 1.6 %collective-permute-start.13 = (bf16[2,256,384]{2,1,0:T(8,128)(2,1)S(1)}, bf16[2,256,384]{2,1,0:T(8,128)(2,1)S(1)}, u32[]{:S(2)}, u32[]{:S(2)}) collective-permute-start(bf16[2,256,384]{2,1,0:T(8,128)(2,1)S(1)} %x_first_kernel.1), channel_id=1, source_target_pairs={{0,2},{2,0},{1,3},{3,1},{4,6},{6,4},{5,7},{7,5},{8,10},{10,8},{9,1... | collective-permute-start | bytes 1179656 | tf_op jit(solution)/shard_map/ppermute | solution.py:563
  79.2 0.1 z_first_kernel.1
  79.3 3.1 %collective-permute-start.12 = (bf16[2,2,256,128]{3,2,1,0:T(8,128)(2,1)S(1)}, bf16[2,2,256,128]{3,2,1,0:T(8,128)(2,1)S(1)}, u32[]{:S(2)}, u32[]{:S(2)}) collective-permute-start(bf16[2,2,256,128]{3,2,1,0:T(8,128)(2,1)S(1)} %z_first_kernel.1), channel_id=1, source_target_pairs={{0,16},{4,20},{8,24},{20,4},{24,8},{28,12},{1,17},{5,21},{9,25},{2... | collective-permute-start | bytes 786440 | tf_op jit(solution)/shard_map/ppermute | solution.py:465
  82.5 6.4 %collective-permute-done.13.got_x = bf16[2,256,384]{2,1,0:T(8,128)(2,1)S(1)} collective-permute-done((bf16[2,256,384]{2,1,0:T(8,128)(2,1)S(1)}, bf16[2,256,384]{2,1,0:T(8,128)(2,1)S(1)}, u32[]{:S(2)}, u32[]{:S(2)}) %collective-permute-start.13) | collective-permute-done | bytes 393248 | tf_op jit(solution)/shard_map/ppermute | solution.py:563
  88.8 0.1 z_second_kernel.1
  89.0 15.0 %collective-permute-done.12.got_z = bf16[2,2,256,128]{3,2,1,0:T(8,128)(2,1)S(1)} collective-permute-done((bf16[2,2,256,128]{3,2,1,0:T(8,128)(2,1)S(1)}, bf16[2,2,256,128]{3,2,1,0:T(8,128)(2,1)S(1)}, u32[]{:S(2)}, u32[]{:S(2)}) %collective-permute-start.12) | collective-permute-done | bytes 262176 | tf_op jit(solution)/shard_map/ppermute | solution.py:465
  103.9 0.0 collective-permute-done.10.got_this
  103.9 0.1 x_second_kernel.1
  104.1 0.1 collective-permute-start.14
  104.2 1.9 %collective-permute-start.15 = (bf16[2,256,384]{2,1,0:T(8,128)(2,1)S(1)}, bf16[2,256,384]{2,1,0:T(8,128)(2,1)S(1)}, u32[]{:S(2)}, u32[]{:S(2)}) collective-permute-start(bf16[2,256,384]{2,1,0:T(8,128)(2,1)S(1)} %z_second_kernel.1), channel_id=1, source_target_pairs={{0,16},{4,20},{8,24},{20,4},{24,8},{28,12},{1,17},{5,21},{9,25},{2... | collective-permute-start | bytes 1179656 | tf_op jit(solution)/shard_map/ppermute | solution.py:465
  106.1 12.0 %collective-permute-done.14 = bf16[2,256,512]{2,1,0:T(8,128)(2,1)} collective-permute-done((bf16[2,256,512]{2,1,0:T(8,128)(2,1)S(1)}, bf16[2,256,512]{2,1,0:T(8,128)(2,1)}, u32[]{:S(2)}, u32[]{:S(2)}) %collective-permute-start.14) | collective-permute-done | bytes 524320 | tf_op jit(solution)/shard_map/ppermute | solution.py:568
  118.1 1.7 %fusion.2 = f32[2,256,512]{2,1,0:T(8,128)S(1)} fusion(f32[2,256,512]{2,1,0:T(8,128)S(1)} %get-tuple-element.52, bf16[2,256,512]{2,1,0:T(8,128)(2,1)} %collective-permute-done.14, f32[2,256,2048]{2,1,0:T(8,128)} %spectrum.1, s32[]{:T(128)S(6)} %select_n.3, bf16[2,2,256,512]{3,2,1,0:T(8,128)(2,1)S(1)} %collective-permute-done.10.got_this, ...), kind=kLoop, calls=%fused_computation.3 | loop fusion | flops 1835008 | bytes 4325380 | tf_op jit(solution)/shard_map/add | solution.py:576
  119.8 1.1 convert_add_fusion.1
  (8 shorter events, 0.1 us)
Async XLA Ops:
  0.0 4.6 %copy-start = (bf16[8,1024,256]{2,1,0:T(8,128)(2,1)S(1)}, bf16[8,1024,256]{2,1,0:T(8,128)(2,1)}, u32[]{:S(2)}) copy-start(bf16[8,1024,256]{2,1,0:T(8,128)(2,1)} %constant.18.clone.table) | copy-start | bytes 12582916
  0.9 2.4 %copy-start.1 = (f32[2,256,2048]{2,1,0:T(8,128)S(1)}, f32[2,256,2048]{2,1,0:T(8,128)}, u32[]{:S(2)}) copy-start(f32[2,256,2048]{2,1,0:T(8,128)} %spectrum.1) | copy-start | bytes 12582916
  7.6 28.1 %copy-start.2 = (bf16[8,256,1024]{2,1,0:T(8,128)(2,1)S(1)}, bf16[8,256,1024]{2,1,0:T(8,128)(2,1)}, u32[]{:S(2)}) copy-start(bf16[8,256,1024]{2,1,0:T(8,128)(2,1)} %constant.17.clone.table) | copy-start | bytes 12582916
  7.6 28.1 %copy-start.3 = (f32[2,128,1024]{2,1,0:T(8,128)S(1)}, f32[2,128,1024]{2,1,0:T(8,128)}, u32[]{:S(2)}) copy-start(f32[2,128,1024]{2,1,0:T(8,128)} %images) | copy-start | bytes 3145732
  7.6 11.1 %collective-permute-start = (bf16[4,256,128]{2,1,0:T(8,128)(2,1)S(1)}, bf16[4,256,128]{2,1,0:T(8,128)(2,1)S(1)}, u32[]{:S(2)}, u32[]{:S(2)}) collective-permute-start(bf16[4,256,128]{2,1,0:T(8,128)(2,1)S(1)} %get-tuple-element.33), channel_id=1, source_target_pairs={{4,0},{8,16},{12,20},{16,8},{20,12},{24,28},{5,1},{9,17},{13,21},{... | collective-permute-start | bytes 786440 | tf_op jit(solution)/shard_map/ppermute | solution.py:465
  9.2 23.1 %collective-permute-start.1 = (bf16[4,256,128]{2,1,0:T(8,128)(2,1)S(1)}, bf16[4,256,128]{2,1,0:T(8,128)(2,1)S(1)}, u32[]{:S(2)}, u32[]{:S(2)}) collective-permute-start(bf16[4,256,128]{2,1,0:T(8,128)(2,1)S(1)} %get-tuple-element.39), channel_id=1, source_target_pairs={{4,24},{8,28},{12,16},{16,12},{20,0},{24,4},{5,25},{9,29},{13,17},... | collective-permute-start | bytes 786440 | tf_op jit(solution)/shard_map/ppermute | solution.py:465
  16.7 19.5 %collective-permute-start.5 = (bf16[4,256,128]{2,1,0:T(8,128)(2,1)S(1)}, bf16[4,256,128]{2,1,0:T(8,128)(2,1)S(1)}, u32[]{:S(2)}, u32[]{:S(2)}) collective-permute-start(bf16[4,256,128]{2,1,0:T(8,128)(2,1)S(1)} %get-tuple-element.45), channel_id=1, source_target_pairs={{4,12},{8,0},{12,4},{16,24},{20,28},{24,16},{5,13},{9,1},{13,5},{1... | collective-permute-start | bytes 786440 | tf_op jit(solution)/shard_map/ppermute | solution.py:465
  18.7 18.6 %collective-permute-start.3 = (bf16[4,256,128]{2,1,0:T(8,128)(2,1)S(1)}, bf16[4,256,128]{2,1,0:T(8,128)(2,1)S(1)}, u32[]{:S(2)}, u32[]{:S(2)}) collective-permute-start(bf16[4,256,128]{2,1,0:T(8,128)(2,1)S(1)} %last_far_blocks.1), channel_id=1, source_target_pairs={{4,20},{8,24},{12,28},{16,0},{20,4},{24,8},{0,16},{28,12},{5,21},{... | collective-permute-start | bytes 786440 | tf_op jit(solution)/shard_map/ppermute | solution.py:465
  29.0 8.3 %collective-permute-start.4 = (bf16[4,256,128]{2,1,0:T(8,128)(2,1)S(1)}, bf16[4,256,128]{2,1,0:T(8,128)(2,1)S(1)}, u32[]{:S(2)}, u32[]{:S(2)}) collective-permute-start(bf16[4,256,128]{2,1,0:T(8,128)(2,1)S(1)} %get-tuple-element.44), channel_id=1, source_target_pairs={{4,0},{8,12},{12,8},{16,20},{20,16},{24,28},{5,1},{9,13},{13,9},{1... | collective-permute-start | bytes 786440 | tf_op jit(solution)/shard_map/ppermute | solution.py:465
  30.3 24.9 %collective-permute-start.6 = (bf16[4,256,128]{2,1,0:T(8,128)(2,1)S(1)}, bf16[4,256,128]{2,1,0:T(8,128)(2,1)S(1)}, u32[]{:S(2)}, u32[]{:S(2)}) collective-permute-start(bf16[4,256,128]{2,1,0:T(8,128)(2,1)S(1)} %get-tuple-element.46), channel_id=1, source_target_pairs={{4,8},{8,4},{12,0},{16,28},{20,24},{24,20},{5,9},{9,5},{13,1},{17,... | collective-permute-start | bytes 786440 | tf_op jit(solution)/shard_map/ppermute | solution.py:465
  32.3 23.0 %collective-permute-start.2 = (bf16[4,256,128]{2,1,0:T(8,128)(2,1)S(1)}, bf16[4,256,128]{2,1,0:T(8,128)(2,1)S(1)}, u32[]{:S(2)}, u32[]{:S(2)}) collective-permute-start(bf16[4,256,128]{2,1,0:T(8,128)(2,1)S(1)} %get-tuple-element.40), channel_id=1, source_target_pairs={{4,28},{8,20},{12,24},{16,4},{20,8},{24,0},{5,29},{9,21},{13,25},{... | collective-permute-start | bytes 786440 | tf_op jit(solution)/shard_map/ppermute | solution.py:465
  60.6 8.5 %collective-permute-start.7 = (bf16[4,256,128]{2,1,0:T(8,128)(2,1)S(1)}, bf16[4,256,128]{2,1,0:T(8,128)(2,1)S(1)}, u32[]{:S(2)}, u32[]{:S(2)}) collective-permute-start(bf16[4,256,128]{2,1,0:T(8,128)(2,1)S(1)} %get-tuple-element.48), channel_id=1, source_target_pairs={{0,4},{4,0},{8,12},{12,8},{16,20},{20,16},{24,28},{28,24},{1,5},{5... | collective-permute-start | bytes 786440 | tf_op jit(solution)/shard_map/ppermute | solution.py:465
  60.6 8.4 %collective-permute-start.8 = (bf16[4,256,128]{2,1,0:T(8,128)(2,1)S(1)}, bf16[4,256,128]{2,1,0:T(8,128)(2,1)S(1)}, u32[]{:S(2)}, u32[]{:S(2)}) collective-permute-start(bf16[4,256,128]{2,1,0:T(8,128)(2,1)S(1)} %get-tuple-element.49), channel_id=1, source_target_pairs={{0,8},{4,12},{8,0},{12,4},{16,24},{20,28},{24,16},{28,20},{1,9},{5... | collective-permute-start | bytes 786440 | tf_op jit(solution)/shard_map/ppermute | solution.py:465
  60.8 11.1 %collective-permute-start.9 = (bf16[4,256,128]{2,1,0:T(8,128)(2,1)S(1)}, bf16[4,256,128]{2,1,0:T(8,128)(2,1)S(1)}, u32[]{:S(2)}, u32[]{:S(2)}) collective-permute-start(bf16[4,256,128]{2,1,0:T(8,128)(2,1)S(1)} %get-tuple-element.50), channel_id=1, source_target_pairs={{0,12},{4,8},{8,4},{12,0},{16,28},{20,24},{24,20},{28,16},{1,13},{... | collective-permute-start | bytes 786440 | tf_op jit(solution)/shard_map/ppermute | solution.py:465
  74.6 3.0 %collective-permute-start.11 = (bf16[2,2,256,512]{3,2,1,0:T(8,128)(2,1)S(1)}, bf16[2,2,256,512]{3,2,1,0:T(8,128)(2,1)S(1)}, u32[]{:S(2)}, u32[]{:S(2)}) collective-permute-start(bf16[2,2,256,512]{3,2,1,0:T(8,128)(2,1)S(1)} %get-tuple-element.57), channel_id=1, source_target_pairs={{0,1},{1,0},{2,3},{3,2},{4,5},{5,4},{6,7},{7,6},{8,9},{9,8},{10,11... | collective-permute-start | bytes 3145736 | tf_op jit(solution)/shard_map/ppermute | solution.py:543
  74.6 29.3 %collective-permute-start.10 = (bf16[2,2,256,512]{3,2,1,0:T(8,128)(2,1)S(1)}, bf16[2,2,256,512]{3,2,1,0:T(8,128)(2,1)S(1)}, u32[]{:S(2)}, u32[]{:S(2)}) collective-permute-start(bf16[2,2,256,512]{3,2,1,0:T(8,128)(2,1)S(1)} %get-tuple-element.53), channel_id=1, source_target_pairs={{0,1},{1,0},{2,3},{3,2},{4,5},{5,4},{6,7},{7,6},{8,9},{9,8},{10,11... | collective-permute-start | bytes 3145736 | tf_op jit(solution)/shard_map/ppermute | solution.py:544
  77.7 11.2 %collective-permute-start.13 = (bf16[2,256,384]{2,1,0:T(8,128)(2,1)S(1)}, bf16[2,256,384]{2,1,0:T(8,128)(2,1)S(1)}, u32[]{:S(2)}, u32[]{:S(2)}) collective-permute-start(bf16[2,256,384]{2,1,0:T(8,128)(2,1)S(1)} %x_first_kernel.1), channel_id=1, source_target_pairs={{0,2},{2,0},{1,3},{3,1},{4,6},{6,4},{5,7},{7,5},{8,10},{10,8},{9,1... | collective-permute-start | bytes 1179656 | tf_op jit(solution)/shard_map/ppermute | solution.py:563
  79.3 24.6 %collective-permute-start.12 = (bf16[2,2,256,128]{3,2,1,0:T(8,128)(2,1)S(1)}, bf16[2,2,256,128]{3,2,1,0:T(8,128)(2,1)S(1)}, u32[]{:S(2)}, u32[]{:S(2)}) collective-permute-start(bf16[2,2,256,128]{3,2,1,0:T(8,128)(2,1)S(1)} %z_first_kernel.1), channel_id=1, source_target_pairs={{0,16},{4,20},{8,24},{20,4},{24,8},{28,12},{1,17},{5,21},{9,25},{2... | collective-permute-start | bytes 786440 | tf_op jit(solution)/shard_map/ppermute | solution.py:465
  104.1 14.0 %collective-permute-start.14 = (bf16[2,256,512]{2,1,0:T(8,128)(2,1)S(1)}, bf16[2,256,512]{2,1,0:T(8,128)(2,1)}, u32[]{:S(2)}, u32[]{:S(2)}) collective-permute-start(bf16[2,256,512]{2,1,0:T(8,128)(2,1)S(1)} %x_second_kernel.1), channel_id=1, source_target_pairs={{0,2},{2,0},{1,3},{3,1},{4,6},{6,4},{5,7},{7,5},{8,10},{10,8},{9,1... | collective-permute-start | bytes 1572872 | tf_op jit(solution)/shard_map/ppermute | solution.py:568
  104.2 15.6 %collective-permute-start.15 = (bf16[2,256,384]{2,1,0:T(8,128)(2,1)S(1)}, bf16[2,256,384]{2,1,0:T(8,128)(2,1)S(1)}, u32[]{:S(2)}, u32[]{:S(2)}) collective-permute-start(bf16[2,256,384]{2,1,0:T(8,128)(2,1)S(1)} %z_second_kernel.1), channel_id=1, source_target_pairs={{0,16},{4,20},{8,24},{20,4},{24,8},{28,12},{1,17},{5,21},{9,25},{2... | collective-permute-start | bytes 1179656 | tf_op jit(solution)/shard_map/ppermute | solution.py:465

commit v11 on v7

--- a/solution.py
+++ b/solution.py
@@ -370,6 +370,32 @@
     update_columns(True, starts, table, back, outs)
 
 
+def z_first_kernel(that_near, that_far, got_that, out):
+    cols = out.shape[3]
+    for i, kept in enumerate((that_near, that_far)):
+        total = kept[:, :, :cols] + got_that[i, :, :, :cols].astype(jnp.float32)
+        out[i] = total.astype(out.dtype)
+
+
+def x_first_kernel(that_far, got_that, out):
+    cols = that_far.shape[2] - out.shape[2]
+    total = that_far[:, :, cols:] + got_that[1, :, :, cols:].astype(jnp.float32)
+    out[...] = total.astype(out.dtype)
+
+
+def z_second_kernel(that_near, got_that, got_x, out):
+    cols = that_near.shape[2] - out.shape[2]
+    total = that_near[:, :, cols:] + got_that[0, :, :, cols:].astype(jnp.float32)
+    out[...] = (total + got_x[...].astype(jnp.float32)).astype(out.dtype)
+
+
+def x_second_kernel(this_far, got_this, got_z, out):
+    cols = got_z.shape[3]
+    total = this_far[...] + got_this[1].astype(jnp.float32)
+    out[:, :, cols:] = total[:, :, cols:].astype(out.dtype)
+    out[:, :, :cols] = (total[:, :, :cols] + got_z[1].astype(jnp.float32)).astype(out.dtype)
+
+
 def local_call(kernel, out_shape, spaces, scratch, flops, moved, name):
     return pl.pallas_call(
         kernel,
@@ -488,7 +514,11 @@
         permute(strips[d], [(s, s ^ d) for s in range(SLABS)]) for d in range(1, HALF)
     ]
     share = width // 2
+    first = share // 4
     piece = (2, rows, share)
+    cores = [(0, 1), (1, 0), (2, 3), (3, 2)]
+    planes = [(0, 2), (2, 0), (1, 3), (3, 1)]
+    across = [(s, s ^ 4) for s in range(SLABS) if FIRST < s ^ 4 < LAST]
     sent_this, sent_that, back = local_call(
         sent_kernel,
         [
@@ -502,8 +532,6 @@
         8 * 2**20,
         "update_sent",
     )(starts, by_col, *home)
-    cores = [(0, 1), (1, 0), (2, 3), (3, 2)]
-    planes = [(0, 2), (2, 0), (1, 3), (3, 1)]
     got_that = lax.ppermute(sent_that, "led", cores)
     got_this = lax.ppermute(sent_this, "led", cores)
     this_near, this_far, that_near, that_far = local_call(
@@ -516,30 +544,29 @@
         "update_kept",
     )(starts, by_col, back)
 
-    def summed(*values):
-        return sum(value.astype(jnp.float32) for value in values)
-
-    across = [(s, s ^ 4) for s in range(SLABS) if FIRST < s ^ 4 < LAST]
-    from_x = []
-    for i in range(2):
-        here = slice(i * rows // 2, (i + 1) * rows // 2)
-        over = summed(that_far[:, here], got_that[1, :, here]).astype(bf16)
-        from_x.append((here, lax.ppermute(over, "led", planes)))
-    from_z = []
-    over = None
-    over_this = summed(this_far, got_this[1]).astype(bf16)
-    for here, got in from_x:
-        if over is None:
-            got, over_this = lax.optimization_barrier((got, over_this))
-        else:
-            over, got = lax.optimization_barrier((over, got))
-        over = summed(that_near[:, here], got_that[0, :, here], got).astype(bf16)
-        from_z.append(permute(over, across))
-    over_this = lax.ppermute(over_this, "led", planes)
-    own_part = lax.dynamic_slice_in_dim(spectrum, led_at * share, share, 2)
-    base = own_part + summed(this_near, got_this[0], over_this)
-    base, *from_z = lax.optimization_barrier((base, *from_z))
-    return base + summed(jnp.concatenate(from_z, 1))
+    def sum_call(kernel, shape, *values):
+        out_shape = jax.ShapeDtypeStruct(shape, bf16)
+        specs = [vmem] * len(values)
+        return local_call(kernel, out_shape, specs, [], 0, 2**20, kernel.__name__)(*values)
+
+    over = sum_call(z_first_kernel, (2, 2, rows, first), that_near, that_far, got_that)
+    got_z_first = permute(over, across)
+    over = sum_call(x_first_kernel, (2, rows, share - first), that_far, got_that)
+    got_x = lax.ppermute(over, "led", planes)
+    over = sum_call(z_second_kernel, (2, rows, share - first), that_near, got_that, got_x)
+    got_z_second = permute(over, across)
+    over = sum_call(x_second_kernel, piece, this_far, got_this, got_z_first)
+    got_x = lax.ppermute(over, "led", planes)
+
+    def widen(value, before):
+        after = share - before - value.shape[2]
+        return jnp.pad(value.astype(jnp.float32), ((0, 0), (0, 0), (before, after)))
+
+    base = lax.dynamic_slice_in_dim(spectrum, led_at * share, share, 2)
+    base += this_near + got_this[0].astype(jnp.float32) + got_x.astype(jnp.float32)
+    base += widen(got_z_first[0], 0)
+    base, got_z_second = lax.optimization_barrier((base, got_z_second))
+    return base + widen(got_z_second, first)
 
 
 def solution(mesh):

time: 123 us -> 115 us (0.935)
  waiting for transfers between devices: 51.1 us -> 44.4 us
  other arithmetic: 7.97 us -> 4.03 us
  Pallas kernels: 17.1 us -> 20 us
    ppermute x3 -> x2, waiting for transfers between devices: 19.8 us -> 9.61 us  [body_slabs(): got_x = lax.ppermute(over, 'led', planes)]
    convert_element_type x4 -> x0, other arithmetic: 4.23 us -> none  [the longest x2 2.19 us: body_slabs(): over = summed(that_near[:, here], got_that[0, :, here], got).astype(bf16)]
    ppermute x13, waiting for transfers between devices: 31.3 us -> 34.8 us  [permute(): return lax.ppermute(sent, 'slab', pairs)]
    pallas_call x0 -> x4, Pallas kernels: none -> 3 us  [sum_call(): local_call(kernel, out_shape, specs, [], 0, 2 ** 20, kernel.__name__)]
    ppermute x3 -> x2, starting transfers between devices: 3.51 us -> 2.99 us  [body_slabs(): got_x = lax.ppermute(over, 'led', planes)]
  transfers between devices with their start and end apart: 18 -> 17, of which waited for: 8 -> 8; matrix products, arithmetic and copies ran while one was open for 5% -> 2% of each run, Pallas kernels for 5% -> 8%
where the time goes in v11:
time: 115 us; the launch traced here: 114 us
  waiting for transfers between devices  44.4 us (39%)
  starting transfers between devices  42.9 us (37%)
  Pallas kernels  20 us (17%)
  other arithmetic  4.03 us (4%)
  local copies, waits for them, and re-layouts  2.42 us (2%)
    ppermute x13, starting transfers between devices, permute(): return lax.ppermute(sent, 'slab', pairs)  39.3 us
    ppermute x13, waiting for transfers between devices, permute(): return lax.ppermute(sent, 'slab', pairs)  34.8 us
    ppermute x2, waiting for transfers between devices, body_slabs(): got_x = lax.ppermute(over, 'led', planes)  9.61 us
    pallas_call x1, Pallas kernels, body_slabs(): local_call(field_kernel, [sent_block] * HALF, [vmem] * 11, [pltpu.VMEM((w...  5.3 us
    pallas_call x2, Pallas kernels, rows_call(): local_call(functools.partial(rows_kernel, which), [sent_block] * count, [...  4.69 us
    pallas_call x4, Pallas kernels, sum_call(): local_call(kernel, out_shape, specs, [], 0, 2 ** 20, kernel.__name__)  3 us
    ppermute x2, starting transfers between devices, body_slabs(): got_x = lax.ppermute(over, 'led', planes)  2.99 us
    pallas_call x1, Pallas kernels, body_slabs(): local_call(sent_kernel, [jax.ShapeDtypeStruct((2,) + piece, bf16), jax.Sh...  2.65 us
  transfers between devices with their start and end apart: 17, of which 8 were waited for; matrix products, arithmetic and copies ran while one was open for 2% of the time, Pallas kernels for 8%

profile of v11, /device:TPU:4, one launch (start us, length us, event | category | flops | bytes accessed | tf_op | source)
XLA Modules:
  0.0 114.0 jit_solution(8767860395787785779)
XLA Ops:
  0.0 0.9 pad_add_fusion.starts
  0.9 2.4 %copy-done.1 = f32[2,256,2048]{2,1,0:T(8,128)S(1)} copy-done((f32[2,256,2048]{2,1,0:T(8,128)S(1)}, f32[2,256,2048]{2,1,0:T(8,128)}, u32[]{:S(2)}) %copy-start.1) | copy-done | bytes 4194328
  3.3 1.4 %windows.1.window = bf16[1024,1024]{1,0:T(8,128)(2,1)S(1)} custom-call(s32[4]{0:T(128)S(1)} %pad_add_fusion.starts, f32[2,256,2048]{2,1,0:T(8,128)S(1)} %copy-done.1), custom_call_target="tpu_custom_call" | custom-call | bytes 6291456 | tf_op jit(solution)/shard_map/windows/pallas_call | solution.py:433
  4.7 1.8 %rows_round_1.1 = (bf16[4,256,128]{2,1,0:T(8,128)(2,1)S(1)}, bf16[4,256,128]{2,1,0:T(8,128)(2,1)S(1)}, bf16[4,256,128]{2,1,0:T(8,128)(2,1)S(1)}) custom-call(bf16[1024,1024]{1,0:T(8,128)(2,1)S(1)} %windows.1.window, bf16[8,1024,256]{2,1,0:T(8,128)(2,1)S(1)} %copy-done), custom_call_target="tpu_custom_call" | custom-call | flops 1610612736 | bytes 5242880 | tf_op jit(solution)/shard_map/rows_round_1/pallas_call | solution.py:445
  6.5 1.3 %collective-permute-start = (bf16[4,256,128]{2,1,0:T(8,128)(2,1)S(1)}, bf16[4,256,128]{2,1,0:T(8,128)(2,1)S(1)}, u32[]{:S(2)}, u32[]{:S(2)}) collective-permute-start(bf16[4,256,128]{2,1,0:T(8,128)(2,1)S(1)} %get-tuple-element.34), channel_id=1, source_target_pairs={{8,16},{12,20},{16,8},{20,12},{4,0},{24,28},{9,17},{13,21},{17,9},... | collective-permute-start | bytes 786440 | tf_op jit(solution)/shard_map/ppermute | solution.py:458
  7.8 1.3 %collective-permute-start.1 = (bf16[4,256,128]{2,1,0:T(8,128)(2,1)S(1)}, bf16[4,256,128]{2,1,0:T(8,128)(2,1)S(1)}, u32[]{:S(2)}, u32[]{:S(2)}) collective-permute-start(bf16[4,256,128]{2,1,0:T(8,128)(2,1)S(1)} %get-tuple-element.43), channel_id=1, source_target_pairs={{8,20},{12,16},{16,12},{20,8},{4,0},{24,28},{9,21},{13,17},{17,13}... | collective-permute-start | bytes 786440 | tf_op jit(solution)/shard_map/ppermute | solution.py:458
  9.1 0.0 copy-start.2
  9.1 0.0 copy-start.3
  9.1 6.9 %collective-permute-start.6 = (bf16[4,256,128]{2,1,0:T(8,128)(2,1)S(1)}, bf16[4,256,128]{2,1,0:T(8,128)(2,1)S(1)}, u32[]{:S(2)}, u32[]{:S(2)}) collective-permute-start(bf16[4,256,128]{2,1,0:T(8,128)(2,1)S(1)} %get-tuple-element.48), channel_id=1, source_target_pairs={{4,12},{8,0},{12,4},{16,24},{20,28},{24,16},{5,13},{9,1},{13,5},{1... | collective-permute-start | bytes 786440 | tf_op jit(solution)/shard_map/ppermute | solution.py:458
  16.1 2.9 %rows_round_2.1 = (bf16[4,256,128]{2,1,0:T(8,128)(2,1)S(1)}, bf16[4,256,128]{2,1,0:T(8,128)(2,1)S(1)}, bf16[4,256,128]{2,1,0:T(8,128)(2,1)S(1)}, bf16[4,256,128]...) custom-call(bf16[1024,1024]{1,0:T(8,128)(2,1)S(1)} %windows.1.window, bf16[8,1024,256]{2,1,0:T(8,128)(2,1)S(1)} %copy-done), custom_call_target="tpu_custom_call" | custom-call | flops 2684354560 | bytes 5242880 | tf_op jit(solution)/shard_map/rows_round_2/pallas_call | solution.py:445
  18.9 0.0 collective-permute-done.got.rest_0_
  19.0 1.2 %collective-permute-start.2 = (bf16[4,256,128]{2,1,0:T(8,128)(2,1)S(1)}, bf16[4,256,128]{2,1,0:T(8,128)(2,1)S(1)}, u32[]{:S(2)}, u32[]{:S(2)}) collective-permute-start(bf16[4,256,128]{2,1,0:T(8,128)(2,1)S(1)} %class_4_blocks.1), channel_id=1, source_target_pairs={{0,16},{4,20},{8,24},{12,28},{16,0},{20,4},{24,8},{28,12},{1,17},{... | collective-permute-start | bytes 786440 | tf_op jit(solution)/shard_map/ppermute | solution.py:458
  20.2 1.3 %collective-permute-start.4 = (bf16[4,256,128]{2,1,0:T(8,128)(2,1)S(1)}, bf16[4,256,128]{2,1,0:T(8,128)(2,1)S(1)}, u32[]{:S(2)}, u32[]{:S(2)}) collective-permute-start(bf16[4,256,128]{2,1,0:T(8,128)(2,1)S(1)} %get-tuple-element.45.own), channel_id=1, source_target_pairs={{8,28},{12,24},{16,4},{20,0},{9,29},{13,25},{17,5},{21,1},{10,30},... | collective-permute-start | bytes 786440 | tf_op jit(solution)/shard_map/ppermute | solution.py:458
  21.5 0.0 collective-permute-done.1.got.rest_1_
  21.6 6.0 %collective-permute-start.3 = (bf16[4,256,128]{2,1,0:T(8,128)(2,1)S(1)}, bf16[4,256,128]{2,1,0:T(8,128)(2,1)S(1)}, u32[]{:S(2)}, u32[]{:S(2)}) collective-permute-start(bf16[4,256,128]{2,1,0:T(8,128)(2,1)S(1)} %class_6_blocks.1), channel_id=1, source_target_pairs={{0,24},{4,28},{24,0},{28,4},{1,25},{5,29},{25,1},{29,5},{2,26},{6,... | collective-permute-start | bytes 786440 | tf_op jit(solution)/shard_map/ppermute | solution.py:458
  27.6 1.5 %collective-permute-start.5 = (bf16[4,256,128]{2,1,0:T(8,128)(2,1)S(1)}, bf16[4,256,128]{2,1,0:T(8,128)(2,1)S(1)}, u32[]{:S(2)}, u32[]{:S(2)}) collective-permute-start(bf16[4,256,128]{2,1,0:T(8,128)(2,1)S(1)} %get-tuple-element.47), channel_id=1, source_target_pairs={{4,0},{8,12},{12,8},{16,20},{20,16},{24,28},{5,1},{9,13},{13,9},{1... | collective-permute-start | bytes 786440 | tf_op jit(solution)/shard_map/ppermute | solution.py:458
  29.0 0.0 collective-permute-done.6.rest_7_
  29.0 12.4 %collective-permute-start.7 = (bf16[4,256,128]{2,1,0:T(8,128)(2,1)S(1)}, bf16[4,256,128]{2,1,0:T(8,128)(2,1)S(1)}, u32[]{:S(2)}, u32[]{:S(2)}) collective-permute-start(bf16[4,256,128]{2,1,0:T(8,128)(2,1)S(1)} %get-tuple-element.49), channel_id=1, source_target_pairs={{4,8},{8,4},{12,0},{16,28},{20,24},{24,20},{5,9},{9,5},{13,1},{17,... | collective-permute-start | bytes 786440 | tf_op jit(solution)/shard_map/ppermute | solution.py:458
  41.5 0.6 amplitude.1
  42.0 0.0 collective-permute-done.3.rest_3_
  42.0 3.5 %collective-permute-done.4.rest_4_ = bf16[4,256,128]{2,1,0:T(8,128)(2,1)S(1)} collective-permute-done((bf16[4,256,128]{2,1,0:T(8,128)(2,1)S(1)}, bf16[4,256,128]{2,1,0:T(8,128)(2,1)S(1)}, u32[]{:S(2)}, u32[]{:S(2)}) %collective-permute-start.4) | collective-permute-done | bytes 262176 | tf_op jit(solution)/shard_map/ppermute | solution.py:458
  45.6 0.0 collective-permute-done.5.rest_6_
  45.6 5.5 %collective-permute-done.7.rest_8_ = bf16[4,256,128]{2,1,0:T(8,128)(2,1)S(1)} collective-permute-done((bf16[4,256,128]{2,1,0:T(8,128)(2,1)S(1)}, bf16[4,256,128]{2,1,0:T(8,128)(2,1)S(1)}, u32[]{:S(2)}, u32[]{:S(2)}) %collective-permute-start.7) | collective-permute-done | bytes 262176 | tf_op jit(solution)/shard_map/ppermute | solution.py:458
  51.1 5.3 %modulus_step.1 = (bf16[4,256,128]{2,1,0:T(8,128)(2,1)S(1)}, bf16[4,256,128]{2,1,0:T(8,128)(2,1)S(1)}, bf16[4,256,128]{2,1,0:T(8,128)(2,1)S(1)}, bf16[4,256,128]{2,1,0:T(8,128)(2,1)S(1)}) custom-call(f32[1024,256]{1,0:T(8,128)S(1)} %get-tuple-element.40.amplitude, bf16[8,256,1024]{2,1,0:T(8,128)(2,1)S(1)} %get-tuple-element.41.table, ...), custom_call_target="tpu_custom_call" | custom-call | flops 4294967296 | bytes 12582912 | tf_op jit(solution)/shard_map/modulus_step/pallas_call | solution.py:497
  56.4 0.2 collective-permute-start.10
  56.6 1.5 %collective-permute-start.8 = (bf16[4,256,128]{2,1,0:T(8,128)(2,1)S(1)}, bf16[4,256,128]{2,1,0:T(8,128)(2,1)S(1)}, u32[]{:S(2)}, u32[]{:S(2)}) collective-permute-start(bf16[4,256,128]{2,1,0:T(8,128)(2,1)S(1)} %get-tuple-element.51), channel_id=1, source_target_pairs={{0,4},{4,0},{8,12},{12,8},{16,20},{20,16},{24,28},{28,24},{1,5},{5... | collective-permute-start | bytes 786440 | tf_op jit(solution)/shard_map/ppermute | solution.py:458
  58.1 1.9 %collective-permute-start.9 = (bf16[4,256,128]{2,1,0:T(8,128)(2,1)S(1)}, bf16[4,256,128]{2,1,0:T(8,128)(2,1)S(1)}, u32[]{:S(2)}, u32[]{:S(2)}) collective-permute-start(bf16[4,256,128]{2,1,0:T(8,128)(2,1)S(1)} %get-tuple-element.52), channel_id=1, source_target_pairs={{0,8},{4,12},{8,0},{12,4},{16,24},{20,28},{24,16},{28,20},{1,9},{5... | collective-permute-start | bytes 786440 | tf_op jit(solution)/shard_map/ppermute | solution.py:458
  59.9 6.6 %collective-permute-done.10.rest_3_ = bf16[4,256,128]{2,1,0:T(8,128)(2,1)S(1)} collective-permute-done((bf16[4,256,128]{2,1,0:T(8,128)(2,1)S(1)}, bf16[4,256,128]{2,1,0:T(8,128)(2,1)S(1)}, u32[]{:S(2)}, u32[]{:S(2)}) %collective-permute-start.10) | collective-permute-done | bytes 262176 | tf_op jit(solution)/shard_map/ppermute | solution.py:458
  66.6 3.8 %collective-permute-done.8.rest_1_ = bf16[4,256,128]{2,1,0:T(8,128)(2,1)S(1)} collective-permute-done((bf16[4,256,128]{2,1,0:T(8,128)(2,1)S(1)}, bf16[4,256,128]{2,1,0:T(8,128)(2,1)S(1)}, u32[]{:S(2)}, u32[]{:S(2)}) %collective-permute-start.8) | collective-permute-done | bytes 262176 | tf_op jit(solution)/shard_map/ppermute | solution.py:458
  70.4 0.9 collective-permute-done.9.rest_2_
  71.3 2.6 %update_sent.1 = (bf16[2,2,256,512]{3,2,1,0:T(8,128)(2,1)S(1)}, bf16[2,2,256,512]{3,2,1,0:T(8,128)(2,1)S(1)}, bf16[1024,512]{1,0:T(8,128)(2,1)S(1)}) custom-call(s32[4]{0:T(128)S(1)} %pad_add_fusion.starts, bf16[8,1024,256]{2,1,0:T(8,128)(2,1)S(1)} %copy-done, bf16[4,256,128]{2,1,0:T(8,128)(2,1)S(1)} %get-tuple-element.50.rest_0_, ...), custom_call_target="tpu_custom_call" | custom-call | flops 1073741824 | bytes 8388608 | tf_op jit(solution)/shard_map/update_sent/pallas_call | solution.py:522
  73.9 0.1 collective-permute-start.12
  74.0 0.5 collective-permute-start.11
  74.5 2.4 %update_kept.1 = (f32[2,256,512]{2,1,0:T(8,128)S(1)}, f32[2,256,512]{2,1,0:T(8,128)S(1)}, f32[2,256,512]{2,1,0:T(8,128)S(1)}, f32[2,256,512]{2,1,0:T(8,128)S(1)}) custom-call(s32[4]{0:T(128)S(1)} %pad_add_fusion.starts, bf16[8,1024,256]{2,1,0:T(8,128)(2,1)S(1)} %copy-done, bf16[1024,512]{1,0:T(8,128)(2,1)S(1)} %get-tuple-element.54.back), custom_call_target="tpu_custom_call" | custom-call | flops 1073741824 | bytes 10485760 | tf_op jit(solution)/shard_map/update_kept/pallas_call | solution.py:537
  77.0 0.0 copy-start.4
  77.0 0.1 z_first_kernel.1
  77.1 2.0 %collective-permute-start.13 = (bf16[2,2,256,128]{3,2,1,0:T(8,128)(2,1)S(1)}, bf16[2,2,256,128]{3,2,1,0:T(8,128)(2,1)S(1)}, u32[]{:S(2)}, u32[]{:S(2)}) collective-permute-start(bf16[2,2,256,128]{3,2,1,0:T(8,128)(2,1)S(1)} %z_first_kernel.1), channel_id=1, source_target_pairs={{0,16},{4,20},{8,24},{20,4},{24,8},{28,12},{1,17},{5,21},{9,25},{2... | collective-permute-start | bytes 786440 | tf_op jit(solution)/shard_map/ppermute | solution.py:458
  79.1 0.8 x_first_kernel.1
  79.9 1.5 %collective-permute-start.15 = (bf16[2,256,384]{2,1,0:T(8,128)(2,1)}, bf16[2,256,384]{2,1,0:T(8,128)(2,1)}, u32[]{:S(2)}, u32[]{:S(2)}) collective-permute-start(bf16[2,256,384]{2,1,0:T(8,128)(2,1)} %x_first_kernel.1), channel_id=1, source_target_pairs={{0,2},{2,0},{1,3},{3,1},{4,6},{6,4},{5,7},{7,5},{8,10},{10,8},{9,1... | collective-permute-start | bytes 1179656 | tf_op jit(solution)/shard_map/ppermute | solution.py:555
  81.4 12.1 %collective-permute-done.13.got_z = bf16[2,2,256,128]{3,2,1,0:T(8,128)(2,1)S(1)} collective-permute-done((bf16[2,2,256,128]{3,2,1,0:T(8,128)(2,1)S(1)}, bf16[2,2,256,128]{3,2,1,0:T(8,128)(2,1)S(1)}, u32[]{:S(2)}, u32[]{:S(2)}) %collective-permute-start.13) | collective-permute-done | bytes 262176 | tf_op jit(solution)/shard_map/ppermute | solution.py:458
  93.5 1.0 x_second_kernel.1
  94.4 1.5 %collective-permute-start.14 = (bf16[2,256,512]{2,1,0:T(8,128)(2,1)}, bf16[2,256,512]{2,1,0:T(8,128)(2,1)}, u32[]{:S(2)}, u32[]{:S(2)}) collective-permute-start(bf16[2,256,512]{2,1,0:T(8,128)(2,1)} %x_second_kernel.1), channel_id=1, source_target_pairs={{0,2},{2,0},{1,3},{3,1},{4,6},{6,4},{5,7},{7,5},{8,10},{10,8},{9,1... | collective-permute-start | bytes 1572872 | tf_op jit(solution)/shard_map/ppermute | solution.py:559
  95.9 1.1 z_second_kernel.1
  97.1 1.9 %collective-permute-start.16 = (bf16[2,256,384]{2,1,0:T(8,128)(2,1)S(1)}, bf16[2,256,384]{2,1,0:T(8,128)(2,1)S(1)}, u32[]{:S(2)}, u32[]{:S(2)}) collective-permute-start(bf16[2,256,384]{2,1,0:T(8,128)(2,1)S(1)} %z_second_kernel.1), channel_id=1, source_target_pairs={{0,16},{4,20},{8,24},{20,4},{24,8},{28,12},{1,17},{5,21},{9,25},{2... | collective-permute-start | bytes 1179656 | tf_op jit(solution)/shard_map/ppermute | solution.py:458
  99.0 9.6 %collective-permute-done.14 = bf16[2,256,512]{2,1,0:T(8,128)(2,1)} collective-permute-done((bf16[2,256,512]{2,1,0:T(8,128)(2,1)}, bf16[2,256,512]{2,1,0:T(8,128)(2,1)}, u32[]{:S(2)}, u32[]{:S(2)}) %collective-permute-start.14) | collective-permute-done | bytes 524320 | tf_op jit(solution)/shard_map/ppermute | solution.py:559
  108.6 2.0 %fusion.2 = f32[2,256,512]{2,1,0:T(8,128)S(1)} fusion(f32[2,256,512]{2,1,0:T(8,128)} %copy-done.4, bf16[2,256,512]{2,1,0:T(8,128)(2,1)} %collective-permute-done.14, f32[2,256,2048]{2,1,0:T(8,128)} %spectrum.1, s32[]{:T(128)S(6)} %select_n.3, bf16[2,2,256,512]{3,2,1,0:T(8,128)(2,1)S(1)} %collective-permute-done.11.got_this, ...), kind=kLoop, calls=%fused_computation.3 | loop fusion | flops 1835008 | bytes 4325380 | tf_op jit(solution)/shard_map/add | solution.py:567
  110.6 2.3 %collective-permute-done.16 = bf16[2,256,384]{2,1,0:T(8,128)(2,1)S(1)} collective-permute-done((bf16[2,256,384]{2,1,0:T(8,128)(2,1)S(1)}, bf16[2,256,384]{2,1,0:T(8,128)(2,1)S(1)}, u32[]{:S(2)}, u32[]{:S(2)}) %collective-permute-start.16) | collective-permute-done | bytes 393248 | tf_op jit(solution)/shard_map/ppermute | solution.py:458
  112.9 1.1 convert_add_fusion.1
  (13 shorter events, 0.1 us)
Async XLA Ops:
  0.0 4.6 %copy-start = (bf16[8,1024,256]{2,1,0:T(8,128)(2,1)S(1)}, bf16[8,1024,256]{2,1,0:T(8,128)(2,1)}, u32[]{:S(2)}) copy-start(bf16[8,1024,256]{2,1,0:T(8,128)(2,1)} %constant.18.clone.table) | copy-start | bytes 12582916
  0.9 2.4 %copy-start.1 = (f32[2,256,2048]{2,1,0:T(8,128)S(1)}, f32[2,256,2048]{2,1,0:T(8,128)}, u32[]{:S(2)}) copy-start(f32[2,256,2048]{2,1,0:T(8,128)} %spectrum.1) | copy-start | bytes 12582916
  6.5 12.5 %collective-permute-start = (bf16[4,256,128]{2,1,0:T(8,128)(2,1)S(1)}, bf16[4,256,128]{2,1,0:T(8,128)(2,1)S(1)}, u32[]{:S(2)}, u32[]{:S(2)}) collective-permute-start(bf16[4,256,128]{2,1,0:T(8,128)(2,1)S(1)} %get-tuple-element.34), channel_id=1, source_target_pairs={{8,16},{12,20},{16,8},{20,12},{4,0},{24,28},{9,17},{13,21},{17,9},... | collective-permute-start | bytes 786440 | tf_op jit(solution)/shard_map/ppermute | solution.py:458
  7.8 13.7 %collective-permute-start.1 = (bf16[4,256,128]{2,1,0:T(8,128)(2,1)S(1)}, bf16[4,256,128]{2,1,0:T(8,128)(2,1)S(1)}, u32[]{:S(2)}, u32[]{:S(2)}) collective-permute-start(bf16[4,256,128]{2,1,0:T(8,128)(2,1)S(1)} %get-tuple-element.43), channel_id=1, source_target_pairs={{8,20},{12,16},{16,12},{20,8},{4,0},{24,28},{9,21},{13,17},{17,13}... | collective-permute-start | bytes 786440 | tf_op jit(solution)/shard_map/ppermute | solution.py:458
  9.1 32.4 %copy-start.2 = (bf16[8,256,1024]{2,1,0:T(8,128)(2,1)S(1)}, bf16[8,256,1024]{2,1,0:T(8,128)(2,1)}, u32[]{:S(2)}) copy-start(bf16[8,256,1024]{2,1,0:T(8,128)(2,1)} %constant.17.clone.table) | copy-start | bytes 12582916
  9.1 32.4 %copy-start.3 = (f32[2,128,1024]{2,1,0:T(8,128)S(1)}, f32[2,128,1024]{2,1,0:T(8,128)}, u32[]{:S(2)}) copy-start(f32[2,128,1024]{2,1,0:T(8,128)} %images) | copy-start | bytes 3145732
  9.1 19.9 %collective-permute-start.6 = (bf16[4,256,128]{2,1,0:T(8,128)(2,1)S(1)}, bf16[4,256,128]{2,1,0:T(8,128)(2,1)S(1)}, u32[]{:S(2)}, u32[]{:S(2)}) collective-permute-start(bf16[4,256,128]{2,1,0:T(8,128)(2,1)S(1)} %get-tuple-element.48), channel_id=1, source_target_pairs={{4,12},{8,0},{12,4},{16,24},{20,28},{24,16},{5,13},{9,1},{13,5},{1... | collective-permute-start | bytes 786440 | tf_op jit(solution)/shard_map/ppermute | solution.py:458
  19.0 23.0 %collective-permute-start.2 = (bf16[4,256,128]{2,1,0:T(8,128)(2,1)S(1)}, bf16[4,256,128]{2,1,0:T(8,128)(2,1)S(1)}, u32[]{:S(2)}, u32[]{:S(2)}) collective-permute-start(bf16[4,256,128]{2,1,0:T(8,128)(2,1)S(1)} %class_4_blocks.1), channel_id=1, source_target_pairs={{0,16},{4,20},{8,24},{12,28},{16,0},{20,4},{24,8},{28,12},{1,17},{... | collective-permute-start | bytes 786440 | tf_op jit(solution)/shard_map/ppermute | solution.py:458
  20.2 25.3 %collective-permute-start.4 = (bf16[4,256,128]{2,1,0:T(8,128)(2,1)S(1)}, bf16[4,256,128]{2,1,0:T(8,128)(2,1)S(1)}, u32[]{:S(2)}, u32[]{:S(2)}) collective-permute-start(bf16[4,256,128]{2,1,0:T(8,128)(2,1)S(1)} %get-tuple-element.45.own), channel_id=1, source_target_pairs={{8,28},{12,24},{16,4},{20,0},{9,29},{13,25},{17,5},{21,1},{10,30},... | collective-permute-start | bytes 786440 | tf_op jit(solution)/shard_map/ppermute | solution.py:458
  21.6 20.5 %collective-permute-start.3 = (bf16[4,256,128]{2,1,0:T(8,128)(2,1)S(1)}, bf16[4,256,128]{2,1,0:T(8,128)(2,1)S(1)}, u32[]{:S(2)}, u32[]{:S(2)}) collective-permute-start(bf16[4,256,128]{2,1,0:T(8,128)(2,1)S(1)} %class_6_blocks.1), channel_id=1, source_target_pairs={{0,24},{4,28},{24,0},{28,4},{1,25},{5,29},{25,1},{29,5},{2,26},{6,... | collective-permute-start | bytes 786440 | tf_op jit(solution)/shard_map/ppermute | solution.py:458
  27.6 18.0 %collective-permute-start.5 = (bf16[4,256,128]{2,1,0:T(8,128)(2,1)S(1)}, bf16[4,256,128]{2,1,0:T(8,128)(2,1)S(1)}, u32[]{:S(2)}, u32[]{:S(2)}) collective-permute-start(bf16[4,256,128]{2,1,0:T(8,128)(2,1)S(1)} %get-tuple-element.47), channel_id=1, source_target_pairs={{4,0},{8,12},{12,8},{16,20},{20,16},{24,28},{5,1},{9,13},{13,9},{1... | collective-permute-start | bytes 786440 | tf_op jit(solution)/shard_map/ppermute | solution.py:458
  29.0 22.0 %collective-permute-start.7 = (bf16[4,256,128]{2,1,0:T(8,128)(2,1)S(1)}, bf16[4,256,128]{2,1,0:T(8,128)(2,1)S(1)}, u32[]{:S(2)}, u32[]{:S(2)}) collective-permute-start(bf16[4,256,128]{2,1,0:T(8,128)(2,1)S(1)} %get-tuple-element.49), channel_id=1, source_target_pairs={{4,8},{8,4},{12,0},{16,28},{20,24},{24,20},{5,9},{9,5},{13,1},{17,... | collective-permute-start | bytes 786440 | tf_op jit(solution)/shard_map/ppermute | solution.py:458
  56.4 10.2 %collective-permute-start.10 = (bf16[4,256,128]{2,1,0:T(8,128)(2,1)S(1)}, bf16[4,256,128]{2,1,0:T(8,128)(2,1)S(1)}, u32[]{:S(2)}, u32[]{:S(2)}) collective-permute-start(bf16[4,256,128]{2,1,0:T(8,128)(2,1)S(1)} %get-tuple-element.53), channel_id=1, source_target_pairs={{0,12},{4,8},{8,4},{12,0},{16,28},{20,24},{24,20},{28,16},{1,13},{... | collective-permute-start | bytes 786440 | tf_op jit(solution)/shard_map/ppermute | solution.py:458
  56.6 13.8 %collective-permute-start.8 = (bf16[4,256,128]{2,1,0:T(8,128)(2,1)S(1)}, bf16[4,256,128]{2,1,0:T(8,128)(2,1)S(1)}, u32[]{:S(2)}, u32[]{:S(2)}) collective-permute-start(bf16[4,256,128]{2,1,0:T(8,128)(2,1)S(1)} %get-tuple-element.51), channel_id=1, source_target_pairs={{0,4},{4,0},{8,12},{12,8},{16,20},{20,16},{24,28},{28,24},{1,5},{5... | collective-permute-start | bytes 786440 | tf_op jit(solution)/shard_map/ppermute | solution.py:458
  58.1 13.2 %collective-permute-start.9 = (bf16[4,256,128]{2,1,0:T(8,128)(2,1)S(1)}, bf16[4,256,128]{2,1,0:T(8,128)(2,1)S(1)}, u32[]{:S(2)}, u32[]{:S(2)}) collective-permute-start(bf16[4,256,128]{2,1,0:T(8,128)(2,1)S(1)} %get-tuple-element.52), channel_id=1, source_target_pairs={{0,8},{4,12},{8,0},{12,4},{16,24},{20,28},{24,16},{28,20},{1,9},{5... | collective-permute-start | bytes 786440 | tf_op jit(solution)/shard_map/ppermute | solution.py:458
  73.9 3.0 %collective-permute-start.12 = (bf16[2,2,256,512]{3,2,1,0:T(8,128)(2,1)S(1)}, bf16[2,2,256,512]{3,2,1,0:T(8,128)(2,1)S(1)}, u32[]{:S(2)}, u32[]{:S(2)}) collective-permute-start(bf16[2,2,256,512]{3,2,1,0:T(8,128)(2,1)S(1)} %get-tuple-element.60), channel_id=1, source_target_pairs={{0,1},{1,0},{2,3},{3,2},{4,5},{5,4},{6,7},{7,6},{8,9},{9,8},{10,11... | collective-permute-start | bytes 3145736 | tf_op jit(solution)/shard_map/ppermute | solution.py:535
  74.0 7.3 %collective-permute-start.11 = (bf16[2,2,256,512]{3,2,1,0:T(8,128)(2,1)S(1)}, bf16[2,2,256,512]{3,2,1,0:T(8,128)(2,1)S(1)}, u32[]{:S(2)}, u32[]{:S(2)}) collective-permute-start(bf16[2,2,256,512]{3,2,1,0:T(8,128)(2,1)S(1)} %get-tuple-element.56), channel_id=1, source_target_pairs={{0,1},{1,0},{2,3},{3,2},{4,5},{5,4},{6,7},{7,6},{8,9},{9,8},{10,11... | collective-permute-start | bytes 3145736 | tf_op jit(solution)/shard_map/ppermute | solution.py:536
  77.0 4.4 %copy-start.4 = (f32[2,256,512]{2,1,0:T(8,128)}, f32[2,256,512]{2,1,0:T(8,128)S(1)}, u32[]{:S(2)}) copy-start(f32[2,256,512]{2,1,0:T(8,128)S(1)} %get-tuple-element.55) | copy-start | bytes 3145732
  77.1 16.4 %collective-permute-start.13 = (bf16[2,2,256,128]{3,2,1,0:T(8,128)(2,1)S(1)}, bf16[2,2,256,128]{3,2,1,0:T(8,128)(2,1)S(1)}, u32[]{:S(2)}, u32[]{:S(2)}) collective-permute-start(bf16[2,2,256,128]{3,2,1,0:T(8,128)(2,1)S(1)} %z_first_kernel.1), channel_id=1, source_target_pairs={{0,16},{4,20},{8,24},{20,4},{24,8},{28,12},{1,17},{5,21},{9,25},{2... | collective-permute-start | bytes 786440 | tf_op jit(solution)/shard_map/ppermute | solution.py:458
  79.9 16.1 %collective-permute-start.15 = (bf16[2,256,384]{2,1,0:T(8,128)(2,1)}, bf16[2,256,384]{2,1,0:T(8,128)(2,1)}, u32[]{:S(2)}, u32[]{:S(2)}) collective-permute-start(bf16[2,256,384]{2,1,0:T(8,128)(2,1)} %x_first_kernel.1), channel_id=1, source_target_pairs={{0,2},{2,0},{1,3},{3,1},{4,6},{6,4},{5,7},{7,5},{8,10},{10,8},{9,1... | collective-permute-start | bytes 1179656 | tf_op jit(solution)/shard_map/ppermute | solution.py:555
  94.4 14.2 %collective-permute-start.14 = (bf16[2,256,512]{2,1,0:T(8,128)(2,1)}, bf16[2,256,512]{2,1,0:T(8,128)(2,1)}, u32[]{:S(2)}, u32[]{:S(2)}) collective-permute-start(bf16[2,256,512]{2,1,0:T(8,128)(2,1)} %x_second_kernel.1), channel_id=1, source_target_pairs={{0,2},{2,0},{1,3},{3,1},{4,6},{6,4},{5,7},{7,5},{8,10},{10,8},{9,1... | collective-permute-start | bytes 1572872 | tf_op jit(solution)/shard_map/ppermute | solution.py:559
  97.1 15.8 %collective-permute-start.16 = (bf16[2,256,384]{2,1,0:T(8,128)(2,1)S(1)}, bf16[2,256,384]{2,1,0:T(8,128)(2,1)S(1)}, u32[]{:S(2)}, u32[]{:S(2)}) collective-permute-start(bf16[2,256,384]{2,1,0:T(8,128)(2,1)S(1)} %z_second_kernel.1), channel_id=1, source_target_pairs={{0,16},{4,20},{8,24},{20,4},{24,8},{28,12},{1,17},{5,21},{9,25},{2... | collective-permute-start | bytes 1179656 | tf_op jit(solution)/shard_map/ppermute | solution.py:458

commit v12 on v11

--- a/solution.py
+++ b/solution.py
@@ -468,10 +468,13 @@
     got_b = permute(first_b, [(s, s ^ 7) for s in INNER] + handed)
     near_2 = permute(near_2, [(s, s ^ 2) for s in windowed])
     second_a, second_b, near_0, near_1, near_3 = rows_call(slice(3, SLABS), "rows_round_2")
-    got_a, second_a, second_b, near_1, near_3, images = lax.optimization_barrier(
-        (got_a, second_a, second_b, near_1, near_3, images)
+    got_a, near_2, second_a, second_b, near_1, near_3, images = lax.optimization_barrier(
+        (got_a, near_2, second_a, second_b, near_1, near_3, images)
     )
     outer_pairs = [(s, s ^ 6) for s in range(SLABS) if s not in INNER]
+    near_1 = permute(near_1, [(s, s ^ 1) for s in windowed])
+    near_3 = permute(near_3, [(s, s ^ 3) for s in windowed])
+    near_1, got_b = lax.optimization_barrier((near_1, got_b))
     far_columns = [
         got_a,
         got_b,
@@ -479,8 +482,6 @@
         permute(choose(got_b, second_b, "class_6_blocks"), outer_pairs),
         permute(second_b, [(s, s ^ 5) for s in INNER]),
     ]
-    near_1 = permute(near_1, [(s, s ^ 1) for s in windowed])
-    near_3 = permute(near_3, [(s, s ^ 3) for s in windowed])
     near_columns = [near_0, near_1, near_2, near_3]
     amplitude, by_row = local_call(
         amplitude_kernel,
@@ -563,8 +564,9 @@
         return jnp.pad(value.astype(jnp.float32), ((0, 0), (0, 0), (before, after)))
 
     base = lax.dynamic_slice_in_dim(spectrum, led_at * share, share, 2)
-    base += this_near + got_this[0].astype(jnp.float32) + got_x.astype(jnp.float32)
-    base += widen(got_z_first[0], 0)
+    base += this_near + got_this[0].astype(jnp.float32) + widen(got_z_first[0], 0)
+    base, got_x = lax.optimization_barrier((base, got_x))
+    base += got_x.astype(jnp.float32)
     base, got_z_second = lax.optimization_barrier((base, got_z_second))
     return base + widen(got_z_second, first)
 

time: 115 us -> 113 us (0.983)
  starting transfers between devices: 42.9 us -> 34.4 us
  waiting for transfers between devices: 44.4 us -> 50.6 us
    ppermute x13, starting transfers between devices: 39.3 us -> 30.8 us  [permute(): return lax.ppermute(sent, 'slab', pairs)]
    ppermute x13, waiting for transfers between devices: 34.8 us -> 42.9 us  [permute(): return lax.ppermute(sent, 'slab', pairs)]
    ppermute x2, waiting for transfers between devices: 9.61 us -> 7.77 us  [body_slabs(): got_x = lax.ppermute(over, 'led', planes)]
    add x1 -> x2, other arithmetic: 2.02 us -> 3.04 us  [the longest x1 1.82 us: body_slabs(): base += this_near + got_this[0].astype(jnp.float32) + widen(got_z_first[0...]
  transfers between devices with their start and end apart: 17 -> 17, of which waited for: 8 -> 10; matrix products, arithmetic and copies ran while one was open for 2% -> 3% of each run, Pallas kernels for 8% -> 8%
where the time goes in v12:
time: 113 us
  waiting for transfers between devices  50.6 us (45%)
  starting transfers between devices  34.4 us (30%)
  Pallas kernels  20.1 us (18%)
  other arithmetic  5.06 us (4%)
  local copies, waits for them, and re-layouts  2.42 us (2%)
    ppermute x13, waiting for transfers between devices, permute(): return lax.ppermute(sent, 'slab', pairs)  42.9 us
    ppermute x13, starting transfers between devices, permute(): return lax.ppermute(sent, 'slab', pairs)  30.8 us
    ppermute x2, waiting for transfers between devices, body_slabs(): got_x = lax.ppermute(over, 'led', planes)  7.77 us
    pallas_call x1, Pallas kernels, body_slabs(): local_call(field_kernel, [sent_block] * HALF, [vmem] * 11, [pltpu.VMEM((w...  5.31 us
    pallas_call x2, Pallas kernels, rows_call(): local_call(functools.partial(rows_kernel, which), [sent_block] * count, [...  4.69 us
    ppermute x2, starting transfers between devices, body_slabs(): got_x = lax.ppermute(over, 'led', planes)  3 us
    pallas_call x4, Pallas kernels, sum_call(): local_call(kernel, out_shape, specs, [], 0, 2 ** 20, kernel.__name__)  3 us
    pallas_call x1, Pallas kernels, body_slabs(): local_call(sent_kernel, [jax.ShapeDtypeStruct((2,) + piece, bf16), jax.Sh...  2.64 us
  transfers between devices with their start and end apart: 17, of which 10 were waited for; matrix products, arithmetic and copies ran while one was open for 3% of the time, Pallas kernels for 8%

profile of v12, /device:TPU:4, one launch (start us, length us, event | category | flops | bytes accessed | tf_op | source)
XLA Modules:
  0.0 112.9 jit_solution(14279967152890562007)
XLA Ops:
  0.0 0.9 pad_add_fusion.starts
  0.9 2.4 %copy-done.1 = f32[2,256,2048]{2,1,0:T(8,128)S(1)} copy-done((f32[2,256,2048]{2,1,0:T(8,128)S(1)}, f32[2,256,2048]{2,1,0:T(8,128)}, u32[]{:S(2)}) %copy-start.1) | copy-done | bytes 4194328
  3.3 1.4 %windows.1.window = bf16[1024,1024]{1,0:T(8,128)(2,1)S(1)} custom-call(s32[4]{0:T(128)S(1)} %pad_add_fusion.starts, f32[2,256,2048]{2,1,0:T(8,128)S(1)} %copy-done.1), custom_call_target="tpu_custom_call" | custom-call | bytes 6291456 | tf_op jit(solution)/shard_map/windows/pallas_call | solution.py:433
  4.7 1.8 %rows_round_1.1 = (bf16[4,256,128]{2,1,0:T(8,128)(2,1)S(1)}, bf16[4,256,128]{2,1,0:T(8,128)(2,1)S(1)}, bf16[4,256,128]{2,1,0:T(8,128)(2,1)S(1)}) custom-call(bf16[1024,1024]{1,0:T(8,128)(2,1)S(1)} %windows.1.window, bf16[8,1024,256]{2,1,0:T(8,128)(2,1)S(1)} %copy-done), custom_call_target="tpu_custom_call" | custom-call | flops 1610612736 | bytes 5242880 | tf_op jit(solution)/shard_map/rows_round_1/pallas_call | solution.py:445
  6.5 1.3 %collective-permute-start = (bf16[4,256,128]{2,1,0:T(8,128)(2,1)S(1)}, bf16[4,256,128]{2,1,0:T(8,128)(2,1)S(1)}, u32[]{:S(2)}, u32[]{:S(2)}) collective-permute-start(bf16[4,256,128]{2,1,0:T(8,128)(2,1)S(1)} %get-tuple-element.39), channel_id=1, source_target_pairs={{8,16},{12,20},{16,8},{20,12},{4,0},{24,28},{9,17},{13,21},{17,9},... | collective-permute-start | bytes 786440 | tf_op jit(solution)/shard_map/ppermute | solution.py:458
  7.8 5.7 %collective-permute-start.1 = (bf16[4,256,128]{2,1,0:T(8,128)(2,1)S(1)}, bf16[4,256,128]{2,1,0:T(8,128)(2,1)S(1)}, u32[]{:S(2)}, u32[]{:S(2)}) collective-permute-start(bf16[4,256,128]{2,1,0:T(8,128)(2,1)S(1)} %get-tuple-element.40), channel_id=1, source_target_pairs={{4,12},{8,0},{12,4},{16,24},{20,28},{24,16},{5,13},{9,1},{13,5},{1... | collective-permute-start | bytes 786440 | tf_op jit(solution)/shard_map/ppermute | solution.py:458
  13.5 0.0 copy-start.2
  13.5 0.0 copy-start.3
  13.5 1.6 %collective-permute-start.3 = (bf16[4,256,128]{2,1,0:T(8,128)(2,1)S(1)}, bf16[4,256,128]{2,1,0:T(8,128)(2,1)S(1)}, u32[]{:S(2)}, u32[]{:S(2)}) collective-permute-start(bf16[4,256,128]{2,1,0:T(8,128)(2,1)S(1)} %get-tuple-element.50), channel_id=1, source_target_pairs={{8,20},{12,16},{16,12},{20,8},{4,0},{24,28},{9,21},{13,17},{17,13}... | collective-permute-start | bytes 786440 | tf_op jit(solution)/shard_map/ppermute | solution.py:458
  15.1 2.9 %rows_round_2.1 = (bf16[4,256,128]{2,1,0:T(8,128)(2,1)S(1)}, bf16[4,256,128]{2,1,0:T(8,128)(2,1)S(1)}, bf16[4,256,128]{2,1,0:T(8,128)(2,1)S(1)}, bf16[4,256,128]...) custom-call(bf16[1024,1024]{1,0:T(8,128)(2,1)S(1)} %windows.1.window, bf16[8,1024,256]{2,1,0:T(8,128)(2,1)S(1)} %copy-done), custom_call_target="tpu_custom_call" | custom-call | flops 2684354560 | bytes 5242880 | tf_op jit(solution)/shard_map/rows_round_2/pallas_call | solution.py:445
  18.0 1.5 %collective-permute-done.1.rest_7_ = bf16[4,256,128]{2,1,0:T(8,128)(2,1)S(1)} collective-permute-done((bf16[4,256,128]{2,1,0:T(8,128)(2,1)S(1)}, bf16[4,256,128]{2,1,0:T(8,128)(2,1)S(1)}, u32[]{:S(2)}, u32[]{:S(2)}) %collective-permute-start.1) | collective-permute-done | bytes 262176 | tf_op jit(solution)/shard_map/ppermute | solution.py:458
  19.5 1.8 %collective-permute-start.2 = (bf16[4,256,128]{2,1,0:T(8,128)(2,1)S(1)}, bf16[4,256,128]{2,1,0:T(8,128)(2,1)S(1)}, u32[]{:S(2)}, u32[]{:S(2)}) collective-permute-start(bf16[4,256,128]{2,1,0:T(8,128)(2,1)S(1)} %get-tuple-element.49), channel_id=1, source_target_pairs={{4,0},{8,12},{12,8},{16,20},{20,16},{24,28},{5,1},{9,13},{13,9},{1... | collective-permute-start | bytes 786440 | tf_op jit(solution)/shard_map/ppermute | solution.py:458
  21.3 3.2 %collective-permute-start.4 = (bf16[4,256,128]{2,1,0:T(8,128)(2,1)S(1)}, bf16[4,256,128]{2,1,0:T(8,128)(2,1)S(1)}, u32[]{:S(2)}, u32[]{:S(2)}) collective-permute-start(bf16[4,256,128]{2,1,0:T(8,128)(2,1)S(1)} %class_4_blocks.1), channel_id=1, source_target_pairs={{0,16},{4,20},{8,24},{12,28},{16,0},{20,4},{24,8},{28,12},{1,17},{... | collective-permute-start | bytes 786440 | tf_op jit(solution)/shard_map/ppermute | solution.py:458
  24.5 1.3 %collective-permute-start.6 = (bf16[4,256,128]{2,1,0:T(8,128)(2,1)S(1)}, bf16[4,256,128]{2,1,0:T(8,128)(2,1)S(1)}, u32[]{:S(2)}, u32[]{:S(2)}) collective-permute-start(bf16[4,256,128]{2,1,0:T(8,128)(2,1)S(1)} %get-tuple-element.53.own), channel_id=1, source_target_pairs={{8,28},{12,24},{16,4},{20,0},{9,29},{13,25},{17,5},{21,1},{10,30},... | collective-permute-start | bytes 786440 | tf_op jit(solution)/shard_map/ppermute | solution.py:458
  25.8 5.5 %collective-permute-start.7 = (bf16[4,256,128]{2,1,0:T(8,128)(2,1)S(1)}, bf16[4,256,128]{2,1,0:T(8,128)(2,1)S(1)}, u32[]{:S(2)}, u32[]{:S(2)}) collective-permute-start(bf16[4,256,128]{2,1,0:T(8,128)(2,1)S(1)} %get-tuple-element.57), channel_id=1, source_target_pairs={{4,8},{8,4},{12,0},{16,28},{20,24},{24,20},{5,9},{9,5},{13,1},{17,... | collective-permute-start | bytes 786440 | tf_op jit(solution)/shard_map/ppermute | solution.py:458
  31.3 0.0 collective-permute-done.2.rest_6_
  31.4 1.9 %collective-permute-start.5 = (bf16[4,256,128]{2,1,0:T(8,128)(2,1)S(1)}, bf16[4,256,128]{2,1,0:T(8,128)(2,1)S(1)}, u32[]{:S(2)}, u32[]{:S(2)}) collective-permute-start(bf16[4,256,128]{2,1,0:T(8,128)(2,1)S(1)} %class_6_blocks.1), channel_id=1, source_target_pairs={{0,24},{4,28},{24,0},{28,4},{1,25},{5,29},{25,1},{29,5},{2,26},{6,... | collective-permute-start | bytes 786440 | tf_op jit(solution)/shard_map/ppermute | solution.py:458
  33.3 0.6 amplitude.1
  33.9 8.8 %collective-permute-done.4.rest_2_ = bf16[4,256,128]{2,1,0:T(8,128)(2,1)S(1)} collective-permute-done((bf16[4,256,128]{2,1,0:T(8,128)(2,1)S(1)}, bf16[4,256,128]{2,1,0:T(8,128)(2,1)S(1)}, u32[]{:S(2)}, u32[]{:S(2)}) %collective-permute-start.4) | collective-permute-done | bytes 262176 | tf_op jit(solution)/shard_map/ppermute | solution.py:458
  42.7 3.9 %collective-permute-done.6.rest_4_ = bf16[4,256,128]{2,1,0:T(8,128)(2,1)S(1)} collective-permute-done((bf16[4,256,128]{2,1,0:T(8,128)(2,1)S(1)}, bf16[4,256,128]{2,1,0:T(8,128)(2,1)S(1)}, u32[]{:S(2)}, u32[]{:S(2)}) %collective-permute-start.6) | collective-permute-done | bytes 262176 | tf_op jit(solution)/shard_map/ppermute | solution.py:458
  46.6 3.6 %collective-permute-done.7.rest_8_ = bf16[4,256,128]{2,1,0:T(8,128)(2,1)S(1)} collective-permute-done((bf16[4,256,128]{2,1,0:T(8,128)(2,1)S(1)}, bf16[4,256,128]{2,1,0:T(8,128)(2,1)S(1)}, u32[]{:S(2)}, u32[]{:S(2)}) %collective-permute-start.7) | collective-permute-done | bytes 262176 | tf_op jit(solution)/shard_map/ppermute | solution.py:458
  50.2 5.3 %modulus_step.1 = (bf16[4,256,128]{2,1,0:T(8,128)(2,1)S(1)}, bf16[4,256,128]{2,1,0:T(8,128)(2,1)S(1)}, bf16[4,256,128]{2,1,0:T(8,128)(2,1)S(1)}, bf16[4,256,128]{2,1,0:T(8,128)(2,1)S(1)}) custom-call(f32[1024,256]{1,0:T(8,128)S(1)} %get-tuple-element.46.amplitude, bf16[8,256,1024]{2,1,0:T(8,128)(2,1)S(1)} %get-tuple-element.47.table, ...), custom_call_target="tpu_custom_call" | custom-call | flops 4294967296 | bytes 12582912 | tf_op jit(solution)/shard_map/modulus_step/pallas_call | solution.py:498
  55.5 0.1 collective-permute-start.10
  55.6 2.4 %collective-permute-start.8 = (bf16[4,256,128]{2,1,0:T(8,128)(2,1)S(1)}, bf16[4,256,128]{2,1,0:T(8,128)(2,1)S(1)}, u32[]{:S(2)}, u32[]{:S(2)}) collective-permute-start(bf16[4,256,128]{2,1,0:T(8,128)(2,1)S(1)} %get-tuple-element.59), channel_id=1, source_target_pairs={{0,4},{4,0},{8,12},{12,8},{16,20},{20,16},{24,28},{28,24},{1,5},{5... | collective-permute-start | bytes 786440 | tf_op jit(solution)/shard_map/ppermute | solution.py:458
  58.0 1.4 %collective-permute-start.9 = (bf16[4,256,128]{2,1,0:T(8,128)(2,1)S(1)}, bf16[4,256,128]{2,1,0:T(8,128)(2,1)S(1)}, u32[]{:S(2)}, u32[]{:S(2)}) collective-permute-start(bf16[4,256,128]{2,1,0:T(8,128)(2,1)S(1)} %get-tuple-element.60), channel_id=1, source_target_pairs={{0,8},{4,12},{8,0},{12,4},{16,24},{20,28},{24,16},{28,20},{1,9},{5... | collective-permute-start | bytes 786440 | tf_op jit(solution)/shard_map/ppermute | solution.py:458
  59.4 6.3 %collective-permute-done.10.rest_3_ = bf16[4,256,128]{2,1,0:T(8,128)(2,1)S(1)} collective-permute-done((bf16[4,256,128]{2,1,0:T(8,128)(2,1)S(1)}, bf16[4,256,128]{2,1,0:T(8,128)(2,1)S(1)}, u32[]{:S(2)}, u32[]{:S(2)}) %collective-permute-start.10) | collective-permute-done | bytes 262176 | tf_op jit(solution)/shard_map/ppermute | solution.py:458
  65.6 2.7 %collective-permute-done.8.rest_1_ = bf16[4,256,128]{2,1,0:T(8,128)(2,1)S(1)} collective-permute-done((bf16[4,256,128]{2,1,0:T(8,128)(2,1)S(1)}, bf16[4,256,128]{2,1,0:T(8,128)(2,1)S(1)}, u32[]{:S(2)}, u32[]{:S(2)}) %collective-permute-start.8) | collective-permute-done | bytes 262176 | tf_op jit(solution)/shard_map/ppermute | solution.py:458
  68.4 1.7 %collective-permute-done.9.rest_2_ = bf16[4,256,128]{2,1,0:T(8,128)(2,1)S(1)} collective-permute-done((bf16[4,256,128]{2,1,0:T(8,128)(2,1)S(1)}, bf16[4,256,128]{2,1,0:T(8,128)(2,1)S(1)}, u32[]{:S(2)}, u32[]{:S(2)}) %collective-permute-start.9) | collective-permute-done | bytes 262176 | tf_op jit(solution)/shard_map/ppermute | solution.py:458
  70.1 2.6 %update_sent.1 = (bf16[2,2,256,512]{3,2,1,0:T(8,128)(2,1)S(1)}, bf16[2,2,256,512]{3,2,1,0:T(8,128)(2,1)S(1)}, bf16[1024,512]{1,0:T(8,128)(2,1)S(1)}) custom-call(s32[4]{0:T(128)S(1)} %pad_add_fusion.starts, bf16[8,1024,256]{2,1,0:T(8,128)(2,1)S(1)} %copy-done, bf16[4,256,128]{2,1,0:T(8,128)(2,1)S(1)} %get-tuple-element.58.rest_0_, ...), custom_call_target="tpu_custom_call" | custom-call | flops 1073741824 | bytes 8388608 | tf_op jit(solution)/shard_map/update_sent/pallas_call | solution.py:523
  72.8 0.1 collective-permute-start.12
  72.8 0.5 collective-permute-start.11
  73.3 2.4 %update_kept.1 = (f32[2,256,512]{2,1,0:T(8,128)S(1)}, f32[2,256,512]{2,1,0:T(8,128)S(1)}, f32[2,256,512]{2,1,0:T(8,128)S(1)}, f32[2,256,512]{2,1,0:T(8,128)S(1)}) custom-call(s32[4]{0:T(128)S(1)} %pad_add_fusion.starts, bf16[8,1024,256]{2,1,0:T(8,128)(2,1)S(1)} %copy-done, bf16[1024,512]{1,0:T(8,128)(2,1)S(1)} %get-tuple-element.62.back), custom_call_target="tpu_custom_call" | custom-call | flops 1073741824 | bytes 10485760 | tf_op jit(solution)/shard_map/update_kept/pallas_call | solution.py:538
  75.8 0.0 copy-start.4
  75.8 0.0 collective-permute-done.12.got_that
  75.8 0.1 z_first_kernel.1
  75.9 2.8 %collective-permute-start.13 = (bf16[2,2,256,128]{3,2,1,0:T(8,128)(2,1)S(1)}, bf16[2,2,256,128]{3,2,1,0:T(8,128)(2,1)S(1)}, u32[]{:S(2)}, u32[]{:S(2)}) collective-permute-start(bf16[2,2,256,128]{3,2,1,0:T(8,128)(2,1)S(1)} %z_first_kernel.1), channel_id=1, source_target_pairs={{0,16},{4,20},{8,24},{20,4},{24,8},{28,12},{1,17},{5,21},{9,25},{2... | collective-permute-start | bytes 786440 | tf_op jit(solution)/shard_map/ppermute | solution.py:458
  78.8 0.8 x_first_kernel.1
  79.6 1.5 %collective-permute-start.15 = (bf16[2,256,384]{2,1,0:T(8,128)(2,1)}, bf16[2,256,384]{2,1,0:T(8,128)(2,1)}, u32[]{:S(2)}, u32[]{:S(2)}) collective-permute-start(bf16[2,256,384]{2,1,0:T(8,128)(2,1)} %x_first_kernel.1), channel_id=1, source_target_pairs={{0,2},{2,0},{1,3},{3,1},{4,6},{6,4},{5,7},{7,5},{8,10},{10,8},{9,1... | collective-permute-start | bytes 1179656 | tf_op jit(solution)/shard_map/ppermute | solution.py:556
  81.1 11.2 %collective-permute-done.13.got_z = bf16[2,2,256,128]{3,2,1,0:T(8,128)(2,1)S(1)} collective-permute-done((bf16[2,2,256,128]{3,2,1,0:T(8,128)(2,1)S(1)}, bf16[2,2,256,128]{3,2,1,0:T(8,128)(2,1)S(1)}, u32[]{:S(2)}, u32[]{:S(2)}) %collective-permute-start.13) | collective-permute-done | bytes 262176 | tf_op jit(solution)/shard_map/ppermute | solution.py:458
  92.3 1.0 x_second_kernel.1
  93.3 1.5 %collective-permute-start.14 = (bf16[2,256,512]{2,1,0:T(8,128)(2,1)}, bf16[2,256,512]{2,1,0:T(8,128)(2,1)}, u32[]{:S(2)}, u32[]{:S(2)}) collective-permute-start(bf16[2,256,512]{2,1,0:T(8,128)(2,1)} %x_second_kernel.1), channel_id=1, source_target_pairs={{0,2},{2,0},{1,3},{3,1},{4,6},{6,4},{5,7},{7,5},{8,10},{10,8},{9,1... | collective-permute-start | bytes 1572872 | tf_op jit(solution)/shard_map/ppermute | solution.py:560
  94.8 1.1 z_second_kernel.1
  95.9 1.9 %collective-permute-start.16 = (bf16[2,256,384]{2,1,0:T(8,128)(2,1)S(1)}, bf16[2,256,384]{2,1,0:T(8,128)(2,1)S(1)}, u32[]{:S(2)}, u32[]{:S(2)}) collective-permute-start(bf16[2,256,384]{2,1,0:T(8,128)(2,1)S(1)} %z_second_kernel.1), channel_id=1, source_target_pairs={{0,16},{4,20},{8,24},{20,4},{24,8},{28,12},{1,17},{5,21},{9,25},{2... | collective-permute-start | bytes 1179656 | tf_op jit(solution)/shard_map/ppermute | solution.py:458
  97.8 1.8 %fusion.1 = f32[2,256,512]{2,1,0:T(8,128)S(1)} fusion(f32[2,256,512]{2,1,0:T(8,128)} %copy-done.4, f32[2,256,2048]{2,1,0:T(8,128)} %spectrum.1, s32[]{:T(128)S(6)} %select_n.3, bf16[2,2,256,512]{3,2,1,0:T(8,128)(2,1)S(1)} %collective-permute-done.11.got_this, bf16[2,256,128]{2,1,0:T(8,128)(2,1)S(1)} %slice_bitcast_fusion.1), kind=kLoop, calls=%fused_computation.2 | loop fusion | flops 1310720 | bytes 3801092 | tf_op jit(solution)/shard_map/add | solution.py:567
  99.7 7.8 %collective-permute-done.14 = bf16[2,256,512]{2,1,0:T(8,128)(2,1)} collective-permute-done((bf16[2,256,512]{2,1,0:T(8,128)(2,1)}, bf16[2,256,512]{2,1,0:T(8,128)(2,1)}, u32[]{:S(2)}, u32[]{:S(2)}) %collective-permute-start.14) | collective-permute-done | bytes 524320 | tf_op jit(solution)/shard_map/ppermute | solution.py:560
  107.4 1.2 %convert_add_fusion.2 = f32[2,256,512]{2,1,0:T(8,128)S(1)} fusion(f32[2,256,512]{2,1,0:T(8,128)S(1)} %fusion.1, bf16[2,256,512]{2,1,0:T(8,128)(2,1)} %collective-permute-done.14), kind=kLoop, calls=%fused_computation.4 | loop fusion | flops 524288 | bytes 2621440 | tf_op jit(solution)/shard_map/add | solution.py:569
  108.7 3.1 %collective-permute-done.16 = bf16[2,256,384]{2,1,0:T(8,128)(2,1)S(1)} collective-permute-done((bf16[2,256,384]{2,1,0:T(8,128)(2,1)S(1)}, bf16[2,256,384]{2,1,0:T(8,128)(2,1)S(1)}, u32[]{:S(2)}, u32[]{:S(2)}) %collective-permute-start.16) | collective-permute-done | bytes 393248 | tf_op jit(solution)/shard_map/ppermute | solution.py:458
  111.7 1.1 convert_add_fusion.1
  (14 shorter events, 0.1 us)
Async XLA Ops:
  0.0 4.6 %copy-start = (bf16[8,1024,256]{2,1,0:T(8,128)(2,1)S(1)}, bf16[8,1024,256]{2,1,0:T(8,128)(2,1)}, u32[]{:S(2)}) copy-start(bf16[8,1024,256]{2,1,0:T(8,128)(2,1)} %constant.18.clone.table) | copy-start | bytes 12582916
  0.9 2.4 %copy-start.1 = (f32[2,256,2048]{2,1,0:T(8,128)S(1)}, f32[2,256,2048]{2,1,0:T(8,128)}, u32[]{:S(2)}) copy-start(f32[2,256,2048]{2,1,0:T(8,128)} %spectrum.1) | copy-start | bytes 12582916
  6.5 11.5 %collective-permute-start = (bf16[4,256,128]{2,1,0:T(8,128)(2,1)S(1)}, bf16[4,256,128]{2,1,0:T(8,128)(2,1)S(1)}, u32[]{:S(2)}, u32[]{:S(2)}) collective-permute-start(bf16[4,256,128]{2,1,0:T(8,128)(2,1)S(1)} %get-tuple-element.39), channel_id=1, source_target_pairs={{8,16},{12,20},{16,8},{20,12},{4,0},{24,28},{9,17},{13,21},{17,9},... | collective-permute-start | bytes 786440 | tf_op jit(solution)/shard_map/ppermute | solution.py:458
  7.8 11.7 %collective-permute-start.1 = (bf16[4,256,128]{2,1,0:T(8,128)(2,1)S(1)}, bf16[4,256,128]{2,1,0:T(8,128)(2,1)S(1)}, u32[]{:S(2)}, u32[]{:S(2)}) collective-permute-start(bf16[4,256,128]{2,1,0:T(8,128)(2,1)S(1)} %get-tuple-element.40), channel_id=1, source_target_pairs={{4,12},{8,0},{12,4},{16,24},{20,28},{24,16},{5,13},{9,1},{13,5},{1... | collective-permute-start | bytes 786440 | tf_op jit(solution)/shard_map/ppermute | solution.py:458
  13.5 19.9 %copy-start.2 = (bf16[8,256,1024]{2,1,0:T(8,128)(2,1)S(1)}, bf16[8,256,1024]{2,1,0:T(8,128)(2,1)}, u32[]{:S(2)}) copy-start(bf16[8,256,1024]{2,1,0:T(8,128)(2,1)} %constant.17.clone.table) | copy-start | bytes 12582916
  13.5 19.9 %copy-start.3 = (f32[2,128,1024]{2,1,0:T(8,128)S(1)}, f32[2,128,1024]{2,1,0:T(8,128)}, u32[]{:S(2)}) copy-start(f32[2,128,1024]{2,1,0:T(8,128)} %images) | copy-start | bytes 3145732
  13.5 17.8 %collective-permute-start.3 = (bf16[4,256,128]{2,1,0:T(8,128)(2,1)S(1)}, bf16[4,256,128]{2,1,0:T(8,128)(2,1)S(1)}, u32[]{:S(2)}, u32[]{:S(2)}) collective-permute-start(bf16[4,256,128]{2,1,0:T(8,128)(2,1)S(1)} %get-tuple-element.50), channel_id=1, source_target_pairs={{8,20},{12,16},{16,12},{20,8},{4,0},{24,28},{9,21},{13,17},{17,13}... | collective-permute-start | bytes 786440 | tf_op jit(solution)/shard_map/ppermute | solution.py:458
  19.5 11.9 %collective-permute-start.2 = (bf16[4,256,128]{2,1,0:T(8,128)(2,1)S(1)}, bf16[4,256,128]{2,1,0:T(8,128)(2,1)S(1)}, u32[]{:S(2)}, u32[]{:S(2)}) collective-permute-start(bf16[4,256,128]{2,1,0:T(8,128)(2,1)S(1)} %get-tuple-element.49), channel_id=1, source_target_pairs={{4,0},{8,12},{12,8},{16,20},{20,16},{24,28},{5,1},{9,13},{13,9},{1... | collective-permute-start | bytes 786440 | tf_op jit(solution)/shard_map/ppermute | solution.py:458
  21.3 21.4 %collective-permute-start.4 = (bf16[4,256,128]{2,1,0:T(8,128)(2,1)S(1)}, bf16[4,256,128]{2,1,0:T(8,128)(2,1)S(1)}, u32[]{:S(2)}, u32[]{:S(2)}) collective-permute-start(bf16[4,256,128]{2,1,0:T(8,128)(2,1)S(1)} %class_4_blocks.1), channel_id=1, source_target_pairs={{0,16},{4,20},{8,24},{12,28},{16,0},{20,4},{24,8},{28,12},{1,17},{... | collective-permute-start | bytes 786440 | tf_op jit(solution)/shard_map/ppermute | solution.py:458
  24.5 22.1 %collective-permute-start.6 = (bf16[4,256,128]{2,1,0:T(8,128)(2,1)S(1)}, bf16[4,256,128]{2,1,0:T(8,128)(2,1)S(1)}, u32[]{:S(2)}, u32[]{:S(2)}) collective-permute-start(bf16[4,256,128]{2,1,0:T(8,128)(2,1)S(1)} %get-tuple-element.53.own), channel_id=1, source_target_pairs={{8,28},{12,24},{16,4},{20,0},{9,29},{13,25},{17,5},{21,1},{10,30},... | collective-permute-start | bytes 786440 | tf_op jit(solution)/shard_map/ppermute | solution.py:458
  25.8 24.4 %collective-permute-start.7 = (bf16[4,256,128]{2,1,0:T(8,128)(2,1)S(1)}, bf16[4,256,128]{2,1,0:T(8,128)(2,1)S(1)}, u32[]{:S(2)}, u32[]{:S(2)}) collective-permute-start(bf16[4,256,128]{2,1,0:T(8,128)(2,1)S(1)} %get-tuple-element.57), channel_id=1, source_target_pairs={{4,8},{8,4},{12,0},{16,28},{20,24},{24,20},{5,9},{9,5},{13,1},{17,... | collective-permute-start | bytes 786440 | tf_op jit(solution)/shard_map/ppermute | solution.py:458
  31.4 18.8 %collective-permute-start.5 = (bf16[4,256,128]{2,1,0:T(8,128)(2,1)S(1)}, bf16[4,256,128]{2,1,0:T(8,128)(2,1)S(1)}, u32[]{:S(2)}, u32[]{:S(2)}) collective-permute-start(bf16[4,256,128]{2,1,0:T(8,128)(2,1)S(1)} %class_6_blocks.1), channel_id=1, source_target_pairs={{0,24},{4,28},{24,0},{28,4},{1,25},{5,29},{25,1},{29,5},{2,26},{6,... | collective-permute-start | bytes 786440 | tf_op jit(solution)/shard_map/ppermute | solution.py:458
  55.5 10.1 %collective-permute-start.10 = (bf16[4,256,128]{2,1,0:T(8,128)(2,1)S(1)}, bf16[4,256,128]{2,1,0:T(8,128)(2,1)S(1)}, u32[]{:S(2)}, u32[]{:S(2)}) collective-permute-start(bf16[4,256,128]{2,1,0:T(8,128)(2,1)S(1)} %get-tuple-element.61), channel_id=1, source_target_pairs={{0,12},{4,8},{8,4},{12,0},{16,28},{20,24},{24,20},{28,16},{1,13},{... | collective-permute-start | bytes 786440 | tf_op jit(solution)/shard_map/ppermute | solution.py:458
  55.6 12.8 %collective-permute-start.8 = (bf16[4,256,128]{2,1,0:T(8,128)(2,1)S(1)}, bf16[4,256,128]{2,1,0:T(8,128)(2,1)S(1)}, u32[]{:S(2)}, u32[]{:S(2)}) collective-permute-start(bf16[4,256,128]{2,1,0:T(8,128)(2,1)S(1)} %get-tuple-element.59), channel_id=1, source_target_pairs={{0,4},{4,0},{8,12},{12,8},{16,20},{20,16},{24,28},{28,24},{1,5},{5... | collective-permute-start | bytes 786440 | tf_op jit(solution)/shard_map/ppermute | solution.py:458
  58.0 12.1 %collective-permute-start.9 = (bf16[4,256,128]{2,1,0:T(8,128)(2,1)S(1)}, bf16[4,256,128]{2,1,0:T(8,128)(2,1)S(1)}, u32[]{:S(2)}, u32[]{:S(2)}) collective-permute-start(bf16[4,256,128]{2,1,0:T(8,128)(2,1)S(1)} %get-tuple-element.60), channel_id=1, source_target_pairs={{0,8},{4,12},{8,0},{12,4},{16,24},{20,28},{24,16},{28,20},{1,9},{5... | collective-permute-start | bytes 786440 | tf_op jit(solution)/shard_map/ppermute | solution.py:458
  72.8 3.0 %collective-permute-start.12 = (bf16[2,2,256,512]{3,2,1,0:T(8,128)(2,1)S(1)}, bf16[2,2,256,512]{3,2,1,0:T(8,128)(2,1)S(1)}, u32[]{:S(2)}, u32[]{:S(2)}) collective-permute-start(bf16[2,2,256,512]{3,2,1,0:T(8,128)(2,1)S(1)} %get-tuple-element.67), channel_id=1, source_target_pairs={{0,1},{1,0},{2,3},{3,2},{4,5},{5,4},{6,7},{7,6},{8,9},{9,8},{10,11... | collective-permute-start | bytes 3145736 | tf_op jit(solution)/shard_map/ppermute | solution.py:536
  72.8 8.2 %collective-permute-start.11 = (bf16[2,2,256,512]{3,2,1,0:T(8,128)(2,1)S(1)}, bf16[2,2,256,512]{3,2,1,0:T(8,128)(2,1)S(1)}, u32[]{:S(2)}, u32[]{:S(2)}) collective-permute-start(bf16[2,2,256,512]{3,2,1,0:T(8,128)(2,1)S(1)} %get-tuple-element.64), channel_id=1, source_target_pairs={{0,1},{1,0},{2,3},{3,2},{4,5},{5,4},{6,7},{7,6},{8,9},{9,8},{10,11... | collective-permute-start | bytes 3145736 | tf_op jit(solution)/shard_map/ppermute | solution.py:537
  75.8 5.3 %copy-start.4 = (f32[2,256,512]{2,1,0:T(8,128)}, f32[2,256,512]{2,1,0:T(8,128)S(1)}, u32[]{:S(2)}) copy-start(f32[2,256,512]{2,1,0:T(8,128)S(1)} %get-tuple-element.63) | copy-start | bytes 3145732
  75.9 16.4 %collective-permute-start.13 = (bf16[2,2,256,128]{3,2,1,0:T(8,128)(2,1)S(1)}, bf16[2,2,256,128]{3,2,1,0:T(8,128)(2,1)S(1)}, u32[]{:S(2)}, u32[]{:S(2)}) collective-permute-start(bf16[2,2,256,128]{3,2,1,0:T(8,128)(2,1)S(1)} %z_first_kernel.1), channel_id=1, source_target_pairs={{0,16},{4,20},{8,24},{20,4},{24,8},{28,12},{1,17},{5,21},{9,25},{2... | collective-permute-start | bytes 786440 | tf_op jit(solution)/shard_map/ppermute | solution.py:458
  79.6 15.2 %collective-permute-start.15 = (bf16[2,256,384]{2,1,0:T(8,128)(2,1)}, bf16[2,256,384]{2,1,0:T(8,128)(2,1)}, u32[]{:S(2)}, u32[]{:S(2)}) collective-permute-start(bf16[2,256,384]{2,1,0:T(8,128)(2,1)} %x_first_kernel.1), channel_id=1, source_target_pairs={{0,2},{2,0},{1,3},{3,1},{4,6},{6,4},{5,7},{7,5},{8,10},{10,8},{9,1... | collective-permute-start | bytes 1179656 | tf_op jit(solution)/shard_map/ppermute | solution.py:556
  93.3 14.2 %collective-permute-start.14 = (bf16[2,256,512]{2,1,0:T(8,128)(2,1)}, bf16[2,256,512]{2,1,0:T(8,128)(2,1)}, u32[]{:S(2)}, u32[]{:S(2)}) collective-permute-start(bf16[2,256,512]{2,1,0:T(8,128)(2,1)} %x_second_kernel.1), channel_id=1, source_target_pairs={{0,2},{2,0},{1,3},{3,1},{4,6},{6,4},{5,7},{7,5},{8,10},{10,8},{9,1... | collective-permute-start | bytes 1572872 | tf_op jit(solution)/shard_map/ppermute | solution.py:560
  95.9 15.8 %collective-permute-start.16 = (bf16[2,256,384]{2,1,0:T(8,128)(2,1)S(1)}, bf16[2,256,384]{2,1,0:T(8,128)(2,1)S(1)}, u32[]{:S(2)}, u32[]{:S(2)}) collective-permute-start(bf16[2,256,384]{2,1,0:T(8,128)(2,1)S(1)} %z_second_kernel.1), channel_id=1, source_target_pairs={{0,16},{4,20},{8,24},{20,4},{24,8},{28,12},{1,17},{5,21},{9,25},{2... | collective-permute-start | bytes 1179656 | tf_op jit(solution)/shard_map/ppermute | solution.py:458

commit v13 on v12

--- a/solution.py
+++ b/solution.py
@@ -389,11 +389,16 @@
     out[...] = (total + got_x[...].astype(jnp.float32)).astype(out.dtype)
 
 
-def x_second_kernel(this_far, got_this, got_z, out):
-    cols = got_z.shape[3]
-    total = this_far[...] + got_this[1].astype(jnp.float32)
-    out[:, :, cols:] = total[:, :, cols:].astype(out.dtype)
-    out[:, :, :cols] = (total[:, :, :cols] + got_z[1].astype(jnp.float32)).astype(out.dtype)
+def x_own_kernel(this_far, got_this, out):
+    cols = this_far.shape[2] - out.shape[2]
+    total = this_far[:, :, cols:] + got_this[1, :, :, cols:].astype(jnp.float32)
+    out[...] = total.astype(out.dtype)
+
+
+def x_last_kernel(this_far, got_this, got_z, out):
+    cols = out.shape[2]
+    total = this_far[:, :, :cols] + got_this[1, :, :, :cols].astype(jnp.float32)
+    out[...] = (total + got_z[1].astype(jnp.float32)).astype(out.dtype)
 
 
 def local_call(kernel, out_shape, spaces, scratch, flops, moved, name):
@@ -554,10 +559,13 @@
     got_z_first = permute(over, across)
     over = sum_call(x_first_kernel, (2, rows, share - first), that_far, got_that)
     got_x = lax.ppermute(over, "led", planes)
-    over = sum_call(z_second_kernel, (2, rows, share - first), that_near, got_that, got_x)
-    got_z_second = permute(over, across)
-    over = sum_call(x_second_kernel, piece, this_far, got_this, got_z_first)
-    got_x = lax.ppermute(over, "led", planes)
+    over_z = sum_call(z_second_kernel, (2, rows, share - first), that_near, got_that, got_x)
+    got_z_second = permute(over_z, across)
+    over = sum_call(x_own_kernel, (2, rows, share - first), this_far, got_this)
+    got_x_own = lax.ppermute(over, "led", planes)
+    over, got_z_first = lax.optimization_barrier((over_z, got_z_first))
+    over = sum_call(x_last_kernel, (2, rows, first), this_far, got_this, got_z_first)
+    got_x_last = lax.ppermute(over, "led", planes)
 
     def widen(value, before):
         after = share - before - value.shape[2]
@@ -565,8 +573,8 @@
 
     base = lax.dynamic_slice_in_dim(spectrum, led_at * share, share, 2)
     base += this_near + got_this[0].astype(jnp.float32) + widen(got_z_first[0], 0)
-    base, got_x = lax.optimization_barrier((base, got_x))
-    base += got_x.astype(jnp.float32)
+    base, got_x_own, got_x_last = lax.optimization_barrier((base, got_x_own, got_x_last))
+    base += widen(got_x_own, first) + widen(got_x_last, 0)
     base, got_z_second = lax.optimization_barrier((base, got_z_second))
     return base + widen(got_z_second, first)
 

time: 113 us -> 116 us (1.027)
  waiting for transfers between devices: 50.6 us -> 52.2 us
  other arithmetic: 5.06 us -> 3.67 us
  local copies, waits for them, and re-layouts: 2.42 us -> 3.65 us
    ppermute x0 -> x2, waiting for transfers between devices: none -> 3.78 us  [the longest x1 3.78 us: body_slabs(): got_x_last = lax.ppermute(over, 'led', planes)]
    ppermute x13, waiting for transfers between devices: 42.9 us -> 40.8 us  [permute(): return lax.ppermute(sent, 'slab', pairs)]
    ppermute x2 -> x1, starting transfers between devices: 3 us -> 1.49 us  [body_slabs(): got_x = lax.ppermute(over, 'led', planes)]
    ppermute x2 -> x1, waiting for transfers between devices: 7.77 us -> 6.42 us  [body_slabs(): got_x = lax.ppermute(over, 'led', planes)]
    unnamed x10 -> x16, local copies, waits for them, and re-layouts: 2.41 us -> 3.64 us
    pallas_call x4 -> x5, Pallas kernels: 3 us -> 2.93 us  [sum_call(): local_call(kernel, out_shape, specs, [], 0, 2 ** 20, kernel.__name__)]
  transfers between devices with their start and end apart: 17 -> 18, of which waited for: 10 -> 12; matrix products, arithmetic and copies ran while one was open for 3% -> 1% of each run, Pallas kernels for 8% -> 8%
where the time goes in v13:
time: 116 us; the launch traced here: 115 us
  waiting for transfers between devices  52.2 us (45%)
  starting transfers between devices  34.4 us (30%)
  Pallas kernels  20.9 us (18%)
  other arithmetic  3.67 us (3%)
  local copies, waits for them, and re-layouts  3.65 us (3%)
    ppermute x13, waiting for transfers between devices, permute(): return lax.ppermute(sent, 'slab', pairs)  40.8 us
    ppermute x13, starting transfers between devices, permute(): return lax.ppermute(sent, 'slab', pairs)  31.7 us
    ppermute x1, waiting for transfers between devices, body_slabs(): got_x = lax.ppermute(over, 'led', planes)  6.42 us
    pallas_call x1, Pallas kernels, body_slabs(): local_call(field_kernel, [sent_block] * HALF, [vmem] * 11, [pltpu.VMEM((w...  5.31 us
    pallas_call x2, Pallas kernels, rows_call(): local_call(functools.partial(rows_kernel, which), [sent_block] * count, [...  4.69 us
    ppermute x1, waiting for transfers between devices, body_slabs(): got_x_last = lax.ppermute(over, 'led', planes)  3.78 us
    unnamed x16, local copies, waits for them, and re-layouts  3.64 us
    pallas_call x1, Pallas kernels, body_slabs(): local_call(sent_kernel, [jax.ShapeDtypeStruct((2,) + piece, bf16), jax.Sh...  3.59 us
  transfers between devices with their start and end apart: 18, of which 12 were waited for; matrix products, arithmetic and copies ran while one was open for 1% of the time, Pallas kernels for 8%

profile of v13, /device:TPU:4, one launch (start us, length us, event | category | flops | bytes accessed | tf_op | source)
XLA Modules:
  0.0 115.2 jit_solution(9605946351919629685)
XLA Ops:
  0.0 0.9 pad_add_fusion.starts
  0.9 2.4 %copy-done.1 = f32[2,256,2048]{2,1,0:T(8,128)S(1)} copy-done((f32[2,256,2048]{2,1,0:T(8,128)S(1)}, f32[2,256,2048]{2,1,0:T(8,128)}, u32[]{:S(2)}) %copy-start.1) | copy-done | bytes 4194328
  3.3 1.4 %windows.1.window = bf16[1024,1024]{1,0:T(8,128)(2,1)S(1)} custom-call(s32[4]{0:T(128)S(1)} %pad_add_fusion.starts, f32[2,256,2048]{2,1,0:T(8,128)S(1)} %copy-done.1), custom_call_target="tpu_custom_call" | custom-call | bytes 6291456 | tf_op jit(solution)/shard_map/windows/pallas_call | solution.py:438
  4.7 1.8 %rows_round_1.1 = (bf16[4,256,128]{2,1,0:T(8,128)(2,1)S(1)}, bf16[4,256,128]{2,1,0:T(8,128)(2,1)S(1)}, bf16[4,256,128]{2,1,0:T(8,128)(2,1)S(1)}) custom-call(bf16[1024,1024]{1,0:T(8,128)(2,1)S(1)} %windows.1.window, bf16[8,1024,256]{2,1,0:T(8,128)(2,1)S(1)} %copy-done), custom_call_target="tpu_custom_call" | custom-call | flops 1610612736 | bytes 5242880 | tf_op jit(solution)/shard_map/rows_round_1/pallas_call | solution.py:450
  6.5 1.3 %collective-permute-start = (bf16[4,256,128]{2,1,0:T(8,128)(2,1)S(1)}, bf16[4,256,128]{2,1,0:T(8,128)(2,1)S(1)}, u32[]{:S(2)}, u32[]{:S(2)}) collective-permute-start(bf16[4,256,128]{2,1,0:T(8,128)(2,1)S(1)} %get-tuple-element.41), channel_id=1, source_target_pairs={{8,16},{12,20},{16,8},{20,12},{4,0},{24,28},{9,17},{13,21},{17,9},... | collective-permute-start | bytes 786440 | tf_op jit(solution)/shard_map/ppermute | solution.py:463
  7.8 5.7 %collective-permute-start.1 = (bf16[4,256,128]{2,1,0:T(8,128)(2,1)S(1)}, bf16[4,256,128]{2,1,0:T(8,128)(2,1)S(1)}, u32[]{:S(2)}, u32[]{:S(2)}) collective-permute-start(bf16[4,256,128]{2,1,0:T(8,128)(2,1)S(1)} %get-tuple-element.42), channel_id=1, source_target_pairs={{4,12},{8,0},{12,4},{16,24},{20,28},{24,16},{5,13},{9,1},{13,5},{1... | collective-permute-start | bytes 786440 | tf_op jit(solution)/shard_map/ppermute | solution.py:463
  13.5 0.0 copy-start.2
  13.5 1.6 %collective-permute-start.3 = (bf16[4,256,128]{2,1,0:T(8,128)(2,1)S(1)}, bf16[4,256,128]{2,1,0:T(8,128)(2,1)S(1)}, u32[]{:S(2)}, u32[]{:S(2)}) collective-permute-start(bf16[4,256,128]{2,1,0:T(8,128)(2,1)S(1)} %get-tuple-element.52), channel_id=1, source_target_pairs={{8,20},{12,16},{16,12},{20,8},{4,0},{24,28},{9,21},{13,17},{17,13}... | collective-permute-start | bytes 786440 | tf_op jit(solution)/shard_map/ppermute | solution.py:463
  15.1 2.9 %rows_round_2.1 = (bf16[4,256,128]{2,1,0:T(8,128)(2,1)S(1)}, bf16[4,256,128]{2,1,0:T(8,128)(2,1)S(1)}, bf16[4,256,128]{2,1,0:T(8,128)(2,1)S(1)}, bf16[4,256,128]...) custom-call(bf16[1024,1024]{1,0:T(8,128)(2,1)S(1)} %windows.1.window, bf16[8,1024,256]{2,1,0:T(8,128)(2,1)S(1)} %copy-done), custom_call_target="tpu_custom_call" | custom-call | flops 2684354560 | bytes 5242880 | tf_op jit(solution)/shard_map/rows_round_2/pallas_call | solution.py:450
  18.0 1.5 %collective-permute-done.1.rest_7_ = bf16[4,256,128]{2,1,0:T(8,128)(2,1)S(1)} collective-permute-done((bf16[4,256,128]{2,1,0:T(8,128)(2,1)S(1)}, bf16[4,256,128]{2,1,0:T(8,128)(2,1)S(1)}, u32[]{:S(2)}, u32[]{:S(2)}) %collective-permute-start.1) | collective-permute-done | bytes 262176 | tf_op jit(solution)/shard_map/ppermute | solution.py:463
  19.5 1.8 %collective-permute-start.2 = (bf16[4,256,128]{2,1,0:T(8,128)(2,1)S(1)}, bf16[4,256,128]{2,1,0:T(8,128)(2,1)S(1)}, u32[]{:S(2)}, u32[]{:S(2)}) collective-permute-start(bf16[4,256,128]{2,1,0:T(8,128)(2,1)S(1)} %get-tuple-element.51), channel_id=1, source_target_pairs={{4,0},{8,12},{12,8},{16,20},{20,16},{24,28},{5,1},{9,13},{13,9},{1... | collective-permute-start | bytes 786440 | tf_op jit(solution)/shard_map/ppermute | solution.py:463
  21.3 3.2 %collective-permute-start.4 = (bf16[4,256,128]{2,1,0:T(8,128)(2,1)S(1)}, bf16[4,256,128]{2,1,0:T(8,128)(2,1)S(1)}, u32[]{:S(2)}, u32[]{:S(2)}) collective-permute-start(bf16[4,256,128]{2,1,0:T(8,128)(2,1)S(1)} %class_4_blocks.1), channel_id=1, source_target_pairs={{0,16},{4,20},{8,24},{12,28},{16,0},{20,4},{24,8},{28,12},{1,17},{... | collective-permute-start | bytes 786440 | tf_op jit(solution)/shard_map/ppermute | solution.py:463
  24.5 1.3 %collective-permute-start.6 = (bf16[4,256,128]{2,1,0:T(8,128)(2,1)S(1)}, bf16[4,256,128]{2,1,0:T(8,128)(2,1)S(1)}, u32[]{:S(2)}, u32[]{:S(2)}) collective-permute-start(bf16[4,256,128]{2,1,0:T(8,128)(2,1)S(1)} %get-tuple-element.55.own), channel_id=1, source_target_pairs={{8,28},{12,24},{16,4},{20,0},{9,29},{13,25},{17,5},{21,1},{10,30},... | collective-permute-start | bytes 786440 | tf_op jit(solution)/shard_map/ppermute | solution.py:463
  25.8 5.5 %collective-permute-start.7 = (bf16[4,256,128]{2,1,0:T(8,128)(2,1)S(1)}, bf16[4,256,128]{2,1,0:T(8,128)(2,1)S(1)}, u32[]{:S(2)}, u32[]{:S(2)}) collective-permute-start(bf16[4,256,128]{2,1,0:T(8,128)(2,1)S(1)} %get-tuple-element.59), channel_id=1, source_target_pairs={{4,8},{8,4},{12,0},{16,28},{20,24},{24,20},{5,9},{9,5},{13,1},{17,... | collective-permute-start | bytes 786440 | tf_op jit(solution)/shard_map/ppermute | solution.py:463
  31.4 1.9 %collective-permute-start.5 = (bf16[4,256,128]{2,1,0:T(8,128)(2,1)S(1)}, bf16[4,256,128]{2,1,0:T(8,128)(2,1)S(1)}, u32[]{:S(2)}, u32[]{:S(2)}) collective-permute-start(bf16[4,256,128]{2,1,0:T(8,128)(2,1)S(1)} %class_6_blocks.1), channel_id=1, source_target_pairs={{0,24},{4,28},{24,0},{28,4},{1,25},{5,29},{25,1},{29,5},{2,26},{6,... | collective-permute-start | bytes 786440 | tf_op jit(solution)/shard_map/ppermute | solution.py:463
  33.3 0.6 amplitude.1
  33.9 8.8 %collective-permute-done.4.rest_2_ = bf16[4,256,128]{2,1,0:T(8,128)(2,1)S(1)} collective-permute-done((bf16[4,256,128]{2,1,0:T(8,128)(2,1)S(1)}, bf16[4,256,128]{2,1,0:T(8,128)(2,1)S(1)}, u32[]{:S(2)}, u32[]{:S(2)}) %collective-permute-start.4) | collective-permute-done | bytes 262176 | tf_op jit(solution)/shard_map/ppermute | solution.py:463
  42.7 3.9 %collective-permute-done.6.rest_4_ = bf16[4,256,128]{2,1,0:T(8,128)(2,1)S(1)} collective-permute-done((bf16[4,256,128]{2,1,0:T(8,128)(2,1)S(1)}, bf16[4,256,128]{2,1,0:T(8,128)(2,1)S(1)}, u32[]{:S(2)}, u32[]{:S(2)}) %collective-permute-start.6) | collective-permute-done | bytes 262176 | tf_op jit(solution)/shard_map/ppermute | solution.py:463
  46.6 3.6 %collective-permute-done.7.rest_8_ = bf16[4,256,128]{2,1,0:T(8,128)(2,1)S(1)} collective-permute-done((bf16[4,256,128]{2,1,0:T(8,128)(2,1)S(1)}, bf16[4,256,128]{2,1,0:T(8,128)(2,1)S(1)}, u32[]{:S(2)}, u32[]{:S(2)}) %collective-permute-start.7) | collective-permute-done | bytes 262176 | tf_op jit(solution)/shard_map/ppermute | solution.py:463
  50.2 5.3 %modulus_step.1 = (bf16[4,256,128]{2,1,0:T(8,128)(2,1)S(1)}, bf16[4,256,128]{2,1,0:T(8,128)(2,1)S(1)}, bf16[4,256,128]{2,1,0:T(8,128)(2,1)S(1)}, bf16[4,256,128]{2,1,0:T(8,128)(2,1)S(1)}) custom-call(f32[1024,256]{1,0:T(8,128)S(1)} %get-tuple-element.48.amplitude, bf16[8,256,1024]{2,1,0:T(8,128)(2,1)S(1)} %get-tuple-element.49.table, ...), custom_call_target="tpu_custom_call" | custom-call | flops 4294967296 | bytes 12582912 | tf_op jit(solution)/shard_map/modulus_step/pallas_call | solution.py:503
  55.5 0.1 collective-permute-start.10
  55.6 2.4 %collective-permute-start.8 = (bf16[4,256,128]{2,1,0:T(8,128)(2,1)S(1)}, bf16[4,256,128]{2,1,0:T(8,128)(2,1)S(1)}, u32[]{:S(2)}, u32[]{:S(2)}) collective-permute-start(bf16[4,256,128]{2,1,0:T(8,128)(2,1)S(1)} %get-tuple-element.61), channel_id=1, source_target_pairs={{0,4},{4,0},{8,12},{12,8},{16,20},{20,16},{24,28},{28,24},{1,5},{5... | collective-permute-start | bytes 786440 | tf_op jit(solution)/shard_map/ppermute | solution.py:463
  58.0 1.4 %collective-permute-start.9 = (bf16[4,256,128]{2,1,0:T(8,128)(2,1)S(1)}, bf16[4,256,128]{2,1,0:T(8,128)(2,1)S(1)}, u32[]{:S(2)}, u32[]{:S(2)}) collective-permute-start(bf16[4,256,128]{2,1,0:T(8,128)(2,1)S(1)} %get-tuple-element.62), channel_id=1, source_target_pairs={{0,8},{4,12},{8,0},{12,4},{16,24},{20,28},{24,16},{28,20},{1,9},{5... | collective-permute-start | bytes 786440 | tf_op jit(solution)/shard_map/ppermute | solution.py:463
  59.4 6.3 %collective-permute-done.10.rest_3_ = bf16[4,256,128]{2,1,0:T(8,128)(2,1)S(1)} collective-permute-done((bf16[4,256,128]{2,1,0:T(8,128)(2,1)S(1)}, bf16[4,256,128]{2,1,0:T(8,128)(2,1)S(1)}, u32[]{:S(2)}, u32[]{:S(2)}) %collective-permute-start.10) | collective-permute-done | bytes 262176 | tf_op jit(solution)/shard_map/ppermute | solution.py:463
  65.6 2.7 %collective-permute-done.8.rest_1_ = bf16[4,256,128]{2,1,0:T(8,128)(2,1)S(1)} collective-permute-done((bf16[4,256,128]{2,1,0:T(8,128)(2,1)S(1)}, bf16[4,256,128]{2,1,0:T(8,128)(2,1)S(1)}, u32[]{:S(2)}, u32[]{:S(2)}) %collective-permute-start.8) | collective-permute-done | bytes 262176 | tf_op jit(solution)/shard_map/ppermute | solution.py:463
  68.4 1.7 %collective-permute-done.9.rest_2_ = bf16[4,256,128]{2,1,0:T(8,128)(2,1)S(1)} collective-permute-done((bf16[4,256,128]{2,1,0:T(8,128)(2,1)S(1)}, bf16[4,256,128]{2,1,0:T(8,128)(2,1)S(1)}, u32[]{:S(2)}, u32[]{:S(2)}) %collective-permute-start.9) | collective-permute-done | bytes 262176 | tf_op jit(solution)/shard_map/ppermute | solution.py:463
  70.1 3.6 %update_sent.1 = (bf16[2,2,256,512]{3,2,1,0:T(8,128)(2,1)}, bf16[2,2,256,512]{3,2,1,0:T(8,128)(2,1)S(1)}, bf16[1024,512]{1,0:T(8,128)(2,1)S(1)}) custom-call(s32[4]{0:T(128)S(1)} %pad_add_fusion.starts, bf16[8,1024,256]{2,1,0:T(8,128)(2,1)S(1)} %copy-done, bf16[4,256,128]{2,1,0:T(8,128)(2,1)S(1)} %get-tuple-element.60.rest_0_, ...), custom_call_target="tpu_custom_call" | custom-call | flops 1073741824 | bytes 8388608 | tf_op jit(solution)/shard_map/update_sent/pallas_call | solution.py:528
  73.7 0.5 collective-permute-start.11
  74.2 2.4 %update_kept.1 = (f32[2,256,512]{2,1,0:T(8,128)S(1)}, f32[2,256,512]{2,1,0:T(8,128)S(1)}, f32[2,256,512]{2,1,0:T(8,128)S(1)}, f32[2,256,512]{2,1,0:T(8,128)S(1)}) custom-call(s32[4]{0:T(128)S(1)} %pad_add_fusion.starts, bf16[8,1024,256]{2,1,0:T(8,128)(2,1)S(1)} %copy-done, bf16[1024,512]{1,0:T(8,128)(2,1)S(1)} %get-tuple-element.64.back), custom_call_target="tpu_custom_call" | custom-call | flops 1073741824 | bytes 10485760 | tf_op jit(solution)/shard_map/update_kept/pallas_call | solution.py:543
  76.7 1.2 %collective-permute-done.12.got_that = bf16[2,2,256,512]{3,2,1,0:T(8,128)(2,1)S(1)} collective-permute-done((bf16[2,2,256,512]{3,2,1,0:T(8,128)(2,1)S(1)}, bf16[2,2,256,512]{3,2,1,0:T(8,128)(2,1)S(1)}, u32[]{:S(2)}, u32[]{:S(2)}) %collective-permute-start.12) | collective-permute-done | bytes 1048608 | tf_op jit(solution)/shard_map/ppermute | solution.py:541
  77.8 0.9 x_first_kernel.1
  78.7 1.5 %collective-permute-start.13 = (bf16[2,256,384]{2,1,0:T(8,128)(2,1)}, bf16[2,256,384]{2,1,0:T(8,128)(2,1)}, u32[]{:S(2)}, u32[]{:S(2)}) collective-permute-start(bf16[2,256,384]{2,1,0:T(8,128)(2,1)} %x_first_kernel.1), channel_id=1, source_target_pairs={{0,2},{2,0},{1,3},{3,1},{4,6},{6,4},{5,7},{7,5},{8,10},{10,8},{9,1... | collective-permute-start | bytes 1179656 | tf_op jit(solution)/shard_map/ppermute | solution.py:561
  80.2 0.8 z_first_kernel.1
  81.0 2.8 %collective-permute-start.14 = (bf16[2,2,256,128]{3,2,1,0:T(8,128)(2,1)}, bf16[2,2,256,128]{3,2,1,0:T(8,128)(2,1)S(1)}, u32[]{:S(2)}, u32[]{:S(2)}) collective-permute-start(bf16[2,2,256,128]{3,2,1,0:T(8,128)(2,1)} %z_first_kernel.1), channel_id=1, source_target_pairs={{0,16},{4,20},{8,24},{20,4},{24,8},{28,12},{1,17},{5,21},{9,25},{2... | collective-permute-start | bytes 786440 | tf_op jit(solution)/shard_map/ppermute | solution.py:463
  83.9 0.1 x_own_kernel.1
  84.0 0.6 collective-permute-start.15
  84.6 6.4 %collective-permute-done.13.got_x = bf16[2,256,384]{2,1,0:T(8,128)(2,1)} collective-permute-done((bf16[2,256,384]{2,1,0:T(8,128)(2,1)}, bf16[2,256,384]{2,1,0:T(8,128)(2,1)}, u32[]{:S(2)}, u32[]{:S(2)}) %collective-permute-start.13) | collective-permute-done | bytes 393248 | tf_op jit(solution)/shard_map/ppermute | solution.py:561
  91.0 1.2 %copy-done.4 = f32[2,256,512]{2,1,0:T(8,128)S(1)} copy-done((f32[2,256,512]{2,1,0:T(8,128)S(1)}, f32[2,256,512]{2,1,0:T(8,128)}, u32[]{:S(2)}) %copy-start.4) | copy-done | bytes 1048600
  92.2 1.1 z_second_kernel.1
  93.3 2.8 %collective-permute-start.17 = (bf16[2,256,384]{2,1,0:T(8,128)(2,1)S(1)}, bf16[2,256,384]{2,1,0:T(8,128)(2,1)S(1)}, u32[]{:S(2)}, u32[]{:S(2)}) collective-permute-start(bf16[2,256,384]{2,1,0:T(8,128)(2,1)S(1)} %z_second_kernel.1), channel_id=1, source_target_pairs={{0,16},{4,20},{8,24},{20,4},{24,8},{28,12},{1,17},{5,21},{9,25},{2... | collective-permute-start | bytes 1179656 | tf_op jit(solution)/shard_map/ppermute | solution.py:463
  96.2 9.6 %collective-permute-done.14.got_z = bf16[2,2,256,128]{3,2,1,0:T(8,128)(2,1)S(1)} collective-permute-done((bf16[2,2,256,128]{3,2,1,0:T(8,128)(2,1)}, bf16[2,2,256,128]{3,2,1,0:T(8,128)(2,1)S(1)}, u32[]{:S(2)}, u32[]{:S(2)}) %collective-permute-start.14) | collective-permute-done | bytes 262176 | tf_op jit(solution)/shard_map/ppermute | solution.py:463
  105.8 0.1 x_last_kernel.1
  105.8 0.1 collective-permute-start.16
  105.9 1.5 %fusion.1 = f32[2,256,512]{2,1,0:T(8,128)S(1)} fusion(f32[2,256,512]{2,1,0:T(8,128)S(1)} %copy-done.7, f32[2,256,2048]{2,1,0:T(8,128)} %spectrum.1, s32[]{:T(128)S(6)} %select_n.3, bf16[2,2,256,512]{3,2,1,0:T(8,128)(2,1)S(1)} %collective-permute-done.11.got_this, bf16[2,256,128]{2,1,0:T(8,128)(2,1)S(1)} %slice_bitcast_fusion.1), kind=kLoop, calls=%fused_computation.2 | loop fusion | flops 1310720 | bytes 3801092 | tf_op jit(solution)/shard_map/add | solution.py:575
  107.4 3.8 %collective-permute-done.16 = bf16[2,256,128]{2,1,0:T(8,128)(2,1)S(1)} collective-permute-done((bf16[2,256,128]{2,1,0:T(8,128)(2,1)S(1)}, bf16[2,256,128]{2,1,0:T(8,128)(2,1)S(1)}, u32[]{:S(2)}, u32[]{:S(2)}) %collective-permute-start.16) | collective-permute-done | bytes 131104 | tf_op jit(solution)/shard_map/ppermute | solution.py:568
  111.2 0.2 add_add_fusion
  111.4 2.7 %collective-permute-done.17 = bf16[2,256,384]{2,1,0:T(8,128)(2,1)S(1)} collective-permute-done((bf16[2,256,384]{2,1,0:T(8,128)(2,1)S(1)}, bf16[2,256,384]{2,1,0:T(8,128)(2,1)S(1)}, u32[]{:S(2)}, u32[]{:S(2)}) %collective-permute-start.17) | collective-permute-done | bytes 393248 | tf_op jit(solution)/shard_map/ppermute | solution.py:463
  114.1 1.1 convert_add_fusion.1
  (23 shorter events, 0.1 us)
Async XLA Ops:
  0.0 4.6 %copy-start = (bf16[8,1024,256]{2,1,0:T(8,128)(2,1)S(1)}, bf16[8,1024,256]{2,1,0:T(8,128)(2,1)}, u32[]{:S(2)}) copy-start(bf16[8,1024,256]{2,1,0:T(8,128)(2,1)} %constant.18.clone.table) | copy-start | bytes 12582916
  0.9 2.4 %copy-start.1 = (f32[2,256,2048]{2,1,0:T(8,128)S(1)}, f32[2,256,2048]{2,1,0:T(8,128)}, u32[]{:S(2)}) copy-start(f32[2,256,2048]{2,1,0:T(8,128)} %spectrum.1) | copy-start | bytes 12582916
  6.5 11.5 %collective-permute-start = (bf16[4,256,128]{2,1,0:T(8,128)(2,1)S(1)}, bf16[4,256,128]{2,1,0:T(8,128)(2,1)S(1)}, u32[]{:S(2)}, u32[]{:S(2)}) collective-permute-start(bf16[4,256,128]{2,1,0:T(8,128)(2,1)S(1)} %get-tuple-element.41), channel_id=1, source_target_pairs={{8,16},{12,20},{16,8},{20,12},{4,0},{24,28},{9,17},{13,21},{17,9},... | collective-permute-start | bytes 786440 | tf_op jit(solution)/shard_map/ppermute | solution.py:463
  7.8 11.7 %collective-permute-start.1 = (bf16[4,256,128]{2,1,0:T(8,128)(2,1)S(1)}, bf16[4,256,128]{2,1,0:T(8,128)(2,1)S(1)}, u32[]{:S(2)}, u32[]{:S(2)}) collective-permute-start(bf16[4,256,128]{2,1,0:T(8,128)(2,1)S(1)} %get-tuple-element.42), channel_id=1, source_target_pairs={{4,12},{8,0},{12,4},{16,24},{20,28},{24,16},{5,13},{9,1},{13,5},{1... | collective-permute-start | bytes 786440 | tf_op jit(solution)/shard_map/ppermute | solution.py:463
  13.5 19.9 %copy-start.2 = (bf16[8,256,1024]{2,1,0:T(8,128)(2,1)S(1)}, bf16[8,256,1024]{2,1,0:T(8,128)(2,1)}, u32[]{:S(2)}) copy-start(bf16[8,256,1024]{2,1,0:T(8,128)(2,1)} %constant.17.clone.table) | copy-start | bytes 12582916
  13.5 19.9 %copy-start.5 = (f32[2,128,1024]{2,1,0:T(8,128)S(1)}, f32[2,128,1024]{2,1,0:T(8,128)}, u32[]{:S(2)}) copy-start(f32[2,128,1024]{2,1,0:T(8,128)} %images) | copy-start | bytes 3145732
  13.5 17.8 %collective-permute-start.3 = (bf16[4,256,128]{2,1,0:T(8,128)(2,1)S(1)}, bf16[4,256,128]{2,1,0:T(8,128)(2,1)S(1)}, u32[]{:S(2)}, u32[]{:S(2)}) collective-permute-start(bf16[4,256,128]{2,1,0:T(8,128)(2,1)S(1)} %get-tuple-element.52), channel_id=1, source_target_pairs={{8,20},{12,16},{16,12},{20,8},{4,0},{24,28},{9,21},{13,17},{17,13}... | collective-permute-start | bytes 786440 | tf_op jit(solution)/shard_map/ppermute | solution.py:463
  19.5 11.9 %collective-permute-start.2 = (bf16[4,256,128]{2,1,0:T(8,128)(2,1)S(1)}, bf16[4,256,128]{2,1,0:T(8,128)(2,1)S(1)}, u32[]{:S(2)}, u32[]{:S(2)}) collective-permute-start(bf16[4,256,128]{2,1,0:T(8,128)(2,1)S(1)} %get-tuple-element.51), channel_id=1, source_target_pairs={{4,0},{8,12},{12,8},{16,20},{20,16},{24,28},{5,1},{9,13},{13,9},{1... | collective-permute-start | bytes 786440 | tf_op jit(solution)/shard_map/ppermute | solution.py:463
  21.3 21.4 %collective-permute-start.4 = (bf16[4,256,128]{2,1,0:T(8,128)(2,1)S(1)}, bf16[4,256,128]{2,1,0:T(8,128)(2,1)S(1)}, u32[]{:S(2)}, u32[]{:S(2)}) collective-permute-start(bf16[4,256,128]{2,1,0:T(8,128)(2,1)S(1)} %class_4_blocks.1), channel_id=1, source_target_pairs={{0,16},{4,20},{8,24},{12,28},{16,0},{20,4},{24,8},{28,12},{1,17},{... | collective-permute-start | bytes 786440 | tf_op jit(solution)/shard_map/ppermute | solution.py:463
  24.5 22.1 %collective-permute-start.6 = (bf16[4,256,128]{2,1,0:T(8,128)(2,1)S(1)}, bf16[4,256,128]{2,1,0:T(8,128)(2,1)S(1)}, u32[]{:S(2)}, u32[]{:S(2)}) collective-permute-start(bf16[4,256,128]{2,1,0:T(8,128)(2,1)S(1)} %get-tuple-element.55.own), channel_id=1, source_target_pairs={{8,28},{12,24},{16,4},{20,0},{9,29},{13,25},{17,5},{21,1},{10,30},... | collective-permute-start | bytes 786440 | tf_op jit(solution)/shard_map/ppermute | solution.py:463
  25.8 24.4 %collective-permute-start.7 = (bf16[4,256,128]{2,1,0:T(8,128)(2,1)S(1)}, bf16[4,256,128]{2,1,0:T(8,128)(2,1)S(1)}, u32[]{:S(2)}, u32[]{:S(2)}) collective-permute-start(bf16[4,256,128]{2,1,0:T(8,128)(2,1)S(1)} %get-tuple-element.59), channel_id=1, source_target_pairs={{4,8},{8,4},{12,0},{16,28},{20,24},{24,20},{5,9},{9,5},{13,1},{17,... | collective-permute-start | bytes 786440 | tf_op jit(solution)/shard_map/ppermute | solution.py:463
  31.4 18.8 %collective-permute-start.5 = (bf16[4,256,128]{2,1,0:T(8,128)(2,1)S(1)}, bf16[4,256,128]{2,1,0:T(8,128)(2,1)S(1)}, u32[]{:S(2)}, u32[]{:S(2)}) collective-permute-start(bf16[4,256,128]{2,1,0:T(8,128)(2,1)S(1)} %class_6_blocks.1), channel_id=1, source_target_pairs={{0,24},{4,28},{24,0},{28,4},{1,25},{5,29},{25,1},{29,5},{2,26},{6,... | collective-permute-start | bytes 786440 | tf_op jit(solution)/shard_map/ppermute | solution.py:463
  55.5 10.1 %collective-permute-start.10 = (bf16[4,256,128]{2,1,0:T(8,128)(2,1)S(1)}, bf16[4,256,128]{2,1,0:T(8,128)(2,1)S(1)}, u32[]{:S(2)}, u32[]{:S(2)}) collective-permute-start(bf16[4,256,128]{2,1,0:T(8,128)(2,1)S(1)} %get-tuple-element.63), channel_id=1, source_target_pairs={{0,12},{4,8},{8,4},{12,0},{16,28},{20,24},{24,20},{28,16},{1,13},{... | collective-permute-start | bytes 786440 | tf_op jit(solution)/shard_map/ppermute | solution.py:463
  55.6 12.8 %collective-permute-start.8 = (bf16[4,256,128]{2,1,0:T(8,128)(2,1)S(1)}, bf16[4,256,128]{2,1,0:T(8,128)(2,1)S(1)}, u32[]{:S(2)}, u32[]{:S(2)}) collective-permute-start(bf16[4,256,128]{2,1,0:T(8,128)(2,1)S(1)} %get-tuple-element.61), channel_id=1, source_target_pairs={{0,4},{4,0},{8,12},{12,8},{16,20},{20,16},{24,28},{28,24},{1,5},{5... | collective-permute-start | bytes 786440 | tf_op jit(solution)/shard_map/ppermute | solution.py:463
  58.0 12.1 %collective-permute-start.9 = (bf16[4,256,128]{2,1,0:T(8,128)(2,1)S(1)}, bf16[4,256,128]{2,1,0:T(8,128)(2,1)S(1)}, u32[]{:S(2)}, u32[]{:S(2)}) collective-permute-start(bf16[4,256,128]{2,1,0:T(8,128)(2,1)S(1)} %get-tuple-element.62), channel_id=1, source_target_pairs={{0,8},{4,12},{8,0},{12,4},{16,24},{20,28},{24,16},{28,20},{1,9},{5... | collective-permute-start | bytes 786440 | tf_op jit(solution)/shard_map/ppermute | solution.py:463
  73.7 4.1 %collective-permute-start.12 = (bf16[2,2,256,512]{3,2,1,0:T(8,128)(2,1)S(1)}, bf16[2,2,256,512]{3,2,1,0:T(8,128)(2,1)S(1)}, u32[]{:S(2)}, u32[]{:S(2)}) collective-permute-start(bf16[2,2,256,512]{3,2,1,0:T(8,128)(2,1)S(1)} %get-tuple-element.68), channel_id=1, source_target_pairs={{0,1},{1,0},{2,3},{3,2},{4,5},{5,4},{6,7},{7,6},{8,9},{9,8},{10,11... | collective-permute-start | bytes 3145736 | tf_op jit(solution)/shard_map/ppermute | solution.py:541
  73.7 10.2 %collective-permute-start.11 = (bf16[2,2,256,512]{3,2,1,0:T(8,128)(2,1)}, bf16[2,2,256,512]{3,2,1,0:T(8,128)(2,1)S(1)}, u32[]{:S(2)}, u32[]{:S(2)}) collective-permute-start(bf16[2,2,256,512]{3,2,1,0:T(8,128)(2,1)} %get-tuple-element.66), channel_id=1, source_target_pairs={{0,1},{1,0},{2,3},{3,2},{4,5},{5,4},{6,7},{7,6},{8,9},{9,8},{10,11... | collective-permute-start | bytes 3145736 | tf_op jit(solution)/shard_map/ppermute | solution.py:542
  76.7 4.4 %copy-start.3 = (f32[2,256,512]{2,1,0:T(8,128)}, f32[2,256,512]{2,1,0:T(8,128)S(1)}, u32[]{:S(2)}) copy-start(f32[2,256,512]{2,1,0:T(8,128)S(1)} %get-tuple-element.67.that_near) | copy-start | bytes 3145732
  76.7 7.2 %copy-start.6 = (f32[2,256,512]{2,1,0:T(8,128)}, f32[2,256,512]{2,1,0:T(8,128)S(1)}, u32[]{:S(2)}) copy-start(f32[2,256,512]{2,1,0:T(8,128)S(1)} %get-tuple-element.65) | copy-start | bytes 3145732
  78.7 12.3 %collective-permute-start.13 = (bf16[2,256,384]{2,1,0:T(8,128)(2,1)}, bf16[2,256,384]{2,1,0:T(8,128)(2,1)}, u32[]{:S(2)}, u32[]{:S(2)}) collective-permute-start(bf16[2,256,384]{2,1,0:T(8,128)(2,1)} %x_first_kernel.1), channel_id=1, source_target_pairs={{0,2},{2,0},{1,3},{3,1},{4,6},{6,4},{5,7},{7,5},{8,10},{10,8},{9,1... | collective-permute-start | bytes 1179656 | tf_op jit(solution)/shard_map/ppermute | solution.py:561
  81.0 24.7 %collective-permute-start.14 = (bf16[2,2,256,128]{3,2,1,0:T(8,128)(2,1)}, bf16[2,2,256,128]{3,2,1,0:T(8,128)(2,1)S(1)}, u32[]{:S(2)}, u32[]{:S(2)}) collective-permute-start(bf16[2,2,256,128]{3,2,1,0:T(8,128)(2,1)} %z_first_kernel.1), channel_id=1, source_target_pairs={{0,16},{4,20},{8,24},{20,4},{24,8},{28,12},{1,17},{5,21},{9,25},{2... | collective-permute-start | bytes 786440 | tf_op jit(solution)/shard_map/ppermute | solution.py:463
  83.9 22.0 %copy-start.7 = (f32[2,256,512]{2,1,0:T(8,128)S(1)}, f32[2,256,512]{2,1,0:T(8,128)}, u32[]{:S(2)}) copy-start(f32[2,256,512]{2,1,0:T(8,128)} %copy-done.6) | copy-start | bytes 3145732
  84.0 23.5 %collective-permute-start.15 = (bf16[2,256,384]{2,1,0:T(8,128)(2,1)S(1)}, bf16[2,256,384]{2,1,0:T(8,128)(2,1)S(1)}, u32[]{:S(2)}, u32[]{:S(2)}) collective-permute-start(bf16[2,256,384]{2,1,0:T(8,128)(2,1)S(1)} %x_own_kernel.1), channel_id=1, source_target_pairs={{0,2},{2,0},{1,3},{3,1},{4,6},{6,4},{5,7},{7,5},{8,10},{10,8},{9,1... | collective-permute-start | bytes 1179656 | tf_op jit(solution)/shard_map/ppermute | solution.py:565
  91.0 1.2 %copy-start.4 = (f32[2,256,512]{2,1,0:T(8,128)S(1)}, f32[2,256,512]{2,1,0:T(8,128)}, u32[]{:S(2)}) copy-start(f32[2,256,512]{2,1,0:T(8,128)} %copy-done.3) | copy-start | bytes 3145732
  93.3 20.8 %collective-permute-start.17 = (bf16[2,256,384]{2,1,0:T(8,128)(2,1)S(1)}, bf16[2,256,384]{2,1,0:T(8,128)(2,1)S(1)}, u32[]{:S(2)}, u32[]{:S(2)}) collective-permute-start(bf16[2,256,384]{2,1,0:T(8,128)(2,1)S(1)} %z_second_kernel.1), channel_id=1, source_target_pairs={{0,16},{4,20},{8,24},{20,4},{24,8},{28,12},{1,17},{5,21},{9,25},{2... | collective-permute-start | bytes 1179656 | tf_op jit(solution)/shard_map/ppermute | solution.py:463
  105.8 5.4 %collective-permute-start.16 = (bf16[2,256,128]{2,1,0:T(8,128)(2,1)S(1)}, bf16[2,256,128]{2,1,0:T(8,128)(2,1)S(1)}, u32[]{:S(2)}, u32[]{:S(2)}) collective-permute-start(bf16[2,256,128]{2,1,0:T(8,128)(2,1)S(1)} %x_last_kernel.1), channel_id=1, source_target_pairs={{0,2},{2,0},{1,3},{3,1},{4,6},{6,4},{5,7},{7,5},{8,10},{10,8},{9,1... | collective-permute-start | bytes 393224 | tf_op jit(solution)/shard_map/ppermute | solution.py:568

commit v14 on v13

--- a/solution.py
+++ b/solution.py
@@ -395,10 +395,12 @@
     out[...] = total.astype(out.dtype)
 
 
-def x_last_kernel(this_far, got_this, got_z, out):
+def x_last_kernel(this_far, got_this, got_z, got_by_y, out):
     cols = out.shape[2]
     total = this_far[:, :, :cols] + got_this[1, :, :, :cols].astype(jnp.float32)
-    out[...] = (total + got_z[1].astype(jnp.float32)).astype(out.dtype)
+    for got in (got_z, got_by_y):
+        total += got[1].astype(jnp.float32)
+    out[...] = total.astype(out.dtype)
 
 
 def local_call(kernel, out_shape, spaces, scratch, flops, moved, name):
@@ -556,7 +558,12 @@
         return local_call(kernel, out_shape, specs, [], 0, 2**20, kernel.__name__)(*values)
 
     over = sum_call(z_first_kernel, (2, 2, rows, first), that_near, that_far, got_that)
-    got_z_first = permute(over, across)
+    by_y = {2: 3, 5: 4}
+    relayed = permute(over, list(by_y.items()))
+    got_z_first = (
+        permute(over, [(s, to) for s, to in across if s not in by_y]),
+        permute(relayed, [(by, s ^ 4) for s, by in by_y.items()]),
+    )
     over = sum_call(x_first_kernel, (2, rows, share - first), that_far, got_that)
     got_x = lax.ppermute(over, "led", planes)
     over_z = sum_call(z_second_kernel, (2, rows, share - first), that_near, got_that, got_x)
@@ -564,7 +571,7 @@
     over = sum_call(x_own_kernel, (2, rows, share - first), this_far, got_this)
     got_x_own = lax.ppermute(over, "led", planes)
     over, got_z_first = lax.optimization_barrier((over_z, got_z_first))
-    over = sum_call(x_last_kernel, (2, rows, first), this_far, got_this, got_z_first)
+    over = sum_call(x_last_kernel, (2, rows, first), this_far, got_this, *got_z_first)
     got_x_last = lax.ppermute(over, "led", planes)
 
     def widen(value, before):
@@ -572,7 +579,8 @@
         return jnp.pad(value.astype(jnp.float32), ((0, 0), (0, 0), (before, after)))
 
     base = lax.dynamic_slice_in_dim(spectrum, led_at * share, share, 2)
-    base += this_near + got_this[0].astype(jnp.float32) + widen(got_z_first[0], 0)
+    base += this_near + got_this[0].astype(jnp.float32)
+    base += widen(sum(got[0].astype(jnp.float32) for got in got_z_first), 0)
     base, got_x_own, got_x_last = lax.optimization_barrier((base, got_x_own, got_x_last))
     base += widen(got_x_own, first) + widen(got_x_last, 0)
     base, got_z_second = lax.optimization_barrier((base, got_z_second))

time: 116 us -> 119 us (1.026)
  waiting for transfers between devices: 52.2 us -> 42.1 us
  starting transfers between devices: 34.4 us -> 43.7 us
  local copies, waits for them, and re-layouts: 3.65 us -> 5.57 us
    ppermute x13 -> x15, starting transfers between devices: 31.7 us -> 39.6 us  [permute(): return lax.ppermute(sent, 'slab', pairs)]
    ppermute x13 -> x15, waiting for transfers between devices: 40.8 us -> 36 us  [permute(): return lax.ppermute(sent, 'slab', pairs)]
    ppermute x1, waiting for transfers between devices: 6.42 us -> 3.3 us  [body_slabs(): got_x = lax.ppermute(over, 'led', planes)]
    unnamed x16, local copies, waits for them, and re-layouts: 3.64 us -> 5.57 us
    ppermute x1, starting transfers between devices: 0.07 us -> 1.38 us  [body_slabs(): got_x_last = lax.ppermute(over, 'led', planes)]
    ppermute x1, waiting for transfers between devices: 3.78 us -> 2.58 us  [body_slabs(): got_x_last = lax.ppermute(over, 'led', planes)]
    add x1 -> x2, other arithmetic: 1.5 us -> 2.44 us  [body_slabs(): base += widen(sum((got[0].astype(jnp.float32) for got in got_z_first)), 0)]
  transfers between devices with their start and end apart: 18 -> 20, of which waited for: 12 -> 12; matrix products, arithmetic and copies ran while one was open for 1% -> 2% of each run, Pallas kernels for 8% -> 8%
where the time goes in v14:
time: 119 us; the launch traced here: 118 us
  starting transfers between devices  43.7 us (37%)
  waiting for transfers between devices  42.1 us (35%)
  Pallas kernels  21.8 us (18%)
  local copies, waits for them, and re-layouts  5.57 us (5%)
  other arithmetic  4.6 us (4%)
    ppermute x15, starting transfers between devices, permute(): return lax.ppermute(sent, 'slab', pairs)  39.6 us
    ppermute x15, waiting for transfers between devices, permute(): return lax.ppermute(sent, 'slab', pairs)  36 us
    unnamed x16, local copies, waits for them, and re-layouts  5.57 us
    pallas_call x1, Pallas kernels, body_slabs(): local_call(field_kernel, [sent_block] * HALF, [vmem] * 11, [pltpu.VMEM((w...  5.31 us
    pallas_call x2, Pallas kernels, rows_call(): local_call(functools.partial(rows_kernel, which), [sent_block] * count, [...  4.69 us
    pallas_call x5, Pallas kernels, sum_call(): local_call(kernel, out_shape, specs, [], 0, 2 ** 20, kernel.__name__)  3.85 us
    pallas_call x1, Pallas kernels, body_slabs(): local_call(sent_kernel, [jax.ShapeDtypeStruct((2,) + piece, bf16), jax.Sh...  3.59 us
    ppermute x1, waiting for transfers between devices, body_slabs(): got_x = lax.ppermute(over, 'led', planes)  3.3 us
  transfers between devices with their start and end apart: 20, of which 12 were waited for; matrix products, arithmetic and copies ran while one was open for 2% of the time, Pallas kernels for 8%

profile of v14, /device:TPU:4, one launch (start us, length us, event | category | flops | bytes accessed | tf_op | source)
XLA Modules:
  0.0 118.1 jit_solution(7606331153901004660)
XLA Ops:
  0.0 0.9 pad_add_fusion.starts
  0.9 2.4 %copy-done.1 = f32[2,256,2048]{2,1,0:T(8,128)S(1)} copy-done((f32[2,256,2048]{2,1,0:T(8,128)S(1)}, f32[2,256,2048]{2,1,0:T(8,128)}, u32[]{:S(2)}) %copy-start.1) | copy-done | bytes 4194328
  3.3 1.4 %windows.1.window = bf16[1024,1024]{1,0:T(8,128)(2,1)S(1)} custom-call(s32[4]{0:T(128)S(1)} %pad_add_fusion.starts, f32[2,256,2048]{2,1,0:T(8,128)S(1)} %copy-done.1), custom_call_target="tpu_custom_call" | custom-call | bytes 6291456 | tf_op jit(solution)/shard_map/windows/pallas_call | solution.py:440
  4.7 1.8 %rows_round_1.1 = (bf16[4,256,128]{2,1,0:T(8,128)(2,1)S(1)}, bf16[4,256,128]{2,1,0:T(8,128)(2,1)S(1)}, bf16[4,256,128]{2,1,0:T(8,128)(2,1)S(1)}) custom-call(bf16[1024,1024]{1,0:T(8,128)(2,1)S(1)} %windows.1.window, bf16[8,1024,256]{2,1,0:T(8,128)(2,1)S(1)} %copy-done), custom_call_target="tpu_custom_call" | custom-call | flops 1610612736 | bytes 5242880 | tf_op jit(solution)/shard_map/rows_round_1/pallas_call | solution.py:452
  6.5 1.3 %collective-permute-start = (bf16[4,256,128]{2,1,0:T(8,128)(2,1)S(1)}, bf16[4,256,128]{2,1,0:T(8,128)(2,1)S(1)}, u32[]{:S(2)}, u32[]{:S(2)}) collective-permute-start(bf16[4,256,128]{2,1,0:T(8,128)(2,1)S(1)} %get-tuple-element.42), channel_id=1, source_target_pairs={{8,16},{12,20},{16,8},{20,12},{4,0},{24,28},{9,17},{13,21},{17,9},... | collective-permute-start | bytes 786440 | tf_op jit(solution)/shard_map/ppermute | solution.py:465
  7.8 5.7 %collective-permute-start.1 = (bf16[4,256,128]{2,1,0:T(8,128)(2,1)S(1)}, bf16[4,256,128]{2,1,0:T(8,128)(2,1)S(1)}, u32[]{:S(2)}, u32[]{:S(2)}) collective-permute-start(bf16[4,256,128]{2,1,0:T(8,128)(2,1)S(1)} %get-tuple-element.43), channel_id=1, source_target_pairs={{4,12},{8,0},{12,4},{16,24},{20,28},{24,16},{5,13},{9,1},{13,5},{1... | collective-permute-start | bytes 786440 | tf_op jit(solution)/shard_map/ppermute | solution.py:465
  13.5 1.6 %collective-permute-start.3 = (bf16[4,256,128]{2,1,0:T(8,128)(2,1)S(1)}, bf16[4,256,128]{2,1,0:T(8,128)(2,1)S(1)}, u32[]{:S(2)}, u32[]{:S(2)}) collective-permute-start(bf16[4,256,128]{2,1,0:T(8,128)(2,1)S(1)} %get-tuple-element.53), channel_id=1, source_target_pairs={{8,20},{12,16},{16,12},{20,8},{4,0},{24,28},{9,21},{13,17},{17,13}... | collective-permute-start | bytes 786440 | tf_op jit(solution)/shard_map/ppermute | solution.py:465
  15.1 2.9 %rows_round_2.1 = (bf16[4,256,128]{2,1,0:T(8,128)(2,1)S(1)}, bf16[4,256,128]{2,1,0:T(8,128)(2,1)S(1)}, bf16[4,256,128]{2,1,0:T(8,128)(2,1)S(1)}, bf16[4,256,128]...) custom-call(bf16[1024,1024]{1,0:T(8,128)(2,1)S(1)} %windows.1.window, bf16[8,1024,256]{2,1,0:T(8,128)(2,1)S(1)} %copy-done), custom_call_target="tpu_custom_call" | custom-call | flops 2684354560 | bytes 5242880 | tf_op jit(solution)/shard_map/rows_round_2/pallas_call | solution.py:452
  18.0 1.5 %collective-permute-done.1.rest_7_ = bf16[4,256,128]{2,1,0:T(8,128)(2,1)S(1)} collective-permute-done((bf16[4,256,128]{2,1,0:T(8,128)(2,1)S(1)}, bf16[4,256,128]{2,1,0:T(8,128)(2,1)S(1)}, u32[]{:S(2)}, u32[]{:S(2)}) %collective-permute-start.1) | collective-permute-done | bytes 262176 | tf_op jit(solution)/shard_map/ppermute | solution.py:465
  19.5 1.8 %collective-permute-start.2 = (bf16[4,256,128]{2,1,0:T(8,128)(2,1)S(1)}, bf16[4,256,128]{2,1,0:T(8,128)(2,1)S(1)}, u32[]{:S(2)}, u32[]{:S(2)}) collective-permute-start(bf16[4,256,128]{2,1,0:T(8,128)(2,1)S(1)} %get-tuple-element.52), channel_id=1, source_target_pairs={{4,0},{8,12},{12,8},{16,20},{20,16},{24,28},{5,1},{9,13},{13,9},{1... | collective-permute-start | bytes 786440 | tf_op jit(solution)/shard_map/ppermute | solution.py:465
  21.3 3.2 %collective-permute-start.4 = (bf16[4,256,128]{2,1,0:T(8,128)(2,1)S(1)}, bf16[4,256,128]{2,1,0:T(8,128)(2,1)S(1)}, u32[]{:S(2)}, u32[]{:S(2)}) collective-permute-start(bf16[4,256,128]{2,1,0:T(8,128)(2,1)S(1)} %class_4_blocks.1), channel_id=1, source_target_pairs={{0,16},{4,20},{8,24},{12,28},{16,0},{20,4},{24,8},{28,12},{1,17},{... | collective-permute-start | bytes 786440 | tf_op jit(solution)/shard_map/ppermute | solution.py:465
  24.5 1.3 %collective-permute-start.6 = (bf16[4,256,128]{2,1,0:T(8,128)(2,1)S(1)}, bf16[4,256,128]{2,1,0:T(8,128)(2,1)S(1)}, u32[]{:S(2)}, u32[]{:S(2)}) collective-permute-start(bf16[4,256,128]{2,1,0:T(8,128)(2,1)S(1)} %get-tuple-element.56.own), channel_id=1, source_target_pairs={{8,28},{12,24},{16,4},{20,0},{9,29},{13,25},{17,5},{21,1},{10,30},... | collective-permute-start | bytes 786440 | tf_op jit(solution)/shard_map/ppermute | solution.py:465
  25.8 5.5 %collective-permute-start.7 = (bf16[4,256,128]{2,1,0:T(8,128)(2,1)S(1)}, bf16[4,256,128]{2,1,0:T(8,128)(2,1)S(1)}, u32[]{:S(2)}, u32[]{:S(2)}) collective-permute-start(bf16[4,256,128]{2,1,0:T(8,128)(2,1)S(1)} %get-tuple-element.60), channel_id=1, source_target_pairs={{4,8},{8,4},{12,0},{16,28},{20,24},{24,20},{5,9},{9,5},{13,1},{17,... | collective-permute-start | bytes 786440 | tf_op jit(solution)/shard_map/ppermute | solution.py:465
  31.4 1.9 %collective-permute-start.5 = (bf16[4,256,128]{2,1,0:T(8,128)(2,1)S(1)}, bf16[4,256,128]{2,1,0:T(8,128)(2,1)S(1)}, u32[]{:S(2)}, u32[]{:S(2)}) collective-permute-start(bf16[4,256,128]{2,1,0:T(8,128)(2,1)S(1)} %class_6_blocks.1), channel_id=1, source_target_pairs={{0,24},{4,28},{24,0},{28,4},{1,25},{5,29},{25,1},{29,5},{2,26},{6,... | collective-permute-start | bytes 786440 | tf_op jit(solution)/shard_map/ppermute | solution.py:465
  33.3 0.6 amplitude.1
  33.9 8.8 %collective-permute-done.4.rest_2_ = bf16[4,256,128]{2,1,0:T(8,128)(2,1)S(1)} collective-permute-done((bf16[4,256,128]{2,1,0:T(8,128)(2,1)S(1)}, bf16[4,256,128]{2,1,0:T(8,128)(2,1)S(1)}, u32[]{:S(2)}, u32[]{:S(2)}) %collective-permute-start.4) | collective-permute-done | bytes 262176 | tf_op jit(solution)/shard_map/ppermute | solution.py:465
  42.7 3.9 %collective-permute-done.6.rest_4_ = bf16[4,256,128]{2,1,0:T(8,128)(2,1)S(1)} collective-permute-done((bf16[4,256,128]{2,1,0:T(8,128)(2,1)S(1)}, bf16[4,256,128]{2,1,0:T(8,128)(2,1)S(1)}, u32[]{:S(2)}, u32[]{:S(2)}) %collective-permute-start.6) | collective-permute-done | bytes 262176 | tf_op jit(solution)/shard_map/ppermute | solution.py:465
  46.6 3.6 %collective-permute-done.7.rest_8_ = bf16[4,256,128]{2,1,0:T(8,128)(2,1)S(1)} collective-permute-done((bf16[4,256,128]{2,1,0:T(8,128)(2,1)S(1)}, bf16[4,256,128]{2,1,0:T(8,128)(2,1)S(1)}, u32[]{:S(2)}, u32[]{:S(2)}) %collective-permute-start.7) | collective-permute-done | bytes 262176 | tf_op jit(solution)/shard_map/ppermute | solution.py:465
  50.2 5.3 %modulus_step.1 = (bf16[4,256,128]{2,1,0:T(8,128)(2,1)S(1)}, bf16[4,256,128]{2,1,0:T(8,128)(2,1)S(1)}, bf16[4,256,128]{2,1,0:T(8,128)(2,1)S(1)}, bf16[4,256,128]{2,1,0:T(8,128)(2,1)S(1)}) custom-call(f32[1024,256]{1,0:T(8,128)S(1)} %get-tuple-element.49.amplitude, bf16[8,256,1024]{2,1,0:T(8,128)(2,1)S(1)} %get-tuple-element.50.table, ...), custom_call_target="tpu_custom_call" | custom-call | flops 4294967296 | bytes 12582912 | tf_op jit(solution)/shard_map/modulus_step/pallas_call | solution.py:505
  55.6 2.4 %collective-permute-start.8 = (bf16[4,256,128]{2,1,0:T(8,128)(2,1)S(1)}, bf16[4,256,128]{2,1,0:T(8,128)(2,1)S(1)}, u32[]{:S(2)}, u32[]{:S(2)}) collective-permute-start(bf16[4,256,128]{2,1,0:T(8,128)(2,1)S(1)} %get-tuple-element.62), channel_id=1, source_target_pairs={{0,4},{4,0},{8,12},{12,8},{16,20},{20,16},{24,28},{28,24},{1,5},{5... | collective-permute-start | bytes 786440 | tf_op jit(solution)/shard_map/ppermute | solution.py:465
  58.0 1.4 %collective-permute-start.9 = (bf16[4,256,128]{2,1,0:T(8,128)(2,1)S(1)}, bf16[4,256,128]{2,1,0:T(8,128)(2,1)S(1)}, u32[]{:S(2)}, u32[]{:S(2)}) collective-permute-start(bf16[4,256,128]{2,1,0:T(8,128)(2,1)S(1)} %get-tuple-element.63), channel_id=1, source_target_pairs={{0,8},{4,12},{8,0},{12,4},{16,24},{20,28},{24,16},{28,20},{1,9},{5... | collective-permute-start | bytes 786440 | tf_op jit(solution)/shard_map/ppermute | solution.py:465
  59.4 6.3 %collective-permute-done.10.rest_3_ = bf16[4,256,128]{2,1,0:T(8,128)(2,1)S(1)} collective-permute-done((bf16[4,256,128]{2,1,0:T(8,128)(2,1)S(1)}, bf16[4,256,128]{2,1,0:T(8,128)(2,1)S(1)}, u32[]{:S(2)}, u32[]{:S(2)}) %collective-permute-start.10) | collective-permute-done | bytes 262176 | tf_op jit(solution)/shard_map/ppermute | solution.py:465
  65.6 2.7 %collective-permute-done.8.rest_1_ = bf16[4,256,128]{2,1,0:T(8,128)(2,1)S(1)} collective-permute-done((bf16[4,256,128]{2,1,0:T(8,128)(2,1)S(1)}, bf16[4,256,128]{2,1,0:T(8,128)(2,1)S(1)}, u32[]{:S(2)}, u32[]{:S(2)}) %collective-permute-start.8) | collective-permute-done | bytes 262176 | tf_op jit(solution)/shard_map/ppermute | solution.py:465
  68.4 1.7 %collective-permute-done.9.rest_2_ = bf16[4,256,128]{2,1,0:T(8,128)(2,1)S(1)} collective-permute-done((bf16[4,256,128]{2,1,0:T(8,128)(2,1)S(1)}, bf16[4,256,128]{2,1,0:T(8,128)(2,1)S(1)}, u32[]{:S(2)}, u32[]{:S(2)}) %collective-permute-start.9) | collective-permute-done | bytes 262176 | tf_op jit(solution)/shard_map/ppermute | solution.py:465
  70.1 3.6 %update_sent.1 = (bf16[2,2,256,512]{3,2,1,0:T(8,128)(2,1)}, bf16[2,2,256,512]{3,2,1,0:T(8,128)(2,1)S(1)}, bf16[1024,512]{1,0:T(8,128)(2,1)S(1)}) custom-call(s32[4]{0:T(128)S(1)} %pad_add_fusion.starts, bf16[8,1024,256]{2,1,0:T(8,128)(2,1)S(1)} %copy-done, bf16[4,256,128]{2,1,0:T(8,128)(2,1)S(1)} %get-tuple-element.61.rest_0_, ...), custom_call_target="tpu_custom_call" | custom-call | flops 1073741824 | bytes 8388608 | tf_op jit(solution)/shard_map/update_sent/pallas_call | solution.py:530
  73.7 0.5 collective-permute-start.11
  74.2 2.4 %update_kept.1 = (f32[2,256,512]{2,1,0:T(8,128)S(1)}, f32[2,256,512]{2,1,0:T(8,128)S(1)}, f32[2,256,512]{2,1,0:T(8,128)S(1)}, f32[2,256,512]{2,1,0:T(8,128)S(1)}) custom-call(s32[4]{0:T(128)S(1)} %pad_add_fusion.starts, bf16[8,1024,256]{2,1,0:T(8,128)(2,1)S(1)} %copy-done, bf16[1024,512]{1,0:T(8,128)(2,1)S(1)} %get-tuple-element.65.back), custom_call_target="tpu_custom_call" | custom-call | flops 1073741824 | bytes 10485760 | tf_op jit(solution)/shard_map/update_kept/pallas_call | solution.py:545
  76.7 1.0 copy-done.6
  77.6 0.2 collective-permute-done.12.got_that
  77.8 0.8 z_first_kernel.1
  78.6 1.0 copy-done.3
  79.6 1.3 %collective-permute-start.15 = (bf16[2,2,256,128]{3,2,1,0:T(8,128)(2,1)}, bf16[2,2,256,128]{3,2,1,0:T(8,128)(2,1)}, u32[]{:S(2)}, u32[]{:S(2)}) collective-permute-start(bf16[2,2,256,128]{3,2,1,0:T(8,128)(2,1)} %z_first_kernel.1), channel_id=1, source_target_pairs={{8,12},{20,16},{9,13},{21,17},{10,14},{22,18},{11,15},{23,19}} | collective-permute-start | bytes 786440 | tf_op jit(solution)/shard_map/ppermute | solution.py:465
  81.0 0.8 x_first_kernel.1
  81.8 1.5 %collective-permute-start.13 = (bf16[2,256,384]{2,1,0:T(8,128)(2,1)}, bf16[2,256,384]{2,1,0:T(8,128)(2,1)}, u32[]{:S(2)}, u32[]{:S(2)}) collective-permute-start(bf16[2,256,384]{2,1,0:T(8,128)(2,1)} %x_first_kernel.1), channel_id=1, source_target_pairs={{0,2},{2,0},{1,3},{3,1},{4,6},{6,4},{5,7},{7,5},{8,10},{10,8},{9,1... | collective-permute-start | bytes 1179656 | tf_op jit(solution)/shard_map/ppermute | solution.py:568
  83.3 5.4 %collective-permute-start.14 = (bf16[2,2,256,128]{3,2,1,0:T(8,128)(2,1)}, bf16[2,2,256,128]{3,2,1,0:T(8,128)(2,1)S(1)}, u32[]{:S(2)}, u32[]{:S(2)}) collective-permute-start(bf16[2,2,256,128]{3,2,1,0:T(8,128)(2,1)} %z_first_kernel.1), channel_id=1, source_target_pairs={{0,16},{4,20},{24,8},{28,12},{1,17},{5,21},{25,9},{29,13},{2,18},{... | collective-permute-start | bytes 786440 | tf_op jit(solution)/shard_map/ppermute | solution.py:465
  88.7 1.3 %collective-permute-start.16 = (bf16[2,2,256,128]{3,2,1,0:T(8,128)(2,1)}, bf16[2,2,256,128]{3,2,1,0:T(8,128)(2,1)}, u32[]{:S(2)}, u32[]{:S(2)}) collective-permute-start(bf16[2,2,256,128]{3,2,1,0:T(8,128)(2,1)} %collective-permute-done.15), channel_id=1, source_target_pairs={{12,24},{16,4},{13,25},{17,5},{14,26},{18,6},{15,27},{19,7}} | collective-permute-start | bytes 786440 | tf_op jit(solution)/shard_map/ppermute | solution.py:465
  90.1 0.7 collective-permute-start.17
  90.8 3.3 %collective-permute-done.13.got_x = bf16[2,256,384]{2,1,0:T(8,128)(2,1)} collective-permute-done((bf16[2,256,384]{2,1,0:T(8,128)(2,1)}, bf16[2,256,384]{2,1,0:T(8,128)(2,1)}, u32[]{:S(2)}, u32[]{:S(2)}) %collective-permute-start.13) | collective-permute-done | bytes 393248 | tf_op jit(solution)/shard_map/ppermute | solution.py:568
  94.1 1.2 %copy-done.4 = f32[2,256,512]{2,1,0:T(8,128)S(1)} copy-done((f32[2,256,512]{2,1,0:T(8,128)S(1)}, f32[2,256,512]{2,1,0:T(8,128)}, u32[]{:S(2)}) %copy-start.4) | copy-done | bytes 1048600
  95.3 1.1 z_second_kernel.1
  96.4 5.5 %collective-permute-start.19 = (bf16[2,256,384]{2,1,0:T(8,128)(2,1)S(1)}, bf16[2,256,384]{2,1,0:T(8,128)(2,1)S(1)}, u32[]{:S(2)}, u32[]{:S(2)}) collective-permute-start(bf16[2,256,384]{2,1,0:T(8,128)(2,1)S(1)} %z_second_kernel.1), channel_id=1, source_target_pairs={{0,16},{4,20},{8,24},{20,4},{24,8},{28,12},{1,17},{5,21},{9,25},{2... | collective-permute-start | bytes 1179656 | tf_op jit(solution)/shard_map/ppermute | solution.py:465
  102.0 0.9 add_bitcast_fusion
  103.0 1.0 x_last_kernel.1
  104.0 1.4 %collective-permute-start.18 = (bf16[2,256,128]{2,1,0:T(8,128)(2,1)S(1)}, bf16[2,256,128]{2,1,0:T(8,128)(2,1)S(1)}, u32[]{:S(2)}, u32[]{:S(2)}) collective-permute-start(bf16[2,256,128]{2,1,0:T(8,128)(2,1)S(1)} %x_last_kernel.1), channel_id=1, source_target_pairs={{0,2},{2,0},{1,3},{3,1},{4,6},{6,4},{5,7},{7,5},{8,10},{10,8},{9,1... | collective-permute-start | bytes 393224 | tf_op jit(solution)/shard_map/ppermute | solution.py:575
  105.4 1.5 %fusion.1 = f32[2,256,512]{2,1,0:T(8,128)S(1)} fusion(f32[2,256,512]{2,1,0:T(8,128)S(1)} %copy-done.7, f32[2,256,128]{2,1,0:T(8,128)S(1)} %add_bitcast_fusion, f32[2,256,2048]{2,1,0:T(8,128)} %spectrum.1, s32[]{:T(128)S(6)} %select_n.3, bf16[2,2,256,512]{3,2,1,0:T(8,128)(2,1)S(1)} %collective-permute-done.11.got_this), kind=kLoop, calls=%fused_computation.2 | loop fusion | flops 1048576 | bytes 3932164 | tf_op jit(solution)/shard_map/add | solution.py:583
  106.9 2.6 %collective-permute-done.18 = bf16[2,256,128]{2,1,0:T(8,128)(2,1)S(1)} collective-permute-done((bf16[2,256,128]{2,1,0:T(8,128)(2,1)S(1)}, bf16[2,256,128]{2,1,0:T(8,128)(2,1)S(1)}, u32[]{:S(2)}, u32[]{:S(2)}) %collective-permute-start.18) | collective-permute-done | bytes 131104 | tf_op jit(solution)/shard_map/ppermute | solution.py:575
  109.6 7.4 %collective-permute-done.19 = bf16[2,256,384]{2,1,0:T(8,128)(2,1)S(1)} collective-permute-done((bf16[2,256,384]{2,1,0:T(8,128)(2,1)S(1)}, bf16[2,256,384]{2,1,0:T(8,128)(2,1)S(1)}, u32[]{:S(2)}, u32[]{:S(2)}) %collective-permute-start.19) | collective-permute-done | bytes 393248 | tf_op jit(solution)/shard_map/ppermute | solution.py:465
  117.0 1.1 convert_add_fusion.1
  (27 shorter events, 0.5 us)
Async XLA Ops:
  0.0 4.6 %copy-start = (bf16[8,1024,256]{2,1,0:T(8,128)(2,1)S(1)}, bf16[8,1024,256]{2,1,0:T(8,128)(2,1)}, u32[]{:S(2)}) copy-start(bf16[8,1024,256]{2,1,0:T(8,128)(2,1)} %constant.19.clone.table) | copy-start | bytes 12582916
  0.9 2.4 %copy-start.1 = (f32[2,256,2048]{2,1,0:T(8,128)S(1)}, f32[2,256,2048]{2,1,0:T(8,128)}, u32[]{:S(2)}) copy-start(f32[2,256,2048]{2,1,0:T(8,128)} %spectrum.1) | copy-start | bytes 12582916
  6.5 11.5 %collective-permute-start = (bf16[4,256,128]{2,1,0:T(8,128)(2,1)S(1)}, bf16[4,256,128]{2,1,0:T(8,128)(2,1)S(1)}, u32[]{:S(2)}, u32[]{:S(2)}) collective-permute-start(bf16[4,256,128]{2,1,0:T(8,128)(2,1)S(1)} %get-tuple-element.42), channel_id=1, source_target_pairs={{8,16},{12,20},{16,8},{20,12},{4,0},{24,28},{9,17},{13,21},{17,9},... | collective-permute-start | bytes 786440 | tf_op jit(solution)/shard_map/ppermute | solution.py:465
  7.8 11.7 %collective-permute-start.1 = (bf16[4,256,128]{2,1,0:T(8,128)(2,1)S(1)}, bf16[4,256,128]{2,1,0:T(8,128)(2,1)S(1)}, u32[]{:S(2)}, u32[]{:S(2)}) collective-permute-start(bf16[4,256,128]{2,1,0:T(8,128)(2,1)S(1)} %get-tuple-element.43), channel_id=1, source_target_pairs={{4,12},{8,0},{12,4},{16,24},{20,28},{24,16},{5,13},{9,1},{13,5},{1... | collective-permute-start | bytes 786440 | tf_op jit(solution)/shard_map/ppermute | solution.py:465
  13.5 19.9 %copy-start.2 = (bf16[8,256,1024]{2,1,0:T(8,128)(2,1)S(1)}, bf16[8,256,1024]{2,1,0:T(8,128)(2,1)}, u32[]{:S(2)}) copy-start(bf16[8,256,1024]{2,1,0:T(8,128)(2,1)} %constant.18.clone.table) | copy-start | bytes 12582916
  13.5 19.9 %copy-start.5 = (f32[2,128,1024]{2,1,0:T(8,128)S(1)}, f32[2,128,1024]{2,1,0:T(8,128)}, u32[]{:S(2)}) copy-start(f32[2,128,1024]{2,1,0:T(8,128)} %images) | copy-start | bytes 3145732
  13.5 17.8 %collective-permute-start.3 = (bf16[4,256,128]{2,1,0:T(8,128)(2,1)S(1)}, bf16[4,256,128]{2,1,0:T(8,128)(2,1)S(1)}, u32[]{:S(2)}, u32[]{:S(2)}) collective-permute-start(bf16[4,256,128]{2,1,0:T(8,128)(2,1)S(1)} %get-tuple-element.53), channel_id=1, source_target_pairs={{8,20},{12,16},{16,12},{20,8},{4,0},{24,28},{9,21},{13,17},{17,13}... | collective-permute-start | bytes 786440 | tf_op jit(solution)/shard_map/ppermute | solution.py:465
  19.5 11.9 %collective-permute-start.2 = (bf16[4,256,128]{2,1,0:T(8,128)(2,1)S(1)}, bf16[4,256,128]{2,1,0:T(8,128)(2,1)S(1)}, u32[]{:S(2)}, u32[]{:S(2)}) collective-permute-start(bf16[4,256,128]{2,1,0:T(8,128)(2,1)S(1)} %get-tuple-element.52), channel_id=1, source_target_pairs={{4,0},{8,12},{12,8},{16,20},{20,16},{24,28},{5,1},{9,13},{13,9},{1... | collective-permute-start | bytes 786440 | tf_op jit(solution)/shard_map/ppermute | solution.py:465
  21.3 21.4 %collective-permute-start.4 = (bf16[4,256,128]{2,1,0:T(8,128)(2,1)S(1)}, bf16[4,256,128]{2,1,0:T(8,128)(2,1)S(1)}, u32[]{:S(2)}, u32[]{:S(2)}) collective-permute-start(bf16[4,256,128]{2,1,0:T(8,128)(2,1)S(1)} %class_4_blocks.1), channel_id=1, source_target_pairs={{0,16},{4,20},{8,24},{12,28},{16,0},{20,4},{24,8},{28,12},{1,17},{... | collective-permute-start | bytes 786440 | tf_op jit(solution)/shard_map/ppermute | solution.py:465
  24.5 22.1 %collective-permute-start.6 = (bf16[4,256,128]{2,1,0:T(8,128)(2,1)S(1)}, bf16[4,256,128]{2,1,0:T(8,128)(2,1)S(1)}, u32[]{:S(2)}, u32[]{:S(2)}) collective-permute-start(bf16[4,256,128]{2,1,0:T(8,128)(2,1)S(1)} %get-tuple-element.56.own), channel_id=1, source_target_pairs={{8,28},{12,24},{16,4},{20,0},{9,29},{13,25},{17,5},{21,1},{10,30},... | collective-permute-start | bytes 786440 | tf_op jit(solution)/shard_map/ppermute | solution.py:465
  25.8 24.4 %collective-permute-start.7 = (bf16[4,256,128]{2,1,0:T(8,128)(2,1)S(1)}, bf16[4,256,128]{2,1,0:T(8,128)(2,1)S(1)}, u32[]{:S(2)}, u32[]{:S(2)}) collective-permute-start(bf16[4,256,128]{2,1,0:T(8,128)(2,1)S(1)} %get-tuple-element.60), channel_id=1, source_target_pairs={{4,8},{8,4},{12,0},{16,28},{20,24},{24,20},{5,9},{9,5},{13,1},{17,... | collective-permute-start | bytes 786440 | tf_op jit(solution)/shard_map/ppermute | solution.py:465
  31.4 18.8 %collective-permute-start.5 = (bf16[4,256,128]{2,1,0:T(8,128)(2,1)S(1)}, bf16[4,256,128]{2,1,0:T(8,128)(2,1)S(1)}, u32[]{:S(2)}, u32[]{:S(2)}) collective-permute-start(bf16[4,256,128]{2,1,0:T(8,128)(2,1)S(1)} %class_6_blocks.1), channel_id=1, source_target_pairs={{0,24},{4,28},{24,0},{28,4},{1,25},{5,29},{25,1},{29,5},{2,26},{6,... | collective-permute-start | bytes 786440 | tf_op jit(solution)/shard_map/ppermute | solution.py:465
  55.5 10.1 %collective-permute-start.10 = (bf16[4,256,128]{2,1,0:T(8,128)(2,1)S(1)}, bf16[4,256,128]{2,1,0:T(8,128)(2,1)S(1)}, u32[]{:S(2)}, u32[]{:S(2)}) collective-permute-start(bf16[4,256,128]{2,1,0:T(8,128)(2,1)S(1)} %get-tuple-element.64), channel_id=1, source_target_pairs={{0,12},{4,8},{8,4},{12,0},{16,28},{20,24},{24,20},{28,16},{1,13},{... | collective-permute-start | bytes 786440 | tf_op jit(solution)/shard_map/ppermute | solution.py:465
  55.6 12.8 %collective-permute-start.8 = (bf16[4,256,128]{2,1,0:T(8,128)(2,1)S(1)}, bf16[4,256,128]{2,1,0:T(8,128)(2,1)S(1)}, u32[]{:S(2)}, u32[]{:S(2)}) collective-permute-start(bf16[4,256,128]{2,1,0:T(8,128)(2,1)S(1)} %get-tuple-element.62), channel_id=1, source_target_pairs={{0,4},{4,0},{8,12},{12,8},{16,20},{20,16},{24,28},{28,24},{1,5},{5... | collective-permute-start | bytes 786440 | tf_op jit(solution)/shard_map/ppermute | solution.py:465
  58.0 12.1 %collective-permute-start.9 = (bf16[4,256,128]{2,1,0:T(8,128)(2,1)S(1)}, bf16[4,256,128]{2,1,0:T(8,128)(2,1)S(1)}, u32[]{:S(2)}, u32[]{:S(2)}) collective-permute-start(bf16[4,256,128]{2,1,0:T(8,128)(2,1)S(1)} %get-tuple-element.63), channel_id=1, source_target_pairs={{0,8},{4,12},{8,0},{12,4},{16,24},{20,28},{24,16},{28,20},{1,9},{5... | collective-permute-start | bytes 786440 | tf_op jit(solution)/shard_map/ppermute | solution.py:465
  73.7 4.1 %collective-permute-start.12 = (bf16[2,2,256,512]{3,2,1,0:T(8,128)(2,1)S(1)}, bf16[2,2,256,512]{3,2,1,0:T(8,128)(2,1)S(1)}, u32[]{:S(2)}, u32[]{:S(2)}) collective-permute-start(bf16[2,2,256,512]{3,2,1,0:T(8,128)(2,1)S(1)} %get-tuple-element.69), channel_id=1, source_target_pairs={{0,1},{1,0},{2,3},{3,2},{4,5},{5,4},{6,7},{7,6},{8,9},{9,8},{10,11... | collective-permute-start | bytes 3145736 | tf_op jit(solution)/shard_map/ppermute | solution.py:543
  73.7 16.3 %collective-permute-start.11 = (bf16[2,2,256,512]{3,2,1,0:T(8,128)(2,1)}, bf16[2,2,256,512]{3,2,1,0:T(8,128)(2,1)S(1)}, u32[]{:S(2)}, u32[]{:S(2)}) collective-permute-start(bf16[2,2,256,512]{3,2,1,0:T(8,128)(2,1)} %get-tuple-element.67), channel_id=1, source_target_pairs={{0,1},{1,0},{2,3},{3,2},{4,5},{5,4},{6,7},{7,6},{8,9},{9,8},{10,11... | collective-permute-start | bytes 3145736 | tf_op jit(solution)/shard_map/ppermute | solution.py:544
  76.7 1.0 copy-start.6
  78.6 1.0 copy-start.3
  79.6 9.0 %collective-permute-start.15 = (bf16[2,2,256,128]{3,2,1,0:T(8,128)(2,1)}, bf16[2,2,256,128]{3,2,1,0:T(8,128)(2,1)}, u32[]{:S(2)}, u32[]{:S(2)}) collective-permute-start(bf16[2,2,256,128]{3,2,1,0:T(8,128)(2,1)} %z_first_kernel.1), channel_id=1, source_target_pairs={{8,12},{20,16},{9,13},{21,17},{10,14},{22,18},{11,15},{23,19}} | collective-permute-start | bytes 786440 | tf_op jit(solution)/shard_map/ppermute | solution.py:465
  81.8 12.3 %collective-permute-start.13 = (bf16[2,256,384]{2,1,0:T(8,128)(2,1)}, bf16[2,256,384]{2,1,0:T(8,128)(2,1)}, u32[]{:S(2)}, u32[]{:S(2)}) collective-permute-start(bf16[2,256,384]{2,1,0:T(8,128)(2,1)} %x_first_kernel.1), channel_id=1, source_target_pairs={{0,2},{2,0},{1,3},{3,1},{4,6},{6,4},{5,7},{7,5},{8,10},{10,8},{9,1... | collective-permute-start | bytes 1179656 | tf_op jit(solution)/shard_map/ppermute | solution.py:568
  83.3 18.6 %collective-permute-start.14 = (bf16[2,2,256,128]{3,2,1,0:T(8,128)(2,1)}, bf16[2,2,256,128]{3,2,1,0:T(8,128)(2,1)S(1)}, u32[]{:S(2)}, u32[]{:S(2)}) collective-permute-start(bf16[2,2,256,128]{3,2,1,0:T(8,128)(2,1)} %z_first_kernel.1), channel_id=1, source_target_pairs={{0,16},{4,20},{24,8},{28,12},{1,17},{5,21},{25,9},{29,13},{2,18},{... | collective-permute-start | bytes 786440 | tf_op jit(solution)/shard_map/ppermute | solution.py:465
  88.7 13.4 %collective-permute-start.16 = (bf16[2,2,256,128]{3,2,1,0:T(8,128)(2,1)}, bf16[2,2,256,128]{3,2,1,0:T(8,128)(2,1)}, u32[]{:S(2)}, u32[]{:S(2)}) collective-permute-start(bf16[2,2,256,128]{3,2,1,0:T(8,128)(2,1)} %collective-permute-done.15), channel_id=1, source_target_pairs={{12,24},{16,4},{13,25},{17,5},{14,26},{18,6},{15,27},{19,7}} | collective-permute-start | bytes 786440 | tf_op jit(solution)/shard_map/ppermute | solution.py:465
  90.0 15.4 %copy-start.7 = (f32[2,256,512]{2,1,0:T(8,128)S(1)}, f32[2,256,512]{2,1,0:T(8,128)}, u32[]{:S(2)}) copy-start(f32[2,256,512]{2,1,0:T(8,128)} %copy-done.6) | copy-start | bytes 3145732
  90.1 16.8 %collective-permute-start.17 = (bf16[2,256,384]{2,1,0:T(8,128)(2,1)S(1)}, bf16[2,256,384]{2,1,0:T(8,128)(2,1)S(1)}, u32[]{:S(2)}, u32[]{:S(2)}) collective-permute-start(bf16[2,256,384]{2,1,0:T(8,128)(2,1)S(1)} %x_own_kernel.1), channel_id=1, source_target_pairs={{0,2},{2,0},{1,3},{3,1},{4,6},{6,4},{5,7},{7,5},{8,10},{10,8},{9,1... | collective-permute-start | bytes 1179656 | tf_op jit(solution)/shard_map/ppermute | solution.py:572
  94.1 1.2 %copy-start.4 = (f32[2,256,512]{2,1,0:T(8,128)S(1)}, f32[2,256,512]{2,1,0:T(8,128)}, u32[]{:S(2)}) copy-start(f32[2,256,512]{2,1,0:T(8,128)} %copy-done.3) | copy-start | bytes 3145732
  96.4 20.6 %collective-permute-start.19 = (bf16[2,256,384]{2,1,0:T(8,128)(2,1)S(1)}, bf16[2,256,384]{2,1,0:T(8,128)(2,1)S(1)}, u32[]{:S(2)}, u32[]{:S(2)}) collective-permute-start(bf16[2,256,384]{2,1,0:T(8,128)(2,1)S(1)} %z_second_kernel.1), channel_id=1, source_target_pairs={{0,16},{4,20},{8,24},{20,4},{24,8},{28,12},{1,17},{5,21},{9,25},{2... | collective-permute-start | bytes 1179656 | tf_op jit(solution)/shard_map/ppermute | solution.py:465
  104.0 5.5 %collective-permute-start.18 = (bf16[2,256,128]{2,1,0:T(8,128)(2,1)S(1)}, bf16[2,256,128]{2,1,0:T(8,128)(2,1)S(1)}, u32[]{:S(2)}, u32[]{:S(2)}) collective-permute-start(bf16[2,256,128]{2,1,0:T(8,128)(2,1)S(1)} %x_last_kernel.1), channel_id=1, source_target_pairs={{0,2},{2,0},{1,3},{3,1},{4,6},{6,4},{5,7},{7,5},{8,10},{10,8},{9,1... | collective-permute-start | bytes 393224 | tf_op jit(solution)/shard_map/ppermute | solution.py:575

commit v15 on v12

--- a/solution.py
+++ b/solution.py
@@ -201,7 +201,7 @@
 
 def classes_of(position):
     hands_over = is_one_of(position, PASSED)
-    return (jnp.where(hands_over, 5, 6), 7, 2, 4, jnp.where(hands_over, 6, 5), 0, 1, 3)
+    return (jnp.where(hands_over, 5, 6), 7, 2, 3, 4, jnp.where(hands_over, 6, 5), 0, 1)
 
 
 def rows_kernel(which, window, table, *outs):
@@ -452,7 +452,7 @@
             name,
         )(window, by_col)
 
-    first_a, first_b, near_2 = rows_call(slice(0, 3), "rows_round_1")
+    first_a, first_b, near_2, near_3 = rows_call(slice(0, 4), "rows_round_1")
 
     def permute(sent, pairs):
         return lax.ppermute(sent, "slab", pairs)
@@ -467,14 +467,14 @@
     got_a = permute(first_a, [(s, s ^ 6) for s in INNER] + handed)
     got_b = permute(first_b, [(s, s ^ 7) for s in INNER] + handed)
     near_2 = permute(near_2, [(s, s ^ 2) for s in windowed])
-    second_a, second_b, near_0, near_1, near_3 = rows_call(slice(3, SLABS), "rows_round_2")
-    got_a, near_2, second_a, second_b, near_1, near_3, images = lax.optimization_barrier(
-        (got_a, near_2, second_a, second_b, near_1, near_3, images)
+    near_3 = permute(near_3, [(s, s ^ 3) for s in windowed])
+    second_a, second_b, near_0, near_1 = rows_call(slice(4, SLABS), "rows_round_2")
+    got_a, second_a, second_b, near_1, images = lax.optimization_barrier(
+        (got_a, second_a, second_b, near_1, images)
     )
     outer_pairs = [(s, s ^ 6) for s in range(SLABS) if s not in INNER]
     near_1 = permute(near_1, [(s, s ^ 1) for s in windowed])
-    near_3 = permute(near_3, [(s, s ^ 3) for s in windowed])
-    near_1, got_b = lax.optimization_barrier((near_1, got_b))
+    near_1, near_2, near_3, got_b = lax.optimization_barrier((near_1, near_2, near_3, got_b))
     far_columns = [
         got_a,
         got_b,

time: 113 us -> 115 us (1.018)
  starting transfers between devices: 34.4 us -> 38.1 us
  waiting for transfers between devices: 50.6 us -> 48.2 us
    ppermute x13, starting transfers between devices: 30.8 us -> 34.6 us  [permute(): return lax.ppermute(sent, 'slab', pairs)]
    ppermute x13, waiting for transfers between devices: 42.9 us -> 40.5 us  [permute(): return lax.ppermute(sent, 'slab', pairs)]
  transfers between devices with their start and end apart: 17 -> 17, of which waited for: 10 -> 11; matrix products, arithmetic and copies ran while one was open for 3% -> 3% of each run, Pallas kernels for 8% -> 7%
where the time goes in v15:
time: 115 us; the launch traced here: 114 us
  waiting for transfers between devices  48.2 us (42%)
  starting transfers between devices  38.1 us (33%)
  Pallas kernels  20 us (17%)
  other arithmetic  5.06 us (4%)
  local copies, waits for them, and re-layouts  2.42 us (2%)
    ppermute x13, waiting for transfers between devices, permute(): return lax.ppermute(sent, 'slab', pairs)  40.5 us
    ppermute x13, starting transfers between devices, permute(): return lax.ppermute(sent, 'slab', pairs)  34.6 us
    ppermute x2, waiting for transfers between devices, body_slabs(): got_x = lax.ppermute(over, 'led', planes)  7.78 us
    pallas_call x1, Pallas kernels, body_slabs(): local_call(field_kernel, [sent_block] * HALF, [vmem] * 11, [pltpu.VMEM((w...  5.31 us
    pallas_call x2, Pallas kernels, rows_call(): local_call(functools.partial(rows_kernel, which), [sent_block] * count, [...  4.69 us
    pallas_call x4, Pallas kernels, sum_call(): local_call(kernel, out_shape, specs, [], 0, 2 ** 20, kernel.__name__)  3 us
    ppermute x2, starting transfers between devices, body_slabs(): got_x = lax.ppermute(over, 'led', planes)  2.96 us
    pallas_call x1, Pallas kernels, body_slabs(): local_call(sent_kernel, [jax.ShapeDtypeStruct((2,) + piece, bf16), jax.Sh...  2.64 us
  transfers between devices with their start and end apart: 17, of which 11 were waited for; matrix products, arithmetic and copies ran while one was open for 3% of the time, Pallas kernels for 7%

profile of v15, /device:TPU:4, one launch (start us, length us, event | category | flops | bytes accessed | tf_op | source)
XLA Modules:
  0.0 114.1 jit_solution(8889087591509267107)
XLA Ops:
  0.0 0.9 pad_add_fusion.starts
  0.9 2.4 %copy-done.1 = f32[2,256,2048]{2,1,0:T(8,128)S(1)} copy-done((f32[2,256,2048]{2,1,0:T(8,128)S(1)}, f32[2,256,2048]{2,1,0:T(8,128)}, u32[]{:S(2)}) %copy-start.1) | copy-done | bytes 4194328
  3.3 1.4 %windows.1.window = bf16[1024,1024]{1,0:T(8,128)(2,1)S(1)} custom-call(s32[4]{0:T(128)S(1)} %pad_add_fusion.starts, f32[2,256,2048]{2,1,0:T(8,128)S(1)} %copy-done.1), custom_call_target="tpu_custom_call" | custom-call | bytes 6291456 | tf_op jit(solution)/shard_map/windows/pallas_call | solution.py:433
  4.7 2.3 %rows_round_1.1 = (bf16[4,256,128]{2,1,0:T(8,128)(2,1)S(1)}, bf16[4,256,128]{2,1,0:T(8,128)(2,1)S(1)}, bf16[4,256,128]{2,1,0:T(8,128)(2,1)S(1)}, bf16[4,256,128]{2,1,0:T(8,128)(2,1)S(1)}) custom-call(bf16[1024,1024]{1,0:T(8,128)(2,1)S(1)} %windows.1.window, bf16[8,1024,256]{2,1,0:T(8,128)(2,1)S(1)} %copy-done), custom_call_target="tpu_custom_call" | custom-call | flops 2147483648 | bytes 5242880 | tf_op jit(solution)/shard_map/rows_round_1/pallas_call | solution.py:445
  7.0 1.3 %collective-permute-start = (bf16[4,256,128]{2,1,0:T(8,128)(2,1)S(1)}, bf16[4,256,128]{2,1,0:T(8,128)(2,1)S(1)}, u32[]{:S(2)}, u32[]{:S(2)}) collective-permute-start(bf16[4,256,128]{2,1,0:T(8,128)(2,1)S(1)} %get-tuple-element.39), channel_id=1, source_target_pairs={{8,16},{12,20},{16,8},{20,12},{4,0},{24,28},{9,17},{13,21},{17,9},... | collective-permute-start | bytes 786440 | tf_op jit(solution)/shard_map/ppermute | solution.py:458
  8.3 5.7 %collective-permute-start.2 = (bf16[4,256,128]{2,1,0:T(8,128)(2,1)S(1)}, bf16[4,256,128]{2,1,0:T(8,128)(2,1)S(1)}, u32[]{:S(2)}, u32[]{:S(2)}) collective-permute-start(bf16[4,256,128]{2,1,0:T(8,128)(2,1)S(1)} %get-tuple-element.48), channel_id=1, source_target_pairs={{4,12},{8,0},{12,4},{16,24},{20,28},{24,16},{5,13},{9,1},{13,5},{1... | collective-permute-start | bytes 786440 | tf_op jit(solution)/shard_map/ppermute | solution.py:458
  14.0 1.9 %collective-permute-start.3 = (bf16[4,256,128]{2,1,0:T(8,128)(2,1)S(1)}, bf16[4,256,128]{2,1,0:T(8,128)(2,1)S(1)}, u32[]{:S(2)}, u32[]{:S(2)}) collective-permute-start(bf16[4,256,128]{2,1,0:T(8,128)(2,1)S(1)} %get-tuple-element.49), channel_id=1, source_target_pairs={{4,8},{8,4},{12,0},{16,28},{20,24},{24,20},{5,9},{9,5},{13,1},{17,... | collective-permute-start | bytes 786440 | tf_op jit(solution)/shard_map/ppermute | solution.py:458
  15.9 0.0 copy-start.2
  15.9 0.0 copy-start.3
  15.9 1.6 %collective-permute-start.4 = (bf16[4,256,128]{2,1,0:T(8,128)(2,1)S(1)}, bf16[4,256,128]{2,1,0:T(8,128)(2,1)S(1)}, u32[]{:S(2)}, u32[]{:S(2)}) collective-permute-start(bf16[4,256,128]{2,1,0:T(8,128)(2,1)S(1)} %get-tuple-element.50), channel_id=1, source_target_pairs={{8,20},{12,16},{16,12},{20,8},{4,0},{24,28},{9,21},{13,17},{17,13}... | collective-permute-start | bytes 786440 | tf_op jit(solution)/shard_map/ppermute | solution.py:458
  17.5 2.3 %rows_round_2.1 = (bf16[4,256,128]{2,1,0:T(8,128)(2,1)S(1)}, bf16[4,256,128]{2,1,0:T(8,128)(2,1)S(1)}, bf16[4,256,128]{2,1,0:T(8,128)(2,1)S(1)}, bf16[4,256,128]{2,1,0:T(8,128)(2,1)S(1)}) custom-call(bf16[1024,1024]{1,0:T(8,128)(2,1)S(1)} %windows.1.window, bf16[8,1024,256]{2,1,0:T(8,128)(2,1)S(1)} %copy-done), custom_call_target="tpu_custom_call" | custom-call | flops 2147483648 | bytes 5242880 | tf_op jit(solution)/shard_map/rows_round_2/pallas_call | solution.py:445
  19.9 1.3 %collective-permute-start.1 = (bf16[4,256,128]{2,1,0:T(8,128)(2,1)S(1)}, bf16[4,256,128]{2,1,0:T(8,128)(2,1)S(1)}, u32[]{:S(2)}, u32[]{:S(2)}) collective-permute-start(bf16[4,256,128]{2,1,0:T(8,128)(2,1)S(1)} %get-tuple-element.47), channel_id=1, source_target_pairs={{4,0},{8,12},{12,8},{16,20},{20,16},{24,28},{5,1},{9,13},{13,9},{1... | collective-permute-start | bytes 786440 | tf_op jit(solution)/shard_map/ppermute | solution.py:458
  21.2 5.7 %collective-permute-start.5 = (bf16[4,256,128]{2,1,0:T(8,128)(2,1)S(1)}, bf16[4,256,128]{2,1,0:T(8,128)(2,1)S(1)}, u32[]{:S(2)}, u32[]{:S(2)}) collective-permute-start(bf16[4,256,128]{2,1,0:T(8,128)(2,1)S(1)} %class_4_blocks.1), channel_id=1, source_target_pairs={{0,16},{4,20},{8,24},{12,28},{16,0},{20,4},{24,8},{28,12},{1,17},{... | collective-permute-start | bytes 786440 | tf_op jit(solution)/shard_map/ppermute | solution.py:458
  26.9 0.0 collective-permute-done.2.rest_7_
  26.9 1.3 %collective-permute-start.7 = (bf16[4,256,128]{2,1,0:T(8,128)(2,1)S(1)}, bf16[4,256,128]{2,1,0:T(8,128)(2,1)S(1)}, u32[]{:S(2)}, u32[]{:S(2)}) collective-permute-start(bf16[4,256,128]{2,1,0:T(8,128)(2,1)S(1)} %get-tuple-element.53.own), channel_id=1, source_target_pairs={{8,28},{12,24},{16,4},{20,0},{9,29},{13,25},{17,5},{21,1},{10,30},... | collective-permute-start | bytes 786440 | tf_op jit(solution)/shard_map/ppermute | solution.py:458
  28.2 0.2 collective-permute-done.3.rest_8_
  28.4 1.1 collective-permute-done.4.got.rest_1_
  29.5 4.5 %collective-permute-done.1.rest_6_ = bf16[4,256,128]{2,1,0:T(8,128)(2,1)S(1)} collective-permute-done((bf16[4,256,128]{2,1,0:T(8,128)(2,1)S(1)}, bf16[4,256,128]{2,1,0:T(8,128)(2,1)S(1)}, u32[]{:S(2)}, u32[]{:S(2)}) %collective-permute-start.1) | collective-permute-done | bytes 262176 | tf_op jit(solution)/shard_map/ppermute | solution.py:458
  34.0 5.7 %collective-permute-start.6 = (bf16[4,256,128]{2,1,0:T(8,128)(2,1)S(1)}, bf16[4,256,128]{2,1,0:T(8,128)(2,1)S(1)}, u32[]{:S(2)}, u32[]{:S(2)}) collective-permute-start(bf16[4,256,128]{2,1,0:T(8,128)(2,1)S(1)} %class_6_blocks.1), channel_id=1, source_target_pairs={{0,24},{4,28},{24,0},{28,4},{1,25},{5,29},{25,1},{29,5},{2,26},{6,... | collective-permute-start | bytes 786440 | tf_op jit(solution)/shard_map/ppermute | solution.py:458
  39.8 0.6 amplitude.1
  40.3 8.6 %collective-permute-done.5.rest_2_ = bf16[4,256,128]{2,1,0:T(8,128)(2,1)S(1)} collective-permute-done((bf16[4,256,128]{2,1,0:T(8,128)(2,1)S(1)}, bf16[4,256,128]{2,1,0:T(8,128)(2,1)S(1)}, u32[]{:S(2)}, u32[]{:S(2)}) %collective-permute-start.5) | collective-permute-done | bytes 262176 | tf_op jit(solution)/shard_map/ppermute | solution.py:458
  48.9 1.2 %collective-permute-done.7.rest_4_ = bf16[4,256,128]{2,1,0:T(8,128)(2,1)S(1)} collective-permute-done((bf16[4,256,128]{2,1,0:T(8,128)(2,1)S(1)}, bf16[4,256,128]{2,1,0:T(8,128)(2,1)S(1)}, u32[]{:S(2)}, u32[]{:S(2)}) %collective-permute-start.7) | collective-permute-done | bytes 262176 | tf_op jit(solution)/shard_map/ppermute | solution.py:458
  50.1 5.3 %modulus_step.1 = (bf16[4,256,128]{2,1,0:T(8,128)(2,1)S(1)}, bf16[4,256,128]{2,1,0:T(8,128)(2,1)S(1)}, bf16[4,256,128]{2,1,0:T(8,128)(2,1)S(1)}, bf16[4,256,128]{2,1,0:T(8,128)(2,1)S(1)}) custom-call(f32[1024,256]{1,0:T(8,128)S(1)} %get-tuple-element.44.amplitude, bf16[8,256,1024]{2,1,0:T(8,128)(2,1)S(1)} %get-tuple-element.45.table, ...), custom_call_target="tpu_custom_call" | custom-call | flops 4294967296 | bytes 12582912 | tf_op jit(solution)/shard_map/modulus_step/pallas_call | solution.py:498
  55.4 2.5 %collective-permute-start.10 = (bf16[4,256,128]{2,1,0:T(8,128)(2,1)S(1)}, bf16[4,256,128]{2,1,0:T(8,128)(2,1)S(1)}, u32[]{:S(2)}, u32[]{:S(2)}) collective-permute-start(bf16[4,256,128]{2,1,0:T(8,128)(2,1)S(1)} %get-tuple-element.61), channel_id=1, source_target_pairs={{0,12},{4,8},{8,4},{12,0},{16,28},{20,24},{24,20},{28,16},{1,13},{... | collective-permute-start | bytes 786440 | tf_op jit(solution)/shard_map/ppermute | solution.py:458
  57.9 1.9 %collective-permute-start.8 = (bf16[4,256,128]{2,1,0:T(8,128)(2,1)S(1)}, bf16[4,256,128]{2,1,0:T(8,128)(2,1)S(1)}, u32[]{:S(2)}, u32[]{:S(2)}) collective-permute-start(bf16[4,256,128]{2,1,0:T(8,128)(2,1)S(1)} %get-tuple-element.59), channel_id=1, source_target_pairs={{0,4},{4,0},{8,12},{12,8},{16,20},{20,16},{24,28},{28,24},{1,5},{5... | collective-permute-start | bytes 786440 | tf_op jit(solution)/shard_map/ppermute | solution.py:458
  59.7 1.4 %collective-permute-start.9 = (bf16[4,256,128]{2,1,0:T(8,128)(2,1)S(1)}, bf16[4,256,128]{2,1,0:T(8,128)(2,1)S(1)}, u32[]{:S(2)}, u32[]{:S(2)}) collective-permute-start(bf16[4,256,128]{2,1,0:T(8,128)(2,1)S(1)} %get-tuple-element.60), channel_id=1, source_target_pairs={{0,8},{4,12},{8,0},{12,4},{16,24},{20,28},{24,16},{28,20},{1,9},{5... | collective-permute-start | bytes 786440 | tf_op jit(solution)/shard_map/ppermute | solution.py:458
  61.1 3.6 %collective-permute-done.10.rest_3_ = bf16[4,256,128]{2,1,0:T(8,128)(2,1)S(1)} collective-permute-done((bf16[4,256,128]{2,1,0:T(8,128)(2,1)S(1)}, bf16[4,256,128]{2,1,0:T(8,128)(2,1)S(1)}, u32[]{:S(2)}, u32[]{:S(2)}) %collective-permute-start.10) | collective-permute-done | bytes 262176 | tf_op jit(solution)/shard_map/ppermute | solution.py:458
  64.7 4.8 %collective-permute-done.8.rest_1_ = bf16[4,256,128]{2,1,0:T(8,128)(2,1)S(1)} collective-permute-done((bf16[4,256,128]{2,1,0:T(8,128)(2,1)S(1)}, bf16[4,256,128]{2,1,0:T(8,128)(2,1)S(1)}, u32[]{:S(2)}, u32[]{:S(2)}) %collective-permute-start.8) | collective-permute-done | bytes 262176 | tf_op jit(solution)/shard_map/ppermute | solution.py:458
  69.5 1.9 %collective-permute-done.9.rest_2_ = bf16[4,256,128]{2,1,0:T(8,128)(2,1)S(1)} collective-permute-done((bf16[4,256,128]{2,1,0:T(8,128)(2,1)S(1)}, bf16[4,256,128]{2,1,0:T(8,128)(2,1)S(1)}, u32[]{:S(2)}, u32[]{:S(2)}) %collective-permute-start.9) | collective-permute-done | bytes 262176 | tf_op jit(solution)/shard_map/ppermute | solution.py:458
  71.4 2.6 %update_sent.1 = (bf16[2,2,256,512]{3,2,1,0:T(8,128)(2,1)S(1)}, bf16[2,2,256,512]{3,2,1,0:T(8,128)(2,1)S(1)}, bf16[1024,512]{1,0:T(8,128)(2,1)S(1)}) custom-call(s32[4]{0:T(128)S(1)} %pad_add_fusion.starts, bf16[8,1024,256]{2,1,0:T(8,128)(2,1)S(1)} %copy-done, bf16[4,256,128]{2,1,0:T(8,128)(2,1)S(1)} %get-tuple-element.58.rest_0_, ...), custom_call_target="tpu_custom_call" | custom-call | flops 1073741824 | bytes 8388608 | tf_op jit(solution)/shard_map/update_sent/pallas_call | solution.py:523
  74.0 0.1 collective-permute-start.12
  74.1 0.5 collective-permute-start.11
  74.6 2.4 %update_kept.1 = (f32[2,256,512]{2,1,0:T(8,128)S(1)}, f32[2,256,512]{2,1,0:T(8,128)S(1)}, f32[2,256,512]{2,1,0:T(8,128)S(1)}, f32[2,256,512]{2,1,0:T(8,128)S(1)}) custom-call(s32[4]{0:T(128)S(1)} %pad_add_fusion.starts, bf16[8,1024,256]{2,1,0:T(8,128)(2,1)S(1)} %copy-done, bf16[1024,512]{1,0:T(8,128)(2,1)S(1)} %get-tuple-element.62.back), custom_call_target="tpu_custom_call" | custom-call | flops 1073741824 | bytes 10485760 | tf_op jit(solution)/shard_map/update_kept/pallas_call | solution.py:538
  77.1 0.0 copy-start.4
  77.1 0.1 z_first_kernel.1
  77.2 2.6 %collective-permute-start.13 = (bf16[2,2,256,128]{3,2,1,0:T(8,128)(2,1)S(1)}, bf16[2,2,256,128]{3,2,1,0:T(8,128)(2,1)S(1)}, u32[]{:S(2)}, u32[]{:S(2)}) collective-permute-start(bf16[2,2,256,128]{3,2,1,0:T(8,128)(2,1)S(1)} %z_first_kernel.1), channel_id=1, source_target_pairs={{0,16},{4,20},{8,24},{20,4},{24,8},{28,12},{1,17},{5,21},{9,25},{2... | collective-permute-start | bytes 786440 | tf_op jit(solution)/shard_map/ppermute | solution.py:458
  79.8 0.8 x_first_kernel.1
  80.6 1.5 %collective-permute-start.15 = (bf16[2,256,384]{2,1,0:T(8,128)(2,1)}, bf16[2,256,384]{2,1,0:T(8,128)(2,1)}, u32[]{:S(2)}, u32[]{:S(2)}) collective-permute-start(bf16[2,256,384]{2,1,0:T(8,128)(2,1)} %x_first_kernel.1), channel_id=1, source_target_pairs={{0,2},{2,0},{1,3},{3,1},{4,6},{6,4},{5,7},{7,5},{8,10},{10,8},{9,1... | collective-permute-start | bytes 1179656 | tf_op jit(solution)/shard_map/ppermute | solution.py:556
  82.1 11.5 %collective-permute-done.13.got_z = bf16[2,2,256,128]{3,2,1,0:T(8,128)(2,1)S(1)} collective-permute-done((bf16[2,2,256,128]{3,2,1,0:T(8,128)(2,1)S(1)}, bf16[2,2,256,128]{3,2,1,0:T(8,128)(2,1)S(1)}, u32[]{:S(2)}, u32[]{:S(2)}) %collective-permute-start.13) | collective-permute-done | bytes 262176 | tf_op jit(solution)/shard_map/ppermute | solution.py:458
  93.6 1.0 x_second_kernel.1
  94.5 1.5 %collective-permute-start.14 = (bf16[2,256,512]{2,1,0:T(8,128)(2,1)}, bf16[2,256,512]{2,1,0:T(8,128)(2,1)}, u32[]{:S(2)}, u32[]{:S(2)}) collective-permute-start(bf16[2,256,512]{2,1,0:T(8,128)(2,1)} %x_second_kernel.1), channel_id=1, source_target_pairs={{0,2},{2,0},{1,3},{3,1},{4,6},{6,4},{5,7},{7,5},{8,10},{10,8},{9,1... | collective-permute-start | bytes 1572872 | tf_op jit(solution)/shard_map/ppermute | solution.py:560
  96.0 1.1 z_second_kernel.1
  97.2 1.9 %collective-permute-start.16 = (bf16[2,256,384]{2,1,0:T(8,128)(2,1)S(1)}, bf16[2,256,384]{2,1,0:T(8,128)(2,1)S(1)}, u32[]{:S(2)}, u32[]{:S(2)}) collective-permute-start(bf16[2,256,384]{2,1,0:T(8,128)(2,1)S(1)} %z_second_kernel.1), channel_id=1, source_target_pairs={{0,16},{4,20},{8,24},{20,4},{24,8},{28,12},{1,17},{5,21},{9,25},{2... | collective-permute-start | bytes 1179656 | tf_op jit(solution)/shard_map/ppermute | solution.py:458
  99.1 1.8 %fusion.1 = f32[2,256,512]{2,1,0:T(8,128)S(1)} fusion(f32[2,256,512]{2,1,0:T(8,128)} %copy-done.4, f32[2,256,2048]{2,1,0:T(8,128)} %spectrum.1, s32[]{:T(128)S(6)} %select_n.3, bf16[2,2,256,512]{3,2,1,0:T(8,128)(2,1)S(1)} %collective-permute-done.11.got_this, bf16[2,256,128]{2,1,0:T(8,128)(2,1)S(1)} %slice_bitcast_fusion.1), kind=kLoop, calls=%fused_computation.2 | loop fusion | flops 1310720 | bytes 3801092 | tf_op jit(solution)/shard_map/add | solution.py:567
  100.9 7.8 %collective-permute-done.14 = bf16[2,256,512]{2,1,0:T(8,128)(2,1)} collective-permute-done((bf16[2,256,512]{2,1,0:T(8,128)(2,1)}, bf16[2,256,512]{2,1,0:T(8,128)(2,1)}, u32[]{:S(2)}, u32[]{:S(2)}) %collective-permute-start.14) | collective-permute-done | bytes 524320 | tf_op jit(solution)/shard_map/ppermute | solution.py:560
  108.7 1.2 %convert_add_fusion.2 = f32[2,256,512]{2,1,0:T(8,128)S(1)} fusion(f32[2,256,512]{2,1,0:T(8,128)S(1)} %fusion.1, bf16[2,256,512]{2,1,0:T(8,128)(2,1)} %collective-permute-done.14), kind=kLoop, calls=%fused_computation.4 | loop fusion | flops 524288 | bytes 2621440 | tf_op jit(solution)/shard_map/add | solution.py:569
  109.9 3.1 %collective-permute-done.16 = bf16[2,256,384]{2,1,0:T(8,128)(2,1)S(1)} collective-permute-done((bf16[2,256,384]{2,1,0:T(8,128)(2,1)S(1)}, bf16[2,256,384]{2,1,0:T(8,128)(2,1)S(1)}, u32[]{:S(2)}, u32[]{:S(2)}) %collective-permute-start.16) | collective-permute-done | bytes 393248 | tf_op jit(solution)/shard_map/ppermute | solution.py:458
  113.0 1.1 convert_add_fusion.1
  (14 shorter events, 0.1 us)
Async XLA Ops:
  0.0 4.6 %copy-start = (bf16[8,1024,256]{2,1,0:T(8,128)(2,1)S(1)}, bf16[8,1024,256]{2,1,0:T(8,128)(2,1)}, u32[]{:S(2)}) copy-start(bf16[8,1024,256]{2,1,0:T(8,128)(2,1)} %constant.18.clone.table) | copy-start | bytes 12582916
  0.9 2.4 %copy-start.1 = (f32[2,256,2048]{2,1,0:T(8,128)S(1)}, f32[2,256,2048]{2,1,0:T(8,128)}, u32[]{:S(2)}) copy-start(f32[2,256,2048]{2,1,0:T(8,128)} %spectrum.1) | copy-start | bytes 12582916
  7.0 12.9 %collective-permute-start = (bf16[4,256,128]{2,1,0:T(8,128)(2,1)S(1)}, bf16[4,256,128]{2,1,0:T(8,128)(2,1)S(1)}, u32[]{:S(2)}, u32[]{:S(2)}) collective-permute-start(bf16[4,256,128]{2,1,0:T(8,128)(2,1)S(1)} %get-tuple-element.39), channel_id=1, source_target_pairs={{8,16},{12,20},{16,8},{20,12},{4,0},{24,28},{9,17},{13,21},{17,9},... | collective-permute-start | bytes 786440 | tf_op jit(solution)/shard_map/ppermute | solution.py:458
  8.3 18.6 %collective-permute-start.2 = (bf16[4,256,128]{2,1,0:T(8,128)(2,1)S(1)}, bf16[4,256,128]{2,1,0:T(8,128)(2,1)S(1)}, u32[]{:S(2)}, u32[]{:S(2)}) collective-permute-start(bf16[4,256,128]{2,1,0:T(8,128)(2,1)S(1)} %get-tuple-element.48), channel_id=1, source_target_pairs={{4,12},{8,0},{12,4},{16,24},{20,28},{24,16},{5,13},{9,1},{13,5},{1... | collective-permute-start | bytes 786440 | tf_op jit(solution)/shard_map/ppermute | solution.py:458
  14.0 14.4 %collective-permute-start.3 = (bf16[4,256,128]{2,1,0:T(8,128)(2,1)S(1)}, bf16[4,256,128]{2,1,0:T(8,128)(2,1)S(1)}, u32[]{:S(2)}, u32[]{:S(2)}) collective-permute-start(bf16[4,256,128]{2,1,0:T(8,128)(2,1)S(1)} %get-tuple-element.49), channel_id=1, source_target_pairs={{4,8},{8,4},{12,0},{16,28},{20,24},{24,20},{5,9},{9,5},{13,1},{17,... | collective-permute-start | bytes 786440 | tf_op jit(solution)/shard_map/ppermute | solution.py:458
  15.9 23.8 %copy-start.2 = (bf16[8,256,1024]{2,1,0:T(8,128)(2,1)S(1)}, bf16[8,256,1024]{2,1,0:T(8,128)(2,1)}, u32[]{:S(2)}) copy-start(bf16[8,256,1024]{2,1,0:T(8,128)(2,1)} %constant.17.clone.table) | copy-start | bytes 12582916
  15.9 23.8 %copy-start.3 = (f32[2,128,1024]{2,1,0:T(8,128)S(1)}, f32[2,128,1024]{2,1,0:T(8,128)}, u32[]{:S(2)}) copy-start(f32[2,128,1024]{2,1,0:T(8,128)} %images) | copy-start | bytes 3145732
  15.9 13.5 %collective-permute-start.4 = (bf16[4,256,128]{2,1,0:T(8,128)(2,1)S(1)}, bf16[4,256,128]{2,1,0:T(8,128)(2,1)S(1)}, u32[]{:S(2)}, u32[]{:S(2)}) collective-permute-start(bf16[4,256,128]{2,1,0:T(8,128)(2,1)S(1)} %get-tuple-element.50), channel_id=1, source_target_pairs={{8,20},{12,16},{16,12},{20,8},{4,0},{24,28},{9,21},{13,17},{17,13}... | collective-permute-start | bytes 786440 | tf_op jit(solution)/shard_map/ppermute | solution.py:458
  19.9 14.1 %collective-permute-start.1 = (bf16[4,256,128]{2,1,0:T(8,128)(2,1)S(1)}, bf16[4,256,128]{2,1,0:T(8,128)(2,1)S(1)}, u32[]{:S(2)}, u32[]{:S(2)}) collective-permute-start(bf16[4,256,128]{2,1,0:T(8,128)(2,1)S(1)} %get-tuple-element.47), channel_id=1, source_target_pairs={{4,0},{8,12},{12,8},{16,20},{20,16},{24,28},{5,1},{9,13},{13,9},{1... | collective-permute-start | bytes 786440 | tf_op jit(solution)/shard_map/ppermute | solution.py:458
  21.2 27.7 %collective-permute-start.5 = (bf16[4,256,128]{2,1,0:T(8,128)(2,1)S(1)}, bf16[4,256,128]{2,1,0:T(8,128)(2,1)S(1)}, u32[]{:S(2)}, u32[]{:S(2)}) collective-permute-start(bf16[4,256,128]{2,1,0:T(8,128)(2,1)S(1)} %class_4_blocks.1), channel_id=1, source_target_pairs={{0,16},{4,20},{8,24},{12,28},{16,0},{20,4},{24,8},{28,12},{1,17},{... | collective-permute-start | bytes 786440 | tf_op jit(solution)/shard_map/ppermute | solution.py:458
  26.9 23.2 %collective-permute-start.7 = (bf16[4,256,128]{2,1,0:T(8,128)(2,1)S(1)}, bf16[4,256,128]{2,1,0:T(8,128)(2,1)S(1)}, u32[]{:S(2)}, u32[]{:S(2)}) collective-permute-start(bf16[4,256,128]{2,1,0:T(8,128)(2,1)S(1)} %get-tuple-element.53.own), channel_id=1, source_target_pairs={{8,28},{12,24},{16,4},{20,0},{9,29},{13,25},{17,5},{21,1},{10,30},... | collective-permute-start | bytes 786440 | tf_op jit(solution)/shard_map/ppermute | solution.py:458
  34.0 16.1 %collective-permute-start.6 = (bf16[4,256,128]{2,1,0:T(8,128)(2,1)S(1)}, bf16[4,256,128]{2,1,0:T(8,128)(2,1)S(1)}, u32[]{:S(2)}, u32[]{:S(2)}) collective-permute-start(bf16[4,256,128]{2,1,0:T(8,128)(2,1)S(1)} %class_6_blocks.1), channel_id=1, source_target_pairs={{0,24},{4,28},{24,0},{28,4},{1,25},{5,29},{25,1},{29,5},{2,26},{6,... | collective-permute-start | bytes 786440 | tf_op jit(solution)/shard_map/ppermute | solution.py:458
  55.4 9.3 %collective-permute-start.10 = (bf16[4,256,128]{2,1,0:T(8,128)(2,1)S(1)}, bf16[4,256,128]{2,1,0:T(8,128)(2,1)S(1)}, u32[]{:S(2)}, u32[]{:S(2)}) collective-permute-start(bf16[4,256,128]{2,1,0:T(8,128)(2,1)S(1)} %get-tuple-element.61), channel_id=1, source_target_pairs={{0,12},{4,8},{8,4},{12,0},{16,28},{20,24},{24,20},{28,16},{1,13},{... | collective-permute-start | bytes 786440 | tf_op jit(solution)/shard_map/ppermute | solution.py:458
  57.9 11.6 %collective-permute-start.8 = (bf16[4,256,128]{2,1,0:T(8,128)(2,1)S(1)}, bf16[4,256,128]{2,1,0:T(8,128)(2,1)S(1)}, u32[]{:S(2)}, u32[]{:S(2)}) collective-permute-start(bf16[4,256,128]{2,1,0:T(8,128)(2,1)S(1)} %get-tuple-element.59), channel_id=1, source_target_pairs={{0,4},{4,0},{8,12},{12,8},{16,20},{20,16},{24,28},{28,24},{1,5},{5... | collective-permute-start | bytes 786440 | tf_op jit(solution)/shard_map/ppermute | solution.py:458
  59.7 11.6 %collective-permute-start.9 = (bf16[4,256,128]{2,1,0:T(8,128)(2,1)S(1)}, bf16[4,256,128]{2,1,0:T(8,128)(2,1)S(1)}, u32[]{:S(2)}, u32[]{:S(2)}) collective-permute-start(bf16[4,256,128]{2,1,0:T(8,128)(2,1)S(1)} %get-tuple-element.60), channel_id=1, source_target_pairs={{0,8},{4,12},{8,0},{12,4},{16,24},{20,28},{24,16},{28,20},{1,9},{5... | collective-permute-start | bytes 786440 | tf_op jit(solution)/shard_map/ppermute | solution.py:458
  74.0 3.0 %collective-permute-start.12 = (bf16[2,2,256,512]{3,2,1,0:T(8,128)(2,1)S(1)}, bf16[2,2,256,512]{3,2,1,0:T(8,128)(2,1)S(1)}, u32[]{:S(2)}, u32[]{:S(2)}) collective-permute-start(bf16[2,2,256,512]{3,2,1,0:T(8,128)(2,1)S(1)} %get-tuple-element.67), channel_id=1, source_target_pairs={{0,1},{1,0},{2,3},{3,2},{4,5},{5,4},{6,7},{7,6},{8,9},{9,8},{10,11... | collective-permute-start | bytes 3145736 | tf_op jit(solution)/shard_map/ppermute | solution.py:536
  74.1 8.0 %collective-permute-start.11 = (bf16[2,2,256,512]{3,2,1,0:T(8,128)(2,1)S(1)}, bf16[2,2,256,512]{3,2,1,0:T(8,128)(2,1)S(1)}, u32[]{:S(2)}, u32[]{:S(2)}) collective-permute-start(bf16[2,2,256,512]{3,2,1,0:T(8,128)(2,1)S(1)} %get-tuple-element.64), channel_id=1, source_target_pairs={{0,1},{1,0},{2,3},{3,2},{4,5},{5,4},{6,7},{7,6},{8,9},{9,8},{10,11... | collective-permute-start | bytes 3145736 | tf_op jit(solution)/shard_map/ppermute | solution.py:537
  77.1 5.0 %copy-start.4 = (f32[2,256,512]{2,1,0:T(8,128)}, f32[2,256,512]{2,1,0:T(8,128)S(1)}, u32[]{:S(2)}) copy-start(f32[2,256,512]{2,1,0:T(8,128)S(1)} %get-tuple-element.63) | copy-start | bytes 3145732
  77.2 16.4 %collective-permute-start.13 = (bf16[2,2,256,128]{3,2,1,0:T(8,128)(2,1)S(1)}, bf16[2,2,256,128]{3,2,1,0:T(8,128)(2,1)S(1)}, u32[]{:S(2)}, u32[]{:S(2)}) collective-permute-start(bf16[2,2,256,128]{3,2,1,0:T(8,128)(2,1)S(1)} %z_first_kernel.1), channel_id=1, source_target_pairs={{0,16},{4,20},{8,24},{20,4},{24,8},{28,12},{1,17},{5,21},{9,25},{2... | collective-permute-start | bytes 786440 | tf_op jit(solution)/shard_map/ppermute | solution.py:458
  80.6 15.4 %collective-permute-start.15 = (bf16[2,256,384]{2,1,0:T(8,128)(2,1)}, bf16[2,256,384]{2,1,0:T(8,128)(2,1)}, u32[]{:S(2)}, u32[]{:S(2)}) collective-permute-start(bf16[2,256,384]{2,1,0:T(8,128)(2,1)} %x_first_kernel.1), channel_id=1, source_target_pairs={{0,2},{2,0},{1,3},{3,1},{4,6},{6,4},{5,7},{7,5},{8,10},{10,8},{9,1... | collective-permute-start | bytes 1179656 | tf_op jit(solution)/shard_map/ppermute | solution.py:556
  94.5 14.2 %collective-permute-start.14 = (bf16[2,256,512]{2,1,0:T(8,128)(2,1)}, bf16[2,256,512]{2,1,0:T(8,128)(2,1)}, u32[]{:S(2)}, u32[]{:S(2)}) collective-permute-start(bf16[2,256,512]{2,1,0:T(8,128)(2,1)} %x_second_kernel.1), channel_id=1, source_target_pairs={{0,2},{2,0},{1,3},{3,1},{4,6},{6,4},{5,7},{7,5},{8,10},{10,8},{9,1... | collective-permute-start | bytes 1572872 | tf_op jit(solution)/shard_map/ppermute | solution.py:560
  97.2 15.8 %collective-permute-start.16 = (bf16[2,256,384]{2,1,0:T(8,128)(2,1)S(1)}, bf16[2,256,384]{2,1,0:T(8,128)(2,1)S(1)}, u32[]{:S(2)}, u32[]{:S(2)}) collective-permute-start(bf16[2,256,384]{2,1,0:T(8,128)(2,1)S(1)} %z_second_kernel.1), channel_id=1, source_target_pairs={{0,16},{4,20},{8,24},{20,4},{24,8},{28,12},{1,17},{5,21},{9,25},{2... | collective-permute-start | bytes 1179656 | tf_op jit(solution)/shard_map/ppermute | solution.py:458

commit v16 on v12

--- a/solution.py
+++ b/solution.py
@@ -259,15 +259,15 @@
 
     @pl.when(is_one_of(position, INNER))
     def _():
-        add(far[0], jnp.bitwise_xor(position, 6))
-        add(far[1], jnp.bitwise_xor(position, 7))
-        add(far[2], jnp.bitwise_xor(position, jnp.where(ends, 5, 4)))
+        add(far[1], jnp.bitwise_xor(position, 6))
+        add(far[2], jnp.bitwise_xor(position, 7))
+        add(far[3], jnp.bitwise_xor(position, jnp.where(ends, 5, 4)))
 
     @pl.when(jnp.logical_or(passes, hands_over))
     def _():
-        add(far[2], jnp.bitwise_xor(position, 4))
-        add(far[3], jnp.bitwise_xor(position, jnp.where(hands_over, 7, 6)))
-        add(far[4], jnp.bitwise_xor(position, 5))
+        add(far[3], jnp.bitwise_xor(position, 4))
+        add(far[4], jnp.bitwise_xor(position, jnp.where(hands_over, 7, 6)))
+        add(far[0], jnp.bitwise_xor(position, 5))
 
     for first in range(0, steps, group):
         product = dot(
@@ -472,16 +472,15 @@
         (got_a, near_2, second_a, second_b, near_1, near_3, images)
     )
     outer_pairs = [(s, s ^ 6) for s in range(SLABS) if s not in INNER]
+    inner_5 = permute(second_b, [(s, s ^ 5) for s in INNER])
     near_1 = permute(near_1, [(s, s ^ 1) for s in windowed])
     near_3 = permute(near_3, [(s, s ^ 3) for s in windowed])
     near_1, got_b = lax.optimization_barrier((near_1, got_b))
-    far_columns = [
-        got_a,
-        got_b,
-        permute(choose(got_a, second_a, "class_4_blocks"), [(s, s ^ 4) for s in range(SLABS)]),
-        permute(choose(got_b, second_b, "class_6_blocks"), outer_pairs),
-        permute(second_b, [(s, s ^ 5) for s in INNER]),
-    ]
+    class_4 = permute(
+        choose(got_a, second_a, "class_4_blocks"), [(s, s ^ 4) for s in range(SLABS)]
+    )
+    outer_6 = permute(choose(got_b, second_b, "class_6_blocks"), outer_pairs)
+    far_columns = [inner_5, got_a, got_b, class_4, outer_6]
     near_columns = [near_0, near_1, near_2, near_3]
     amplitude, by_row = local_call(
         amplitude_kernel,

time: 113 us -> 113 us (level)
  no operation moved by 1% of the time
where the time goes in v16:
time: 113 us
  waiting for transfers between devices  50.6 us (45%)
  starting transfers between devices  34.4 us (30%)
  Pallas kernels  20.1 us (18%)
  other arithmetic  5.06 us (4%)
  local copies, waits for them, and re-layouts  2.42 us (2%)
    ppermute x13, waiting for transfers between devices, permute(): return lax.ppermute(sent, 'slab', pairs)  42.9 us
    ppermute x13, starting transfers between devices, permute(): return lax.ppermute(sent, 'slab', pairs)  30.8 us
    ppermute x2, waiting for transfers between devices, body_slabs(): got_x = lax.ppermute(over, 'led', planes)  7.77 us
    pallas_call x1, Pallas kernels, body_slabs(): local_call(field_kernel, [sent_block] * HALF, [vmem] * 11, [pltpu.VMEM((w...  5.31 us
    pallas_call x2, Pallas kernels, rows_call(): local_call(functools.partial(rows_kernel, which), [sent_block] * count, [...  4.69 us
    ppermute x2, starting transfers between devices, body_slabs(): got_x = lax.ppermute(over, 'led', planes)  3 us
    pallas_call x4, Pallas kernels, sum_call(): local_call(kernel, out_shape, specs, [], 0, 2 ** 20, kernel.__name__)  3 us
    pallas_call x1, Pallas kernels, body_slabs(): local_call(sent_kernel, [jax.ShapeDtypeStruct((2,) + piece, bf16), jax.Sh...  2.64 us
  transfers between devices with their start and end apart: 17, of which 10 were waited for; matrix products, arithmetic and copies ran while one was open for 3% of the time, Pallas kernels for 8%

profile of v16, /device:TPU:4, one launch (start us, length us, event | category | flops | bytes accessed | tf_op | source)
XLA Modules:
  0.0 112.9 jit_solution(12476921446979896763)
XLA Ops:
  0.0 0.9 pad_add_fusion.starts
  0.9 2.4 %copy-done.1 = f32[2,256,2048]{2,1,0:T(8,128)S(1)} copy-done((f32[2,256,2048]{2,1,0:T(8,128)S(1)}, f32[2,256,2048]{2,1,0:T(8,128)}, u32[]{:S(2)}) %copy-start.1) | copy-done | bytes 4194328
  3.3 1.4 %windows.1.window = bf16[1024,1024]{1,0:T(8,128)(2,1)S(1)} custom-call(s32[4]{0:T(128)S(1)} %pad_add_fusion.starts, f32[2,256,2048]{2,1,0:T(8,128)S(1)} %copy-done.1), custom_call_target="tpu_custom_call" | custom-call | bytes 6291456 | tf_op jit(solution)/shard_map/windows/pallas_call | solution.py:433
  4.7 1.8 %rows_round_1.1 = (bf16[4,256,128]{2,1,0:T(8,128)(2,1)S(1)}, bf16[4,256,128]{2,1,0:T(8,128)(2,1)S(1)}, bf16[4,256,128]{2,1,0:T(8,128)(2,1)S(1)}) custom-call(bf16[1024,1024]{1,0:T(8,128)(2,1)S(1)} %windows.1.window, bf16[8,1024,256]{2,1,0:T(8,128)(2,1)S(1)} %copy-done), custom_call_target="tpu_custom_call" | custom-call | flops 1610612736 | bytes 5242880 | tf_op jit(solution)/shard_map/rows_round_1/pallas_call | solution.py:445
  6.5 1.3 %collective-permute-start = (bf16[4,256,128]{2,1,0:T(8,128)(2,1)S(1)}, bf16[4,256,128]{2,1,0:T(8,128)(2,1)S(1)}, u32[]{:S(2)}, u32[]{:S(2)}) collective-permute-start(bf16[4,256,128]{2,1,0:T(8,128)(2,1)S(1)} %get-tuple-element.39), channel_id=1, source_target_pairs={{8,16},{12,20},{16,8},{20,12},{4,0},{24,28},{9,17},{13,21},{17,9},... | collective-permute-start | bytes 786440 | tf_op jit(solution)/shard_map/ppermute | solution.py:458
  7.8 5.7 %collective-permute-start.1 = (bf16[4,256,128]{2,1,0:T(8,128)(2,1)S(1)}, bf16[4,256,128]{2,1,0:T(8,128)(2,1)S(1)}, u32[]{:S(2)}, u32[]{:S(2)}) collective-permute-start(bf16[4,256,128]{2,1,0:T(8,128)(2,1)S(1)} %get-tuple-element.40), channel_id=1, source_target_pairs={{4,12},{8,0},{12,4},{16,24},{20,28},{24,16},{5,13},{9,1},{13,5},{1... | collective-permute-start | bytes 786440 | tf_op jit(solution)/shard_map/ppermute | solution.py:458
  13.5 0.0 copy-start.2
  13.5 0.0 copy-start.3
  13.5 1.6 %collective-permute-start.4 = (bf16[4,256,128]{2,1,0:T(8,128)(2,1)S(1)}, bf16[4,256,128]{2,1,0:T(8,128)(2,1)S(1)}, u32[]{:S(2)}, u32[]{:S(2)}) collective-permute-start(bf16[4,256,128]{2,1,0:T(8,128)(2,1)S(1)} %get-tuple-element.51), channel_id=1, source_target_pairs={{8,20},{12,16},{16,12},{20,8},{4,0},{24,28},{9,21},{13,17},{17,13}... | collective-permute-start | bytes 786440 | tf_op jit(solution)/shard_map/ppermute | solution.py:458
  15.1 2.9 %rows_round_2.1 = (bf16[4,256,128]{2,1,0:T(8,128)(2,1)S(1)}, bf16[4,256,128]{2,1,0:T(8,128)(2,1)S(1)}, bf16[4,256,128]{2,1,0:T(8,128)(2,1)S(1)}, bf16[4,256,128]...) custom-call(bf16[1024,1024]{1,0:T(8,128)(2,1)S(1)} %windows.1.window, bf16[8,1024,256]{2,1,0:T(8,128)(2,1)S(1)} %copy-done), custom_call_target="tpu_custom_call" | custom-call | flops 2684354560 | bytes 5242880 | tf_op jit(solution)/shard_map/rows_round_2/pallas_call | solution.py:445
  18.0 1.5 %collective-permute-done.1.rest_7_ = bf16[4,256,128]{2,1,0:T(8,128)(2,1)S(1)} collective-permute-done((bf16[4,256,128]{2,1,0:T(8,128)(2,1)S(1)}, bf16[4,256,128]{2,1,0:T(8,128)(2,1)S(1)}, u32[]{:S(2)}, u32[]{:S(2)}) %collective-permute-start.1) | collective-permute-done | bytes 262176 | tf_op jit(solution)/shard_map/ppermute | solution.py:458
  19.5 1.8 %collective-permute-start.3 = (bf16[4,256,128]{2,1,0:T(8,128)(2,1)S(1)}, bf16[4,256,128]{2,1,0:T(8,128)(2,1)S(1)}, u32[]{:S(2)}, u32[]{:S(2)}) collective-permute-start(bf16[4,256,128]{2,1,0:T(8,128)(2,1)S(1)} %get-tuple-element.50), channel_id=1, source_target_pairs={{4,0},{8,12},{12,8},{16,20},{20,16},{24,28},{5,1},{9,13},{13,9},{1... | collective-permute-start | bytes 786440 | tf_op jit(solution)/shard_map/ppermute | solution.py:458
  21.3 3.2 %collective-permute-start.5 = (bf16[4,256,128]{2,1,0:T(8,128)(2,1)S(1)}, bf16[4,256,128]{2,1,0:T(8,128)(2,1)S(1)}, u32[]{:S(2)}, u32[]{:S(2)}) collective-permute-start(bf16[4,256,128]{2,1,0:T(8,128)(2,1)S(1)} %class_4_blocks.1), channel_id=1, source_target_pairs={{0,16},{4,20},{8,24},{12,28},{16,0},{20,4},{24,8},{28,12},{1,17},{... | collective-permute-start | bytes 786440 | tf_op jit(solution)/shard_map/ppermute | solution.py:458
  24.5 1.3 %collective-permute-start.2 = (bf16[4,256,128]{2,1,0:T(8,128)(2,1)S(1)}, bf16[4,256,128]{2,1,0:T(8,128)(2,1)S(1)}, u32[]{:S(2)}, u32[]{:S(2)}) collective-permute-start(bf16[4,256,128]{2,1,0:T(8,128)(2,1)S(1)} %get-tuple-element.48.own), channel_id=1, source_target_pairs={{8,28},{12,24},{16,4},{20,0},{9,29},{13,25},{17,5},{21,1},{10,30},... | collective-permute-start | bytes 786440 | tf_op jit(solution)/shard_map/ppermute | solution.py:458
  25.8 5.5 %collective-permute-start.7 = (bf16[4,256,128]{2,1,0:T(8,128)(2,1)S(1)}, bf16[4,256,128]{2,1,0:T(8,128)(2,1)S(1)}, u32[]{:S(2)}, u32[]{:S(2)}) collective-permute-start(bf16[4,256,128]{2,1,0:T(8,128)(2,1)S(1)} %get-tuple-element.57), channel_id=1, source_target_pairs={{4,8},{8,4},{12,0},{16,28},{20,24},{24,20},{5,9},{9,5},{13,1},{17,... | collective-permute-start | bytes 786440 | tf_op jit(solution)/shard_map/ppermute | solution.py:458
  31.3 0.0 collective-permute-done.3.rest_6_
  31.4 1.9 %collective-permute-start.6 = (bf16[4,256,128]{2,1,0:T(8,128)(2,1)S(1)}, bf16[4,256,128]{2,1,0:T(8,128)(2,1)S(1)}, u32[]{:S(2)}, u32[]{:S(2)}) collective-permute-start(bf16[4,256,128]{2,1,0:T(8,128)(2,1)S(1)} %class_6_blocks.1), channel_id=1, source_target_pairs={{0,24},{4,28},{24,0},{28,4},{1,25},{5,29},{25,1},{29,5},{2,26},{6,... | collective-permute-start | bytes 786440 | tf_op jit(solution)/shard_map/ppermute | solution.py:458
  33.3 0.6 amplitude.1
  33.9 8.8 %collective-permute-done.5.rest_3_ = bf16[4,256,128]{2,1,0:T(8,128)(2,1)S(1)} collective-permute-done((bf16[4,256,128]{2,1,0:T(8,128)(2,1)S(1)}, bf16[4,256,128]{2,1,0:T(8,128)(2,1)S(1)}, u32[]{:S(2)}, u32[]{:S(2)}) %collective-permute-start.5) | collective-permute-done | bytes 262176 | tf_op jit(solution)/shard_map/ppermute | solution.py:458
  42.7 3.9 %collective-permute-done.2.rest_0_ = bf16[4,256,128]{2,1,0:T(8,128)(2,1)S(1)} collective-permute-done((bf16[4,256,128]{2,1,0:T(8,128)(2,1)S(1)}, bf16[4,256,128]{2,1,0:T(8,128)(2,1)S(1)}, u32[]{:S(2)}, u32[]{:S(2)}) %collective-permute-start.2) | collective-permute-done | bytes 262176 | tf_op jit(solution)/shard_map/ppermute | solution.py:458
  46.6 3.6 %collective-permute-done.7.rest_8_ = bf16[4,256,128]{2,1,0:T(8,128)(2,1)S(1)} collective-permute-done((bf16[4,256,128]{2,1,0:T(8,128)(2,1)S(1)}, bf16[4,256,128]{2,1,0:T(8,128)(2,1)S(1)}, u32[]{:S(2)}, u32[]{:S(2)}) %collective-permute-start.7) | collective-permute-done | bytes 262176 | tf_op jit(solution)/shard_map/ppermute | solution.py:458
  50.2 5.3 %modulus_step.1 = (bf16[4,256,128]{2,1,0:T(8,128)(2,1)S(1)}, bf16[4,256,128]{2,1,0:T(8,128)(2,1)S(1)}, bf16[4,256,128]{2,1,0:T(8,128)(2,1)S(1)}, bf16[4,256,128]{2,1,0:T(8,128)(2,1)S(1)}) custom-call(f32[1024,256]{1,0:T(8,128)S(1)} %get-tuple-element.46.amplitude, bf16[8,256,1024]{2,1,0:T(8,128)(2,1)S(1)} %get-tuple-element.47.table, ...), custom_call_target="tpu_custom_call" | custom-call | flops 4294967296 | bytes 12582912 | tf_op jit(solution)/shard_map/modulus_step/pallas_call | solution.py:497
  55.5 0.1 collective-permute-start.10
  55.6 2.4 %collective-permute-start.8 = (bf16[4,256,128]{2,1,0:T(8,128)(2,1)S(1)}, bf16[4,256,128]{2,1,0:T(8,128)(2,1)S(1)}, u32[]{:S(2)}, u32[]{:S(2)}) collective-permute-start(bf16[4,256,128]{2,1,0:T(8,128)(2,1)S(1)} %get-tuple-element.59), channel_id=1, source_target_pairs={{0,4},{4,0},{8,12},{12,8},{16,20},{20,16},{24,28},{28,24},{1,5},{5... | collective-permute-start | bytes 786440 | tf_op jit(solution)/shard_map/ppermute | solution.py:458
  58.0 1.4 %collective-permute-start.9 = (bf16[4,256,128]{2,1,0:T(8,128)(2,1)S(1)}, bf16[4,256,128]{2,1,0:T(8,128)(2,1)S(1)}, u32[]{:S(2)}, u32[]{:S(2)}) collective-permute-start(bf16[4,256,128]{2,1,0:T(8,128)(2,1)S(1)} %get-tuple-element.60), channel_id=1, source_target_pairs={{0,8},{4,12},{8,0},{12,4},{16,24},{20,28},{24,16},{28,20},{1,9},{5... | collective-permute-start | bytes 786440 | tf_op jit(solution)/shard_map/ppermute | solution.py:458
  59.4 6.3 %collective-permute-done.10.rest_3_ = bf16[4,256,128]{2,1,0:T(8,128)(2,1)S(1)} collective-permute-done((bf16[4,256,128]{2,1,0:T(8,128)(2,1)S(1)}, bf16[4,256,128]{2,1,0:T(8,128)(2,1)S(1)}, u32[]{:S(2)}, u32[]{:S(2)}) %collective-permute-start.10) | collective-permute-done | bytes 262176 | tf_op jit(solution)/shard_map/ppermute | solution.py:458
  65.6 2.7 %collective-permute-done.8.rest_1_ = bf16[4,256,128]{2,1,0:T(8,128)(2,1)S(1)} collective-permute-done((bf16[4,256,128]{2,1,0:T(8,128)(2,1)S(1)}, bf16[4,256,128]{2,1,0:T(8,128)(2,1)S(1)}, u32[]{:S(2)}, u32[]{:S(2)}) %collective-permute-start.8) | collective-permute-done | bytes 262176 | tf_op jit(solution)/shard_map/ppermute | solution.py:458
  68.4 1.7 %collective-permute-done.9.rest_2_ = bf16[4,256,128]{2,1,0:T(8,128)(2,1)S(1)} collective-permute-done((bf16[4,256,128]{2,1,0:T(8,128)(2,1)S(1)}, bf16[4,256,128]{2,1,0:T(8,128)(2,1)S(1)}, u32[]{:S(2)}, u32[]{:S(2)}) %collective-permute-start.9) | collective-permute-done | bytes 262176 | tf_op jit(solution)/shard_map/ppermute | solution.py:458
  70.1 2.6 %update_sent.1 = (bf16[2,2,256,512]{3,2,1,0:T(8,128)(2,1)S(1)}, bf16[2,2,256,512]{3,2,1,0:T(8,128)(2,1)S(1)}, bf16[1024,512]{1,0:T(8,128)(2,1)S(1)}) custom-call(s32[4]{0:T(128)S(1)} %pad_add_fusion.starts, bf16[8,1024,256]{2,1,0:T(8,128)(2,1)S(1)} %copy-done, bf16[4,256,128]{2,1,0:T(8,128)(2,1)S(1)} %get-tuple-element.58.rest_0_, ...), custom_call_target="tpu_custom_call" | custom-call | flops 1073741824 | bytes 8388608 | tf_op jit(solution)/shard_map/update_sent/pallas_call | solution.py:522
  72.8 0.1 collective-permute-start.12
  72.8 0.5 collective-permute-start.11
  73.3 2.4 %update_kept.1 = (f32[2,256,512]{2,1,0:T(8,128)S(1)}, f32[2,256,512]{2,1,0:T(8,128)S(1)}, f32[2,256,512]{2,1,0:T(8,128)S(1)}, f32[2,256,512]{2,1,0:T(8,128)S(1)}) custom-call(s32[4]{0:T(128)S(1)} %pad_add_fusion.starts, bf16[8,1024,256]{2,1,0:T(8,128)(2,1)S(1)} %copy-done, bf16[1024,512]{1,0:T(8,128)(2,1)S(1)} %get-tuple-element.62.back), custom_call_target="tpu_custom_call" | custom-call | flops 1073741824 | bytes 10485760 | tf_op jit(solution)/shard_map/update_kept/pallas_call | solution.py:537
  75.8 0.0 copy-start.4
  75.8 0.0 collective-permute-done.12.got_that
  75.8 0.1 z_first_kernel.1
  75.9 2.8 %collective-permute-start.13 = (bf16[2,2,256,128]{3,2,1,0:T(8,128)(2,1)S(1)}, bf16[2,2,256,128]{3,2,1,0:T(8,128)(2,1)S(1)}, u32[]{:S(2)}, u32[]{:S(2)}) collective-permute-start(bf16[2,2,256,128]{3,2,1,0:T(8,128)(2,1)S(1)} %z_first_kernel.1), channel_id=1, source_target_pairs={{0,16},{4,20},{8,24},{20,4},{24,8},{28,12},{1,17},{5,21},{9,25},{2... | collective-permute-start | bytes 786440 | tf_op jit(solution)/shard_map/ppermute | solution.py:458
  78.8 0.8 x_first_kernel.1
  79.6 1.5 %collective-permute-start.15 = (bf16[2,256,384]{2,1,0:T(8,128)(2,1)}, bf16[2,256,384]{2,1,0:T(8,128)(2,1)}, u32[]{:S(2)}, u32[]{:S(2)}) collective-permute-start(bf16[2,256,384]{2,1,0:T(8,128)(2,1)} %x_first_kernel.1), channel_id=1, source_target_pairs={{0,2},{2,0},{1,3},{3,1},{4,6},{6,4},{5,7},{7,5},{8,10},{10,8},{9,1... | collective-permute-start | bytes 1179656 | tf_op jit(solution)/shard_map/ppermute | solution.py:555
  81.1 11.2 %collective-permute-done.13.got_z = bf16[2,2,256,128]{3,2,1,0:T(8,128)(2,1)S(1)} collective-permute-done((bf16[2,2,256,128]{3,2,1,0:T(8,128)(2,1)S(1)}, bf16[2,2,256,128]{3,2,1,0:T(8,128)(2,1)S(1)}, u32[]{:S(2)}, u32[]{:S(2)}) %collective-permute-start.13) | collective-permute-done | bytes 262176 | tf_op jit(solution)/shard_map/ppermute | solution.py:458
  92.3 1.0 x_second_kernel.1
  93.3 1.5 %collective-permute-start.14 = (bf16[2,256,512]{2,1,0:T(8,128)(2,1)}, bf16[2,256,512]{2,1,0:T(8,128)(2,1)}, u32[]{:S(2)}, u32[]{:S(2)}) collective-permute-start(bf16[2,256,512]{2,1,0:T(8,128)(2,1)} %x_second_kernel.1), channel_id=1, source_target_pairs={{0,2},{2,0},{1,3},{3,1},{4,6},{6,4},{5,7},{7,5},{8,10},{10,8},{9,1... | collective-permute-start | bytes 1572872 | tf_op jit(solution)/shard_map/ppermute | solution.py:559
  94.8 1.1 z_second_kernel.1
  95.9 1.9 %collective-permute-start.16 = (bf16[2,256,384]{2,1,0:T(8,128)(2,1)S(1)}, bf16[2,256,384]{2,1,0:T(8,128)(2,1)S(1)}, u32[]{:S(2)}, u32[]{:S(2)}) collective-permute-start(bf16[2,256,384]{2,1,0:T(8,128)(2,1)S(1)} %z_second_kernel.1), channel_id=1, source_target_pairs={{0,16},{4,20},{8,24},{20,4},{24,8},{28,12},{1,17},{5,21},{9,25},{2... | collective-permute-start | bytes 1179656 | tf_op jit(solution)/shard_map/ppermute | solution.py:458
  97.8 1.8 %fusion.1 = f32[2,256,512]{2,1,0:T(8,128)S(1)} fusion(f32[2,256,512]{2,1,0:T(8,128)} %copy-done.4, f32[2,256,2048]{2,1,0:T(8,128)} %spectrum.1, s32[]{:T(128)S(6)} %select_n.3, bf16[2,2,256,512]{3,2,1,0:T(8,128)(2,1)S(1)} %collective-permute-done.11.got_this, bf16[2,256,128]{2,1,0:T(8,128)(2,1)S(1)} %slice_bitcast_fusion.1), kind=kLoop, calls=%fused_computation.2 | loop fusion | flops 1310720 | bytes 3801092 | tf_op jit(solution)/shard_map/add | solution.py:566
  99.7 7.8 %collective-permute-done.14 = bf16[2,256,512]{2,1,0:T(8,128)(2,1)} collective-permute-done((bf16[2,256,512]{2,1,0:T(8,128)(2,1)}, bf16[2,256,512]{2,1,0:T(8,128)(2,1)}, u32[]{:S(2)}, u32[]{:S(2)}) %collective-permute-start.14) | collective-permute-done | bytes 524320 | tf_op jit(solution)/shard_map/ppermute | solution.py:559
  107.4 1.2 %convert_add_fusion.2 = f32[2,256,512]{2,1,0:T(8,128)S(1)} fusion(f32[2,256,512]{2,1,0:T(8,128)S(1)} %fusion.1, bf16[2,256,512]{2,1,0:T(8,128)(2,1)} %collective-permute-done.14), kind=kLoop, calls=%fused_computation.4 | loop fusion | flops 524288 | bytes 2621440 | tf_op jit(solution)/shard_map/add | solution.py:568
  108.7 3.1 %collective-permute-done.16 = bf16[2,256,384]{2,1,0:T(8,128)(2,1)S(1)} collective-permute-done((bf16[2,256,384]{2,1,0:T(8,128)(2,1)S(1)}, bf16[2,256,384]{2,1,0:T(8,128)(2,1)S(1)}, u32[]{:S(2)}, u32[]{:S(2)}) %collective-permute-start.16) | collective-permute-done | bytes 393248 | tf_op jit(solution)/shard_map/ppermute | solution.py:458
  111.7 1.1 convert_add_fusion.1
  (14 shorter events, 0.1 us)
Async XLA Ops:
  0.0 4.6 %copy-start = (bf16[8,1024,256]{2,1,0:T(8,128)(2,1)S(1)}, bf16[8,1024,256]{2,1,0:T(8,128)(2,1)}, u32[]{:S(2)}) copy-start(bf16[8,1024,256]{2,1,0:T(8,128)(2,1)} %constant.18.clone.table) | copy-start | bytes 12582916
  0.9 2.4 %copy-start.1 = (f32[2,256,2048]{2,1,0:T(8,128)S(1)}, f32[2,256,2048]{2,1,0:T(8,128)}, u32[]{:S(2)}) copy-start(f32[2,256,2048]{2,1,0:T(8,128)} %spectrum.1) | copy-start | bytes 12582916
  6.5 11.5 %collective-permute-start = (bf16[4,256,128]{2,1,0:T(8,128)(2,1)S(1)}, bf16[4,256,128]{2,1,0:T(8,128)(2,1)S(1)}, u32[]{:S(2)}, u32[]{:S(2)}) collective-permute-start(bf16[4,256,128]{2,1,0:T(8,128)(2,1)S(1)} %get-tuple-element.39), channel_id=1, source_target_pairs={{8,16},{12,20},{16,8},{20,12},{4,0},{24,28},{9,17},{13,21},{17,9},... | collective-permute-start | bytes 786440 | tf_op jit(solution)/shard_map/ppermute | solution.py:458
  7.8 11.7 %collective-permute-start.1 = (bf16[4,256,128]{2,1,0:T(8,128)(2,1)S(1)}, bf16[4,256,128]{2,1,0:T(8,128)(2,1)S(1)}, u32[]{:S(2)}, u32[]{:S(2)}) collective-permute-start(bf16[4,256,128]{2,1,0:T(8,128)(2,1)S(1)} %get-tuple-element.40), channel_id=1, source_target_pairs={{4,12},{8,0},{12,4},{16,24},{20,28},{24,16},{5,13},{9,1},{13,5},{1... | collective-permute-start | bytes 786440 | tf_op jit(solution)/shard_map/ppermute | solution.py:458
  13.5 19.9 %copy-start.2 = (bf16[8,256,1024]{2,1,0:T(8,128)(2,1)S(1)}, bf16[8,256,1024]{2,1,0:T(8,128)(2,1)}, u32[]{:S(2)}) copy-start(bf16[8,256,1024]{2,1,0:T(8,128)(2,1)} %constant.17.clone.table) | copy-start | bytes 12582916
  13.5 19.9 %copy-start.3 = (f32[2,128,1024]{2,1,0:T(8,128)S(1)}, f32[2,128,1024]{2,1,0:T(8,128)}, u32[]{:S(2)}) copy-start(f32[2,128,1024]{2,1,0:T(8,128)} %images) | copy-start | bytes 3145732
  13.5 17.8 %collective-permute-start.4 = (bf16[4,256,128]{2,1,0:T(8,128)(2,1)S(1)}, bf16[4,256,128]{2,1,0:T(8,128)(2,1)S(1)}, u32[]{:S(2)}, u32[]{:S(2)}) collective-permute-start(bf16[4,256,128]{2,1,0:T(8,128)(2,1)S(1)} %get-tuple-element.51), channel_id=1, source_target_pairs={{8,20},{12,16},{16,12},{20,8},{4,0},{24,28},{9,21},{13,17},{17,13}... | collective-permute-start | bytes 786440 | tf_op jit(solution)/shard_map/ppermute | solution.py:458
  19.5 11.9 %collective-permute-start.3 = (bf16[4,256,128]{2,1,0:T(8,128)(2,1)S(1)}, bf16[4,256,128]{2,1,0:T(8,128)(2,1)S(1)}, u32[]{:S(2)}, u32[]{:S(2)}) collective-permute-start(bf16[4,256,128]{2,1,0:T(8,128)(2,1)S(1)} %get-tuple-element.50), channel_id=1, source_target_pairs={{4,0},{8,12},{12,8},{16,20},{20,16},{24,28},{5,1},{9,13},{13,9},{1... | collective-permute-start | bytes 786440 | tf_op jit(solution)/shard_map/ppermute | solution.py:458
  21.3 21.4 %collective-permute-start.5 = (bf16[4,256,128]{2,1,0:T(8,128)(2,1)S(1)}, bf16[4,256,128]{2,1,0:T(8,128)(2,1)S(1)}, u32[]{:S(2)}, u32[]{:S(2)}) collective-permute-start(bf16[4,256,128]{2,1,0:T(8,128)(2,1)S(1)} %class_4_blocks.1), channel_id=1, source_target_pairs={{0,16},{4,20},{8,24},{12,28},{16,0},{20,4},{24,8},{28,12},{1,17},{... | collective-permute-start | bytes 786440 | tf_op jit(solution)/shard_map/ppermute | solution.py:458
  24.5 22.1 %collective-permute-start.2 = (bf16[4,256,128]{2,1,0:T(8,128)(2,1)S(1)}, bf16[4,256,128]{2,1,0:T(8,128)(2,1)S(1)}, u32[]{:S(2)}, u32[]{:S(2)}) collective-permute-start(bf16[4,256,128]{2,1,0:T(8,128)(2,1)S(1)} %get-tuple-element.48.own), channel_id=1, source_target_pairs={{8,28},{12,24},{16,4},{20,0},{9,29},{13,25},{17,5},{21,1},{10,30},... | collective-permute-start | bytes 786440 | tf_op jit(solution)/shard_map/ppermute | solution.py:458
  25.8 24.4 %collective-permute-start.7 = (bf16[4,256,128]{2,1,0:T(8,128)(2,1)S(1)}, bf16[4,256,128]{2,1,0:T(8,128)(2,1)S(1)}, u32[]{:S(2)}, u32[]{:S(2)}) collective-permute-start(bf16[4,256,128]{2,1,0:T(8,128)(2,1)S(1)} %get-tuple-element.57), channel_id=1, source_target_pairs={{4,8},{8,4},{12,0},{16,28},{20,24},{24,20},{5,9},{9,5},{13,1},{17,... | collective-permute-start | bytes 786440 | tf_op jit(solution)/shard_map/ppermute | solution.py:458
  31.4 18.8 %collective-permute-start.6 = (bf16[4,256,128]{2,1,0:T(8,128)(2,1)S(1)}, bf16[4,256,128]{2,1,0:T(8,128)(2,1)S(1)}, u32[]{:S(2)}, u32[]{:S(2)}) collective-permute-start(bf16[4,256,128]{2,1,0:T(8,128)(2,1)S(1)} %class_6_blocks.1), channel_id=1, source_target_pairs={{0,24},{4,28},{24,0},{28,4},{1,25},{5,29},{25,1},{29,5},{2,26},{6,... | collective-permute-start | bytes 786440 | tf_op jit(solution)/shard_map/ppermute | solution.py:458
  55.5 10.1 %collective-permute-start.10 = (bf16[4,256,128]{2,1,0:T(8,128)(2,1)S(1)}, bf16[4,256,128]{2,1,0:T(8,128)(2,1)S(1)}, u32[]{:S(2)}, u32[]{:S(2)}) collective-permute-start(bf16[4,256,128]{2,1,0:T(8,128)(2,1)S(1)} %get-tuple-element.61), channel_id=1, source_target_pairs={{0,12},{4,8},{8,4},{12,0},{16,28},{20,24},{24,20},{28,16},{1,13},{... | collective-permute-start | bytes 786440 | tf_op jit(solution)/shard_map/ppermute | solution.py:458
  55.6 12.8 %collective-permute-start.8 = (bf16[4,256,128]{2,1,0:T(8,128)(2,1)S(1)}, bf16[4,256,128]{2,1,0:T(8,128)(2,1)S(1)}, u32[]{:S(2)}, u32[]{:S(2)}) collective-permute-start(bf16[4,256,128]{2,1,0:T(8,128)(2,1)S(1)} %get-tuple-element.59), channel_id=1, source_target_pairs={{0,4},{4,0},{8,12},{12,8},{16,20},{20,16},{24,28},{28,24},{1,5},{5... | collective-permute-start | bytes 786440 | tf_op jit(solution)/shard_map/ppermute | solution.py:458
  58.0 12.1 %collective-permute-start.9 = (bf16[4,256,128]{2,1,0:T(8,128)(2,1)S(1)}, bf16[4,256,128]{2,1,0:T(8,128)(2,1)S(1)}, u32[]{:S(2)}, u32[]{:S(2)}) collective-permute-start(bf16[4,256,128]{2,1,0:T(8,128)(2,1)S(1)} %get-tuple-element.60), channel_id=1, source_target_pairs={{0,8},{4,12},{8,0},{12,4},{16,24},{20,28},{24,16},{28,20},{1,9},{5... | collective-permute-start | bytes 786440 | tf_op jit(solution)/shard_map/ppermute | solution.py:458
  72.8 3.0 %collective-permute-start.12 = (bf16[2,2,256,512]{3,2,1,0:T(8,128)(2,1)S(1)}, bf16[2,2,256,512]{3,2,1,0:T(8,128)(2,1)S(1)}, u32[]{:S(2)}, u32[]{:S(2)}) collective-permute-start(bf16[2,2,256,512]{3,2,1,0:T(8,128)(2,1)S(1)} %get-tuple-element.67), channel_id=1, source_target_pairs={{0,1},{1,0},{2,3},{3,2},{4,5},{5,4},{6,7},{7,6},{8,9},{9,8},{10,11... | collective-permute-start | bytes 3145736 | tf_op jit(solution)/shard_map/ppermute | solution.py:535
  72.8 8.2 %collective-permute-start.11 = (bf16[2,2,256,512]{3,2,1,0:T(8,128)(2,1)S(1)}, bf16[2,2,256,512]{3,2,1,0:T(8,128)(2,1)S(1)}, u32[]{:S(2)}, u32[]{:S(2)}) collective-permute-start(bf16[2,2,256,512]{3,2,1,0:T(8,128)(2,1)S(1)} %get-tuple-element.64), channel_id=1, source_target_pairs={{0,1},{1,0},{2,3},{3,2},{4,5},{5,4},{6,7},{7,6},{8,9},{9,8},{10,11... | collective-permute-start | bytes 3145736 | tf_op jit(solution)/shard_map/ppermute | solution.py:536
  75.8 5.3 %copy-start.4 = (f32[2,256,512]{2,1,0:T(8,128)}, f32[2,256,512]{2,1,0:T(8,128)S(1)}, u32[]{:S(2)}) copy-start(f32[2,256,512]{2,1,0:T(8,128)S(1)} %get-tuple-element.63) | copy-start | bytes 3145732
  75.9 16.4 %collective-permute-start.13 = (bf16[2,2,256,128]{3,2,1,0:T(8,128)(2,1)S(1)}, bf16[2,2,256,128]{3,2,1,0:T(8,128)(2,1)S(1)}, u32[]{:S(2)}, u32[]{:S(2)}) collective-permute-start(bf16[2,2,256,128]{3,2,1,0:T(8,128)(2,1)S(1)} %z_first_kernel.1), channel_id=1, source_target_pairs={{0,16},{4,20},{8,24},{20,4},{24,8},{28,12},{1,17},{5,21},{9,25},{2... | collective-permute-start | bytes 786440 | tf_op jit(solution)/shard_map/ppermute | solution.py:458
  79.6 15.2 %collective-permute-start.15 = (bf16[2,256,384]{2,1,0:T(8,128)(2,1)}, bf16[2,256,384]{2,1,0:T(8,128)(2,1)}, u32[]{:S(2)}, u32[]{:S(2)}) collective-permute-start(bf16[2,256,384]{2,1,0:T(8,128)(2,1)} %x_first_kernel.1), channel_id=1, source_target_pairs={{0,2},{2,0},{1,3},{3,1},{4,6},{6,4},{5,7},{7,5},{8,10},{10,8},{9,1... | collective-permute-start | bytes 1179656 | tf_op jit(solution)/shard_map/ppermute | solution.py:555
  93.3 14.2 %collective-permute-start.14 = (bf16[2,256,512]{2,1,0:T(8,128)(2,1)}, bf16[2,256,512]{2,1,0:T(8,128)(2,1)}, u32[]{:S(2)}, u32[]{:S(2)}) collective-permute-start(bf16[2,256,512]{2,1,0:T(8,128)(2,1)} %x_second_kernel.1), channel_id=1, source_target_pairs={{0,2},{2,0},{1,3},{3,1},{4,6},{6,4},{5,7},{7,5},{8,10},{10,8},{9,1... | collective-permute-start | bytes 1572872 | tf_op jit(solution)/shard_map/ppermute | solution.py:559
  95.9 15.8 %collective-permute-start.16 = (bf16[2,256,384]{2,1,0:T(8,128)(2,1)S(1)}, bf16[2,256,384]{2,1,0:T(8,128)(2,1)S(1)}, u32[]{:S(2)}, u32[]{:S(2)}) collective-permute-start(bf16[2,256,384]{2,1,0:T(8,128)(2,1)S(1)} %z_second_kernel.1), channel_id=1, source_target_pairs={{0,16},{4,20},{8,24},{20,4},{24,8},{28,12},{1,17},{5,21},{9,25},{2... | collective-permute-start | bytes 1179656 | tf_op jit(solution)/shard_map/ppermute | solution.py:458

commit v17 on v15

--- a/solution.py
+++ b/solution.py
@@ -201,7 +201,7 @@
 
 def classes_of(position):
     hands_over = is_one_of(position, PASSED)
-    return (jnp.where(hands_over, 5, 6), 7, 2, 3, 4, jnp.where(hands_over, 6, 5), 0, 1)
+    return (jnp.where(hands_over, 5, 6), 7, 3, 4, jnp.where(hands_over, 6, 5), 0, 1, 2)
 
 
 def rows_kernel(which, window, table, *outs):
@@ -396,14 +396,14 @@
     out[:, :, :cols] = (total[:, :, :cols] + got_z[1].astype(jnp.float32)).astype(out.dtype)
 
 
-def local_call(kernel, out_shape, spaces, scratch, flops, moved, name):
+def local_call(kernel, out_shape, spaces, scratch, flops, moved, name, limit=32):
     return pl.pallas_call(
         kernel,
         out_shape=out_shape,
         in_specs=[pl.BlockSpec(memory_space=space) for space in spaces],
         out_specs=jax.tree.map(lambda _: pl.BlockSpec(memory_space=pltpu.VMEM), out_shape),
         scratch_shapes=scratch,
-        compiler_params=pltpu.CompilerParams(vmem_limit_bytes=32 * 2**20),
+        compiler_params=pltpu.CompilerParams(vmem_limit_bytes=limit * 2**20),
         cost_estimate=pl.CostEstimate(flops=flops, bytes_accessed=moved, transcendentals=0),
         name=name,
     )
@@ -452,7 +452,7 @@
             name,
         )(window, by_col)
 
-    first_a, first_b, near_2, near_3 = rows_call(slice(0, 4), "rows_round_1")
+    first_a, first_b, near_3 = rows_call(slice(0, 3), "rows_round_1")
 
     def permute(sent, pairs):
         return lax.ppermute(sent, "slab", pairs)
@@ -466,15 +466,15 @@
     windowed = range(FIRST + 1, LAST)
     got_a = permute(first_a, [(s, s ^ 6) for s in INNER] + handed)
     got_b = permute(first_b, [(s, s ^ 7) for s in INNER] + handed)
-    near_2 = permute(near_2, [(s, s ^ 2) for s in windowed])
     near_3 = permute(near_3, [(s, s ^ 3) for s in windowed])
-    second_a, second_b, near_0, near_1 = rows_call(slice(4, SLABS), "rows_round_2")
-    got_a, second_a, second_b, near_1, images = lax.optimization_barrier(
-        (got_a, second_a, second_b, near_1, images)
+    second_a, second_b, near_0, near_1, near_2 = rows_call(slice(3, SLABS), "rows_round_2")
+    got_a, second_a, second_b, near_1, near_2, images = lax.optimization_barrier(
+        (got_a, second_a, second_b, near_1, near_2, images)
     )
     outer_pairs = [(s, s ^ 6) for s in range(SLABS) if s not in INNER]
     near_1 = permute(near_1, [(s, s ^ 1) for s in windowed])
-    near_1, near_2, near_3, got_b = lax.optimization_barrier((near_1, near_2, near_3, got_b))
+    near_2 = permute(near_2, [(s, s ^ 2) for s in windowed])
+    near_1, near_3, got_b = lax.optimization_barrier((near_1, near_3, got_b))
     far_columns = [
         got_a,
         got_b,
@@ -532,6 +532,7 @@
         flops // 4,
         8 * 2**20,
         "update_sent",
+        16,
     )(starts, by_col, *home)
     got_that = lax.ppermute(sent_that, "led", cores)
     got_this = lax.ppermute(sent_this, "led", cores)
@@ -543,12 +544,13 @@
         flops // 4,
         10 * 2**20,
         "update_kept",
+        16,
     )(starts, by_col, back)
 
     def sum_call(kernel, shape, *values):
         out_shape = jax.ShapeDtypeStruct(shape, bf16)
         specs = [vmem] * len(values)
-        return local_call(kernel, out_shape, specs, [], 0, 2**20, kernel.__name__)(*values)
+        return local_call(kernel, out_shape, specs, [], 0, 2**20, kernel.__name__, 12)(*values)
 
     over = sum_call(z_first_kernel, (2, 2, rows, first), that_near, that_far, got_that)
     got_z_first = permute(over, across)

time: 115 us -> 118 us (1.026)
  waiting for transfers between devices: 48.2 us -> 50.2 us
    ppermute x13, waiting for transfers between devices: 40.5 us -> 42.7 us  [permute(): return lax.ppermute(sent, 'slab', pairs)]
  transfers between devices with their start and end apart: 17 -> 17, of which waited for: 11 -> 8; matrix products, arithmetic and copies ran while one was open for 3% -> 3% of each run, Pallas kernels for 7% -> 8%
where the time goes in v17:
time: 118 us; the launch traced here: 117 us
  waiting for transfers between devices  50.2 us (43%)
  starting transfers between devices  39 us (33%)
  Pallas kernels  20.1 us (17%)
  other arithmetic  5.06 us (4%)
  local copies, waits for them, and re-layouts  2.42 us (2%)
    ppermute x13, waiting for transfers between devices, permute(): return lax.ppermute(sent, 'slab', pairs)  42.7 us
    ppermute x13, starting transfers between devices, permute(): return lax.ppermute(sent, 'slab', pairs)  34.5 us
    ppermute x2, waiting for transfers between devices, body_slabs(): got_x = lax.ppermute(over, 'led', planes)  7.53 us
    pallas_call x1, Pallas kernels, body_slabs(): local_call(field_kernel, [sent_block] * HALF, [vmem] * 11, [pltpu.VMEM((w...  5.3 us
    pallas_call x2, Pallas kernels, rows_call(): local_call(functools.partial(rows_kernel, which), [sent_block] * count, [...  4.69 us
    ppermute x2, starting transfers between devices, body_slabs(): got_x = lax.ppermute(over, 'led', planes)  3.99 us
    pallas_call x4, Pallas kernels, sum_call(): local_call(kernel, out_shape, specs, [], 0, 2 ** 20, kernel.__name__, 12)  3.02 us
    pallas_call x1, Pallas kernels, body_slabs(): local_call(sent_kernel, [jax.ShapeDtypeStruct((2,) + piece, bf16), jax.Sh...  2.67 us
  transfers between devices with their start and end apart: 17, of which 8 were waited for; matrix products, arithmetic and copies ran while one was open for 3% of the time, Pallas kernels for 8%

profile of v17, /device:TPU:4, one launch (start us, length us, event | category | flops | bytes accessed | tf_op | source)
XLA Modules:
  0.0 117.1 jit_solution(4698093677965872898)
XLA Ops:
  0.0 0.9 pad_add_fusion.starts
  0.9 2.4 %copy-done.1 = f32[2,256,2048]{2,1,0:T(8,128)S(1)} copy-done((f32[2,256,2048]{2,1,0:T(8,128)S(1)}, f32[2,256,2048]{2,1,0:T(8,128)}, u32[]{:S(2)}) %copy-start.1) | copy-done | bytes 4194328
  3.3 1.4 %windows.1.window = bf16[1024,1024]{1,0:T(8,128)(2,1)S(1)} custom-call(s32[4]{0:T(128)S(1)} %pad_add_fusion.starts, f32[2,256,2048]{2,1,0:T(8,128)S(1)} %copy-done.1), custom_call_target="tpu_custom_call" | custom-call | bytes 6291456 | tf_op jit(solution)/shard_map/windows/pallas_call | solution.py:433
  4.7 1.8 %rows_round_1.1 = (bf16[4,256,128]{2,1,0:T(8,128)(2,1)S(1)}, bf16[4,256,128]{2,1,0:T(8,128)(2,1)S(1)}, bf16[4,256,128]{2,1,0:T(8,128)(2,1)S(1)}) custom-call(bf16[1024,1024]{1,0:T(8,128)(2,1)S(1)} %windows.1.window, bf16[8,1024,256]{2,1,0:T(8,128)(2,1)S(1)} %copy-done), custom_call_target="tpu_custom_call" | custom-call | flops 1610612736 | bytes 5242880 | tf_op jit(solution)/shard_map/rows_round_1/pallas_call | solution.py:445
  6.5 1.3 %collective-permute-start = (bf16[4,256,128]{2,1,0:T(8,128)(2,1)S(1)}, bf16[4,256,128]{2,1,0:T(8,128)(2,1)S(1)}, u32[]{:S(2)}, u32[]{:S(2)}) collective-permute-start(bf16[4,256,128]{2,1,0:T(8,128)(2,1)S(1)} %get-tuple-element.39), channel_id=1, source_target_pairs={{8,16},{12,20},{16,8},{20,12},{4,0},{24,28},{9,17},{13,21},{17,9},... | collective-permute-start | bytes 786440 | tf_op jit(solution)/shard_map/ppermute | solution.py:458
  7.8 5.6 %collective-permute-start.2 = (bf16[4,256,128]{2,1,0:T(8,128)(2,1)S(1)}, bf16[4,256,128]{2,1,0:T(8,128)(2,1)S(1)}, u32[]{:S(2)}, u32[]{:S(2)}) collective-permute-start(bf16[4,256,128]{2,1,0:T(8,128)(2,1)S(1)} %get-tuple-element.49), channel_id=1, source_target_pairs={{4,8},{8,4},{12,0},{16,28},{20,24},{24,20},{5,9},{9,5},{13,1},{17,... | collective-permute-start | bytes 786440 | tf_op jit(solution)/shard_map/ppermute | solution.py:458
  13.4 0.0 copy-start.2
  13.4 0.0 copy-start.3
  13.4 1.6 %collective-permute-start.3 = (bf16[4,256,128]{2,1,0:T(8,128)(2,1)S(1)}, bf16[4,256,128]{2,1,0:T(8,128)(2,1)S(1)}, u32[]{:S(2)}, u32[]{:S(2)}) collective-permute-start(bf16[4,256,128]{2,1,0:T(8,128)(2,1)S(1)} %get-tuple-element.50), channel_id=1, source_target_pairs={{8,20},{12,16},{16,12},{20,8},{4,0},{24,28},{9,21},{13,17},{17,13}... | collective-permute-start | bytes 786440 | tf_op jit(solution)/shard_map/ppermute | solution.py:458
  15.0 2.9 %rows_round_2.1 = (bf16[4,256,128]{2,1,0:T(8,128)(2,1)S(1)}, bf16[4,256,128]{2,1,0:T(8,128)(2,1)S(1)}, bf16[4,256,128]{2,1,0:T(8,128)(2,1)S(1)}, bf16[4,256,128]...) custom-call(bf16[1024,1024]{1,0:T(8,128)(2,1)S(1)} %windows.1.window, bf16[8,1024,256]{2,1,0:T(8,128)(2,1)S(1)} %copy-done), custom_call_target="tpu_custom_call" | custom-call | flops 2684354560 | bytes 5242880 | tf_op jit(solution)/shard_map/rows_round_2/pallas_call | solution.py:445
  17.9 2.1 %collective-permute-done.got.rest_0_ = bf16[4,256,128]{2,1,0:T(8,128)(2,1)S(1)} collective-permute-done((bf16[4,256,128]{2,1,0:T(8,128)(2,1)S(1)}, bf16[4,256,128]{2,1,0:T(8,128)(2,1)S(1)}, u32[]{:S(2)}, u32[]{:S(2)}) %collective-permute-start) | collective-permute-done | bytes 262176 | tf_op jit(solution)/shard_map/ppermute | solution.py:458
  20.0 4.4 %collective-permute-start.1 = (bf16[4,256,128]{2,1,0:T(8,128)(2,1)S(1)}, bf16[4,256,128]{2,1,0:T(8,128)(2,1)S(1)}, u32[]{:S(2)}, u32[]{:S(2)}) collective-permute-start(bf16[4,256,128]{2,1,0:T(8,128)(2,1)S(1)} %get-tuple-element.48), channel_id=1, source_target_pairs={{4,0},{8,12},{12,8},{16,20},{20,16},{24,28},{5,1},{9,13},{13,9},{1... | collective-permute-start | bytes 786440 | tf_op jit(solution)/shard_map/ppermute | solution.py:458
  24.5 0.1 collective-permute-start.4
  24.6 1.3 %collective-permute-start.6 = (bf16[4,256,128]{2,1,0:T(8,128)(2,1)S(1)}, bf16[4,256,128]{2,1,0:T(8,128)(2,1)S(1)}, u32[]{:S(2)}, u32[]{:S(2)}) collective-permute-start(bf16[4,256,128]{2,1,0:T(8,128)(2,1)S(1)} %get-tuple-element.53.own), channel_id=1, source_target_pairs={{8,28},{12,24},{16,4},{20,0},{9,29},{13,25},{17,5},{21,1},{10,30},... | collective-permute-start | bytes 786440 | tf_op jit(solution)/shard_map/ppermute | solution.py:458
  25.9 0.0 collective-permute-done.2.rest_8_
  25.9 8.8 %collective-permute-start.7 = (bf16[4,256,128]{2,1,0:T(8,128)(2,1)S(1)}, bf16[4,256,128]{2,1,0:T(8,128)(2,1)S(1)}, u32[]{:S(2)}, u32[]{:S(2)}) collective-permute-start(bf16[4,256,128]{2,1,0:T(8,128)(2,1)S(1)} %get-tuple-element.56), channel_id=1, source_target_pairs={{4,12},{8,0},{12,4},{16,24},{20,28},{24,16},{5,13},{9,1},{13,5},{1... | collective-permute-start | bytes 786440 | tf_op jit(solution)/shard_map/ppermute | solution.py:458
  34.7 0.0 collective-permute-done.1.rest_6_
  34.8 4.0 %collective-permute-start.5 = (bf16[4,256,128]{2,1,0:T(8,128)(2,1)S(1)}, bf16[4,256,128]{2,1,0:T(8,128)(2,1)S(1)}, u32[]{:S(2)}, u32[]{:S(2)}) collective-permute-start(bf16[4,256,128]{2,1,0:T(8,128)(2,1)S(1)} %class_6_blocks.1), channel_id=1, source_target_pairs={{0,24},{4,28},{24,0},{28,4},{1,25},{5,29},{25,1},{29,5},{2,26},{6,... | collective-permute-start | bytes 786440 | tf_op jit(solution)/shard_map/ppermute | solution.py:458
  38.8 0.6 amplitude.1
  39.4 0.0 collective-permute-done.4.rest_2_
  39.4 8.5 %collective-permute-done.6.rest_4_ = bf16[4,256,128]{2,1,0:T(8,128)(2,1)S(1)} collective-permute-done((bf16[4,256,128]{2,1,0:T(8,128)(2,1)S(1)}, bf16[4,256,128]{2,1,0:T(8,128)(2,1)S(1)}, u32[]{:S(2)}, u32[]{:S(2)}) %collective-permute-start.6) | collective-permute-done | bytes 262176 | tf_op jit(solution)/shard_map/ppermute | solution.py:458
  47.8 6.5 %collective-permute-done.7.rest_7_ = bf16[4,256,128]{2,1,0:T(8,128)(2,1)S(1)} collective-permute-done((bf16[4,256,128]{2,1,0:T(8,128)(2,1)S(1)}, bf16[4,256,128]{2,1,0:T(8,128)(2,1)S(1)}, u32[]{:S(2)}, u32[]{:S(2)}) %collective-permute-start.7) | collective-permute-done | bytes 262176 | tf_op jit(solution)/shard_map/ppermute | solution.py:458
  54.3 0.0 collective-permute-done.5.rest_3_
  54.3 5.3 %modulus_step.1 = (bf16[4,256,128]{2,1,0:T(8,128)(2,1)S(1)}, bf16[4,256,128]{2,1,0:T(8,128)(2,1)S(1)}, bf16[4,256,128]{2,1,0:T(8,128)(2,1)S(1)}, bf16[4,256,128]{2,1,0:T(8,128)(2,1)S(1)}) custom-call(f32[1024,256]{1,0:T(8,128)S(1)} %get-tuple-element.45.amplitude, bf16[8,256,1024]{2,1,0:T(8,128)(2,1)S(1)} %get-tuple-element.46.table, ...), custom_call_target="tpu_custom_call" | custom-call | flops 4294967296 | bytes 12582912 | tf_op jit(solution)/shard_map/modulus_step/pallas_call | solution.py:498
  59.6 0.1 collective-permute-start.10
  59.7 1.0 collective-permute-start.8
  60.8 2.4 %collective-permute-start.9 = (bf16[4,256,128]{2,1,0:T(8,128)(2,1)S(1)}, bf16[4,256,128]{2,1,0:T(8,128)(2,1)S(1)}, u32[]{:S(2)}, u32[]{:S(2)}) collective-permute-start(bf16[4,256,128]{2,1,0:T(8,128)(2,1)S(1)} %get-tuple-element.60), channel_id=1, source_target_pairs={{0,8},{4,12},{8,0},{12,4},{16,24},{20,28},{24,16},{28,20},{1,9},{5... | collective-permute-start | bytes 786440 | tf_op jit(solution)/shard_map/ppermute | solution.py:458
  63.2 6.6 %collective-permute-done.10.rest_3_ = bf16[4,256,128]{2,1,0:T(8,128)(2,1)S(1)} collective-permute-done((bf16[4,256,128]{2,1,0:T(8,128)(2,1)S(1)}, bf16[4,256,128]{2,1,0:T(8,128)(2,1)S(1)}, u32[]{:S(2)}, u32[]{:S(2)}) %collective-permute-start.10) | collective-permute-done | bytes 262176 | tf_op jit(solution)/shard_map/ppermute | solution.py:458
  69.8 3.8 %collective-permute-done.8.rest_1_ = bf16[4,256,128]{2,1,0:T(8,128)(2,1)S(1)} collective-permute-done((bf16[4,256,128]{2,1,0:T(8,128)(2,1)S(1)}, bf16[4,256,128]{2,1,0:T(8,128)(2,1)S(1)}, u32[]{:S(2)}, u32[]{:S(2)}) %collective-permute-start.8) | collective-permute-done | bytes 262176 | tf_op jit(solution)/shard_map/ppermute | solution.py:458
  73.6 2.7 %update_sent.1 = (bf16[2,2,256,512]{3,2,1,0:T(8,128)(2,1)S(1)}, bf16[2,2,256,512]{3,2,1,0:T(8,128)(2,1)S(1)}, bf16[1024,512]{1,0:T(8,128)(2,1)S(1)}) custom-call(s32[4]{0:T(128)S(1)} %pad_add_fusion.starts, bf16[8,1024,256]{2,1,0:T(8,128)(2,1)S(1)} %copy-done, bf16[4,256,128]{2,1,0:T(8,128)(2,1)S(1)} %get-tuple-element.58.rest_0_, ...), custom_call_target="tpu_custom_call" | custom-call | flops 1073741824 | bytes 8388608 | tf_op jit(solution)/shard_map/update_sent/pallas_call | solution.py:523
  76.3 0.1 collective-permute-start.12
  76.4 0.5 collective-permute-start.11
  76.9 2.4 %update_kept.1 = (f32[2,256,512]{2,1,0:T(8,128)S(1)}, f32[2,256,512]{2,1,0:T(8,128)S(1)}, f32[2,256,512]{2,1,0:T(8,128)S(1)}, f32[2,256,512]{2,1,0:T(8,128)S(1)}) custom-call(s32[4]{0:T(128)S(1)} %pad_add_fusion.starts, bf16[8,1024,256]{2,1,0:T(8,128)(2,1)S(1)} %copy-done, bf16[1024,512]{1,0:T(8,128)(2,1)S(1)} %get-tuple-element.62.back), custom_call_target="tpu_custom_call" | custom-call | flops 1073741824 | bytes 10485760 | tf_op jit(solution)/shard_map/update_kept/pallas_call | solution.py:539
  79.3 0.0 copy-start.4
  79.3 0.1 z_first_kernel.1
  79.5 1.9 %collective-permute-start.13 = (bf16[2,2,256,128]{3,2,1,0:T(8,128)(2,1)S(1)}, bf16[2,2,256,128]{3,2,1,0:T(8,128)(2,1)S(1)}, u32[]{:S(2)}, u32[]{:S(2)}) collective-permute-start(bf16[2,2,256,128]{3,2,1,0:T(8,128)(2,1)S(1)} %z_first_kernel.1), channel_id=1, source_target_pairs={{0,16},{4,20},{8,24},{20,4},{24,8},{28,12},{1,17},{5,21},{9,25},{2... | collective-permute-start | bytes 786440 | tf_op jit(solution)/shard_map/ppermute | solution.py:458
  81.4 0.8 x_first_kernel.1
  82.2 2.0 %collective-permute-start.15 = (bf16[2,256,384]{2,1,0:T(8,128)(2,1)}, bf16[2,256,384]{2,1,0:T(8,128)(2,1)}, u32[]{:S(2)}, u32[]{:S(2)}) collective-permute-start(bf16[2,256,384]{2,1,0:T(8,128)(2,1)} %x_first_kernel.1), channel_id=1, source_target_pairs={{0,2},{2,0},{1,3},{3,1},{4,6},{6,4},{5,7},{7,5},{8,10},{10,8},{9,1... | collective-permute-start | bytes 1179656 | tf_op jit(solution)/shard_map/ppermute | solution.py:558
  84.2 11.8 %collective-permute-done.13.got_z = bf16[2,2,256,128]{3,2,1,0:T(8,128)(2,1)S(1)} collective-permute-done((bf16[2,2,256,128]{3,2,1,0:T(8,128)(2,1)S(1)}, bf16[2,2,256,128]{3,2,1,0:T(8,128)(2,1)S(1)}, u32[]{:S(2)}, u32[]{:S(2)}) %collective-permute-start.13) | collective-permute-done | bytes 262176 | tf_op jit(solution)/shard_map/ppermute | solution.py:458
  96.0 1.0 x_second_kernel.1
  96.9 2.0 %collective-permute-start.14 = (bf16[2,256,512]{2,1,0:T(8,128)(2,1)}, bf16[2,256,512]{2,1,0:T(8,128)(2,1)}, u32[]{:S(2)}, u32[]{:S(2)}) collective-permute-start(bf16[2,256,512]{2,1,0:T(8,128)(2,1)} %x_second_kernel.1), channel_id=1, source_target_pairs={{0,2},{2,0},{1,3},{3,1},{4,6},{6,4},{5,7},{7,5},{8,10},{10,8},{9,1... | collective-permute-start | bytes 1572872 | tf_op jit(solution)/shard_map/ppermute | solution.py:562
  99.0 1.1 z_second_kernel.1
  100.1 1.9 %collective-permute-start.16 = (bf16[2,256,384]{2,1,0:T(8,128)(2,1)S(1)}, bf16[2,256,384]{2,1,0:T(8,128)(2,1)S(1)}, u32[]{:S(2)}, u32[]{:S(2)}) collective-permute-start(bf16[2,256,384]{2,1,0:T(8,128)(2,1)S(1)} %z_second_kernel.1), channel_id=1, source_target_pairs={{0,16},{4,20},{8,24},{20,4},{24,8},{28,12},{1,17},{5,21},{9,25},{2... | collective-permute-start | bytes 1179656 | tf_op jit(solution)/shard_map/ppermute | solution.py:458
  102.0 1.8 %fusion.1 = f32[2,256,512]{2,1,0:T(8,128)S(1)} fusion(f32[2,256,512]{2,1,0:T(8,128)} %copy-done.4, f32[2,256,2048]{2,1,0:T(8,128)} %spectrum.1, s32[]{:T(128)S(6)} %select_n.3, bf16[2,2,256,512]{3,2,1,0:T(8,128)(2,1)S(1)} %collective-permute-done.11.got_this, bf16[2,256,128]{2,1,0:T(8,128)(2,1)S(1)} %slice_bitcast_fusion.1), kind=kLoop, calls=%fused_computation.2 | loop fusion | flops 1310720 | bytes 3801092 | tf_op jit(solution)/shard_map/add | solution.py:569
  103.9 7.5 %collective-permute-done.14 = bf16[2,256,512]{2,1,0:T(8,128)(2,1)} collective-permute-done((bf16[2,256,512]{2,1,0:T(8,128)(2,1)}, bf16[2,256,512]{2,1,0:T(8,128)(2,1)}, u32[]{:S(2)}, u32[]{:S(2)}) %collective-permute-start.14) | collective-permute-done | bytes 524320 | tf_op jit(solution)/shard_map/ppermute | solution.py:562
  111.4 1.2 %convert_add_fusion.2 = f32[2,256,512]{2,1,0:T(8,128)S(1)} fusion(f32[2,256,512]{2,1,0:T(8,128)S(1)} %fusion.1, bf16[2,256,512]{2,1,0:T(8,128)(2,1)} %collective-permute-done.14), kind=kLoop, calls=%fused_computation.4 | loop fusion | flops 524288 | bytes 2621440 | tf_op jit(solution)/shard_map/add | solution.py:571
  112.6 3.4 %collective-permute-done.16 = bf16[2,256,384]{2,1,0:T(8,128)(2,1)S(1)} collective-permute-done((bf16[2,256,384]{2,1,0:T(8,128)(2,1)S(1)}, bf16[2,256,384]{2,1,0:T(8,128)(2,1)S(1)}, u32[]{:S(2)}, u32[]{:S(2)}) %collective-permute-start.16) | collective-permute-done | bytes 393248 | tf_op jit(solution)/shard_map/ppermute | solution.py:458
  116.0 1.1 convert_add_fusion.1
  (14 shorter events, 0.1 us)
Async XLA Ops:
  0.0 4.6 %copy-start = (bf16[8,1024,256]{2,1,0:T(8,128)(2,1)S(1)}, bf16[8,1024,256]{2,1,0:T(8,128)(2,1)}, u32[]{:S(2)}) copy-start(bf16[8,1024,256]{2,1,0:T(8,128)(2,1)} %constant.18.clone.table) | copy-start | bytes 12582916
  0.9 2.4 %copy-start.1 = (f32[2,256,2048]{2,1,0:T(8,128)S(1)}, f32[2,256,2048]{2,1,0:T(8,128)}, u32[]{:S(2)}) copy-start(f32[2,256,2048]{2,1,0:T(8,128)} %spectrum.1) | copy-start | bytes 12582916
  6.5 13.6 %collective-permute-start = (bf16[4,256,128]{2,1,0:T(8,128)(2,1)S(1)}, bf16[4,256,128]{2,1,0:T(8,128)(2,1)S(1)}, u32[]{:S(2)}, u32[]{:S(2)}) collective-permute-start(bf16[4,256,128]{2,1,0:T(8,128)(2,1)S(1)} %get-tuple-element.39), channel_id=1, source_target_pairs={{8,16},{12,20},{16,8},{20,12},{4,0},{24,28},{9,17},{13,21},{17,9},... | collective-permute-start | bytes 786440 | tf_op jit(solution)/shard_map/ppermute | solution.py:458
  7.8 18.1 %collective-permute-start.2 = (bf16[4,256,128]{2,1,0:T(8,128)(2,1)S(1)}, bf16[4,256,128]{2,1,0:T(8,128)(2,1)S(1)}, u32[]{:S(2)}, u32[]{:S(2)}) collective-permute-start(bf16[4,256,128]{2,1,0:T(8,128)(2,1)S(1)} %get-tuple-element.49), channel_id=1, source_target_pairs={{4,8},{8,4},{12,0},{16,28},{20,24},{24,20},{5,9},{9,5},{13,1},{17,... | collective-permute-start | bytes 786440 | tf_op jit(solution)/shard_map/ppermute | solution.py:458
  13.4 25.4 %copy-start.2 = (bf16[8,256,1024]{2,1,0:T(8,128)(2,1)S(1)}, bf16[8,256,1024]{2,1,0:T(8,128)(2,1)}, u32[]{:S(2)}) copy-start(bf16[8,256,1024]{2,1,0:T(8,128)(2,1)} %constant.17.clone.table) | copy-start | bytes 12582916
  13.4 25.4 %copy-start.3 = (f32[2,128,1024]{2,1,0:T(8,128)S(1)}, f32[2,128,1024]{2,1,0:T(8,128)}, u32[]{:S(2)}) copy-start(f32[2,128,1024]{2,1,0:T(8,128)} %images) | copy-start | bytes 3145732
  13.4 21.3 %collective-permute-start.3 = (bf16[4,256,128]{2,1,0:T(8,128)(2,1)S(1)}, bf16[4,256,128]{2,1,0:T(8,128)(2,1)S(1)}, u32[]{:S(2)}, u32[]{:S(2)}) collective-permute-start(bf16[4,256,128]{2,1,0:T(8,128)(2,1)S(1)} %get-tuple-element.50), channel_id=1, source_target_pairs={{8,20},{12,16},{16,12},{20,8},{4,0},{24,28},{9,21},{13,17},{17,13}... | collective-permute-start | bytes 786440 | tf_op jit(solution)/shard_map/ppermute | solution.py:458
  20.0 14.7 %collective-permute-start.1 = (bf16[4,256,128]{2,1,0:T(8,128)(2,1)S(1)}, bf16[4,256,128]{2,1,0:T(8,128)(2,1)S(1)}, u32[]{:S(2)}, u32[]{:S(2)}) collective-permute-start(bf16[4,256,128]{2,1,0:T(8,128)(2,1)S(1)} %get-tuple-element.48), channel_id=1, source_target_pairs={{4,0},{8,12},{12,8},{16,20},{20,16},{24,28},{5,1},{9,13},{13,9},{1... | collective-permute-start | bytes 786440 | tf_op jit(solution)/shard_map/ppermute | solution.py:458
  24.5 14.9 %collective-permute-start.4 = (bf16[4,256,128]{2,1,0:T(8,128)(2,1)S(1)}, bf16[4,256,128]{2,1,0:T(8,128)(2,1)S(1)}, u32[]{:S(2)}, u32[]{:S(2)}) collective-permute-start(bf16[4,256,128]{2,1,0:T(8,128)(2,1)S(1)} %class_4_blocks.1), channel_id=1, source_target_pairs={{0,16},{4,20},{8,24},{12,28},{16,0},{20,4},{24,8},{28,12},{1,17},{... | collective-permute-start | bytes 786440 | tf_op jit(solution)/shard_map/ppermute | solution.py:458
  24.6 23.3 %collective-permute-start.6 = (bf16[4,256,128]{2,1,0:T(8,128)(2,1)S(1)}, bf16[4,256,128]{2,1,0:T(8,128)(2,1)S(1)}, u32[]{:S(2)}, u32[]{:S(2)}) collective-permute-start(bf16[4,256,128]{2,1,0:T(8,128)(2,1)S(1)} %get-tuple-element.53.own), channel_id=1, source_target_pairs={{8,28},{12,24},{16,4},{20,0},{9,29},{13,25},{17,5},{21,1},{10,30},... | collective-permute-start | bytes 786440 | tf_op jit(solution)/shard_map/ppermute | solution.py:458
  25.9 28.5 %collective-permute-start.7 = (bf16[4,256,128]{2,1,0:T(8,128)(2,1)S(1)}, bf16[4,256,128]{2,1,0:T(8,128)(2,1)S(1)}, u32[]{:S(2)}, u32[]{:S(2)}) collective-permute-start(bf16[4,256,128]{2,1,0:T(8,128)(2,1)S(1)} %get-tuple-element.56), channel_id=1, source_target_pairs={{4,12},{8,0},{12,4},{16,24},{20,28},{24,16},{5,13},{9,1},{13,5},{1... | collective-permute-start | bytes 786440 | tf_op jit(solution)/shard_map/ppermute | solution.py:458
  34.8 19.6 %collective-permute-start.5 = (bf16[4,256,128]{2,1,0:T(8,128)(2,1)S(1)}, bf16[4,256,128]{2,1,0:T(8,128)(2,1)S(1)}, u32[]{:S(2)}, u32[]{:S(2)}) collective-permute-start(bf16[4,256,128]{2,1,0:T(8,128)(2,1)S(1)} %class_6_blocks.1), channel_id=1, source_target_pairs={{0,24},{4,28},{24,0},{28,4},{1,25},{5,29},{25,1},{29,5},{2,26},{6,... | collective-permute-start | bytes 786440 | tf_op jit(solution)/shard_map/ppermute | solution.py:458
  59.6 10.2 %collective-permute-start.10 = (bf16[4,256,128]{2,1,0:T(8,128)(2,1)S(1)}, bf16[4,256,128]{2,1,0:T(8,128)(2,1)S(1)}, u32[]{:S(2)}, u32[]{:S(2)}) collective-permute-start(bf16[4,256,128]{2,1,0:T(8,128)(2,1)S(1)} %get-tuple-element.61), channel_id=1, source_target_pairs={{0,12},{4,8},{8,4},{12,0},{16,28},{20,24},{24,20},{28,16},{1,13},{... | collective-permute-start | bytes 786440 | tf_op jit(solution)/shard_map/ppermute | solution.py:458
  59.7 13.9 %collective-permute-start.8 = (bf16[4,256,128]{2,1,0:T(8,128)(2,1)S(1)}, bf16[4,256,128]{2,1,0:T(8,128)(2,1)S(1)}, u32[]{:S(2)}, u32[]{:S(2)}) collective-permute-start(bf16[4,256,128]{2,1,0:T(8,128)(2,1)S(1)} %get-tuple-element.59), channel_id=1, source_target_pairs={{0,4},{4,0},{8,12},{12,8},{16,20},{20,16},{24,28},{28,24},{1,5},{5... | collective-permute-start | bytes 786440 | tf_op jit(solution)/shard_map/ppermute | solution.py:458
  60.8 12.9 %collective-permute-start.9 = (bf16[4,256,128]{2,1,0:T(8,128)(2,1)S(1)}, bf16[4,256,128]{2,1,0:T(8,128)(2,1)S(1)}, u32[]{:S(2)}, u32[]{:S(2)}) collective-permute-start(bf16[4,256,128]{2,1,0:T(8,128)(2,1)S(1)} %get-tuple-element.60), channel_id=1, source_target_pairs={{0,8},{4,12},{8,0},{12,4},{16,24},{20,28},{24,16},{28,20},{1,9},{5... | collective-permute-start | bytes 786440 | tf_op jit(solution)/shard_map/ppermute | solution.py:458
  76.3 3.0 %collective-permute-start.12 = (bf16[2,2,256,512]{3,2,1,0:T(8,128)(2,1)S(1)}, bf16[2,2,256,512]{3,2,1,0:T(8,128)(2,1)S(1)}, u32[]{:S(2)}, u32[]{:S(2)}) collective-permute-start(bf16[2,2,256,512]{3,2,1,0:T(8,128)(2,1)S(1)} %get-tuple-element.67), channel_id=1, source_target_pairs={{0,1},{1,0},{2,3},{3,2},{4,5},{5,4},{6,7},{7,6},{8,9},{9,8},{10,11... | collective-permute-start | bytes 3145736 | tf_op jit(solution)/shard_map/ppermute | solution.py:537
  76.4 7.8 %collective-permute-start.11 = (bf16[2,2,256,512]{3,2,1,0:T(8,128)(2,1)S(1)}, bf16[2,2,256,512]{3,2,1,0:T(8,128)(2,1)S(1)}, u32[]{:S(2)}, u32[]{:S(2)}) collective-permute-start(bf16[2,2,256,512]{3,2,1,0:T(8,128)(2,1)S(1)} %get-tuple-element.64), channel_id=1, source_target_pairs={{0,1},{1,0},{2,3},{3,2},{4,5},{5,4},{6,7},{7,6},{8,9},{9,8},{10,11... | collective-permute-start | bytes 3145736 | tf_op jit(solution)/shard_map/ppermute | solution.py:538
  79.3 4.9 %copy-start.4 = (f32[2,256,512]{2,1,0:T(8,128)}, f32[2,256,512]{2,1,0:T(8,128)S(1)}, u32[]{:S(2)}) copy-start(f32[2,256,512]{2,1,0:T(8,128)S(1)} %get-tuple-element.63) | copy-start | bytes 3145732
  79.5 16.5 %collective-permute-start.13 = (bf16[2,2,256,128]{3,2,1,0:T(8,128)(2,1)S(1)}, bf16[2,2,256,128]{3,2,1,0:T(8,128)(2,1)S(1)}, u32[]{:S(2)}, u32[]{:S(2)}) collective-permute-start(bf16[2,2,256,128]{3,2,1,0:T(8,128)(2,1)S(1)} %z_first_kernel.1), channel_id=1, source_target_pairs={{0,16},{4,20},{8,24},{20,4},{24,8},{28,12},{1,17},{5,21},{9,25},{2... | collective-permute-start | bytes 786440 | tf_op jit(solution)/shard_map/ppermute | solution.py:458
  82.2 16.7 %collective-permute-start.15 = (bf16[2,256,384]{2,1,0:T(8,128)(2,1)}, bf16[2,256,384]{2,1,0:T(8,128)(2,1)}, u32[]{:S(2)}, u32[]{:S(2)}) collective-permute-start(bf16[2,256,384]{2,1,0:T(8,128)(2,1)} %x_first_kernel.1), channel_id=1, source_target_pairs={{0,2},{2,0},{1,3},{3,1},{4,6},{6,4},{5,7},{7,5},{8,10},{10,8},{9,1... | collective-permute-start | bytes 1179656 | tf_op jit(solution)/shard_map/ppermute | solution.py:558
  96.9 14.4 %collective-permute-start.14 = (bf16[2,256,512]{2,1,0:T(8,128)(2,1)}, bf16[2,256,512]{2,1,0:T(8,128)(2,1)}, u32[]{:S(2)}, u32[]{:S(2)}) collective-permute-start(bf16[2,256,512]{2,1,0:T(8,128)(2,1)} %x_second_kernel.1), channel_id=1, source_target_pairs={{0,2},{2,0},{1,3},{3,1},{4,6},{6,4},{5,7},{7,5},{8,10},{10,8},{9,1... | collective-permute-start | bytes 1572872 | tf_op jit(solution)/shard_map/ppermute | solution.py:562
  100.1 15.9 %collective-permute-start.16 = (bf16[2,256,384]{2,1,0:T(8,128)(2,1)S(1)}, bf16[2,256,384]{2,1,0:T(8,128)(2,1)S(1)}, u32[]{:S(2)}, u32[]{:S(2)}) collective-permute-start(bf16[2,256,384]{2,1,0:T(8,128)(2,1)S(1)} %z_second_kernel.1), channel_id=1, source_target_pairs={{0,16},{4,20},{8,24},{20,4},{24,8},{28,12},{1,17},{5,21},{9,25},{2... | collective-permute-start | bytes 1179656 | tf_op jit(solution)/shard_map/ppermute | solution.py:458

commit v18 on v13

--- a/solution.py
+++ b/solution.py
@@ -370,17 +370,13 @@
     update_columns(True, starts, table, back, outs)
 
 
-def z_first_kernel(that_near, that_far, got_that, out):
-    cols = out.shape[3]
-    for i, kept in enumerate((that_near, that_far)):
-        total = kept[:, :, :cols] + got_that[i, :, :, :cols].astype(jnp.float32)
-        out[i] = total.astype(out.dtype)
-
-
-def x_first_kernel(that_far, got_that, out):
-    cols = that_far.shape[2] - out.shape[2]
-    total = that_far[:, :, cols:] + got_that[1, :, :, cols:].astype(jnp.float32)
-    out[...] = total.astype(out.dtype)
+def first_kernel(that_near, that_far, got_that, z_out, x_out):
+    cols = z_out.shape[3]
+    near = that_near[:, :, :cols] + got_that[0, :, :, :cols].astype(jnp.float32)
+    far = that_far[...] + got_that[1].astype(jnp.float32)
+    z_out[0] = near.astype(z_out.dtype)
+    z_out[1] = far[:, :, :cols].astype(z_out.dtype)
+    x_out[...] = far[:, :, cols:].astype(x_out.dtype)
 
 
 def z_second_kernel(that_near, got_that, got_x, out):
@@ -401,14 +397,14 @@
     out[...] = (total + got_z[1].astype(jnp.float32)).astype(out.dtype)
 
 
-def local_call(kernel, out_shape, spaces, scratch, flops, moved, name):
+def local_call(kernel, out_shape, spaces, scratch, flops, moved, name, limit=32):
     return pl.pallas_call(
         kernel,
         out_shape=out_shape,
         in_specs=[pl.BlockSpec(memory_space=space) for space in spaces],
         out_specs=jax.tree.map(lambda _: pl.BlockSpec(memory_space=pltpu.VMEM), out_shape),
         scratch_shapes=scratch,
-        compiler_params=pltpu.CompilerParams(vmem_limit_bytes=32 * 2**20),
+        compiler_params=pltpu.CompilerParams(vmem_limit_bytes=limit * 2**20),
         cost_estimate=pl.CostEstimate(flops=flops, bytes_accessed=moved, transcendentals=0),
         name=name,
     )
@@ -537,6 +533,7 @@
         flops // 4,
         8 * 2**20,
         "update_sent",
+        16,
     )(starts, by_col, *home)
     got_that = lax.ppermute(sent_that, "led", cores)
     got_this = lax.ppermute(sent_this, "led", cores)
@@ -548,23 +545,26 @@
         flops // 4,
         10 * 2**20,
         "update_kept",
+        16,
     )(starts, by_col, back)
 
-    def sum_call(kernel, shape, *values):
-        out_shape = jax.ShapeDtypeStruct(shape, bf16)
+    def sum_call(kernel, shapes, *values):
+        out_shape = [jax.ShapeDtypeStruct(shape, bf16) for shape in shapes]
         specs = [vmem] * len(values)
-        return local_call(kernel, out_shape, specs, [], 0, 2**20, kernel.__name__)(*values)
-
-    over = sum_call(z_first_kernel, (2, 2, rows, first), that_near, that_far, got_that)
-    got_z_first = permute(over, across)
-    over = sum_call(x_first_kernel, (2, rows, share - first), that_far, got_that)
-    got_x = lax.ppermute(over, "led", planes)
-    over_z = sum_call(z_second_kernel, (2, rows, share - first), that_near, got_that, got_x)
+        return local_call(kernel, out_shape, specs, [], 0, 2**20, kernel.__name__, 12)(*values)
+
+    rest = (2, rows, share - first)
+    over_z, over_x = sum_call(
+        first_kernel, [(2, 2, rows, first), rest], that_near, that_far, got_that
+    )
+    got_z_first = permute(over_z, across)
+    got_x = lax.ppermute(over_x, "led", planes)
+    (over_z,) = sum_call(z_second_kernel, [rest], that_near, got_that, got_x)
     got_z_second = permute(over_z, across)
-    over = sum_call(x_own_kernel, (2, rows, share - first), this_far, got_this)
+    (over,) = sum_call(x_own_kernel, [rest], this_far, got_this)
     got_x_own = lax.ppermute(over, "led", planes)
     over, got_z_first = lax.optimization_barrier((over_z, got_z_first))
-    over = sum_call(x_last_kernel, (2, rows, first), this_far, got_this, got_z_first)
+    (over,) = sum_call(x_last_kernel, [(2, rows, first)], this_far, got_this, got_z_first)
     got_x_last = lax.ppermute(over, "led", planes)
 
     def widen(value, before):

time: 116 us -> 116 us (level)
  starting transfers between devices: 34.4 us -> 35.7 us
    ppermute x1, starting transfers between devices: 0.07 us -> 1.34 us  [body_slabs(): got_x_last = lax.ppermute(over, 'led', planes)]
    ppermute x1, waiting for transfers between devices: 3.78 us -> 2.6 us  [body_slabs(): got_x_last = lax.ppermute(over, 'led', planes)]
    pallas_call x5 -> x4, Pallas kernels: 2.93 us -> 2.25 us  [sum_call(): local_call(kernel, out_shape, specs, [], 0, 2 ** 20, kernel.__name__, 12)]
  transfers between devices with their start and end apart: 18 -> 18, of which waited for: 12 -> 12; matrix products, arithmetic and copies ran while one was open for 1% -> 1% of each run, Pallas kernels for 8% -> 7%
where the time goes in v18:
time: 116 us
  waiting for transfers between devices  51.3 us (44%)
  starting transfers between devices  35.7 us (31%)
  Pallas kernels  20.2 us (17%)
  local copies, waits for them, and re-layouts  4.62 us (4%)
  other arithmetic  3.69 us (3%)
    ppermute x13, waiting for transfers between devices, permute(): return lax.ppermute(sent, 'slab', pairs)  40.3 us
    ppermute x13, starting transfers between devices, permute(): return lax.ppermute(sent, 'slab', pairs)  31.7 us
    ppermute x1, waiting for transfers between devices, body_slabs(): got_x = lax.ppermute(over_x, 'led', planes)  7.25 us
    pallas_call x1, Pallas kernels, body_slabs(): local_call(field_kernel, [sent_block] * HALF, [vmem] * 11, [pltpu.VMEM((w...  5.31 us
    pallas_call x2, Pallas kernels, rows_call(): local_call(functools.partial(rows_kernel, which), [sent_block] * count, [...  4.69 us
    unnamed x16, local copies, waits for them, and re-layouts  4.61 us
    pallas_call x1, Pallas kernels, body_slabs(): local_call(sent_kernel, [jax.ShapeDtypeStruct((2,) + piece, bf16), jax.Sh...  3.59 us
    ppermute x1, waiting for transfers between devices, body_slabs(): got_x_last = lax.ppermute(over, 'led', planes)  2.6 us
  transfers between devices with their start and end apart: 18, of which 12 were waited for; matrix products, arithmetic and copies ran while one was open for 1% of the time, Pallas kernels for 7%

profile of v18, /device:TPU:4, one launch (start us, length us, event | category | flops | bytes accessed | tf_op | source)
XLA Modules:
  0.0 115.8 jit_solution(18198094152440331915)
XLA Ops:
  0.0 0.9 pad_add_fusion.starts
  0.9 2.4 %copy-done.1 = f32[2,256,2048]{2,1,0:T(8,128)S(1)} copy-done((f32[2,256,2048]{2,1,0:T(8,128)S(1)}, f32[2,256,2048]{2,1,0:T(8,128)}, u32[]{:S(2)}) %copy-start.1) | copy-done | bytes 4194328
  3.3 1.4 %windows.1.window = bf16[1024,1024]{1,0:T(8,128)(2,1)S(1)} custom-call(s32[4]{0:T(128)S(1)} %pad_add_fusion.starts, f32[2,256,2048]{2,1,0:T(8,128)S(1)} %copy-done.1), custom_call_target="tpu_custom_call" | custom-call | bytes 6291456 | tf_op jit(solution)/shard_map/windows/pallas_call | solution.py:434
  4.7 1.8 %rows_round_1.1 = (bf16[4,256,128]{2,1,0:T(8,128)(2,1)S(1)}, bf16[4,256,128]{2,1,0:T(8,128)(2,1)S(1)}, bf16[4,256,128]{2,1,0:T(8,128)(2,1)S(1)}) custom-call(bf16[1024,1024]{1,0:T(8,128)(2,1)S(1)} %windows.1.window, bf16[8,1024,256]{2,1,0:T(8,128)(2,1)S(1)} %copy-done), custom_call_target="tpu_custom_call" | custom-call | flops 1610612736 | bytes 5242880 | tf_op jit(solution)/shard_map/rows_round_1/pallas_call | solution.py:446
  6.5 1.3 %collective-permute-start = (bf16[4,256,128]{2,1,0:T(8,128)(2,1)S(1)}, bf16[4,256,128]{2,1,0:T(8,128)(2,1)S(1)}, u32[]{:S(2)}, u32[]{:S(2)}) collective-permute-start(bf16[4,256,128]{2,1,0:T(8,128)(2,1)S(1)} %get-tuple-element.43), channel_id=1, source_target_pairs={{8,16},{12,20},{16,8},{20,12},{4,0},{24,28},{9,17},{13,21},{17,9},... | collective-permute-start | bytes 786440 | tf_op jit(solution)/shard_map/ppermute | solution.py:459
  7.8 5.7 %collective-permute-start.1 = (bf16[4,256,128]{2,1,0:T(8,128)(2,1)S(1)}, bf16[4,256,128]{2,1,0:T(8,128)(2,1)S(1)}, u32[]{:S(2)}, u32[]{:S(2)}) collective-permute-start(bf16[4,256,128]{2,1,0:T(8,128)(2,1)S(1)} %get-tuple-element.44), channel_id=1, source_target_pairs={{4,12},{8,0},{12,4},{16,24},{20,28},{24,16},{5,13},{9,1},{13,5},{1... | collective-permute-start | bytes 786440 | tf_op jit(solution)/shard_map/ppermute | solution.py:459
  13.5 0.0 copy-start.2
  13.5 1.6 %collective-permute-start.3 = (bf16[4,256,128]{2,1,0:T(8,128)(2,1)S(1)}, bf16[4,256,128]{2,1,0:T(8,128)(2,1)S(1)}, u32[]{:S(2)}, u32[]{:S(2)}) collective-permute-start(bf16[4,256,128]{2,1,0:T(8,128)(2,1)S(1)} %get-tuple-element.54), channel_id=1, source_target_pairs={{8,20},{12,16},{16,12},{20,8},{4,0},{24,28},{9,21},{13,17},{17,13}... | collective-permute-start | bytes 786440 | tf_op jit(solution)/shard_map/ppermute | solution.py:459
  15.1 2.9 %rows_round_2.1 = (bf16[4,256,128]{2,1,0:T(8,128)(2,1)S(1)}, bf16[4,256,128]{2,1,0:T(8,128)(2,1)S(1)}, bf16[4,256,128]{2,1,0:T(8,128)(2,1)S(1)}, bf16[4,256,128]...) custom-call(bf16[1024,1024]{1,0:T(8,128)(2,1)S(1)} %windows.1.window, bf16[8,1024,256]{2,1,0:T(8,128)(2,1)S(1)} %copy-done), custom_call_target="tpu_custom_call" | custom-call | flops 2684354560 | bytes 5242880 | tf_op jit(solution)/shard_map/rows_round_2/pallas_call | solution.py:446
  18.0 1.5 %collective-permute-done.1.rest_7_ = bf16[4,256,128]{2,1,0:T(8,128)(2,1)S(1)} collective-permute-done((bf16[4,256,128]{2,1,0:T(8,128)(2,1)S(1)}, bf16[4,256,128]{2,1,0:T(8,128)(2,1)S(1)}, u32[]{:S(2)}, u32[]{:S(2)}) %collective-permute-start.1) | collective-permute-done | bytes 262176 | tf_op jit(solution)/shard_map/ppermute | solution.py:459
  19.5 1.8 %collective-permute-start.2 = (bf16[4,256,128]{2,1,0:T(8,128)(2,1)S(1)}, bf16[4,256,128]{2,1,0:T(8,128)(2,1)S(1)}, u32[]{:S(2)}, u32[]{:S(2)}) collective-permute-start(bf16[4,256,128]{2,1,0:T(8,128)(2,1)S(1)} %get-tuple-element.53), channel_id=1, source_target_pairs={{4,0},{8,12},{12,8},{16,20},{20,16},{24,28},{5,1},{9,13},{13,9},{1... | collective-permute-start | bytes 786440 | tf_op jit(solution)/shard_map/ppermute | solution.py:459
  21.3 3.2 %collective-permute-start.4 = (bf16[4,256,128]{2,1,0:T(8,128)(2,1)S(1)}, bf16[4,256,128]{2,1,0:T(8,128)(2,1)S(1)}, u32[]{:S(2)}, u32[]{:S(2)}) collective-permute-start(bf16[4,256,128]{2,1,0:T(8,128)(2,1)S(1)} %class_4_blocks.1), channel_id=1, source_target_pairs={{0,16},{4,20},{8,24},{12,28},{16,0},{20,4},{24,8},{28,12},{1,17},{... | collective-permute-start | bytes 786440 | tf_op jit(solution)/shard_map/ppermute | solution.py:459
  24.5 1.3 %collective-permute-start.6 = (bf16[4,256,128]{2,1,0:T(8,128)(2,1)S(1)}, bf16[4,256,128]{2,1,0:T(8,128)(2,1)S(1)}, u32[]{:S(2)}, u32[]{:S(2)}) collective-permute-start(bf16[4,256,128]{2,1,0:T(8,128)(2,1)S(1)} %get-tuple-element.57.own), channel_id=1, source_target_pairs={{8,28},{12,24},{16,4},{20,0},{9,29},{13,25},{17,5},{21,1},{10,30},... | collective-permute-start | bytes 786440 | tf_op jit(solution)/shard_map/ppermute | solution.py:459
  25.8 5.5 %collective-permute-start.7 = (bf16[4,256,128]{2,1,0:T(8,128)(2,1)S(1)}, bf16[4,256,128]{2,1,0:T(8,128)(2,1)S(1)}, u32[]{:S(2)}, u32[]{:S(2)}) collective-permute-start(bf16[4,256,128]{2,1,0:T(8,128)(2,1)S(1)} %get-tuple-element.61), channel_id=1, source_target_pairs={{4,8},{8,4},{12,0},{16,28},{20,24},{24,20},{5,9},{9,5},{13,1},{17,... | collective-permute-start | bytes 786440 | tf_op jit(solution)/shard_map/ppermute | solution.py:459
  31.4 1.9 %collective-permute-start.5 = (bf16[4,256,128]{2,1,0:T(8,128)(2,1)S(1)}, bf16[4,256,128]{2,1,0:T(8,128)(2,1)S(1)}, u32[]{:S(2)}, u32[]{:S(2)}) collective-permute-start(bf16[4,256,128]{2,1,0:T(8,128)(2,1)S(1)} %class_6_blocks.1), channel_id=1, source_target_pairs={{0,24},{4,28},{24,0},{28,4},{1,25},{5,29},{25,1},{29,5},{2,26},{6,... | collective-permute-start | bytes 786440 | tf_op jit(solution)/shard_map/ppermute | solution.py:459
  33.3 0.6 amplitude.1
  33.9 8.8 %collective-permute-done.4.rest_2_ = bf16[4,256,128]{2,1,0:T(8,128)(2,1)S(1)} collective-permute-done((bf16[4,256,128]{2,1,0:T(8,128)(2,1)S(1)}, bf16[4,256,128]{2,1,0:T(8,128)(2,1)S(1)}, u32[]{:S(2)}, u32[]{:S(2)}) %collective-permute-start.4) | collective-permute-done | bytes 262176 | tf_op jit(solution)/shard_map/ppermute | solution.py:459
  42.7 3.9 %collective-permute-done.6.rest_4_ = bf16[4,256,128]{2,1,0:T(8,128)(2,1)S(1)} collective-permute-done((bf16[4,256,128]{2,1,0:T(8,128)(2,1)S(1)}, bf16[4,256,128]{2,1,0:T(8,128)(2,1)S(1)}, u32[]{:S(2)}, u32[]{:S(2)}) %collective-permute-start.6) | collective-permute-done | bytes 262176 | tf_op jit(solution)/shard_map/ppermute | solution.py:459
  46.6 3.6 %collective-permute-done.7.rest_8_ = bf16[4,256,128]{2,1,0:T(8,128)(2,1)S(1)} collective-permute-done((bf16[4,256,128]{2,1,0:T(8,128)(2,1)S(1)}, bf16[4,256,128]{2,1,0:T(8,128)(2,1)S(1)}, u32[]{:S(2)}, u32[]{:S(2)}) %collective-permute-start.7) | collective-permute-done | bytes 262176 | tf_op jit(solution)/shard_map/ppermute | solution.py:459
  50.2 5.3 %modulus_step.1 = (bf16[4,256,128]{2,1,0:T(8,128)(2,1)S(1)}, bf16[4,256,128]{2,1,0:T(8,128)(2,1)S(1)}, bf16[4,256,128]{2,1,0:T(8,128)(2,1)S(1)}, bf16[4,256,128]{2,1,0:T(8,128)(2,1)S(1)}) custom-call(f32[1024,256]{1,0:T(8,128)S(1)} %get-tuple-element.50.amplitude, bf16[8,256,1024]{2,1,0:T(8,128)(2,1)S(1)} %get-tuple-element.51.table, ...), custom_call_target="tpu_custom_call" | custom-call | flops 4294967296 | bytes 12582912 | tf_op jit(solution)/shard_map/modulus_step/pallas_call | solution.py:499
  55.5 0.1 collective-permute-start.10
  55.6 2.4 %collective-permute-start.8 = (bf16[4,256,128]{2,1,0:T(8,128)(2,1)S(1)}, bf16[4,256,128]{2,1,0:T(8,128)(2,1)S(1)}, u32[]{:S(2)}, u32[]{:S(2)}) collective-permute-start(bf16[4,256,128]{2,1,0:T(8,128)(2,1)S(1)} %get-tuple-element.63), channel_id=1, source_target_pairs={{0,4},{4,0},{8,12},{12,8},{16,20},{20,16},{24,28},{28,24},{1,5},{5... | collective-permute-start | bytes 786440 | tf_op jit(solution)/shard_map/ppermute | solution.py:459
  58.0 1.4 %collective-permute-start.9 = (bf16[4,256,128]{2,1,0:T(8,128)(2,1)S(1)}, bf16[4,256,128]{2,1,0:T(8,128)(2,1)S(1)}, u32[]{:S(2)}, u32[]{:S(2)}) collective-permute-start(bf16[4,256,128]{2,1,0:T(8,128)(2,1)S(1)} %get-tuple-element.64), channel_id=1, source_target_pairs={{0,8},{4,12},{8,0},{12,4},{16,24},{20,28},{24,16},{28,20},{1,9},{5... | collective-permute-start | bytes 786440 | tf_op jit(solution)/shard_map/ppermute | solution.py:459
  59.4 6.3 %collective-permute-done.10.rest_3_ = bf16[4,256,128]{2,1,0:T(8,128)(2,1)S(1)} collective-permute-done((bf16[4,256,128]{2,1,0:T(8,128)(2,1)S(1)}, bf16[4,256,128]{2,1,0:T(8,128)(2,1)S(1)}, u32[]{:S(2)}, u32[]{:S(2)}) %collective-permute-start.10) | collective-permute-done | bytes 262176 | tf_op jit(solution)/shard_map/ppermute | solution.py:459
  65.6 2.7 %collective-permute-done.8.rest_1_ = bf16[4,256,128]{2,1,0:T(8,128)(2,1)S(1)} collective-permute-done((bf16[4,256,128]{2,1,0:T(8,128)(2,1)S(1)}, bf16[4,256,128]{2,1,0:T(8,128)(2,1)S(1)}, u32[]{:S(2)}, u32[]{:S(2)}) %collective-permute-start.8) | collective-permute-done | bytes 262176 | tf_op jit(solution)/shard_map/ppermute | solution.py:459
  68.4 1.7 %collective-permute-done.9.rest_2_ = bf16[4,256,128]{2,1,0:T(8,128)(2,1)S(1)} collective-permute-done((bf16[4,256,128]{2,1,0:T(8,128)(2,1)S(1)}, bf16[4,256,128]{2,1,0:T(8,128)(2,1)S(1)}, u32[]{:S(2)}, u32[]{:S(2)}) %collective-permute-start.9) | collective-permute-done | bytes 262176 | tf_op jit(solution)/shard_map/ppermute | solution.py:459
  70.1 3.6 %update_sent.1 = (bf16[2,2,256,512]{3,2,1,0:T(8,128)(2,1)}, bf16[2,2,256,512]{3,2,1,0:T(8,128)(2,1)S(1)}, bf16[1024,512]{1,0:T(8,128)(2,1)S(1)}) custom-call(s32[4]{0:T(128)S(1)} %pad_add_fusion.starts, bf16[8,1024,256]{2,1,0:T(8,128)(2,1)S(1)} %copy-done, bf16[4,256,128]{2,1,0:T(8,128)(2,1)S(1)} %get-tuple-element.62.rest_0_, ...), custom_call_target="tpu_custom_call" | custom-call | flops 1073741824 | bytes 8388608 | tf_op jit(solution)/shard_map/update_sent/pallas_call | solution.py:524
  73.7 0.5 collective-permute-start.11
  74.2 2.4 %update_kept.1 = (f32[2,256,512]{2,1,0:T(8,128)S(1)}, f32[2,256,512]{2,1,0:T(8,128)S(1)}, f32[2,256,512]{2,1,0:T(8,128)S(1)}, f32[2,256,512]{2,1,0:T(8,128)S(1)}) custom-call(s32[4]{0:T(128)S(1)} %pad_add_fusion.starts, bf16[8,1024,256]{2,1,0:T(8,128)(2,1)S(1)} %copy-done, bf16[1024,512]{1,0:T(8,128)(2,1)S(1)} %get-tuple-element.66.back), custom_call_target="tpu_custom_call" | custom-call | flops 1073741824 | bytes 10485760 | tf_op jit(solution)/shard_map/update_kept/pallas_call | solution.py:540
  76.7 1.2 %collective-permute-done.12.got_that = bf16[2,2,256,512]{3,2,1,0:T(8,128)(2,1)S(1)} collective-permute-done((bf16[2,2,256,512]{3,2,1,0:T(8,128)(2,1)S(1)}, bf16[2,2,256,512]{3,2,1,0:T(8,128)(2,1)S(1)}, u32[]{:S(2)}, u32[]{:S(2)}) %collective-permute-start.12) | collective-permute-done | bytes 1048608 | tf_op jit(solution)/shard_map/ppermute | solution.py:538
  77.8 1.0 first_kernel.1
  78.8 1.0 copy-done.3
  79.8 1.5 %collective-permute-start.13 = (bf16[2,256,384]{2,1,0:T(8,128)(2,1)}, bf16[2,256,384]{2,1,0:T(8,128)(2,1)}, u32[]{:S(2)}, u32[]{:S(2)}) collective-permute-start(bf16[2,256,384]{2,1,0:T(8,128)(2,1)} %get-tuple-element.72), channel_id=1, source_target_pairs={{0,2},{2,0},{1,3},{3,1},{4,6},{6,4},{5,7},{7,5},{8,10},{10,8},{9,1... | collective-permute-start | bytes 1179656 | tf_op jit(solution)/shard_map/ppermute | solution.py:561
  81.3 2.8 %collective-permute-start.14 = (bf16[2,2,256,128]{3,2,1,0:T(8,128)(2,1)}, bf16[2,2,256,128]{3,2,1,0:T(8,128)(2,1)S(1)}, u32[]{:S(2)}, u32[]{:S(2)}) collective-permute-start(bf16[2,2,256,128]{3,2,1,0:T(8,128)(2,1)} %get-tuple-element.73), channel_id=1, source_target_pairs={{0,16},{4,20},{8,24},{20,4},{24,8},{28,12},{1,17},{5,21},{9,25},{2... | collective-permute-start | bytes 786440 | tf_op jit(solution)/shard_map/ppermute | solution.py:459
  84.2 0.1 x_own_kernel.1
  84.2 0.6 collective-permute-start.15
  84.8 7.2 %collective-permute-done.13.got_x = bf16[2,256,384]{2,1,0:T(8,128)(2,1)} collective-permute-done((bf16[2,256,384]{2,1,0:T(8,128)(2,1)}, bf16[2,256,384]{2,1,0:T(8,128)(2,1)}, u32[]{:S(2)}, u32[]{:S(2)}) %collective-permute-start.13) | collective-permute-done | bytes 393248 | tf_op jit(solution)/shard_map/ppermute | solution.py:561
  92.1 1.2 %copy-done.4 = f32[2,256,512]{2,1,0:T(8,128)S(1)} copy-done((f32[2,256,512]{2,1,0:T(8,128)S(1)}, f32[2,256,512]{2,1,0:T(8,128)}, u32[]{:S(2)}) %copy-start.4) | copy-done | bytes 1048600
  93.3 1.1 z_second_kernel.1
  94.4 2.8 %collective-permute-start.17 = (bf16[2,256,384]{2,1,0:T(8,128)(2,1)S(1)}, bf16[2,256,384]{2,1,0:T(8,128)(2,1)S(1)}, u32[]{:S(2)}, u32[]{:S(2)}) collective-permute-start(bf16[2,256,384]{2,1,0:T(8,128)(2,1)S(1)} %z_second_kernel.1), channel_id=1, source_target_pairs={{0,16},{4,20},{8,24},{20,4},{24,8},{28,12},{1,17},{5,21},{9,25},{2... | collective-permute-start | bytes 1179656 | tf_op jit(solution)/shard_map/ppermute | solution.py:459
  97.3 0.2 collective-permute-done.14.got_z
  97.5 0.1 x_last_kernel.1
  97.6 1.3 %collective-permute-start.16 = (bf16[2,256,128]{2,1,0:T(8,128)(2,1)S(1)}, bf16[2,256,128]{2,1,0:T(8,128)(2,1)S(1)}, u32[]{:S(2)}, u32[]{:S(2)}) collective-permute-start(bf16[2,256,128]{2,1,0:T(8,128)(2,1)S(1)} %x_last_kernel.1), channel_id=1, source_target_pairs={{0,2},{2,0},{1,3},{3,1},{4,6},{6,4},{5,7},{7,5},{8,10},{10,8},{9,1... | collective-permute-start | bytes 393224 | tf_op jit(solution)/shard_map/ppermute | solution.py:568
  98.9 1.5 %fusion.1 = f32[2,256,512]{2,1,0:T(8,128)S(1)} fusion(f32[2,256,512]{2,1,0:T(8,128)S(1)} %copy-done.7, f32[2,256,2048]{2,1,0:T(8,128)} %spectrum.1, s32[]{:T(128)S(6)} %select_n.3, bf16[2,2,256,512]{3,2,1,0:T(8,128)(2,1)S(1)} %collective-permute-done.11.got_this, bf16[2,256,128]{2,1,0:T(8,128)(2,1)S(1)} %slice_bitcast_fusion.1), kind=kLoop, calls=%fused_computation.2 | loop fusion | flops 1310720 | bytes 3801092 | tf_op jit(solution)/shard_map/add | solution.py:575
  100.5 2.6 %collective-permute-done.16 = bf16[2,256,128]{2,1,0:T(8,128)(2,1)S(1)} collective-permute-done((bf16[2,256,128]{2,1,0:T(8,128)(2,1)S(1)}, bf16[2,256,128]{2,1,0:T(8,128)(2,1)S(1)}, u32[]{:S(2)}, u32[]{:S(2)}) %collective-permute-start.16) | collective-permute-done | bytes 131104 | tf_op jit(solution)/shard_map/ppermute | solution.py:568
  103.1 0.2 add_add_fusion
  103.3 11.5 %collective-permute-done.17 = bf16[2,256,384]{2,1,0:T(8,128)(2,1)S(1)} collective-permute-done((bf16[2,256,384]{2,1,0:T(8,128)(2,1)S(1)}, bf16[2,256,384]{2,1,0:T(8,128)(2,1)S(1)}, u32[]{:S(2)}, u32[]{:S(2)}) %collective-permute-start.17) | collective-permute-done | bytes 393248 | tf_op jit(solution)/shard_map/ppermute | solution.py:459
  114.7 1.1 convert_add_fusion.1
  (22 shorter events, 0.1 us)
Async XLA Ops:
  0.0 4.6 %copy-start = (bf16[8,1024,256]{2,1,0:T(8,128)(2,1)S(1)}, bf16[8,1024,256]{2,1,0:T(8,128)(2,1)}, u32[]{:S(2)}) copy-start(bf16[8,1024,256]{2,1,0:T(8,128)(2,1)} %constant.18.clone.table) | copy-start | bytes 12582916
  0.9 2.4 %copy-start.1 = (f32[2,256,2048]{2,1,0:T(8,128)S(1)}, f32[2,256,2048]{2,1,0:T(8,128)}, u32[]{:S(2)}) copy-start(f32[2,256,2048]{2,1,0:T(8,128)} %spectrum.1) | copy-start | bytes 12582916
  6.5 11.5 %collective-permute-start = (bf16[4,256,128]{2,1,0:T(8,128)(2,1)S(1)}, bf16[4,256,128]{2,1,0:T(8,128)(2,1)S(1)}, u32[]{:S(2)}, u32[]{:S(2)}) collective-permute-start(bf16[4,256,128]{2,1,0:T(8,128)(2,1)S(1)} %get-tuple-element.43), channel_id=1, source_target_pairs={{8,16},{12,20},{16,8},{20,12},{4,0},{24,28},{9,17},{13,21},{17,9},... | collective-permute-start | bytes 786440 | tf_op jit(solution)/shard_map/ppermute | solution.py:459
  7.8 11.7 %collective-permute-start.1 = (bf16[4,256,128]{2,1,0:T(8,128)(2,1)S(1)}, bf16[4,256,128]{2,1,0:T(8,128)(2,1)S(1)}, u32[]{:S(2)}, u32[]{:S(2)}) collective-permute-start(bf16[4,256,128]{2,1,0:T(8,128)(2,1)S(1)} %get-tuple-element.44), channel_id=1, source_target_pairs={{4,12},{8,0},{12,4},{16,24},{20,28},{24,16},{5,13},{9,1},{13,5},{1... | collective-permute-start | bytes 786440 | tf_op jit(solution)/shard_map/ppermute | solution.py:459
  13.5 19.9 %copy-start.2 = (bf16[8,256,1024]{2,1,0:T(8,128)(2,1)S(1)}, bf16[8,256,1024]{2,1,0:T(8,128)(2,1)}, u32[]{:S(2)}) copy-start(bf16[8,256,1024]{2,1,0:T(8,128)(2,1)} %constant.17.clone.table) | copy-start | bytes 12582916
  13.5 19.9 %copy-start.5 = (f32[2,128,1024]{2,1,0:T(8,128)S(1)}, f32[2,128,1024]{2,1,0:T(8,128)}, u32[]{:S(2)}) copy-start(f32[2,128,1024]{2,1,0:T(8,128)} %images) | copy-start | bytes 3145732
  13.5 17.8 %collective-permute-start.3 = (bf16[4,256,128]{2,1,0:T(8,128)(2,1)S(1)}, bf16[4,256,128]{2,1,0:T(8,128)(2,1)S(1)}, u32[]{:S(2)}, u32[]{:S(2)}) collective-permute-start(bf16[4,256,128]{2,1,0:T(8,128)(2,1)S(1)} %get-tuple-element.54), channel_id=1, source_target_pairs={{8,20},{12,16},{16,12},{20,8},{4,0},{24,28},{9,21},{13,17},{17,13}... | collective-permute-start | bytes 786440 | tf_op jit(solution)/shard_map/ppermute | solution.py:459
  19.5 11.9 %collective-permute-start.2 = (bf16[4,256,128]{2,1,0:T(8,128)(2,1)S(1)}, bf16[4,256,128]{2,1,0:T(8,128)(2,1)S(1)}, u32[]{:S(2)}, u32[]{:S(2)}) collective-permute-start(bf16[4,256,128]{2,1,0:T(8,128)(2,1)S(1)} %get-tuple-element.53), channel_id=1, source_target_pairs={{4,0},{8,12},{12,8},{16,20},{20,16},{24,28},{5,1},{9,13},{13,9},{1... | collective-permute-start | bytes 786440 | tf_op jit(solution)/shard_map/ppermute | solution.py:459
  21.3 21.4 %collective-permute-start.4 = (bf16[4,256,128]{2,1,0:T(8,128)(2,1)S(1)}, bf16[4,256,128]{2,1,0:T(8,128)(2,1)S(1)}, u32[]{:S(2)}, u32[]{:S(2)}) collective-permute-start(bf16[4,256,128]{2,1,0:T(8,128)(2,1)S(1)} %class_4_blocks.1), channel_id=1, source_target_pairs={{0,16},{4,20},{8,24},{12,28},{16,0},{20,4},{24,8},{28,12},{1,17},{... | collective-permute-start | bytes 786440 | tf_op jit(solution)/shard_map/ppermute | solution.py:459
  24.5 22.1 %collective-permute-start.6 = (bf16[4,256,128]{2,1,0:T(8,128)(2,1)S(1)}, bf16[4,256,128]{2,1,0:T(8,128)(2,1)S(1)}, u32[]{:S(2)}, u32[]{:S(2)}) collective-permute-start(bf16[4,256,128]{2,1,0:T(8,128)(2,1)S(1)} %get-tuple-element.57.own), channel_id=1, source_target_pairs={{8,28},{12,24},{16,4},{20,0},{9,29},{13,25},{17,5},{21,1},{10,30},... | collective-permute-start | bytes 786440 | tf_op jit(solution)/shard_map/ppermute | solution.py:459
  25.8 24.4 %collective-permute-start.7 = (bf16[4,256,128]{2,1,0:T(8,128)(2,1)S(1)}, bf16[4,256,128]{2,1,0:T(8,128)(2,1)S(1)}, u32[]{:S(2)}, u32[]{:S(2)}) collective-permute-start(bf16[4,256,128]{2,1,0:T(8,128)(2,1)S(1)} %get-tuple-element.61), channel_id=1, source_target_pairs={{4,8},{8,4},{12,0},{16,28},{20,24},{24,20},{5,9},{9,5},{13,1},{17,... | collective-permute-start | bytes 786440 | tf_op jit(solution)/shard_map/ppermute | solution.py:459
  31.4 18.8 %collective-permute-start.5 = (bf16[4,256,128]{2,1,0:T(8,128)(2,1)S(1)}, bf16[4,256,128]{2,1,0:T(8,128)(2,1)S(1)}, u32[]{:S(2)}, u32[]{:S(2)}) collective-permute-start(bf16[4,256,128]{2,1,0:T(8,128)(2,1)S(1)} %class_6_blocks.1), channel_id=1, source_target_pairs={{0,24},{4,28},{24,0},{28,4},{1,25},{5,29},{25,1},{29,5},{2,26},{6,... | collective-permute-start | bytes 786440 | tf_op jit(solution)/shard_map/ppermute | solution.py:459
  55.5 10.1 %collective-permute-start.10 = (bf16[4,256,128]{2,1,0:T(8,128)(2,1)S(1)}, bf16[4,256,128]{2,1,0:T(8,128)(2,1)S(1)}, u32[]{:S(2)}, u32[]{:S(2)}) collective-permute-start(bf16[4,256,128]{2,1,0:T(8,128)(2,1)S(1)} %get-tuple-element.65), channel_id=1, source_target_pairs={{0,12},{4,8},{8,4},{12,0},{16,28},{20,24},{24,20},{28,16},{1,13},{... | collective-permute-start | bytes 786440 | tf_op jit(solution)/shard_map/ppermute | solution.py:459
  55.6 12.8 %collective-permute-start.8 = (bf16[4,256,128]{2,1,0:T(8,128)(2,1)S(1)}, bf16[4,256,128]{2,1,0:T(8,128)(2,1)S(1)}, u32[]{:S(2)}, u32[]{:S(2)}) collective-permute-start(bf16[4,256,128]{2,1,0:T(8,128)(2,1)S(1)} %get-tuple-element.63), channel_id=1, source_target_pairs={{0,4},{4,0},{8,12},{12,8},{16,20},{20,16},{24,28},{28,24},{1,5},{5... | collective-permute-start | bytes 786440 | tf_op jit(solution)/shard_map/ppermute | solution.py:459
  58.0 12.1 %collective-permute-start.9 = (bf16[4,256,128]{2,1,0:T(8,128)(2,1)S(1)}, bf16[4,256,128]{2,1,0:T(8,128)(2,1)S(1)}, u32[]{:S(2)}, u32[]{:S(2)}) collective-permute-start(bf16[4,256,128]{2,1,0:T(8,128)(2,1)S(1)} %get-tuple-element.64), channel_id=1, source_target_pairs={{0,8},{4,12},{8,0},{12,4},{16,24},{20,28},{24,16},{28,20},{1,9},{5... | collective-permute-start | bytes 786440 | tf_op jit(solution)/shard_map/ppermute | solution.py:459
  73.7 4.1 %collective-permute-start.12 = (bf16[2,2,256,512]{3,2,1,0:T(8,128)(2,1)S(1)}, bf16[2,2,256,512]{3,2,1,0:T(8,128)(2,1)S(1)}, u32[]{:S(2)}, u32[]{:S(2)}) collective-permute-start(bf16[2,2,256,512]{3,2,1,0:T(8,128)(2,1)S(1)} %get-tuple-element.70), channel_id=1, source_target_pairs={{0,1},{1,0},{2,3},{3,2},{4,5},{5,4},{6,7},{7,6},{8,9},{9,8},{10,11... | collective-permute-start | bytes 3145736 | tf_op jit(solution)/shard_map/ppermute | solution.py:538
  73.7 10.5 %collective-permute-start.11 = (bf16[2,2,256,512]{3,2,1,0:T(8,128)(2,1)}, bf16[2,2,256,512]{3,2,1,0:T(8,128)(2,1)S(1)}, u32[]{:S(2)}, u32[]{:S(2)}) collective-permute-start(bf16[2,2,256,512]{3,2,1,0:T(8,128)(2,1)} %get-tuple-element.68), channel_id=1, source_target_pairs={{0,1},{1,0},{2,3},{3,2},{4,5},{5,4},{6,7},{7,6},{8,9},{9,8},{10,11... | collective-permute-start | bytes 3145736 | tf_op jit(solution)/shard_map/ppermute | solution.py:539
  76.7 2.2 %copy-start.6 = (f32[2,256,512]{2,1,0:T(8,128)}, f32[2,256,512]{2,1,0:T(8,128)S(1)}, u32[]{:S(2)}) copy-start(f32[2,256,512]{2,1,0:T(8,128)S(1)} %get-tuple-element.67) | copy-start | bytes 3145732
  78.8 1.0 copy-start.3
  79.8 12.3 %collective-permute-start.13 = (bf16[2,256,384]{2,1,0:T(8,128)(2,1)}, bf16[2,256,384]{2,1,0:T(8,128)(2,1)}, u32[]{:S(2)}, u32[]{:S(2)}) collective-permute-start(bf16[2,256,384]{2,1,0:T(8,128)(2,1)} %get-tuple-element.72), channel_id=1, source_target_pairs={{0,2},{2,0},{1,3},{3,1},{4,6},{6,4},{5,7},{7,5},{8,10},{10,8},{9,1... | collective-permute-start | bytes 1179656 | tf_op jit(solution)/shard_map/ppermute | solution.py:561
  81.3 16.2 %collective-permute-start.14 = (bf16[2,2,256,128]{3,2,1,0:T(8,128)(2,1)}, bf16[2,2,256,128]{3,2,1,0:T(8,128)(2,1)S(1)}, u32[]{:S(2)}, u32[]{:S(2)}) collective-permute-start(bf16[2,2,256,128]{3,2,1,0:T(8,128)(2,1)} %get-tuple-element.73), channel_id=1, source_target_pairs={{0,16},{4,20},{8,24},{20,4},{24,8},{28,12},{1,17},{5,21},{9,25},{2... | collective-permute-start | bytes 786440 | tf_op jit(solution)/shard_map/ppermute | solution.py:459
  84.1 14.8 %copy-start.7 = (f32[2,256,512]{2,1,0:T(8,128)S(1)}, f32[2,256,512]{2,1,0:T(8,128)}, u32[]{:S(2)}) copy-start(f32[2,256,512]{2,1,0:T(8,128)} %copy-done.6) | copy-start | bytes 3145732
  84.2 16.2 %collective-permute-start.15 = (bf16[2,256,384]{2,1,0:T(8,128)(2,1)S(1)}, bf16[2,256,384]{2,1,0:T(8,128)(2,1)S(1)}, u32[]{:S(2)}, u32[]{:S(2)}) collective-permute-start(bf16[2,256,384]{2,1,0:T(8,128)(2,1)S(1)} %x_own_kernel.1), channel_id=1, source_target_pairs={{0,2},{2,0},{1,3},{3,1},{4,6},{6,4},{5,7},{7,5},{8,10},{10,8},{9,1... | collective-permute-start | bytes 1179656 | tf_op jit(solution)/shard_map/ppermute | solution.py:565
  92.1 1.2 %copy-start.4 = (f32[2,256,512]{2,1,0:T(8,128)S(1)}, f32[2,256,512]{2,1,0:T(8,128)}, u32[]{:S(2)}) copy-start(f32[2,256,512]{2,1,0:T(8,128)} %copy-done.3) | copy-start | bytes 3145732
  94.4 20.3 %collective-permute-start.17 = (bf16[2,256,384]{2,1,0:T(8,128)(2,1)S(1)}, bf16[2,256,384]{2,1,0:T(8,128)(2,1)S(1)}, u32[]{:S(2)}, u32[]{:S(2)}) collective-permute-start(bf16[2,256,384]{2,1,0:T(8,128)(2,1)S(1)} %z_second_kernel.1), channel_id=1, source_target_pairs={{0,16},{4,20},{8,24},{20,4},{24,8},{28,12},{1,17},{5,21},{9,25},{2... | collective-permute-start | bytes 1179656 | tf_op jit(solution)/shard_map/ppermute | solution.py:459
  97.6 5.5 %collective-permute-start.16 = (bf16[2,256,128]{2,1,0:T(8,128)(2,1)S(1)}, bf16[2,256,128]{2,1,0:T(8,128)(2,1)S(1)}, u32[]{:S(2)}, u32[]{:S(2)}) collective-permute-start(bf16[2,256,128]{2,1,0:T(8,128)(2,1)S(1)} %x_last_kernel.1), channel_id=1, source_target_pairs={{0,2},{2,0},{1,3},{3,1},{4,6},{6,4},{5,7},{7,5},{8,10},{10,8},{9,1... | collective-permute-start | bytes 393224 | tf_op jit(solution)/shard_map/ppermute | solution.py:568

commit v19 on v18

--- a/solution.py
+++ b/solution.py
@@ -372,8 +372,8 @@
 
 def first_kernel(that_near, that_far, got_that, z_out, x_out):
     cols = z_out.shape[3]
-    near = that_near[:, :, :cols] + got_that[0, :, :, :cols].astype(jnp.float32)
-    far = that_far[...] + got_that[1].astype(jnp.float32)
+    near = that_near[:, :, :cols].astype(jnp.float32) + got_that[0, :, :, :cols].astype(jnp.float32)
+    far = that_far[...].astype(jnp.float32) + got_that[1].astype(jnp.float32)
     z_out[0] = near.astype(z_out.dtype)
     z_out[1] = far[:, :, :cols].astype(z_out.dtype)
     x_out[...] = far[:, :, cols:].astype(x_out.dtype)
@@ -381,19 +381,19 @@
 
 def z_second_kernel(that_near, got_that, got_x, out):
     cols = that_near.shape[2] - out.shape[2]
-    total = that_near[:, :, cols:] + got_that[0, :, :, cols:].astype(jnp.float32)
+    total = that_near[:, :, cols:].astype(jnp.float32) + got_that[0, :, :, cols:].astype(jnp.float32)
     out[...] = (total + got_x[...].astype(jnp.float32)).astype(out.dtype)
 
 
 def x_own_kernel(this_far, got_this, out):
     cols = this_far.shape[2] - out.shape[2]
-    total = this_far[:, :, cols:] + got_this[1, :, :, cols:].astype(jnp.float32)
+    total = this_far[:, :, cols:].astype(jnp.float32) + got_this[1, :, :, cols:].astype(jnp.float32)
     out[...] = total.astype(out.dtype)
 
 
 def x_last_kernel(this_far, got_this, got_z, out):
     cols = out.shape[2]
-    total = this_far[:, :, :cols] + got_this[1, :, :, :cols].astype(jnp.float32)
+    total = this_far[:, :, :cols].astype(jnp.float32) + got_this[1, :, :, :cols].astype(jnp.float32)
     out[...] = (total + got_z[1].astype(jnp.float32)).astype(out.dtype)
 
 
@@ -539,7 +539,7 @@
     got_this = lax.ppermute(sent_this, "led", cores)
     this_near, this_far, that_near, that_far = local_call(
         kept_kernel,
-        [jax.ShapeDtypeStruct(piece, jnp.float32)] * 4,
+        [jax.ShapeDtypeStruct(piece, jnp.float32)] + [jax.ShapeDtypeStruct(piece, bf16)] * 3,
         [smem, vmem, vmem],
         [],
         flops // 4,

time: 116 us -> 115 us (level)
  starting transfers between devices: 35.7 us -> 34.4 us
  local copies, waits for them, and re-layouts: 4.62 us -> 3.4 us
    ppermute x1, starting transfers between devices: 1.34 us -> 0.07 us  [body_slabs(): got_x_last = lax.ppermute(over, 'led', planes)]
    unnamed x16 -> x12, local copies, waits for them, and re-layouts: 4.61 us -> 3.39 us
where the time goes in v19:
time: 115 us
  waiting for transfers between devices  52.4 us (46%)
  starting transfers between devices  34.4 us (30%)
  Pallas kernels  20.3 us (18%)
  other arithmetic  3.71 us (3%)
  local copies, waits for them, and re-layouts  3.4 us (3%)
    ppermute x13, waiting for transfers between devices, permute(): return lax.ppermute(sent, 'slab', pairs)  41.4 us
    ppermute x13, starting transfers between devices, permute(): return lax.ppermute(sent, 'slab', pairs)  31.7 us
    ppermute x1, waiting for transfers between devices, body_slabs(): got_x = lax.ppermute(over_x, 'led', planes)  7.22 us
    pallas_call x1, Pallas kernels, body_slabs(): local_call(field_kernel, [sent_block] * HALF, [vmem] * 11, [pltpu.VMEM((w...  5.31 us
    pallas_call x2, Pallas kernels, rows_call(): local_call(functools.partial(rows_kernel, which), [sent_block] * count, [...  4.69 us
    ppermute x1, waiting for transfers between devices, body_slabs(): got_x_last = lax.ppermute(over, 'led', planes)  3.76 us
    pallas_call x1, Pallas kernels, body_slabs(): local_call(sent_kernel, [jax.ShapeDtypeStruct((2,) + piece, bf16), jax.Sh...  3.59 us
    unnamed x12, local copies, waits for them, and re-layouts  3.39 us
  transfers between devices with their start and end apart: 18, of which 12 were waited for; matrix products, arithmetic and copies ran while one was open for 1% of the time, Pallas kernels for 7%

profile of v19, /device:TPU:4, one launch (start us, length us, event | category | flops | bytes accessed | tf_op | source)
XLA Modules:
  0.0 114.6 jit_solution(15879515687986768178)
XLA Ops:
  0.0 0.9 pad_add_fusion.starts
  0.9 2.4 %copy-done.1 = f32[2,256,2048]{2,1,0:T(8,128)S(1)} copy-done((f32[2,256,2048]{2,1,0:T(8,128)S(1)}, f32[2,256,2048]{2,1,0:T(8,128)}, u32[]{:S(2)}) %copy-start.1) | copy-done | bytes 4194328
  3.3 1.4 %windows.1.window = bf16[1024,1024]{1,0:T(8,128)(2,1)S(1)} custom-call(s32[4]{0:T(128)S(1)} %pad_add_fusion.starts, f32[2,256,2048]{2,1,0:T(8,128)S(1)} %copy-done.1), custom_call_target="tpu_custom_call" | custom-call | bytes 6291456 | tf_op jit(solution)/shard_map/windows/pallas_call | solution.py:434
  4.7 1.8 %rows_round_1.1 = (bf16[4,256,128]{2,1,0:T(8,128)(2,1)S(1)}, bf16[4,256,128]{2,1,0:T(8,128)(2,1)S(1)}, bf16[4,256,128]{2,1,0:T(8,128)(2,1)S(1)}) custom-call(bf16[1024,1024]{1,0:T(8,128)(2,1)S(1)} %windows.1.window, bf16[8,1024,256]{2,1,0:T(8,128)(2,1)S(1)} %copy-done), custom_call_target="tpu_custom_call" | custom-call | flops 1610612736 | bytes 5242880 | tf_op jit(solution)/shard_map/rows_round_1/pallas_call | solution.py:446
  6.5 1.3 %collective-permute-start = (bf16[4,256,128]{2,1,0:T(8,128)(2,1)S(1)}, bf16[4,256,128]{2,1,0:T(8,128)(2,1)S(1)}, u32[]{:S(2)}, u32[]{:S(2)}) collective-permute-start(bf16[4,256,128]{2,1,0:T(8,128)(2,1)S(1)} %get-tuple-element.43), channel_id=1, source_target_pairs={{8,16},{12,20},{16,8},{20,12},{4,0},{24,28},{9,17},{13,21},{17,9},... | collective-permute-start | bytes 786440 | tf_op jit(solution)/shard_map/ppermute | solution.py:459
  7.8 5.7 %collective-permute-start.1 = (bf16[4,256,128]{2,1,0:T(8,128)(2,1)S(1)}, bf16[4,256,128]{2,1,0:T(8,128)(2,1)S(1)}, u32[]{:S(2)}, u32[]{:S(2)}) collective-permute-start(bf16[4,256,128]{2,1,0:T(8,128)(2,1)S(1)} %get-tuple-element.44), channel_id=1, source_target_pairs={{4,12},{8,0},{12,4},{16,24},{20,28},{24,16},{5,13},{9,1},{13,5},{1... | collective-permute-start | bytes 786440 | tf_op jit(solution)/shard_map/ppermute | solution.py:459
  13.5 0.0 copy-start.2
  13.5 0.0 copy-start.3
  13.5 1.6 %collective-permute-start.3 = (bf16[4,256,128]{2,1,0:T(8,128)(2,1)S(1)}, bf16[4,256,128]{2,1,0:T(8,128)(2,1)S(1)}, u32[]{:S(2)}, u32[]{:S(2)}) collective-permute-start(bf16[4,256,128]{2,1,0:T(8,128)(2,1)S(1)} %get-tuple-element.54), channel_id=1, source_target_pairs={{8,20},{12,16},{16,12},{20,8},{4,0},{24,28},{9,21},{13,17},{17,13}... | collective-permute-start | bytes 786440 | tf_op jit(solution)/shard_map/ppermute | solution.py:459
  15.1 2.9 %rows_round_2.1 = (bf16[4,256,128]{2,1,0:T(8,128)(2,1)S(1)}, bf16[4,256,128]{2,1,0:T(8,128)(2,1)S(1)}, bf16[4,256,128]{2,1,0:T(8,128)(2,1)S(1)}, bf16[4,256,128]...) custom-call(bf16[1024,1024]{1,0:T(8,128)(2,1)S(1)} %windows.1.window, bf16[8,1024,256]{2,1,0:T(8,128)(2,1)S(1)} %copy-done), custom_call_target="tpu_custom_call" | custom-call | flops 2684354560 | bytes 5242880 | tf_op jit(solution)/shard_map/rows_round_2/pallas_call | solution.py:446
  18.0 1.5 %collective-permute-done.1.rest_7_ = bf16[4,256,128]{2,1,0:T(8,128)(2,1)S(1)} collective-permute-done((bf16[4,256,128]{2,1,0:T(8,128)(2,1)S(1)}, bf16[4,256,128]{2,1,0:T(8,128)(2,1)S(1)}, u32[]{:S(2)}, u32[]{:S(2)}) %collective-permute-start.1) | collective-permute-done | bytes 262176 | tf_op jit(solution)/shard_map/ppermute | solution.py:459
  19.5 1.8 %collective-permute-start.2 = (bf16[4,256,128]{2,1,0:T(8,128)(2,1)S(1)}, bf16[4,256,128]{2,1,0:T(8,128)(2,1)S(1)}, u32[]{:S(2)}, u32[]{:S(2)}) collective-permute-start(bf16[4,256,128]{2,1,0:T(8,128)(2,1)S(1)} %get-tuple-element.53), channel_id=1, source_target_pairs={{4,0},{8,12},{12,8},{16,20},{20,16},{24,28},{5,1},{9,13},{13,9},{1... | collective-permute-start | bytes 786440 | tf_op jit(solution)/shard_map/ppermute | solution.py:459
  21.3 3.2 %collective-permute-start.4 = (bf16[4,256,128]{2,1,0:T(8,128)(2,1)S(1)}, bf16[4,256,128]{2,1,0:T(8,128)(2,1)S(1)}, u32[]{:S(2)}, u32[]{:S(2)}) collective-permute-start(bf16[4,256,128]{2,1,0:T(8,128)(2,1)S(1)} %class_4_blocks.1), channel_id=1, source_target_pairs={{0,16},{4,20},{8,24},{12,28},{16,0},{20,4},{24,8},{28,12},{1,17},{... | collective-permute-start | bytes 786440 | tf_op jit(solution)/shard_map/ppermute | solution.py:459
  24.5 1.3 %collective-permute-start.6 = (bf16[4,256,128]{2,1,0:T(8,128)(2,1)S(1)}, bf16[4,256,128]{2,1,0:T(8,128)(2,1)S(1)}, u32[]{:S(2)}, u32[]{:S(2)}) collective-permute-start(bf16[4,256,128]{2,1,0:T(8,128)(2,1)S(1)} %get-tuple-element.57.own), channel_id=1, source_target_pairs={{8,28},{12,24},{16,4},{20,0},{9,29},{13,25},{17,5},{21,1},{10,30},... | collective-permute-start | bytes 786440 | tf_op jit(solution)/shard_map/ppermute | solution.py:459
  25.8 5.5 %collective-permute-start.7 = (bf16[4,256,128]{2,1,0:T(8,128)(2,1)S(1)}, bf16[4,256,128]{2,1,0:T(8,128)(2,1)S(1)}, u32[]{:S(2)}, u32[]{:S(2)}) collective-permute-start(bf16[4,256,128]{2,1,0:T(8,128)(2,1)S(1)} %get-tuple-element.61), channel_id=1, source_target_pairs={{4,8},{8,4},{12,0},{16,28},{20,24},{24,20},{5,9},{9,5},{13,1},{17,... | collective-permute-start | bytes 786440 | tf_op jit(solution)/shard_map/ppermute | solution.py:459
  31.4 1.9 %collective-permute-start.5 = (bf16[4,256,128]{2,1,0:T(8,128)(2,1)S(1)}, bf16[4,256,128]{2,1,0:T(8,128)(2,1)S(1)}, u32[]{:S(2)}, u32[]{:S(2)}) collective-permute-start(bf16[4,256,128]{2,1,0:T(8,128)(2,1)S(1)} %class_6_blocks.1), channel_id=1, source_target_pairs={{0,24},{4,28},{24,0},{28,4},{1,25},{5,29},{25,1},{29,5},{2,26},{6,... | collective-permute-start | bytes 786440 | tf_op jit(solution)/shard_map/ppermute | solution.py:459
  33.3 0.6 amplitude.1
  33.9 8.8 %collective-permute-done.4.rest_2_ = bf16[4,256,128]{2,1,0:T(8,128)(2,1)S(1)} collective-permute-done((bf16[4,256,128]{2,1,0:T(8,128)(2,1)S(1)}, bf16[4,256,128]{2,1,0:T(8,128)(2,1)S(1)}, u32[]{:S(2)}, u32[]{:S(2)}) %collective-permute-start.4) | collective-permute-done | bytes 262176 | tf_op jit(solution)/shard_map/ppermute | solution.py:459
  42.7 3.9 %collective-permute-done.6.rest_4_ = bf16[4,256,128]{2,1,0:T(8,128)(2,1)S(1)} collective-permute-done((bf16[4,256,128]{2,1,0:T(8,128)(2,1)S(1)}, bf16[4,256,128]{2,1,0:T(8,128)(2,1)S(1)}, u32[]{:S(2)}, u32[]{:S(2)}) %collective-permute-start.6) | collective-permute-done | bytes 262176 | tf_op jit(solution)/shard_map/ppermute | solution.py:459
  46.6 3.6 %collective-permute-done.7.rest_8_ = bf16[4,256,128]{2,1,0:T(8,128)(2,1)S(1)} collective-permute-done((bf16[4,256,128]{2,1,0:T(8,128)(2,1)S(1)}, bf16[4,256,128]{2,1,0:T(8,128)(2,1)S(1)}, u32[]{:S(2)}, u32[]{:S(2)}) %collective-permute-start.7) | collective-permute-done | bytes 262176 | tf_op jit(solution)/shard_map/ppermute | solution.py:459
  50.2 5.3 %modulus_step.1 = (bf16[4,256,128]{2,1,0:T(8,128)(2,1)S(1)}, bf16[4,256,128]{2,1,0:T(8,128)(2,1)S(1)}, bf16[4,256,128]{2,1,0:T(8,128)(2,1)S(1)}, bf16[4,256,128]{2,1,0:T(8,128)(2,1)S(1)}) custom-call(f32[1024,256]{1,0:T(8,128)S(1)} %get-tuple-element.50.amplitude, bf16[8,256,1024]{2,1,0:T(8,128)(2,1)S(1)} %get-tuple-element.51.table, ...), custom_call_target="tpu_custom_call" | custom-call | flops 4294967296 | bytes 12582912 | tf_op jit(solution)/shard_map/modulus_step/pallas_call | solution.py:499
  55.5 0.1 collective-permute-start.10
  55.6 2.4 %collective-permute-start.8 = (bf16[4,256,128]{2,1,0:T(8,128)(2,1)S(1)}, bf16[4,256,128]{2,1,0:T(8,128)(2,1)S(1)}, u32[]{:S(2)}, u32[]{:S(2)}) collective-permute-start(bf16[4,256,128]{2,1,0:T(8,128)(2,1)S(1)} %get-tuple-element.63), channel_id=1, source_target_pairs={{0,4},{4,0},{8,12},{12,8},{16,20},{20,16},{24,28},{28,24},{1,5},{5... | collective-permute-start | bytes 786440 | tf_op jit(solution)/shard_map/ppermute | solution.py:459
  58.0 1.4 %collective-permute-start.9 = (bf16[4,256,128]{2,1,0:T(8,128)(2,1)S(1)}, bf16[4,256,128]{2,1,0:T(8,128)(2,1)S(1)}, u32[]{:S(2)}, u32[]{:S(2)}) collective-permute-start(bf16[4,256,128]{2,1,0:T(8,128)(2,1)S(1)} %get-tuple-element.64), channel_id=1, source_target_pairs={{0,8},{4,12},{8,0},{12,4},{16,24},{20,28},{24,16},{28,20},{1,9},{5... | collective-permute-start | bytes 786440 | tf_op jit(solution)/shard_map/ppermute | solution.py:459
  59.4 6.3 %collective-permute-done.10.rest_3_ = bf16[4,256,128]{2,1,0:T(8,128)(2,1)S(1)} collective-permute-done((bf16[4,256,128]{2,1,0:T(8,128)(2,1)S(1)}, bf16[4,256,128]{2,1,0:T(8,128)(2,1)S(1)}, u32[]{:S(2)}, u32[]{:S(2)}) %collective-permute-start.10) | collective-permute-done | bytes 262176 | tf_op jit(solution)/shard_map/ppermute | solution.py:459
  65.6 2.7 %collective-permute-done.8.rest_1_ = bf16[4,256,128]{2,1,0:T(8,128)(2,1)S(1)} collective-permute-done((bf16[4,256,128]{2,1,0:T(8,128)(2,1)S(1)}, bf16[4,256,128]{2,1,0:T(8,128)(2,1)S(1)}, u32[]{:S(2)}, u32[]{:S(2)}) %collective-permute-start.8) | collective-permute-done | bytes 262176 | tf_op jit(solution)/shard_map/ppermute | solution.py:459
  68.4 1.7 %collective-permute-done.9.rest_2_ = bf16[4,256,128]{2,1,0:T(8,128)(2,1)S(1)} collective-permute-done((bf16[4,256,128]{2,1,0:T(8,128)(2,1)S(1)}, bf16[4,256,128]{2,1,0:T(8,128)(2,1)S(1)}, u32[]{:S(2)}, u32[]{:S(2)}) %collective-permute-start.9) | collective-permute-done | bytes 262176 | tf_op jit(solution)/shard_map/ppermute | solution.py:459
  70.1 3.6 %update_sent.1 = (bf16[2,2,256,512]{3,2,1,0:T(8,128)(2,1)}, bf16[2,2,256,512]{3,2,1,0:T(8,128)(2,1)S(1)}, bf16[1024,512]{1,0:T(8,128)(2,1)S(1)}) custom-call(s32[4]{0:T(128)S(1)} %pad_add_fusion.starts, bf16[8,1024,256]{2,1,0:T(8,128)(2,1)S(1)} %copy-done, bf16[4,256,128]{2,1,0:T(8,128)(2,1)S(1)} %get-tuple-element.62.rest_0_, ...), custom_call_target="tpu_custom_call" | custom-call | flops 1073741824 | bytes 8388608 | tf_op jit(solution)/shard_map/update_sent/pallas_call | solution.py:524
  73.7 0.5 collective-permute-start.11
  74.2 2.6 %update_kept.1 = (f32[2,256,512]{2,1,0:T(8,128)S(1)}, bf16[2,256,512]{2,1,0:T(8,128)(2,1)S(1)}, bf16[2,256,512]{2,1,0:T(8,128)(2,1)S(1)}, bf16[2,256,512]{2,1,0:T(8,128)(2,1)S(1)}) custom-call(s32[4]{0:T(128)S(1)} %pad_add_fusion.starts, bf16[8,1024,256]{2,1,0:T(8,128)(2,1)S(1)} %copy-done, bf16[1024,512]{1,0:T(8,128)(2,1)S(1)} %get-tuple-element.66.back), custom_call_target="tpu_custom_call" | custom-call | flops 1073741824 | bytes 10485760 | tf_op jit(solution)/shard_map/update_kept/pallas_call | solution.py:540
  76.8 1.0 copy-done.4
  77.8 0.1 collective-permute-done.12.got_that
  77.8 0.9 first_kernel.1
  78.8 1.5 %collective-permute-start.13 = (bf16[2,256,384]{2,1,0:T(8,128)(2,1)}, bf16[2,256,384]{2,1,0:T(8,128)(2,1)}, u32[]{:S(2)}, u32[]{:S(2)}) collective-permute-start(bf16[2,256,384]{2,1,0:T(8,128)(2,1)} %get-tuple-element.72), channel_id=1, source_target_pairs={{0,2},{2,0},{1,3},{3,1},{4,6},{6,4},{5,7},{7,5},{8,10},{10,8},{9,1... | collective-permute-start | bytes 1179656 | tf_op jit(solution)/shard_map/ppermute | solution.py:561
  80.2 2.8 %collective-permute-start.14 = (bf16[2,2,256,128]{3,2,1,0:T(8,128)(2,1)}, bf16[2,2,256,128]{3,2,1,0:T(8,128)(2,1)S(1)}, u32[]{:S(2)}, u32[]{:S(2)}) collective-permute-start(bf16[2,2,256,128]{3,2,1,0:T(8,128)(2,1)} %get-tuple-element.73), channel_id=1, source_target_pairs={{0,16},{4,20},{8,24},{20,4},{24,8},{28,12},{1,17},{5,21},{9,25},{2... | collective-permute-start | bytes 786440 | tf_op jit(solution)/shard_map/ppermute | solution.py:459
  83.1 0.1 x_own_kernel.1
  83.2 0.6 collective-permute-start.15
  83.8 7.2 %collective-permute-done.13.got_x = bf16[2,256,384]{2,1,0:T(8,128)(2,1)} collective-permute-done((bf16[2,256,384]{2,1,0:T(8,128)(2,1)}, bf16[2,256,384]{2,1,0:T(8,128)(2,1)}, u32[]{:S(2)}, u32[]{:S(2)}) %collective-permute-start.13) | collective-permute-done | bytes 393248 | tf_op jit(solution)/shard_map/ppermute | solution.py:561
  91.0 1.1 z_second_kernel.1
  92.2 2.8 %collective-permute-start.17 = (bf16[2,256,384]{2,1,0:T(8,128)(2,1)S(1)}, bf16[2,256,384]{2,1,0:T(8,128)(2,1)S(1)}, u32[]{:S(2)}, u32[]{:S(2)}) collective-permute-start(bf16[2,256,384]{2,1,0:T(8,128)(2,1)S(1)} %z_second_kernel.1), channel_id=1, source_target_pairs={{0,16},{4,20},{8,24},{20,4},{24,8},{28,12},{1,17},{5,21},{9,25},{2... | collective-permute-start | bytes 1179656 | tf_op jit(solution)/shard_map/ppermute | solution.py:459
  95.0 10.1 %collective-permute-done.14.got_z = bf16[2,2,256,128]{3,2,1,0:T(8,128)(2,1)S(1)} collective-permute-done((bf16[2,2,256,128]{3,2,1,0:T(8,128)(2,1)}, bf16[2,2,256,128]{3,2,1,0:T(8,128)(2,1)S(1)}, u32[]{:S(2)}, u32[]{:S(2)}) %collective-permute-start.14) | collective-permute-done | bytes 262176 | tf_op jit(solution)/shard_map/ppermute | solution.py:459
  105.1 0.1 x_last_kernel.1
  105.2 0.1 collective-permute-start.16
  105.3 1.5 %fusion.1 = f32[2,256,512]{2,1,0:T(8,128)S(1)} fusion(f32[2,256,512]{2,1,0:T(8,128)S(1)} %copy-done.5, f32[2,256,2048]{2,1,0:T(8,128)} %spectrum.1, s32[]{:T(128)S(6)} %select_n.3, bf16[2,2,256,512]{3,2,1,0:T(8,128)(2,1)S(1)} %collective-permute-done.11.got_this, bf16[2,256,128]{2,1,0:T(8,128)(2,1)S(1)} %slice_bitcast_fusion.1), kind=kLoop, calls=%fused_computation.2 | loop fusion | flops 1310720 | bytes 3801092 | tf_op jit(solution)/shard_map/add | solution.py:575
  106.8 3.8 %collective-permute-done.16 = bf16[2,256,128]{2,1,0:T(8,128)(2,1)S(1)} collective-permute-done((bf16[2,256,128]{2,1,0:T(8,128)(2,1)S(1)}, bf16[2,256,128]{2,1,0:T(8,128)(2,1)S(1)}, u32[]{:S(2)}, u32[]{:S(2)}) %collective-permute-start.16) | collective-permute-done | bytes 131104 | tf_op jit(solution)/shard_map/ppermute | solution.py:568
  110.6 0.2 add_add_fusion
  110.7 2.7 %collective-permute-done.17 = bf16[2,256,384]{2,1,0:T(8,128)(2,1)S(1)} collective-permute-done((bf16[2,256,384]{2,1,0:T(8,128)(2,1)S(1)}, bf16[2,256,384]{2,1,0:T(8,128)(2,1)S(1)}, u32[]{:S(2)}, u32[]{:S(2)}) %collective-permute-start.17) | collective-permute-done | bytes 393248 | tf_op jit(solution)/shard_map/ppermute | solution.py:459
  113.4 1.1 convert_add_fusion.1
  (18 shorter events, 0.1 us)
Async XLA Ops:
  0.0 4.6 %copy-start = (bf16[8,1024,256]{2,1,0:T(8,128)(2,1)S(1)}, bf16[8,1024,256]{2,1,0:T(8,128)(2,1)}, u32[]{:S(2)}) copy-start(bf16[8,1024,256]{2,1,0:T(8,128)(2,1)} %constant.18.clone.table) | copy-start | bytes 12582916
  0.9 2.4 %copy-start.1 = (f32[2,256,2048]{2,1,0:T(8,128)S(1)}, f32[2,256,2048]{2,1,0:T(8,128)}, u32[]{:S(2)}) copy-start(f32[2,256,2048]{2,1,0:T(8,128)} %spectrum.1) | copy-start | bytes 12582916
  6.5 11.5 %collective-permute-start = (bf16[4,256,128]{2,1,0:T(8,128)(2,1)S(1)}, bf16[4,256,128]{2,1,0:T(8,128)(2,1)S(1)}, u32[]{:S(2)}, u32[]{:S(2)}) collective-permute-start(bf16[4,256,128]{2,1,0:T(8,128)(2,1)S(1)} %get-tuple-element.43), channel_id=1, source_target_pairs={{8,16},{12,20},{16,8},{20,12},{4,0},{24,28},{9,17},{13,21},{17,9},... | collective-permute-start | bytes 786440 | tf_op jit(solution)/shard_map/ppermute | solution.py:459
  7.8 11.7 %collective-permute-start.1 = (bf16[4,256,128]{2,1,0:T(8,128)(2,1)S(1)}, bf16[4,256,128]{2,1,0:T(8,128)(2,1)S(1)}, u32[]{:S(2)}, u32[]{:S(2)}) collective-permute-start(bf16[4,256,128]{2,1,0:T(8,128)(2,1)S(1)} %get-tuple-element.44), channel_id=1, source_target_pairs={{4,12},{8,0},{12,4},{16,24},{20,28},{24,16},{5,13},{9,1},{13,5},{1... | collective-permute-start | bytes 786440 | tf_op jit(solution)/shard_map/ppermute | solution.py:459
  13.5 19.9 %copy-start.2 = (bf16[8,256,1024]{2,1,0:T(8,128)(2,1)S(1)}, bf16[8,256,1024]{2,1,0:T(8,128)(2,1)}, u32[]{:S(2)}) copy-start(bf16[8,256,1024]{2,1,0:T(8,128)(2,1)} %constant.17.clone.table) | copy-start | bytes 12582916
  13.5 19.9 %copy-start.3 = (f32[2,128,1024]{2,1,0:T(8,128)S(1)}, f32[2,128,1024]{2,1,0:T(8,128)}, u32[]{:S(2)}) copy-start(f32[2,128,1024]{2,1,0:T(8,128)} %images) | copy-start | bytes 3145732
  13.5 17.8 %collective-permute-start.3 = (bf16[4,256,128]{2,1,0:T(8,128)(2,1)S(1)}, bf16[4,256,128]{2,1,0:T(8,128)(2,1)S(1)}, u32[]{:S(2)}, u32[]{:S(2)}) collective-permute-start(bf16[4,256,128]{2,1,0:T(8,128)(2,1)S(1)} %get-tuple-element.54), channel_id=1, source_target_pairs={{8,20},{12,16},{16,12},{20,8},{4,0},{24,28},{9,21},{13,17},{17,13}... | collective-permute-start | bytes 786440 | tf_op jit(solution)/shard_map/ppermute | solution.py:459
  19.5 11.9 %collective-permute-start.2 = (bf16[4,256,128]{2,1,0:T(8,128)(2,1)S(1)}, bf16[4,256,128]{2,1,0:T(8,128)(2,1)S(1)}, u32[]{:S(2)}, u32[]{:S(2)}) collective-permute-start(bf16[4,256,128]{2,1,0:T(8,128)(2,1)S(1)} %get-tuple-element.53), channel_id=1, source_target_pairs={{4,0},{8,12},{12,8},{16,20},{20,16},{24,28},{5,1},{9,13},{13,9},{1... | collective-permute-start | bytes 786440 | tf_op jit(solution)/shard_map/ppermute | solution.py:459
  21.3 21.4 %collective-permute-start.4 = (bf16[4,256,128]{2,1,0:T(8,128)(2,1)S(1)}, bf16[4,256,128]{2,1,0:T(8,128)(2,1)S(1)}, u32[]{:S(2)}, u32[]{:S(2)}) collective-permute-start(bf16[4,256,128]{2,1,0:T(8,128)(2,1)S(1)} %class_4_blocks.1), channel_id=1, source_target_pairs={{0,16},{4,20},{8,24},{12,28},{16,0},{20,4},{24,8},{28,12},{1,17},{... | collective-permute-start | bytes 786440 | tf_op jit(solution)/shard_map/ppermute | solution.py:459
  24.5 22.1 %collective-permute-start.6 = (bf16[4,256,128]{2,1,0:T(8,128)(2,1)S(1)}, bf16[4,256,128]{2,1,0:T(8,128)(2,1)S(1)}, u32[]{:S(2)}, u32[]{:S(2)}) collective-permute-start(bf16[4,256,128]{2,1,0:T(8,128)(2,1)S(1)} %get-tuple-element.57.own), channel_id=1, source_target_pairs={{8,28},{12,24},{16,4},{20,0},{9,29},{13,25},{17,5},{21,1},{10,30},... | collective-permute-start | bytes 786440 | tf_op jit(solution)/shard_map/ppermute | solution.py:459
  25.8 24.4 %collective-permute-start.7 = (bf16[4,256,128]{2,1,0:T(8,128)(2,1)S(1)}, bf16[4,256,128]{2,1,0:T(8,128)(2,1)S(1)}, u32[]{:S(2)}, u32[]{:S(2)}) collective-permute-start(bf16[4,256,128]{2,1,0:T(8,128)(2,1)S(1)} %get-tuple-element.61), channel_id=1, source_target_pairs={{4,8},{8,4},{12,0},{16,28},{20,24},{24,20},{5,9},{9,5},{13,1},{17,... | collective-permute-start | bytes 786440 | tf_op jit(solution)/shard_map/ppermute | solution.py:459
  31.4 18.8 %collective-permute-start.5 = (bf16[4,256,128]{2,1,0:T(8,128)(2,1)S(1)}, bf16[4,256,128]{2,1,0:T(8,128)(2,1)S(1)}, u32[]{:S(2)}, u32[]{:S(2)}) collective-permute-start(bf16[4,256,128]{2,1,0:T(8,128)(2,1)S(1)} %class_6_blocks.1), channel_id=1, source_target_pairs={{0,24},{4,28},{24,0},{28,4},{1,25},{5,29},{25,1},{29,5},{2,26},{6,... | collective-permute-start | bytes 786440 | tf_op jit(solution)/shard_map/ppermute | solution.py:459
  55.5 10.1 %collective-permute-start.10 = (bf16[4,256,128]{2,1,0:T(8,128)(2,1)S(1)}, bf16[4,256,128]{2,1,0:T(8,128)(2,1)S(1)}, u32[]{:S(2)}, u32[]{:S(2)}) collective-permute-start(bf16[4,256,128]{2,1,0:T(8,128)(2,1)S(1)} %get-tuple-element.65), channel_id=1, source_target_pairs={{0,12},{4,8},{8,4},{12,0},{16,28},{20,24},{24,20},{28,16},{1,13},{... | collective-permute-start | bytes 786440 | tf_op jit(solution)/shard_map/ppermute | solution.py:459
  55.6 12.8 %collective-permute-start.8 = (bf16[4,256,128]{2,1,0:T(8,128)(2,1)S(1)}, bf16[4,256,128]{2,1,0:T(8,128)(2,1)S(1)}, u32[]{:S(2)}, u32[]{:S(2)}) collective-permute-start(bf16[4,256,128]{2,1,0:T(8,128)(2,1)S(1)} %get-tuple-element.63), channel_id=1, source_target_pairs={{0,4},{4,0},{8,12},{12,8},{16,20},{20,16},{24,28},{28,24},{1,5},{5... | collective-permute-start | bytes 786440 | tf_op jit(solution)/shard_map/ppermute | solution.py:459
  58.0 12.1 %collective-permute-start.9 = (bf16[4,256,128]{2,1,0:T(8,128)(2,1)S(1)}, bf16[4,256,128]{2,1,0:T(8,128)(2,1)S(1)}, u32[]{:S(2)}, u32[]{:S(2)}) collective-permute-start(bf16[4,256,128]{2,1,0:T(8,128)(2,1)S(1)} %get-tuple-element.64), channel_id=1, source_target_pairs={{0,8},{4,12},{8,0},{12,4},{16,24},{20,28},{24,16},{28,20},{1,9},{5... | collective-permute-start | bytes 786440 | tf_op jit(solution)/shard_map/ppermute | solution.py:459
  73.7 4.1 %collective-permute-start.12 = (bf16[2,2,256,512]{3,2,1,0:T(8,128)(2,1)S(1)}, bf16[2,2,256,512]{3,2,1,0:T(8,128)(2,1)S(1)}, u32[]{:S(2)}, u32[]{:S(2)}) collective-permute-start(bf16[2,2,256,512]{3,2,1,0:T(8,128)(2,1)S(1)} %get-tuple-element.70), channel_id=1, source_target_pairs={{0,1},{1,0},{2,3},{3,2},{4,5},{5,4},{6,7},{7,6},{8,9},{9,8},{10,11... | collective-permute-start | bytes 3145736 | tf_op jit(solution)/shard_map/ppermute | solution.py:538
  73.7 9.4 %collective-permute-start.11 = (bf16[2,2,256,512]{3,2,1,0:T(8,128)(2,1)}, bf16[2,2,256,512]{3,2,1,0:T(8,128)(2,1)S(1)}, u32[]{:S(2)}, u32[]{:S(2)}) collective-permute-start(bf16[2,2,256,512]{3,2,1,0:T(8,128)(2,1)} %get-tuple-element.68), channel_id=1, source_target_pairs={{0,1},{1,0},{2,3},{3,2},{4,5},{5,4},{6,7},{7,6},{8,9},{9,8},{10,11... | collective-permute-start | bytes 3145736 | tf_op jit(solution)/shard_map/ppermute | solution.py:539
  76.8 1.0 copy-start.4
  78.8 12.3 %collective-permute-start.13 = (bf16[2,256,384]{2,1,0:T(8,128)(2,1)}, bf16[2,256,384]{2,1,0:T(8,128)(2,1)}, u32[]{:S(2)}, u32[]{:S(2)}) collective-permute-start(bf16[2,256,384]{2,1,0:T(8,128)(2,1)} %get-tuple-element.72), channel_id=1, source_target_pairs={{0,2},{2,0},{1,3},{3,1},{4,6},{6,4},{5,7},{7,5},{8,10},{10,8},{9,1... | collective-permute-start | bytes 1179656 | tf_op jit(solution)/shard_map/ppermute | solution.py:561
  80.2 24.9 %collective-permute-start.14 = (bf16[2,2,256,128]{3,2,1,0:T(8,128)(2,1)}, bf16[2,2,256,128]{3,2,1,0:T(8,128)(2,1)S(1)}, u32[]{:S(2)}, u32[]{:S(2)}) collective-permute-start(bf16[2,2,256,128]{3,2,1,0:T(8,128)(2,1)} %get-tuple-element.73), channel_id=1, source_target_pairs={{0,16},{4,20},{8,24},{20,4},{24,8},{28,12},{1,17},{5,21},{9,25},{2... | collective-permute-start | bytes 786440 | tf_op jit(solution)/shard_map/ppermute | solution.py:459
  83.1 22.2 %copy-start.5 = (f32[2,256,512]{2,1,0:T(8,128)S(1)}, f32[2,256,512]{2,1,0:T(8,128)}, u32[]{:S(2)}) copy-start(f32[2,256,512]{2,1,0:T(8,128)} %copy-done.4) | copy-start | bytes 3145732
  83.2 23.6 %collective-permute-start.15 = (bf16[2,256,384]{2,1,0:T(8,128)(2,1)S(1)}, bf16[2,256,384]{2,1,0:T(8,128)(2,1)S(1)}, u32[]{:S(2)}, u32[]{:S(2)}) collective-permute-start(bf16[2,256,384]{2,1,0:T(8,128)(2,1)S(1)} %x_own_kernel.1), channel_id=1, source_target_pairs={{0,2},{2,0},{1,3},{3,1},{4,6},{6,4},{5,7},{7,5},{8,10},{10,8},{9,1... | collective-permute-start | bytes 1179656 | tf_op jit(solution)/shard_map/ppermute | solution.py:565
  92.2 21.3 %collective-permute-start.17 = (bf16[2,256,384]{2,1,0:T(8,128)(2,1)S(1)}, bf16[2,256,384]{2,1,0:T(8,128)(2,1)S(1)}, u32[]{:S(2)}, u32[]{:S(2)}) collective-permute-start(bf16[2,256,384]{2,1,0:T(8,128)(2,1)S(1)} %z_second_kernel.1), channel_id=1, source_target_pairs={{0,16},{4,20},{8,24},{20,4},{24,8},{28,12},{1,17},{5,21},{9,25},{2... | collective-permute-start | bytes 1179656 | tf_op jit(solution)/shard_map/ppermute | solution.py:459
  105.2 5.4 %collective-permute-start.16 = (bf16[2,256,128]{2,1,0:T(8,128)(2,1)S(1)}, bf16[2,256,128]{2,1,0:T(8,128)(2,1)S(1)}, u32[]{:S(2)}, u32[]{:S(2)}) collective-permute-start(bf16[2,256,128]{2,1,0:T(8,128)(2,1)S(1)} %x_last_kernel.1), channel_id=1, source_target_pairs={{0,2},{2,0},{1,3},{3,1},{4,6},{6,4},{5,7},{7,5},{8,10},{10,8},{9,1... | collective-permute-start | bytes 393224 | tf_op jit(solution)/shard_map/ppermute | solution.py:568

commit v20 on v12

--- a/solution.py
+++ b/solution.py
@@ -474,7 +474,7 @@
     outer_pairs = [(s, s ^ 6) for s in range(SLABS) if s not in INNER]
     near_1 = permute(near_1, [(s, s ^ 1) for s in windowed])
     near_3 = permute(near_3, [(s, s ^ 3) for s in windowed])
-    near_1, got_b = lax.optimization_barrier((near_1, got_b))
+    near_3, got_b = lax.optimization_barrier((near_3, got_b))
     far_columns = [
         got_a,
         got_b,

time: 113 us -> 111 us (0.982)
  starting transfers between devices: 34.4 us -> 30.5 us
  waiting for transfers between devices: 50.6 us -> 52 us
    ppermute x13, starting transfers between devices: 30.8 us -> 26.9 us  [permute(): return lax.ppermute(sent, 'slab', pairs)]
    ppermute x13, waiting for transfers between devices: 42.9 us -> 44.3 us  [permute(): return lax.ppermute(sent, 'slab', pairs)]
  transfers between devices with their start and end apart: 17 -> 17, of which waited for: 10 -> 9; matrix products, arithmetic and copies ran while one was open for 3% -> 3% of each run, Pallas kernels for 8% -> 8%
where the time goes in v20:
time: 111 us; the launch traced here: 110 us
  waiting for transfers between devices  52 us (47%)
  starting transfers between devices  30.5 us (27%)
  Pallas kernels  20 us (18%)
  other arithmetic  5.06 us (5%)
  local copies, waits for them, and re-layouts  2.42 us (2%)
    ppermute x13, waiting for transfers between devices, permute(): return lax.ppermute(sent, 'slab', pairs)  44.3 us
    ppermute x13, starting transfers between devices, permute(): return lax.ppermute(sent, 'slab', pairs)  26.9 us
    ppermute x2, waiting for transfers between devices, body_slabs(): got_x = lax.ppermute(over, 'led', planes)  7.77 us
    pallas_call x1, Pallas kernels, body_slabs(): local_call(field_kernel, [sent_block] * HALF, [vmem] * 11, [pltpu.VMEM((w...  5.31 us
    pallas_call x2, Pallas kernels, rows_call(): local_call(functools.partial(rows_kernel, which), [sent_block] * count, [...  4.69 us
    ppermute x2, starting transfers between devices, body_slabs(): got_x = lax.ppermute(over, 'led', planes)  3.01 us
    pallas_call x4, Pallas kernels, sum_call(): local_call(kernel, out_shape, specs, [], 0, 2 ** 20, kernel.__name__)  3 us
    pallas_call x1, Pallas kernels, body_slabs(): local_call(sent_kernel, [jax.ShapeDtypeStruct((2,) + piece, bf16), jax.Sh...  2.65 us
  transfers between devices with their start and end apart: 17, of which 9 were waited for; matrix products, arithmetic and copies ran while one was open for 3% of the time, Pallas kernels for 8%

profile of v20, /device:TPU:4, one launch (start us, length us, event | category | flops | bytes accessed | tf_op | source)
XLA Modules:
  0.0 110.3 jit_solution(3475261549687118825)
XLA Ops:
  0.0 0.9 pad_add_fusion.starts
  0.9 2.4 %copy-done.1 = f32[2,256,2048]{2,1,0:T(8,128)S(1)} copy-done((f32[2,256,2048]{2,1,0:T(8,128)S(1)}, f32[2,256,2048]{2,1,0:T(8,128)}, u32[]{:S(2)}) %copy-start.1) | copy-done | bytes 4194328
  3.3 1.4 %windows.1.window = bf16[1024,1024]{1,0:T(8,128)(2,1)S(1)} custom-call(s32[4]{0:T(128)S(1)} %pad_add_fusion.starts, f32[2,256,2048]{2,1,0:T(8,128)S(1)} %copy-done.1), custom_call_target="tpu_custom_call" | custom-call | bytes 6291456 | tf_op jit(solution)/shard_map/windows/pallas_call | solution.py:433
  4.7 1.8 %rows_round_1.1 = (bf16[4,256,128]{2,1,0:T(8,128)(2,1)S(1)}, bf16[4,256,128]{2,1,0:T(8,128)(2,1)S(1)}, bf16[4,256,128]{2,1,0:T(8,128)(2,1)S(1)}) custom-call(bf16[1024,1024]{1,0:T(8,128)(2,1)S(1)} %windows.1.window, bf16[8,1024,256]{2,1,0:T(8,128)(2,1)S(1)} %copy-done), custom_call_target="tpu_custom_call" | custom-call | flops 1610612736 | bytes 5242880 | tf_op jit(solution)/shard_map/rows_round_1/pallas_call | solution.py:445
  6.5 1.3 %collective-permute-start = (bf16[4,256,128]{2,1,0:T(8,128)(2,1)S(1)}, bf16[4,256,128]{2,1,0:T(8,128)(2,1)S(1)}, u32[]{:S(2)}, u32[]{:S(2)}) collective-permute-start(bf16[4,256,128]{2,1,0:T(8,128)(2,1)S(1)} %get-tuple-element.39), channel_id=1, source_target_pairs={{8,16},{12,20},{16,8},{20,12},{4,0},{24,28},{9,17},{13,21},{17,9},... | collective-permute-start | bytes 786440 | tf_op jit(solution)/shard_map/ppermute | solution.py:458
  7.8 5.7 %collective-permute-start.1 = (bf16[4,256,128]{2,1,0:T(8,128)(2,1)S(1)}, bf16[4,256,128]{2,1,0:T(8,128)(2,1)S(1)}, u32[]{:S(2)}, u32[]{:S(2)}) collective-permute-start(bf16[4,256,128]{2,1,0:T(8,128)(2,1)S(1)} %get-tuple-element.40), channel_id=1, source_target_pairs={{4,12},{8,0},{12,4},{16,24},{20,28},{24,16},{5,13},{9,1},{13,5},{1... | collective-permute-start | bytes 786440 | tf_op jit(solution)/shard_map/ppermute | solution.py:458
  13.5 0.0 copy-start.2
  13.5 0.0 copy-start.3
  13.5 1.6 %collective-permute-start.3 = (bf16[4,256,128]{2,1,0:T(8,128)(2,1)S(1)}, bf16[4,256,128]{2,1,0:T(8,128)(2,1)S(1)}, u32[]{:S(2)}, u32[]{:S(2)}) collective-permute-start(bf16[4,256,128]{2,1,0:T(8,128)(2,1)S(1)} %get-tuple-element.50), channel_id=1, source_target_pairs={{8,20},{12,16},{16,12},{20,8},{4,0},{24,28},{9,21},{13,17},{17,13}... | collective-permute-start | bytes 786440 | tf_op jit(solution)/shard_map/ppermute | solution.py:458
  15.1 2.9 %rows_round_2.1 = (bf16[4,256,128]{2,1,0:T(8,128)(2,1)S(1)}, bf16[4,256,128]{2,1,0:T(8,128)(2,1)S(1)}, bf16[4,256,128]{2,1,0:T(8,128)(2,1)S(1)}, bf16[4,256,128]...) custom-call(bf16[1024,1024]{1,0:T(8,128)(2,1)S(1)} %windows.1.window, bf16[8,1024,256]{2,1,0:T(8,128)(2,1)S(1)} %copy-done), custom_call_target="tpu_custom_call" | custom-call | flops 2684354560 | bytes 5242880 | tf_op jit(solution)/shard_map/rows_round_2/pallas_call | solution.py:445
  18.0 0.0 collective-permute-done.got.rest_0_
  18.0 1.5 %collective-permute-done.1.rest_7_ = bf16[4,256,128]{2,1,0:T(8,128)(2,1)S(1)} collective-permute-done((bf16[4,256,128]{2,1,0:T(8,128)(2,1)S(1)}, bf16[4,256,128]{2,1,0:T(8,128)(2,1)S(1)}, u32[]{:S(2)}, u32[]{:S(2)}) %collective-permute-start.1) | collective-permute-done | bytes 262176 | tf_op jit(solution)/shard_map/ppermute | solution.py:458
  19.5 2.9 %collective-permute-start.2 = (bf16[4,256,128]{2,1,0:T(8,128)(2,1)S(1)}, bf16[4,256,128]{2,1,0:T(8,128)(2,1)S(1)}, u32[]{:S(2)}, u32[]{:S(2)}) collective-permute-start(bf16[4,256,128]{2,1,0:T(8,128)(2,1)S(1)} %get-tuple-element.49), channel_id=1, source_target_pairs={{4,8},{8,4},{12,0},{16,28},{20,24},{24,20},{5,9},{9,5},{13,1},{17,... | collective-permute-start | bytes 786440 | tf_op jit(solution)/shard_map/ppermute | solution.py:458
  22.4 3.3 %collective-permute-start.4 = (bf16[4,256,128]{2,1,0:T(8,128)(2,1)S(1)}, bf16[4,256,128]{2,1,0:T(8,128)(2,1)S(1)}, u32[]{:S(2)}, u32[]{:S(2)}) collective-permute-start(bf16[4,256,128]{2,1,0:T(8,128)(2,1)S(1)} %class_4_blocks.1), channel_id=1, source_target_pairs={{0,16},{4,20},{8,24},{12,28},{16,0},{20,4},{24,8},{28,12},{1,17},{... | collective-permute-start | bytes 786440 | tf_op jit(solution)/shard_map/ppermute | solution.py:458
  25.7 1.3 %collective-permute-start.6 = (bf16[4,256,128]{2,1,0:T(8,128)(2,1)S(1)}, bf16[4,256,128]{2,1,0:T(8,128)(2,1)S(1)}, u32[]{:S(2)}, u32[]{:S(2)}) collective-permute-start(bf16[4,256,128]{2,1,0:T(8,128)(2,1)S(1)} %get-tuple-element.53.own), channel_id=1, source_target_pairs={{8,28},{12,24},{16,4},{20,0},{9,29},{13,25},{17,5},{21,1},{10,30},... | collective-permute-start | bytes 786440 | tf_op jit(solution)/shard_map/ppermute | solution.py:458
  27.0 1.6 %collective-permute-start.7 = (bf16[4,256,128]{2,1,0:T(8,128)(2,1)S(1)}, bf16[4,256,128]{2,1,0:T(8,128)(2,1)S(1)}, u32[]{:S(2)}, u32[]{:S(2)}) collective-permute-start(bf16[4,256,128]{2,1,0:T(8,128)(2,1)S(1)} %get-tuple-element.55), channel_id=1, source_target_pairs={{4,0},{8,12},{12,8},{16,20},{20,16},{24,28},{5,1},{9,13},{13,9},{1... | collective-permute-start | bytes 786440 | tf_op jit(solution)/shard_map/ppermute | solution.py:458
  28.6 6.7 %collective-permute-done.2.rest_8_ = bf16[4,256,128]{2,1,0:T(8,128)(2,1)S(1)} collective-permute-done((bf16[4,256,128]{2,1,0:T(8,128)(2,1)S(1)}, bf16[4,256,128]{2,1,0:T(8,128)(2,1)S(1)}, u32[]{:S(2)}, u32[]{:S(2)}) %collective-permute-start.2) | collective-permute-done | bytes 262176 | tf_op jit(solution)/shard_map/ppermute | solution.py:458
  35.3 1.9 %collective-permute-start.5 = (bf16[4,256,128]{2,1,0:T(8,128)(2,1)S(1)}, bf16[4,256,128]{2,1,0:T(8,128)(2,1)S(1)}, u32[]{:S(2)}, u32[]{:S(2)}) collective-permute-start(bf16[4,256,128]{2,1,0:T(8,128)(2,1)S(1)} %class_6_blocks.1), channel_id=1, source_target_pairs={{0,24},{4,28},{24,0},{28,4},{1,25},{5,29},{25,1},{29,5},{2,26},{6,... | collective-permute-start | bytes 786440 | tf_op jit(solution)/shard_map/ppermute | solution.py:458
  37.2 0.6 amplitude.1
  37.8 0.0 collective-permute-done.4.rest_2_
  37.8 9.0 %collective-permute-done.6.rest_4_ = bf16[4,256,128]{2,1,0:T(8,128)(2,1)S(1)} collective-permute-done((bf16[4,256,128]{2,1,0:T(8,128)(2,1)S(1)}, bf16[4,256,128]{2,1,0:T(8,128)(2,1)S(1)}, u32[]{:S(2)}, u32[]{:S(2)}) %collective-permute-start.6) | collective-permute-done | bytes 262176 | tf_op jit(solution)/shard_map/ppermute | solution.py:458
  46.9 5.3 %modulus_step.1 = (bf16[4,256,128]{2,1,0:T(8,128)(2,1)S(1)}, bf16[4,256,128]{2,1,0:T(8,128)(2,1)S(1)}, bf16[4,256,128]{2,1,0:T(8,128)(2,1)S(1)}, bf16[4,256,128]{2,1,0:T(8,128)(2,1)S(1)}) custom-call(f32[1024,256]{1,0:T(8,128)S(1)} %get-tuple-element.46.amplitude, bf16[8,256,1024]{2,1,0:T(8,128)(2,1)S(1)} %get-tuple-element.47.table, ...), custom_call_target="tpu_custom_call" | custom-call | flops 4294967296 | bytes 12582912 | tf_op jit(solution)/shard_map/modulus_step/pallas_call | solution.py:498
  52.2 0.2 collective-permute-start.10
  52.4 2.0 %collective-permute-start.8 = (bf16[4,256,128]{2,1,0:T(8,128)(2,1)S(1)}, bf16[4,256,128]{2,1,0:T(8,128)(2,1)S(1)}, u32[]{:S(2)}, u32[]{:S(2)}) collective-permute-start(bf16[4,256,128]{2,1,0:T(8,128)(2,1)S(1)} %get-tuple-element.59), channel_id=1, source_target_pairs={{0,4},{4,0},{8,12},{12,8},{16,20},{20,16},{24,28},{28,24},{1,5},{5... | collective-permute-start | bytes 786440 | tf_op jit(solution)/shard_map/ppermute | solution.py:458
  54.4 1.4 %collective-permute-start.9 = (bf16[4,256,128]{2,1,0:T(8,128)(2,1)S(1)}, bf16[4,256,128]{2,1,0:T(8,128)(2,1)S(1)}, u32[]{:S(2)}, u32[]{:S(2)}) collective-permute-start(bf16[4,256,128]{2,1,0:T(8,128)(2,1)S(1)} %get-tuple-element.60), channel_id=1, source_target_pairs={{0,8},{4,12},{8,0},{12,4},{16,24},{20,28},{24,16},{28,20},{1,9},{5... | collective-permute-start | bytes 786440 | tf_op jit(solution)/shard_map/ppermute | solution.py:458
  55.7 6.7 %collective-permute-done.10.rest_3_ = bf16[4,256,128]{2,1,0:T(8,128)(2,1)S(1)} collective-permute-done((bf16[4,256,128]{2,1,0:T(8,128)(2,1)S(1)}, bf16[4,256,128]{2,1,0:T(8,128)(2,1)S(1)}, u32[]{:S(2)}, u32[]{:S(2)}) %collective-permute-start.10) | collective-permute-done | bytes 262176 | tf_op jit(solution)/shard_map/ppermute | solution.py:458
  62.4 3.7 %collective-permute-done.8.rest_1_ = bf16[4,256,128]{2,1,0:T(8,128)(2,1)S(1)} collective-permute-done((bf16[4,256,128]{2,1,0:T(8,128)(2,1)S(1)}, bf16[4,256,128]{2,1,0:T(8,128)(2,1)S(1)}, u32[]{:S(2)}, u32[]{:S(2)}) %collective-permute-start.8) | collective-permute-done | bytes 262176 | tf_op jit(solution)/shard_map/ppermute | solution.py:458
  66.2 1.4 %collective-permute-done.9.rest_2_ = bf16[4,256,128]{2,1,0:T(8,128)(2,1)S(1)} collective-permute-done((bf16[4,256,128]{2,1,0:T(8,128)(2,1)S(1)}, bf16[4,256,128]{2,1,0:T(8,128)(2,1)S(1)}, u32[]{:S(2)}, u32[]{:S(2)}) %collective-permute-start.9) | collective-permute-done | bytes 262176 | tf_op jit(solution)/shard_map/ppermute | solution.py:458
  67.6 2.6 %update_sent.1 = (bf16[2,2,256,512]{3,2,1,0:T(8,128)(2,1)S(1)}, bf16[2,2,256,512]{3,2,1,0:T(8,128)(2,1)S(1)}, bf16[1024,512]{1,0:T(8,128)(2,1)S(1)}) custom-call(s32[4]{0:T(128)S(1)} %pad_add_fusion.starts, bf16[8,1024,256]{2,1,0:T(8,128)(2,1)S(1)} %copy-done, bf16[4,256,128]{2,1,0:T(8,128)(2,1)S(1)} %get-tuple-element.58.rest_0_, ...), custom_call_target="tpu_custom_call" | custom-call | flops 1073741824 | bytes 8388608 | tf_op jit(solution)/shard_map/update_sent/pallas_call | solution.py:523
  70.2 0.1 collective-permute-start.12
  70.3 0.5 collective-permute-start.11
  70.8 2.4 %update_kept.1 = (f32[2,256,512]{2,1,0:T(8,128)S(1)}, f32[2,256,512]{2,1,0:T(8,128)S(1)}, f32[2,256,512]{2,1,0:T(8,128)S(1)}, f32[2,256,512]{2,1,0:T(8,128)S(1)}) custom-call(s32[4]{0:T(128)S(1)} %pad_add_fusion.starts, bf16[8,1024,256]{2,1,0:T(8,128)(2,1)S(1)} %copy-done, bf16[1024,512]{1,0:T(8,128)(2,1)S(1)} %get-tuple-element.62.back), custom_call_target="tpu_custom_call" | custom-call | flops 1073741824 | bytes 10485760 | tf_op jit(solution)/shard_map/update_kept/pallas_call | solution.py:538
  73.2 0.0 copy-start.4
  73.3 0.0 collective-permute-done.12.got_that
  73.3 0.1 z_first_kernel.1
  73.4 1.9 %collective-permute-start.13 = (bf16[2,2,256,128]{3,2,1,0:T(8,128)(2,1)S(1)}, bf16[2,2,256,128]{3,2,1,0:T(8,128)(2,1)S(1)}, u32[]{:S(2)}, u32[]{:S(2)}) collective-permute-start(bf16[2,2,256,128]{3,2,1,0:T(8,128)(2,1)S(1)} %z_first_kernel.1), channel_id=1, source_target_pairs={{0,16},{4,20},{8,24},{20,4},{24,8},{28,12},{1,17},{5,21},{9,25},{2... | collective-permute-start | bytes 786440 | tf_op jit(solution)/shard_map/ppermute | solution.py:458
  75.3 0.8 x_first_kernel.1
  76.1 1.5 %collective-permute-start.15 = (bf16[2,256,384]{2,1,0:T(8,128)(2,1)}, bf16[2,256,384]{2,1,0:T(8,128)(2,1)}, u32[]{:S(2)}, u32[]{:S(2)}) collective-permute-start(bf16[2,256,384]{2,1,0:T(8,128)(2,1)} %x_first_kernel.1), channel_id=1, source_target_pairs={{0,2},{2,0},{1,3},{3,1},{4,6},{6,4},{5,7},{7,5},{8,10},{10,8},{9,1... | collective-permute-start | bytes 1179656 | tf_op jit(solution)/shard_map/ppermute | solution.py:556
  77.6 12.1 %collective-permute-done.13.got_z = bf16[2,2,256,128]{3,2,1,0:T(8,128)(2,1)S(1)} collective-permute-done((bf16[2,2,256,128]{3,2,1,0:T(8,128)(2,1)S(1)}, bf16[2,2,256,128]{3,2,1,0:T(8,128)(2,1)S(1)}, u32[]{:S(2)}, u32[]{:S(2)}) %collective-permute-start.13) | collective-permute-done | bytes 262176 | tf_op jit(solution)/shard_map/ppermute | solution.py:458
  89.8 1.0 x_second_kernel.1
  90.7 1.5 %collective-permute-start.14 = (bf16[2,256,512]{2,1,0:T(8,128)(2,1)}, bf16[2,256,512]{2,1,0:T(8,128)(2,1)}, u32[]{:S(2)}, u32[]{:S(2)}) collective-permute-start(bf16[2,256,512]{2,1,0:T(8,128)(2,1)} %x_second_kernel.1), channel_id=1, source_target_pairs={{0,2},{2,0},{1,3},{3,1},{4,6},{6,4},{5,7},{7,5},{8,10},{10,8},{9,1... | collective-permute-start | bytes 1572872 | tf_op jit(solution)/shard_map/ppermute | solution.py:560
  92.2 1.1 %z_second_kernel.1 = bf16[2,256,384]{2,1,0:T(8,128)(2,1)S(1)} custom-call(f32[2,256,512]{2,1,0:T(8,128)S(1)} %get-tuple-element.65.that_near, bf16[2,2,256,512]{3,2,1,0:T(8,128)(2,1)S(1)} %collective-permute-done.12.got_that, bf16[2,256,384]{2,1,0:T(8,128)(2,1)} %collective-permute-done.15.got_x), custom_call_target="tpu_custom_call" | custom-call | bytes 1048576 | tf_op jit(solution)/shard_map/z_second_kernel/pallas_call | solution.py:551
  93.4 1.9 %collective-permute-start.16 = (bf16[2,256,384]{2,1,0:T(8,128)(2,1)S(1)}, bf16[2,256,384]{2,1,0:T(8,128)(2,1)S(1)}, u32[]{:S(2)}, u32[]{:S(2)}) collective-permute-start(bf16[2,256,384]{2,1,0:T(8,128)(2,1)S(1)} %z_second_kernel.1), channel_id=1, source_target_pairs={{0,16},{4,20},{8,24},{20,4},{24,8},{28,12},{1,17},{5,21},{9,25},{2... | collective-permute-start | bytes 1179656 | tf_op jit(solution)/shard_map/ppermute | solution.py:458
  95.3 1.8 %fusion.1 = f32[2,256,512]{2,1,0:T(8,128)S(1)} fusion(f32[2,256,512]{2,1,0:T(8,128)} %copy-done.4, f32[2,256,2048]{2,1,0:T(8,128)} %spectrum.1, s32[]{:T(128)S(6)} %select_n.3, bf16[2,2,256,512]{3,2,1,0:T(8,128)(2,1)S(1)} %collective-permute-done.11.got_this, bf16[2,256,128]{2,1,0:T(8,128)(2,1)S(1)} %slice_bitcast_fusion.1), kind=kLoop, calls=%fused_computation.2 | loop fusion | flops 1310720 | bytes 3801092 | tf_op jit(solution)/shard_map/add | solution.py:567
  97.1 7.8 %collective-permute-done.14 = bf16[2,256,512]{2,1,0:T(8,128)(2,1)} collective-permute-done((bf16[2,256,512]{2,1,0:T(8,128)(2,1)}, bf16[2,256,512]{2,1,0:T(8,128)(2,1)}, u32[]{:S(2)}, u32[]{:S(2)}) %collective-permute-start.14) | collective-permute-done | bytes 524320 | tf_op jit(solution)/shard_map/ppermute | solution.py:560
  104.9 1.2 %convert_add_fusion.2 = f32[2,256,512]{2,1,0:T(8,128)S(1)} fusion(f32[2,256,512]{2,1,0:T(8,128)S(1)} %fusion.1, bf16[2,256,512]{2,1,0:T(8,128)(2,1)} %collective-permute-done.14), kind=kLoop, calls=%fused_computation.4 | loop fusion | flops 524288 | bytes 2621440 | tf_op jit(solution)/shard_map/add | solution.py:569
  106.1 3.1 %collective-permute-done.16 = bf16[2,256,384]{2,1,0:T(8,128)(2,1)S(1)} collective-permute-done((bf16[2,256,384]{2,1,0:T(8,128)(2,1)S(1)}, bf16[2,256,384]{2,1,0:T(8,128)(2,1)S(1)}, u32[]{:S(2)}, u32[]{:S(2)}) %collective-permute-start.16) | collective-permute-done | bytes 393248 | tf_op jit(solution)/shard_map/ppermute | solution.py:458
  109.2 1.1 %convert_add_fusion.1 = f32[2,256,512]{2,1,0:T(8,128)} fusion(f32[2,256,512]{2,1,0:T(8,128)S(1)} %convert_add_fusion.2, bf16[2,256,384]{2,1,0:T(8,128)(2,1)S(1)} %collective-permute-done.16), kind=kLoop, calls=%fused_computation.3 | loop fusion | flops 524288 | bytes 2490368 | tf_op jit(solution)/shard_map/add | solution.py:571
  (14 shorter events, 0.1 us)
Async XLA Ops:
  0.0 4.6 %copy-start = (bf16[8,1024,256]{2,1,0:T(8,128)(2,1)S(1)}, bf16[8,1024,256]{2,1,0:T(8,128)(2,1)}, u32[]{:S(2)}) copy-start(bf16[8,1024,256]{2,1,0:T(8,128)(2,1)} %constant.18.clone.table) | copy-start | bytes 12582916
  0.9 2.4 %copy-start.1 = (f32[2,256,2048]{2,1,0:T(8,128)S(1)}, f32[2,256,2048]{2,1,0:T(8,128)}, u32[]{:S(2)}) copy-start(f32[2,256,2048]{2,1,0:T(8,128)} %spectrum.1) | copy-start | bytes 12582916
  6.5 11.5 %collective-permute-start = (bf16[4,256,128]{2,1,0:T(8,128)(2,1)S(1)}, bf16[4,256,128]{2,1,0:T(8,128)(2,1)S(1)}, u32[]{:S(2)}, u32[]{:S(2)}) collective-permute-start(bf16[4,256,128]{2,1,0:T(8,128)(2,1)S(1)} %get-tuple-element.39), channel_id=1, source_target_pairs={{8,16},{12,20},{16,8},{20,12},{4,0},{24,28},{9,17},{13,21},{17,9},... | collective-permute-start | bytes 786440 | tf_op jit(solution)/shard_map/ppermute | solution.py:458
  7.8 11.7 %collective-permute-start.1 = (bf16[4,256,128]{2,1,0:T(8,128)(2,1)S(1)}, bf16[4,256,128]{2,1,0:T(8,128)(2,1)S(1)}, u32[]{:S(2)}, u32[]{:S(2)}) collective-permute-start(bf16[4,256,128]{2,1,0:T(8,128)(2,1)S(1)} %get-tuple-element.40), channel_id=1, source_target_pairs={{4,12},{8,0},{12,4},{16,24},{20,28},{24,16},{5,13},{9,1},{13,5},{1... | collective-permute-start | bytes 786440 | tf_op jit(solution)/shard_map/ppermute | solution.py:458
  13.5 23.8 %copy-start.2 = (bf16[8,256,1024]{2,1,0:T(8,128)(2,1)S(1)}, bf16[8,256,1024]{2,1,0:T(8,128)(2,1)}, u32[]{:S(2)}) copy-start(bf16[8,256,1024]{2,1,0:T(8,128)(2,1)} %constant.17.clone.table) | copy-start | bytes 12582916
  13.5 23.8 %copy-start.3 = (f32[2,128,1024]{2,1,0:T(8,128)S(1)}, f32[2,128,1024]{2,1,0:T(8,128)}, u32[]{:S(2)}) copy-start(f32[2,128,1024]{2,1,0:T(8,128)} %images) | copy-start | bytes 3145732
  13.5 15.1 %collective-permute-start.3 = (bf16[4,256,128]{2,1,0:T(8,128)(2,1)S(1)}, bf16[4,256,128]{2,1,0:T(8,128)(2,1)S(1)}, u32[]{:S(2)}, u32[]{:S(2)}) collective-permute-start(bf16[4,256,128]{2,1,0:T(8,128)(2,1)S(1)} %get-tuple-element.50), channel_id=1, source_target_pairs={{8,20},{12,16},{16,12},{20,8},{4,0},{24,28},{9,21},{13,17},{17,13}... | collective-permute-start | bytes 786440 | tf_op jit(solution)/shard_map/ppermute | solution.py:458
  19.5 15.8 %collective-permute-start.2 = (bf16[4,256,128]{2,1,0:T(8,128)(2,1)S(1)}, bf16[4,256,128]{2,1,0:T(8,128)(2,1)S(1)}, u32[]{:S(2)}, u32[]{:S(2)}) collective-permute-start(bf16[4,256,128]{2,1,0:T(8,128)(2,1)S(1)} %get-tuple-element.49), channel_id=1, source_target_pairs={{4,8},{8,4},{12,0},{16,28},{20,24},{24,20},{5,9},{9,5},{13,1},{17,... | collective-permute-start | bytes 786440 | tf_op jit(solution)/shard_map/ppermute | solution.py:458
  22.4 15.4 %collective-permute-start.4 = (bf16[4,256,128]{2,1,0:T(8,128)(2,1)S(1)}, bf16[4,256,128]{2,1,0:T(8,128)(2,1)S(1)}, u32[]{:S(2)}, u32[]{:S(2)}) collective-permute-start(bf16[4,256,128]{2,1,0:T(8,128)(2,1)S(1)} %class_4_blocks.1), channel_id=1, source_target_pairs={{0,16},{4,20},{8,24},{12,28},{16,0},{20,4},{24,8},{28,12},{1,17},{... | collective-permute-start | bytes 786440 | tf_op jit(solution)/shard_map/ppermute | solution.py:458
  25.7 21.1 %collective-permute-start.6 = (bf16[4,256,128]{2,1,0:T(8,128)(2,1)S(1)}, bf16[4,256,128]{2,1,0:T(8,128)(2,1)S(1)}, u32[]{:S(2)}, u32[]{:S(2)}) collective-permute-start(bf16[4,256,128]{2,1,0:T(8,128)(2,1)S(1)} %get-tuple-element.53.own), channel_id=1, source_target_pairs={{8,28},{12,24},{16,4},{20,0},{9,29},{13,25},{17,5},{21,1},{10,30},... | collective-permute-start | bytes 786440 | tf_op jit(solution)/shard_map/ppermute | solution.py:458
  27.0 19.9 %collective-permute-start.7 = (bf16[4,256,128]{2,1,0:T(8,128)(2,1)S(1)}, bf16[4,256,128]{2,1,0:T(8,128)(2,1)S(1)}, u32[]{:S(2)}, u32[]{:S(2)}) collective-permute-start(bf16[4,256,128]{2,1,0:T(8,128)(2,1)S(1)} %get-tuple-element.55), channel_id=1, source_target_pairs={{4,0},{8,12},{12,8},{16,20},{20,16},{24,28},{5,1},{9,13},{13,9},{1... | collective-permute-start | bytes 786440 | tf_op jit(solution)/shard_map/ppermute | solution.py:458
  35.3 11.6 %collective-permute-start.5 = (bf16[4,256,128]{2,1,0:T(8,128)(2,1)S(1)}, bf16[4,256,128]{2,1,0:T(8,128)(2,1)S(1)}, u32[]{:S(2)}, u32[]{:S(2)}) collective-permute-start(bf16[4,256,128]{2,1,0:T(8,128)(2,1)S(1)} %class_6_blocks.1), channel_id=1, source_target_pairs={{0,24},{4,28},{24,0},{28,4},{1,25},{5,29},{25,1},{29,5},{2,26},{6,... | collective-permute-start | bytes 786440 | tf_op jit(solution)/shard_map/ppermute | solution.py:458
  52.2 10.3 %collective-permute-start.10 = (bf16[4,256,128]{2,1,0:T(8,128)(2,1)S(1)}, bf16[4,256,128]{2,1,0:T(8,128)(2,1)S(1)}, u32[]{:S(2)}, u32[]{:S(2)}) collective-permute-start(bf16[4,256,128]{2,1,0:T(8,128)(2,1)S(1)} %get-tuple-element.61), channel_id=1, source_target_pairs={{0,12},{4,8},{8,4},{12,0},{16,28},{20,24},{24,20},{28,16},{1,13},{... | collective-permute-start | bytes 786440 | tf_op jit(solution)/shard_map/ppermute | solution.py:458
  52.4 13.8 %collective-permute-start.8 = (bf16[4,256,128]{2,1,0:T(8,128)(2,1)S(1)}, bf16[4,256,128]{2,1,0:T(8,128)(2,1)S(1)}, u32[]{:S(2)}, u32[]{:S(2)}) collective-permute-start(bf16[4,256,128]{2,1,0:T(8,128)(2,1)S(1)} %get-tuple-element.59), channel_id=1, source_target_pairs={{0,4},{4,0},{8,12},{12,8},{16,20},{20,16},{24,28},{28,24},{1,5},{5... | collective-permute-start | bytes 786440 | tf_op jit(solution)/shard_map/ppermute | solution.py:458
  54.4 13.2 %collective-permute-start.9 = (bf16[4,256,128]{2,1,0:T(8,128)(2,1)S(1)}, bf16[4,256,128]{2,1,0:T(8,128)(2,1)S(1)}, u32[]{:S(2)}, u32[]{:S(2)}) collective-permute-start(bf16[4,256,128]{2,1,0:T(8,128)(2,1)S(1)} %get-tuple-element.60), channel_id=1, source_target_pairs={{0,8},{4,12},{8,0},{12,4},{16,24},{20,28},{24,16},{28,20},{1,9},{5... | collective-permute-start | bytes 786440 | tf_op jit(solution)/shard_map/ppermute | solution.py:458
  70.2 3.0 %collective-permute-start.12 = (bf16[2,2,256,512]{3,2,1,0:T(8,128)(2,1)S(1)}, bf16[2,2,256,512]{3,2,1,0:T(8,128)(2,1)S(1)}, u32[]{:S(2)}, u32[]{:S(2)}) collective-permute-start(bf16[2,2,256,512]{3,2,1,0:T(8,128)(2,1)S(1)} %get-tuple-element.67), channel_id=1, source_target_pairs={{0,1},{1,0},{2,3},{3,2},{4,5},{5,4},{6,7},{7,6},{8,9},{9,8},{10,11... | collective-permute-start | bytes 3145736 | tf_op jit(solution)/shard_map/ppermute | solution.py:536
  70.3 7.3 %collective-permute-start.11 = (bf16[2,2,256,512]{3,2,1,0:T(8,128)(2,1)S(1)}, bf16[2,2,256,512]{3,2,1,0:T(8,128)(2,1)S(1)}, u32[]{:S(2)}, u32[]{:S(2)}) collective-permute-start(bf16[2,2,256,512]{3,2,1,0:T(8,128)(2,1)S(1)} %get-tuple-element.64), channel_id=1, source_target_pairs={{0,1},{1,0},{2,3},{3,2},{4,5},{5,4},{6,7},{7,6},{8,9},{9,8},{10,11... | collective-permute-start | bytes 3145736 | tf_op jit(solution)/shard_map/ppermute | solution.py:537
  73.2 4.4 %copy-start.4 = (f32[2,256,512]{2,1,0:T(8,128)}, f32[2,256,512]{2,1,0:T(8,128)S(1)}, u32[]{:S(2)}) copy-start(f32[2,256,512]{2,1,0:T(8,128)S(1)} %get-tuple-element.63) | copy-start | bytes 3145732
  73.4 16.4 %collective-permute-start.13 = (bf16[2,2,256,128]{3,2,1,0:T(8,128)(2,1)S(1)}, bf16[2,2,256,128]{3,2,1,0:T(8,128)(2,1)S(1)}, u32[]{:S(2)}, u32[]{:S(2)}) collective-permute-start(bf16[2,2,256,128]{3,2,1,0:T(8,128)(2,1)S(1)} %z_first_kernel.1), channel_id=1, source_target_pairs={{0,16},{4,20},{8,24},{20,4},{24,8},{28,12},{1,17},{5,21},{9,25},{2... | collective-permute-start | bytes 786440 | tf_op jit(solution)/shard_map/ppermute | solution.py:458
  76.1 16.1 %collective-permute-start.15 = (bf16[2,256,384]{2,1,0:T(8,128)(2,1)}, bf16[2,256,384]{2,1,0:T(8,128)(2,1)}, u32[]{:S(2)}, u32[]{:S(2)}) collective-permute-start(bf16[2,256,384]{2,1,0:T(8,128)(2,1)} %x_first_kernel.1), channel_id=1, source_target_pairs={{0,2},{2,0},{1,3},{3,1},{4,6},{6,4},{5,7},{7,5},{8,10},{10,8},{9,1... | collective-permute-start | bytes 1179656 | tf_op jit(solution)/shard_map/ppermute | solution.py:556
  90.7 14.2 %collective-permute-start.14 = (bf16[2,256,512]{2,1,0:T(8,128)(2,1)}, bf16[2,256,512]{2,1,0:T(8,128)(2,1)}, u32[]{:S(2)}, u32[]{:S(2)}) collective-permute-start(bf16[2,256,512]{2,1,0:T(8,128)(2,1)} %x_second_kernel.1), channel_id=1, source_target_pairs={{0,2},{2,0},{1,3},{3,1},{4,6},{6,4},{5,7},{7,5},{8,10},{10,8},{9,1... | collective-permute-start | bytes 1572872 | tf_op jit(solution)/shard_map/ppermute | solution.py:560
  93.4 15.8 %collective-permute-start.16 = (bf16[2,256,384]{2,1,0:T(8,128)(2,1)S(1)}, bf16[2,256,384]{2,1,0:T(8,128)(2,1)S(1)}, u32[]{:S(2)}, u32[]{:S(2)}) collective-permute-start(bf16[2,256,384]{2,1,0:T(8,128)(2,1)S(1)} %z_second_kernel.1), channel_id=1, source_target_pairs={{0,16},{4,20},{8,24},{20,4},{24,8},{28,12},{1,17},{5,21},{9,25},{2... | collective-permute-start | bytes 1179656 | tf_op jit(solution)/shard_map/ppermute | solution.py:458

commit v21 on v20

--- a/solution.py
+++ b/solution.py
@@ -475,12 +475,15 @@
     near_1 = permute(near_1, [(s, s ^ 1) for s in windowed])
     near_3 = permute(near_3, [(s, s ^ 3) for s in windowed])
     near_3, got_b = lax.optimization_barrier((near_3, got_b))
+    third = choose(got_a, second_b, "class_5_blocks")
+    inner_5 = permute(third, [(s, s ^ 5) for s in INNER])
+    third, second_a = lax.optimization_barrier((third, second_a))
     far_columns = [
         got_a,
         got_b,
         permute(choose(got_a, second_a, "class_4_blocks"), [(s, s ^ 4) for s in range(SLABS)]),
         permute(choose(got_b, second_b, "class_6_blocks"), outer_pairs),
-        permute(second_b, [(s, s ^ 5) for s in INNER]),
+        inner_5,
     ]
     near_columns = [near_0, near_1, near_2, near_3]
     amplitude, by_row = local_call(

time: 111 us -> 112 us (level)
  starting transfers between devices: 30.5 us -> 36 us
  waiting for transfers between devices: 52 us -> 47.2 us
    ppermute x13, starting transfers between devices: 26.9 us -> 32.5 us  [permute(): return lax.ppermute(sent, 'slab', pairs)]
    ppermute x13, waiting for transfers between devices: 44.3 us -> 39.4 us  [permute(): return lax.ppermute(sent, 'slab', pairs)]
where the time goes in v21:
time: 112 us; the launch traced here: 111 us
  waiting for transfers between devices  47.2 us (42%)
  starting transfers between devices  36 us (32%)
  Pallas kernels  20.1 us (18%)
  other arithmetic  5.06 us (5%)
  local copies, waits for them, and re-layouts  2.42 us (2%)
    ppermute x13, waiting for transfers between devices, permute(): return lax.ppermute(sent, 'slab', pairs)  39.4 us
    ppermute x13, starting transfers between devices, permute(): return lax.ppermute(sent, 'slab', pairs)  32.5 us
    ppermute x2, waiting for transfers between devices, body_slabs(): got_x = lax.ppermute(over, 'led', planes)  7.77 us
    pallas_call x1, Pallas kernels, body_slabs(): local_call(field_kernel, [sent_block] * HALF, [vmem] * 11, [pltpu.VMEM((w...  5.31 us
    pallas_call x2, Pallas kernels, rows_call(): local_call(functools.partial(rows_kernel, which), [sent_block] * count, [...  4.69 us
    pallas_call x4, Pallas kernels, sum_call(): local_call(kernel, out_shape, specs, [], 0, 2 ** 20, kernel.__name__)  3 us
    ppermute x2, starting transfers between devices, body_slabs(): got_x = lax.ppermute(over, 'led', planes)  3 us
    pallas_call x1, Pallas kernels, body_slabs(): local_call(sent_kernel, [jax.ShapeDtypeStruct((2,) + piece, bf16), jax.Sh...  2.64 us
  transfers between devices with their start and end apart: 17, of which 9 were waited for; matrix products, arithmetic and copies ran while one was open for 3% of the time, Pallas kernels for 8%

profile of v21, /device:TPU:4, one launch (start us, length us, event | category | flops | bytes accessed | tf_op | source)
XLA Modules:
  0.0 111.1 jit_solution(15864936388361625850)
XLA Ops:
  0.0 0.9 pad_add_fusion.starts
  0.9 2.4 %copy-done.1 = f32[2,256,2048]{2,1,0:T(8,128)S(1)} copy-done((f32[2,256,2048]{2,1,0:T(8,128)S(1)}, f32[2,256,2048]{2,1,0:T(8,128)}, u32[]{:S(2)}) %copy-start.1) | copy-done | bytes 4194328
  3.3 1.4 %windows.1.window = bf16[1024,1024]{1,0:T(8,128)(2,1)S(1)} custom-call(s32[4]{0:T(128)S(1)} %pad_add_fusion.starts, f32[2,256,2048]{2,1,0:T(8,128)S(1)} %copy-done.1), custom_call_target="tpu_custom_call" | custom-call | bytes 6291456 | tf_op jit(solution)/shard_map/windows/pallas_call | solution.py:433
  4.7 1.8 %rows_round_1.1 = (bf16[4,256,128]{2,1,0:T(8,128)(2,1)S(1)}, bf16[4,256,128]{2,1,0:T(8,128)(2,1)S(1)}, bf16[4,256,128]{2,1,0:T(8,128)(2,1)S(1)}) custom-call(bf16[1024,1024]{1,0:T(8,128)(2,1)S(1)} %windows.1.window, bf16[8,1024,256]{2,1,0:T(8,128)(2,1)S(1)} %copy-done), custom_call_target="tpu_custom_call" | custom-call | flops 1610612736 | bytes 5242880 | tf_op jit(solution)/shard_map/rows_round_1/pallas_call | solution.py:445
  6.5 1.3 %collective-permute-start = (bf16[4,256,128]{2,1,0:T(8,128)(2,1)S(1)}, bf16[4,256,128]{2,1,0:T(8,128)(2,1)S(1)}, u32[]{:S(2)}, u32[]{:S(2)}) collective-permute-start(bf16[4,256,128]{2,1,0:T(8,128)(2,1)S(1)} %get-tuple-element.40), channel_id=1, source_target_pairs={{8,16},{12,20},{16,8},{20,12},{4,0},{24,28},{9,17},{13,21},{17,9},... | collective-permute-start | bytes 786440 | tf_op jit(solution)/shard_map/ppermute | solution.py:458
  7.8 5.7 %collective-permute-start.1 = (bf16[4,256,128]{2,1,0:T(8,128)(2,1)S(1)}, bf16[4,256,128]{2,1,0:T(8,128)(2,1)S(1)}, u32[]{:S(2)}, u32[]{:S(2)}) collective-permute-start(bf16[4,256,128]{2,1,0:T(8,128)(2,1)S(1)} %get-tuple-element.41), channel_id=1, source_target_pairs={{4,12},{8,0},{12,4},{16,24},{20,28},{24,16},{5,13},{9,1},{13,5},{1... | collective-permute-start | bytes 786440 | tf_op jit(solution)/shard_map/ppermute | solution.py:458
  13.5 0.0 copy-start.2
  13.5 0.0 copy-start.3
  13.5 1.6 %collective-permute-start.3 = (bf16[4,256,128]{2,1,0:T(8,128)(2,1)S(1)}, bf16[4,256,128]{2,1,0:T(8,128)(2,1)S(1)}, u32[]{:S(2)}, u32[]{:S(2)}) collective-permute-start(bf16[4,256,128]{2,1,0:T(8,128)(2,1)S(1)} %get-tuple-element.51), channel_id=1, source_target_pairs={{8,20},{12,16},{16,12},{20,8},{4,0},{24,28},{9,21},{13,17},{17,13}... | collective-permute-start | bytes 786440 | tf_op jit(solution)/shard_map/ppermute | solution.py:458
  15.1 2.9 %rows_round_2.1 = (bf16[4,256,128]{2,1,0:T(8,128)(2,1)S(1)}, bf16[4,256,128]{2,1,0:T(8,128)(2,1)S(1)}, bf16[4,256,128]{2,1,0:T(8,128)(2,1)S(1)}, bf16[4,256,128]...) custom-call(bf16[1024,1024]{1,0:T(8,128)(2,1)S(1)} %windows.1.window, bf16[8,1024,256]{2,1,0:T(8,128)(2,1)S(1)} %copy-done), custom_call_target="tpu_custom_call" | custom-call | flops 2684354560 | bytes 5242880 | tf_op jit(solution)/shard_map/rows_round_2/pallas_call | solution.py:445
  18.0 1.5 %collective-permute-done.1.rest_7_ = bf16[4,256,128]{2,1,0:T(8,128)(2,1)S(1)} collective-permute-done((bf16[4,256,128]{2,1,0:T(8,128)(2,1)S(1)}, bf16[4,256,128]{2,1,0:T(8,128)(2,1)S(1)}, u32[]{:S(2)}, u32[]{:S(2)}) %collective-permute-start.1) | collective-permute-done | bytes 262176 | tf_op jit(solution)/shard_map/ppermute | solution.py:458
  19.5 2.9 %collective-permute-start.2 = (bf16[4,256,128]{2,1,0:T(8,128)(2,1)S(1)}, bf16[4,256,128]{2,1,0:T(8,128)(2,1)S(1)}, u32[]{:S(2)}, u32[]{:S(2)}) collective-permute-start(bf16[4,256,128]{2,1,0:T(8,128)(2,1)S(1)} %get-tuple-element.50), channel_id=1, source_target_pairs={{4,8},{8,4},{12,0},{16,28},{20,24},{24,20},{5,9},{9,5},{13,1},{17,... | collective-permute-start | bytes 786440 | tf_op jit(solution)/shard_map/ppermute | solution.py:458
  22.4 1.3 %collective-permute-start.6 = (bf16[4,256,128]{2,1,0:T(8,128)(2,1)S(1)}, bf16[4,256,128]{2,1,0:T(8,128)(2,1)S(1)}, u32[]{:S(2)}, u32[]{:S(2)}) collective-permute-start(bf16[4,256,128]{2,1,0:T(8,128)(2,1)S(1)} %class_5_blocks.1), channel_id=1, source_target_pairs={{8,28},{12,24},{16,4},{20,0},{9,29},{13,25},{17,5},{21,1},{10,30},... | collective-permute-start | bytes 786440 | tf_op jit(solution)/shard_map/ppermute | solution.py:458
  23.7 3.3 %collective-permute-start.4 = (bf16[4,256,128]{2,1,0:T(8,128)(2,1)S(1)}, bf16[4,256,128]{2,1,0:T(8,128)(2,1)S(1)}, u32[]{:S(2)}, u32[]{:S(2)}) collective-permute-start(bf16[4,256,128]{2,1,0:T(8,128)(2,1)S(1)} %class_4_blocks.1), channel_id=1, source_target_pairs={{0,16},{4,20},{8,24},{12,28},{16,0},{20,4},{24,8},{28,12},{1,17},{... | collective-permute-start | bytes 786440 | tf_op jit(solution)/shard_map/ppermute | solution.py:458
  27.1 3.7 %collective-permute-start.7 = (bf16[4,256,128]{2,1,0:T(8,128)(2,1)S(1)}, bf16[4,256,128]{2,1,0:T(8,128)(2,1)S(1)}, u32[]{:S(2)}, u32[]{:S(2)}) collective-permute-start(bf16[4,256,128]{2,1,0:T(8,128)(2,1)S(1)} %get-tuple-element.57), channel_id=1, source_target_pairs={{4,0},{8,12},{12,8},{16,20},{20,16},{24,28},{5,1},{9,13},{13,9},{1... | collective-permute-start | bytes 786440 | tf_op jit(solution)/shard_map/ppermute | solution.py:458
  30.7 0.0 collective-permute-done.3.got.rest_1_
  30.8 0.7 collective-permute-done.2.rest_8_
  31.5 5.3 %collective-permute-start.5 = (bf16[4,256,128]{2,1,0:T(8,128)(2,1)S(1)}, bf16[4,256,128]{2,1,0:T(8,128)(2,1)S(1)}, u32[]{:S(2)}, u32[]{:S(2)}) collective-permute-start(bf16[4,256,128]{2,1,0:T(8,128)(2,1)S(1)} %class_6_blocks.1), channel_id=1, source_target_pairs={{0,24},{4,28},{24,0},{28,4},{1,25},{5,29},{25,1},{29,5},{2,26},{6,... | collective-permute-start | bytes 786440 | tf_op jit(solution)/shard_map/ppermute | solution.py:458
  36.9 0.6 amplitude.1
  37.4 11.2 %collective-permute-done.4.rest_2_ = bf16[4,256,128]{2,1,0:T(8,128)(2,1)S(1)} collective-permute-done((bf16[4,256,128]{2,1,0:T(8,128)(2,1)S(1)}, bf16[4,256,128]{2,1,0:T(8,128)(2,1)S(1)}, u32[]{:S(2)}, u32[]{:S(2)}) %collective-permute-start.4) | collective-permute-done | bytes 262176 | tf_op jit(solution)/shard_map/ppermute | solution.py:458
  48.6 0.0 collective-permute-done.6.rest_4_
  48.6 0.0 collective-permute-done.7.rest_6_
  48.6 5.3 %modulus_step.1 = (bf16[4,256,128]{2,1,0:T(8,128)(2,1)S(1)}, bf16[4,256,128]{2,1,0:T(8,128)(2,1)S(1)}, bf16[4,256,128]{2,1,0:T(8,128)(2,1)S(1)}, bf16[4,256,128]{2,1,0:T(8,128)(2,1)S(1)}) custom-call(f32[1024,256]{1,0:T(8,128)S(1)} %get-tuple-element.47.amplitude, bf16[8,256,1024]{2,1,0:T(8,128)(2,1)S(1)} %get-tuple-element.48.table, ...), custom_call_target="tpu_custom_call" | custom-call | flops 4294967296 | bytes 12582912 | tf_op jit(solution)/shard_map/modulus_step/pallas_call | solution.py:501
  54.0 0.1 collective-permute-start.10
  54.0 2.1 %collective-permute-start.8 = (bf16[4,256,128]{2,1,0:T(8,128)(2,1)S(1)}, bf16[4,256,128]{2,1,0:T(8,128)(2,1)S(1)}, u32[]{:S(2)}, u32[]{:S(2)}) collective-permute-start(bf16[4,256,128]{2,1,0:T(8,128)(2,1)S(1)} %get-tuple-element.61), channel_id=1, source_target_pairs={{0,4},{4,0},{8,12},{12,8},{16,20},{20,16},{24,28},{28,24},{1,5},{5... | collective-permute-start | bytes 786440 | tf_op jit(solution)/shard_map/ppermute | solution.py:458
  56.2 1.4 %collective-permute-start.9 = (bf16[4,256,128]{2,1,0:T(8,128)(2,1)S(1)}, bf16[4,256,128]{2,1,0:T(8,128)(2,1)S(1)}, u32[]{:S(2)}, u32[]{:S(2)}) collective-permute-start(bf16[4,256,128]{2,1,0:T(8,128)(2,1)S(1)} %get-tuple-element.62), channel_id=1, source_target_pairs={{0,8},{4,12},{8,0},{12,4},{16,24},{20,28},{24,16},{28,20},{1,9},{5... | collective-permute-start | bytes 786440 | tf_op jit(solution)/shard_map/ppermute | solution.py:458
  57.6 6.3 %collective-permute-done.10.rest_3_ = bf16[4,256,128]{2,1,0:T(8,128)(2,1)S(1)} collective-permute-done((bf16[4,256,128]{2,1,0:T(8,128)(2,1)S(1)}, bf16[4,256,128]{2,1,0:T(8,128)(2,1)S(1)}, u32[]{:S(2)}, u32[]{:S(2)}) %collective-permute-start.10) | collective-permute-done | bytes 262176 | tf_op jit(solution)/shard_map/ppermute | solution.py:458
  63.9 2.7 %collective-permute-done.8.rest_1_ = bf16[4,256,128]{2,1,0:T(8,128)(2,1)S(1)} collective-permute-done((bf16[4,256,128]{2,1,0:T(8,128)(2,1)S(1)}, bf16[4,256,128]{2,1,0:T(8,128)(2,1)S(1)}, u32[]{:S(2)}, u32[]{:S(2)}) %collective-permute-start.8) | collective-permute-done | bytes 262176 | tf_op jit(solution)/shard_map/ppermute | solution.py:458
  66.5 1.8 %collective-permute-done.9.rest_2_ = bf16[4,256,128]{2,1,0:T(8,128)(2,1)S(1)} collective-permute-done((bf16[4,256,128]{2,1,0:T(8,128)(2,1)S(1)}, bf16[4,256,128]{2,1,0:T(8,128)(2,1)S(1)}, u32[]{:S(2)}, u32[]{:S(2)}) %collective-permute-start.9) | collective-permute-done | bytes 262176 | tf_op jit(solution)/shard_map/ppermute | solution.py:458
  68.3 2.6 %update_sent.1 = (bf16[2,2,256,512]{3,2,1,0:T(8,128)(2,1)S(1)}, bf16[2,2,256,512]{3,2,1,0:T(8,128)(2,1)S(1)}, bf16[1024,512]{1,0:T(8,128)(2,1)S(1)}) custom-call(s32[4]{0:T(128)S(1)} %pad_add_fusion.starts, bf16[8,1024,256]{2,1,0:T(8,128)(2,1)S(1)} %copy-done, bf16[4,256,128]{2,1,0:T(8,128)(2,1)S(1)} %get-tuple-element.60.rest_0_, ...), custom_call_target="tpu_custom_call" | custom-call | flops 1073741824 | bytes 8388608 | tf_op jit(solution)/shard_map/update_sent/pallas_call | solution.py:526
  71.0 0.1 collective-permute-start.12
  71.0 0.5 collective-permute-start.11
  71.5 2.4 %update_kept.1 = (f32[2,256,512]{2,1,0:T(8,128)S(1)}, f32[2,256,512]{2,1,0:T(8,128)S(1)}, f32[2,256,512]{2,1,0:T(8,128)S(1)}, f32[2,256,512]{2,1,0:T(8,128)S(1)}) custom-call(s32[4]{0:T(128)S(1)} %pad_add_fusion.starts, bf16[8,1024,256]{2,1,0:T(8,128)(2,1)S(1)} %copy-done, bf16[1024,512]{1,0:T(8,128)(2,1)S(1)} %get-tuple-element.64.back), custom_call_target="tpu_custom_call" | custom-call | flops 1073741824 | bytes 10485760 | tf_op jit(solution)/shard_map/update_kept/pallas_call | solution.py:541
  74.0 0.0 copy-start.4
  74.0 0.1 z_first_kernel.1
  74.1 1.9 %collective-permute-start.13 = (bf16[2,2,256,128]{3,2,1,0:T(8,128)(2,1)S(1)}, bf16[2,2,256,128]{3,2,1,0:T(8,128)(2,1)S(1)}, u32[]{:S(2)}, u32[]{:S(2)}) collective-permute-start(bf16[2,2,256,128]{3,2,1,0:T(8,128)(2,1)S(1)} %z_first_kernel.1), channel_id=1, source_target_pairs={{0,16},{4,20},{8,24},{20,4},{24,8},{28,12},{1,17},{5,21},{9,25},{2... | collective-permute-start | bytes 786440 | tf_op jit(solution)/shard_map/ppermute | solution.py:458
  76.1 0.8 x_first_kernel.1
  76.9 1.5 %collective-permute-start.15 = (bf16[2,256,384]{2,1,0:T(8,128)(2,1)}, bf16[2,256,384]{2,1,0:T(8,128)(2,1)}, u32[]{:S(2)}, u32[]{:S(2)}) collective-permute-start(bf16[2,256,384]{2,1,0:T(8,128)(2,1)} %x_first_kernel.1), channel_id=1, source_target_pairs={{0,2},{2,0},{1,3},{3,1},{4,6},{6,4},{5,7},{7,5},{8,10},{10,8},{9,1... | collective-permute-start | bytes 1179656 | tf_op jit(solution)/shard_map/ppermute | solution.py:559
  78.4 12.1 %collective-permute-done.13.got_z = bf16[2,2,256,128]{3,2,1,0:T(8,128)(2,1)S(1)} collective-permute-done((bf16[2,2,256,128]{3,2,1,0:T(8,128)(2,1)S(1)}, bf16[2,2,256,128]{3,2,1,0:T(8,128)(2,1)S(1)}, u32[]{:S(2)}, u32[]{:S(2)}) %collective-permute-start.13) | collective-permute-done | bytes 262176 | tf_op jit(solution)/shard_map/ppermute | solution.py:458
  90.5 1.0 x_second_kernel.1
  91.5 1.5 %collective-permute-start.14 = (bf16[2,256,512]{2,1,0:T(8,128)(2,1)}, bf16[2,256,512]{2,1,0:T(8,128)(2,1)}, u32[]{:S(2)}, u32[]{:S(2)}) collective-permute-start(bf16[2,256,512]{2,1,0:T(8,128)(2,1)} %x_second_kernel.1), channel_id=1, source_target_pairs={{0,2},{2,0},{1,3},{3,1},{4,6},{6,4},{5,7},{7,5},{8,10},{10,8},{9,1... | collective-permute-start | bytes 1572872 | tf_op jit(solution)/shard_map/ppermute | solution.py:563
  93.0 1.1 %z_second_kernel.1 = bf16[2,256,384]{2,1,0:T(8,128)(2,1)S(1)} custom-call(f32[2,256,512]{2,1,0:T(8,128)S(1)} %get-tuple-element.67.that_near, bf16[2,2,256,512]{3,2,1,0:T(8,128)(2,1)S(1)} %collective-permute-done.12.got_that, bf16[2,256,384]{2,1,0:T(8,128)(2,1)} %collective-permute-done.15.got_x), custom_call_target="tpu_custom_call" | custom-call | bytes 1048576 | tf_op jit(solution)/shard_map/z_second_kernel/pallas_call | solution.py:554
  94.1 1.9 %collective-permute-start.16 = (bf16[2,256,384]{2,1,0:T(8,128)(2,1)S(1)}, bf16[2,256,384]{2,1,0:T(8,128)(2,1)S(1)}, u32[]{:S(2)}, u32[]{:S(2)}) collective-permute-start(bf16[2,256,384]{2,1,0:T(8,128)(2,1)S(1)} %z_second_kernel.1), channel_id=1, source_target_pairs={{0,16},{4,20},{8,24},{20,4},{24,8},{28,12},{1,17},{5,21},{9,25},{2... | collective-permute-start | bytes 1179656 | tf_op jit(solution)/shard_map/ppermute | solution.py:458
  96.0 1.8 %fusion.1 = f32[2,256,512]{2,1,0:T(8,128)S(1)} fusion(f32[2,256,512]{2,1,0:T(8,128)} %copy-done.4, f32[2,256,2048]{2,1,0:T(8,128)} %spectrum.1, s32[]{:T(128)S(6)} %select_n.3, bf16[2,2,256,512]{3,2,1,0:T(8,128)(2,1)S(1)} %collective-permute-done.11.got_this, bf16[2,256,128]{2,1,0:T(8,128)(2,1)S(1)} %slice_bitcast_fusion.1), kind=kLoop, calls=%fused_computation.2 | loop fusion | flops 1310720 | bytes 3801092 | tf_op jit(solution)/shard_map/add | solution.py:570
  97.9 7.8 %collective-permute-done.14 = bf16[2,256,512]{2,1,0:T(8,128)(2,1)} collective-permute-done((bf16[2,256,512]{2,1,0:T(8,128)(2,1)}, bf16[2,256,512]{2,1,0:T(8,128)(2,1)}, u32[]{:S(2)}, u32[]{:S(2)}) %collective-permute-start.14) | collective-permute-done | bytes 524320 | tf_op jit(solution)/shard_map/ppermute | solution.py:563
  105.6 1.2 %convert_add_fusion.2 = f32[2,256,512]{2,1,0:T(8,128)S(1)} fusion(f32[2,256,512]{2,1,0:T(8,128)S(1)} %fusion.1, bf16[2,256,512]{2,1,0:T(8,128)(2,1)} %collective-permute-done.14), kind=kLoop, calls=%fused_computation.4 | loop fusion | flops 524288 | bytes 2621440 | tf_op jit(solution)/shard_map/add | solution.py:572
  106.8 3.1 %collective-permute-done.16 = bf16[2,256,384]{2,1,0:T(8,128)(2,1)S(1)} collective-permute-done((bf16[2,256,384]{2,1,0:T(8,128)(2,1)S(1)}, bf16[2,256,384]{2,1,0:T(8,128)(2,1)S(1)}, u32[]{:S(2)}, u32[]{:S(2)}) %collective-permute-start.16) | collective-permute-done | bytes 393248 | tf_op jit(solution)/shard_map/ppermute | solution.py:458
  109.9 1.1 %convert_add_fusion.1 = f32[2,256,512]{2,1,0:T(8,128)} fusion(f32[2,256,512]{2,1,0:T(8,128)S(1)} %convert_add_fusion.2, bf16[2,256,384]{2,1,0:T(8,128)(2,1)S(1)} %collective-permute-done.16), kind=kLoop, calls=%fused_computation.3 | loop fusion | flops 524288 | bytes 2490368 | tf_op jit(solution)/shard_map/add | solution.py:574
  (15 shorter events, 0.1 us)
Async XLA Ops:
  0.0 4.6 %copy-start = (bf16[8,1024,256]{2,1,0:T(8,128)(2,1)S(1)}, bf16[8,1024,256]{2,1,0:T(8,128)(2,1)}, u32[]{:S(2)}) copy-start(bf16[8,1024,256]{2,1,0:T(8,128)(2,1)} %constant.18.clone.table) | copy-start | bytes 12582916
  0.9 2.4 %copy-start.1 = (f32[2,256,2048]{2,1,0:T(8,128)S(1)}, f32[2,256,2048]{2,1,0:T(8,128)}, u32[]{:S(2)}) copy-start(f32[2,256,2048]{2,1,0:T(8,128)} %spectrum.1) | copy-start | bytes 12582916
  6.5 11.5 %collective-permute-start = (bf16[4,256,128]{2,1,0:T(8,128)(2,1)S(1)}, bf16[4,256,128]{2,1,0:T(8,128)(2,1)S(1)}, u32[]{:S(2)}, u32[]{:S(2)}) collective-permute-start(bf16[4,256,128]{2,1,0:T(8,128)(2,1)S(1)} %get-tuple-element.40), channel_id=1, source_target_pairs={{8,16},{12,20},{16,8},{20,12},{4,0},{24,28},{9,17},{13,21},{17,9},... | collective-permute-start | bytes 786440 | tf_op jit(solution)/shard_map/ppermute | solution.py:458
  7.8 11.7 %collective-permute-start.1 = (bf16[4,256,128]{2,1,0:T(8,128)(2,1)S(1)}, bf16[4,256,128]{2,1,0:T(8,128)(2,1)S(1)}, u32[]{:S(2)}, u32[]{:S(2)}) collective-permute-start(bf16[4,256,128]{2,1,0:T(8,128)(2,1)S(1)} %get-tuple-element.41), channel_id=1, source_target_pairs={{4,12},{8,0},{12,4},{16,24},{20,28},{24,16},{5,13},{9,1},{13,5},{1... | collective-permute-start | bytes 786440 | tf_op jit(solution)/shard_map/ppermute | solution.py:458
  13.5 23.4 %copy-start.2 = (bf16[8,256,1024]{2,1,0:T(8,128)(2,1)S(1)}, bf16[8,256,1024]{2,1,0:T(8,128)(2,1)}, u32[]{:S(2)}) copy-start(bf16[8,256,1024]{2,1,0:T(8,128)(2,1)} %constant.17.clone.table) | copy-start | bytes 12582916
  13.5 23.4 %copy-start.3 = (f32[2,128,1024]{2,1,0:T(8,128)S(1)}, f32[2,128,1024]{2,1,0:T(8,128)}, u32[]{:S(2)}) copy-start(f32[2,128,1024]{2,1,0:T(8,128)} %images) | copy-start | bytes 3145732
  13.5 17.3 %collective-permute-start.3 = (bf16[4,256,128]{2,1,0:T(8,128)(2,1)S(1)}, bf16[4,256,128]{2,1,0:T(8,128)(2,1)S(1)}, u32[]{:S(2)}, u32[]{:S(2)}) collective-permute-start(bf16[4,256,128]{2,1,0:T(8,128)(2,1)S(1)} %get-tuple-element.51), channel_id=1, source_target_pairs={{8,20},{12,16},{16,12},{20,8},{4,0},{24,28},{9,21},{13,17},{17,13}... | collective-permute-start | bytes 786440 | tf_op jit(solution)/shard_map/ppermute | solution.py:458
  19.5 12.0 %collective-permute-start.2 = (bf16[4,256,128]{2,1,0:T(8,128)(2,1)S(1)}, bf16[4,256,128]{2,1,0:T(8,128)(2,1)S(1)}, u32[]{:S(2)}, u32[]{:S(2)}) collective-permute-start(bf16[4,256,128]{2,1,0:T(8,128)(2,1)S(1)} %get-tuple-element.50), channel_id=1, source_target_pairs={{4,8},{8,4},{12,0},{16,28},{20,24},{24,20},{5,9},{9,5},{13,1},{17,... | collective-permute-start | bytes 786440 | tf_op jit(solution)/shard_map/ppermute | solution.py:458
  22.4 26.2 %collective-permute-start.6 = (bf16[4,256,128]{2,1,0:T(8,128)(2,1)S(1)}, bf16[4,256,128]{2,1,0:T(8,128)(2,1)S(1)}, u32[]{:S(2)}, u32[]{:S(2)}) collective-permute-start(bf16[4,256,128]{2,1,0:T(8,128)(2,1)S(1)} %class_5_blocks.1), channel_id=1, source_target_pairs={{8,28},{12,24},{16,4},{20,0},{9,29},{13,25},{17,5},{21,1},{10,30},... | collective-permute-start | bytes 786440 | tf_op jit(solution)/shard_map/ppermute | solution.py:458
  23.7 24.9 %collective-permute-start.4 = (bf16[4,256,128]{2,1,0:T(8,128)(2,1)S(1)}, bf16[4,256,128]{2,1,0:T(8,128)(2,1)S(1)}, u32[]{:S(2)}, u32[]{:S(2)}) collective-permute-start(bf16[4,256,128]{2,1,0:T(8,128)(2,1)S(1)} %class_4_blocks.1), channel_id=1, source_target_pairs={{0,16},{4,20},{8,24},{12,28},{16,0},{20,4},{24,8},{28,12},{1,17},{... | collective-permute-start | bytes 786440 | tf_op jit(solution)/shard_map/ppermute | solution.py:458
  27.1 21.6 %collective-permute-start.7 = (bf16[4,256,128]{2,1,0:T(8,128)(2,1)S(1)}, bf16[4,256,128]{2,1,0:T(8,128)(2,1)S(1)}, u32[]{:S(2)}, u32[]{:S(2)}) collective-permute-start(bf16[4,256,128]{2,1,0:T(8,128)(2,1)S(1)} %get-tuple-element.57), channel_id=1, source_target_pairs={{4,0},{8,12},{12,8},{16,20},{20,16},{24,28},{5,1},{9,13},{13,9},{1... | collective-permute-start | bytes 786440 | tf_op jit(solution)/shard_map/ppermute | solution.py:458
  31.5 17.1 %collective-permute-start.5 = (bf16[4,256,128]{2,1,0:T(8,128)(2,1)S(1)}, bf16[4,256,128]{2,1,0:T(8,128)(2,1)S(1)}, u32[]{:S(2)}, u32[]{:S(2)}) collective-permute-start(bf16[4,256,128]{2,1,0:T(8,128)(2,1)S(1)} %class_6_blocks.1), channel_id=1, source_target_pairs={{0,24},{4,28},{24,0},{28,4},{1,25},{5,29},{25,1},{29,5},{2,26},{6,... | collective-permute-start | bytes 786440 | tf_op jit(solution)/shard_map/ppermute | solution.py:458
  54.0 9.9 %collective-permute-start.10 = (bf16[4,256,128]{2,1,0:T(8,128)(2,1)S(1)}, bf16[4,256,128]{2,1,0:T(8,128)(2,1)S(1)}, u32[]{:S(2)}, u32[]{:S(2)}) collective-permute-start(bf16[4,256,128]{2,1,0:T(8,128)(2,1)S(1)} %get-tuple-element.63), channel_id=1, source_target_pairs={{0,12},{4,8},{8,4},{12,0},{16,28},{20,24},{24,20},{28,16},{1,13},{... | collective-permute-start | bytes 786440 | tf_op jit(solution)/shard_map/ppermute | solution.py:458
  54.0 12.5 %collective-permute-start.8 = (bf16[4,256,128]{2,1,0:T(8,128)(2,1)S(1)}, bf16[4,256,128]{2,1,0:T(8,128)(2,1)S(1)}, u32[]{:S(2)}, u32[]{:S(2)}) collective-permute-start(bf16[4,256,128]{2,1,0:T(8,128)(2,1)S(1)} %get-tuple-element.61), channel_id=1, source_target_pairs={{0,4},{4,0},{8,12},{12,8},{16,20},{20,16},{24,28},{28,24},{1,5},{5... | collective-permute-start | bytes 786440 | tf_op jit(solution)/shard_map/ppermute | solution.py:458
  56.2 12.1 %collective-permute-start.9 = (bf16[4,256,128]{2,1,0:T(8,128)(2,1)S(1)}, bf16[4,256,128]{2,1,0:T(8,128)(2,1)S(1)}, u32[]{:S(2)}, u32[]{:S(2)}) collective-permute-start(bf16[4,256,128]{2,1,0:T(8,128)(2,1)S(1)} %get-tuple-element.62), channel_id=1, source_target_pairs={{0,8},{4,12},{8,0},{12,4},{16,24},{20,28},{24,16},{28,20},{1,9},{5... | collective-permute-start | bytes 786440 | tf_op jit(solution)/shard_map/ppermute | solution.py:458
  71.0 3.0 %collective-permute-start.12 = (bf16[2,2,256,512]{3,2,1,0:T(8,128)(2,1)S(1)}, bf16[2,2,256,512]{3,2,1,0:T(8,128)(2,1)S(1)}, u32[]{:S(2)}, u32[]{:S(2)}) collective-permute-start(bf16[2,2,256,512]{3,2,1,0:T(8,128)(2,1)S(1)} %get-tuple-element.69), channel_id=1, source_target_pairs={{0,1},{1,0},{2,3},{3,2},{4,5},{5,4},{6,7},{7,6},{8,9},{9,8},{10,11... | collective-permute-start | bytes 3145736 | tf_op jit(solution)/shard_map/ppermute | solution.py:539
  71.0 7.3 %collective-permute-start.11 = (bf16[2,2,256,512]{3,2,1,0:T(8,128)(2,1)S(1)}, bf16[2,2,256,512]{3,2,1,0:T(8,128)(2,1)S(1)}, u32[]{:S(2)}, u32[]{:S(2)}) collective-permute-start(bf16[2,2,256,512]{3,2,1,0:T(8,128)(2,1)S(1)} %get-tuple-element.66), channel_id=1, source_target_pairs={{0,1},{1,0},{2,3},{3,2},{4,5},{5,4},{6,7},{7,6},{8,9},{9,8},{10,11... | collective-permute-start | bytes 3145736 | tf_op jit(solution)/shard_map/ppermute | solution.py:540
  74.0 4.4 %copy-start.4 = (f32[2,256,512]{2,1,0:T(8,128)}, f32[2,256,512]{2,1,0:T(8,128)S(1)}, u32[]{:S(2)}) copy-start(f32[2,256,512]{2,1,0:T(8,128)S(1)} %get-tuple-element.65) | copy-start | bytes 3145732
  74.1 16.4 %collective-permute-start.13 = (bf16[2,2,256,128]{3,2,1,0:T(8,128)(2,1)S(1)}, bf16[2,2,256,128]{3,2,1,0:T(8,128)(2,1)S(1)}, u32[]{:S(2)}, u32[]{:S(2)}) collective-permute-start(bf16[2,2,256,128]{3,2,1,0:T(8,128)(2,1)S(1)} %z_first_kernel.1), channel_id=1, source_target_pairs={{0,16},{4,20},{8,24},{20,4},{24,8},{28,12},{1,17},{5,21},{9,25},{2... | collective-permute-start | bytes 786440 | tf_op jit(solution)/shard_map/ppermute | solution.py:458
  76.9 16.1 %collective-permute-start.15 = (bf16[2,256,384]{2,1,0:T(8,128)(2,1)}, bf16[2,256,384]{2,1,0:T(8,128)(2,1)}, u32[]{:S(2)}, u32[]{:S(2)}) collective-permute-start(bf16[2,256,384]{2,1,0:T(8,128)(2,1)} %x_first_kernel.1), channel_id=1, source_target_pairs={{0,2},{2,0},{1,3},{3,1},{4,6},{6,4},{5,7},{7,5},{8,10},{10,8},{9,1... | collective-permute-start | bytes 1179656 | tf_op jit(solution)/shard_map/ppermute | solution.py:559
  91.5 14.2 %collective-permute-start.14 = (bf16[2,256,512]{2,1,0:T(8,128)(2,1)}, bf16[2,256,512]{2,1,0:T(8,128)(2,1)}, u32[]{:S(2)}, u32[]{:S(2)}) collective-permute-start(bf16[2,256,512]{2,1,0:T(8,128)(2,1)} %x_second_kernel.1), channel_id=1, source_target_pairs={{0,2},{2,0},{1,3},{3,1},{4,6},{6,4},{5,7},{7,5},{8,10},{10,8},{9,1... | collective-permute-start | bytes 1572872 | tf_op jit(solution)/shard_map/ppermute | solution.py:563
  94.1 15.8 %collective-permute-start.16 = (bf16[2,256,384]{2,1,0:T(8,128)(2,1)S(1)}, bf16[2,256,384]{2,1,0:T(8,128)(2,1)S(1)}, u32[]{:S(2)}, u32[]{:S(2)}) collective-permute-start(bf16[2,256,384]{2,1,0:T(8,128)(2,1)S(1)} %z_second_kernel.1), channel_id=1, source_target_pairs={{0,16},{4,20},{8,24},{20,4},{24,8},{28,12},{1,17},{5,21},{9,25},{2... | collective-permute-start | bytes 1179656 | tf_op jit(solution)/shard_map/ppermute | solution.py:458

commit v22 on v20

--- a/solution.py
+++ b/solution.py
@@ -468,9 +468,8 @@
     got_b = permute(first_b, [(s, s ^ 7) for s in INNER] + handed)
     near_2 = permute(near_2, [(s, s ^ 2) for s in windowed])
     second_a, second_b, near_0, near_1, near_3 = rows_call(slice(3, SLABS), "rows_round_2")
-    got_a, near_2, second_a, second_b, near_1, near_3, images = lax.optimization_barrier(
-        (got_a, near_2, second_a, second_b, near_1, near_3, images)
-    )
+    got_a, second_a, near_3, images = lax.optimization_barrier((got_a, second_a, near_3, images))
+    _, near_2, second_b, near_1 = lax.optimization_barrier((got_a, near_2, second_b, near_1))
     outer_pairs = [(s, s ^ 6) for s in range(SLABS) if s not in INNER]
     near_1 = permute(near_1, [(s, s ^ 1) for s in windowed])
     near_3 = permute(near_3, [(s, s ^ 3) for s in windowed])

time: 111 us -> 111 us (level)
  starting transfers between devices: 30.5 us -> 40.5 us
  waiting for transfers between devices: 52 us -> 42.5 us
    ppermute x13, starting transfers between devices: 26.9 us -> 37 us  [permute(): return lax.ppermute(sent, 'slab', pairs)]
    ppermute x13, waiting for transfers between devices: 44.3 us -> 34.7 us  [permute(): return lax.ppermute(sent, 'slab', pairs)]
  transfers between devices with their start and end apart: 17 -> 17, of which waited for: 9 -> 8; matrix products, arithmetic and copies ran while one was open for 3% -> 3% of each run, Pallas kernels for 8% -> 8%
where the time goes in v22:
time: 111 us
  waiting for transfers between devices  42.5 us (38%)
  starting transfers between devices  40.5 us (36%)
  Pallas kernels  20 us (18%)
  other arithmetic  5.06 us (5%)
  local copies, waits for them, and re-layouts  2.42 us (2%)
    ppermute x13, starting transfers between devices, permute(): return lax.ppermute(sent, 'slab', pairs)  37 us
    ppermute x13, waiting for transfers between devices, permute(): return lax.ppermute(sent, 'slab', pairs)  34.7 us
    ppermute x2, waiting for transfers between devices, body_slabs(): got_x = lax.ppermute(over, 'led', planes)  7.79 us
    pallas_call x1, Pallas kernels, body_slabs(): local_call(field_kernel, [sent_block] * HALF, [vmem] * 11, [pltpu.VMEM((w...  5.3 us
    pallas_call x2, Pallas kernels, rows_call(): local_call(functools.partial(rows_kernel, which), [sent_block] * count, [...  4.69 us
    pallas_call x4, Pallas kernels, sum_call(): local_call(kernel, out_shape, specs, [], 0, 2 ** 20, kernel.__name__)  3 us
    ppermute x2, starting transfers between devices, body_slabs(): got_x = lax.ppermute(over, 'led', planes)  2.96 us
    pallas_call x1, Pallas kernels, body_slabs(): local_call(sent_kernel, [jax.ShapeDtypeStruct((2,) + piece, bf16), jax.Sh...  2.65 us
  transfers between devices with their start and end apart: 17, of which 8 were waited for; matrix products, arithmetic and copies ran while one was open for 3% of the time, Pallas kernels for 8%

profile of v22, /device:TPU:4, one launch (start us, length us, event | category | flops | bytes accessed | tf_op | source)
XLA Modules:
  0.0 110.8 jit_solution(7164129058901672367)
XLA Ops:
  0.0 0.9 pad_add_fusion.starts
  0.9 2.4 %copy-done.1 = f32[2,256,2048]{2,1,0:T(8,128)S(1)} copy-done((f32[2,256,2048]{2,1,0:T(8,128)S(1)}, f32[2,256,2048]{2,1,0:T(8,128)}, u32[]{:S(2)}) %copy-start.1) | copy-done | bytes 4194328
  3.3 1.4 %windows.1.window = bf16[1024,1024]{1,0:T(8,128)(2,1)S(1)} custom-call(s32[4]{0:T(128)S(1)} %pad_add_fusion.starts, f32[2,256,2048]{2,1,0:T(8,128)S(1)} %copy-done.1), custom_call_target="tpu_custom_call" | custom-call | bytes 6291456 | tf_op jit(solution)/shard_map/windows/pallas_call | solution.py:433
  4.7 1.8 %rows_round_1.1 = (bf16[4,256,128]{2,1,0:T(8,128)(2,1)S(1)}, bf16[4,256,128]{2,1,0:T(8,128)(2,1)S(1)}, bf16[4,256,128]{2,1,0:T(8,128)(2,1)S(1)}) custom-call(bf16[1024,1024]{1,0:T(8,128)(2,1)S(1)} %windows.1.window, bf16[8,1024,256]{2,1,0:T(8,128)(2,1)S(1)} %copy-done), custom_call_target="tpu_custom_call" | custom-call | flops 1610612736 | bytes 5242880 | tf_op jit(solution)/shard_map/rows_round_1/pallas_call | solution.py:445
  6.5 1.3 %collective-permute-start = (bf16[4,256,128]{2,1,0:T(8,128)(2,1)S(1)}, bf16[4,256,128]{2,1,0:T(8,128)(2,1)S(1)}, u32[]{:S(2)}, u32[]{:S(2)}) collective-permute-start(bf16[4,256,128]{2,1,0:T(8,128)(2,1)S(1)} %get-tuple-element.39), channel_id=1, source_target_pairs={{8,16},{12,20},{16,8},{20,12},{4,0},{24,28},{9,17},{13,21},{17,9},... | collective-permute-start | bytes 786440 | tf_op jit(solution)/shard_map/ppermute | solution.py:458
  7.8 5.7 %collective-permute-start.4 = (bf16[4,256,128]{2,1,0:T(8,128)(2,1)S(1)}, bf16[4,256,128]{2,1,0:T(8,128)(2,1)S(1)}, u32[]{:S(2)}, u32[]{:S(2)}) collective-permute-start(bf16[4,256,128]{2,1,0:T(8,128)(2,1)S(1)} %get-tuple-element.50), channel_id=1, source_target_pairs={{4,12},{8,0},{12,4},{16,24},{20,28},{24,16},{5,13},{9,1},{13,5},{1... | collective-permute-start | bytes 786440 | tf_op jit(solution)/shard_map/ppermute | solution.py:458
  13.5 0.0 copy-start.2
  13.5 0.0 copy-start.3
  13.5 1.6 %collective-permute-start.2 = (bf16[4,256,128]{2,1,0:T(8,128)(2,1)S(1)}, bf16[4,256,128]{2,1,0:T(8,128)(2,1)S(1)}, u32[]{:S(2)}, u32[]{:S(2)}) collective-permute-start(bf16[4,256,128]{2,1,0:T(8,128)(2,1)S(1)} %get-tuple-element.47), channel_id=1, source_target_pairs={{8,20},{12,16},{16,12},{20,8},{4,0},{24,28},{9,21},{13,17},{17,13}... | collective-permute-start | bytes 786440 | tf_op jit(solution)/shard_map/ppermute | solution.py:458
  15.1 2.9 %rows_round_2.1 = (bf16[4,256,128]{2,1,0:T(8,128)(2,1)S(1)}, bf16[4,256,128]{2,1,0:T(8,128)(2,1)S(1)}, bf16[4,256,128]{2,1,0:T(8,128)(2,1)S(1)}, bf16[4,256,128]...) custom-call(bf16[1024,1024]{1,0:T(8,128)(2,1)S(1)} %windows.1.window, bf16[8,1024,256]{2,1,0:T(8,128)(2,1)S(1)} %copy-done), custom_call_target="tpu_custom_call" | custom-call | flops 2684354560 | bytes 5242880 | tf_op jit(solution)/shard_map/rows_round_2/pallas_call | solution.py:445
  18.0 0.0 collective-permute-done.got.rest_0_
  18.0 4.4 %collective-permute-start.1 = (bf16[4,256,128]{2,1,0:T(8,128)(2,1)S(1)}, bf16[4,256,128]{2,1,0:T(8,128)(2,1)S(1)}, u32[]{:S(2)}, u32[]{:S(2)}) collective-permute-start(bf16[4,256,128]{2,1,0:T(8,128)(2,1)S(1)} %get-tuple-element.46), channel_id=1, source_target_pairs={{4,8},{8,4},{12,0},{16,28},{20,24},{24,20},{5,9},{9,5},{13,1},{17,... | collective-permute-start | bytes 786440 | tf_op jit(solution)/shard_map/ppermute | solution.py:458
  22.4 0.0 collective-permute-done.4.rest_7_
  22.4 1.3 %collective-permute-start.6 = (bf16[4,256,128]{2,1,0:T(8,128)(2,1)S(1)}, bf16[4,256,128]{2,1,0:T(8,128)(2,1)S(1)}, u32[]{:S(2)}, u32[]{:S(2)}) collective-permute-start(bf16[4,256,128]{2,1,0:T(8,128)(2,1)S(1)} %get-tuple-element.53.own), channel_id=1, source_target_pairs={{8,28},{12,24},{16,4},{20,0},{9,29},{13,25},{17,5},{21,1},{10,30},... | collective-permute-start | bytes 786440 | tf_op jit(solution)/shard_map/ppermute | solution.py:458
  23.7 0.3 collective-permute-start.3
  24.0 6.6 %collective-permute-start.7 = (bf16[4,256,128]{2,1,0:T(8,128)(2,1)S(1)}, bf16[4,256,128]{2,1,0:T(8,128)(2,1)S(1)}, u32[]{:S(2)}, u32[]{:S(2)}) collective-permute-start(bf16[4,256,128]{2,1,0:T(8,128)(2,1)S(1)} %get-tuple-element.55), channel_id=1, source_target_pairs={{4,0},{8,12},{12,8},{16,20},{20,16},{24,28},{5,1},{9,13},{13,9},{1... | collective-permute-start | bytes 786440 | tf_op jit(solution)/shard_map/ppermute | solution.py:458
  30.7 0.0 collective-permute-done.2.got.rest_1_
  30.8 6.1 %collective-permute-start.5 = (bf16[4,256,128]{2,1,0:T(8,128)(2,1)S(1)}, bf16[4,256,128]{2,1,0:T(8,128)(2,1)S(1)}, u32[]{:S(2)}, u32[]{:S(2)}) collective-permute-start(bf16[4,256,128]{2,1,0:T(8,128)(2,1)S(1)} %class_6_blocks.1), channel_id=1, source_target_pairs={{0,24},{4,28},{24,0},{28,4},{1,25},{5,29},{25,1},{29,5},{2,26},{6,... | collective-permute-start | bytes 786440 | tf_op jit(solution)/shard_map/ppermute | solution.py:458
  36.9 0.6 amplitude.1
  37.4 8.5 %collective-permute-done.6.rest_4_ = bf16[4,256,128]{2,1,0:T(8,128)(2,1)S(1)} collective-permute-done((bf16[4,256,128]{2,1,0:T(8,128)(2,1)S(1)}, bf16[4,256,128]{2,1,0:T(8,128)(2,1)S(1)}, u32[]{:S(2)}, u32[]{:S(2)}) %collective-permute-start.6) | collective-permute-done | bytes 262176 | tf_op jit(solution)/shard_map/ppermute | solution.py:458
  45.9 0.4 collective-permute-done.3.rest_2_
  46.3 0.0 collective-permute-done.7.rest_6_
  46.3 5.3 %modulus_step.1 = (bf16[4,256,128]{2,1,0:T(8,128)(2,1)S(1)}, bf16[4,256,128]{2,1,0:T(8,128)(2,1)S(1)}, bf16[4,256,128]{2,1,0:T(8,128)(2,1)S(1)}, bf16[4,256,128]{2,1,0:T(8,128)(2,1)S(1)}) custom-call(f32[1024,256]{1,0:T(8,128)S(1)} %get-tuple-element.43.amplitude, bf16[8,256,1024]{2,1,0:T(8,128)(2,1)S(1)} %get-tuple-element.44.table, ...), custom_call_target="tpu_custom_call" | custom-call | flops 4294967296 | bytes 12582912 | tf_op jit(solution)/shard_map/modulus_step/pallas_call | solution.py:497
  51.6 0.1 collective-permute-start.10
  51.7 4.4 %collective-permute-start.8 = (bf16[4,256,128]{2,1,0:T(8,128)(2,1)S(1)}, bf16[4,256,128]{2,1,0:T(8,128)(2,1)S(1)}, u32[]{:S(2)}, u32[]{:S(2)}) collective-permute-start(bf16[4,256,128]{2,1,0:T(8,128)(2,1)S(1)} %get-tuple-element.59), channel_id=1, source_target_pairs={{0,4},{4,0},{8,12},{12,8},{16,20},{20,16},{24,28},{28,24},{1,5},{5... | collective-permute-start | bytes 786440 | tf_op jit(solution)/shard_map/ppermute | solution.py:458
  56.1 1.4 %collective-permute-start.9 = (bf16[4,256,128]{2,1,0:T(8,128)(2,1)S(1)}, bf16[4,256,128]{2,1,0:T(8,128)(2,1)S(1)}, u32[]{:S(2)}, u32[]{:S(2)}) collective-permute-start(bf16[4,256,128]{2,1,0:T(8,128)(2,1)S(1)} %get-tuple-element.60), channel_id=1, source_target_pairs={{0,8},{4,12},{8,0},{12,4},{16,24},{20,28},{24,16},{28,20},{1,9},{5... | collective-permute-start | bytes 786440 | tf_op jit(solution)/shard_map/ppermute | solution.py:458
  57.5 3.0 %collective-permute-done.10.rest_3_ = bf16[4,256,128]{2,1,0:T(8,128)(2,1)S(1)} collective-permute-done((bf16[4,256,128]{2,1,0:T(8,128)(2,1)S(1)}, bf16[4,256,128]{2,1,0:T(8,128)(2,1)S(1)}, u32[]{:S(2)}, u32[]{:S(2)}) %collective-permute-start.10) | collective-permute-done | bytes 262176 | tf_op jit(solution)/shard_map/ppermute | solution.py:458
  60.5 5.7 %collective-permute-done.8.rest_1_ = bf16[4,256,128]{2,1,0:T(8,128)(2,1)S(1)} collective-permute-done((bf16[4,256,128]{2,1,0:T(8,128)(2,1)S(1)}, bf16[4,256,128]{2,1,0:T(8,128)(2,1)S(1)}, u32[]{:S(2)}, u32[]{:S(2)}) %collective-permute-start.8) | collective-permute-done | bytes 262176 | tf_op jit(solution)/shard_map/ppermute | solution.py:458
  66.2 1.9 %collective-permute-done.9.rest_2_ = bf16[4,256,128]{2,1,0:T(8,128)(2,1)S(1)} collective-permute-done((bf16[4,256,128]{2,1,0:T(8,128)(2,1)S(1)}, bf16[4,256,128]{2,1,0:T(8,128)(2,1)S(1)}, u32[]{:S(2)}, u32[]{:S(2)}) %collective-permute-start.9) | collective-permute-done | bytes 262176 | tf_op jit(solution)/shard_map/ppermute | solution.py:458
  68.1 2.6 %update_sent.1 = (bf16[2,2,256,512]{3,2,1,0:T(8,128)(2,1)S(1)}, bf16[2,2,256,512]{3,2,1,0:T(8,128)(2,1)S(1)}, bf16[1024,512]{1,0:T(8,128)(2,1)S(1)}) custom-call(s32[4]{0:T(128)S(1)} %pad_add_fusion.starts, bf16[8,1024,256]{2,1,0:T(8,128)(2,1)S(1)} %copy-done, bf16[4,256,128]{2,1,0:T(8,128)(2,1)S(1)} %get-tuple-element.58.rest_0_, ...), custom_call_target="tpu_custom_call" | custom-call | flops 1073741824 | bytes 8388608 | tf_op jit(solution)/shard_map/update_sent/pallas_call | solution.py:522
  70.8 0.1 collective-permute-start.12
  70.8 0.5 collective-permute-start.11
  71.3 2.4 %update_kept.1 = (f32[2,256,512]{2,1,0:T(8,128)S(1)}, f32[2,256,512]{2,1,0:T(8,128)S(1)}, f32[2,256,512]{2,1,0:T(8,128)S(1)}, f32[2,256,512]{2,1,0:T(8,128)S(1)}) custom-call(s32[4]{0:T(128)S(1)} %pad_add_fusion.starts, bf16[8,1024,256]{2,1,0:T(8,128)(2,1)S(1)} %copy-done, bf16[1024,512]{1,0:T(8,128)(2,1)S(1)} %get-tuple-element.62.back), custom_call_target="tpu_custom_call" | custom-call | flops 1073741824 | bytes 10485760 | tf_op jit(solution)/shard_map/update_kept/pallas_call | solution.py:537
  73.8 0.0 copy-start.4
  73.8 0.1 z_first_kernel.1
  73.9 1.9 %collective-permute-start.13 = (bf16[2,2,256,128]{3,2,1,0:T(8,128)(2,1)S(1)}, bf16[2,2,256,128]{3,2,1,0:T(8,128)(2,1)S(1)}, u32[]{:S(2)}, u32[]{:S(2)}) collective-permute-start(bf16[2,2,256,128]{3,2,1,0:T(8,128)(2,1)S(1)} %z_first_kernel.1), channel_id=1, source_target_pairs={{0,16},{4,20},{8,24},{20,4},{24,8},{28,12},{1,17},{5,21},{9,25},{2... | collective-permute-start | bytes 786440 | tf_op jit(solution)/shard_map/ppermute | solution.py:458
  75.8 0.8 x_first_kernel.1
  76.7 1.5 %collective-permute-start.15 = (bf16[2,256,384]{2,1,0:T(8,128)(2,1)}, bf16[2,256,384]{2,1,0:T(8,128)(2,1)}, u32[]{:S(2)}, u32[]{:S(2)}) collective-permute-start(bf16[2,256,384]{2,1,0:T(8,128)(2,1)} %x_first_kernel.1), channel_id=1, source_target_pairs={{0,2},{2,0},{1,3},{3,1},{4,6},{6,4},{5,7},{7,5},{8,10},{10,8},{9,1... | collective-permute-start | bytes 1179656 | tf_op jit(solution)/shard_map/ppermute | solution.py:555
  78.1 12.1 %collective-permute-done.13.got_z = bf16[2,2,256,128]{3,2,1,0:T(8,128)(2,1)S(1)} collective-permute-done((bf16[2,2,256,128]{3,2,1,0:T(8,128)(2,1)S(1)}, bf16[2,2,256,128]{3,2,1,0:T(8,128)(2,1)S(1)}, u32[]{:S(2)}, u32[]{:S(2)}) %collective-permute-start.13) | collective-permute-done | bytes 262176 | tf_op jit(solution)/shard_map/ppermute | solution.py:458
  90.3 1.0 x_second_kernel.1
  91.2 1.5 %collective-permute-start.14 = (bf16[2,256,512]{2,1,0:T(8,128)(2,1)}, bf16[2,256,512]{2,1,0:T(8,128)(2,1)}, u32[]{:S(2)}, u32[]{:S(2)}) collective-permute-start(bf16[2,256,512]{2,1,0:T(8,128)(2,1)} %x_second_kernel.1), channel_id=1, source_target_pairs={{0,2},{2,0},{1,3},{3,1},{4,6},{6,4},{5,7},{7,5},{8,10},{10,8},{9,1... | collective-permute-start | bytes 1572872 | tf_op jit(solution)/shard_map/ppermute | solution.py:559
  92.8 1.1 %z_second_kernel.1 = bf16[2,256,384]{2,1,0:T(8,128)(2,1)S(1)} custom-call(f32[2,256,512]{2,1,0:T(8,128)S(1)} %get-tuple-element.65.that_near, bf16[2,2,256,512]{3,2,1,0:T(8,128)(2,1)S(1)} %collective-permute-done.12.got_that, bf16[2,256,384]{2,1,0:T(8,128)(2,1)} %collective-permute-done.15.got_x), custom_call_target="tpu_custom_call" | custom-call | bytes 1048576 | tf_op jit(solution)/shard_map/z_second_kernel/pallas_call | solution.py:550
  93.9 1.9 %collective-permute-start.16 = (bf16[2,256,384]{2,1,0:T(8,128)(2,1)S(1)}, bf16[2,256,384]{2,1,0:T(8,128)(2,1)S(1)}, u32[]{:S(2)}, u32[]{:S(2)}) collective-permute-start(bf16[2,256,384]{2,1,0:T(8,128)(2,1)S(1)} %z_second_kernel.1), channel_id=1, source_target_pairs={{0,16},{4,20},{8,24},{20,4},{24,8},{28,12},{1,17},{5,21},{9,25},{2... | collective-permute-start | bytes 1179656 | tf_op jit(solution)/shard_map/ppermute | solution.py:458
  95.8 1.8 %fusion.1 = f32[2,256,512]{2,1,0:T(8,128)S(1)} fusion(f32[2,256,512]{2,1,0:T(8,128)} %copy-done.4, f32[2,256,2048]{2,1,0:T(8,128)} %spectrum.1, s32[]{:T(128)S(6)} %select_n.3, bf16[2,2,256,512]{3,2,1,0:T(8,128)(2,1)S(1)} %collective-permute-done.11.got_this, bf16[2,256,128]{2,1,0:T(8,128)(2,1)S(1)} %slice_bitcast_fusion.1), kind=kLoop, calls=%fused_computation.2 | loop fusion | flops 1310720 | bytes 3801092 | tf_op jit(solution)/shard_map/add | solution.py:566
  97.6 7.8 %collective-permute-done.14 = bf16[2,256,512]{2,1,0:T(8,128)(2,1)} collective-permute-done((bf16[2,256,512]{2,1,0:T(8,128)(2,1)}, bf16[2,256,512]{2,1,0:T(8,128)(2,1)}, u32[]{:S(2)}, u32[]{:S(2)}) %collective-permute-start.14) | collective-permute-done | bytes 524320 | tf_op jit(solution)/shard_map/ppermute | solution.py:559
  105.4 1.2 %convert_add_fusion.2 = f32[2,256,512]{2,1,0:T(8,128)S(1)} fusion(f32[2,256,512]{2,1,0:T(8,128)S(1)} %fusion.1, bf16[2,256,512]{2,1,0:T(8,128)(2,1)} %collective-permute-done.14), kind=kLoop, calls=%fused_computation.4 | loop fusion | flops 524288 | bytes 2621440 | tf_op jit(solution)/shard_map/add | solution.py:568
  106.6 3.1 %collective-permute-done.16 = bf16[2,256,384]{2,1,0:T(8,128)(2,1)S(1)} collective-permute-done((bf16[2,256,384]{2,1,0:T(8,128)(2,1)S(1)}, bf16[2,256,384]{2,1,0:T(8,128)(2,1)S(1)}, u32[]{:S(2)}, u32[]{:S(2)}) %collective-permute-start.16) | collective-permute-done | bytes 393248 | tf_op jit(solution)/shard_map/ppermute | solution.py:458
  109.7 1.1 %convert_add_fusion.1 = f32[2,256,512]{2,1,0:T(8,128)} fusion(f32[2,256,512]{2,1,0:T(8,128)S(1)} %convert_add_fusion.2, bf16[2,256,384]{2,1,0:T(8,128)(2,1)S(1)} %collective-permute-done.16), kind=kLoop, calls=%fused_computation.3 | loop fusion | flops 524288 | bytes 2490368 | tf_op jit(solution)/shard_map/add | solution.py:570
  (14 shorter events, 0.1 us)
Async XLA Ops:
  0.0 4.6 %copy-start = (bf16[8,1024,256]{2,1,0:T(8,128)(2,1)S(1)}, bf16[8,1024,256]{2,1,0:T(8,128)(2,1)}, u32[]{:S(2)}) copy-start(bf16[8,1024,256]{2,1,0:T(8,128)(2,1)} %constant.18.clone.table) | copy-start | bytes 12582916
  0.9 2.4 %copy-start.1 = (f32[2,256,2048]{2,1,0:T(8,128)S(1)}, f32[2,256,2048]{2,1,0:T(8,128)}, u32[]{:S(2)}) copy-start(f32[2,256,2048]{2,1,0:T(8,128)} %spectrum.1) | copy-start | bytes 12582916
  6.5 11.5 %collective-permute-start = (bf16[4,256,128]{2,1,0:T(8,128)(2,1)S(1)}, bf16[4,256,128]{2,1,0:T(8,128)(2,1)S(1)}, u32[]{:S(2)}, u32[]{:S(2)}) collective-permute-start(bf16[4,256,128]{2,1,0:T(8,128)(2,1)S(1)} %get-tuple-element.39), channel_id=1, source_target_pairs={{8,16},{12,20},{16,8},{20,12},{4,0},{24,28},{9,17},{13,21},{17,9},... | collective-permute-start | bytes 786440 | tf_op jit(solution)/shard_map/ppermute | solution.py:458
  7.8 14.6 %collective-permute-start.4 = (bf16[4,256,128]{2,1,0:T(8,128)(2,1)S(1)}, bf16[4,256,128]{2,1,0:T(8,128)(2,1)S(1)}, u32[]{:S(2)}, u32[]{:S(2)}) collective-permute-start(bf16[4,256,128]{2,1,0:T(8,128)(2,1)S(1)} %get-tuple-element.50), channel_id=1, source_target_pairs={{4,12},{8,0},{12,4},{16,24},{20,28},{24,16},{5,13},{9,1},{13,5},{1... | collective-permute-start | bytes 786440 | tf_op jit(solution)/shard_map/ppermute | solution.py:458
  13.5 23.4 %copy-start.2 = (bf16[8,256,1024]{2,1,0:T(8,128)(2,1)S(1)}, bf16[8,256,1024]{2,1,0:T(8,128)(2,1)}, u32[]{:S(2)}) copy-start(bf16[8,256,1024]{2,1,0:T(8,128)(2,1)} %constant.17.clone.table) | copy-start | bytes 12582916
  13.5 23.4 %copy-start.3 = (f32[2,128,1024]{2,1,0:T(8,128)S(1)}, f32[2,128,1024]{2,1,0:T(8,128)}, u32[]{:S(2)}) copy-start(f32[2,128,1024]{2,1,0:T(8,128)} %images) | copy-start | bytes 3145732
  13.5 17.2 %collective-permute-start.2 = (bf16[4,256,128]{2,1,0:T(8,128)(2,1)S(1)}, bf16[4,256,128]{2,1,0:T(8,128)(2,1)S(1)}, u32[]{:S(2)}, u32[]{:S(2)}) collective-permute-start(bf16[4,256,128]{2,1,0:T(8,128)(2,1)S(1)} %get-tuple-element.47), channel_id=1, source_target_pairs={{8,20},{12,16},{16,12},{20,8},{4,0},{24,28},{9,21},{13,17},{17,13}... | collective-permute-start | bytes 786440 | tf_op jit(solution)/shard_map/ppermute | solution.py:458
  18.0 12.8 %collective-permute-start.1 = (bf16[4,256,128]{2,1,0:T(8,128)(2,1)S(1)}, bf16[4,256,128]{2,1,0:T(8,128)(2,1)S(1)}, u32[]{:S(2)}, u32[]{:S(2)}) collective-permute-start(bf16[4,256,128]{2,1,0:T(8,128)(2,1)S(1)} %get-tuple-element.46), channel_id=1, source_target_pairs={{4,8},{8,4},{12,0},{16,28},{20,24},{24,20},{5,9},{9,5},{13,1},{17,... | collective-permute-start | bytes 786440 | tf_op jit(solution)/shard_map/ppermute | solution.py:458
  22.4 23.5 %collective-permute-start.6 = (bf16[4,256,128]{2,1,0:T(8,128)(2,1)S(1)}, bf16[4,256,128]{2,1,0:T(8,128)(2,1)S(1)}, u32[]{:S(2)}, u32[]{:S(2)}) collective-permute-start(bf16[4,256,128]{2,1,0:T(8,128)(2,1)S(1)} %get-tuple-element.53.own), channel_id=1, source_target_pairs={{8,28},{12,24},{16,4},{20,0},{9,29},{13,25},{17,5},{21,1},{10,30},... | collective-permute-start | bytes 786440 | tf_op jit(solution)/shard_map/ppermute | solution.py:458
  23.7 22.6 %collective-permute-start.3 = (bf16[4,256,128]{2,1,0:T(8,128)(2,1)S(1)}, bf16[4,256,128]{2,1,0:T(8,128)(2,1)S(1)}, u32[]{:S(2)}, u32[]{:S(2)}) collective-permute-start(bf16[4,256,128]{2,1,0:T(8,128)(2,1)S(1)} %class_4_blocks.1), channel_id=1, source_target_pairs={{0,16},{4,20},{8,24},{12,28},{16,0},{20,4},{24,8},{28,12},{1,17},{... | collective-permute-start | bytes 786440 | tf_op jit(solution)/shard_map/ppermute | solution.py:458
  24.0 22.3 %collective-permute-start.7 = (bf16[4,256,128]{2,1,0:T(8,128)(2,1)S(1)}, bf16[4,256,128]{2,1,0:T(8,128)(2,1)S(1)}, u32[]{:S(2)}, u32[]{:S(2)}) collective-permute-start(bf16[4,256,128]{2,1,0:T(8,128)(2,1)S(1)} %get-tuple-element.55), channel_id=1, source_target_pairs={{4,0},{8,12},{12,8},{16,20},{20,16},{24,28},{5,1},{9,13},{13,9},{1... | collective-permute-start | bytes 786440 | tf_op jit(solution)/shard_map/ppermute | solution.py:458
  30.8 15.5 %collective-permute-start.5 = (bf16[4,256,128]{2,1,0:T(8,128)(2,1)S(1)}, bf16[4,256,128]{2,1,0:T(8,128)(2,1)S(1)}, u32[]{:S(2)}, u32[]{:S(2)}) collective-permute-start(bf16[4,256,128]{2,1,0:T(8,128)(2,1)S(1)} %class_6_blocks.1), channel_id=1, source_target_pairs={{0,24},{4,28},{24,0},{28,4},{1,25},{5,29},{25,1},{29,5},{2,26},{6,... | collective-permute-start | bytes 786440 | tf_op jit(solution)/shard_map/ppermute | solution.py:458
  51.6 8.9 %collective-permute-start.10 = (bf16[4,256,128]{2,1,0:T(8,128)(2,1)S(1)}, bf16[4,256,128]{2,1,0:T(8,128)(2,1)S(1)}, u32[]{:S(2)}, u32[]{:S(2)}) collective-permute-start(bf16[4,256,128]{2,1,0:T(8,128)(2,1)S(1)} %get-tuple-element.61), channel_id=1, source_target_pairs={{0,12},{4,8},{8,4},{12,0},{16,28},{20,24},{24,20},{28,16},{1,13},{... | collective-permute-start | bytes 786440 | tf_op jit(solution)/shard_map/ppermute | solution.py:458
  51.7 14.5 %collective-permute-start.8 = (bf16[4,256,128]{2,1,0:T(8,128)(2,1)S(1)}, bf16[4,256,128]{2,1,0:T(8,128)(2,1)S(1)}, u32[]{:S(2)}, u32[]{:S(2)}) collective-permute-start(bf16[4,256,128]{2,1,0:T(8,128)(2,1)S(1)} %get-tuple-element.59), channel_id=1, source_target_pairs={{0,4},{4,0},{8,12},{12,8},{16,20},{20,16},{24,28},{28,24},{1,5},{5... | collective-permute-start | bytes 786440 | tf_op jit(solution)/shard_map/ppermute | solution.py:458
  56.1 12.0 %collective-permute-start.9 = (bf16[4,256,128]{2,1,0:T(8,128)(2,1)S(1)}, bf16[4,256,128]{2,1,0:T(8,128)(2,1)S(1)}, u32[]{:S(2)}, u32[]{:S(2)}) collective-permute-start(bf16[4,256,128]{2,1,0:T(8,128)(2,1)S(1)} %get-tuple-element.60), channel_id=1, source_target_pairs={{0,8},{4,12},{8,0},{12,4},{16,24},{20,28},{24,16},{28,20},{1,9},{5... | collective-permute-start | bytes 786440 | tf_op jit(solution)/shard_map/ppermute | solution.py:458
  70.8 3.0 %collective-permute-start.12 = (bf16[2,2,256,512]{3,2,1,0:T(8,128)(2,1)S(1)}, bf16[2,2,256,512]{3,2,1,0:T(8,128)(2,1)S(1)}, u32[]{:S(2)}, u32[]{:S(2)}) collective-permute-start(bf16[2,2,256,512]{3,2,1,0:T(8,128)(2,1)S(1)} %get-tuple-element.67), channel_id=1, source_target_pairs={{0,1},{1,0},{2,3},{3,2},{4,5},{5,4},{6,7},{7,6},{8,9},{9,8},{10,11... | collective-permute-start | bytes 3145736 | tf_op jit(solution)/shard_map/ppermute | solution.py:535
  70.8 7.3 %collective-permute-start.11 = (bf16[2,2,256,512]{3,2,1,0:T(8,128)(2,1)S(1)}, bf16[2,2,256,512]{3,2,1,0:T(8,128)(2,1)S(1)}, u32[]{:S(2)}, u32[]{:S(2)}) collective-permute-start(bf16[2,2,256,512]{3,2,1,0:T(8,128)(2,1)S(1)} %get-tuple-element.64), channel_id=1, source_target_pairs={{0,1},{1,0},{2,3},{3,2},{4,5},{5,4},{6,7},{7,6},{8,9},{9,8},{10,11... | collective-permute-start | bytes 3145736 | tf_op jit(solution)/shard_map/ppermute | solution.py:536
  73.8 4.4 %copy-start.4 = (f32[2,256,512]{2,1,0:T(8,128)}, f32[2,256,512]{2,1,0:T(8,128)S(1)}, u32[]{:S(2)}) copy-start(f32[2,256,512]{2,1,0:T(8,128)S(1)} %get-tuple-element.63) | copy-start | bytes 3145732
  73.9 16.4 %collective-permute-start.13 = (bf16[2,2,256,128]{3,2,1,0:T(8,128)(2,1)S(1)}, bf16[2,2,256,128]{3,2,1,0:T(8,128)(2,1)S(1)}, u32[]{:S(2)}, u32[]{:S(2)}) collective-permute-start(bf16[2,2,256,128]{3,2,1,0:T(8,128)(2,1)S(1)} %z_first_kernel.1), channel_id=1, source_target_pairs={{0,16},{4,20},{8,24},{20,4},{24,8},{28,12},{1,17},{5,21},{9,25},{2... | collective-permute-start | bytes 786440 | tf_op jit(solution)/shard_map/ppermute | solution.py:458
  76.7 16.1 %collective-permute-start.15 = (bf16[2,256,384]{2,1,0:T(8,128)(2,1)}, bf16[2,256,384]{2,1,0:T(8,128)(2,1)}, u32[]{:S(2)}, u32[]{:S(2)}) collective-permute-start(bf16[2,256,384]{2,1,0:T(8,128)(2,1)} %x_first_kernel.1), channel_id=1, source_target_pairs={{0,2},{2,0},{1,3},{3,1},{4,6},{6,4},{5,7},{7,5},{8,10},{10,8},{9,1... | collective-permute-start | bytes 1179656 | tf_op jit(solution)/shard_map/ppermute | solution.py:555
  91.2 14.2 %collective-permute-start.14 = (bf16[2,256,512]{2,1,0:T(8,128)(2,1)}, bf16[2,256,512]{2,1,0:T(8,128)(2,1)}, u32[]{:S(2)}, u32[]{:S(2)}) collective-permute-start(bf16[2,256,512]{2,1,0:T(8,128)(2,1)} %x_second_kernel.1), channel_id=1, source_target_pairs={{0,2},{2,0},{1,3},{3,1},{4,6},{6,4},{5,7},{7,5},{8,10},{10,8},{9,1... | collective-permute-start | bytes 1572872 | tf_op jit(solution)/shard_map/ppermute | solution.py:559
  93.9 15.8 %collective-permute-start.16 = (bf16[2,256,384]{2,1,0:T(8,128)(2,1)S(1)}, bf16[2,256,384]{2,1,0:T(8,128)(2,1)S(1)}, u32[]{:S(2)}, u32[]{:S(2)}) collective-permute-start(bf16[2,256,384]{2,1,0:T(8,128)(2,1)S(1)} %z_second_kernel.1), channel_id=1, source_target_pairs={{0,16},{4,20},{8,24},{20,4},{24,8},{28,12},{1,17},{5,21},{9,25},{2... | collective-permute-start | bytes 1179656 | tf_op jit(solution)/shard_map/ppermute | solution.py:458

commit v23 on v20

--- a/solution.py
+++ b/solution.py
@@ -373,25 +373,25 @@
 def z_first_kernel(that_near, that_far, got_that, out):
     cols = out.shape[3]
     for i, kept in enumerate((that_near, that_far)):
-        total = kept[:, :, :cols] + got_that[i, :, :, :cols].astype(jnp.float32)
+        total = kept[:, :, :cols].astype(jnp.float32) + got_that[i, :, :, :cols].astype(jnp.float32)
         out[i] = total.astype(out.dtype)
 
 
 def x_first_kernel(that_far, got_that, out):
     cols = that_far.shape[2] - out.shape[2]
-    total = that_far[:, :, cols:] + got_that[1, :, :, cols:].astype(jnp.float32)
+    total = that_far[:, :, cols:].astype(jnp.float32) + got_that[1, :, :, cols:].astype(jnp.float32)
     out[...] = total.astype(out.dtype)
 
 
 def z_second_kernel(that_near, got_that, got_x, out):
     cols = that_near.shape[2] - out.shape[2]
-    total = that_near[:, :, cols:] + got_that[0, :, :, cols:].astype(jnp.float32)
+    total = that_near[:, :, cols:].astype(jnp.float32) + got_that[0, :, :, cols:].astype(jnp.float32)
     out[...] = (total + got_x[...].astype(jnp.float32)).astype(out.dtype)
 
 
 def x_second_kernel(this_far, got_this, got_z, out):
     cols = got_z.shape[3]
-    total = this_far[...] + got_this[1].astype(jnp.float32)
+    total = this_far[...].astype(jnp.float32) + got_this[1].astype(jnp.float32)
     out[:, :, cols:] = total[:, :, cols:].astype(out.dtype)
     out[:, :, :cols] = (total[:, :, :cols] + got_z[1].astype(jnp.float32)).astype(out.dtype)
 
@@ -537,7 +537,7 @@
     got_this = lax.ppermute(sent_this, "led", cores)
     this_near, this_far, that_near, that_far = local_call(
         kept_kernel,
-        [jax.ShapeDtypeStruct(piece, jnp.float32)] * 4,
+        [jax.ShapeDtypeStruct(piece, jnp.float32)] + [jax.ShapeDtypeStruct(piece, bf16)] * 3,
         [smem, vmem, vmem],
         [],
         flops // 4,

time: 111 us -> 111 us (level)
  transfers between devices with their start and end apart: 17 -> 17, of which waited for: 9 -> 9; matrix products, arithmetic and copies ran while one was open for 3% -> 3% of each run, Pallas kernels for 8% -> 7%
where the time goes in v23:
time: 111 us; the launch traced here: 110 us
  waiting for transfers between devices  52.8 us (48%)
  starting transfers between devices  30.5 us (27%)
  Pallas kernels  19.4 us (17%)
  other arithmetic  5.05 us (5%)
  local copies, waits for them, and re-layouts  2.42 us (2%)
    ppermute x13, waiting for transfers between devices, permute(): return lax.ppermute(sent, 'slab', pairs)  45.3 us
    ppermute x13, starting transfers between devices, permute(): return lax.ppermute(sent, 'slab', pairs)  26.9 us
    ppermute x2, waiting for transfers between devices, body_slabs(): got_x = lax.ppermute(over, 'led', planes)  7.54 us
    pallas_call x1, Pallas kernels, body_slabs(): local_call(field_kernel, [sent_block] * HALF, [vmem] * 11, [pltpu.VMEM((w...  5.31 us
    pallas_call x2, Pallas kernels, rows_call(): local_call(functools.partial(rows_kernel, which), [sent_block] * count, [...  4.69 us
    ppermute x2, starting transfers between devices, body_slabs(): got_x = lax.ppermute(over, 'led', planes)  3.07 us
    pallas_call x1, Pallas kernels, body_slabs(): local_call(sent_kernel, [jax.ShapeDtypeStruct((2,) + piece, bf16), jax.Sh...  2.66 us
    pallas_call x1, Pallas kernels, body_slabs(): local_call(kept_kernel, [jax.ShapeDtypeStruct(piece, jnp.float32)] + [jax...  2.57 us
  transfers between devices with their start and end apart: 17, of which 9 were waited for; matrix products, arithmetic and copies ran while one was open for 3% of the time, Pallas kernels for 7%

profile of v23, /device:TPU:4, one launch (start us, length us, event | category | flops | bytes accessed | tf_op | source)
XLA Modules:
  0.0 110.5 jit_solution(10900710342328395137)
XLA Ops:
  0.0 0.9 pad_add_fusion.starts
  0.9 2.4 %copy-done.1 = f32[2,256,2048]{2,1,0:T(8,128)S(1)} copy-done((f32[2,256,2048]{2,1,0:T(8,128)S(1)}, f32[2,256,2048]{2,1,0:T(8,128)}, u32[]{:S(2)}) %copy-start.1) | copy-done | bytes 4194328
  3.3 1.4 %windows.1.window = bf16[1024,1024]{1,0:T(8,128)(2,1)S(1)} custom-call(s32[4]{0:T(128)S(1)} %pad_add_fusion.starts, f32[2,256,2048]{2,1,0:T(8,128)S(1)} %copy-done.1), custom_call_target="tpu_custom_call" | custom-call | bytes 6291456 | tf_op jit(solution)/shard_map/windows/pallas_call | solution.py:433
  4.7 1.8 %rows_round_1.1 = (bf16[4,256,128]{2,1,0:T(8,128)(2,1)S(1)}, bf16[4,256,128]{2,1,0:T(8,128)(2,1)S(1)}, bf16[4,256,128]{2,1,0:T(8,128)(2,1)S(1)}) custom-call(bf16[1024,1024]{1,0:T(8,128)(2,1)S(1)} %windows.1.window, bf16[8,1024,256]{2,1,0:T(8,128)(2,1)S(1)} %copy-done), custom_call_target="tpu_custom_call" | custom-call | flops 1610612736 | bytes 5242880 | tf_op jit(solution)/shard_map/rows_round_1/pallas_call | solution.py:445
  6.5 1.3 %collective-permute-start = (bf16[4,256,128]{2,1,0:T(8,128)(2,1)S(1)}, bf16[4,256,128]{2,1,0:T(8,128)(2,1)S(1)}, u32[]{:S(2)}, u32[]{:S(2)}) collective-permute-start(bf16[4,256,128]{2,1,0:T(8,128)(2,1)S(1)} %get-tuple-element.39), channel_id=1, source_target_pairs={{8,16},{12,20},{16,8},{20,12},{4,0},{24,28},{9,17},{13,21},{17,9},... | collective-permute-start | bytes 786440 | tf_op jit(solution)/shard_map/ppermute | solution.py:458
  7.8 5.7 %collective-permute-start.1 = (bf16[4,256,128]{2,1,0:T(8,128)(2,1)S(1)}, bf16[4,256,128]{2,1,0:T(8,128)(2,1)S(1)}, u32[]{:S(2)}, u32[]{:S(2)}) collective-permute-start(bf16[4,256,128]{2,1,0:T(8,128)(2,1)S(1)} %get-tuple-element.40), channel_id=1, source_target_pairs={{4,12},{8,0},{12,4},{16,24},{20,28},{24,16},{5,13},{9,1},{13,5},{1... | collective-permute-start | bytes 786440 | tf_op jit(solution)/shard_map/ppermute | solution.py:458
  13.5 0.0 copy-start.2
  13.5 0.0 copy-start.3
  13.5 1.6 %collective-permute-start.3 = (bf16[4,256,128]{2,1,0:T(8,128)(2,1)S(1)}, bf16[4,256,128]{2,1,0:T(8,128)(2,1)S(1)}, u32[]{:S(2)}, u32[]{:S(2)}) collective-permute-start(bf16[4,256,128]{2,1,0:T(8,128)(2,1)S(1)} %get-tuple-element.50), channel_id=1, source_target_pairs={{8,20},{12,16},{16,12},{20,8},{4,0},{24,28},{9,21},{13,17},{17,13}... | collective-permute-start | bytes 786440 | tf_op jit(solution)/shard_map/ppermute | solution.py:458
  15.1 2.9 %rows_round_2.1 = (bf16[4,256,128]{2,1,0:T(8,128)(2,1)S(1)}, bf16[4,256,128]{2,1,0:T(8,128)(2,1)S(1)}, bf16[4,256,128]{2,1,0:T(8,128)(2,1)S(1)}, bf16[4,256,128]...) custom-call(bf16[1024,1024]{1,0:T(8,128)(2,1)S(1)} %windows.1.window, bf16[8,1024,256]{2,1,0:T(8,128)(2,1)S(1)} %copy-done), custom_call_target="tpu_custom_call" | custom-call | flops 2684354560 | bytes 5242880 | tf_op jit(solution)/shard_map/rows_round_2/pallas_call | solution.py:445
  18.0 0.0 collective-permute-done.got.rest_0_
  18.0 1.5 %collective-permute-done.1.rest_7_ = bf16[4,256,128]{2,1,0:T(8,128)(2,1)S(1)} collective-permute-done((bf16[4,256,128]{2,1,0:T(8,128)(2,1)S(1)}, bf16[4,256,128]{2,1,0:T(8,128)(2,1)S(1)}, u32[]{:S(2)}, u32[]{:S(2)}) %collective-permute-start.1) | collective-permute-done | bytes 262176 | tf_op jit(solution)/shard_map/ppermute | solution.py:458
  19.5 2.9 %collective-permute-start.2 = (bf16[4,256,128]{2,1,0:T(8,128)(2,1)S(1)}, bf16[4,256,128]{2,1,0:T(8,128)(2,1)S(1)}, u32[]{:S(2)}, u32[]{:S(2)}) collective-permute-start(bf16[4,256,128]{2,1,0:T(8,128)(2,1)S(1)} %get-tuple-element.49), channel_id=1, source_target_pairs={{4,8},{8,4},{12,0},{16,28},{20,24},{24,20},{5,9},{9,5},{13,1},{17,... | collective-permute-start | bytes 786440 | tf_op jit(solution)/shard_map/ppermute | solution.py:458
  22.4 3.3 %collective-permute-start.4 = (bf16[4,256,128]{2,1,0:T(8,128)(2,1)S(1)}, bf16[4,256,128]{2,1,0:T(8,128)(2,1)S(1)}, u32[]{:S(2)}, u32[]{:S(2)}) collective-permute-start(bf16[4,256,128]{2,1,0:T(8,128)(2,1)S(1)} %class_4_blocks.1), channel_id=1, source_target_pairs={{0,16},{4,20},{8,24},{12,28},{16,0},{20,4},{24,8},{28,12},{1,17},{... | collective-permute-start | bytes 786440 | tf_op jit(solution)/shard_map/ppermute | solution.py:458
  25.7 1.3 %collective-permute-start.6 = (bf16[4,256,128]{2,1,0:T(8,128)(2,1)S(1)}, bf16[4,256,128]{2,1,0:T(8,128)(2,1)S(1)}, u32[]{:S(2)}, u32[]{:S(2)}) collective-permute-start(bf16[4,256,128]{2,1,0:T(8,128)(2,1)S(1)} %get-tuple-element.53.own), channel_id=1, source_target_pairs={{8,28},{12,24},{16,4},{20,0},{9,29},{13,25},{17,5},{21,1},{10,30},... | collective-permute-start | bytes 786440 | tf_op jit(solution)/shard_map/ppermute | solution.py:458
  27.0 1.6 %collective-permute-start.7 = (bf16[4,256,128]{2,1,0:T(8,128)(2,1)S(1)}, bf16[4,256,128]{2,1,0:T(8,128)(2,1)S(1)}, u32[]{:S(2)}, u32[]{:S(2)}) collective-permute-start(bf16[4,256,128]{2,1,0:T(8,128)(2,1)S(1)} %get-tuple-element.55), channel_id=1, source_target_pairs={{4,0},{8,12},{12,8},{16,20},{20,16},{24,28},{5,1},{9,13},{13,9},{1... | collective-permute-start | bytes 786440 | tf_op jit(solution)/shard_map/ppermute | solution.py:458
  28.6 6.7 %collective-permute-done.2.rest_8_ = bf16[4,256,128]{2,1,0:T(8,128)(2,1)S(1)} collective-permute-done((bf16[4,256,128]{2,1,0:T(8,128)(2,1)S(1)}, bf16[4,256,128]{2,1,0:T(8,128)(2,1)S(1)}, u32[]{:S(2)}, u32[]{:S(2)}) %collective-permute-start.2) | collective-permute-done | bytes 262176 | tf_op jit(solution)/shard_map/ppermute | solution.py:458
  35.3 1.9 %collective-permute-start.5 = (bf16[4,256,128]{2,1,0:T(8,128)(2,1)S(1)}, bf16[4,256,128]{2,1,0:T(8,128)(2,1)S(1)}, u32[]{:S(2)}, u32[]{:S(2)}) collective-permute-start(bf16[4,256,128]{2,1,0:T(8,128)(2,1)S(1)} %class_6_blocks.1), channel_id=1, source_target_pairs={{0,24},{4,28},{24,0},{28,4},{1,25},{5,29},{25,1},{29,5},{2,26},{6,... | collective-permute-start | bytes 786440 | tf_op jit(solution)/shard_map/ppermute | solution.py:458
  37.2 0.6 amplitude.1
  37.8 0.0 collective-permute-done.4.rest_2_
  37.8 9.0 %collective-permute-done.6.rest_4_ = bf16[4,256,128]{2,1,0:T(8,128)(2,1)S(1)} collective-permute-done((bf16[4,256,128]{2,1,0:T(8,128)(2,1)S(1)}, bf16[4,256,128]{2,1,0:T(8,128)(2,1)S(1)}, u32[]{:S(2)}, u32[]{:S(2)}) %collective-permute-start.6) | collective-permute-done | bytes 262176 | tf_op jit(solution)/shard_map/ppermute | solution.py:458
  46.8 0.0 collective-permute-done.7.rest_6_
  46.9 5.3 %modulus_step.1 = (bf16[4,256,128]{2,1,0:T(8,128)(2,1)S(1)}, bf16[4,256,128]{2,1,0:T(8,128)(2,1)S(1)}, bf16[4,256,128]{2,1,0:T(8,128)(2,1)S(1)}, bf16[4,256,128]{2,1,0:T(8,128)(2,1)S(1)}) custom-call(f32[1024,256]{1,0:T(8,128)S(1)} %get-tuple-element.46.amplitude, bf16[8,256,1024]{2,1,0:T(8,128)(2,1)S(1)} %get-tuple-element.47.table, ...), custom_call_target="tpu_custom_call" | custom-call | flops 4294967296 | bytes 12582912 | tf_op jit(solution)/shard_map/modulus_step/pallas_call | solution.py:498
  52.2 0.2 collective-permute-start.10
  52.4 2.0 %collective-permute-start.8 = (bf16[4,256,128]{2,1,0:T(8,128)(2,1)S(1)}, bf16[4,256,128]{2,1,0:T(8,128)(2,1)S(1)}, u32[]{:S(2)}, u32[]{:S(2)}) collective-permute-start(bf16[4,256,128]{2,1,0:T(8,128)(2,1)S(1)} %get-tuple-element.59), channel_id=1, source_target_pairs={{0,4},{4,0},{8,12},{12,8},{16,20},{20,16},{24,28},{28,24},{1,5},{5... | collective-permute-start | bytes 786440 | tf_op jit(solution)/shard_map/ppermute | solution.py:458
  54.4 1.4 %collective-permute-start.9 = (bf16[4,256,128]{2,1,0:T(8,128)(2,1)S(1)}, bf16[4,256,128]{2,1,0:T(8,128)(2,1)S(1)}, u32[]{:S(2)}, u32[]{:S(2)}) collective-permute-start(bf16[4,256,128]{2,1,0:T(8,128)(2,1)S(1)} %get-tuple-element.60), channel_id=1, source_target_pairs={{0,8},{4,12},{8,0},{12,4},{16,24},{20,28},{24,16},{28,20},{1,9},{5... | collective-permute-start | bytes 786440 | tf_op jit(solution)/shard_map/ppermute | solution.py:458
  55.7 6.7 %collective-permute-done.10.rest_3_ = bf16[4,256,128]{2,1,0:T(8,128)(2,1)S(1)} collective-permute-done((bf16[4,256,128]{2,1,0:T(8,128)(2,1)S(1)}, bf16[4,256,128]{2,1,0:T(8,128)(2,1)S(1)}, u32[]{:S(2)}, u32[]{:S(2)}) %collective-permute-start.10) | collective-permute-done | bytes 262176 | tf_op jit(solution)/shard_map/ppermute | solution.py:458
  62.4 3.7 %collective-permute-done.8.rest_1_ = bf16[4,256,128]{2,1,0:T(8,128)(2,1)S(1)} collective-permute-done((bf16[4,256,128]{2,1,0:T(8,128)(2,1)S(1)}, bf16[4,256,128]{2,1,0:T(8,128)(2,1)S(1)}, u32[]{:S(2)}, u32[]{:S(2)}) %collective-permute-start.8) | collective-permute-done | bytes 262176 | tf_op jit(solution)/shard_map/ppermute | solution.py:458
  66.2 1.4 %collective-permute-done.9.rest_2_ = bf16[4,256,128]{2,1,0:T(8,128)(2,1)S(1)} collective-permute-done((bf16[4,256,128]{2,1,0:T(8,128)(2,1)S(1)}, bf16[4,256,128]{2,1,0:T(8,128)(2,1)S(1)}, u32[]{:S(2)}, u32[]{:S(2)}) %collective-permute-start.9) | collective-permute-done | bytes 262176 | tf_op jit(solution)/shard_map/ppermute | solution.py:458
  67.6 2.7 %update_sent.1 = (bf16[2,2,256,512]{3,2,1,0:T(8,128)(2,1)S(1)}, bf16[2,2,256,512]{3,2,1,0:T(8,128)(2,1)S(1)}, bf16[1024,512]{1,0:T(8,128)(2,1)S(1)}) custom-call(s32[4]{0:T(128)S(1)} %pad_add_fusion.starts, bf16[8,1024,256]{2,1,0:T(8,128)(2,1)S(1)} %copy-done, bf16[4,256,128]{2,1,0:T(8,128)(2,1)S(1)} %get-tuple-element.58.rest_0_, ...), custom_call_target="tpu_custom_call" | custom-call | flops 1073741824 | bytes 8388608 | tf_op jit(solution)/shard_map/update_sent/pallas_call | solution.py:523
  70.2 0.1 collective-permute-start.12
  70.3 0.5 collective-permute-start.11
  70.8 2.6 %update_kept.1 = (f32[2,256,512]{2,1,0:T(8,128)S(1)}, bf16[2,256,512]{2,1,0:T(8,128)(2,1)S(1)}, bf16[2,256,512]{2,1,0:T(8,128)(2,1)S(1)}, bf16[2,256,512]{2,1,0:T(8,128)(2,1)S(1)}) custom-call(s32[4]{0:T(128)S(1)} %pad_add_fusion.starts, bf16[8,1024,256]{2,1,0:T(8,128)(2,1)S(1)} %copy-done, bf16[1024,512]{1,0:T(8,128)(2,1)S(1)} %get-tuple-element.62.back), custom_call_target="tpu_custom_call" | custom-call | flops 1073741824 | bytes 10485760 | tf_op jit(solution)/shard_map/update_kept/pallas_call | solution.py:538
  73.4 0.0 copy-start.4
  73.4 0.1 z_first_kernel.1
  73.5 1.9 %collective-permute-start.13 = (bf16[2,2,256,128]{3,2,1,0:T(8,128)(2,1)S(1)}, bf16[2,2,256,128]{3,2,1,0:T(8,128)(2,1)S(1)}, u32[]{:S(2)}, u32[]{:S(2)}) collective-permute-start(bf16[2,2,256,128]{3,2,1,0:T(8,128)(2,1)S(1)} %z_first_kernel.1), channel_id=1, source_target_pairs={{0,16},{4,20},{8,24},{20,4},{24,8},{28,12},{1,17},{5,21},{9,25},{2... | collective-permute-start | bytes 786440 | tf_op jit(solution)/shard_map/ppermute | solution.py:458
  75.4 0.9 x_first_kernel.1
  76.3 1.5 %collective-permute-start.15 = (bf16[2,256,384]{2,1,0:T(8,128)(2,1)}, bf16[2,256,384]{2,1,0:T(8,128)(2,1)}, u32[]{:S(2)}, u32[]{:S(2)}) collective-permute-start(bf16[2,256,384]{2,1,0:T(8,128)(2,1)} %x_first_kernel.1), channel_id=1, source_target_pairs={{0,2},{2,0},{1,3},{3,1},{4,6},{6,4},{5,7},{7,5},{8,10},{10,8},{9,1... | collective-permute-start | bytes 1179656 | tf_op jit(solution)/shard_map/ppermute | solution.py:556
  77.8 12.1 %collective-permute-done.13.got_z = bf16[2,2,256,128]{3,2,1,0:T(8,128)(2,1)S(1)} collective-permute-done((bf16[2,2,256,128]{3,2,1,0:T(8,128)(2,1)S(1)}, bf16[2,2,256,128]{3,2,1,0:T(8,128)(2,1)S(1)}, u32[]{:S(2)}, u32[]{:S(2)}) %collective-permute-start.13) | collective-permute-done | bytes 262176 | tf_op jit(solution)/shard_map/ppermute | solution.py:458
  89.9 0.1 x_second_kernel.1
  90.0 1.6 %collective-permute-start.14 = (bf16[2,256,512]{2,1,0:T(8,128)(2,1)S(1)}, bf16[2,256,512]{2,1,0:T(8,128)(2,1)}, u32[]{:S(2)}, u32[]{:S(2)}) collective-permute-start(bf16[2,256,512]{2,1,0:T(8,128)(2,1)S(1)} %x_second_kernel.1), channel_id=1, source_target_pairs={{0,2},{2,0},{1,3},{3,1},{4,6},{6,4},{5,7},{7,5},{8,10},{10,8},{9,1... | collective-permute-start | bytes 1572872 | tf_op jit(solution)/shard_map/ppermute | solution.py:560
  91.6 1.1 %z_second_kernel.1 = bf16[2,256,384]{2,1,0:T(8,128)(2,1)S(1)} custom-call(bf16[2,256,512]{2,1,0:T(8,128)(2,1)S(1)} %get-tuple-element.65.that_near, bf16[2,2,256,512]{3,2,1,0:T(8,128)(2,1)S(1)} %collective-permute-done.12.got_that, bf16[2,256,384]{2,1,0:T(8,128)(2,1)} %collective-permute-done.15.got_x), custom_call_target="tpu_custom_call" | custom-call | bytes 1048576 | tf_op jit(solution)/shard_map/z_second_kernel/pallas_call | solution.py:551
  92.8 1.9 %collective-permute-start.16 = (bf16[2,256,384]{2,1,0:T(8,128)(2,1)S(1)}, bf16[2,256,384]{2,1,0:T(8,128)(2,1)S(1)}, u32[]{:S(2)}, u32[]{:S(2)}) collective-permute-start(bf16[2,256,384]{2,1,0:T(8,128)(2,1)S(1)} %z_second_kernel.1), channel_id=1, source_target_pairs={{0,16},{4,20},{8,24},{20,4},{24,8},{28,12},{1,17},{5,21},{9,25},{2... | collective-permute-start | bytes 1179656 | tf_op jit(solution)/shard_map/ppermute | solution.py:458
  94.7 1.8 %fusion.1 = f32[2,256,512]{2,1,0:T(8,128)S(1)} fusion(f32[2,256,512]{2,1,0:T(8,128)} %copy-done.4, f32[2,256,2048]{2,1,0:T(8,128)} %spectrum.1, s32[]{:T(128)S(6)} %select_n.3, bf16[2,2,256,512]{3,2,1,0:T(8,128)(2,1)S(1)} %collective-permute-done.11.got_this, bf16[2,256,128]{2,1,0:T(8,128)(2,1)S(1)} %slice_bitcast_fusion.1), kind=kLoop, calls=%fused_computation.2 | loop fusion | flops 1310720 | bytes 3801092 | tf_op jit(solution)/shard_map/add | solution.py:567
  96.5 7.5 %collective-permute-done.14 = bf16[2,256,512]{2,1,0:T(8,128)(2,1)} collective-permute-done((bf16[2,256,512]{2,1,0:T(8,128)(2,1)S(1)}, bf16[2,256,512]{2,1,0:T(8,128)(2,1)}, u32[]{:S(2)}, u32[]{:S(2)}) %collective-permute-start.14) | collective-permute-done | bytes 524320 | tf_op jit(solution)/shard_map/ppermute | solution.py:560
  104.1 1.2 %convert_add_fusion.2 = f32[2,256,512]{2,1,0:T(8,128)S(1)} fusion(f32[2,256,512]{2,1,0:T(8,128)S(1)} %fusion.1, bf16[2,256,512]{2,1,0:T(8,128)(2,1)} %collective-permute-done.14), kind=kLoop, calls=%fused_computation.4 | loop fusion | flops 524288 | bytes 2621440 | tf_op jit(solution)/shard_map/add | solution.py:569
  105.3 4.1 %collective-permute-done.16 = bf16[2,256,384]{2,1,0:T(8,128)(2,1)S(1)} collective-permute-done((bf16[2,256,384]{2,1,0:T(8,128)(2,1)S(1)}, bf16[2,256,384]{2,1,0:T(8,128)(2,1)S(1)}, u32[]{:S(2)}, u32[]{:S(2)}) %collective-permute-start.16) | collective-permute-done | bytes 393248 | tf_op jit(solution)/shard_map/ppermute | solution.py:458
  109.4 1.1 %convert_add_fusion.1 = f32[2,256,512]{2,1,0:T(8,128)} fusion(f32[2,256,512]{2,1,0:T(8,128)S(1)} %convert_add_fusion.2, bf16[2,256,384]{2,1,0:T(8,128)(2,1)S(1)} %collective-permute-done.16), kind=kLoop, calls=%fused_computation.3 | loop fusion | flops 524288 | bytes 2490368 | tf_op jit(solution)/shard_map/add | solution.py:571
  (14 shorter events, 0.1 us)
Async XLA Ops:
  0.0 4.6 %copy-start = (bf16[8,1024,256]{2,1,0:T(8,128)(2,1)S(1)}, bf16[8,1024,256]{2,1,0:T(8,128)(2,1)}, u32[]{:S(2)}) copy-start(bf16[8,1024,256]{2,1,0:T(8,128)(2,1)} %constant.18.clone.table) | copy-start | bytes 12582916
  0.9 2.4 %copy-start.1 = (f32[2,256,2048]{2,1,0:T(8,128)S(1)}, f32[2,256,2048]{2,1,0:T(8,128)}, u32[]{:S(2)}) copy-start(f32[2,256,2048]{2,1,0:T(8,128)} %spectrum.1) | copy-start | bytes 12582916
  6.5 11.5 %collective-permute-start = (bf16[4,256,128]{2,1,0:T(8,128)(2,1)S(1)}, bf16[4,256,128]{2,1,0:T(8,128)(2,1)S(1)}, u32[]{:S(2)}, u32[]{:S(2)}) collective-permute-start(bf16[4,256,128]{2,1,0:T(8,128)(2,1)S(1)} %get-tuple-element.39), channel_id=1, source_target_pairs={{8,16},{12,20},{16,8},{20,12},{4,0},{24,28},{9,17},{13,21},{17,9},... | collective-permute-start | bytes 786440 | tf_op jit(solution)/shard_map/ppermute | solution.py:458
  7.8 11.7 %collective-permute-start.1 = (bf16[4,256,128]{2,1,0:T(8,128)(2,1)S(1)}, bf16[4,256,128]{2,1,0:T(8,128)(2,1)S(1)}, u32[]{:S(2)}, u32[]{:S(2)}) collective-permute-start(bf16[4,256,128]{2,1,0:T(8,128)(2,1)S(1)} %get-tuple-element.40), channel_id=1, source_target_pairs={{4,12},{8,0},{12,4},{16,24},{20,28},{24,16},{5,13},{9,1},{13,5},{1... | collective-permute-start | bytes 786440 | tf_op jit(solution)/shard_map/ppermute | solution.py:458
  13.5 23.8 %copy-start.2 = (bf16[8,256,1024]{2,1,0:T(8,128)(2,1)S(1)}, bf16[8,256,1024]{2,1,0:T(8,128)(2,1)}, u32[]{:S(2)}) copy-start(bf16[8,256,1024]{2,1,0:T(8,128)(2,1)} %constant.17.clone.table) | copy-start | bytes 12582916
  13.5 23.8 %copy-start.3 = (f32[2,128,1024]{2,1,0:T(8,128)S(1)}, f32[2,128,1024]{2,1,0:T(8,128)}, u32[]{:S(2)}) copy-start(f32[2,128,1024]{2,1,0:T(8,128)} %images) | copy-start | bytes 3145732
  13.5 15.1 %collective-permute-start.3 = (bf16[4,256,128]{2,1,0:T(8,128)(2,1)S(1)}, bf16[4,256,128]{2,1,0:T(8,128)(2,1)S(1)}, u32[]{:S(2)}, u32[]{:S(2)}) collective-permute-start(bf16[4,256,128]{2,1,0:T(8,128)(2,1)S(1)} %get-tuple-element.50), channel_id=1, source_target_pairs={{8,20},{12,16},{16,12},{20,8},{4,0},{24,28},{9,21},{13,17},{17,13}... | collective-permute-start | bytes 786440 | tf_op jit(solution)/shard_map/ppermute | solution.py:458
  19.5 15.8 %collective-permute-start.2 = (bf16[4,256,128]{2,1,0:T(8,128)(2,1)S(1)}, bf16[4,256,128]{2,1,0:T(8,128)(2,1)S(1)}, u32[]{:S(2)}, u32[]{:S(2)}) collective-permute-start(bf16[4,256,128]{2,1,0:T(8,128)(2,1)S(1)} %get-tuple-element.49), channel_id=1, source_target_pairs={{4,8},{8,4},{12,0},{16,28},{20,24},{24,20},{5,9},{9,5},{13,1},{17,... | collective-permute-start | bytes 786440 | tf_op jit(solution)/shard_map/ppermute | solution.py:458
  22.4 15.4 %collective-permute-start.4 = (bf16[4,256,128]{2,1,0:T(8,128)(2,1)S(1)}, bf16[4,256,128]{2,1,0:T(8,128)(2,1)S(1)}, u32[]{:S(2)}, u32[]{:S(2)}) collective-permute-start(bf16[4,256,128]{2,1,0:T(8,128)(2,1)S(1)} %class_4_blocks.1), channel_id=1, source_target_pairs={{0,16},{4,20},{8,24},{12,28},{16,0},{20,4},{24,8},{28,12},{1,17},{... | collective-permute-start | bytes 786440 | tf_op jit(solution)/shard_map/ppermute | solution.py:458
  25.7 21.1 %collective-permute-start.6 = (bf16[4,256,128]{2,1,0:T(8,128)(2,1)S(1)}, bf16[4,256,128]{2,1,0:T(8,128)(2,1)S(1)}, u32[]{:S(2)}, u32[]{:S(2)}) collective-permute-start(bf16[4,256,128]{2,1,0:T(8,128)(2,1)S(1)} %get-tuple-element.53.own), channel_id=1, source_target_pairs={{8,28},{12,24},{16,4},{20,0},{9,29},{13,25},{17,5},{21,1},{10,30},... | collective-permute-start | bytes 786440 | tf_op jit(solution)/shard_map/ppermute | solution.py:458
  27.0 19.9 %collective-permute-start.7 = (bf16[4,256,128]{2,1,0:T(8,128)(2,1)S(1)}, bf16[4,256,128]{2,1,0:T(8,128)(2,1)S(1)}, u32[]{:S(2)}, u32[]{:S(2)}) collective-permute-start(bf16[4,256,128]{2,1,0:T(8,128)(2,1)S(1)} %get-tuple-element.55), channel_id=1, source_target_pairs={{4,0},{8,12},{12,8},{16,20},{20,16},{24,28},{5,1},{9,13},{13,9},{1... | collective-permute-start | bytes 786440 | tf_op jit(solution)/shard_map/ppermute | solution.py:458
  35.3 11.6 %collective-permute-start.5 = (bf16[4,256,128]{2,1,0:T(8,128)(2,1)S(1)}, bf16[4,256,128]{2,1,0:T(8,128)(2,1)S(1)}, u32[]{:S(2)}, u32[]{:S(2)}) collective-permute-start(bf16[4,256,128]{2,1,0:T(8,128)(2,1)S(1)} %class_6_blocks.1), channel_id=1, source_target_pairs={{0,24},{4,28},{24,0},{28,4},{1,25},{5,29},{25,1},{29,5},{2,26},{6,... | collective-permute-start | bytes 786440 | tf_op jit(solution)/shard_map/ppermute | solution.py:458
  52.2 10.3 %collective-permute-start.10 = (bf16[4,256,128]{2,1,0:T(8,128)(2,1)S(1)}, bf16[4,256,128]{2,1,0:T(8,128)(2,1)S(1)}, u32[]{:S(2)}, u32[]{:S(2)}) collective-permute-start(bf16[4,256,128]{2,1,0:T(8,128)(2,1)S(1)} %get-tuple-element.61), channel_id=1, source_target_pairs={{0,12},{4,8},{8,4},{12,0},{16,28},{20,24},{24,20},{28,16},{1,13},{... | collective-permute-start | bytes 786440 | tf_op jit(solution)/shard_map/ppermute | solution.py:458
  52.4 13.8 %collective-permute-start.8 = (bf16[4,256,128]{2,1,0:T(8,128)(2,1)S(1)}, bf16[4,256,128]{2,1,0:T(8,128)(2,1)S(1)}, u32[]{:S(2)}, u32[]{:S(2)}) collective-permute-start(bf16[4,256,128]{2,1,0:T(8,128)(2,1)S(1)} %get-tuple-element.59), channel_id=1, source_target_pairs={{0,4},{4,0},{8,12},{12,8},{16,20},{20,16},{24,28},{28,24},{1,5},{5... | collective-permute-start | bytes 786440 | tf_op jit(solution)/shard_map/ppermute | solution.py:458
  54.4 13.2 %collective-permute-start.9 = (bf16[4,256,128]{2,1,0:T(8,128)(2,1)S(1)}, bf16[4,256,128]{2,1,0:T(8,128)(2,1)S(1)}, u32[]{:S(2)}, u32[]{:S(2)}) collective-permute-start(bf16[4,256,128]{2,1,0:T(8,128)(2,1)S(1)} %get-tuple-element.60), channel_id=1, source_target_pairs={{0,8},{4,12},{8,0},{12,4},{16,24},{20,28},{24,16},{28,20},{1,9},{5... | collective-permute-start | bytes 786440 | tf_op jit(solution)/shard_map/ppermute | solution.py:458
  70.2 3.2 %collective-permute-start.12 = (bf16[2,2,256,512]{3,2,1,0:T(8,128)(2,1)S(1)}, bf16[2,2,256,512]{3,2,1,0:T(8,128)(2,1)S(1)}, u32[]{:S(2)}, u32[]{:S(2)}) collective-permute-start(bf16[2,2,256,512]{3,2,1,0:T(8,128)(2,1)S(1)} %get-tuple-element.67), channel_id=1, source_target_pairs={{0,1},{1,0},{2,3},{3,2},{4,5},{5,4},{6,7},{7,6},{8,9},{9,8},{10,11... | collective-permute-start | bytes 3145736 | tf_op jit(solution)/shard_map/ppermute | solution.py:536
  70.3 7.5 %collective-permute-start.11 = (bf16[2,2,256,512]{3,2,1,0:T(8,128)(2,1)S(1)}, bf16[2,2,256,512]{3,2,1,0:T(8,128)(2,1)S(1)}, u32[]{:S(2)}, u32[]{:S(2)}) collective-permute-start(bf16[2,2,256,512]{3,2,1,0:T(8,128)(2,1)S(1)} %get-tuple-element.64), channel_id=1, source_target_pairs={{0,1},{1,0},{2,3},{3,2},{4,5},{5,4},{6,7},{7,6},{8,9},{9,8},{10,11... | collective-permute-start | bytes 3145736 | tf_op jit(solution)/shard_map/ppermute | solution.py:537
  73.4 4.4 %copy-start.4 = (f32[2,256,512]{2,1,0:T(8,128)}, f32[2,256,512]{2,1,0:T(8,128)S(1)}, u32[]{:S(2)}) copy-start(f32[2,256,512]{2,1,0:T(8,128)S(1)} %get-tuple-element.63) | copy-start | bytes 3145732
  73.5 16.4 %collective-permute-start.13 = (bf16[2,2,256,128]{3,2,1,0:T(8,128)(2,1)S(1)}, bf16[2,2,256,128]{3,2,1,0:T(8,128)(2,1)S(1)}, u32[]{:S(2)}, u32[]{:S(2)}) collective-permute-start(bf16[2,2,256,128]{3,2,1,0:T(8,128)(2,1)S(1)} %z_first_kernel.1), channel_id=1, source_target_pairs={{0,16},{4,20},{8,24},{20,4},{24,8},{28,12},{1,17},{5,21},{9,25},{2... | collective-permute-start | bytes 786440 | tf_op jit(solution)/shard_map/ppermute | solution.py:458
  76.3 15.3 %collective-permute-start.15 = (bf16[2,256,384]{2,1,0:T(8,128)(2,1)}, bf16[2,256,384]{2,1,0:T(8,128)(2,1)}, u32[]{:S(2)}, u32[]{:S(2)}) collective-permute-start(bf16[2,256,384]{2,1,0:T(8,128)(2,1)} %x_first_kernel.1), channel_id=1, source_target_pairs={{0,2},{2,0},{1,3},{3,1},{4,6},{6,4},{5,7},{7,5},{8,10},{10,8},{9,1... | collective-permute-start | bytes 1179656 | tf_op jit(solution)/shard_map/ppermute | solution.py:556
  90.0 14.0 %collective-permute-start.14 = (bf16[2,256,512]{2,1,0:T(8,128)(2,1)S(1)}, bf16[2,256,512]{2,1,0:T(8,128)(2,1)}, u32[]{:S(2)}, u32[]{:S(2)}) collective-permute-start(bf16[2,256,512]{2,1,0:T(8,128)(2,1)S(1)} %x_second_kernel.1), channel_id=1, source_target_pairs={{0,2},{2,0},{1,3},{3,1},{4,6},{6,4},{5,7},{7,5},{8,10},{10,8},{9,1... | collective-permute-start | bytes 1572872 | tf_op jit(solution)/shard_map/ppermute | solution.py:560
  92.8 16.6 %collective-permute-start.16 = (bf16[2,256,384]{2,1,0:T(8,128)(2,1)S(1)}, bf16[2,256,384]{2,1,0:T(8,128)(2,1)S(1)}, u32[]{:S(2)}, u32[]{:S(2)}) collective-permute-start(bf16[2,256,384]{2,1,0:T(8,128)(2,1)S(1)} %z_second_kernel.1), channel_id=1, source_target_pairs={{0,16},{4,20},{8,24},{20,4},{24,8},{28,12},{1,17},{5,21},{9,25},{2... | collective-permute-start | bytes 1179656 | tf_op jit(solution)/shard_map/ppermute | solution.py:458

commit v24 on v13

--- a/solution.py
+++ b/solution.py
@@ -479,7 +479,7 @@
     outer_pairs = [(s, s ^ 6) for s in range(SLABS) if s not in INNER]
     near_1 = permute(near_1, [(s, s ^ 1) for s in windowed])
     near_3 = permute(near_3, [(s, s ^ 3) for s in windowed])
-    near_1, got_b = lax.optimization_barrier((near_1, got_b))
+    near_3, got_b = lax.optimization_barrier((near_3, got_b))
     far_columns = [
         got_a,
         got_b,
@@ -559,11 +559,10 @@
     got_z_first = permute(over, across)
     over = sum_call(x_first_kernel, (2, rows, share - first), that_far, got_that)
     got_x = lax.ppermute(over, "led", planes)
-    over_z = sum_call(z_second_kernel, (2, rows, share - first), that_near, got_that, got_x)
-    got_z_second = permute(over_z, across)
+    over = sum_call(z_second_kernel, (2, rows, share - first), that_near, got_that, got_x)
+    got_z_second = permute(over, across)
     over = sum_call(x_own_kernel, (2, rows, share - first), this_far, got_this)
     got_x_own = lax.ppermute(over, "led", planes)
-    over, got_z_first = lax.optimization_barrier((over_z, got_z_first))
     over = sum_call(x_last_kernel, (2, rows, first), this_far, got_this, got_z_first)
     got_x_last = lax.ppermute(over, "led", planes)
 

time: 116 us -> 115 us (level)
  starting transfers between devices: 34.4 us -> 31.1 us
  waiting for transfers between devices: 52.2 us -> 53.8 us
    ppermute x13, waiting for transfers between devices: 40.8 us -> 50.9 us  [permute(): return lax.ppermute(sent, 'slab', pairs)]
    ppermute x1, waiting for transfers between devices: 6.42 us -> 0.01 us  [body_slabs(): got_x = lax.ppermute(over, 'led', planes)]
    ppermute x13, starting transfers between devices: 31.7 us -> 26.9 us  [permute(): return lax.ppermute(sent, 'slab', pairs)]
    ppermute x1, starting transfers between devices: 0.07 us -> 1.55 us  [body_slabs(): got_x_last = lax.ppermute(over, 'led', planes)]
  transfers between devices with their start and end apart: 18 -> 18, of which waited for: 12 -> 10; matrix products, arithmetic and copies ran while one was open for 1% -> 1% of each run, Pallas kernels for 8% -> 8%
where the time goes in v24:
time: 115 us; the launch traced here: 114 us
  waiting for transfers between devices  53.8 us (47%)
  starting transfers between devices  31.1 us (27%)
  Pallas kernels  20.9 us (18%)
  local copies, waits for them, and re-layouts  4.36 us (4%)
  other arithmetic  3.67 us (3%)
    ppermute x13, waiting for transfers between devices, permute(): return lax.ppermute(sent, 'slab', pairs)  50.9 us
    ppermute x13, starting transfers between devices, permute(): return lax.ppermute(sent, 'slab', pairs)  26.9 us
    pallas_call x1, Pallas kernels, body_slabs(): local_call(field_kernel, [sent_block] * HALF, [vmem] * 11, [pltpu.VMEM((w...  5.31 us
    pallas_call x2, Pallas kernels, rows_call(): local_call(functools.partial(rows_kernel, which), [sent_block] * count, [...  4.69 us
    unnamed x16, local copies, waits for them, and re-layouts  4.35 us
    pallas_call x1, Pallas kernels, body_slabs(): local_call(sent_kernel, [jax.ShapeDtypeStruct((2,) + piece, bf16), jax.Sh...  3.59 us
    pallas_call x5, Pallas kernels, sum_call(): local_call(kernel, out_shape, specs, [], 0, 2 ** 20, kernel.__name__)  2.91 us
    ppermute x1, waiting for transfers between devices, body_slabs(): got_x_last = lax.ppermute(over, 'led', planes)  2.65 us
  transfers between devices with their start and end apart: 18, of which 10 were waited for; matrix products, arithmetic and copies ran while one was open for 1% of the time, Pallas kernels for 8%

profile of v24, /device:TPU:4, one launch (start us, length us, event | category | flops | bytes accessed | tf_op | source)
XLA Modules:
  0.0 114.0 jit_solution(3232141071844119877)
XLA Ops:
  0.0 0.9 pad_add_fusion.starts
  0.9 2.4 %copy-done.1 = f32[2,256,2048]{2,1,0:T(8,128)S(1)} copy-done((f32[2,256,2048]{2,1,0:T(8,128)S(1)}, f32[2,256,2048]{2,1,0:T(8,128)}, u32[]{:S(2)}) %copy-start.1) | copy-done | bytes 4194328
  3.3 1.4 %windows.1.window = bf16[1024,1024]{1,0:T(8,128)(2,1)S(1)} custom-call(s32[4]{0:T(128)S(1)} %pad_add_fusion.starts, f32[2,256,2048]{2,1,0:T(8,128)S(1)} %copy-done.1), custom_call_target="tpu_custom_call" | custom-call | bytes 6291456 | tf_op jit(solution)/shard_map/windows/pallas_call | solution.py:438
  4.7 1.8 %rows_round_1.1 = (bf16[4,256,128]{2,1,0:T(8,128)(2,1)S(1)}, bf16[4,256,128]{2,1,0:T(8,128)(2,1)S(1)}, bf16[4,256,128]{2,1,0:T(8,128)(2,1)S(1)}) custom-call(bf16[1024,1024]{1,0:T(8,128)(2,1)S(1)} %windows.1.window, bf16[8,1024,256]{2,1,0:T(8,128)(2,1)S(1)} %copy-done), custom_call_target="tpu_custom_call" | custom-call | flops 1610612736 | bytes 5242880 | tf_op jit(solution)/shard_map/rows_round_1/pallas_call | solution.py:450
  6.5 1.3 %collective-permute-start = (bf16[4,256,128]{2,1,0:T(8,128)(2,1)S(1)}, bf16[4,256,128]{2,1,0:T(8,128)(2,1)S(1)}, u32[]{:S(2)}, u32[]{:S(2)}) collective-permute-start(bf16[4,256,128]{2,1,0:T(8,128)(2,1)S(1)} %get-tuple-element.40), channel_id=1, source_target_pairs={{8,16},{12,20},{16,8},{20,12},{4,0},{24,28},{9,17},{13,21},{17,9},... | collective-permute-start | bytes 786440 | tf_op jit(solution)/shard_map/ppermute | solution.py:463
  7.8 5.7 %collective-permute-start.1 = (bf16[4,256,128]{2,1,0:T(8,128)(2,1)S(1)}, bf16[4,256,128]{2,1,0:T(8,128)(2,1)S(1)}, u32[]{:S(2)}, u32[]{:S(2)}) collective-permute-start(bf16[4,256,128]{2,1,0:T(8,128)(2,1)S(1)} %get-tuple-element.41), channel_id=1, source_target_pairs={{4,12},{8,0},{12,4},{16,24},{20,28},{24,16},{5,13},{9,1},{13,5},{1... | collective-permute-start | bytes 786440 | tf_op jit(solution)/shard_map/ppermute | solution.py:463
  13.5 0.0 copy-start.2
  13.5 0.0 copy-start.5
  13.5 1.6 %collective-permute-start.3 = (bf16[4,256,128]{2,1,0:T(8,128)(2,1)S(1)}, bf16[4,256,128]{2,1,0:T(8,128)(2,1)S(1)}, u32[]{:S(2)}, u32[]{:S(2)}) collective-permute-start(bf16[4,256,128]{2,1,0:T(8,128)(2,1)S(1)} %get-tuple-element.51), channel_id=1, source_target_pairs={{8,20},{12,16},{16,12},{20,8},{4,0},{24,28},{9,21},{13,17},{17,13}... | collective-permute-start | bytes 786440 | tf_op jit(solution)/shard_map/ppermute | solution.py:463
  15.1 2.9 %rows_round_2.1 = (bf16[4,256,128]{2,1,0:T(8,128)(2,1)S(1)}, bf16[4,256,128]{2,1,0:T(8,128)(2,1)S(1)}, bf16[4,256,128]{2,1,0:T(8,128)(2,1)S(1)}, bf16[4,256,128]...) custom-call(bf16[1024,1024]{1,0:T(8,128)(2,1)S(1)} %windows.1.window, bf16[8,1024,256]{2,1,0:T(8,128)(2,1)S(1)} %copy-done), custom_call_target="tpu_custom_call" | custom-call | flops 2684354560 | bytes 5242880 | tf_op jit(solution)/shard_map/rows_round_2/pallas_call | solution.py:450
  18.0 1.5 %collective-permute-done.1.rest_7_ = bf16[4,256,128]{2,1,0:T(8,128)(2,1)S(1)} collective-permute-done((bf16[4,256,128]{2,1,0:T(8,128)(2,1)S(1)}, bf16[4,256,128]{2,1,0:T(8,128)(2,1)S(1)}, u32[]{:S(2)}, u32[]{:S(2)}) %collective-permute-start.1) | collective-permute-done | bytes 262176 | tf_op jit(solution)/shard_map/ppermute | solution.py:463
  19.5 2.9 %collective-permute-start.2 = (bf16[4,256,128]{2,1,0:T(8,128)(2,1)S(1)}, bf16[4,256,128]{2,1,0:T(8,128)(2,1)S(1)}, u32[]{:S(2)}, u32[]{:S(2)}) collective-permute-start(bf16[4,256,128]{2,1,0:T(8,128)(2,1)S(1)} %get-tuple-element.50), channel_id=1, source_target_pairs={{4,8},{8,4},{12,0},{16,28},{20,24},{24,20},{5,9},{9,5},{13,1},{17,... | collective-permute-start | bytes 786440 | tf_op jit(solution)/shard_map/ppermute | solution.py:463
  22.4 3.3 %collective-permute-start.4 = (bf16[4,256,128]{2,1,0:T(8,128)(2,1)S(1)}, bf16[4,256,128]{2,1,0:T(8,128)(2,1)S(1)}, u32[]{:S(2)}, u32[]{:S(2)}) collective-permute-start(bf16[4,256,128]{2,1,0:T(8,128)(2,1)S(1)} %class_4_blocks.1), channel_id=1, source_target_pairs={{0,16},{4,20},{8,24},{12,28},{16,0},{20,4},{24,8},{28,12},{1,17},{... | collective-permute-start | bytes 786440 | tf_op jit(solution)/shard_map/ppermute | solution.py:463
  25.7 1.3 %collective-permute-start.6 = (bf16[4,256,128]{2,1,0:T(8,128)(2,1)S(1)}, bf16[4,256,128]{2,1,0:T(8,128)(2,1)S(1)}, u32[]{:S(2)}, u32[]{:S(2)}) collective-permute-start(bf16[4,256,128]{2,1,0:T(8,128)(2,1)S(1)} %get-tuple-element.54.own), channel_id=1, source_target_pairs={{8,28},{12,24},{16,4},{20,0},{9,29},{13,25},{17,5},{21,1},{10,30},... | collective-permute-start | bytes 786440 | tf_op jit(solution)/shard_map/ppermute | solution.py:463
  27.0 1.6 %collective-permute-start.7 = (bf16[4,256,128]{2,1,0:T(8,128)(2,1)S(1)}, bf16[4,256,128]{2,1,0:T(8,128)(2,1)S(1)}, u32[]{:S(2)}, u32[]{:S(2)}) collective-permute-start(bf16[4,256,128]{2,1,0:T(8,128)(2,1)S(1)} %get-tuple-element.56), channel_id=1, source_target_pairs={{4,0},{8,12},{12,8},{16,20},{20,16},{24,28},{5,1},{9,13},{13,9},{1... | collective-permute-start | bytes 786440 | tf_op jit(solution)/shard_map/ppermute | solution.py:463
  28.6 6.7 %collective-permute-done.2.rest_8_ = bf16[4,256,128]{2,1,0:T(8,128)(2,1)S(1)} collective-permute-done((bf16[4,256,128]{2,1,0:T(8,128)(2,1)S(1)}, bf16[4,256,128]{2,1,0:T(8,128)(2,1)S(1)}, u32[]{:S(2)}, u32[]{:S(2)}) %collective-permute-start.2) | collective-permute-done | bytes 262176 | tf_op jit(solution)/shard_map/ppermute | solution.py:463
  35.3 1.9 %collective-permute-start.5 = (bf16[4,256,128]{2,1,0:T(8,128)(2,1)S(1)}, bf16[4,256,128]{2,1,0:T(8,128)(2,1)S(1)}, u32[]{:S(2)}, u32[]{:S(2)}) collective-permute-start(bf16[4,256,128]{2,1,0:T(8,128)(2,1)S(1)} %class_6_blocks.1), channel_id=1, source_target_pairs={{0,24},{4,28},{24,0},{28,4},{1,25},{5,29},{25,1},{29,5},{2,26},{6,... | collective-permute-start | bytes 786440 | tf_op jit(solution)/shard_map/ppermute | solution.py:463
  37.2 0.6 amplitude.1
  37.8 9.0 %collective-permute-done.6.rest_4_ = bf16[4,256,128]{2,1,0:T(8,128)(2,1)S(1)} collective-permute-done((bf16[4,256,128]{2,1,0:T(8,128)(2,1)S(1)}, bf16[4,256,128]{2,1,0:T(8,128)(2,1)S(1)}, u32[]{:S(2)}, u32[]{:S(2)}) %collective-permute-start.6) | collective-permute-done | bytes 262176 | tf_op jit(solution)/shard_map/ppermute | solution.py:463
  46.9 5.3 %modulus_step.1 = (bf16[4,256,128]{2,1,0:T(8,128)(2,1)S(1)}, bf16[4,256,128]{2,1,0:T(8,128)(2,1)S(1)}, bf16[4,256,128]{2,1,0:T(8,128)(2,1)S(1)}, bf16[4,256,128]{2,1,0:T(8,128)(2,1)S(1)}) custom-call(f32[1024,256]{1,0:T(8,128)S(1)} %get-tuple-element.47.amplitude, bf16[8,256,1024]{2,1,0:T(8,128)(2,1)S(1)} %get-tuple-element.48.table, ...), custom_call_target="tpu_custom_call" | custom-call | flops 4294967296 | bytes 12582912 | tf_op jit(solution)/shard_map/modulus_step/pallas_call | solution.py:503
  52.2 0.2 collective-permute-start.10
  52.4 2.0 %collective-permute-start.8 = (bf16[4,256,128]{2,1,0:T(8,128)(2,1)S(1)}, bf16[4,256,128]{2,1,0:T(8,128)(2,1)S(1)}, u32[]{:S(2)}, u32[]{:S(2)}) collective-permute-start(bf16[4,256,128]{2,1,0:T(8,128)(2,1)S(1)} %get-tuple-element.60), channel_id=1, source_target_pairs={{0,4},{4,0},{8,12},{12,8},{16,20},{20,16},{24,28},{28,24},{1,5},{5... | collective-permute-start | bytes 786440 | tf_op jit(solution)/shard_map/ppermute | solution.py:463
  54.4 1.4 %collective-permute-start.9 = (bf16[4,256,128]{2,1,0:T(8,128)(2,1)S(1)}, bf16[4,256,128]{2,1,0:T(8,128)(2,1)S(1)}, u32[]{:S(2)}, u32[]{:S(2)}) collective-permute-start(bf16[4,256,128]{2,1,0:T(8,128)(2,1)S(1)} %get-tuple-element.61), channel_id=1, source_target_pairs={{0,8},{4,12},{8,0},{12,4},{16,24},{20,28},{24,16},{28,20},{1,9},{5... | collective-permute-start | bytes 786440 | tf_op jit(solution)/shard_map/ppermute | solution.py:463
  55.7 6.7 %collective-permute-done.10.rest_3_ = bf16[4,256,128]{2,1,0:T(8,128)(2,1)S(1)} collective-permute-done((bf16[4,256,128]{2,1,0:T(8,128)(2,1)S(1)}, bf16[4,256,128]{2,1,0:T(8,128)(2,1)S(1)}, u32[]{:S(2)}, u32[]{:S(2)}) %collective-permute-start.10) | collective-permute-done | bytes 262176 | tf_op jit(solution)/shard_map/ppermute | solution.py:463
  62.4 3.7 %collective-permute-done.8.rest_1_ = bf16[4,256,128]{2,1,0:T(8,128)(2,1)S(1)} collective-permute-done((bf16[4,256,128]{2,1,0:T(8,128)(2,1)S(1)}, bf16[4,256,128]{2,1,0:T(8,128)(2,1)S(1)}, u32[]{:S(2)}, u32[]{:S(2)}) %collective-permute-start.8) | collective-permute-done | bytes 262176 | tf_op jit(solution)/shard_map/ppermute | solution.py:463
  66.2 1.4 %collective-permute-done.9.rest_2_ = bf16[4,256,128]{2,1,0:T(8,128)(2,1)S(1)} collective-permute-done((bf16[4,256,128]{2,1,0:T(8,128)(2,1)S(1)}, bf16[4,256,128]{2,1,0:T(8,128)(2,1)S(1)}, u32[]{:S(2)}, u32[]{:S(2)}) %collective-permute-start.9) | collective-permute-done | bytes 262176 | tf_op jit(solution)/shard_map/ppermute | solution.py:463
  67.6 3.6 %update_sent.1 = (bf16[2,2,256,512]{3,2,1,0:T(8,128)(2,1)}, bf16[2,2,256,512]{3,2,1,0:T(8,128)(2,1)S(1)}, bf16[1024,512]{1,0:T(8,128)(2,1)S(1)}) custom-call(s32[4]{0:T(128)S(1)} %pad_add_fusion.starts, bf16[8,1024,256]{2,1,0:T(8,128)(2,1)S(1)} %copy-done, bf16[4,256,128]{2,1,0:T(8,128)(2,1)S(1)} %get-tuple-element.59.rest_0_, ...), custom_call_target="tpu_custom_call" | custom-call | flops 1073741824 | bytes 8388608 | tf_op jit(solution)/shard_map/update_sent/pallas_call | solution.py:528
  71.2 0.5 collective-permute-start.11
  71.7 2.4 %update_kept.1 = (f32[2,256,512]{2,1,0:T(8,128)S(1)}, f32[2,256,512]{2,1,0:T(8,128)S(1)}, f32[2,256,512]{2,1,0:T(8,128)S(1)}, f32[2,256,512]{2,1,0:T(8,128)S(1)}) custom-call(s32[4]{0:T(128)S(1)} %pad_add_fusion.starts, bf16[8,1024,256]{2,1,0:T(8,128)(2,1)S(1)} %copy-done, bf16[1024,512]{1,0:T(8,128)(2,1)S(1)} %get-tuple-element.63.back), custom_call_target="tpu_custom_call" | custom-call | flops 1073741824 | bytes 10485760 | tf_op jit(solution)/shard_map/update_kept/pallas_call | solution.py:543
  74.1 1.0 copy-done.6
  75.1 0.2 collective-permute-done.12.got_that
  75.3 0.8 z_first_kernel.1
  76.1 1.0 copy-done.3
  77.1 1.9 %collective-permute-start.13 = (bf16[2,2,256,128]{3,2,1,0:T(8,128)(2,1)}, bf16[2,2,256,128]{3,2,1,0:T(8,128)(2,1)S(1)}, u32[]{:S(2)}, u32[]{:S(2)}) collective-permute-start(bf16[2,2,256,128]{3,2,1,0:T(8,128)(2,1)} %z_first_kernel.1), channel_id=1, source_target_pairs={{0,16},{4,20},{8,24},{20,4},{24,8},{28,12},{1,17},{5,21},{9,25},{2... | collective-permute-start | bytes 786440 | tf_op jit(solution)/shard_map/ppermute | solution.py:463
  79.0 0.8 x_first_kernel.1
  79.8 1.5 %collective-permute-start.16 = (bf16[2,256,384]{2,1,0:T(8,128)(2,1)}, bf16[2,256,384]{2,1,0:T(8,128)(2,1)}, u32[]{:S(2)}, u32[]{:S(2)}) collective-permute-start(bf16[2,256,384]{2,1,0:T(8,128)(2,1)} %x_first_kernel.1), channel_id=1, source_target_pairs={{0,2},{2,0},{1,3},{3,1},{4,6},{6,4},{5,7},{7,5},{8,10},{10,8},{9,1... | collective-permute-start | bytes 1179656 | tf_op jit(solution)/shard_map/ppermute | solution.py:561
  81.3 0.1 x_own_kernel.1
  81.4 0.6 collective-permute-start.14
  82.0 11.6 %collective-permute-done.13.got_z = bf16[2,2,256,128]{3,2,1,0:T(8,128)(2,1)S(1)} collective-permute-done((bf16[2,2,256,128]{3,2,1,0:T(8,128)(2,1)}, bf16[2,2,256,128]{3,2,1,0:T(8,128)(2,1)S(1)}, u32[]{:S(2)}, u32[]{:S(2)}) %collective-permute-start.13) | collective-permute-done | bytes 262176 | tf_op jit(solution)/shard_map/ppermute | solution.py:463
  93.6 0.1 x_last_kernel.1
  93.6 1.6 %collective-permute-start.15 = (bf16[2,256,128]{2,1,0:T(8,128)(2,1)S(1)}, bf16[2,256,128]{2,1,0:T(8,128)(2,1)S(1)}, u32[]{:S(2)}, u32[]{:S(2)}) collective-permute-start(bf16[2,256,128]{2,1,0:T(8,128)(2,1)S(1)} %x_last_kernel.1), channel_id=1, source_target_pairs={{0,2},{2,0},{1,3},{3,1},{4,6},{6,4},{5,7},{7,5},{8,10},{10,8},{9,1... | collective-permute-start | bytes 393224 | tf_op jit(solution)/shard_map/ppermute | solution.py:567
  95.2 1.1 z_second_kernel.1
  96.3 1.9 %collective-permute-start.17 = (bf16[2,256,384]{2,1,0:T(8,128)(2,1)S(1)}, bf16[2,256,384]{2,1,0:T(8,128)(2,1)S(1)}, u32[]{:S(2)}, u32[]{:S(2)}) collective-permute-start(bf16[2,256,384]{2,1,0:T(8,128)(2,1)S(1)} %z_second_kernel.1), channel_id=1, source_target_pairs={{0,16},{4,20},{8,24},{20,4},{24,8},{28,12},{1,17},{5,21},{9,25},{2... | collective-permute-start | bytes 1179656 | tf_op jit(solution)/shard_map/ppermute | solution.py:463
  98.3 1.5 %fusion.1 = f32[2,256,512]{2,1,0:T(8,128)S(1)} fusion(f32[2,256,512]{2,1,0:T(8,128)S(1)} %copy-done.7, f32[2,256,2048]{2,1,0:T(8,128)} %spectrum.1, s32[]{:T(128)S(6)} %select_n.3, bf16[2,2,256,512]{3,2,1,0:T(8,128)(2,1)S(1)} %collective-permute-done.11.got_this, bf16[2,256,128]{2,1,0:T(8,128)(2,1)S(1)} %slice_bitcast_fusion.1), kind=kLoop, calls=%fused_computation.2 | loop fusion | flops 1310720 | bytes 3801092 | tf_op jit(solution)/shard_map/add | solution.py:574
  99.8 2.6 %collective-permute-done.15 = bf16[2,256,128]{2,1,0:T(8,128)(2,1)S(1)} collective-permute-done((bf16[2,256,128]{2,1,0:T(8,128)(2,1)S(1)}, bf16[2,256,128]{2,1,0:T(8,128)(2,1)S(1)}, u32[]{:S(2)}, u32[]{:S(2)}) %collective-permute-start.15) | collective-permute-done | bytes 131104 | tf_op jit(solution)/shard_map/ppermute | solution.py:567
  102.4 0.2 add_add_fusion
  102.6 10.3 %collective-permute-done.17 = bf16[2,256,384]{2,1,0:T(8,128)(2,1)S(1)} collective-permute-done((bf16[2,256,384]{2,1,0:T(8,128)(2,1)S(1)}, bf16[2,256,384]{2,1,0:T(8,128)(2,1)S(1)}, u32[]{:S(2)}, u32[]{:S(2)}) %collective-permute-start.17) | collective-permute-done | bytes 393248 | tf_op jit(solution)/shard_map/ppermute | solution.py:463
  112.9 1.1 convert_add_fusion.1
  (23 shorter events, 0.1 us)
Async XLA Ops:
  0.0 4.6 %copy-start = (bf16[8,1024,256]{2,1,0:T(8,128)(2,1)S(1)}, bf16[8,1024,256]{2,1,0:T(8,128)(2,1)}, u32[]{:S(2)}) copy-start(bf16[8,1024,256]{2,1,0:T(8,128)(2,1)} %constant.18.clone.table) | copy-start | bytes 12582916
  0.9 2.4 %copy-start.1 = (f32[2,256,2048]{2,1,0:T(8,128)S(1)}, f32[2,256,2048]{2,1,0:T(8,128)}, u32[]{:S(2)}) copy-start(f32[2,256,2048]{2,1,0:T(8,128)} %spectrum.1) | copy-start | bytes 12582916
  6.5 11.5 %collective-permute-start = (bf16[4,256,128]{2,1,0:T(8,128)(2,1)S(1)}, bf16[4,256,128]{2,1,0:T(8,128)(2,1)S(1)}, u32[]{:S(2)}, u32[]{:S(2)}) collective-permute-start(bf16[4,256,128]{2,1,0:T(8,128)(2,1)S(1)} %get-tuple-element.40), channel_id=1, source_target_pairs={{8,16},{12,20},{16,8},{20,12},{4,0},{24,28},{9,17},{13,21},{17,9},... | collective-permute-start | bytes 786440 | tf_op jit(solution)/shard_map/ppermute | solution.py:463
  7.8 11.7 %collective-permute-start.1 = (bf16[4,256,128]{2,1,0:T(8,128)(2,1)S(1)}, bf16[4,256,128]{2,1,0:T(8,128)(2,1)S(1)}, u32[]{:S(2)}, u32[]{:S(2)}) collective-permute-start(bf16[4,256,128]{2,1,0:T(8,128)(2,1)S(1)} %get-tuple-element.41), channel_id=1, source_target_pairs={{4,12},{8,0},{12,4},{16,24},{20,28},{24,16},{5,13},{9,1},{13,5},{1... | collective-permute-start | bytes 786440 | tf_op jit(solution)/shard_map/ppermute | solution.py:463
  13.5 23.8 %copy-start.2 = (bf16[8,256,1024]{2,1,0:T(8,128)(2,1)S(1)}, bf16[8,256,1024]{2,1,0:T(8,128)(2,1)}, u32[]{:S(2)}) copy-start(bf16[8,256,1024]{2,1,0:T(8,128)(2,1)} %constant.17.clone.table) | copy-start | bytes 12582916
  13.5 23.8 %copy-start.5 = (f32[2,128,1024]{2,1,0:T(8,128)S(1)}, f32[2,128,1024]{2,1,0:T(8,128)}, u32[]{:S(2)}) copy-start(f32[2,128,1024]{2,1,0:T(8,128)} %images) | copy-start | bytes 3145732
  13.5 15.1 %collective-permute-start.3 = (bf16[4,256,128]{2,1,0:T(8,128)(2,1)S(1)}, bf16[4,256,128]{2,1,0:T(8,128)(2,1)S(1)}, u32[]{:S(2)}, u32[]{:S(2)}) collective-permute-start(bf16[4,256,128]{2,1,0:T(8,128)(2,1)S(1)} %get-tuple-element.51), channel_id=1, source_target_pairs={{8,20},{12,16},{16,12},{20,8},{4,0},{24,28},{9,21},{13,17},{17,13}... | collective-permute-start | bytes 786440 | tf_op jit(solution)/shard_map/ppermute | solution.py:463
  19.5 15.8 %collective-permute-start.2 = (bf16[4,256,128]{2,1,0:T(8,128)(2,1)S(1)}, bf16[4,256,128]{2,1,0:T(8,128)(2,1)S(1)}, u32[]{:S(2)}, u32[]{:S(2)}) collective-permute-start(bf16[4,256,128]{2,1,0:T(8,128)(2,1)S(1)} %get-tuple-element.50), channel_id=1, source_target_pairs={{4,8},{8,4},{12,0},{16,28},{20,24},{24,20},{5,9},{9,5},{13,1},{17,... | collective-permute-start | bytes 786440 | tf_op jit(solution)/shard_map/ppermute | solution.py:463
  22.4 15.4 %collective-permute-start.4 = (bf16[4,256,128]{2,1,0:T(8,128)(2,1)S(1)}, bf16[4,256,128]{2,1,0:T(8,128)(2,1)S(1)}, u32[]{:S(2)}, u32[]{:S(2)}) collective-permute-start(bf16[4,256,128]{2,1,0:T(8,128)(2,1)S(1)} %class_4_blocks.1), channel_id=1, source_target_pairs={{0,16},{4,20},{8,24},{12,28},{16,0},{20,4},{24,8},{28,12},{1,17},{... | collective-permute-start | bytes 786440 | tf_op jit(solution)/shard_map/ppermute | solution.py:463
  25.7 21.1 %collective-permute-start.6 = (bf16[4,256,128]{2,1,0:T(8,128)(2,1)S(1)}, bf16[4,256,128]{2,1,0:T(8,128)(2,1)S(1)}, u32[]{:S(2)}, u32[]{:S(2)}) collective-permute-start(bf16[4,256,128]{2,1,0:T(8,128)(2,1)S(1)} %get-tuple-element.54.own), channel_id=1, source_target_pairs={{8,28},{12,24},{16,4},{20,0},{9,29},{13,25},{17,5},{21,1},{10,30},... | collective-permute-start | bytes 786440 | tf_op jit(solution)/shard_map/ppermute | solution.py:463
  27.0 19.9 %collective-permute-start.7 = (bf16[4,256,128]{2,1,0:T(8,128)(2,1)S(1)}, bf16[4,256,128]{2,1,0:T(8,128)(2,1)S(1)}, u32[]{:S(2)}, u32[]{:S(2)}) collective-permute-start(bf16[4,256,128]{2,1,0:T(8,128)(2,1)S(1)} %get-tuple-element.56), channel_id=1, source_target_pairs={{4,0},{8,12},{12,8},{16,20},{20,16},{24,28},{5,1},{9,13},{13,9},{1... | collective-permute-start | bytes 786440 | tf_op jit(solution)/shard_map/ppermute | solution.py:463
  35.3 11.6 %collective-permute-start.5 = (bf16[4,256,128]{2,1,0:T(8,128)(2,1)S(1)}, bf16[4,256,128]{2,1,0:T(8,128)(2,1)S(1)}, u32[]{:S(2)}, u32[]{:S(2)}) collective-permute-start(bf16[4,256,128]{2,1,0:T(8,128)(2,1)S(1)} %class_6_blocks.1), channel_id=1, source_target_pairs={{0,24},{4,28},{24,0},{28,4},{1,25},{5,29},{25,1},{29,5},{2,26},{6,... | collective-permute-start | bytes 786440 | tf_op jit(solution)/shard_map/ppermute | solution.py:463
  52.2 10.3 %collective-permute-start.10 = (bf16[4,256,128]{2,1,0:T(8,128)(2,1)S(1)}, bf16[4,256,128]{2,1,0:T(8,128)(2,1)S(1)}, u32[]{:S(2)}, u32[]{:S(2)}) collective-permute-start(bf16[4,256,128]{2,1,0:T(8,128)(2,1)S(1)} %get-tuple-element.62), channel_id=1, source_target_pairs={{0,12},{4,8},{8,4},{12,0},{16,28},{20,24},{24,20},{28,16},{1,13},{... | collective-permute-start | bytes 786440 | tf_op jit(solution)/shard_map/ppermute | solution.py:463
  52.4 13.8 %collective-permute-start.8 = (bf16[4,256,128]{2,1,0:T(8,128)(2,1)S(1)}, bf16[4,256,128]{2,1,0:T(8,128)(2,1)S(1)}, u32[]{:S(2)}, u32[]{:S(2)}) collective-permute-start(bf16[4,256,128]{2,1,0:T(8,128)(2,1)S(1)} %get-tuple-element.60), channel_id=1, source_target_pairs={{0,4},{4,0},{8,12},{12,8},{16,20},{20,16},{24,28},{28,24},{1,5},{5... | collective-permute-start | bytes 786440 | tf_op jit(solution)/shard_map/ppermute | solution.py:463
  54.4 13.2 %collective-permute-start.9 = (bf16[4,256,128]{2,1,0:T(8,128)(2,1)S(1)}, bf16[4,256,128]{2,1,0:T(8,128)(2,1)S(1)}, u32[]{:S(2)}, u32[]{:S(2)}) collective-permute-start(bf16[4,256,128]{2,1,0:T(8,128)(2,1)S(1)} %get-tuple-element.61), channel_id=1, source_target_pairs={{0,8},{4,12},{8,0},{12,4},{16,24},{20,28},{24,16},{28,20},{1,9},{5... | collective-permute-start | bytes 786440 | tf_op jit(solution)/shard_map/ppermute | solution.py:463
  71.2 4.1 %collective-permute-start.12 = (bf16[2,2,256,512]{3,2,1,0:T(8,128)(2,1)S(1)}, bf16[2,2,256,512]{3,2,1,0:T(8,128)(2,1)S(1)}, u32[]{:S(2)}, u32[]{:S(2)}) collective-permute-start(bf16[2,2,256,512]{3,2,1,0:T(8,128)(2,1)S(1)} %get-tuple-element.68), channel_id=1, source_target_pairs={{0,1},{1,0},{2,3},{3,2},{4,5},{5,4},{6,7},{7,6},{8,9},{9,8},{10,11... | collective-permute-start | bytes 3145736 | tf_op jit(solution)/shard_map/ppermute | solution.py:541
  71.2 10.2 %collective-permute-start.11 = (bf16[2,2,256,512]{3,2,1,0:T(8,128)(2,1)}, bf16[2,2,256,512]{3,2,1,0:T(8,128)(2,1)S(1)}, u32[]{:S(2)}, u32[]{:S(2)}) collective-permute-start(bf16[2,2,256,512]{3,2,1,0:T(8,128)(2,1)} %get-tuple-element.65), channel_id=1, source_target_pairs={{0,1},{1,0},{2,3},{3,2},{4,5},{5,4},{6,7},{7,6},{8,9},{9,8},{10,11... | collective-permute-start | bytes 3145736 | tf_op jit(solution)/shard_map/ppermute | solution.py:542
  74.1 1.0 copy-start.6
  76.1 1.0 copy-start.3
  77.1 16.5 %collective-permute-start.13 = (bf16[2,2,256,128]{3,2,1,0:T(8,128)(2,1)}, bf16[2,2,256,128]{3,2,1,0:T(8,128)(2,1)S(1)}, u32[]{:S(2)}, u32[]{:S(2)}) collective-permute-start(bf16[2,2,256,128]{3,2,1,0:T(8,128)(2,1)} %z_first_kernel.1), channel_id=1, source_target_pairs={{0,16},{4,20},{8,24},{20,4},{24,8},{28,12},{1,17},{5,21},{9,25},{2... | collective-permute-start | bytes 786440 | tf_op jit(solution)/shard_map/ppermute | solution.py:463
  79.8 15.4 %collective-permute-start.16 = (bf16[2,256,384]{2,1,0:T(8,128)(2,1)}, bf16[2,256,384]{2,1,0:T(8,128)(2,1)}, u32[]{:S(2)}, u32[]{:S(2)}) collective-permute-start(bf16[2,256,384]{2,1,0:T(8,128)(2,1)} %x_first_kernel.1), channel_id=1, source_target_pairs={{0,2},{2,0},{1,3},{3,1},{4,6},{6,4},{5,7},{7,5},{8,10},{10,8},{9,1... | collective-permute-start | bytes 1179656 | tf_op jit(solution)/shard_map/ppermute | solution.py:561
  81.3 13.9 %copy-start.4 = (f32[2,256,512]{2,1,0:T(8,128)S(1)}, f32[2,256,512]{2,1,0:T(8,128)}, u32[]{:S(2)}) copy-start(f32[2,256,512]{2,1,0:T(8,128)} %copy-done.3) | copy-start | bytes 3145732
  81.3 16.9 %copy-start.7 = (f32[2,256,512]{2,1,0:T(8,128)S(1)}, f32[2,256,512]{2,1,0:T(8,128)}, u32[]{:S(2)}) copy-start(f32[2,256,512]{2,1,0:T(8,128)} %copy-done.6) | copy-start | bytes 3145732
  81.4 21.0 %collective-permute-start.14 = (bf16[2,256,384]{2,1,0:T(8,128)(2,1)S(1)}, bf16[2,256,384]{2,1,0:T(8,128)(2,1)S(1)}, u32[]{:S(2)}, u32[]{:S(2)}) collective-permute-start(bf16[2,256,384]{2,1,0:T(8,128)(2,1)S(1)} %x_own_kernel.1), channel_id=1, source_target_pairs={{0,2},{2,0},{1,3},{3,1},{4,6},{6,4},{5,7},{7,5},{8,10},{10,8},{9,1... | collective-permute-start | bytes 1179656 | tf_op jit(solution)/shard_map/ppermute | solution.py:565
  93.6 8.8 %collective-permute-start.15 = (bf16[2,256,128]{2,1,0:T(8,128)(2,1)S(1)}, bf16[2,256,128]{2,1,0:T(8,128)(2,1)S(1)}, u32[]{:S(2)}, u32[]{:S(2)}) collective-permute-start(bf16[2,256,128]{2,1,0:T(8,128)(2,1)S(1)} %x_last_kernel.1), channel_id=1, source_target_pairs={{0,2},{2,0},{1,3},{3,1},{4,6},{6,4},{5,7},{7,5},{8,10},{10,8},{9,1... | collective-permute-start | bytes 393224 | tf_op jit(solution)/shard_map/ppermute | solution.py:567
  96.3 16.6 %collective-permute-start.17 = (bf16[2,256,384]{2,1,0:T(8,128)(2,1)S(1)}, bf16[2,256,384]{2,1,0:T(8,128)(2,1)S(1)}, u32[]{:S(2)}, u32[]{:S(2)}) collective-permute-start(bf16[2,256,384]{2,1,0:T(8,128)(2,1)S(1)} %z_second_kernel.1), channel_id=1, source_target_pairs={{0,16},{4,20},{8,24},{20,4},{24,8},{28,12},{1,17},{5,21},{9,25},{2... | collective-permute-start | bytes 1179656 | tf_op jit(solution)/shard_map/ppermute | solution.py:463
